TPU v7x, 32 devices: a whole 2x2x4 slice. The times are simulated.
32 devices in a mesh: cols: 2 (over core), patch: 16 (over z, y, x).
Axes of the slice: x: 2, y: 2, z: 4, core: 2. Of those that a mesh axis runs over, the one named last changes fastest.
Arguments:
- vectors: bfloat16 [65536, 512], P('patch', 'cols'), may hold values from -6 to 6
- blocks: bfloat16 [512, 8, 128, 128], P('patch'), may hold values from -0.09375 to 0.09375
- tile_cols: int32 [512, 8], P('patch'), may hold values from 0 to 511, as said below
- live_tiles: int32 [16], P('patch'), may hold values from 1 to 32, as said below
Outputs:
- result: bfloat16 [65536, 512], P('patch', 'cols')
Inputs may be any that keep to these rules, and one draw needn't show every extreme that they name: `tile_cols`: each listed tile lies within 4 tiles of its own tile row; entries may repeat, and repeated blocks add. `live_tiles`: some patch is full in every draw.
All inputs are finite; a program needn't handle non-finite values.
Results may differ from a plain program's by a relative error of at most 0.0064.
Values may be sent and summed in bfloat16 or wider, within the bound.
No kernel may reach another device: no remote copies, remote signals or barrier semaphores. Data moves between devices by JAX's collectives and lax.ppermute only.
A program may use at most 128 MiB of HBM per device.

v0:
```python
import functools

import jax
import jax.numpy as jnp
from jax import lax
from jax.experimental import pallas as pl
from jax.experimental.pallas import tpu as pltpu
from jax.sharding import PartitionSpec as P

HALO_T = 4
STEPS = 3
ITERS = 8
GROUP = 4

VMEM_LIMIT = 48 * 1024 * 1024
ANY = pl.BlockSpec(memory_space=pl.ANY)
SMEM = pl.BlockSpec(memory_space=pltpu.SMEM)
F32, BF16 = jnp.float32, jnp.bfloat16


def dot(a, b):
    return jnp.dot(a, b, preferred_element_type=F32)


def tile_row(blocks, listed, field):
    wide = jnp.concatenate([blocks(n) for n in range(len(listed))], axis=1)
    tall = jnp.concatenate([field(tile) for tile in listed], axis=0)
    return dot(wide, tall)


def finish(acc, prev, alive):
    value = acc if prev is None else 2.0 * acc - prev.astype(F32)
    return jnp.where(alive, value, 0.0).astype(BF16)


def interior_kernel(first, tiles, nnz, tile, cols_ref, live_ref, *refs):
    if first:
        whole_ref, blocks_ref, out_ref, held, sem = refs
        copies = [pltpu.make_async_copy(whole_ref, held, sem.at[0])]
    else:
        lo_ref, mid_ref, hi_ref, prev_ref, blocks_ref, out_ref, held, sem = refs
        edge = HALO_T
        copies = [
            pltpu.make_async_copy(lo_ref, held.at[pl.ds(0, edge)], sem.at[0]),
            pltpu.make_async_copy(mid_ref, held.at[pl.ds(edge, tiles - 2 * edge)], sem.at[1]),
            pltpu.make_async_copy(hi_ref, held.at[pl.ds(tiles - edge, edge)], sem.at[2]),
        ]
    live = live_ref[0]
    step = pl.program_id(0)

    @pl.when(step == 0)
    def _():
        for copy in copies:
            copy.start()
        for copy in copies:
            copy.wait()
        if first:
            def clear(index, carry):
                held[index] = jnp.zeros(held.shape[1:], BF16)
                return carry
            lax.fori_loop(live, tiles, clear, 0)

    for r in range(GROUP):
        row = HALO_T + step * GROUP + r
        listed = [cols_ref[row, n] for n in range(nnz)]
        acc = tile_row(lambda n: blocks_ref[r, n], listed, lambda c: held[c])
        prev = None if first else prev_ref[r]
        out_ref[r] = finish(acc, prev, row < live)


def interior(first, cols, live, blocks, fields, prev):
    tiles, nnz, tile, _ = blocks.shape
    width = fields[0].shape[-1]
    inner = tiles - 2 * HALO_T
    body = functools.partial(interior_kernel, first, tiles, nnz, tile)
    block_spec = pl.BlockSpec((GROUP, nnz, tile, tile), lambda i: (i + HALO_T // GROUP, 0, 0, 0))
    row_spec = pl.BlockSpec((GROUP, tile, width), lambda i: (i, 0, 0))
    in_specs = [SMEM, SMEM] + [ANY] * len(fields)
    args = [cols, live] + list(fields)
    if not first:
        shift = HALO_T // GROUP if prev.shape[0] == tiles else 0
        in_specs.append(pl.BlockSpec((GROUP, tile, width), lambda i: (i + shift, 0, 0)))
        args.append(prev)
    return pl.pallas_call(
        body,
        grid=(inner // GROUP,),
        in_specs=in_specs + [block_spec],
        out_specs=row_spec,
        out_shape=jax.ShapeDtypeStruct((inner, tile, width), BF16),
        scratch_shapes=[
            pltpu.VMEM((tiles, tile, width), BF16),
            pltpu.SemaphoreType.DMA((3,)),
        ],
        compiler_params=pltpu.CompilerParams(vmem_limit_bytes=VMEM_LIMIT),
        cost_estimate=pl.CostEstimate(
            flops=2 * inner * nnz * tile * tile * width,
            bytes_accessed=inner * nnz * tile * tile * 2 + 3 * tiles * tile * width * 2,
            transcendentals=0,
        ),
        name="interior",
    )(*args, blocks)


def boundary_kernel(first, tiles, nnz, tile, cols_ref, live_ref, *refs):
    edge = HALO_T
    if first:
        below_ref, above_ref, whole_ref, blocks_ref = refs[:4]
        rest = refs[4:]
        own = [
            (whole_ref.at[pl.ds(0, 2 * edge)], edge, 2 * edge),
            (whole_ref.at[pl.ds(tiles - 2 * edge, 2 * edge)], 3 * edge, 2 * edge),
        ]
        lo_out, hi_out, held, stored, sem, block_sem = rest
    else:
        below_ref, above_ref, lo_ref, mid_ref, hi_ref, plo_ref, phi_ref, blocks_ref = refs[:8]
        lo_out, hi_out, held, stored, sem, block_sem, before = refs[8:]
        inner = tiles - 2 * edge
        own = [
            (lo_ref, edge, edge),
            (mid_ref.at[pl.ds(0, edge)], 2 * edge, edge),
            (mid_ref.at[pl.ds(inner - edge, edge)], 3 * edge, edge),
            (hi_ref, 4 * edge, edge),
        ]
    moves = [(src, held.at[pl.ds(at, count)]) for src, at, count in own]
    if not first:
        shift = phi_ref.shape[0] - edge
        moves.append((plo_ref.at[pl.ds(0, edge)], before.at[pl.ds(0, edge)]))
        moves.append((phi_ref.at[pl.ds(shift, edge)], before.at[pl.ds(edge, edge)]))
    moves.append((below_ref, held.at[pl.ds(0, edge)]))
    moves.append((above_ref, held.at[pl.ds(5 * edge, edge)]))
    copies = [
        pltpu.make_async_copy(src, dst, sem.at[i]) for i, (src, dst) in enumerate(moves)
    ]
    for copy in copies:
        copy.start()
    rows = list(range(edge)) + list(range(tiles - edge, tiles))
    fetches = [
        pltpu.make_async_copy(blocks_ref.at[row], stored.at[i], block_sem.at[i])
        for i, row in enumerate(rows)
    ]
    for fetch in fetches:
        fetch.start()
    live = live_ref[0]
    for copy in copies:
        copy.wait()
    if first:
        for own_tile in list(range(2 * edge)) + list(range(tiles - 2 * edge, tiles)):
            at = own_tile + edge if own_tile < 2 * edge else own_tile - tiles + 5 * edge

            @pl.when(own_tile >= live)
            def _():
                held[at] = jnp.zeros(held.shape[1:], BF16)

    for i, row in enumerate(rows):
        fetches[i].wait()
        shift = edge if row < edge else 5 * edge - tiles
        listed = [cols_ref[row, n] + shift for n in range(nnz)]
        acc = tile_row(lambda n: stored[i, n], listed, lambda c: held[c])
        prev = None if first else before[i]
        if row < edge:
            lo_out[row] = finish(acc, prev, row < live)
        else:
            hi_out[row - tiles + edge] = finish(acc, prev, row < live)


def boundary(first, cols, live, blocks, halos, fields, prev):
    tiles, nnz, tile, _ = blocks.shape
    width = fields[0].shape[-1]
    body = functools.partial(boundary_kernel, first, tiles, nnz, tile)
    shape = jax.ShapeDtypeStruct((HALO_T, tile, width), BF16)
    in_specs = [SMEM, SMEM] + [ANY] * (2 + len(fields))
    args = [cols, live] + list(halos) + list(fields)
    scratch = [
        pltpu.VMEM((6 * HALO_T, tile, width), BF16),
        pltpu.VMEM((2 * HALO_T, nnz, tile, tile), BF16),
        pltpu.SemaphoreType.DMA((8,)),
        pltpu.SemaphoreType.DMA((2 * HALO_T,)),
    ]
    if not first:
        in_specs += [ANY] * 2
        args += list(prev)
        scratch.append(pltpu.VMEM((2 * HALO_T, tile, width), BF16))
    out_spec = pl.BlockSpec(memory_space=pltpu.VMEM)
    return pl.pallas_call(
        body,
        in_specs=in_specs + [ANY],
        out_specs=(out_spec, out_spec),
        out_shape=(shape, shape),
        scratch_shapes=scratch,
        compiler_params=pltpu.CompilerParams(vmem_limit_bytes=VMEM_LIMIT),
        cost_estimate=pl.CostEstimate(
            flops=2 * 2 * HALO_T * nnz * tile * tile * width,
            bytes_accessed=2 * HALO_T * nnz * tile * tile * 2 + 10 * HALO_T * tile * width * 2,
            transcendentals=0,
        ),
        name="boundary",
    )(*args, blocks)


def gram_kernel(pairs, chunk, part_ref, *refs):
    fields = refs[: 2 * pairs]
    has_start = len(refs) == 2 * pairs + 4
    out_ref, square, cross = refs[-3:]
    half = square.shape[0] // 2
    square[...] = jnp.zeros(square.shape, F32)
    cross[...] = jnp.zeros(cross.shape, F32)
    is_first = part_ref[0] == 0
    across = (((0,), (0,)), ((), ()))
    for own_ref, other_ref in zip(fields[:pairs], fields[pairs:]):

        def add(index, carry):
            rows = pl.ds(pl.multiple_of(index * chunk, chunk), chunk)
            own, other = own_ref[rows, :], other_ref[rows, :]
            square[...] += lax.dot_general(own, own, across, preferred_element_type=F32)
            left = jnp.where(is_first, own[:, :half], other[:, half:])
            right = jnp.where(is_first, other, own)
            cross[...] += lax.dot_general(left, right, across, preferred_element_type=F32)
            return carry

        lax.fori_loop(0, own_ref.shape[0] // chunk, add, 0)
    blocks = [
        square[:half, :half], square[:half, half:], square[half:, half:],
        cross[:, :half], cross[:, half:],
    ]
    for i, block in enumerate(blocks):
        at = pl.ds(i * half, half)
        out_ref[at, :] = block + refs[2 * pairs][at, :] if has_start else block


def gram_share(part, owns, others, start):
    width = owns[0].shape[1]
    half = width // 2
    chunk = min(owns[0].shape[0], 512)
    body = functools.partial(gram_kernel, len(owns), chunk)
    args = [part] + list(owns) + list(others) + ([] if start is None else [start])
    rows = sum(own.shape[0] for own in owns)
    return pl.pallas_call(
        body,
        in_specs=[SMEM] + [pl.BlockSpec(memory_space=pltpu.VMEM)] * (len(args) - 1),
        out_specs=pl.BlockSpec(memory_space=pltpu.VMEM),
        out_shape=jax.ShapeDtypeStruct((5 * half, half), F32),
        scratch_shapes=[pltpu.VMEM((width, width), F32), pltpu.VMEM((half, width), F32)],
        compiler_params=pltpu.CompilerParams(vmem_limit_bytes=VMEM_LIMIT),
        cost_estimate=pl.CostEstimate(
            flops=2 * rows * width * 3 * half,
            bytes_accessed=2 * rows * width * 2 + 10 * half * half * 4,
            transcendentals=0,
        ),
        name="gram_share",
    )(*args)


def sum_over_patch(share):
    count = lax.axis_size("patch")
    me = lax.axis_index("patch")
    ways = 4
    quarter = me % ways

    def exchange(value, distance):
        return lax.ppermute(value, "patch", [(i, i ^ distance) for i in range(count)])

    parts = share.reshape(ways, -1, share.shape[1])
    pick = lambda d: lax.dynamic_index_in_dim(parts, quarter ^ d, 0, keepdims=False)
    got = [exchange(pick(d), d) for d in range(1, ways)]
    total = (pick(0) + got[0]) + (got[1] + got[2])
    stride = ways
    while stride < count:
        got = [exchange(total, d * stride) for d in range(1, ways)]
        total = (total + got[0]) + (got[1] + got[2])
        stride *= ways
    return jnp.stack([total] + [exchange(total, d) for d in range(1, ways)])


def split(value):
    high = value.astype(BF16)
    return high, (value - high.astype(F32)).astype(BF16)


def product3(left, right_stack):
    high, low = split(left)
    return dot(jnp.concatenate([high, high, low], axis=1), right_stack)


def finish_kernel(
    total_rows, chunk, place_ref, mine_ref, theirs_ref, *refs
):
    fields, out_ref = refs[:6], refs[6]
    shares, x_ref, z_ref, m_ref, stack, wide, result, sem, out_sem = refs[7:]
    part, quarter = place_ref[0], place_ref[1]
    size = x_ref.shape[0]
    width = size // 2
    half = width // 2
    copies = []
    for side in range(2):
        at = 0
        for source in fields[3 * side : 3 * side + 3]:
            rows = source.shape[0]
            target = wide.at[pl.ds(at, rows), pl.ds(side * width, width)]
            copies.append(pltpu.make_async_copy(source, target, sem.at[len(copies)]))
            at += rows
    for copy in copies:
        copy.start()

    piece = mine_ref.shape[1]
    for d in range(4):
        rows = pl.ds(pl.multiple_of((quarter ^ d) * piece, 8), piece)
        shares[part, rows, :] = mine_ref[d]
        shares[1 - part, rows, :] = theirs_ref[d]

    def block(side, index):
        return shares[side, pl.ds(index * half, half), :]

    def place(row, col, value):
        x_ref[pl.ds(row * half, half), pl.ds(col * half, half)] = value
        if row != col:
            x_ref[pl.ds(col * half, half), pl.ds(row * half, half)] = value.T

    for side in range(2):
        place(2 * side, 2 * side, block(side, 0))
        place(2 * side, 2 * side + 1, block(side, 1))
        place(2 * side + 1, 2 * side + 1, block(side, 2))
        place(side, 2, block(side, 3))
        place(side, 3, block(side, 4))

    gram = x_ref[...]
    norm = jnp.sqrt(jnp.sum(gram * gram, keepdims=True))
    x_ref[...] = gram / norm

    def set_middle():
        x = x_ref[...]
        row = lax.broadcasted_iota(jnp.int32, x.shape, 0)
        col = lax.broadcasted_iota(jnp.int32, x.shape, 1)
        middle = jnp.where(row == col, 1.5, 0.0) - 0.5 * x
        high, low = split(middle)
        stack[0:size, :] = high
        stack[size : 2 * size, :] = low
        stack[2 * size :, :] = high
        return middle

    def step_x():
        m_ref[...] = product3(x_ref[...], stack[...])
        x_ref[...] = product3(m_ref[...], stack[...])

    z_ref[...] = set_middle()
    step_x()

    def sweep(index, carry):
        set_middle()
        z_ref[...] = product3(z_ref[...], stack[...])
        step_x()
        return carry

    lax.fori_loop(1, ITERS - 1, sweep, 0)
    set_middle()
    z_ref[...] = product3(z_ref[...], stack[...])

    own = pl.ds(pl.multiple_of(part * width, width), width)
    other = pl.ds(pl.multiple_of((1 - part) * width, width), width)
    rotation = jnp.concatenate([z_ref[own, own], z_ref[other, own]], axis=0).astype(BF16)
    factor = jnp.sqrt(total_rows / norm)
    for copy in copies:
        copy.wait()
    count = wide.shape[0] // chunk
    outs = []
    for i in range(count):
        rows = pl.ds(i * chunk, chunk)
        result[rows, :] = (dot(wide[rows, :], rotation) * factor).astype(BF16)
        outs.append(pltpu.make_async_copy(result.at[rows], out_ref.at[rows], out_sem.at[i]))
        outs[-1].start()
    for out in outs:
        out.wait()


def rotate(place, mine, theirs, owns, others, total_rows):
    width = owns[0].shape[1]
    rows = sum(own.shape[0] for own in owns)
    size = 2 * width
    chunk = min(rows, 512)
    body = functools.partial(finish_kernel, float(total_rows), chunk)
    vmem = pl.BlockSpec(memory_space=pltpu.VMEM)
    matrix = pltpu.VMEM((size, size), F32)
    return pl.pallas_call(
        body,
        in_specs=[SMEM, vmem, vmem] + [ANY] * 6,
        out_specs=ANY,
        out_shape=jax.ShapeDtypeStruct((rows, width), BF16),
        scratch_shapes=[
            pltpu.VMEM((2, 5 * width // 2, width // 2), F32),
            matrix, matrix, matrix,
            pltpu.VMEM((3 * size, size), BF16),
            pltpu.VMEM((rows, size), BF16),
            pltpu.VMEM((rows, width), BF16),
            pltpu.SemaphoreType.DMA((6,)),
            pltpu.SemaphoreType.DMA((rows // chunk,)),
        ],
        compiler_params=pltpu.CompilerParams(vmem_limit_bytes=VMEM_LIMIT),
        cost_estimate=pl.CostEstimate(
            flops=21 * 6 * size**3 + 2 * rows * size * width,
            bytes_accessed=3 * rows * width * 2,
            transcendentals=0,
        ),
        name="rotate",
    )(place, mine, theirs, *owns, *others)


def on_device(vectors, blocks, tile_cols, live_tiles):
    tiles, nnz, tile, _ = blocks.shape
    width = vectors.shape[1]
    edge = HALO_T
    count = lax.axis_size("patch")
    part = lax.axis_index("cols")
    patch = lax.axis_index("patch")
    listed = tile_cols - patch * tiles
    up = [(i, i + 1) for i in range(count - 1)]
    down = [(i + 1, i) for i in range(count - 1)]

    def halos(lo, hi):
        return lax.ppermute(hi, "patch", up), lax.ppermute(lo, "patch", down)

    def sibling(value):
        return lax.ppermute(value, "cols", [(0, 1), (1, 0)])

    start = vectors.reshape(tiles, tile, width)
    alive = (jnp.arange(tiles, dtype=jnp.int32) < live_tiles[0])[:, None, None]
    low = jnp.where(alive[:edge], start[:edge], jnp.zeros((), BF16))
    high = jnp.where(alive[-edge:], start[-edge:], jnp.zeros((), BF16))

    around = halos(low, high)
    mid = interior(True, listed, live_tiles, blocks, (start,), None)
    lo, hi = boundary(True, listed, live_tiles, blocks, around, (start,), None)
    prev = (start, start, start)
    for step in range(STEPS - 1):
        fields = (lo, mid, hi)
        around = halos(lo, hi)
        new_mid = interior(False, listed, live_tiles, blocks, fields, prev[1])
        if step == STEPS - 2:
            flat = new_mid.reshape(-1, width)
            other_mid = sibling(flat)
            part_arg = part.astype(jnp.int32)[None]
            inner_share = gram_share(part_arg, [flat], [other_mid], None)
        lo, hi = boundary(
            False, listed, live_tiles, blocks, around, fields, (prev[0], prev[2])
        )
        prev, mid = fields, new_mid
    lo, mid, hi = (value.reshape(-1, width) for value in (lo, mid, hi))
    other_lo, other_hi = sibling(lo), sibling(hi)
    share = gram_share(part_arg, [lo, hi], [other_lo, other_hi], inner_share)
    mine = sum_over_patch(share)
    theirs = sibling(mine)
    place = jnp.stack([part, patch % 4]).astype(jnp.int32)
    total_rows = tiles * tile * count
    return rotate(
        place, mine, theirs, [lo, mid, hi], [other_lo, other_mid, other_hi], total_rows
    )


def solution(mesh):
    in_specs = (P("patch", "cols"), P("patch", None, None, None), P("patch", None), P("patch"))
    return jax.shard_map(
        on_device, mesh=mesh, in_specs=in_specs, out_specs=P("patch", "cols"), check_vma=False
    )
```

profile of v0, /device:TPU:0, one launch (start us, length us, event | category | flops | bytes accessed | tf_op | source)
XLA Modules:
  0.0 133.3 jit_solution(3875636227496749211)
XLA Ops:
  0.0 0.0 copy-start
  0.0 0.0 copy-start.4
  0.8 0.1 fusion.2
  0.9 1.1 fusion.1
  2.0 0.1 broadcast_select_fusion.1
  2.1 4.9 %collective-permute-start = (bf16[4,128,256]{2,1,0:T(8,128)(2,1)S(1)}, bf16[4,128,256]{2,1,0:T(8,128)(2,1)S(1)}, u32[]{:S(2)}, u32[]{:S(2)}) collective-permute-start(bf16[4,128,256]{2,1,0:T(8,128)(2,1)S(1)} %broadcast_select_fusion.1), channel_id=1, source_target_pairs={{0,1},{1,2},{2,3},{3,4},{4,5},{5,6},{6,7},{7,8},{8,9},{9,10},{10,1... | collective-permute-start | bytes 786440 | tf_op jit(solution)/shard_map/ppermute | solution.py:418
  6.9 0.1 broadcast_select_fusion
  7.0 1.3 collective-permute-start.1
  8.3 0.0 copy-done.4
  8.3 0.1 copy.5
  8.4 9.7 %collective-permute-done.refs_0_ = bf16[4,128,256]{2,1,0:T(8,128)(2,1)S(1)} collective-permute-done((bf16[4,128,256]{2,1,0:T(8,128)(2,1)S(1)}, bf16[4,128,256]{2,1,0:T(8,128)(2,1)S(1)}, u32[]{:S(2)}, u32[]{:S(2)}) %collective-permute-start) | collective-permute-done | bytes 262176 | tf_op jit(solution)/shard_map/ppermute | solution.py:418
  18.1 1.9 %collective-permute-done.1.refs_1_ = bf16[4,128,256]{2,1,0:T(8,128)(2,1)S(1)} collective-permute-done((bf16[4,128,256]{2,1,0:T(8,128)(2,1)S(1)}, bf16[4,128,256]{2,1,0:T(8,128)(2,1)S(1)}, u32[]{:S(2)}, u32[]{:S(2)}) %collective-permute-start.1) | collective-permute-done | bytes 262176 | tf_op jit(solution)/shard_map/ppermute | solution.py:418
  20.0 0.0 copy-done
  20.0 4.3 %boundary.3 = (bf16[4,128,256]{2,1,0:T(8,128)(2,1)S(1)}, bf16[4,128,256]{2,1,0:T(8,128)(2,1)S(1)}) custom-call(s32[32,8]{1,0:T(8,128)S(1)} %broadcast_subtract_fusion.cols_ref, s32[1]{0:T(128)} %copy.6.live_ref, bf16[4,128,256]{2,1,0:T(8,128)(2,1)S(1)} %collective-permute-done.refs_0_, bf16[4,128,256]{2,1,0:T(8,128)(2,1)S(1)} %collective-permute-done.1.refs_1_, ...), custom_call_target="tpu_custom_call" | custom-call | flops 536870912 | bytes 4718592 | tf_op jit(solution)/shard_map/boundary/pallas_call | solution.py:184
  24.4 3.4 %collective-permute-start.2 = (bf16[4,128,256]{2,1,0:T(8,128)(2,1)S(1)}, bf16[4,128,256]{2,1,0:T(8,128)(2,1)S(1)}, u32[]{:S(2)}, u32[]{:S(2)}) collective-permute-start(bf16[4,128,256]{2,1,0:T(8,128)(2,1)S(1)} %get-tuple-element.11.refs_4_.refs_2_.refs_6_), channel_id=1, source_target_pairs={{0,1},{1,2},{2,3},{3,4},{4,5},{5,6},{6,7},{7,8},{8,9},{9,10},{10,1... | collective-permute-start | bytes 786440 | tf_op jit(solution)/shard_map/ppermute | solution.py:418
  27.8 1.3 collective-permute-start.3
  29.1 6.0 %interior.3.refs_3_.refs_1_ = bf16[24,128,256]{2,1,0:T(8,128)(2,1)S(1)} custom-call(s32[32,8]{1,0:T(8,128)S(1)} %broadcast_subtract_fusion.cols_ref, s32[1]{0:T(128)} %copy.6.live_ref, bf16[32,128,256]{2,1,0:T(8,128)(2,1)S(1)} %bitcast.26, bf16[32,8,128,128]{3,2,1,0:T(8,128)(2,1)} %refs_4_.3), custom_call_target="tpu_custom_call" | custom-call | flops 1610612736 | bytes 12582912 | tf_op jit(solution)/shard_map/interior/pallas_call | solution.py:84
  35.1 6.0 %interior.4.refs_3_.refs_1_ = bf16[24,128,256]{2,1,0:T(8,128)(2,1)S(1)} custom-call(s32[32,8]{1,0:T(8,128)S(1)} %broadcast_subtract_fusion.cols_ref, s32[1]{0:T(128)} %copy.6.live_ref, bf16[4,128,256]{2,1,0:T(8,128)(2,1)S(1)} %get-tuple-element.12.refs_2_.refs_0_.refs_5_, bf16[24,128,256]{2,1,0:T(8,128)(2,1)S(1)} %interior.3.refs_3_.refs_1_, ...), custom_call_target="tpu_custom_call" | custom-call | flops 1610612736 | bytes 12582912 | tf_op jit(solution)/shard_map/interior/pallas_call | solution.py:84
  41.1 0.0 collective-permute-done.2.refs_0_
  41.1 0.0 collective-permute-done.3.refs_1_
  41.1 4.4 %boundary.4 = (bf16[4,128,256]{2,1,0:T(8,128)(2,1)S(1)}, bf16[4,128,256]{2,1,0:T(8,128)(2,1)S(1)}) custom-call(s32[32,8]{1,0:T(8,128)S(1)} %broadcast_subtract_fusion.cols_ref, s32[1]{0:T(128)} %copy.6.live_ref, bf16[4,128,256]{2,1,0:T(8,128)(2,1)S(1)} %collective-permute-done.2.refs_0_, bf16[4,128,256]{2,1,0:T(8,128)(2,1)S(1)} %collective-permute-done.3.refs_1_, ...), custom_call_target="tpu_custom_call" | custom-call | flops 536870912 | bytes 4718592 | tf_op jit(solution)/shard_map/boundary/pallas_call | solution.py:184
  45.5 6.0 %interior.5 = bf16[24,128,256]{2,1,0:T(8,128)(2,1)S(1)} custom-call(s32[32,8]{1,0:T(8,128)S(1)} %broadcast_subtract_fusion.cols_ref, s32[1]{0:T(128)} %copy.6.live_ref, bf16[4,128,256]{2,1,0:T(8,128)(2,1)S(1)} %get-tuple-element.14.refs_2_.refs_0_, bf16[24,128,256]{2,1,0:T(8,128)(2,1)S(1)} %interior.4.refs_3_.refs_1_, ...), custom_call_target="tpu_custom_call" | custom-call | flops 1610612736 | bytes 12582912 | tf_op jit(solution)/shard_map/interior/pallas_call | solution.py:84
  51.5 0.1 collective-permute-start.8
  51.5 4.6 %collective-permute-start.4 = (bf16[4,128,256]{2,1,0:T(8,128)(2,1)S(1)}, bf16[4,128,256]{2,1,0:T(8,128)(2,1)S(1)}, u32[]{:S(2)}, u32[]{:S(2)}) collective-permute-start(bf16[4,128,256]{2,1,0:T(8,128)(2,1)S(1)} %get-tuple-element.13.refs_4_.refs_2_), channel_id=1, source_target_pairs={{0,1},{1,2},{2,3},{3,4},{4,5},{5,6},{6,7},{7,8},{8,9},{9,10},{10,1... | collective-permute-start | bytes 786440 | tf_op jit(solution)/shard_map/ppermute | solution.py:418
  56.1 1.5 %collective-permute-start.5 = (bf16[4,128,256]{2,1,0:T(8,128)(2,1)S(1)}, bf16[4,128,256]{2,1,0:T(8,128)(2,1)S(1)}, u32[]{:S(2)}, u32[]{:S(2)}) collective-permute-start(bf16[4,128,256]{2,1,0:T(8,128)(2,1)S(1)} %get-tuple-element.14.refs_2_.refs_0_), channel_id=1, source_target_pairs={{1,0},{2,1},{3,2},{4,3},{5,4},{6,5},{7,6},{8,7},{9,8},{10,9},{11,1... | collective-permute-start | bytes 786440 | tf_op jit(solution)/shard_map/ppermute | solution.py:418
  57.6 4.7 %collective-permute-done.4.refs_0_ = bf16[4,128,256]{2,1,0:T(8,128)(2,1)S(1)} collective-permute-done((bf16[4,128,256]{2,1,0:T(8,128)(2,1)S(1)}, bf16[4,128,256]{2,1,0:T(8,128)(2,1)S(1)}, u32[]{:S(2)}, u32[]{:S(2)}) %collective-permute-start.4) | collective-permute-done | bytes 262176 | tf_op jit(solution)/shard_map/ppermute | solution.py:418
  62.3 7.0 %collective-permute-done.5.refs_1_ = bf16[4,128,256]{2,1,0:T(8,128)(2,1)S(1)} collective-permute-done((bf16[4,128,256]{2,1,0:T(8,128)(2,1)S(1)}, bf16[4,128,256]{2,1,0:T(8,128)(2,1)S(1)}, u32[]{:S(2)}, u32[]{:S(2)}) %collective-permute-start.5) | collective-permute-done | bytes 262176 | tf_op jit(solution)/shard_map/ppermute | solution.py:418
  69.3 5.1 %boundary.5 = (bf16[4,128,256]{2,1,0:T(8,128)(2,1)S(1)}, bf16[4,128,256]{2,1,0:T(8,128)(2,1)}) custom-call(s32[32,8]{1,0:T(8,128)S(1)} %broadcast_subtract_fusion.cols_ref, s32[1]{0:T(128)} %copy.6.live_ref, bf16[4,128,256]{2,1,0:T(8,128)(2,1)S(1)} %collective-permute-done.4.refs_0_, bf16[4,128,256]{2,1,0:T(8,128)(2,1)S(1)} %collective-permute-done.5.refs_1_, ...), custom_call_target="tpu_custom_call" | custom-call | flops 536870912 | bytes 4718592 | tf_op jit(solution)/shard_map/boundary/pallas_call | solution.py:184
  74.4 0.0 copy-start.1
  74.4 0.1 collective-permute-start.7
  74.5 0.5 collective-permute-start.6
  75.0 0.0 collective-permute-done.8.refs_1_.refs_4_
  75.0 1.8 %gram_share.2.refs_4_ = f32[640,128]{1,0:T(8,128)S(1)} custom-call(s32[1]{0:T(128)} %bitcast.part_ref, bf16[3072,256]{1,0:T(8,128)(2,1)S(1)} %bitcast.31, bf16[3072,256]{1,0:T(8,128)(2,1)S(1)} %collective-permute-done.8.refs_1_.refs_4_), custom_call_target="tpu_custom_call" | custom-call | flops 603979776 | bytes 3801088 | tf_op jit(solution)/shard_map/gram_share/pallas_call | solution.py:237
  76.9 0.0 collective-permute-done.7.refs_3_.refs_5_
  76.9 0.0 copy-done.1
  76.9 0.0 collective-permute-done.6.refs_2_.refs_3_
  76.9 0.0 copy-start.2
  76.9 0.9 copy-done.2
  77.8 1.5 %gram_share.3 = f32[640,128]{1,0:T(8,128)S(1)} custom-call(s32[1]{0:T(128)} %bitcast.part_ref, bf16[512,256]{1,0:T(8,128)(2,1)S(1)} %bitcast.36, bf16[512,256]{1,0:T(8,128)(2,1)} %bitcast.7.refs_1_.refs_2_, bf16[512,256]{1,0:T(8,128)(2,1)} %collective-permute-done.6.refs_2_.refs_3_, bf16[512,256]{1,0:T(8,128)(2,1)} %collective-permute-done.7.refs_3_.refs_5_, ...), custom_call_target="tpu_custom_call" | custom-call | flops 201326592 | bytes 1703936 | tf_op jit(solution)/shard_map/gram_share/pallas_call | solution.py:237
  79.4 0.7 dynamic-slice_bitcast_fusion
  80.1 3.2 %collective-permute-start.11 = (f32[160,128]{1,0:T(8,128)}, f32[160,128]{1,0:T(8,128)}, u32[]{:S(2)}, u32[]{:S(2)}) collective-permute-start(f32[160,128]{1,0:T(8,128)} %get-tuple-element.19), channel_id=1, source_target_pairs={{0,3},{1,2},{2,1},{3,0},{4,7},{5,6},{6,5},{7,4},{8,11},{9,10},{10,... | collective-permute-start | bytes 245768 | tf_op jit(solution)/shard_map/ppermute | solution.py:260
  83.3 0.0 collective-permute-start.10
  83.3 0.6 collective-permute-start.9
  83.8 2.6 %collective-permute-done.11 = f32[160,128]{1,0:T(8,128)} collective-permute-done((f32[160,128]{1,0:T(8,128)}, f32[160,128]{1,0:T(8,128)}, u32[]{:S(2)}, u32[]{:S(2)}) %collective-permute-start.11) | collective-permute-done | bytes 81952 | tf_op jit(solution)/shard_map/ppermute | solution.py:260
  86.4 1.6 %collective-permute-done.10 = f32[160,128]{1,0:T(8,128)} collective-permute-done((f32[160,128]{1,0:T(8,128)}, f32[160,128]{1,0:T(8,128)}, u32[]{:S(2)}, u32[]{:S(2)}) %collective-permute-start.10) | collective-permute-done | bytes 81952 | tf_op jit(solution)/shard_map/ppermute | solution.py:260
  88.0 0.0 collective-permute-done.9
  88.0 1.0 fusion
  89.0 5.4 %collective-permute-start.14 = (f32[160,128]{1,0:T(8,128)S(1)}, f32[160,128]{1,0:T(8,128)S(1)}, u32[]{:S(2)}, u32[]{:S(2)}) collective-permute-start(f32[160,128]{1,0:T(8,128)S(1)} %fusion), channel_id=1, source_target_pairs={{0,12},{1,13},{2,14},{3,15},{4,8},{5,9},{6,10},{7,11},{8,4},{9,5},... | collective-permute-start | bytes 245768 | tf_op jit(solution)/shard_map/ppermute | solution.py:260
  94.4 0.0 collective-permute-start.13
  94.4 0.6 collective-permute-start.12
  95.1 2.5 %collective-permute-done.14 = f32[160,128]{1,0:T(8,128)S(1)} collective-permute-done((f32[160,128]{1,0:T(8,128)S(1)}, f32[160,128]{1,0:T(8,128)S(1)}, u32[]{:S(2)}, u32[]{:S(2)}) %collective-permute-start.14) | collective-permute-done | bytes 81952 | tf_op jit(solution)/shard_map/ppermute | solution.py:260
  97.6 3.1 %collective-permute-done.13 = f32[160,128]{1,0:T(8,128)S(1)} collective-permute-done((f32[160,128]{1,0:T(8,128)S(1)}, f32[160,128]{1,0:T(8,128)S(1)}, u32[]{:S(2)}, u32[]{:S(2)}) %collective-permute-start.13) | collective-permute-done | bytes 81952 | tf_op jit(solution)/shard_map/ppermute | solution.py:260
  100.7 0.0 collective-permute-done.12
  100.7 1.7 %collective-permute-start.17 = (f32[160,128]{1,0:T(8,128)S(1)}, f32[160,128]{1,0:T(8,128)S(1)}, u32[]{:S(2)}, u32[]{:S(2)}) collective-permute-start(f32[160,128]{1,0:T(8,128)S(1)} %add_add_fusion), channel_id=1, source_target_pairs={{0,3},{1,2},{2,1},{3,0},{4,7},{5,6},{6,5},{7,4},{8,11},{9,10},{10,... | collective-permute-start | bytes 245768 | tf_op jit(solution)/shard_map/ppermute | solution.py:260
  102.4 0.2 collective-permute-start.16
  102.6 1.7 %collective-permute-start.15 = (f32[160,128]{1,0:T(8,128)S(1)}, f32[160,128]{1,0:T(8,128)S(1)}, u32[]{:S(2)}, u32[]{:S(2)}) collective-permute-start(f32[160,128]{1,0:T(8,128)S(1)} %add_add_fusion), channel_id=1, source_target_pairs={{0,1},{1,0},{2,3},{3,2},{4,5},{5,4},{6,7},{7,6},{8,9},{9,8},{10,11... | collective-permute-start | bytes 245768 | tf_op jit(solution)/shard_map/ppermute | solution.py:260
  104.3 2.4 %collective-permute-done.17 = f32[160,128]{1,0:T(8,128)S(1)} collective-permute-done((f32[160,128]{1,0:T(8,128)S(1)}, f32[160,128]{1,0:T(8,128)S(1)}, u32[]{:S(2)}, u32[]{:S(2)}) %collective-permute-start.17) | collective-permute-done | bytes 81952 | tf_op jit(solution)/shard_map/ppermute | solution.py:260
  106.7 0.7 collective-permute-done.16
  107.4 0.0 collective-permute-done.15
  107.4 0.1 collective-permute-start.18
  107.5 0.1 pad_add_fusion.place_ref
  107.6 1.5 %collective-permute-done.18.theirs_ref = f32[4,160,128]{2,1,0:T(8,128)S(1)} collective-permute-done((f32[4,160,128]{2,1,0:T(8,128)S(1)}, f32[4,160,128]{2,1,0:T(8,128)S(1)}, u32[]{:S(2)}, u32[]{:S(2)}) %collective-permute-start.18) | collective-permute-done | bytes 327712 | tf_op jit(solution)/shard_map/ppermute | solution.py:421
  109.1 0.9 copy-done.3
  110.1 23.1 %rotate.1 = bf16[4096,256]{1,0:T(8,128)(2,1)} custom-call(s32[2]{0:T(128)S(1)} %pad_add_fusion.place_ref, f32[4,160,128]{2,1,0:T(8,128)S(1)} %pad_maximum_fusion.mine_ref, f32[4,160,128]{2,1,0:T(8,128)S(1)} %collective-permute-done.18.theirs_ref, bf16[512,256]{1,0:T(8,128)(2,1)S(1)} %bitcast.37, bf16[3072,256]{1,0:T(8,128)(2,1)S(1)} %bitcast.32, ...), custom_call_target="tpu_custom_call" | custom-call | flops 17985175552 | bytes 6291456 | tf_op jit(solution)/shard_map/rotate/pallas_call | solution.py:382
  (5 shorter events, 0.1 us)
Async XLA Ops:
  0.0 20.0 %copy-start = (bf16[4096,256]{1,0:T(8,128)(2,1)S(1)}, bf16[4096,256]{1,0:T(8,128)(2,1)}, u32[]{:S(2)}) copy-start(bf16[4096,256]{1,0:T(8,128)(2,1)} %param.4) | copy-start | bytes 6291460
  0.0 8.3 %copy-start.4 = (s32[32,8]{0,1:T(8,128)S(1)}, s32[32,8]{0,1:T(8,128)}, u32[]{:S(2)}) copy-start(s32[32,8]{0,1:T(8,128)} %param.6) | copy-start | bytes 3076
  2.1 16.0 %collective-permute-start = (bf16[4,128,256]{2,1,0:T(8,128)(2,1)S(1)}, bf16[4,128,256]{2,1,0:T(8,128)(2,1)S(1)}, u32[]{:S(2)}, u32[]{:S(2)}) collective-permute-start(bf16[4,128,256]{2,1,0:T(8,128)(2,1)S(1)} %broadcast_select_fusion.1), channel_id=1, source_target_pairs={{0,1},{1,2},{2,3},{3,4},{4,5},{5,6},{6,7},{7,8},{8,9},{9,10},{10,1... | collective-permute-start | bytes 786440 | tf_op jit(solution)/shard_map/ppermute | solution.py:418
  7.0 13.0 %collective-permute-start.1 = (bf16[4,128,256]{2,1,0:T(8,128)(2,1)S(1)}, bf16[4,128,256]{2,1,0:T(8,128)(2,1)S(1)}, u32[]{:S(2)}, u32[]{:S(2)}) collective-permute-start(bf16[4,128,256]{2,1,0:T(8,128)(2,1)S(1)} %broadcast_select_fusion), channel_id=1, source_target_pairs={{1,0},{2,1},{3,2},{4,3},{5,4},{6,5},{7,6},{8,7},{9,8},{10,9},{11,1... | collective-permute-start | bytes 786440 | tf_op jit(solution)/shard_map/ppermute | solution.py:418
  24.4 16.7 %collective-permute-start.2 = (bf16[4,128,256]{2,1,0:T(8,128)(2,1)S(1)}, bf16[4,128,256]{2,1,0:T(8,128)(2,1)S(1)}, u32[]{:S(2)}, u32[]{:S(2)}) collective-permute-start(bf16[4,128,256]{2,1,0:T(8,128)(2,1)S(1)} %get-tuple-element.11.refs_4_.refs_2_.refs_6_), channel_id=1, source_target_pairs={{0,1},{1,2},{2,3},{3,4},{4,5},{5,6},{6,7},{7,8},{8,9},{9,10},{10,1... | collective-permute-start | bytes 786440 | tf_op jit(solution)/shard_map/ppermute | solution.py:418
  27.8 13.3 %collective-permute-start.3 = (bf16[4,128,256]{2,1,0:T(8,128)(2,1)S(1)}, bf16[4,128,256]{2,1,0:T(8,128)(2,1)S(1)}, u32[]{:S(2)}, u32[]{:S(2)}) collective-permute-start(bf16[4,128,256]{2,1,0:T(8,128)(2,1)S(1)} %get-tuple-element.12.refs_2_.refs_0_.refs_5_), channel_id=1, source_target_pairs={{1,0},{2,1},{3,2},{4,3},{5,4},{6,5},{7,6},{8,7},{9,8},{10,9},{11,1... | collective-permute-start | bytes 786440 | tf_op jit(solution)/shard_map/ppermute | solution.py:418
  51.5 23.6 %collective-permute-start.8 = (bf16[3072,256]{1,0:T(8,128)(2,1)S(1)}, bf16[3072,256]{1,0:T(8,128)(2,1)S(1)}, u32[]{:S(2)}, u32[]{:S(2)}) collective-permute-start(bf16[3072,256]{1,0:T(8,128)(2,1)S(1)} %bitcast.30), channel_id=1, source_target_pairs={{0,16},{16,0},{1,17},{17,1},{2,18},{18,2},{3,19},{19,3},{4,20},{20... | collective-permute-start | bytes 4718600 | tf_op jit(solution)/shard_map/ppermute | solution.py:421
  51.5 10.8 %collective-permute-start.4 = (bf16[4,128,256]{2,1,0:T(8,128)(2,1)S(1)}, bf16[4,128,256]{2,1,0:T(8,128)(2,1)S(1)}, u32[]{:S(2)}, u32[]{:S(2)}) collective-permute-start(bf16[4,128,256]{2,1,0:T(8,128)(2,1)S(1)} %get-tuple-element.13.refs_4_.refs_2_), channel_id=1, source_target_pairs={{0,1},{1,2},{2,3},{3,4},{4,5},{5,6},{6,7},{7,8},{8,9},{9,10},{10,1... | collective-permute-start | bytes 786440 | tf_op jit(solution)/shard_map/ppermute | solution.py:418
  56.1 13.2 %collective-permute-start.5 = (bf16[4,128,256]{2,1,0:T(8,128)(2,1)S(1)}, bf16[4,128,256]{2,1,0:T(8,128)(2,1)S(1)}, u32[]{:S(2)}, u32[]{:S(2)}) collective-permute-start(bf16[4,128,256]{2,1,0:T(8,128)(2,1)S(1)} %get-tuple-element.14.refs_2_.refs_0_), channel_id=1, source_target_pairs={{1,0},{2,1},{3,2},{4,3},{5,4},{6,5},{7,6},{8,7},{9,8},{10,9},{11,1... | collective-permute-start | bytes 786440 | tf_op jit(solution)/shard_map/ppermute | solution.py:418
  74.4 2.5 %copy-start.1 = (bf16[4,128,256]{2,1,0:T(8,128)(2,1)}, bf16[4,128,256]{2,1,0:T(8,128)(2,1)S(1)}, u32[]{:S(2)}) copy-start(bf16[4,128,256]{2,1,0:T(8,128)(2,1)S(1)} %get-tuple-element.15) | copy-start | bytes 786436
  74.4 2.4 %collective-permute-start.7 = (bf16[512,256]{1,0:T(8,128)(2,1)}, bf16[512,256]{1,0:T(8,128)(2,1)}, u32[]{:S(2)}, u32[]{:S(2)}) collective-permute-start(bf16[512,256]{1,0:T(8,128)(2,1)} %bitcast.7.refs_1_.refs_2_), channel_id=1, source_target_pairs={{0,16},{16,0},{1,17},{17,1},{2,18},{18,2},{3,19},{19,3},{4,20},{20... | collective-permute-start | bytes 786440 | tf_op jit(solution)/shard_map/ppermute | solution.py:421
  74.5 2.4 %collective-permute-start.6 = (bf16[512,256]{1,0:T(8,128)(2,1)S(1)}, bf16[512,256]{1,0:T(8,128)(2,1)}, u32[]{:S(2)}, u32[]{:S(2)}) collective-permute-start(bf16[512,256]{1,0:T(8,128)(2,1)S(1)} %bitcast.35), channel_id=1, source_target_pairs={{0,16},{16,0},{1,17},{17,1},{2,18},{18,2},{3,19},{19,3},{4,20},{20... | collective-permute-start | bytes 786440 | tf_op jit(solution)/shard_map/ppermute | solution.py:421
  76.9 1.0 copy-start.2
  80.1 6.3 %collective-permute-start.11 = (f32[160,128]{1,0:T(8,128)}, f32[160,128]{1,0:T(8,128)}, u32[]{:S(2)}, u32[]{:S(2)}) collective-permute-start(f32[160,128]{1,0:T(8,128)} %get-tuple-element.19), channel_id=1, source_target_pairs={{0,3},{1,2},{2,1},{3,0},{4,7},{5,6},{6,5},{7,4},{8,11},{9,10},{10,... | collective-permute-start | bytes 245768 | tf_op jit(solution)/shard_map/ppermute | solution.py:260
  83.3 4.8 %collective-permute-start.10 = (f32[160,128]{1,0:T(8,128)}, f32[160,128]{1,0:T(8,128)}, u32[]{:S(2)}, u32[]{:S(2)}) collective-permute-start(f32[160,128]{1,0:T(8,128)} %get-tuple-element.20), channel_id=1, source_target_pairs={{0,2},{1,3},{2,0},{3,1},{4,6},{5,7},{6,4},{7,5},{8,10},{9,11},{10,... | collective-permute-start | bytes 245768 | tf_op jit(solution)/shard_map/ppermute | solution.py:260
  83.3 4.8 %collective-permute-start.9 = (f32[160,128]{1,0:T(8,128)S(1)}, f32[160,128]{1,0:T(8,128)}, u32[]{:S(2)}, u32[]{:S(2)}) collective-permute-start(f32[160,128]{1,0:T(8,128)S(1)} %get-tuple-element.21), channel_id=1, source_target_pairs={{0,1},{1,0},{2,3},{3,2},{4,5},{5,4},{6,7},{7,6},{8,9},{9,8},{10,11... | collective-permute-start | bytes 245768 | tf_op jit(solution)/shard_map/ppermute | solution.py:260
  89.0 8.6 %collective-permute-start.14 = (f32[160,128]{1,0:T(8,128)S(1)}, f32[160,128]{1,0:T(8,128)S(1)}, u32[]{:S(2)}, u32[]{:S(2)}) collective-permute-start(f32[160,128]{1,0:T(8,128)S(1)} %fusion), channel_id=1, source_target_pairs={{0,12},{1,13},{2,14},{3,15},{4,8},{5,9},{6,10},{7,11},{8,4},{9,5},... | collective-permute-start | bytes 245768 | tf_op jit(solution)/shard_map/ppermute | solution.py:260
  94.4 6.3 %collective-permute-start.13 = (f32[160,128]{1,0:T(8,128)S(1)}, f32[160,128]{1,0:T(8,128)S(1)}, u32[]{:S(2)}, u32[]{:S(2)}) collective-permute-start(f32[160,128]{1,0:T(8,128)S(1)} %fusion), channel_id=1, source_target_pairs={{0,8},{1,9},{2,10},{3,11},{4,12},{5,13},{6,14},{7,15},{8,0},{9,1},... | collective-permute-start | bytes 245768 | tf_op jit(solution)/shard_map/ppermute | solution.py:260
  94.4 6.3 %collective-permute-start.12 = (f32[160,128]{1,0:T(8,128)S(1)}, f32[160,128]{1,0:T(8,128)S(1)}, u32[]{:S(2)}, u32[]{:S(2)}) collective-permute-start(f32[160,128]{1,0:T(8,128)S(1)} %fusion), channel_id=1, source_target_pairs={{0,4},{1,5},{2,6},{3,7},{4,0},{5,1},{6,2},{7,3},{8,12},{9,13},{10,... | collective-permute-start | bytes 245768 | tf_op jit(solution)/shard_map/ppermute | solution.py:260
  100.7 5.9 %collective-permute-start.17 = (f32[160,128]{1,0:T(8,128)S(1)}, f32[160,128]{1,0:T(8,128)S(1)}, u32[]{:S(2)}, u32[]{:S(2)}) collective-permute-start(f32[160,128]{1,0:T(8,128)S(1)} %add_add_fusion), channel_id=1, source_target_pairs={{0,3},{1,2},{2,1},{3,0},{4,7},{5,6},{6,5},{7,4},{8,11},{9,10},{10,... | collective-permute-start | bytes 245768 | tf_op jit(solution)/shard_map/ppermute | solution.py:260
  102.4 5.0 %collective-permute-start.16 = (f32[160,128]{1,0:T(8,128)S(1)}, f32[160,128]{1,0:T(8,128)S(1)}, u32[]{:S(2)}, u32[]{:S(2)}) collective-permute-start(f32[160,128]{1,0:T(8,128)S(1)} %add_add_fusion), channel_id=1, source_target_pairs={{0,2},{1,3},{2,0},{3,1},{4,6},{5,7},{6,4},{7,5},{8,10},{9,11},{10,... | collective-permute-start | bytes 245768 | tf_op jit(solution)/shard_map/ppermute | solution.py:260
  102.6 4.8 %collective-permute-start.15 = (f32[160,128]{1,0:T(8,128)S(1)}, f32[160,128]{1,0:T(8,128)S(1)}, u32[]{:S(2)}, u32[]{:S(2)}) collective-permute-start(f32[160,128]{1,0:T(8,128)S(1)} %add_add_fusion), channel_id=1, source_target_pairs={{0,1},{1,0},{2,3},{3,2},{4,5},{5,4},{6,7},{7,6},{8,9},{9,8},{10,11... | collective-permute-start | bytes 245768 | tf_op jit(solution)/shard_map/ppermute | solution.py:260
  107.4 1.7 %collective-permute-start.18 = (f32[4,160,128]{2,1,0:T(8,128)S(1)}, f32[4,160,128]{2,1,0:T(8,128)S(1)}, u32[]{:S(2)}, u32[]{:S(2)}) collective-permute-start(f32[4,160,128]{2,1,0:T(8,128)S(1)} %pad_maximum_fusion.mine_ref), channel_id=1, source_target_pairs={{0,16},{16,0},{1,17},{17,1},{2,18},{18,2},{3,19},{19,3},{4,20},{20... | collective-permute-start | bytes 983048 | tf_op jit(solution)/shard_map/ppermute | solution.py:421
  109.1 1.0 copy-start.3
where the time goes:
time: 134 us; the launch traced here: 133 us
  Pallas kernels  58.1 us (43%)
  waiting for transfers between devices  37.8 us (28%)
  starting transfers between devices  31 us (23%)
  local copies, waits for them, and re-layouts  3.82 us (3%)
    ppermute x6, waiting for transfers between devices, halos(): return (lax.ppermute(hi, 'patch', up), lax.ppermute(lo, 'patch', down))  23.3 us
    pallas_call x1, Pallas kernels, rotate(): pl.pallas_call(body, in_specs=[SMEM, vmem, vmem] + [ANY] * 6, out_specs=A...  23.1 us
    pallas_call x3, Pallas kernels, interior(): pl.pallas_call(body, grid=(inner // GROUP,), in_specs=in_specs + [block_s...  17.9 us
    ppermute x6, starting transfers between devices, halos(): return (lax.ppermute(hi, 'patch', up), lax.ppermute(lo, 'patch', down))  16.9 us
    pallas_call x3, Pallas kernels, boundary(): pl.pallas_call(body, in_specs=in_specs + [ANY], out_specs=(out_spec, out_...  13.8 us
    ppermute x9, starting transfers between devices, exchange(): lax.ppermute(value, 'patch', [(i, i ^ distance) for i in range(count)])  13.4 us
    ppermute x9, waiting for transfers between devices, exchange(): lax.ppermute(value, 'patch', [(i, i ^ distance) for i in range(count)])  12.9 us
    pallas_call x2, Pallas kernels, gram_share(): pl.pallas_call(body, in_specs=[SMEM] + [pl.BlockSpec(memory_space=pltpu.V...  3.36 us
  transfers between devices with their start and end apart: 19, of which 11 were waited for; matrix products, arithmetic and copies ran while one was open for 0% of the time, Pallas kernels for 14%

commit v1 on v0

v1 whole, which is shorter than its diff:
```python
import functools

import jax
import jax.numpy as jnp
from jax import lax
from jax.experimental import pallas as pl
from jax.experimental.pallas import tpu as pltpu
from jax.sharding import PartitionSpec as P

HALO_T = 4
STEPS = 3
ITERS = 8
GROUP = 4

SMALL = pl.CostEstimate(flops=1000, bytes_accessed=1000, transcendentals=0)
ANY = pl.BlockSpec(memory_space=pl.ANY)
SMEM = pl.BlockSpec(memory_space=pltpu.SMEM)
F32, BF16 = jnp.float32, jnp.bfloat16


def dot(a, b):
    return jnp.dot(a, b, preferred_element_type=F32)


def tile_row(blocks, listed, field):
    wide = jnp.concatenate([blocks(n) for n in range(len(listed))], axis=1)
    tall = jnp.concatenate([field(tile) for tile in listed], axis=0)
    return dot(wide, tall)


def finish(acc, prev, alive):
    value = acc if prev is None else 2.0 * acc - prev.astype(F32)
    return jnp.where(alive, value, 0.0).astype(BF16)


def rows_kernel(pieces, nnz, has_prev, cols_ref, place_ref, *refs):
    sources = refs[: len(pieces)]
    rest = list(refs[len(pieces) :])
    prev_ref = rest.pop(0) if has_prev else None
    blocks_ref, out_ref, held = rest
    for i, (source, count) in enumerate(zip(sources, pieces)):
        held[pl.ds(place_ref[2 * i + 1], count)] = source[pl.ds(place_ref[2 * i + 2], count)]
    live = place_ref[0]

    def group(index, carry):
        for r in range(GROUP):
            row = index * GROUP + r
            listed = [cols_ref[row, n] for n in range(nnz)]
            acc = tile_row(lambda n: blocks_ref[row, n], listed, lambda c: held[c])
            prev = prev_ref[row] if has_prev else None
            out_ref[row] = finish(acc, prev, row < live)
        return carry

    lax.fori_loop(0, out_ref.shape[0] // GROUP, group, 0)


def tile_rows(cols, live, blocks, window, pieces, prev, name):
    rows, nnz, tile, _ = blocks.shape
    width = pieces[0][0].shape[-1]
    numbers = [live]
    for _, begin, _, slot in pieces:
        numbers += [slot, begin]
    place = jnp.stack([jnp.asarray(number, jnp.int32) for number in numbers])
    whole = pl.BlockSpec(memory_space=pltpu.VMEM)
    args = [cols, place] + [piece[0] for piece in pieces] + ([] if prev is None else [prev])
    return pl.pallas_call(
        functools.partial(rows_kernel, [piece[2] for piece in pieces], nnz, prev is not None),
        in_specs=[SMEM, SMEM] + [whole] * (len(args) - 1),
        out_specs=whole,
        out_shape=jax.ShapeDtypeStruct((rows, tile, width), BF16),
        scratch_shapes=[pltpu.VMEM((window, tile, width), BF16)],
        compiler_params=pltpu.CompilerParams(vmem_limit_bytes=8 * 1024 * 1024),
        cost_estimate=SMALL,
        name=name,
    )(*args, blocks)


def gram_kernel(pairs, chunk, part_ref, *refs):
    fields = refs[: 2 * pairs]
    has_start = len(refs) == 2 * pairs + 4
    out_ref, square, cross = refs[-3:]
    half = square.shape[0] // 2
    square[...] = jnp.zeros(square.shape, F32)
    cross[...] = jnp.zeros(cross.shape, F32)
    is_first = part_ref[0] == 0
    across = (((0,), (0,)), ((), ()))
    for own_ref, other_ref in zip(fields[:pairs], fields[pairs:]):

        def add(index, carry):
            rows = pl.ds(pl.multiple_of(index * chunk, chunk), chunk)
            own, other = own_ref[rows, :], other_ref[rows, :]
            square[...] += lax.dot_general(own, own, across, preferred_element_type=F32)
            left = jnp.where(is_first, own[:, :half], other[:, half:])
            right = jnp.where(is_first, other, own)
            cross[...] += lax.dot_general(left, right, across, preferred_element_type=F32)
            return carry

        lax.fori_loop(0, own_ref.shape[0] // chunk, add, 0)
    blocks = [
        square[:half, :half], square[:half, half:], square[half:, half:],
        cross[:, :half], cross[:, half:],
    ]
    for i, block in enumerate(blocks):
        at = pl.ds(i * half, half)
        out_ref[at, :] = block + refs[2 * pairs][at, :] if has_start else block


def gram_share(part, owns, others, start):
    width = owns[0].shape[1]
    half = width // 2
    chunk = min(own.shape[0] for own in owns)
    body = functools.partial(gram_kernel, len(owns), chunk)
    args = [part] + list(owns) + list(others) + ([] if start is None else [start])
    return pl.pallas_call(
        body,
        in_specs=[SMEM] + [pl.BlockSpec(memory_space=pltpu.VMEM)] * (len(args) - 1),
        out_specs=pl.BlockSpec(memory_space=pltpu.VMEM),
        out_shape=jax.ShapeDtypeStruct((5 * half, half), F32),
        scratch_shapes=[pltpu.VMEM((width, width), F32), pltpu.VMEM((half, width), F32)],
        compiler_params=pltpu.CompilerParams(vmem_limit_bytes=8 * 1024 * 1024),
        cost_estimate=SMALL,
        name="gram_share",
    )(*args)


def sum_over_patch(share):
    count = lax.axis_size("patch")
    me = lax.axis_index("patch")
    ways = 4
    quarter = me % ways

    def exchange(value, distance):
        return lax.ppermute(value, "patch", [(i, i ^ distance) for i in range(count)])

    parts = share.reshape(ways, -1, share.shape[1])
    pick = lambda d: lax.dynamic_index_in_dim(parts, quarter ^ d, 0, keepdims=False)
    got = [exchange(pick(d), d) for d in range(1, ways)]
    total = (pick(0) + got[0]) + (got[1] + got[2])
    stride = ways
    while stride < count:
        got = [exchange(total, d * stride) for d in range(1, ways)]
        total = (total + got[0]) + (got[1] + got[2])
        stride *= ways
    return jnp.stack([total] + [exchange(total, d) for d in range(1, ways)])


def split(value):
    high = value.astype(BF16)
    return high, (value - high.astype(F32)).astype(BF16)


def product3(left, right_stack):
    high, low = split(left)
    return dot(jnp.concatenate([high, high, low], axis=1), right_stack)


def finish_kernel(
    total_rows, chunk, place_ref, mine_ref, theirs_ref, *refs
):
    fields, out_ref = refs[:8], refs[8]
    shares, x_ref, z_ref, m_ref, stack, wide, result, sem, out_sem = refs[9:]
    part, quarter = place_ref[0], place_ref[1]
    size = x_ref.shape[0]
    width = size // 2
    half = width // 2
    copies = []
    for i, source in enumerate(fields):
        rows = source.shape[0]
        at = pl.multiple_of(place_ref[2 + i % 4], rows // 3 if i % 4 in (1, 2) else rows)
        side = i // 4
        target = wide.at[pl.ds(at, rows), pl.ds(side * width, width)]
        copies.append(pltpu.make_async_copy(source, target, sem.at[i]))
    for copy in copies:
        copy.start()

    piece = mine_ref.shape[1]
    for d in range(4):
        rows = pl.ds(pl.multiple_of((quarter ^ d) * piece, 8), piece)
        shares[part, rows, :] = mine_ref[d]
        shares[1 - part, rows, :] = theirs_ref[d]

    def block(side, index):
        return shares[side, pl.ds(index * half, half), :]

    def place(row, col, value):
        x_ref[pl.ds(row * half, half), pl.ds(col * half, half)] = value
        if row != col:
            x_ref[pl.ds(col * half, half), pl.ds(row * half, half)] = value.T

    for side in range(2):
        place(2 * side, 2 * side, block(side, 0))
        place(2 * side, 2 * side + 1, block(side, 1))
        place(2 * side + 1, 2 * side + 1, block(side, 2))
        place(side, 2, block(side, 3))
        place(side, 3, block(side, 4))

    gram = x_ref[...]
    norm = jnp.sqrt(jnp.sum(gram * gram, keepdims=True))
    x_ref[...] = gram / norm

    def set_middle():
        x = x_ref[...]
        row = lax.broadcasted_iota(jnp.int32, x.shape, 0)
        col = lax.broadcasted_iota(jnp.int32, x.shape, 1)
        middle = jnp.where(row == col, 1.5, 0.0) - 0.5 * x
        high, low = split(middle)
        stack[0:size, :] = high
        stack[size : 2 * size, :] = low
        stack[2 * size :, :] = high
        return middle

    def step_x():
        m_ref[...] = product3(x_ref[...], stack[...])
        x_ref[...] = product3(m_ref[...], stack[...])

    z_ref[...] = set_middle()
    step_x()

    def sweep(index, carry):
        set_middle()
        z_ref[...] = product3(z_ref[...], stack[...])
        step_x()
        return carry

    lax.fori_loop(1, ITERS - 1, sweep, 0)
    set_middle()
    z_ref[...] = product3(z_ref[...], stack[...])

    own = pl.ds(pl.multiple_of(part * width, width), width)
    other = pl.ds(pl.multiple_of((1 - part) * width, width), width)
    rotation = jnp.concatenate([z_ref[own, own], z_ref[other, own]], axis=0).astype(BF16)
    factor = jnp.sqrt(total_rows / norm)
    for copy in copies:
        copy.wait()
    count = wide.shape[0] // chunk
    outs = []
    for i in range(count):
        rows = pl.ds(i * chunk, chunk)
        result[rows, :] = (dot(wide[rows, :], rotation) * factor).astype(BF16)
        outs.append(pltpu.make_async_copy(result.at[rows], out_ref.at[rows], out_sem.at[i]))
        outs[-1].start()
    for out in outs:
        out.wait()


def rotate(place, mine, theirs, owns, others, total_rows):
    width = owns[0].shape[1]
    rows = sum(own.shape[0] for own in owns)
    size = 2 * width
    chunk = min(rows, 512)
    body = functools.partial(finish_kernel, float(total_rows), chunk)
    vmem = pl.BlockSpec(memory_space=pltpu.VMEM)
    matrix = pltpu.VMEM((size, size), F32)
    return pl.pallas_call(
        body,
        in_specs=[SMEM, vmem, vmem] + [ANY] * 8,
        out_specs=ANY,
        out_shape=jax.ShapeDtypeStruct((rows, width), BF16),
        scratch_shapes=[
            pltpu.VMEM((2, 5 * width // 2, width // 2), F32),
            matrix, matrix, matrix,
            pltpu.VMEM((3 * size, size), BF16),
            pltpu.VMEM((rows, size), BF16),
            pltpu.VMEM((rows, width), BF16),
            pltpu.SemaphoreType.DMA((8,)),
            pltpu.SemaphoreType.DMA((rows // chunk,)),
        ],
        compiler_params=pltpu.CompilerParams(vmem_limit_bytes=20 * 1024 * 1024),
        cost_estimate=pl.CostEstimate(
            flops=21 * 6 * size**3 + 2 * rows * size * width,
            bytes_accessed=3 * rows * width * 2,
            transcendentals=0,
        ),
        name="rotate",
    )(place, mine, theirs, *owns, *others)


def after(value, *others):
    return lax.optimization_barrier((value, others))[0]


def on_device(vectors, blocks, tile_cols, live_tiles):
    tiles, nnz, tile, _ = blocks.shape
    width = vectors.shape[1]
    edge = HALO_T
    half = tiles // 2 - edge
    count = lax.axis_size("patch")
    part = lax.axis_index("cols")
    patch = lax.axis_index("patch")
    live = live_tiles[0]
    odd = patch % 2
    pairs = {
        "even": [(i, i ^ 1) for i in range(count)],
        "odd": [(i, ((i + 1) ^ 1) - 1) for i in range(1, count - 1)],
    }
    at_end = {"even": 1 - odd, "odd": odd}
    first_row = {name: end * (tiles - edge) for name, end in at_end.items()}
    listed = tile_cols - patch * tiles

    def exchange(name, value):
        return lax.ppermute(value, "patch", pairs[name])

    def sibling(value):
        return lax.ppermute(value, "cols", [(0, 1), (1, 0)])

    start = vectors.reshape(tiles, tile, width)
    alive = (jnp.arange(tiles, dtype=jnp.int32) < live)[:, None, None]

    def masked(begin, rows):
        part_of = lax.dynamic_slice_in_dim(start, begin, rows, 0)
        kept = lax.dynamic_slice_in_dim(alive, begin, rows, 0)
        return jnp.where(kept, part_of, jnp.zeros((), BF16))

    edge_blocks = {
        name: lax.dynamic_slice_in_dim(blocks, row, edge, 0) for name, row in first_row.items()
    }
    edge_cols = {
        name: lax.dynamic_slice_in_dim(listed, row, edge, 0) - (row - edge)
        for name, row in first_row.items()
    }
    low_blocks, high_blocks = blocks[edge : edge + half], blocks[edge + half : tiles - edge]
    low_cols = listed[edge : edge + half]
    high_cols = listed[edge + half : tiles - edge] - half

    def edge_rows(name, halo, now, low, high, prev):
        end = at_end[name]
        pieces = [
            (halo, 0, edge, 2 * edge * end),
            (now, 0, edge, edge),
            (low, 0, edge, 2 * edge + edge * end),
            (high, half - edge, edge, 3 * edge * (1 - end)),
        ]
        return tile_rows(
            edge_cols[name], live - first_row[name], edge_blocks[name], 4 * edge, pieces,
            prev, "edge_" + name,
        )

    def low_rows(even, odd_edge, low, high, prev):
        spare = half + 2 * edge
        pieces = [
            (even, 0, edge, at_end["even"] * spare),
            (odd_edge, 0, edge, at_end["odd"] * spare),
            (low, 0, half, edge),
            (high, 0, edge, edge + half),
        ]
        return tile_rows(
            low_cols, live - edge, low_blocks, spare + edge, pieces, prev, "inner_low"
        )

    def high_rows(even, odd_edge, low, high, prev):
        spare = half + 2 * edge
        last = half + edge
        pieces = [
            (even, 0, edge, spare - edge * at_end["even"]),
            (odd_edge, 0, edge, spare - edge * at_end["odd"]),
            (low, half - edge, edge, 0),
            (high, 0, half, edge),
        ]
        return tile_rows(
            high_cols, live - last, high_blocks, spare + edge, pieces, prev, "inner_high"
        )

    even = masked(first_row["even"], edge)
    even_halo = exchange("even", even)
    odd_edge = masked(first_row["odd"], edge)
    low, high = masked(edge, half), masked(edge + half, half)
    prev = (None,) * 4
    part_arg = part.astype(jnp.int32)[None]
    for step in range(STEPS):
        new_low = low_rows(even, odd_edge, low, high, prev[2])
        even_halo = after(even_halo, new_low)
        odd_halo = exchange("odd", after(odd_edge, even_halo))
        new_even = edge_rows("even", even_halo, even, low, high, prev[0])
        new_high = high_rows(even, odd_edge, low, high, prev[3])
        if step == STEPS - 1:
            flat = [value.reshape(-1, width) for value in (new_even, new_low, new_high)]
            others = [sibling(after(value, even_halo)) for value in flat[1:]]
            share = gram_share(part_arg, flat[1:], others, None)
            others.insert(0, sibling(after(flat[0], share)))
            odd_halo = after(odd_halo, new_even, new_high, share)
        else:
            odd_halo = after(odd_halo, new_even, new_high)
            next_halo = exchange("even", after(new_even, odd_halo))
        new_odd = edge_rows("odd", odd_halo, odd_edge, low, high, prev[1])
        prev = (even, odd_edge, low, high)
        even, odd_edge, low, high = new_even, new_odd, new_low, new_high
        if step < STEPS - 1:
            even_halo = next_halo
    last = odd_edge.reshape(-1, width)
    other_last = sibling(last)
    share = gram_share(part_arg, [flat[0], last], [others[0], other_last], share)
    mine = sum_over_patch(share)
    theirs = sibling(mine)
    place = jnp.stack(
        [
            part, patch % 4, first_row["even"] * tile, edge * tile * jnp.ones_like(patch),
            (edge + half) * tile * jnp.ones_like(patch), first_row["odd"] * tile,
        ]
    ).astype(jnp.int32)
    total_rows = tiles * tile * count
    return rotate(place, mine, theirs, flat + [last], others + [other_last], total_rows)


def solution(mesh):
    in_specs = (P("patch", "cols"), P("patch", None, None, None), P("patch", None), P("patch"))
    return jax.shard_map(
        on_device, mesh=mesh, in_specs=in_specs, out_specs=P("patch", "cols"), check_vma=False
    )
```

time: 134 us -> 143 us (1.067)
  local copies, waits for them, and re-layouts: 3.82 us -> 34.5 us
  waiting for transfers between devices: 37.8 us -> 17 us
  Pallas kernels: 58.1 us -> 52.3 us
  starting transfers between devices: 31 us -> 33.5 us
  other arithmetic: 1.3 us -> 3.32 us
    ppermute x6, waiting for transfers between devices: 23.3 us -> 0.02 us  [exchange(): return lax.ppermute(value, 'patch', pairs[name])]
    unnamed x11 -> x87, local copies, waits for them, and re-layouts: 1.99 us -> 22 us
    dynamic_slice x0 -> x4, local copies, waits for them, and re-layouts: none -> 5.48 us  [the longest x1 2.7 us: on_device(): lax.dynamic_slice_in_dim(blocks, row, edge, 0)]
    slice x2 -> x1, local copies, waits for them, and re-layouts: 1.14 us -> 6.59 us  [on_device(): blocks[edge + half:tiles - edge]]
    pallas_call x7 -> x13, Pallas kernels: 54.8 us -> 49.7 us  [the longest x12 26.2 us: tile_rows(): pl.pallas_call(functools.partial(rows_kernel, [piece[2] for piece in piec...]
    select_n x2, other arithmetic: 0.18 us -> 3.23 us  [masked(): return jnp.where(kept, part_of, jnp.zeros((), BF16))]
    ppermute x4 -> x5, waiting for transfers between devices: 1.55 us -> 3.06 us  [sibling(): return lax.ppermute(value, 'cols', [(0, 1), (1, 0)])]
  transfers between devices with their start and end apart: 19 -> 20, of which waited for: 11 -> 11; matrix products, arithmetic and copies ran while one was open for 0% -> 10% of each run, Pallas kernels for 14% -> 19%
where the time goes in v1:
time: 143 us; the launch traced here: 142 us
  Pallas kernels  52.3 us (37%)
  local copies, waits for them, and re-layouts  34.5 us (24%)
  starting transfers between devices  33.5 us (23%)
  waiting for transfers between devices  17 us (12%)
  other arithmetic  3.32 us (2%)
    pallas_call x12, Pallas kernels, tile_rows(): pl.pallas_call(functools.partial(rows_kernel, [piece[2] for piece in piec...  26.2 us
    pallas_call x1, Pallas kernels, rotate(): pl.pallas_call(body, in_specs=[SMEM, vmem, vmem] + [ANY] * 8, out_specs=A...  23.5 us
    unnamed x87, local copies, waits for them, and re-layouts  22 us
    ppermute x6, starting transfers between devices, exchange(): return lax.ppermute(value, 'patch', pairs[name])  17.8 us
    ppermute x9, starting transfers between devices, exchange(): lax.ppermute(value, 'patch', [(i, i ^ distance) for i in range(count)])  14.5 us
    ppermute x9, waiting for transfers between devices, exchange(): lax.ppermute(value, 'patch', [(i, i ^ distance) for i in range(count)])  14 us
    slice x1, local copies, waits for them, and re-layouts, on_device(): blocks[edge + half:tiles - edge]  6.59 us
    select_n x2, other arithmetic, masked(): return jnp.where(kept, part_of, jnp.zeros((), BF16))  3.23 us
  transfers between devices with their start and end apart: 20, of which 11 were waited for; matrix products, arithmetic and copies ran while one was open for 10% of the time, Pallas kernels for 19%

profile of v1, /device:TPU:0, one launch (start us, length us, event | category | flops | bytes accessed | tf_op | source)
XLA Modules:
  0.0 142.0 jit_solution(3004577913288237901)
XLA Ops:
  0.8 1.8 %dynamic-slice_select_fusion = (bf16[4,128,256]{2,1,0:T(8,128)(2,1)}, bf16[4,128,256]{2,1,0:T(8,128)(2,1)S(1)}) fusion(bf16[32,128,256]{2,1,0:T(8,128)(2,1)} %bitcast.56, s32[]{:T(128)S(6)} %select_n.56, pred[4]{0:T(512)(128)(4,1)S(1)} %get-tuple-element.50, s32[]{:T(128)S(6)} %select_n.54, pred[4]{0:T(512)(128)(4,1)S(1)} %get-tuple-element.51), kind=kLoop, calls=%fused_computation.3 | loop fusion | flops 262144 | bytes 1048592 | tf_op jit(solution)/shard_map/jit(_where)/select_n | solution.py:312
  2.6 2.9 %collective-permute-start = (bf16[4,128,256]{2,1,0:T(8,128)(2,1)S(1)}, bf16[4,128,256]{2,1,0:T(8,128)(2,1)}, u32[]{:S(2)}, u32[]{:S(2)}) collective-permute-start(bf16[4,128,256]{2,1,0:T(8,128)(2,1)S(1)} %get-tuple-element.40.refs_0_.refs_1_.refs_4_), channel_id=1, source_target_pairs={{0,1},{1,0},{2,3},{3,2},{4,5},{5,4},{6,7},{7,6},{8,9},{9,8},{10,11... | collective-permute-start | bytes 786440 | tf_op jit(solution)/shard_map/ppermute | solution.py:301
  5.6 2.6 %fusion.4 = (bf16[1536,256]{1,0:T(8,128)(2,1)}, bf16[1536,256]{1,0:T(8,128)(2,1)}) fusion(bf16[4096,256]{1,0:T(8,128)(2,1)} %param.4), kind=kLoop, calls=%fused_computation.21 | loop fusion | bytes 3145728 | tf_op jit(solution)/shard_map/dynamic_slice | solution.py:310
  8.3 6.6 %fusion.3 = (bf16[12,8,128,128]{3,2,1,0:T(8,128)(2,1)S(1)}, bf16[12,8,128,128]{3,2,1,0:T(8,128)(2,1)}) fusion(bf16[32,8,128,128]{3,2,1,0:T(8,128)(2,1)} %param.5), kind=kLoop, calls=%fused_computation.20 | loop fusion | bytes 12582912 | tf_op jit(solution)/shard_map/slice | solution.py:321
  14.9 1.4 broadcast_select_fusion
  16.4 1.9 %copy-done = bf16[12,8,128,128]{3,2,1,0:T(8,128)(2,1)S(1)} copy-done((bf16[12,8,128,128]{3,2,1,0:T(8,128)(2,1)S(1)}, bf16[12,8,128,128]{3,2,1,0:T(8,128)(2,1)}, u32[]{:S(2)}) %copy-start) | copy-done | bytes 3145752
  18.3 1.1 copy-done.2
  19.4 1.1 copy-done.10
  20.6 2.5 %inner_low.3.refs_2_.refs_4_ = bf16[12,128,256]{2,1,0:T(8,128)(2,1)S(1)} custom-call(s32[12,8]{1,0:T(8,128)S(1)} %get-tuple-element.47.cols_ref, s32[9]{0:T(128)S(1)} %stack.133.place_ref, bf16[4,128,256]{2,1,0:T(8,128)(2,1)S(1)} %get-tuple-element.40.refs_0_.refs_1_.refs_4_, bf16[4,128,256]{2,1,0:T(8,128)(2,1)} %get-tuple-element.20.refs_1_.refs_4_, ...), custom_call_target="tpu_custom_call" | custom-call | flops 1000 | bytes 1000 | tf_op jit(solution)/shard_map/inner_low/pallas_call | solution.py:66
  23.1 0.9 copy-done.7
  24.1 1.1 copy-done.3
  25.2 1.1 copy-done.11
  26.3 2.5 %inner_high.3.refs_3_.refs_4_ = bf16[12,128,256]{2,1,0:T(8,128)(2,1)S(1)} custom-call(s32[12,8]{1,0:T(8,128)S(1)} %get-tuple-element.46.cols_ref, s32[9]{0:T(128)S(1)} %stack.137.place_ref, bf16[4,128,256]{2,1,0:T(8,128)(2,1)S(1)} %get-tuple-element.40.refs_0_.refs_1_.refs_4_, bf16[4,128,256]{2,1,0:T(8,128)(2,1)} %get-tuple-element.20.refs_1_.refs_4_, ...), custom_call_target="tpu_custom_call" | custom-call | flops 1000 | bytes 1000 | tf_op jit(solution)/shard_map/inner_high/pallas_call | solution.py:66
  28.8 0.9 copy-done.14
  29.8 0.8 collective-permute-start.1
  30.7 2.7 %constant_dynamic-slice_fusion = (bf16[4,8,128,128]{3,2,1,0:T(8,128)(2,1)}, bf16[4,8,128,128]{3,2,1,0:T(8,128)(2,1)S(1)}) fusion(bf16[32,8,128,128]{3,2,1,0:T(8,128)(2,1)} %param.5, s32[]{:T(128)S(6)} %select_n.56, s32[]{:T(128)S(6)} %select_n.54), kind=kLoop, calls=%fused_computation.13 | loop fusion | bytes 4194312 | tf_op jit(solution)/shard_map/dynamic_slice | solution.py:315
  33.4 1.7 %edge_even.3.refs_0_.refs_1_.refs_4_ = bf16[4,128,256]{2,1,0:T(8,128)(2,1)S(1)} custom-call(s32[4,8]{1,0:T(4,128)S(1)} %get-tuple-element.45.cols_ref, s32[9]{0:T(128)S(1)} %stack.129.place_ref, bf16[4,128,256]{2,1,0:T(8,128)(2,1)} %collective-permute-done.refs_0_, bf16[4,128,256]{2,1,0:T(8,128)(2,1)S(1)} %copy-done.32, ...), custom_call_target="tpu_custom_call" | custom-call | flops 1000 | bytes 1000 | tf_op jit(solution)/shard_map/edge_even/pallas_call | solution.py:66
  35.2 0.7 copy-done.38
  35.9 5.9 %collective-permute-start.2 = (bf16[4,128,256]{2,1,0:T(8,128)(2,1)S(1)}, bf16[4,128,256]{2,1,0:T(8,128)(2,1)}, u32[]{:S(2)}, u32[]{:S(2)}) collective-permute-start(bf16[4,128,256]{2,1,0:T(8,128)(2,1)S(1)} %edge_even.3.refs_0_.refs_1_.refs_4_), channel_id=1, source_target_pairs={{0,1},{1,0},{2,3},{3,2},{4,5},{5,4},{6,7},{7,6},{8,9},{9,8},{10,11... | collective-permute-start | bytes 786440 | tf_op jit(solution)/shard_map/ppermute | solution.py:301
  41.9 1.3 copy-done.5
  43.2 1.1 copy-done.13
  44.3 1.2 copy-done.23
  45.5 0.9 copy-done.39
  46.5 1.5 %edge_odd.3.refs_1_.refs_4_ = bf16[4,128,256]{2,1,0:T(8,128)(2,1)S(1)} custom-call(s32[4,8]{1,0:T(4,128)S(1)} %get-tuple-element.44.cols_ref, s32[9]{0:T(128)S(1)} %stack.142.place_ref, bf16[4,128,256]{2,1,0:T(8,128)(2,1)S(1)} %copy-done.39, bf16[4,128,256]{2,1,0:T(8,128)(2,1)} %get-tuple-element.20.refs_1_.refs_4_, bf16[12,128,256]{2,1,0:T(8,128)(2,1)S(1)} %copy-done.13, ...), custom_call_target="tpu_custom_call" | custom-call | flops 1000 | bytes 1000 | tf_op jit(solution)/shard_map/edge_odd/pallas_call | solution.py:66
  48.1 1.1 copy-done.8
  49.2 1.1 copy-done.15
  50.3 2.2 %inner_low.4.refs_2_ = bf16[12,128,256]{2,1,0:T(8,128)(2,1)S(1)} custom-call(s32[12,8]{1,0:T(8,128)S(1)} %get-tuple-element.47.cols_ref, s32[9]{0:T(128)S(1)} %stack.133.place_ref, bf16[4,128,256]{2,1,0:T(8,128)(2,1)S(1)} %edge_even.3.refs_0_.refs_1_.refs_4_, bf16[4,128,256]{2,1,0:T(8,128)(2,1)S(1)} %edge_odd.3.refs_1_.refs_4_, ...), custom_call_target="tpu_custom_call" | custom-call | flops 1000 | bytes 1000 | tf_op jit(solution)/shard_map/inner_low/pallas_call | solution.py:66
  52.6 0.8 collective-permute-start.3
  53.4 2.2 %inner_high.4.refs_3_ = bf16[12,128,256]{2,1,0:T(8,128)(2,1)S(1)} custom-call(s32[12,8]{1,0:T(8,128)S(1)} %get-tuple-element.46.cols_ref, s32[9]{0:T(128)S(1)} %stack.137.place_ref, bf16[4,128,256]{2,1,0:T(8,128)(2,1)S(1)} %edge_even.3.refs_0_.refs_1_.refs_4_, bf16[4,128,256]{2,1,0:T(8,128)(2,1)S(1)} %edge_odd.3.refs_1_.refs_4_, ...), custom_call_target="tpu_custom_call" | custom-call | flops 1000 | bytes 1000 | tf_op jit(solution)/shard_map/inner_high/pallas_call | solution.py:66
  55.7 1.8 %edge_even.4.refs_0_.refs_1_ = bf16[4,128,256]{2,1,0:T(8,128)(2,1)S(1)} custom-call(s32[4,8]{1,0:T(4,128)S(1)} %get-tuple-element.45.cols_ref, s32[9]{0:T(128)S(1)} %stack.129.place_ref, bf16[4,128,256]{2,1,0:T(8,128)(2,1)} %collective-permute-done.2.refs_0_, bf16[4,128,256]{2,1,0:T(8,128)(2,1)S(1)} %edge_even.3.refs_0_.refs_1_.refs_4_, ...), custom_call_target="tpu_custom_call" | custom-call | flops 1000 | bytes 1000 | tf_op jit(solution)/shard_map/edge_even/pallas_call | solution.py:66
  57.5 6.5 %collective-permute-start.4 = (bf16[4,128,256]{2,1,0:T(8,128)(2,1)S(1)}, bf16[4,128,256]{2,1,0:T(8,128)(2,1)S(1)}, u32[]{:S(2)}, u32[]{:S(2)}) collective-permute-start(bf16[4,128,256]{2,1,0:T(8,128)(2,1)S(1)} %edge_even.4.refs_0_.refs_1_), channel_id=1, source_target_pairs={{0,1},{1,0},{2,3},{3,2},{4,5},{5,4},{6,7},{7,6},{8,9},{9,8},{10,11... | collective-permute-start | bytes 786440 | tf_op jit(solution)/shard_map/ppermute | solution.py:301
  64.0 2.2 %edge_odd.4.refs_1_ = bf16[4,128,256]{2,1,0:T(8,128)(2,1)} custom-call(s32[4,8]{1,0:T(4,128)S(1)} %get-tuple-element.44.cols_ref, s32[9]{0:T(128)S(1)} %stack.142.place_ref, bf16[4,128,256]{2,1,0:T(8,128)(2,1)S(1)} %collective-permute-done.3.refs_0_, bf16[4,128,256]{2,1,0:T(8,128)(2,1)S(1)} %edge_odd.3.refs_1_.refs_4_, bf16[12,128,256]{2,1,0:T(8,128)(2,1)S(1)} %copy-done.9, ...), custom_call_target="tpu_custom_call" | custom-call | flops 1000 | bytes 1000 | tf_op jit(solution)/shard_map/edge_odd/pallas_call | solution.py:66
  66.2 3.4 %inner_low.5 = bf16[12,128,256]{2,1,0:T(8,128)(2,1)} custom-call(s32[12,8]{1,0:T(8,128)S(1)} %get-tuple-element.47.cols_ref, s32[9]{0:T(128)S(1)} %stack.133.place_ref, bf16[4,128,256]{2,1,0:T(8,128)(2,1)S(1)} %edge_even.4.refs_0_.refs_1_, bf16[4,128,256]{2,1,0:T(8,128)(2,1)} %edge_odd.4.refs_1_, bf16[12,128,256]{2,1,0:T(8,128)(2,1)S(1)} %inner_low.4.refs_2_, ...), custom_call_target="tpu_custom_call" | custom-call | flops 1000 | bytes 1000 | tf_op jit(solution)/shard_map/inner_low/pallas_call | solution.py:66
  69.6 3.4 %inner_high.5 = bf16[12,128,256]{2,1,0:T(8,128)(2,1)} custom-call(s32[12,8]{1,0:T(8,128)S(1)} %get-tuple-element.46.cols_ref, s32[9]{0:T(128)S(1)} %stack.137.place_ref, bf16[4,128,256]{2,1,0:T(8,128)(2,1)S(1)} %edge_even.4.refs_0_.refs_1_, bf16[4,128,256]{2,1,0:T(8,128)(2,1)} %edge_odd.4.refs_1_, bf16[12,128,256]{2,1,0:T(8,128)(2,1)S(1)} %inner_low.4.refs_2_, ...), custom_call_target="tpu_custom_call" | custom-call | flops 1000 | bytes 1000 | tf_op jit(solution)/shard_map/inner_high/pallas_call | solution.py:66
  73.0 0.7 copy-done.36
  73.8 0.5 collective-permute-start.7
  74.3 0.8 collective-permute-start.5
  75.1 1.1 copy-done.18
  76.3 1.1 copy-done.21
  77.4 1.2 copy-done.28
  78.6 0.9 copy-done.35
  79.6 0.9 copy-done.37
  80.5 1.2 edge_even.5
  81.7 2.2 %gram_share.2.refs_4_ = f32[640,128]{1,0:T(8,128)S(1)} custom-call(s32[1]{0:T(128)} %bitcast.part_ref, bf16[1536,256]{1,0:T(8,128)(2,1)} %bitcast.23.refs_0_.refs_1_, bf16[1536,256]{1,0:T(8,128)(2,1)} %bitcast.24.refs_1_.refs_2_, bf16[1536,256]{1,0:T(8,128)(2,1)S(1)} %collective-permute-done.6.refs_2_.refs_5_, ...), custom_call_target="tpu_custom_call" | custom-call | flops 1000 | bytes 1000 | tf_op jit(solution)/shard_map/gram_share/pallas_call | solution.py:114
  84.0 1.6 %edge_odd.5 = bf16[4,128,256]{2,1,0:T(8,128)(2,1)S(1)} custom-call(s32[4,8]{1,0:T(4,128)S(1)} %get-tuple-element.44.cols_ref, s32[9]{0:T(128)S(1)} %stack.142.place_ref, bf16[4,128,256]{2,1,0:T(8,128)(2,1)S(1)} %collective-permute-done.5.refs_0_, bf16[4,128,256]{2,1,0:T(8,128)(2,1)} %edge_odd.4.refs_1_, bf16[12,128,256]{2,1,0:T(8,128)(2,1)S(1)} %copy-done.19, ...), custom_call_target="tpu_custom_call" | custom-call | flops 1000 | bytes 1000 | tf_op jit(solution)/shard_map/edge_odd/pallas_call | solution.py:66
  85.6 0.5 collective-permute-start.9
  86.1 1.0 collective-permute-done.8.refs_2_.refs_4_
  87.1 0.4 collective-permute-done.9.refs_3_.refs_7_
  87.5 0.4 gram_share.3
  87.9 5.1 %collective-permute-start.10 = (f32[160,128]{1,0:T(8,128)S(1)}, f32[160,128]{1,0:T(8,128)S(1)}, u32[]{:S(2)}, u32[]{:S(2)}) collective-permute-start(f32[160,128]{1,0:T(8,128)S(1)} %get-tuple-element.43), channel_id=1, source_target_pairs={{0,1},{1,0},{2,3},{3,2},{4,5},{5,4},{6,7},{7,6},{8,9},{9,8},{10,11... | collective-permute-start | bytes 245768 | tf_op jit(solution)/shard_map/ppermute | solution.py:133
  93.1 1.5 %collective-permute-start.11 = (f32[160,128]{1,0:T(8,128)S(1)}, f32[160,128]{1,0:T(8,128)S(1)}, u32[]{:S(2)}, u32[]{:S(2)}) collective-permute-start(f32[160,128]{1,0:T(8,128)S(1)} %get-tuple-element.42), channel_id=1, source_target_pairs={{0,2},{1,3},{2,0},{3,1},{4,6},{5,7},{6,4},{7,5},{8,10},{9,11},{10,... | collective-permute-start | bytes 245768 | tf_op jit(solution)/shard_map/ppermute | solution.py:133
  94.6 1.2 collective-permute-done.10
  95.8 2.5 %collective-permute-done.11 = f32[160,128]{1,0:T(8,128)S(1)} collective-permute-done((f32[160,128]{1,0:T(8,128)S(1)}, f32[160,128]{1,0:T(8,128)S(1)}, u32[]{:S(2)}, u32[]{:S(2)}) %collective-permute-start.11) | collective-permute-done | bytes 81952 | tf_op jit(solution)/shard_map/ppermute | solution.py:133
  98.3 1.6 %collective-permute-done.12 = f32[160,128]{1,0:T(8,128)S(1)} collective-permute-done((f32[160,128]{1,0:T(8,128)S(1)}, f32[160,128]{1,0:T(8,128)S(1)}, u32[]{:S(2)}, u32[]{:S(2)}) %collective-permute-start.12) | collective-permute-done | bytes 81952 | tf_op jit(solution)/shard_map/ppermute | solution.py:133
  100.0 3.7 %collective-permute-start.14 = (f32[160,128]{1,0:T(8,128)S(1)}, f32[160,128]{1,0:T(8,128)S(1)}, u32[]{:S(2)}, u32[]{:S(2)}) collective-permute-start(f32[160,128]{1,0:T(8,128)S(1)} %fusion), channel_id=1, source_target_pairs={{0,8},{1,9},{2,10},{3,11},{4,12},{5,13},{6,14},{7,15},{8,0},{9,1},... | collective-permute-start | bytes 245768 | tf_op jit(solution)/shard_map/ppermute | solution.py:133
  104.3 4.0 %collective-permute-done.14 = f32[160,128]{1,0:T(8,128)S(1)} collective-permute-done((f32[160,128]{1,0:T(8,128)S(1)}, f32[160,128]{1,0:T(8,128)S(1)}, u32[]{:S(2)}, u32[]{:S(2)}) %collective-permute-start.14) | collective-permute-done | bytes 81952 | tf_op jit(solution)/shard_map/ppermute | solution.py:133
  108.3 1.6 %collective-permute-done.15 = f32[160,128]{1,0:T(8,128)S(1)} collective-permute-done((f32[160,128]{1,0:T(8,128)S(1)}, f32[160,128]{1,0:T(8,128)S(1)}, u32[]{:S(2)}, u32[]{:S(2)}) %collective-permute-start.15) | collective-permute-done | bytes 81952 | tf_op jit(solution)/shard_map/ppermute | solution.py:133
  109.9 0.9 collective-permute-start.18
  110.8 1.2 collective-permute-start.17
  112.0 1.5 %collective-permute-start.16 = (f32[160,128]{1,0:T(8,128)S(1)}, f32[160,128]{1,0:T(8,128)S(1)}, u32[]{:S(2)}, u32[]{:S(2)}) collective-permute-start(f32[160,128]{1,0:T(8,128)S(1)} %add_add_fusion), channel_id=1, source_target_pairs={{0,1},{1,0},{2,3},{3,2},{4,5},{5,4},{6,7},{7,6},{8,9},{9,8},{10,11... | collective-permute-start | bytes 245768 | tf_op jit(solution)/shard_map/ppermute | solution.py:133
  113.5 2.0 %collective-permute-done.18 = f32[160,128]{1,0:T(8,128)S(1)} collective-permute-done((f32[160,128]{1,0:T(8,128)S(1)}, f32[160,128]{1,0:T(8,128)S(1)}, u32[]{:S(2)}, u32[]{:S(2)}) %collective-permute-start.18) | collective-permute-done | bytes 81952 | tf_op jit(solution)/shard_map/ppermute | solution.py:133
  115.4 0.7 collective-permute-done.17
  116.7 1.7 %collective-permute-done.19.theirs_ref = f32[4,160,128]{2,1,0:T(8,128)} collective-permute-done((f32[4,160,128]{2,1,0:T(8,128)S(1)}, f32[4,160,128]{2,1,0:T(8,128)}, u32[]{:S(2)}, u32[]{:S(2)}) %collective-permute-start.19) | collective-permute-done | bytes 327712 | tf_op jit(solution)/shard_map/ppermute | solution.py:304
  118.3 23.5 %rotate.1 = bf16[4096,256]{1,0:T(8,128)(2,1)} custom-call(s32[6]{0:T(128)S(1)} %stack.60.place_ref, f32[4,160,128]{2,1,0:T(8,128)S(1)} %pad_maximum_fusion.mine_ref, f32[4,160,128]{2,1,0:T(8,128)} %collective-permute-done.19.theirs_ref, bf16[512,256]{1,0:T(8,128)(2,1)S(1)} %bitcast.50, bf16[1536,256]{1,0:T(8,128)(2,1)} %bitcast.23.refs_0_.refs_1_, ...), custom_call_target="tpu_custom_call" | custom-call | flops 17985175552 | bytes 6291456 | tf_op jit(solution)/shard_map/rotate/pallas_call | solution.py:254
  (99 shorter events, 2.0 us)
Async XLA Ops:
  0.0 8.3 %copy-start.42 = (s32[32,8]{0,1:T(8,128)S(1)}, s32[32,8]{0,1:T(8,128)}, u32[]{:S(2)}) copy-start(s32[32,8]{0,1:T(8,128)} %param.6) | copy-start | bytes 3076
  2.6 21.4 %copy-start.31 = (bf16[4,128,256]{2,1,0:T(8,128)(2,1)}, bf16[4,128,256]{2,1,0:T(8,128)(2,1)S(1)}, u32[]{:S(2)}) copy-start(bf16[4,128,256]{2,1,0:T(8,128)(2,1)S(1)} %get-tuple-element.40.refs_0_.refs_1_.refs_4_) | copy-start | bytes 786436
  2.6 27.2 %collective-permute-start = (bf16[4,128,256]{2,1,0:T(8,128)(2,1)S(1)}, bf16[4,128,256]{2,1,0:T(8,128)(2,1)}, u32[]{:S(2)}, u32[]{:S(2)}) collective-permute-start(bf16[4,128,256]{2,1,0:T(8,128)(2,1)S(1)} %get-tuple-element.40.refs_0_.refs_1_.refs_4_), channel_id=1, source_target_pairs={{0,1},{1,0},{2,3},{3,2},{4,5},{5,4},{6,7},{7,6},{8,9},{9,8},{10,11... | collective-permute-start | bytes 786440 | tf_op jit(solution)/shard_map/ppermute | solution.py:301
  8.3 6.6 %copy-start.40 = (bf16[1536,256]{1,0:T(8,128)(2,1)S(1)}, bf16[1536,256]{1,0:T(8,128)(2,1)}, u32[]{:S(2)}) copy-start(bf16[1536,256]{1,0:T(8,128)(2,1)} %get-tuple-element.37) | copy-start | bytes 2359300
  8.3 6.6 %copy-start.41 = (bf16[1536,256]{1,0:T(8,128)(2,1)S(1)}, bf16[1536,256]{1,0:T(8,128)(2,1)}, u32[]{:S(2)}) copy-start(bf16[1536,256]{1,0:T(8,128)(2,1)} %get-tuple-element.38) | copy-start | bytes 2359300
  16.4 1.9 %copy-start = (bf16[12,8,128,128]{3,2,1,0:T(8,128)(2,1)S(1)}, bf16[12,8,128,128]{3,2,1,0:T(8,128)(2,1)}, u32[]{:S(2)}) copy-start(bf16[12,8,128,128]{3,2,1,0:T(8,128)(2,1)} %get-tuple-element.36.refs_4_.refs_5_) | copy-start | bytes 9437188
  18.3 1.1 copy-start.2
  19.4 1.1 copy-start.10
  23.1 0.9 copy-start.7
  24.0 1.1 copy-start.3
  25.2 1.1 copy-start.11
  28.8 0.9 copy-start.14
  29.8 3.6 %copy-start.4 = (bf16[12,128,256]{2,1,0:T(8,128)(2,1)S(1)}, bf16[12,128,256]{2,1,0:T(8,128)(2,1)}, u32[]{:S(2)}) copy-start(bf16[12,128,256]{2,1,0:T(8,128)(2,1)} %get-tuple-element.52.refs_3_.refs_4_) | copy-start | bytes 2359300
  29.8 3.6 %copy-start.12 = (bf16[12,128,256]{2,1,0:T(8,128)(2,1)S(1)}, bf16[12,128,256]{2,1,0:T(8,128)(2,1)}, u32[]{:S(2)}) copy-start(bf16[12,128,256]{2,1,0:T(8,128)(2,1)} %get-tuple-element.53.refs_2_.refs_4_) | copy-start | bytes 2359300
  29.8 3.6 %copy-start.32 = (bf16[4,128,256]{2,1,0:T(8,128)(2,1)S(1)}, bf16[4,128,256]{2,1,0:T(8,128)(2,1)}, u32[]{:S(2)}) copy-start(bf16[4,128,256]{2,1,0:T(8,128)(2,1)} %copy-done.31) | copy-start | bytes 786436
  29.8 5.3 %collective-permute-start.1 = (bf16[4,128,256]{2,1,0:T(8,128)(2,1)}, bf16[4,128,256]{2,1,0:T(8,128)(2,1)S(1)}, u32[]{:S(2)}, u32[]{:S(2)}) collective-permute-start(bf16[4,128,256]{2,1,0:T(8,128)(2,1)} %get-tuple-element.20.refs_1_.refs_4_), channel_id=1, source_target_pairs={{1,2},{2,1},{3,4},{4,3},{5,6},{6,5},{7,8},{8,7},{9,10},{10,9},{11,... | collective-permute-start | bytes 786440 | tf_op jit(solution)/shard_map/ppermute | solution.py:301
  33.4 1.8 %copy-start.26 = (bf16[4,8,128,128]{3,2,1,0:T(8,128)(2,1)}, bf16[4,8,128,128]{3,2,1,0:T(8,128)(2,1)S(1)}, u32[]{:S(2)}) copy-start(bf16[4,8,128,128]{3,2,1,0:T(8,128)(2,1)S(1)} %get-tuple-element.34.refs_4_.refs_5_) | copy-start | bytes 3145732
  35.2 0.7 copy-start.38
  35.9 16.7 %collective-permute-start.2 = (bf16[4,128,256]{2,1,0:T(8,128)(2,1)S(1)}, bf16[4,128,256]{2,1,0:T(8,128)(2,1)}, u32[]{:S(2)}, u32[]{:S(2)}) collective-permute-start(bf16[4,128,256]{2,1,0:T(8,128)(2,1)S(1)} %edge_even.3.refs_0_.refs_1_.refs_4_), channel_id=1, source_target_pairs={{0,1},{1,0},{2,3},{3,2},{4,5},{5,4},{6,7},{7,6},{8,9},{9,8},{10,11... | collective-permute-start | bytes 786440 | tf_op jit(solution)/shard_map/ppermute | solution.py:301
  41.9 6.1 %copy-start.1 = (bf16[12,8,128,128]{3,2,1,0:T(8,128)(2,1)S(1)}, bf16[12,8,128,128]{3,2,1,0:T(8,128)(2,1)}, u32[]{:S(2)}) copy-start(bf16[12,8,128,128]{3,2,1,0:T(8,128)(2,1)} %get-tuple-element.36.refs_4_.refs_5_) | copy-start | bytes 9437188
  41.9 1.3 copy-start.5
  43.2 1.1 copy-start.13
  44.3 1.2 copy-start.23
  45.5 0.9 copy-start.39
  48.0 1.1 copy-start.8
  49.2 1.1 copy-start.15
  50.3 13.6 %copy-start.29 = (bf16[4,128,256]{2,1,0:T(8,128)(2,1)}, bf16[4,128,256]{2,1,0:T(8,128)(2,1)S(1)}, u32[]{:S(2)}) copy-start(bf16[4,128,256]{2,1,0:T(8,128)(2,1)S(1)} %edge_odd.3.refs_1_.refs_4_) | copy-start | bytes 786436
  50.3 3.1 %copy-start.6 = (bf16[12,128,256]{2,1,0:T(8,128)(2,1)S(1)}, bf16[12,128,256]{2,1,0:T(8,128)(2,1)}, u32[]{:S(2)}) copy-start(bf16[12,128,256]{2,1,0:T(8,128)(2,1)} %get-tuple-element.52.refs_3_.refs_4_) | copy-start | bytes 2359300
  50.3 3.1 %copy-start.9 = (bf16[12,128,256]{2,1,0:T(8,128)(2,1)S(1)}, bf16[12,128,256]{2,1,0:T(8,128)(2,1)}, u32[]{:S(2)}) copy-start(bf16[12,128,256]{2,1,0:T(8,128)(2,1)} %copy-done.7) | copy-start | bytes 2359300
  52.5 17.1 %copy-start.17 = (bf16[12,128,256]{2,1,0:T(8,128)(2,1)}, bf16[12,128,256]{2,1,0:T(8,128)(2,1)S(1)}, u32[]{:S(2)}) copy-start(bf16[12,128,256]{2,1,0:T(8,128)(2,1)S(1)} %inner_low.4.refs_2_) | copy-start | bytes 2359300
  52.6 3.1 %copy-start.16 = (bf16[12,128,256]{2,1,0:T(8,128)(2,1)S(1)}, bf16[12,128,256]{2,1,0:T(8,128)(2,1)}, u32[]{:S(2)}) copy-start(bf16[12,128,256]{2,1,0:T(8,128)(2,1)} %copy-done.14) | copy-start | bytes 2359300
  52.6 3.1 %copy-start.27 = (bf16[4,8,128,128]{3,2,1,0:T(8,128)(2,1)S(1)}, bf16[4,8,128,128]{3,2,1,0:T(8,128)(2,1)}, u32[]{:S(2)}) copy-start(bf16[4,8,128,128]{3,2,1,0:T(8,128)(2,1)} %copy-done.26) | copy-start | bytes 3145732
  52.6 3.1 %copy-start.33 = (bf16[4,128,256]{2,1,0:T(8,128)(2,1)S(1)}, bf16[4,128,256]{2,1,0:T(8,128)(2,1)}, u32[]{:S(2)}) copy-start(bf16[4,128,256]{2,1,0:T(8,128)(2,1)} %copy-done.31) | copy-start | bytes 786436
  52.6 4.9 %collective-permute-start.3 = (bf16[4,128,256]{2,1,0:T(8,128)(2,1)S(1)}, bf16[4,128,256]{2,1,0:T(8,128)(2,1)S(1)}, u32[]{:S(2)}, u32[]{:S(2)}) collective-permute-start(bf16[4,128,256]{2,1,0:T(8,128)(2,1)S(1)} %edge_odd.3.refs_1_.refs_4_), channel_id=1, source_target_pairs={{1,2},{2,1},{3,4},{4,3},{5,6},{6,5},{7,8},{8,7},{9,10},{10,9},{11,... | collective-permute-start | bytes 786440 | tf_op jit(solution)/shard_map/ppermute | solution.py:301
  55.6 14.0 %copy-start.20 = (bf16[12,128,256]{2,1,0:T(8,128)(2,1)}, bf16[12,128,256]{2,1,0:T(8,128)(2,1)S(1)}, u32[]{:S(2)}) copy-start(bf16[12,128,256]{2,1,0:T(8,128)(2,1)S(1)} %inner_high.4.refs_3_) | copy-start | bytes 2359300
  55.7 8.3 %copy-start.24 = (bf16[4,8,128,128]{3,2,1,0:T(8,128)(2,1)S(1)}, bf16[4,8,128,128]{3,2,1,0:T(8,128)(2,1)}, u32[]{:S(2)}) copy-start(bf16[4,8,128,128]{3,2,1,0:T(8,128)(2,1)} %get-tuple-element.33.refs_4_.refs_5_) | copy-start | bytes 3145732
  57.5 12.2 %copy-start.34 = (bf16[4,128,256]{2,1,0:T(8,128)(2,1)}, bf16[4,128,256]{2,1,0:T(8,128)(2,1)S(1)}, u32[]{:S(2)}) copy-start(bf16[4,128,256]{2,1,0:T(8,128)(2,1)S(1)} %edge_even.4.refs_0_.refs_1_) | copy-start | bytes 786436
  57.5 15.6 %collective-permute-start.4 = (bf16[4,128,256]{2,1,0:T(8,128)(2,1)S(1)}, bf16[4,128,256]{2,1,0:T(8,128)(2,1)S(1)}, u32[]{:S(2)}, u32[]{:S(2)}) collective-permute-start(bf16[4,128,256]{2,1,0:T(8,128)(2,1)S(1)} %edge_even.4.refs_0_.refs_1_), channel_id=1, source_target_pairs={{0,1},{1,0},{2,3},{3,2},{4,5},{5,4},{6,7},{7,6},{8,9},{9,8},{10,11... | collective-permute-start | bytes 786440 | tf_op jit(solution)/shard_map/ppermute | solution.py:301
  73.0 0.7 copy-start.36
  73.8 7.9 %collective-permute-start.6 = (bf16[1536,256]{1,0:T(8,128)(2,1)}, bf16[1536,256]{1,0:T(8,128)(2,1)S(1)}, u32[]{:S(2)}, u32[]{:S(2)}) collective-permute-start(bf16[1536,256]{1,0:T(8,128)(2,1)} %bitcast.23.refs_0_.refs_1_), channel_id=1, source_target_pairs={{0,16},{16,0},{1,17},{17,1},{2,18},{18,2},{3,19},{19,3},{4,20},{20... | collective-permute-start | bytes 2359304 | tf_op jit(solution)/shard_map/ppermute | solution.py:304
  73.8 8.0 %collective-permute-start.7 = (bf16[1536,256]{1,0:T(8,128)(2,1)}, bf16[1536,256]{1,0:T(8,128)(2,1)S(1)}, u32[]{:S(2)}, u32[]{:S(2)}) collective-permute-start(bf16[1536,256]{1,0:T(8,128)(2,1)} %bitcast.24.refs_1_.refs_2_), channel_id=1, source_target_pairs={{0,16},{16,0},{1,17},{17,1},{2,18},{18,2},{3,19},{19,3},{4,20},{20... | collective-permute-start | bytes 2359304 | tf_op jit(solution)/shard_map/ppermute | solution.py:304
  74.3 9.6 %collective-permute-start.5 = (bf16[4,128,256]{2,1,0:T(8,128)(2,1)}, bf16[4,128,256]{2,1,0:T(8,128)(2,1)S(1)}, u32[]{:S(2)}, u32[]{:S(2)}) collective-permute-start(bf16[4,128,256]{2,1,0:T(8,128)(2,1)} %edge_odd.4.refs_1_), channel_id=1, source_target_pairs={{1,2},{2,1},{3,4},{4,3},{5,6},{6,5},{7,8},{8,7},{9,10},{10,9},{11,... | collective-permute-start | bytes 786440 | tf_op jit(solution)/shard_map/ppermute | solution.py:301
  75.1 1.1 copy-start.18
  76.3 1.1 copy-start.21
  77.4 1.2 copy-start.28
  78.6 0.9 copy-start.35
  79.6 0.9 copy-start.37
  80.5 3.4 %copy-start.19 = (bf16[12,128,256]{2,1,0:T(8,128)(2,1)S(1)}, bf16[12,128,256]{2,1,0:T(8,128)(2,1)}, u32[]{:S(2)}) copy-start(bf16[12,128,256]{2,1,0:T(8,128)(2,1)} %copy-done.17) | copy-start | bytes 2359300
  80.5 3.4 %copy-start.22 = (bf16[12,128,256]{2,1,0:T(8,128)(2,1)S(1)}, bf16[12,128,256]{2,1,0:T(8,128)(2,1)}, u32[]{:S(2)}) copy-start(bf16[12,128,256]{2,1,0:T(8,128)(2,1)} %copy-done.20) | copy-start | bytes 2359300
  80.5 3.4 %copy-start.25 = (bf16[4,8,128,128]{3,2,1,0:T(8,128)(2,1)S(1)}, bf16[4,8,128,128]{3,2,1,0:T(8,128)(2,1)}, u32[]{:S(2)}) copy-start(bf16[4,8,128,128]{3,2,1,0:T(8,128)(2,1)} %get-tuple-element.33.refs_4_.refs_5_) | copy-start | bytes 3145732
  80.5 3.4 %copy-start.30 = (bf16[4,128,256]{2,1,0:T(8,128)(2,1)S(1)}, bf16[4,128,256]{2,1,0:T(8,128)(2,1)}, u32[]{:S(2)}) copy-start(bf16[4,128,256]{2,1,0:T(8,128)(2,1)} %copy-done.29) | copy-start | bytes 786436
  85.5 1.6 %collective-permute-start.8 = (bf16[512,256]{1,0:T(8,128)(2,1)S(1)}, bf16[512,256]{1,0:T(8,128)(2,1)S(1)}, u32[]{:S(2)}, u32[]{:S(2)}) collective-permute-start(bf16[512,256]{1,0:T(8,128)(2,1)S(1)} %bitcast.48), channel_id=1, source_target_pairs={{0,16},{16,0},{1,17},{17,1},{2,18},{18,2},{3,19},{19,3},{4,20},{20... | collective-permute-start | bytes 786440 | tf_op jit(solution)/shard_map/ppermute | solution.py:304
  85.6 1.9 %collective-permute-start.9 = (bf16[512,256]{1,0:T(8,128)(2,1)S(1)}, bf16[512,256]{1,0:T(8,128)(2,1)S(1)}, u32[]{:S(2)}, u32[]{:S(2)}) collective-permute-start(bf16[512,256]{1,0:T(8,128)(2,1)S(1)} %bitcast.51), channel_id=1, source_target_pairs={{0,16},{16,0},{1,17},{17,1},{2,18},{18,2},{3,19},{19,3},{4,20},{20... | collective-permute-start | bytes 786440 | tf_op jit(solution)/shard_map/ppermute | solution.py:304
  87.9 7.9 %collective-permute-start.10 = (f32[160,128]{1,0:T(8,128)S(1)}, f32[160,128]{1,0:T(8,128)S(1)}, u32[]{:S(2)}, u32[]{:S(2)}) collective-permute-start(f32[160,128]{1,0:T(8,128)S(1)} %get-tuple-element.43), channel_id=1, source_target_pairs={{0,1},{1,0},{2,3},{3,2},{4,5},{5,4},{6,7},{7,6},{8,9},{9,8},{10,11... | collective-permute-start | bytes 245768 | tf_op jit(solution)/shard_map/ppermute | solution.py:133
  93.1 5.3 %collective-permute-start.11 = (f32[160,128]{1,0:T(8,128)S(1)}, f32[160,128]{1,0:T(8,128)S(1)}, u32[]{:S(2)}, u32[]{:S(2)}) collective-permute-start(f32[160,128]{1,0:T(8,128)S(1)} %get-tuple-element.42), channel_id=1, source_target_pairs={{0,2},{1,3},{2,0},{3,1},{4,6},{5,7},{6,4},{7,5},{8,10},{9,11},{10,... | collective-permute-start | bytes 245768 | tf_op jit(solution)/shard_map/ppermute | solution.py:133
  94.6 5.3 %collective-permute-start.12 = (f32[160,128]{1,0:T(8,128)S(1)}, f32[160,128]{1,0:T(8,128)S(1)}, u32[]{:S(2)}, u32[]{:S(2)}) collective-permute-start(f32[160,128]{1,0:T(8,128)S(1)} %get-tuple-element.41), channel_id=1, source_target_pairs={{0,3},{1,2},{2,1},{3,0},{4,7},{5,6},{6,5},{7,4},{8,11},{9,10},{10,... | collective-permute-start | bytes 245768 | tf_op jit(solution)/shard_map/ppermute | solution.py:133
  100.0 8.3 %collective-permute-start.14 = (f32[160,128]{1,0:T(8,128)S(1)}, f32[160,128]{1,0:T(8,128)S(1)}, u32[]{:S(2)}, u32[]{:S(2)}) collective-permute-start(f32[160,128]{1,0:T(8,128)S(1)} %fusion), channel_id=1, source_target_pairs={{0,8},{1,9},{2,10},{3,11},{4,12},{5,13},{6,14},{7,15},{8,0},{9,1},... | collective-permute-start | bytes 245768 | tf_op jit(solution)/shard_map/ppermute | solution.py:133
  103.6 6.3 %collective-permute-start.15 = (f32[160,128]{1,0:T(8,128)S(1)}, f32[160,128]{1,0:T(8,128)S(1)}, u32[]{:S(2)}, u32[]{:S(2)}) collective-permute-start(f32[160,128]{1,0:T(8,128)S(1)} %fusion), channel_id=1, source_target_pairs={{0,12},{1,13},{2,14},{3,15},{4,8},{5,9},{6,10},{7,11},{8,4},{9,5},... | collective-permute-start | bytes 245768 | tf_op jit(solution)/shard_map/ppermute | solution.py:133
  103.9 6.0 %collective-permute-start.13 = (f32[160,128]{1,0:T(8,128)S(1)}, f32[160,128]{1,0:T(8,128)S(1)}, u32[]{:S(2)}, u32[]{:S(2)}) collective-permute-start(f32[160,128]{1,0:T(8,128)S(1)} %fusion), channel_id=1, source_target_pairs={{0,4},{1,5},{2,6},{3,7},{4,0},{5,1},{6,2},{7,3},{8,12},{9,13},{10,... | collective-permute-start | bytes 245768 | tf_op jit(solution)/shard_map/ppermute | solution.py:133
  109.9 5.5 %collective-permute-start.18 = (f32[160,128]{1,0:T(8,128)S(1)}, f32[160,128]{1,0:T(8,128)S(1)}, u32[]{:S(2)}, u32[]{:S(2)}) collective-permute-start(f32[160,128]{1,0:T(8,128)S(1)} %add_add_fusion), channel_id=1, source_target_pairs={{0,3},{1,2},{2,1},{3,0},{4,7},{5,6},{6,5},{7,4},{8,11},{9,10},{10,... | collective-permute-start | bytes 245768 | tf_op jit(solution)/shard_map/ppermute | solution.py:133
  110.8 5.3 %collective-permute-start.17 = (f32[160,128]{1,0:T(8,128)S(1)}, f32[160,128]{1,0:T(8,128)S(1)}, u32[]{:S(2)}, u32[]{:S(2)}) collective-permute-start(f32[160,128]{1,0:T(8,128)S(1)} %add_add_fusion), channel_id=1, source_target_pairs={{0,2},{1,3},{2,0},{3,1},{4,6},{5,7},{6,4},{7,5},{8,10},{9,11},{10,... | collective-permute-start | bytes 245768 | tf_op jit(solution)/shard_map/ppermute | solution.py:133
  112.0 4.4 %collective-permute-start.16 = (f32[160,128]{1,0:T(8,128)S(1)}, f32[160,128]{1,0:T(8,128)S(1)}, u32[]{:S(2)}, u32[]{:S(2)}) collective-permute-start(f32[160,128]{1,0:T(8,128)S(1)} %add_add_fusion), channel_id=1, source_target_pairs={{0,1},{1,0},{2,3},{3,2},{4,5},{5,4},{6,7},{7,6},{8,9},{9,8},{10,11... | collective-permute-start | bytes 245768 | tf_op jit(solution)/shard_map/ppermute | solution.py:133
  116.5 1.8 %collective-permute-start.19 = (f32[4,160,128]{2,1,0:T(8,128)S(1)}, f32[4,160,128]{2,1,0:T(8,128)}, u32[]{:S(2)}, u32[]{:S(2)}) collective-permute-start(f32[4,160,128]{2,1,0:T(8,128)S(1)} %pad_maximum_fusion.mine_ref), channel_id=1, source_target_pairs={{0,16},{16,0},{1,17},{17,1},{2,18},{18,2},{3,19},{19,3},{4,20},{20... | collective-permute-start | bytes 983048 | tf_op jit(solution)/shard_map/ppermute | solution.py:304

commit v2 on v1

v2 whole, which is shorter than its diff:
```python
import functools

import jax
import jax.numpy as jnp
from jax import lax
from jax.experimental import pallas as pl
from jax.experimental.pallas import tpu as pltpu
from jax.sharding import PartitionSpec as P

HALO_T = 4
STEPS = 3
ITERS = 8
WAYS = 4
GROUP = 4

SMALL = pl.CostEstimate(flops=1000, bytes_accessed=1000, transcendentals=0)
PART, PATCH, LIVE = range(3)
SMALL_VMEM = pltpu.CompilerParams(vmem_limit_bytes=8 * 1024 * 1024)
ANY = pl.BlockSpec(memory_space=pl.ANY)
HBM = pl.BlockSpec(memory_space=pltpu.HBM)
VMEM = pl.BlockSpec(memory_space=pltpu.VMEM)
SMEM = pl.BlockSpec(memory_space=pltpu.SMEM)
F32, BF16 = jnp.float32, jnp.bfloat16


def dot(a, b):
    return jnp.dot(a, b, preferred_element_type=F32)


def tile_row(blocks, listed, field):
    wide = jnp.concatenate([blocks(n) for n in range(len(listed))], axis=1)
    tall = jnp.concatenate([field(tile) for tile in listed], axis=0)
    return dot(wide, tall)


def finish(acc, prev, alive):
    value = acc if prev is None else 2.0 * acc - prev.astype(F32)
    return jnp.where(alive, value, 0.0).astype(BF16)


def at_end(name, info):
    odd = info[PATCH] % 2
    return 1 - odd if name == "even" else odd


def first_edge_kernel(info, whole_ref, out_ref, sem):
    edge, tiles = HALO_T, whole_ref.shape[0]
    first = at_end("even", info) * (tiles - edge)
    copy = pltpu.make_async_copy(whole_ref.at[pl.ds(first, edge)], out_ref, sem)
    copy.start()
    copy.wait()
    clear_dead(out_ref, first, info[LIVE])


def clear_dead(ref, first, live):
    def clear(index, carry):
        ref[index] = jnp.zeros(ref.shape[1:], BF16)
        return carry

    count = ref.shape[0]
    lax.fori_loop(jnp.clip(live - first, 0, count), count, clear, 0)


def prepare_kernel(info, whole_ref, blocks_ref, *refs):
    odd_ref, low_ref, high_ref = refs[:3]
    even_blocks, odd_blocks, low_blocks, high_blocks, sem = refs[3:]
    edge, tiles = HALO_T, whole_ref.shape[0]
    half = tiles // 2 - edge
    even_row = at_end("even", info) * (tiles - edge)
    odd_row = at_end("odd", info) * (tiles - edge)
    moves = [
        (whole_ref, edge, low_ref), (whole_ref, edge + half, high_ref),
        (blocks_ref, edge, low_blocks), (whole_ref, odd_row, odd_ref),
        (blocks_ref, even_row, even_blocks), (blocks_ref, edge + half, high_blocks),
        (blocks_ref, odd_row, odd_blocks),
    ]
    copies = [
        pltpu.make_async_copy(source.at[pl.ds(first, target.shape[0])], target, sem.at[i])
        for i, (source, first, target) in enumerate(moves)
    ]
    for copy in copies:
        copy.start()
    for copy in copies:
        copy.wait()
    live = info[LIVE]
    clear_dead(low_ref, edge, live)
    clear_dead(high_ref, edge + half, live)
    clear_dead(odd_ref, odd_row, live)


def first_edge(info, start):
    _, tile, width = start.shape
    return pl.pallas_call(
        first_edge_kernel,
        in_specs=[SMEM, HBM],
        out_specs=VMEM,
        out_shape=jax.ShapeDtypeStruct((HALO_T, tile, width), BF16),
        scratch_shapes=[pltpu.SemaphoreType.DMA],
        compiler_params=SMALL_VMEM,
        cost_estimate=SMALL,
        name="first_edge",
    )(info, start)


def prepare(info, start, blocks):
    tiles, tile, width = start.shape
    half = tiles // 2 - HALO_T
    counts = (HALO_T, half, half)
    block_counts = (HALO_T, HALO_T, half, half)
    shapes = [jax.ShapeDtypeStruct((count, tile, width), BF16) for count in counts]
    shapes += [
        jax.ShapeDtypeStruct((count,) + blocks.shape[1:], blocks.dtype) for count in block_counts
    ]
    return pl.pallas_call(
        prepare_kernel,
        in_specs=[SMEM, HBM, HBM],
        out_specs=[VMEM] * 7,
        out_shape=shapes,
        scratch_shapes=[pltpu.SemaphoreType.DMA((7,))],
        compiler_params=pltpu.CompilerParams(vmem_limit_bytes=16 * 1024 * 1024),
        cost_estimate=SMALL,
        name="prepare",
    )(info, start, blocks)


def layout(name, info, tiles):
    edge, half = HALO_T, tiles // 2 - HALO_T
    if name in ("even", "odd"):
        end = at_end(name, info)
        first = end * (tiles - edge)
        places = [
            (0, 2 * edge * end), (0, edge), (0, 2 * edge + edge * end),
            (half - edge, 3 * edge * (1 - end)),
        ]
        return first, first - edge, places
    spare = half + 2 * edge
    ends = at_end("even", info), at_end("odd", info)
    if name == "low":
        places = [(0, end * spare) for end in ends] + [(0, edge), (0, edge + half)]
        return edge, 0, places
    places = [(0, spare - edge * end) for end in ends] + [(half - edge, 0), (0, edge)]
    return edge + half, half, places


def rows_kernel(name, counts, tiles, info, cols_ref, *refs):
    sources = refs[:4]
    blocks_ref, out_ref, held = refs[-3:]
    prev_ref = refs[4] if len(refs) == 8 else None
    nnz = blocks_ref.shape[1]
    first, base, places = layout(name, info, tiles)
    for source, count, (begin, slot) in zip(sources, counts, places):
        held[pl.ds(slot, count)] = source[pl.ds(begin, count)]
    live = info[LIVE]
    shift = info[PATCH] * tiles + base

    def group(index, carry):
        for r in range(GROUP):
            row = index * GROUP + r
            listed = [cols_ref[first + row, n] - shift for n in range(nnz)]
            acc = tile_row(lambda n: blocks_ref[row, n], listed, lambda c: held[c])
            prev = None if prev_ref is None else prev_ref[row]
            out_ref[row] = finish(acc, prev, first + row < live)
        return carry

    lax.fori_loop(0, out_ref.shape[0] // GROUP, group, 0)


def tile_rows(name, info, cols, blocks, pieces, prev):
    rows, _, tile, _ = blocks.shape
    tiles = cols.shape[0]
    width = pieces[0].shape[-1]
    edge, half = HALO_T, tiles // 2 - HALO_T
    if name in ("even", "odd"):
        counts, window = (edge,) * 4, 4 * edge
    else:
        counts, window = (edge, edge, half, edge), half + 3 * edge
        if name == "high":
            counts = (edge, edge, edge, half)
    args = list(pieces) + ([] if prev is None else [prev]) + [blocks]
    return pl.pallas_call(
        functools.partial(rows_kernel, name, counts, tiles),
        in_specs=[SMEM, SMEM] + [VMEM] * len(args),
        out_specs=VMEM,
        out_shape=jax.ShapeDtypeStruct((rows, tile, width), BF16),
        scratch_shapes=[pltpu.VMEM((window, tile, width), BF16)],
        compiler_params=SMALL_VMEM,
        cost_estimate=SMALL,
        name="rows_" + name,
    )(info, cols, *args)


def gram_kernel(pairs, chunk, last, info, *refs):
    fields = refs[: 2 * pairs]
    start_ref = refs[2 * pairs] if last else None
    square, cross = refs[-2:]
    half = square.shape[0] // 2
    square[...] = jnp.zeros(square.shape, F32)
    cross[...] = jnp.zeros(cross.shape, F32)
    is_first = info[PART] == 0
    across = (((0,), (0,)), ((), ()))
    for own_ref, other_ref in zip(fields[:pairs], fields[pairs:]):

        def add(index, carry):
            rows = pl.ds(pl.multiple_of(index * chunk, chunk), chunk)
            own, other = own_ref[rows, :], other_ref[rows, :]
            square[...] += lax.dot_general(own, own, across, preferred_element_type=F32)
            left = jnp.where(is_first, own[:, :half], other[:, half:])
            right = jnp.where(is_first, other, own)
            cross[...] += lax.dot_general(left, right, across, preferred_element_type=F32)
            return carry

        lax.fori_loop(0, own_ref.shape[0] // chunk, add, 0)
    blocks = [
        square[:half, :half], square[:half, half:], square[half:, half:],
        cross[:, :half], cross[:, half:],
    ]
    if not last:
        for i, block in enumerate(blocks):
            refs[2 * pairs][pl.ds(i * half, half), :] = block
        return
    outs, share = refs[2 * pairs + 1 : 2 * pairs + 1 + WAYS], refs[-3]
    for i, block in enumerate(blocks):
        at = pl.ds(i * half, half)
        share[at, :] = block + start_ref[at, :]
    piece = outs[0].shape[0]
    quarter = info[PATCH] % WAYS
    for d, out in enumerate(outs):
        out[...] = share[pl.ds(pl.multiple_of((quarter ^ d) * piece, 8), piece), :]


def gram_share(info, owns, others, start):
    width = owns[0].shape[1]
    half = width // 2
    chunk = min(own.shape[0] for own in owns)
    last = start is not None
    args = list(owns) + list(others) + ([start] if last else [])
    shape = jax.ShapeDtypeStruct((5 * half, half), F32)
    piece = jax.ShapeDtypeStruct((5 * half // WAYS, half), F32)
    scratch = [pltpu.VMEM((width, width), F32), pltpu.VMEM((half, width), F32)]
    return pl.pallas_call(
        functools.partial(gram_kernel, len(owns), chunk, last),
        in_specs=[SMEM] + [VMEM] * len(args),
        out_specs=[VMEM] * WAYS if last else VMEM,
        out_shape=[piece] * WAYS if last else shape,
        scratch_shapes=([pltpu.VMEM(shape.shape, F32)] if last else []) + scratch,
        compiler_params=SMALL_VMEM,
        cost_estimate=SMALL,
        name="gram_share",
    )(info, *args)


def add_kernel(a, b, c, d, out):
    out[...] = (a[...] + b[...]) + (c[...] + d[...])


def add_four(values):
    return pl.pallas_call(
        add_kernel,
        in_specs=[VMEM] * WAYS,
        out_specs=VMEM,
        out_shape=jax.ShapeDtypeStruct(values[0].shape, F32),
        compiler_params=SMALL_VMEM,
        cost_estimate=SMALL,
        name="add_four",
    )(*values)


def sum_over_patch(parts):
    count = lax.axis_size("patch")

    def exchange(value, distance):
        return lax.ppermute(value, "patch", [(i, i ^ distance) for i in range(count)])

    total = add_four([parts[0]] + [exchange(parts[d], d) for d in range(1, WAYS)])
    stride = WAYS
    while stride < count:
        total = add_four([total] + [exchange(total, d * stride) for d in range(1, WAYS)])
        stride *= WAYS
    return [total] + [exchange(total, d) for d in range(1, WAYS)]


def split(value):
    high = value.astype(BF16)
    return high, (value - high.astype(F32)).astype(BF16)


def product3(left, right_stack):
    high, low = split(left)
    return dot(jnp.concatenate([high, high, low], axis=1), right_stack)


def finish_kernel(total_rows, chunk, info, *refs):
    mine, theirs = refs[:WAYS], refs[WAYS : 2 * WAYS]
    fields, out_ref = refs[2 * WAYS : 2 * WAYS + 8], refs[2 * WAYS + 8]
    shares, x_ref, z_ref, m_ref, stack, wide, result, sem, out_sem = refs[2 * WAYS + 9 :]
    part, quarter = info[PART], info[PATCH] % WAYS
    size = x_ref.shape[0]
    width = size // 2
    half = width // 2
    edge_size = fields[0].shape[0]
    end = wide.shape[0] - edge_size
    starts = [
        at_end("even", info) * end, edge_size, edge_size + fields[1].shape[0],
        at_end("odd", info) * end,
    ]
    copies = []
    for i, source in enumerate(fields):
        rows = pl.ds(pl.multiple_of(starts[i % 4], edge_size), source.shape[0])
        target = wide.at[rows, pl.ds(i // 4 * width, width)]
        copies.append(pltpu.make_async_copy(source, target, sem.at[i]))
    for copy in copies:
        copy.start()

    piece = mine[0].shape[0]
    for d in range(WAYS):
        rows = pl.ds(pl.multiple_of((quarter ^ d) * piece, 8), piece)
        shares[part, rows, :] = mine[d][...]
        shares[1 - part, rows, :] = theirs[d][...]

    def block(side, index):
        return shares[side, pl.ds(index * half, half), :]

    def place(row, col, value):
        x_ref[pl.ds(row * half, half), pl.ds(col * half, half)] = value
        if row != col:
            x_ref[pl.ds(col * half, half), pl.ds(row * half, half)] = value.T

    for side in range(2):
        place(2 * side, 2 * side, block(side, 0))
        place(2 * side, 2 * side + 1, block(side, 1))
        place(2 * side + 1, 2 * side + 1, block(side, 2))
        place(side, 2, block(side, 3))
        place(side, 3, block(side, 4))

    gram = x_ref[...]
    norm = jnp.sqrt(jnp.sum(gram * gram, keepdims=True))
    x_ref[...] = gram / norm

    def set_middle():
        x = x_ref[...]
        row = lax.broadcasted_iota(jnp.int32, x.shape, 0)
        col = lax.broadcasted_iota(jnp.int32, x.shape, 1)
        middle = jnp.where(row == col, 1.5, 0.0) - 0.5 * x
        high, low = split(middle)
        stack[0:size, :] = high
        stack[size : 2 * size, :] = low
        stack[2 * size :, :] = high
        return middle

    def step_x():
        m_ref[...] = product3(x_ref[...], stack[...])
        x_ref[...] = product3(m_ref[...], stack[...])

    z_ref[...] = set_middle()
    step_x()

    def sweep(index, carry):
        set_middle()
        z_ref[...] = product3(z_ref[...], stack[...])
        step_x()
        return carry

    lax.fori_loop(1, ITERS - 1, sweep, 0)
    set_middle()
    z_ref[...] = product3(z_ref[...], stack[...])

    own = pl.ds(pl.multiple_of(part * width, width), width)
    other = pl.ds(pl.multiple_of((1 - part) * width, width), width)
    rotation = jnp.concatenate([z_ref[own, own], z_ref[other, own]], axis=0).astype(BF16)
    factor = jnp.sqrt(total_rows / norm)
    for copy in copies:
        copy.wait()
    count = wide.shape[0] // chunk
    outs = []
    for i in range(count):
        rows = pl.ds(i * chunk, chunk)
        result[rows, :] = (dot(wide[rows, :], rotation) * factor).astype(BF16)
        outs.append(pltpu.make_async_copy(result.at[rows], out_ref.at[rows], out_sem.at[i]))
        outs[-1].start()
    for out in outs:
        out.wait()


def rotate(info, mine, theirs, owns, others, total_rows):
    width = owns[0].shape[1]
    rows = sum(own.shape[0] for own in owns)
    size = 2 * width
    chunk = min(rows, 512)
    body = functools.partial(finish_kernel, float(total_rows), chunk)
    matrix = pltpu.VMEM((size, size), F32)
    return pl.pallas_call(
        body,
        in_specs=[SMEM] + [VMEM] * (2 * WAYS) + [ANY] * 8,
        out_specs=ANY,
        out_shape=jax.ShapeDtypeStruct((rows, width), BF16),
        scratch_shapes=[
            pltpu.VMEM((2, 5 * width // 2, width // 2), F32),
            matrix, matrix, matrix,
            pltpu.VMEM((3 * size, size), BF16),
            pltpu.VMEM((rows, size), BF16),
            pltpu.VMEM((rows, width), BF16),
            pltpu.SemaphoreType.DMA((8,)),
            pltpu.SemaphoreType.DMA((rows // chunk,)),
        ],
        compiler_params=pltpu.CompilerParams(vmem_limit_bytes=20 * 1024 * 1024),
        cost_estimate=pl.CostEstimate(
            flops=21 * 6 * size**3 + 2 * rows * size * width,
            bytes_accessed=3 * rows * width * 2,
            transcendentals=0,
        ),
        name="rotate",
    )(info, *mine, *theirs, *owns, *others)


def after(value, *others):
    return lax.optimization_barrier((value, others))[0]


def on_device(vectors, blocks, tile_cols, live_tiles):
    tiles, _, tile, _ = blocks.shape
    width = vectors.shape[1]
    count = lax.axis_size("patch")
    pairs = {
        "even": [(i, i ^ 1) for i in range(count)],
        "odd": [(i, ((i + 1) ^ 1) - 1) for i in range(1, count - 1)],
    }

    def exchange(name, value):
        return lax.ppermute(value, "patch", pairs[name])

    def sibling(value):
        return lax.ppermute(value, "cols", [(0, 1), (1, 0)])

    start = vectors.reshape(tiles, tile, width)
    scalars = [lax.axis_index("cols"), lax.axis_index("patch"), live_tiles[0]]
    info = jnp.stack(scalars).astype(jnp.int32)

    even = first_edge(info, start)
    even_halo = exchange("even", even)
    ready = prepare(after(info, even), start, blocks)
    odd, low, high = ready[:3]
    stored = dict(zip(("even", "odd", "low", "high"), ready[3:]))
    prev = dict.fromkeys(stored)

    def rows(name, *pieces):
        return tile_rows(name, info, tile_cols, stored[name], pieces, prev[name])

    for step in range(STEPS):
        new_low = rows("low", even, odd, low, high)
        even_halo = after(even_halo, new_low)
        odd_halo = exchange("odd", after(odd, even_halo))
        new_even = rows("even", even_halo, even, low, high)
        new_high = rows("high", even, odd, low, high)
        if step == STEPS - 1:
            flat = [value.reshape(-1, width) for value in (new_even, new_low, new_high)]
            others = [sibling(after(value, even_halo)) for value in flat[1:]]
            share = gram_share(info, flat[1:], others, None)
            others.insert(0, sibling(after(flat[0], share)))
            odd_halo = after(odd_halo, new_even, new_high, share)
        else:
            odd_halo = after(odd_halo, new_even, new_high)
            even_halo = exchange("even", after(new_even, odd_halo))
        new_odd = rows("odd", odd_halo, odd, low, high)
        prev = {"even": even, "odd": odd, "low": low, "high": high}
        even, odd, low, high = new_even, new_odd, new_low, new_high
    last = odd.reshape(-1, width)
    other_last = sibling(last)
    parts = gram_share(info, [flat[0], last], [others[0], other_last], share)
    mine = sum_over_patch(parts)
    theirs = [sibling(value) for value in mine]
    total_rows = tiles * tile * count
    return rotate(info, mine, theirs, flat + [last], others + [other_last], total_rows)


def solution(mesh):
    in_specs = (P("patch", "cols"), P("patch", None, None, None), P("patch", None), P("patch"))
    return jax.shard_map(
        on_device, mesh=mesh, in_specs=in_specs, out_specs=P("patch", "cols"), check_vma=False
    )
```

time: 143 us -> 125 us (0.87)
  local copies, waits for them, and re-layouts: 34.5 us -> 14.6 us
  starting transfers between devices: 33.5 us -> 40.1 us
  other arithmetic: 3.32 us -> 0.08 us
  Pallas kernels: 52.3 us -> 50 us
  waiting for transfers between devices: 17 us -> 18.7 us
    unnamed x87 -> x37, local copies, waits for them, and re-layouts: 22 us -> 14.6 us
    slice x1 -> x0, local copies, waits for them, and re-layouts: 6.59 us -> none  [on_device(): blocks[edge + half:tiles - edge]]
    dynamic_slice x4 -> x0, local copies, waits for them, and re-layouts: 5.48 us -> none  [the longest x1 2.7 us: on_device(): lax.dynamic_slice_in_dim(blocks, row, edge, 0)]
    ppermute x9, starting transfers between devices: 14.5 us -> 19.7 us  [exchange(): lax.ppermute(value, 'patch', [(i, i ^ distance) for i in range(count)])]
    select_n x2 -> x0, other arithmetic: 3.23 us -> none  [masked(): return jnp.where(kept, part_of, jnp.zeros((), BF16))]
    pallas_call x15 -> x19, Pallas kernels: 52.3 us -> 50 us  [the longest x1 23.2 us: rotate(): pl.pallas_call(body, in_specs=[SMEM] + [VMEM] * (2 * WAYS) + [ANY] * 8, o...]
    ppermute x6, waiting for transfers between devices: 0.02 us -> 1.74 us  [exchange(): return lax.ppermute(value, 'patch', pairs[name])]
    ppermute x6, starting transfers between devices: 17.8 us -> 19.3 us  [exchange(): return lax.ppermute(value, 'patch', pairs[name])]
  transfers between devices with their start and end apart: 20 -> 23, of which waited for: 11 -> 13; matrix products, arithmetic and copies ran while one was open for 10% -> 0% of each run, Pallas kernels for 19% -> 19%
where the time goes in v2:
time: 125 us
  Pallas kernels  50 us (40%)
  starting transfers between devices  40.1 us (32%)
  waiting for transfers between devices  18.7 us (15%)
  local copies, waits for them, and re-layouts  14.6 us (12%)
    pallas_call x1, Pallas kernels, rotate(): pl.pallas_call(body, in_specs=[SMEM] + [VMEM] * (2 * WAYS) + [ANY] * 8, o...  23.2 us
    pallas_call x12, Pallas kernels, tile_rows(): pl.pallas_call(functools.partial(rows_kernel, name, counts, tiles), in_sp...  22.5 us
    ppermute x9, starting transfers between devices, exchange(): lax.ppermute(value, 'patch', [(i, i ^ distance) for i in range(count)])  19.7 us
    ppermute x6, starting transfers between devices, exchange(): return lax.ppermute(value, 'patch', pairs[name])  19.3 us
    unnamed x37, local copies, waits for them, and re-layouts  14.6 us
    ppermute x9, waiting for transfers between devices, exchange(): lax.ppermute(value, 'patch', [(i, i ^ distance) for i in range(count)])  13.6 us
    ppermute x8, waiting for transfers between devices, sibling(): return lax.ppermute(value, 'cols', [(0, 1), (1, 0)])  3.34 us
  transfers between devices with their start and end apart: 23, of which 13 were waited for; matrix products, arithmetic and copies ran while one was open for 0% of the time, Pallas kernels for 19%

profile of v2, /device:TPU:0, one launch (start us, length us, event | category | flops | bytes accessed | tf_op | source)
XLA Modules:
  0.0 124.6 jit_solution(5356557344946939027)
XLA Ops:
  0.7 0.1 pad_add_fusion.info
  0.7 1.6 %copy-done.13 = bf16[4096,256]{1,0:T(8,128)(2,1)S(1)} copy-done((bf16[4096,256]{1,0:T(8,128)(2,1)S(1)}, bf16[4096,256]{1,0:T(8,128)(2,1)}, u32[]{:S(2)}) %copy-start.13) | copy-done | bytes 2097176
  2.3 0.6 first_edge.1.refs_0_.refs_1_.refs_4_
  2.9 3.0 %collective-permute-start = (bf16[4,128,256]{2,1,0:T(8,128)(2,1)S(1)}, bf16[4,128,256]{2,1,0:T(8,128)(2,1)}, u32[]{:S(2)}, u32[]{:S(2)}) collective-permute-start(bf16[4,128,256]{2,1,0:T(8,128)(2,1)S(1)} %first_edge.1.refs_0_.refs_1_.refs_4_), channel_id=1, source_target_pairs={{0,1},{1,0},{2,3},{3,2},{4,5},{5,4},{6,7},{7,6},{8,9},{9,8},{10,11... | collective-permute-start | bytes 786440 | tf_op jit(solution)/shard_map/ppermute | solution.py:429
  5.9 3.4 %copy-done.12 = bf16[32,8,128,128]{3,2,1,0:T(8,128)(2,1)S(1)} copy-done((bf16[32,8,128,128]{3,2,1,0:T(8,128)(2,1)S(1)}, bf16[32,8,128,128]{3,2,1,0:T(8,128)(2,1)}, u32[]{:S(2)}) %copy-start.12) | copy-done | bytes 8388632
  9.3 1.4 %prepare.1 = (bf16[4,128,256]{2,1,0:T(8,128)(2,1)S(1)}, bf16[12,128,256]{2,1,0:T(8,128)(2,1)S(1)}, bf16[12,128,256]{2,1,0:T(8,128)(2,1)S(1)}, bf16[4,8,128,128]{...) custom-call(s32[3]{0:T(128)S(1)} %pad_add_fusion.info, ...), custom_call_target="tpu_custom_call" | custom-call | flops 1000 | bytes 1000 | tf_op jit(solution)/shard_map/prepare/pallas_call | solution.py:114
  10.7 1.6 %copy-done = bf16[12,8,128,128]{3,2,1,0:T(8,128)(2,1)} copy-done((bf16[12,8,128,128]{3,2,1,0:T(8,128)(2,1)}, bf16[12,8,128,128]{3,2,1,0:T(8,128)(2,1)S(1)}, u32[]{:S(2)}) %copy-start) | copy-done | bytes 3145752
  12.3 0.9 copy-done.2
  13.2 0.9 copy-done.5
  14.1 1.0 copy-done.8
  15.1 1.0 copy-done.10
  16.1 0.7 copy-done.15
  16.8 0.1 copy.14.cols_ref
  16.9 1.3 %copy-done.3 = bf16[12,128,256]{2,1,0:T(8,128)(2,1)S(1)} copy-done((bf16[12,128,256]{2,1,0:T(8,128)(2,1)S(1)}, bf16[12,128,256]{2,1,0:T(8,128)(2,1)}, u32[]{:S(2)}) %copy-start.3) | copy-done | bytes 786456
  18.2 1.1 copy-done.6
  19.3 0.9 copy-done.16
  20.3 2.3 %rows_low.3.refs_2_.refs_4_ = bf16[12,128,256]{2,1,0:T(8,128)(2,1)S(1)} custom-call(s32[3]{0:T(128)S(1)} %pad_add_fusion.info, s32[32,8]{1,0:T(8,128)S(1)} %copy.14.cols_ref, bf16[4,128,256]{2,1,0:T(8,128)(2,1)S(1)} %first_edge.1.refs_0_.refs_1_.refs_4_, bf16[4,128,256]{2,1,0:T(8,128)(2,1)S(1)} %copy-done.16, bf16[12,128,256]{2,1,0:T(8,128)(2,1)S(1)} %copy-done.6, ...), custom_call_target="tpu_custom_call" | custom-call | flops 1000 | bytes 1000 | tf_op jit(solution)/shard_map/rows_low/pallas_call | solution.py:180
  22.6 0.0 copy-start.11
  22.6 0.8 collective-permute-start.1
  23.4 2.4 %rows_high.3.refs_3_.refs_4_ = bf16[12,128,256]{2,1,0:T(8,128)(2,1)S(1)} custom-call(s32[3]{0:T(128)S(1)} %pad_add_fusion.info, s32[32,8]{1,0:T(8,128)S(1)} %copy.14.cols_ref, bf16[4,128,256]{2,1,0:T(8,128)(2,1)S(1)} %first_edge.1.refs_0_.refs_1_.refs_4_, bf16[4,128,256]{2,1,0:T(8,128)(2,1)S(1)} %copy-done.16, bf16[12,128,256]{2,1,0:T(8,128)(2,1)S(1)} %copy-done.6, ...), custom_call_target="tpu_custom_call" | custom-call | flops 1000 | bytes 1000 | tf_op jit(solution)/shard_map/rows_high/pallas_call | solution.py:180
  25.8 1.6 %rows_even.3.refs_0_.refs_1_.refs_4_ = bf16[4,128,256]{2,1,0:T(8,128)(2,1)S(1)} custom-call(s32[3]{0:T(128)S(1)} %pad_add_fusion.info, s32[32,8]{1,0:T(8,128)S(1)} %copy.14.cols_ref, bf16[4,128,256]{2,1,0:T(8,128)(2,1)} %collective-permute-done.refs_0_, bf16[4,128,256]{2,1,0:T(8,128)(2,1)S(1)} %first_edge.1.refs_0_.refs_1_.refs_4_, ...), custom_call_target="tpu_custom_call" | custom-call | flops 1000 | bytes 1000 | tf_op jit(solution)/shard_map/rows_even/pallas_call | solution.py:180
  27.5 0.0 collective-permute-done.1.refs_0_
  27.5 7.1 %collective-permute-start.2 = (bf16[4,128,256]{2,1,0:T(8,128)(2,1)S(1)}, bf16[4,128,256]{2,1,0:T(8,128)(2,1)S(1)}, u32[]{:S(2)}, u32[]{:S(2)}) collective-permute-start(bf16[4,128,256]{2,1,0:T(8,128)(2,1)S(1)} %rows_even.3.refs_0_.refs_1_.refs_4_), channel_id=1, source_target_pairs={{0,1},{1,0},{2,3},{3,2},{4,5},{5,4},{6,7},{7,6},{8,9},{9,8},{10,11... | collective-permute-start | bytes 786440 | tf_op jit(solution)/shard_map/ppermute | solution.py:429
  34.6 1.4 %rows_odd.3.refs_1_.refs_4_ = bf16[4,128,256]{2,1,0:T(8,128)(2,1)S(1)} custom-call(s32[3]{0:T(128)S(1)} %pad_add_fusion.info, s32[32,8]{1,0:T(8,128)S(1)} %copy.14.cols_ref, bf16[4,128,256]{2,1,0:T(8,128)(2,1)S(1)} %collective-permute-done.1.refs_0_, bf16[4,128,256]{2,1,0:T(8,128)(2,1)S(1)} %copy-done.16, bf16[12,128,256]{2,1,0:T(8,128)(2,1)S(1)} %copy-done.6, ...), custom_call_target="tpu_custom_call" | custom-call | flops 1000 | bytes 1000 | tf_op jit(solution)/shard_map/rows_odd/pallas_call | solution.py:180
  36.0 2.3 %rows_low.4.refs_2_ = bf16[12,128,256]{2,1,0:T(8,128)(2,1)S(1)} custom-call(s32[3]{0:T(128)S(1)} %pad_add_fusion.info, s32[32,8]{1,0:T(8,128)S(1)} %copy.14.cols_ref, bf16[4,128,256]{2,1,0:T(8,128)(2,1)S(1)} %rows_even.3.refs_0_.refs_1_.refs_4_, bf16[4,128,256]{2,1,0:T(8,128)(2,1)S(1)} %rows_odd.3.refs_1_.refs_4_, ...), custom_call_target="tpu_custom_call" | custom-call | flops 1000 | bytes 1000 | tf_op jit(solution)/shard_map/rows_low/pallas_call | solution.py:180
  38.3 1.7 %collective-permute-done.2.refs_0_ = bf16[4,128,256]{2,1,0:T(8,128)(2,1)S(1)} collective-permute-done((bf16[4,128,256]{2,1,0:T(8,128)(2,1)S(1)}, bf16[4,128,256]{2,1,0:T(8,128)(2,1)S(1)}, u32[]{:S(2)}, u32[]{:S(2)}) %collective-permute-start.2) | collective-permute-done | bytes 262176 | tf_op jit(solution)/shard_map/ppermute | solution.py:429
  40.0 0.7 collective-permute-start.3
  40.7 2.4 %rows_high.4.refs_3_ = bf16[12,128,256]{2,1,0:T(8,128)(2,1)S(1)} custom-call(s32[3]{0:T(128)S(1)} %pad_add_fusion.info, s32[32,8]{1,0:T(8,128)S(1)} %copy.14.cols_ref, bf16[4,128,256]{2,1,0:T(8,128)(2,1)S(1)} %rows_even.3.refs_0_.refs_1_.refs_4_, bf16[4,128,256]{2,1,0:T(8,128)(2,1)S(1)} %rows_odd.3.refs_1_.refs_4_, ...), custom_call_target="tpu_custom_call" | custom-call | flops 1000 | bytes 1000 | tf_op jit(solution)/shard_map/rows_high/pallas_call | solution.py:180
  43.1 1.4 %rows_even.4.refs_0_.refs_1_ = bf16[4,128,256]{2,1,0:T(8,128)(2,1)S(1)} custom-call(s32[3]{0:T(128)S(1)} %pad_add_fusion.info, s32[32,8]{1,0:T(8,128)S(1)} %copy.14.cols_ref, bf16[4,128,256]{2,1,0:T(8,128)(2,1)S(1)} %collective-permute-done.2.refs_0_, bf16[4,128,256]{2,1,0:T(8,128)(2,1)S(1)} %rows_even.3.refs_0_.refs_1_.refs_4_, ...), custom_call_target="tpu_custom_call" | custom-call | flops 1000 | bytes 1000 | tf_op jit(solution)/shard_map/rows_even/pallas_call | solution.py:180
  44.5 6.9 %collective-permute-start.4 = (bf16[4,128,256]{2,1,0:T(8,128)(2,1)S(1)}, bf16[4,128,256]{2,1,0:T(8,128)(2,1)S(1)}, u32[]{:S(2)}, u32[]{:S(2)}) collective-permute-start(bf16[4,128,256]{2,1,0:T(8,128)(2,1)S(1)} %rows_even.4.refs_0_.refs_1_), channel_id=1, source_target_pairs={{0,1},{1,0},{2,3},{3,2},{4,5},{5,4},{6,7},{7,6},{8,9},{9,8},{10,11... | collective-permute-start | bytes 786440 | tf_op jit(solution)/shard_map/ppermute | solution.py:429
  51.4 1.4 %rows_odd.4.refs_1_ = bf16[4,128,256]{2,1,0:T(8,128)(2,1)S(1)} custom-call(s32[3]{0:T(128)S(1)} %pad_add_fusion.info, s32[32,8]{1,0:T(8,128)S(1)} %copy.14.cols_ref, bf16[4,128,256]{2,1,0:T(8,128)(2,1)S(1)} %collective-permute-done.3.refs_0_, bf16[4,128,256]{2,1,0:T(8,128)(2,1)S(1)} %rows_odd.3.refs_1_.refs_4_, ...), custom_call_target="tpu_custom_call" | custom-call | flops 1000 | bytes 1000 | tf_op jit(solution)/shard_map/rows_odd/pallas_call | solution.py:180
  52.7 2.4 %rows_high.5 = bf16[12,128,256]{2,1,0:T(8,128)(2,1)S(1)} custom-call(s32[3]{0:T(128)S(1)} %pad_add_fusion.info, s32[32,8]{1,0:T(8,128)S(1)} %copy.14.cols_ref, bf16[4,128,256]{2,1,0:T(8,128)(2,1)S(1)} %rows_even.4.refs_0_.refs_1_, bf16[4,128,256]{2,1,0:T(8,128)(2,1)S(1)} %rows_odd.4.refs_1_, bf16[12,128,256]{2,1,0:T(8,128)(2,1)S(1)} %rows_low.4.refs_2_, ...), custom_call_target="tpu_custom_call" | custom-call | flops 1000 | bytes 1000 | tf_op jit(solution)/shard_map/rows_high/pallas_call | solution.py:180
  55.1 2.3 %rows_low.5 = bf16[12,128,256]{2,1,0:T(8,128)(2,1)S(1)} custom-call(s32[3]{0:T(128)S(1)} %pad_add_fusion.info, s32[32,8]{1,0:T(8,128)S(1)} %copy.14.cols_ref, bf16[4,128,256]{2,1,0:T(8,128)(2,1)S(1)} %rows_even.4.refs_0_.refs_1_, bf16[4,128,256]{2,1,0:T(8,128)(2,1)S(1)} %rows_odd.4.refs_1_, bf16[12,128,256]{2,1,0:T(8,128)(2,1)S(1)} %rows_low.4.refs_2_, ...), custom_call_target="tpu_custom_call" | custom-call | flops 1000 | bytes 1000 | tf_op jit(solution)/shard_map/rows_low/pallas_call | solution.py:180
  57.4 0.0 collective-permute-done.4.refs_0_
  57.4 0.1 collective-permute-start.6
  57.5 0.5 collective-permute-start.7
  58.0 0.8 collective-permute-start.5
  58.9 1.4 %rows_even.5 = bf16[4,128,256]{2,1,0:T(8,128)(2,1)S(1)} custom-call(s32[3]{0:T(128)S(1)} %pad_add_fusion.info, s32[32,8]{1,0:T(8,128)S(1)} %copy.14.cols_ref, bf16[4,128,256]{2,1,0:T(8,128)(2,1)S(1)} %collective-permute-done.4.refs_0_, bf16[4,128,256]{2,1,0:T(8,128)(2,1)S(1)} %rows_even.4.refs_0_.refs_1_, bf16[12,128,256]{2,1,0:T(8,128)(2,1)S(1)} %rows_low.4.refs_2_, ...), custom_call_target="tpu_custom_call" | custom-call | flops 1000 | bytes 1000 | tf_op jit(solution)/shard_map/rows_even/pallas_call | solution.py:180
  60.2 0.7 collective-permute-done.7.refs_3_.refs_14_
  60.9 1.4 %gram_share.2.refs_4_ = f32[640,128]{1,0:T(8,128)S(1)} custom-call(s32[3]{0:T(128)S(1)} %pad_add_fusion.info, bf16[1536,256]{1,0:T(8,128)(2,1)S(1)} %bitcast.13, bf16[1536,256]{1,0:T(8,128)(2,1)S(1)} %bitcast.10, bf16[1536,256]{1,0:T(8,128)(2,1)S(1)} %collective-permute-done.6.refs_2_.refs_13_, bf16[1536,256]{1,0:T(8,128)(2,1)S(1)} %collective-permute-done.7.refs_3_.refs_14_), custom_call_target="tpu_custom_call" | custom-call | flops 1000 | bytes 1000 | tf_op jit(solution)/shard_map/gram_share/pallas_call | solution.py:240
  62.3 1.4 %rows_odd.5 = bf16[4,128,256]{2,1,0:T(8,128)(2,1)S(1)} custom-call(s32[3]{0:T(128)S(1)} %pad_add_fusion.info, s32[32,8]{1,0:T(8,128)S(1)} %copy.14.cols_ref, bf16[4,128,256]{2,1,0:T(8,128)(2,1)S(1)} %collective-permute-done.5.refs_0_, bf16[4,128,256]{2,1,0:T(8,128)(2,1)S(1)} %rows_odd.4.refs_1_, bf16[12,128,256]{2,1,0:T(8,128)(2,1)S(1)} %rows_low.4.refs_2_, ...), custom_call_target="tpu_custom_call" | custom-call | flops 1000 | bytes 1000 | tf_op jit(solution)/shard_map/rows_odd/pallas_call | solution.py:180
  63.7 0.2 collective-permute-start.9
  63.9 0.4 collective-permute-start.8
  64.3 1.0 collective-permute-done.9.refs_3_.refs_15_
  65.3 0.4 collective-permute-done.8.refs_2_.refs_12_
  65.7 1.0 gram_share.3
  66.7 8.6 %collective-permute-start.10 = (f32[160,128]{1,0:T(8,128)S(1)}, f32[160,128]{1,0:T(8,128)S(1)}, u32[]{:S(2)}, u32[]{:S(2)}) collective-permute-start(f32[160,128]{1,0:T(8,128)S(1)} %get-tuple-element.54), channel_id=1, source_target_pairs={{0,1},{1,0},{2,3},{3,2},{4,5},{5,4},{6,7},{7,6},{8,9},{9,8},{10,11... | collective-permute-start | bytes 245768 | tf_op jit(solution)/shard_map/ppermute | solution.py:272
  75.2 3.1 %collective-permute-start.11 = (f32[160,128]{1,0:T(8,128)S(1)}, f32[160,128]{1,0:T(8,128)S(1)}, u32[]{:S(2)}, u32[]{:S(2)}) collective-permute-start(f32[160,128]{1,0:T(8,128)S(1)} %get-tuple-element.55), channel_id=1, source_target_pairs={{0,2},{1,3},{2,0},{3,1},{4,6},{5,7},{6,4},{7,5},{8,10},{9,11},{10,... | collective-permute-start | bytes 245768 | tf_op jit(solution)/shard_map/ppermute | solution.py:272
  78.3 3.5 %collective-permute-done.11.c = f32[160,128]{1,0:T(8,128)S(1)} collective-permute-done((f32[160,128]{1,0:T(8,128)S(1)}, f32[160,128]{1,0:T(8,128)S(1)}, u32[]{:S(2)}, u32[]{:S(2)}) %collective-permute-start.11) | collective-permute-done | bytes 81952 | tf_op jit(solution)/shard_map/ppermute | solution.py:272
  81.8 1.8 %collective-permute-done.12.d = f32[160,128]{1,0:T(8,128)S(1)} collective-permute-done((f32[160,128]{1,0:T(8,128)S(1)}, f32[160,128]{1,0:T(8,128)S(1)}, u32[]{:S(2)}, u32[]{:S(2)}) %collective-permute-start.12) | collective-permute-done | bytes 81952 | tf_op jit(solution)/shard_map/ppermute | solution.py:272
  83.7 1.5 %collective-permute-start.15 = (f32[160,128]{1,0:T(8,128)S(1)}, f32[160,128]{1,0:T(8,128)S(1)}, u32[]{:S(2)}, u32[]{:S(2)}) collective-permute-start(f32[160,128]{1,0:T(8,128)S(1)} %add_four.2.a), channel_id=1, source_target_pairs={{0,12},{1,13},{2,14},{3,15},{4,8},{5,9},{6,10},{7,11},{8,4},{9,5},... | collective-permute-start | bytes 245768 | tf_op jit(solution)/shard_map/ppermute | solution.py:272
  85.2 0.8 collective-permute-start.14
  86.0 2.2 %collective-permute-start.13 = (f32[160,128]{1,0:T(8,128)S(1)}, f32[160,128]{1,0:T(8,128)S(1)}, u32[]{:S(2)}, u32[]{:S(2)}) collective-permute-start(f32[160,128]{1,0:T(8,128)S(1)} %add_four.2.a), channel_id=1, source_target_pairs={{0,4},{1,5},{2,6},{3,7},{4,0},{5,1},{6,2},{7,3},{8,12},{9,13},{10,... | collective-permute-start | bytes 245768 | tf_op jit(solution)/shard_map/ppermute | solution.py:272
  88.1 2.1 %collective-permute-done.15.d = f32[160,128]{1,0:T(8,128)S(1)} collective-permute-done((f32[160,128]{1,0:T(8,128)S(1)}, f32[160,128]{1,0:T(8,128)S(1)}, u32[]{:S(2)}, u32[]{:S(2)}) %collective-permute-start.15) | collective-permute-done | bytes 81952 | tf_op jit(solution)/shard_map/ppermute | solution.py:272
  90.2 2.5 %collective-permute-done.14.c = f32[160,128]{1,0:T(8,128)S(1)} collective-permute-done((f32[160,128]{1,0:T(8,128)S(1)}, f32[160,128]{1,0:T(8,128)S(1)}, u32[]{:S(2)}, u32[]{:S(2)}) %collective-permute-start.14) | collective-permute-done | bytes 81952 | tf_op jit(solution)/shard_map/ppermute | solution.py:272
  92.7 0.5 collective-permute-start.18
  93.3 2.3 %collective-permute-start.17 = (f32[160,128]{1,0:T(8,128)S(1)}, f32[160,128]{1,0:T(8,128)S(1)}, u32[]{:S(2)}, u32[]{:S(2)}) collective-permute-start(f32[160,128]{1,0:T(8,128)S(1)} %add_four.3.refs_0_), channel_id=1, source_target_pairs={{0,2},{1,3},{2,0},{3,1},{4,6},{5,7},{6,4},{7,5},{8,10},{9,11},{10,... | collective-permute-start | bytes 245768 | tf_op jit(solution)/shard_map/ppermute | solution.py:272
  95.6 0.7 collective-permute-start.16
  96.3 2.0 %collective-permute-done.18.refs_3_ = f32[160,128]{1,0:T(8,128)S(1)} collective-permute-done((f32[160,128]{1,0:T(8,128)S(1)}, f32[160,128]{1,0:T(8,128)S(1)}, u32[]{:S(2)}, u32[]{:S(2)}) %collective-permute-start.18) | collective-permute-done | bytes 81952 | tf_op jit(solution)/shard_map/ppermute | solution.py:272
  98.2 0.6 collective-permute-done.17.refs_2_
  98.9 1.1 collective-permute-done.16.refs_1_
  100.0 0.1 collective-permute-done.21.refs_6_
  100.2 1.1 collective-permute-done.20.refs_5_
  101.3 23.2 %rotate.1 = bf16[4096,256]{1,0:T(8,128)(2,1)} custom-call(s32[3]{0:T(128)S(1)} %pad_add_fusion.info, f32[160,128]{1,0:T(8,128)S(1)} %add_four.3.refs_0_, f32[160,128]{1,0:T(8,128)S(1)} %collective-permute-done.16.refs_1_, f32[160,128]{1,0:T(8,128)S(1)} %collective-permute-done.17.refs_2_, f32[160,128]{1,0:T(8,128)S(1)} %collective-permute-done.18.refs_3_, ...), custom_call_target="tpu_custom_call" | custom-call | flops 17985175552 | bytes 6291456 | tf_op jit(solution)/shard_map/rotate/pallas_call | solution.py:391
  (39 shorter events, 0.1 us)
Async XLA Ops:
  0.7 1.6 %copy-start.13 = (bf16[4096,256]{1,0:T(8,128)(2,1)S(1)}, bf16[4096,256]{1,0:T(8,128)(2,1)}, u32[]{:S(2)}) copy-start(bf16[4096,256]{1,0:T(8,128)(2,1)} %param.4) | copy-start | bytes 6291460
  2.3 3.6 %copy-start.14 = (bf16[4096,256]{1,0:T(8,128)(2,1)S(1)}, bf16[4096,256]{1,0:T(8,128)(2,1)}, u32[]{:S(2)}) copy-start(bf16[4096,256]{1,0:T(8,128)(2,1)} %param.4) | copy-start | bytes 6291460
  2.9 19.6 %collective-permute-start = (bf16[4,128,256]{2,1,0:T(8,128)(2,1)S(1)}, bf16[4,128,256]{2,1,0:T(8,128)(2,1)}, u32[]{:S(2)}, u32[]{:S(2)}) collective-permute-start(bf16[4,128,256]{2,1,0:T(8,128)(2,1)S(1)} %first_edge.1.refs_0_.refs_1_.refs_4_), channel_id=1, source_target_pairs={{0,1},{1,0},{2,3},{3,2},{4,5},{5,4},{6,7},{7,6},{8,9},{9,8},{10,11... | collective-permute-start | bytes 786440 | tf_op jit(solution)/shard_map/ppermute | solution.py:429
  5.9 3.4 %copy-start.12 = (bf16[32,8,128,128]{3,2,1,0:T(8,128)(2,1)S(1)}, bf16[32,8,128,128]{3,2,1,0:T(8,128)(2,1)}, u32[]{:S(2)}) copy-start(bf16[32,8,128,128]{3,2,1,0:T(8,128)(2,1)} %blocks_ref.1) | copy-start | bytes 25165828
  9.3 7.5 %copy-start.17 = (s32[32,8]{0,1:T(8,128)S(1)}, s32[32,8]{0,1:T(8,128)}, u32[]{:S(2)}) copy-start(s32[32,8]{0,1:T(8,128)} %param.6) | copy-start | bytes 3076
  10.7 1.6 %copy-start = (bf16[12,8,128,128]{3,2,1,0:T(8,128)(2,1)}, bf16[12,8,128,128]{3,2,1,0:T(8,128)(2,1)S(1)}, u32[]{:S(2)}) copy-start(bf16[12,8,128,128]{3,2,1,0:T(8,128)(2,1)S(1)} %get-tuple-element.39.refs_4_.refs_5_) | copy-start | bytes 9437188
  12.3 0.9 copy-start.2
  13.2 0.9 copy-start.5
  14.1 1.0 copy-start.8
  15.1 1.0 copy-start.10
  16.1 0.7 copy-start.15
  16.9 6.5 %copy-start.1 = (bf16[12,8,128,128]{3,2,1,0:T(8,128)(2,1)S(1)}, bf16[12,8,128,128]{3,2,1,0:T(8,128)(2,1)}, u32[]{:S(2)}) copy-start(bf16[12,8,128,128]{3,2,1,0:T(8,128)(2,1)} %copy-done) | copy-start | bytes 9437188
  16.9 1.3 %copy-start.3 = (bf16[12,128,256]{2,1,0:T(8,128)(2,1)S(1)}, bf16[12,128,256]{2,1,0:T(8,128)(2,1)}, u32[]{:S(2)}) copy-start(bf16[12,128,256]{2,1,0:T(8,128)(2,1)} %copy-done.2) | copy-start | bytes 2359300
  18.2 1.1 copy-start.6
  19.3 0.9 copy-start.16
  22.6 3.2 %copy-start.11 = (bf16[4,8,128,128]{3,2,1,0:T(8,128)(2,1)S(1)}, bf16[4,8,128,128]{3,2,1,0:T(8,128)(2,1)}, u32[]{:S(2)}) copy-start(bf16[4,8,128,128]{3,2,1,0:T(8,128)(2,1)} %copy-done.10) | copy-start | bytes 3145732
  22.6 4.9 %collective-permute-start.1 = (bf16[4,128,256]{2,1,0:T(8,128)(2,1)S(1)}, bf16[4,128,256]{2,1,0:T(8,128)(2,1)S(1)}, u32[]{:S(2)}, u32[]{:S(2)}) collective-permute-start(bf16[4,128,256]{2,1,0:T(8,128)(2,1)S(1)} %copy-done.16), channel_id=1, source_target_pairs={{1,2},{2,1},{3,4},{4,3},{5,6},{6,5},{7,8},{8,7},{9,10},{10,9},{11,... | collective-permute-start | bytes 786440 | tf_op jit(solution)/shard_map/ppermute | solution.py:429
  25.8 8.8 %copy-start.9 = (bf16[4,8,128,128]{3,2,1,0:T(8,128)(2,1)S(1)}, bf16[4,8,128,128]{3,2,1,0:T(8,128)(2,1)}, u32[]{:S(2)}) copy-start(bf16[4,8,128,128]{3,2,1,0:T(8,128)(2,1)} %copy-done.8) | copy-start | bytes 3145732
  25.8 10.1 %copy-start.7 = (bf16[12,128,256]{2,1,0:T(8,128)(2,1)S(1)}, bf16[12,128,256]{2,1,0:T(8,128)(2,1)}, u32[]{:S(2)}) copy-start(bf16[12,128,256]{2,1,0:T(8,128)(2,1)} %copy-done.5) | copy-start | bytes 2359300
  27.5 12.5 %collective-permute-start.2 = (bf16[4,128,256]{2,1,0:T(8,128)(2,1)S(1)}, bf16[4,128,256]{2,1,0:T(8,128)(2,1)S(1)}, u32[]{:S(2)}, u32[]{:S(2)}) collective-permute-start(bf16[4,128,256]{2,1,0:T(8,128)(2,1)S(1)} %rows_even.3.refs_0_.refs_1_.refs_4_), channel_id=1, source_target_pairs={{0,1},{1,0},{2,3},{3,2},{4,5},{5,4},{6,7},{7,6},{8,9},{9,8},{10,11... | collective-permute-start | bytes 786440 | tf_op jit(solution)/shard_map/ppermute | solution.py:429
  35.9 4.7 %copy-start.4 = (bf16[12,128,256]{2,1,0:T(8,128)(2,1)S(1)}, bf16[12,128,256]{2,1,0:T(8,128)(2,1)}, u32[]{:S(2)}) copy-start(bf16[12,128,256]{2,1,0:T(8,128)(2,1)} %copy-done.2) | copy-start | bytes 2359300
  40.0 4.4 %collective-permute-start.3 = (bf16[4,128,256]{2,1,0:T(8,128)(2,1)S(1)}, bf16[4,128,256]{2,1,0:T(8,128)(2,1)S(1)}, u32[]{:S(2)}, u32[]{:S(2)}) collective-permute-start(bf16[4,128,256]{2,1,0:T(8,128)(2,1)S(1)} %rows_odd.3.refs_1_.refs_4_), channel_id=1, source_target_pairs={{1,2},{2,1},{3,4},{4,3},{5,6},{6,5},{7,8},{8,7},{9,10},{10,9},{11,... | collective-permute-start | bytes 786440 | tf_op jit(solution)/shard_map/ppermute | solution.py:429
  44.5 13.0 %collective-permute-start.4 = (bf16[4,128,256]{2,1,0:T(8,128)(2,1)S(1)}, bf16[4,128,256]{2,1,0:T(8,128)(2,1)S(1)}, u32[]{:S(2)}, u32[]{:S(2)}) collective-permute-start(bf16[4,128,256]{2,1,0:T(8,128)(2,1)S(1)} %rows_even.4.refs_0_.refs_1_), channel_id=1, source_target_pairs={{0,1},{1,0},{2,3},{3,2},{4,5},{5,4},{6,7},{7,6},{8,9},{9,8},{10,11... | collective-permute-start | bytes 786440 | tf_op jit(solution)/shard_map/ppermute | solution.py:429
  57.4 2.8 %collective-permute-start.6 = (bf16[1536,256]{1,0:T(8,128)(2,1)S(1)}, bf16[1536,256]{1,0:T(8,128)(2,1)S(1)}, u32[]{:S(2)}, u32[]{:S(2)}) collective-permute-start(bf16[1536,256]{1,0:T(8,128)(2,1)S(1)} %bitcast.12), channel_id=1, source_target_pairs={{0,16},{16,0},{1,17},{17,1},{2,18},{18,2},{3,19},{19,3},{4,20},{20... | collective-permute-start | bytes 2359304 | tf_op jit(solution)/shard_map/ppermute | solution.py:432
  57.5 3.4 %collective-permute-start.7 = (bf16[1536,256]{1,0:T(8,128)(2,1)S(1)}, bf16[1536,256]{1,0:T(8,128)(2,1)S(1)}, u32[]{:S(2)}, u32[]{:S(2)}) collective-permute-start(bf16[1536,256]{1,0:T(8,128)(2,1)S(1)} %bitcast.9), channel_id=1, source_target_pairs={{0,16},{16,0},{1,17},{17,1},{2,18},{18,2},{3,19},{19,3},{4,20},{20... | collective-permute-start | bytes 2359304 | tf_op jit(solution)/shard_map/ppermute | solution.py:432
  58.0 4.3 %collective-permute-start.5 = (bf16[4,128,256]{2,1,0:T(8,128)(2,1)S(1)}, bf16[4,128,256]{2,1,0:T(8,128)(2,1)S(1)}, u32[]{:S(2)}, u32[]{:S(2)}) collective-permute-start(bf16[4,128,256]{2,1,0:T(8,128)(2,1)S(1)} %rows_odd.4.refs_1_), channel_id=1, source_target_pairs={{1,2},{2,1},{3,4},{4,3},{5,6},{6,5},{7,8},{8,7},{9,10},{10,9},{11,... | collective-permute-start | bytes 786440 | tf_op jit(solution)/shard_map/ppermute | solution.py:429
  63.7 1.6 %collective-permute-start.9 = (bf16[512,256]{1,0:T(8,128)(2,1)S(1)}, bf16[512,256]{1,0:T(8,128)(2,1)S(1)}, u32[]{:S(2)}, u32[]{:S(2)}) collective-permute-start(bf16[512,256]{1,0:T(8,128)(2,1)S(1)} %bitcast.18), channel_id=1, source_target_pairs={{0,16},{16,0},{1,17},{17,1},{2,18},{18,2},{3,19},{19,3},{4,20},{20... | collective-permute-start | bytes 786440 | tf_op jit(solution)/shard_map/ppermute | solution.py:432
  63.9 1.8 %collective-permute-start.8 = (bf16[512,256]{1,0:T(8,128)(2,1)S(1)}, bf16[512,256]{1,0:T(8,128)(2,1)S(1)}, u32[]{:S(2)}, u32[]{:S(2)}) collective-permute-start(bf16[512,256]{1,0:T(8,128)(2,1)S(1)} %bitcast.15), channel_id=1, source_target_pairs={{0,16},{16,0},{1,17},{17,1},{2,18},{18,2},{3,19},{19,3},{4,20},{20... | collective-permute-start | bytes 786440 | tf_op jit(solution)/shard_map/ppermute | solution.py:432
  66.7 11.7 %collective-permute-start.10 = (f32[160,128]{1,0:T(8,128)S(1)}, f32[160,128]{1,0:T(8,128)S(1)}, u32[]{:S(2)}, u32[]{:S(2)}) collective-permute-start(f32[160,128]{1,0:T(8,128)S(1)} %get-tuple-element.54), channel_id=1, source_target_pairs={{0,1},{1,0},{2,3},{3,2},{4,5},{5,4},{6,7},{7,6},{8,9},{9,8},{10,11... | collective-permute-start | bytes 245768 | tf_op jit(solution)/shard_map/ppermute | solution.py:272
  75.2 6.6 %collective-permute-start.11 = (f32[160,128]{1,0:T(8,128)S(1)}, f32[160,128]{1,0:T(8,128)S(1)}, u32[]{:S(2)}, u32[]{:S(2)}) collective-permute-start(f32[160,128]{1,0:T(8,128)S(1)} %get-tuple-element.55), channel_id=1, source_target_pairs={{0,2},{1,3},{2,0},{3,1},{4,6},{5,7},{6,4},{7,5},{8,10},{9,11},{10,... | collective-permute-start | bytes 245768 | tf_op jit(solution)/shard_map/ppermute | solution.py:272
  78.3 5.3 %collective-permute-start.12 = (f32[160,128]{1,0:T(8,128)S(1)}, f32[160,128]{1,0:T(8,128)S(1)}, u32[]{:S(2)}, u32[]{:S(2)}) collective-permute-start(f32[160,128]{1,0:T(8,128)S(1)} %get-tuple-element.56), channel_id=1, source_target_pairs={{0,3},{1,2},{2,1},{3,0},{4,7},{5,6},{6,5},{7,4},{8,11},{9,10},{10,... | collective-permute-start | bytes 245768 | tf_op jit(solution)/shard_map/ppermute | solution.py:272
  83.7 6.6 %collective-permute-start.15 = (f32[160,128]{1,0:T(8,128)S(1)}, f32[160,128]{1,0:T(8,128)S(1)}, u32[]{:S(2)}, u32[]{:S(2)}) collective-permute-start(f32[160,128]{1,0:T(8,128)S(1)} %add_four.2.a), channel_id=1, source_target_pairs={{0,12},{1,13},{2,14},{3,15},{4,8},{5,9},{6,10},{7,11},{8,4},{9,5},... | collective-permute-start | bytes 245768 | tf_op jit(solution)/shard_map/ppermute | solution.py:272
  85.2 7.5 %collective-permute-start.14 = (f32[160,128]{1,0:T(8,128)S(1)}, f32[160,128]{1,0:T(8,128)S(1)}, u32[]{:S(2)}, u32[]{:S(2)}) collective-permute-start(f32[160,128]{1,0:T(8,128)S(1)} %add_four.2.a), channel_id=1, source_target_pairs={{0,8},{1,9},{2,10},{3,11},{4,12},{5,13},{6,14},{7,15},{8,0},{9,1},... | collective-permute-start | bytes 245768 | tf_op jit(solution)/shard_map/ppermute | solution.py:272
  86.0 6.8 %collective-permute-start.13 = (f32[160,128]{1,0:T(8,128)S(1)}, f32[160,128]{1,0:T(8,128)S(1)}, u32[]{:S(2)}, u32[]{:S(2)}) collective-permute-start(f32[160,128]{1,0:T(8,128)S(1)} %add_four.2.a), channel_id=1, source_target_pairs={{0,4},{1,5},{2,6},{3,7},{4,0},{5,1},{6,2},{7,3},{8,12},{9,13},{10,... | collective-permute-start | bytes 245768 | tf_op jit(solution)/shard_map/ppermute | solution.py:272
  92.7 5.5 %collective-permute-start.18 = (f32[160,128]{1,0:T(8,128)S(1)}, f32[160,128]{1,0:T(8,128)S(1)}, u32[]{:S(2)}, u32[]{:S(2)}) collective-permute-start(f32[160,128]{1,0:T(8,128)S(1)} %add_four.3.refs_0_), channel_id=1, source_target_pairs={{0,3},{1,2},{2,1},{3,0},{4,7},{5,6},{6,5},{7,4},{8,11},{9,10},{10,... | collective-permute-start | bytes 245768 | tf_op jit(solution)/shard_map/ppermute | solution.py:272
  93.3 5.6 %collective-permute-start.17 = (f32[160,128]{1,0:T(8,128)S(1)}, f32[160,128]{1,0:T(8,128)S(1)}, u32[]{:S(2)}, u32[]{:S(2)}) collective-permute-start(f32[160,128]{1,0:T(8,128)S(1)} %add_four.3.refs_0_), channel_id=1, source_target_pairs={{0,2},{1,3},{2,0},{3,1},{4,6},{5,7},{6,4},{7,5},{8,10},{9,11},{10,... | collective-permute-start | bytes 245768 | tf_op jit(solution)/shard_map/ppermute | solution.py:272
  95.6 4.4 %collective-permute-start.16 = (f32[160,128]{1,0:T(8,128)S(1)}, f32[160,128]{1,0:T(8,128)S(1)}, u32[]{:S(2)}, u32[]{:S(2)}) collective-permute-start(f32[160,128]{1,0:T(8,128)S(1)} %add_four.3.refs_0_), channel_id=1, source_target_pairs={{0,1},{1,0},{2,3},{3,2},{4,5},{5,4},{6,7},{7,6},{8,9},{9,8},{10,11... | collective-permute-start | bytes 245768 | tf_op jit(solution)/shard_map/ppermute | solution.py:272
  96.3 3.7 %collective-permute-start.19 = (f32[160,128]{1,0:T(8,128)S(1)}, f32[160,128]{1,0:T(8,128)S(1)}, u32[]{:S(2)}, u32[]{:S(2)}) collective-permute-start(f32[160,128]{1,0:T(8,128)S(1)} %add_four.3.refs_0_), channel_id=1, source_target_pairs={{0,16},{16,0},{1,17},{17,1},{2,18},{18,2},{3,19},{19,3},{4,20},{20... | collective-permute-start | bytes 245768 | tf_op jit(solution)/shard_map/ppermute | solution.py:432
  98.2 1.8 %collective-permute-start.22 = (f32[160,128]{1,0:T(8,128)S(1)}, f32[160,128]{1,0:T(8,128)S(1)}, u32[]{:S(2)}, u32[]{:S(2)}) collective-permute-start(f32[160,128]{1,0:T(8,128)S(1)} %collective-permute-done.18.refs_3_), channel_id=1, source_target_pairs={{0,16},{16,0},{1,17},{17,1},{2,18},{18,2},{3,19},{19,3},{4,20},{20... | collective-permute-start | bytes 245768 | tf_op jit(solution)/shard_map/ppermute | solution.py:432
  98.9 1.3 %collective-permute-start.21 = (f32[160,128]{1,0:T(8,128)S(1)}, f32[160,128]{1,0:T(8,128)S(1)}, u32[]{:S(2)}, u32[]{:S(2)}) collective-permute-start(f32[160,128]{1,0:T(8,128)S(1)} %collective-permute-done.17.refs_2_), channel_id=1, source_target_pairs={{0,16},{16,0},{1,17},{17,1},{2,18},{18,2},{3,19},{19,3},{4,20},{20... | collective-permute-start | bytes 245768 | tf_op jit(solution)/shard_map/ppermute | solution.py:432
  100.0 1.3 %collective-permute-start.20 = (f32[160,128]{1,0:T(8,128)S(1)}, f32[160,128]{1,0:T(8,128)S(1)}, u32[]{:S(2)}, u32[]{:S(2)}) collective-permute-start(f32[160,128]{1,0:T(8,128)S(1)} %collective-permute-done.16.refs_1_), channel_id=1, source_target_pairs={{0,16},{16,0},{1,17},{17,1},{2,18},{18,2},{3,19},{19,3},{4,20},{20... | collective-permute-start | bytes 245768 | tf_op jit(solution)/shard_map/ppermute | solution.py:432

commit v3 on v2

--- a/solution.py
+++ b/solution.py
@@ -43,13 +43,20 @@
     return 1 - odd if name == "even" else odd
 
 
-def first_edge_kernel(info, whole_ref, out_ref, sem):
+def edges_kernel(info, whole_ref, even_ref, odd_ref, sem):
     edge, tiles = HALO_T, whole_ref.shape[0]
-    first = at_end("even", info) * (tiles - edge)
-    copy = pltpu.make_async_copy(whole_ref.at[pl.ds(first, edge)], out_ref, sem)
-    copy.start()
-    copy.wait()
-    clear_dead(out_ref, first, info[LIVE])
+    outs = {"even": even_ref, "odd": odd_ref}
+    firsts = {name: at_end(name, info) * (tiles - edge) for name in outs}
+    copies = [
+        pltpu.make_async_copy(whole_ref.at[pl.ds(firsts[name], edge)], outs[name], sem.at[i])
+        for i, name in enumerate(outs)
+    ]
+    for copy in copies:
+        copy.start()
+    for copy in copies:
+        copy.wait()
+    for name in outs:
+        clear_dead(outs[name], firsts[name], info[LIVE])
 
 
 def clear_dead(ref, first, live):
@@ -62,17 +69,15 @@
 
 
 def prepare_kernel(info, whole_ref, blocks_ref, *refs):
-    odd_ref, low_ref, high_ref = refs[:3]
-    even_blocks, odd_blocks, low_blocks, high_blocks, sem = refs[3:]
+    low_ref, high_ref, even_blocks, odd_blocks, low_blocks, high_blocks, sem = refs
     edge, tiles = HALO_T, whole_ref.shape[0]
     half = tiles // 2 - edge
-    even_row = at_end("even", info) * (tiles - edge)
-    odd_row = at_end("odd", info) * (tiles - edge)
     moves = [
         (whole_ref, edge, low_ref), (whole_ref, edge + half, high_ref),
-        (blocks_ref, edge, low_blocks), (whole_ref, odd_row, odd_ref),
-        (blocks_ref, even_row, even_blocks), (blocks_ref, edge + half, high_blocks),
-        (blocks_ref, odd_row, odd_blocks),
+        (blocks_ref, edge, low_blocks),
+        (blocks_ref, at_end("even", info) * (tiles - edge), even_blocks),
+        (blocks_ref, edge + half, high_blocks),
+        (blocks_ref, at_end("odd", info) * (tiles - edge), odd_blocks),
     ]
     copies = [
         pltpu.make_async_copy(source.at[pl.ds(first, target.shape[0])], target, sem.at[i])
@@ -85,38 +90,36 @@
     live = info[LIVE]
     clear_dead(low_ref, edge, live)
     clear_dead(high_ref, edge + half, live)
-    clear_dead(odd_ref, odd_row, live)
-
-
-def first_edge(info, start):
+
+
+def masked_edges(info, start):
     _, tile, width = start.shape
     return pl.pallas_call(
-        first_edge_kernel,
+        edges_kernel,
         in_specs=[SMEM, HBM],
-        out_specs=VMEM,
-        out_shape=jax.ShapeDtypeStruct((HALO_T, tile, width), BF16),
-        scratch_shapes=[pltpu.SemaphoreType.DMA],
-        compiler_params=SMALL_VMEM,
+        out_specs=[VMEM] * 2,
+        out_shape=[jax.ShapeDtypeStruct((HALO_T, tile, width), BF16)] * 2,
+        scratch_shapes=[pltpu.SemaphoreType.DMA((2,))],
+        compiler_params=pltpu.CompilerParams(vmem_limit_bytes=4 * 1024 * 1024),
         cost_estimate=SMALL,
-        name="first_edge",
+        name="masked_edges",
     )(info, start)
 
 
 def prepare(info, start, blocks):
     tiles, tile, width = start.shape
     half = tiles // 2 - HALO_T
-    counts = (HALO_T, half, half)
     block_counts = (HALO_T, HALO_T, half, half)
-    shapes = [jax.ShapeDtypeStruct((count, tile, width), BF16) for count in counts]
+    shapes = [jax.ShapeDtypeStruct((half, tile, width), BF16)] * 2
     shapes += [
         jax.ShapeDtypeStruct((count,) + blocks.shape[1:], blocks.dtype) for count in block_counts
     ]
     return pl.pallas_call(
         prepare_kernel,
         in_specs=[SMEM, HBM, HBM],
-        out_specs=[VMEM] * 7,
+        out_specs=[VMEM] * 6,
         out_shape=shapes,
-        scratch_shapes=[pltpu.SemaphoreType.DMA((7,))],
+        scratch_shapes=[pltpu.SemaphoreType.DMA((6,))],
         compiler_params=pltpu.CompilerParams(vmem_limit_bytes=16 * 1024 * 1024),
         cost_estimate=SMALL,
         name="prepare",
@@ -156,7 +159,7 @@
     def group(index, carry):
         for r in range(GROUP):
             row = index * GROUP + r
-            listed = [cols_ref[first + row, n] - shift for n in range(nnz)]
+            listed = [cols_ref[(first + row) * nnz + n] - shift for n in range(nnz)]
             acc = tile_row(lambda n: blocks_ref[row, n], listed, lambda c: held[c])
             prev = None if prev_ref is None else prev_ref[row]
             out_ref[row] = finish(acc, prev, first + row < live)
@@ -166,8 +169,8 @@
 
 
 def tile_rows(name, info, cols, blocks, pieces, prev):
-    rows, _, tile, _ = blocks.shape
-    tiles = cols.shape[0]
+    rows, nnz, tile, _ = blocks.shape
+    tiles = cols.shape[0] // nnz
     width = pieces[0].shape[-1]
     edge, half = HALO_T, tiles // 2 - HALO_T
     if name in ("even", "odd"):
@@ -284,15 +287,49 @@
     return high, (value - high.astype(F32)).astype(BF16)
 
 
-def product3(left, right_stack):
-    high, low = split(left)
-    return dot(jnp.concatenate([high, high, low], axis=1), right_stack)
+def put_left(ref, row, col, value):
+    size, width = ref.shape[0], value.shape[0]
+    high, low = split(value)
+    for i, piece in enumerate((high, high, low)):
+        ref[pl.ds(row * width, width), pl.ds(i * size + col * width, width)] = piece
+
+
+def put_right(ref, row, col, value):
+    size, width = ref.shape[1], value.shape[0]
+    high, low = split(value)
+    for i, piece in enumerate((high, low, high)):
+        ref[pl.ds(i * size + row * width, width), pl.ds(col * width, width)] = piece
+
+
+def put_symmetric(put, ref, blocks):
+    first, across, second = blocks
+    put(ref, 0, 0, first)
+    put(ref, 0, 1, across)
+    put(ref, 1, 0, across.T)
+    put(ref, 1, 1, second)
+
+
+def product(left_ref, right_ref):
+    width = left_ref.shape[0] // 2
+    second = dot(left_ref[...], right_ref[:, width:])
+    first = dot(left_ref[:width, :], right_ref[:, :width])
+    return first, second[:width], second[width:]
+
+
+def middle(blocks):
+    first, across, second = blocks
+    row = lax.broadcasted_iota(jnp.int32, first.shape, 0)
+    col = lax.broadcasted_iota(jnp.int32, first.shape, 1)
+    diagonal = jnp.where(row == col, 1.5, 0.0)
+    return diagonal - 0.5 * first, -0.5 * across, diagonal - 0.5 * second
 
 
 def finish_kernel(total_rows, chunk, info, *refs):
     mine, theirs = refs[:WAYS], refs[WAYS : 2 * WAYS]
     fields, out_ref = refs[2 * WAYS : 2 * WAYS + 8], refs[2 * WAYS + 8]
-    shares, x_ref, z_ref, m_ref, stack, wide, result, sem, out_sem = refs[2 * WAYS + 9 :]
+    shares, x_ref, x_left, w_left, z_left, m_right, wide, result, sem, out_sem = refs[
+        2 * WAYS + 9 :
+    ]
     part, quarter = info[PART], info[PATCH] % WAYS
     size = x_ref.shape[0]
     width = size // 2
@@ -306,7 +343,8 @@
     copies = []
     for i, source in enumerate(fields):
         rows = pl.ds(pl.multiple_of(starts[i % 4], edge_size), source.shape[0])
-        target = wide.at[rows, pl.ds(i // 4 * width, width)]
+        side = part if i < 4 else 1 - part
+        target = wide.at[rows, pl.ds(pl.multiple_of(side * width, width), width)]
         copies.append(pltpu.make_async_copy(source, target, sem.at[i]))
     for copy in copies:
         copy.start()
@@ -322,51 +360,42 @@
 
     def place(row, col, value):
         x_ref[pl.ds(row * half, half), pl.ds(col * half, half)] = value
-        if row != col:
-            x_ref[pl.ds(col * half, half), pl.ds(row * half, half)] = value.T
 
     for side in range(2):
+        across = block(side, 1)
         place(2 * side, 2 * side, block(side, 0))
-        place(2 * side, 2 * side + 1, block(side, 1))
+        place(2 * side, 2 * side + 1, across)
+        place(2 * side + 1, 2 * side, across.T)
         place(2 * side + 1, 2 * side + 1, block(side, 2))
         place(side, 2, block(side, 3))
         place(side, 3, block(side, 4))
 
-    gram = x_ref[...]
-    norm = jnp.sqrt(jnp.sum(gram * gram, keepdims=True))
-    x_ref[...] = gram / norm
-
-    def set_middle():
-        x = x_ref[...]
-        row = lax.broadcasted_iota(jnp.int32, x.shape, 0)
-        col = lax.broadcasted_iota(jnp.int32, x.shape, 1)
-        middle = jnp.where(row == col, 1.5, 0.0) - 0.5 * x
-        high, low = split(middle)
-        stack[0:size, :] = high
-        stack[size : 2 * size, :] = low
-        stack[2 * size :, :] = high
-        return middle
-
-    def step_x():
-        m_ref[...] = product3(x_ref[...], stack[...])
-        x_ref[...] = product3(m_ref[...], stack[...])
-
-    z_ref[...] = set_middle()
-    step_x()
+    gram = x_ref[:width, :width], x_ref[:width, width:], x_ref[width:, width:]
+    squares = gram[0] * gram[0] + 2.0 * (gram[1] * gram[1]) + gram[2] * gram[2]
+    norm = jnp.sqrt(jnp.sum(squares, keepdims=True))
+    x = tuple(value / norm for value in gram)
+    put_symmetric(put_left, x_left, x)
+    factors = middle(x)
+    put_symmetric(put_right, m_right, factors)
+    put_symmetric(put_left, z_left, factors)
+
+    def advance(first):
+        put_symmetric(put_left, w_left, product(x_left, m_right))
+        if not first:
+            put_symmetric(put_left, z_left, product(z_left, m_right))
+        x = product(w_left, m_right)
+        put_symmetric(put_left, x_left, x)
+        put_symmetric(put_right, m_right, middle(x))
+
+    advance(True)
 
     def sweep(index, carry):
-        set_middle()
-        z_ref[...] = product3(z_ref[...], stack[...])
-        step_x()
+        advance(False)
         return carry
 
     lax.fori_loop(1, ITERS - 1, sweep, 0)
-    set_middle()
-    z_ref[...] = product3(z_ref[...], stack[...])
-
     own = pl.ds(pl.multiple_of(part * width, width), width)
-    other = pl.ds(pl.multiple_of((1 - part) * width, width), width)
-    rotation = jnp.concatenate([z_ref[own, own], z_ref[other, own]], axis=0).astype(BF16)
+    rotation = dot(z_left[...], m_right[:, own]).astype(BF16)
     factor = jnp.sqrt(total_rows / norm)
     for copy in copies:
         copy.wait()
@@ -387,7 +416,7 @@
     size = 2 * width
     chunk = min(rows, 512)
     body = functools.partial(finish_kernel, float(total_rows), chunk)
-    matrix = pltpu.VMEM((size, size), F32)
+    left = pltpu.VMEM((size, 3 * size), BF16)
     return pl.pallas_call(
         body,
         in_specs=[SMEM] + [VMEM] * (2 * WAYS) + [ANY] * 8,
@@ -395,7 +424,8 @@
         out_shape=jax.ShapeDtypeStruct((rows, width), BF16),
         scratch_shapes=[
             pltpu.VMEM((2, 5 * width // 2, width // 2), F32),
-            matrix, matrix, matrix,
+            pltpu.VMEM((size, size), F32),
+            left, left, left,
             pltpu.VMEM((3 * size, size), BF16),
             pltpu.VMEM((rows, size), BF16),
             pltpu.VMEM((rows, width), BF16),
@@ -435,37 +465,41 @@
     scalars = [lax.axis_index("cols"), lax.axis_index("patch"), live_tiles[0]]
     info = jnp.stack(scalars).astype(jnp.int32)
 
-    even = first_edge(info, start)
-    even_halo = exchange("even", even)
+    cols = tile_cols.reshape(-1)
+
+    even, odd = masked_edges(after(info, cols), start)
+    even_halo, odd_halo = exchange("even", even), exchange("odd", odd)
     ready = prepare(after(info, even), start, blocks)
-    odd, low, high = ready[:3]
-    stored = dict(zip(("even", "odd", "low", "high"), ready[3:]))
+    low, high = ready[:2]
+    stored = dict(zip(("even", "odd", "low", "high"), ready[2:]))
     prev = dict.fromkeys(stored)
 
     def rows(name, *pieces):
-        return tile_rows(name, info, tile_cols, stored[name], pieces, prev[name])
+        return tile_rows(name, info, cols, stored[name], pieces, prev[name])
 
     for step in range(STEPS):
+        final = step == STEPS - 1
         new_low = rows("low", even, odd, low, high)
         even_halo = after(even_halo, new_low)
-        odd_halo = exchange("odd", after(odd, even_halo))
         new_even = rows("even", even_halo, even, low, high)
+        if not final:
+            even_halo = exchange("even", new_even)
         new_high = rows("high", even, odd, low, high)
-        if step == STEPS - 1:
+        if final:
             flat = [value.reshape(-1, width) for value in (new_even, new_low, new_high)]
-            others = [sibling(after(value, even_halo)) for value in flat[1:]]
-            share = gram_share(info, flat[1:], others, None)
-            others.insert(0, sibling(after(flat[0], share)))
-            odd_halo = after(odd_halo, new_even, new_high, share)
+            others = [sibling(after(value, new_even)) for value in flat]
+            share = gram_share(info, flat, others, None)
+            odd_halo = after(odd_halo, share)
         else:
             odd_halo = after(odd_halo, new_even, new_high)
-            even_halo = exchange("even", after(new_even, odd_halo))
         new_odd = rows("odd", odd_halo, odd, low, high)
+        if not final:
+            odd_halo = exchange("odd", new_odd)
         prev = {"even": even, "odd": odd, "low": low, "high": high}
         even, odd, low, high = new_even, new_odd, new_low, new_high
     last = odd.reshape(-1, width)
     other_last = sibling(last)
-    parts = gram_share(info, [flat[0], last], [others[0], other_last], share)
+    parts = gram_share(info, [last], [other_last], share)
     mine = sum_over_patch(parts)
     theirs = [sibling(value) for value in mine]
     total_rows = tiles * tile * count

time: 125 us -> 105 us (0.84)
  starting transfers between devices: 40.1 us -> 30 us
  local copies, waits for them, and re-layouts: 14.6 us -> 5.82 us
  Pallas kernels: 50 us -> 45.2 us
  waiting for transfers between devices: 18.7 us -> 22.5 us
    ppermute x6, starting transfers between devices: 19.3 us -> 10.1 us  [exchange(): return lax.ppermute(value, 'patch', pairs[name])]
    unnamed x37 -> x7, local copies, waits for them, and re-layouts: 14.6 us -> 5.74 us
    pallas_call x12, Pallas kernels: 22.5 us -> 19.3 us  [tile_rows(): pl.pallas_call(functools.partial(rows_kernel, name, counts, tiles), in_sp...]
    pallas_call x1, Pallas kernels: 23.2 us -> 20.2 us  [rotate(): pl.pallas_call(body, in_specs=[SMEM] + [VMEM] * (2 * WAYS) + [ANY] * 8, o...]
    ppermute x6, waiting for transfers between devices: 1.74 us -> 3.59 us  [exchange(): return lax.ppermute(value, 'patch', pairs[name])]
    ppermute x8, waiting for transfers between devices: 3.34 us -> 5.01 us  [sibling(): return lax.ppermute(value, 'cols', [(0, 1), (1, 0)])]
  transfers between devices with their start and end apart: 23 -> 23, of which waited for: 13 -> 12; matrix products, arithmetic and copies ran while one was open for 0% -> 0% of each run, Pallas kernels for 19% -> 20%
where the time goes in v3:
time: 105 us
  Pallas kernels  45.2 us (43%)
  starting transfers between devices  30 us (29%)
  waiting for transfers between devices  22.5 us (21%)
  local copies, waits for them, and re-layouts  5.82 us (6%)
  between operations  1.06 us (1%)
    pallas_call x1, Pallas kernels, rotate(): pl.pallas_call(body, in_specs=[SMEM] + [VMEM] * (2 * WAYS) + [ANY] * 8, o...  20.2 us
    pallas_call x12, Pallas kernels, tile_rows(): pl.pallas_call(functools.partial(rows_kernel, name, counts, tiles), in_sp...  19.3 us
    ppermute x9, starting transfers between devices, exchange(): lax.ppermute(value, 'patch', [(i, i ^ distance) for i in range(count)])  19.1 us
    ppermute x9, waiting for transfers between devices, exchange(): lax.ppermute(value, 'patch', [(i, i ^ distance) for i in range(count)])  13.9 us
    ppermute x6, starting transfers between devices, exchange(): return lax.ppermute(value, 'patch', pairs[name])  10.1 us
    unnamed x7, local copies, waits for them, and re-layouts  5.74 us
    ppermute x8, waiting for transfers between devices, sibling(): return lax.ppermute(value, 'cols', [(0, 1), (1, 0)])  5.01 us
    ppermute x6, waiting for transfers between devices, exchange(): return lax.ppermute(value, 'patch', pairs[name])  3.59 us
  transfers between devices with their start and end apart: 23, of which 12 were waited for; matrix products, arithmetic and copies ran while one was open for 0% of the time, Pallas kernels for 20%

profile of v3, /device:TPU:0, one launch (start us, length us, event | category | flops | bytes accessed | tf_op | source)
XLA Modules:
  0.0 104.7 jit_solution(13214328416972248194)
XLA Ops:
  0.7 0.8 copy.5
  1.4 0.1 reshape.18.cols_ref
  1.5 0.1 pad_add_fusion.info
  1.6 1.6 %copy-done.1 = bf16[4096,256]{1,0:T(8,128)(2,1)S(1)} copy-done((bf16[4096,256]{1,0:T(8,128)(2,1)S(1)}, bf16[4096,256]{1,0:T(8,128)(2,1)}, u32[]{:S(2)}) %copy-start.1) | copy-done | bytes 2097176
  3.2 0.7 masked_edges.1
  3.8 3.0 %collective-permute-start.1 = (bf16[4,128,256]{2,1,0:T(8,128)(2,1)S(1)}, bf16[4,128,256]{2,1,0:T(8,128)(2,1)S(1)}, u32[]{:S(2)}, u32[]{:S(2)}) collective-permute-start(bf16[4,128,256]{2,1,0:T(8,128)(2,1)S(1)} %get-tuple-element.30.refs_0_.refs_1_.refs_4_), channel_id=1, source_target_pairs={{0,1},{1,0},{2,3},{3,2},{4,5},{5,4},{6,7},{7,6},{8,9},{9,8},{10,11... | collective-permute-start | bytes 786440 | tf_op jit(solution)/shard_map/ppermute | solution.py:459
  6.8 0.7 collective-permute-start
  7.5 0.0 copy-start
  7.5 3.4 %copy-done = bf16[32,8,128,128]{3,2,1,0:T(8,128)(2,1)S(1)} copy-done((bf16[32,8,128,128]{3,2,1,0:T(8,128)(2,1)S(1)}, bf16[32,8,128,128]{3,2,1,0:T(8,128)(2,1)}, u32[]{:S(2)}) %copy-start) | copy-done | bytes 8388632
  10.9 1.4 %prepare.1 = (bf16[12,128,256]{2,1,0:T(8,128)(2,1)S(1)}, bf16[12,128,256]{2,1,0:T(8,128)(2,1)S(1)}, bf16[4,8,128,128]{3,2,1,0:T(8,128)(2,1)S(1)}, bf16[4,8,128,1...) custom-call(s32[3]{0:T(128)S(1)} %pad_add_fusion.info, ...), custom_call_target="tpu_custom_call" | custom-call | flops 1000 | bytes 1000 | tf_op jit(solution)/shard_map/prepare/pallas_call | solution.py:117
  12.3 2.1 %rows_low.3.refs_2_.refs_4_ = bf16[12,128,256]{2,1,0:T(8,128)(2,1)S(1)} custom-call(s32[3]{0:T(128)S(1)} %pad_add_fusion.info, s32[256]{0:T(256)S(1)} %reshape.18.cols_ref, bf16[4,128,256]{2,1,0:T(8,128)(2,1)S(1)} %get-tuple-element.30.refs_0_.refs_1_.refs_4_, bf16[4,128,256]{2,1,0:T(8,128)(2,1)S(1)} %get-tuple-element.29.refs_1_.refs_4_, ...), custom_call_target="tpu_custom_call" | custom-call | flops 1000 | bytes 1000 | tf_op jit(solution)/shard_map/rows_low/pallas_call | solution.py:183
  14.4 3.6 %collective-permute-done.1.refs_0_ = bf16[4,128,256]{2,1,0:T(8,128)(2,1)S(1)} collective-permute-done((bf16[4,128,256]{2,1,0:T(8,128)(2,1)S(1)}, bf16[4,128,256]{2,1,0:T(8,128)(2,1)S(1)}, u32[]{:S(2)}, u32[]{:S(2)}) %collective-permute-start.1) | collective-permute-done | bytes 262176 | tf_op jit(solution)/shard_map/ppermute | solution.py:459
  18.0 1.1 %rows_even.3.refs_0_.refs_1_.refs_4_ = bf16[4,128,256]{2,1,0:T(8,128)(2,1)S(1)} custom-call(s32[3]{0:T(128)S(1)} %pad_add_fusion.info, s32[256]{0:T(256)S(1)} %reshape.18.cols_ref, bf16[4,128,256]{2,1,0:T(8,128)(2,1)S(1)} %collective-permute-done.1.refs_0_, bf16[4,128,256]{2,1,0:T(8,128)(2,1)S(1)} %get-tuple-element.30.refs_0_.refs_1_.refs_4_, ...), custom_call_target="tpu_custom_call" | custom-call | flops 1000 | bytes 1000 | tf_op jit(solution)/shard_map/rows_even/pallas_call | solution.py:183
  19.1 2.5 %collective-permute-start.3 = (bf16[4,128,256]{2,1,0:T(8,128)(2,1)S(1)}, bf16[4,128,256]{2,1,0:T(8,128)(2,1)S(1)}, u32[]{:S(2)}, u32[]{:S(2)}) collective-permute-start(bf16[4,128,256]{2,1,0:T(8,128)(2,1)S(1)} %rows_even.3.refs_0_.refs_1_.refs_4_), channel_id=1, source_target_pairs={{0,1},{1,0},{2,3},{3,2},{4,5},{5,4},{6,7},{7,6},{8,9},{9,8},{10,11... | collective-permute-start | bytes 786440 | tf_op jit(solution)/shard_map/ppermute | solution.py:459
  21.7 2.1 %rows_high.3.refs_3_.refs_4_ = bf16[12,128,256]{2,1,0:T(8,128)(2,1)S(1)} custom-call(s32[3]{0:T(128)S(1)} %pad_add_fusion.info, s32[256]{0:T(256)S(1)} %reshape.18.cols_ref, bf16[4,128,256]{2,1,0:T(8,128)(2,1)S(1)} %get-tuple-element.30.refs_0_.refs_1_.refs_4_, bf16[4,128,256]{2,1,0:T(8,128)(2,1)S(1)} %get-tuple-element.29.refs_1_.refs_4_, ...), custom_call_target="tpu_custom_call" | custom-call | flops 1000 | bytes 1000 | tf_op jit(solution)/shard_map/rows_high/pallas_call | solution.py:183
  23.8 0.0 collective-permute-done.refs_0_
  23.8 1.1 %rows_odd.3.refs_1_.refs_4_ = bf16[4,128,256]{2,1,0:T(8,128)(2,1)S(1)} custom-call(s32[3]{0:T(128)S(1)} %pad_add_fusion.info, s32[256]{0:T(256)S(1)} %reshape.18.cols_ref, bf16[4,128,256]{2,1,0:T(8,128)(2,1)S(1)} %collective-permute-done.refs_0_, bf16[4,128,256]{2,1,0:T(8,128)(2,1)S(1)} %get-tuple-element.29.refs_1_.refs_4_, ...), custom_call_target="tpu_custom_call" | custom-call | flops 1000 | bytes 1000 | tf_op jit(solution)/shard_map/rows_odd/pallas_call | solution.py:183
  24.9 0.7 collective-permute-start.2
  25.6 2.1 %rows_low.4.refs_2_ = bf16[12,128,256]{2,1,0:T(8,128)(2,1)S(1)} custom-call(s32[3]{0:T(128)S(1)} %pad_add_fusion.info, s32[256]{0:T(256)S(1)} %reshape.18.cols_ref, bf16[4,128,256]{2,1,0:T(8,128)(2,1)S(1)} %rows_even.3.refs_0_.refs_1_.refs_4_, bf16[4,128,256]{2,1,0:T(8,128)(2,1)S(1)} %rows_odd.3.refs_1_.refs_4_, ...), custom_call_target="tpu_custom_call" | custom-call | flops 1000 | bytes 1000 | tf_op jit(solution)/shard_map/rows_low/pallas_call | solution.py:183
  27.7 0.0 collective-permute-done.3.refs_0_
  27.7 1.1 %rows_even.4.refs_0_.refs_1_ = bf16[4,128,256]{2,1,0:T(8,128)(2,1)S(1)} custom-call(s32[3]{0:T(128)S(1)} %pad_add_fusion.info, s32[256]{0:T(256)S(1)} %reshape.18.cols_ref, bf16[4,128,256]{2,1,0:T(8,128)(2,1)S(1)} %collective-permute-done.3.refs_0_, bf16[4,128,256]{2,1,0:T(8,128)(2,1)S(1)} %rows_even.3.refs_0_.refs_1_.refs_4_, ...), custom_call_target="tpu_custom_call" | custom-call | flops 1000 | bytes 1000 | tf_op jit(solution)/shard_map/rows_even/pallas_call | solution.py:183
  28.8 2.3 %collective-permute-start.5 = (bf16[4,128,256]{2,1,0:T(8,128)(2,1)S(1)}, bf16[4,128,256]{2,1,0:T(8,128)(2,1)S(1)}, u32[]{:S(2)}, u32[]{:S(2)}) collective-permute-start(bf16[4,128,256]{2,1,0:T(8,128)(2,1)S(1)} %rows_even.4.refs_0_.refs_1_), channel_id=1, source_target_pairs={{0,1},{1,0},{2,3},{3,2},{4,5},{5,4},{6,7},{7,6},{8,9},{9,8},{10,11... | collective-permute-start | bytes 786440 | tf_op jit(solution)/shard_map/ppermute | solution.py:459
  31.2 2.1 %rows_high.4.refs_3_ = bf16[12,128,256]{2,1,0:T(8,128)(2,1)S(1)} custom-call(s32[3]{0:T(128)S(1)} %pad_add_fusion.info, s32[256]{0:T(256)S(1)} %reshape.18.cols_ref, bf16[4,128,256]{2,1,0:T(8,128)(2,1)S(1)} %rows_even.3.refs_0_.refs_1_.refs_4_, bf16[4,128,256]{2,1,0:T(8,128)(2,1)S(1)} %rows_odd.3.refs_1_.refs_4_, ...), custom_call_target="tpu_custom_call" | custom-call | flops 1000 | bytes 1000 | tf_op jit(solution)/shard_map/rows_high/pallas_call | solution.py:183
  33.3 1.1 %rows_odd.4.refs_1_ = bf16[4,128,256]{2,1,0:T(8,128)(2,1)S(1)} custom-call(s32[3]{0:T(128)S(1)} %pad_add_fusion.info, s32[256]{0:T(256)S(1)} %reshape.18.cols_ref, bf16[4,128,256]{2,1,0:T(8,128)(2,1)S(1)} %collective-permute-done.2.refs_0_, bf16[4,128,256]{2,1,0:T(8,128)(2,1)S(1)} %rows_odd.3.refs_1_.refs_4_, ...), custom_call_target="tpu_custom_call" | custom-call | flops 1000 | bytes 1000 | tf_op jit(solution)/shard_map/rows_odd/pallas_call | solution.py:183
  34.4 2.1 %rows_high.5 = bf16[12,128,256]{2,1,0:T(8,128)(2,1)S(1)} custom-call(s32[3]{0:T(128)S(1)} %pad_add_fusion.info, s32[256]{0:T(256)S(1)} %reshape.18.cols_ref, bf16[4,128,256]{2,1,0:T(8,128)(2,1)S(1)} %rows_even.4.refs_0_.refs_1_, bf16[4,128,256]{2,1,0:T(8,128)(2,1)S(1)} %rows_odd.4.refs_1_, bf16[12,128,256]{2,1,0:T(8,128)(2,1)S(1)} %rows_low.4.refs_2_, ...), custom_call_target="tpu_custom_call" | custom-call | flops 1000 | bytes 1000 | tf_op jit(solution)/shard_map/rows_high/pallas_call | solution.py:183
  36.5 2.1 %rows_low.5 = bf16[12,128,256]{2,1,0:T(8,128)(2,1)S(1)} custom-call(s32[3]{0:T(128)S(1)} %pad_add_fusion.info, s32[256]{0:T(256)S(1)} %reshape.18.cols_ref, bf16[4,128,256]{2,1,0:T(8,128)(2,1)S(1)} %rows_even.4.refs_0_.refs_1_, bf16[4,128,256]{2,1,0:T(8,128)(2,1)S(1)} %rows_odd.4.refs_1_, bf16[12,128,256]{2,1,0:T(8,128)(2,1)S(1)} %rows_low.4.refs_2_, ...), custom_call_target="tpu_custom_call" | custom-call | flops 1000 | bytes 1000 | tf_op jit(solution)/shard_map/rows_low/pallas_call | solution.py:183
  38.7 1.1 %rows_even.5 = bf16[4,128,256]{2,1,0:T(8,128)(2,1)S(1)} custom-call(s32[3]{0:T(128)S(1)} %pad_add_fusion.info, s32[256]{0:T(256)S(1)} %reshape.18.cols_ref, bf16[4,128,256]{2,1,0:T(8,128)(2,1)S(1)} %collective-permute-done.5.refs_0_, bf16[4,128,256]{2,1,0:T(8,128)(2,1)S(1)} %rows_even.4.refs_0_.refs_1_, bf16[12,128,256]{2,1,0:T(8,128)(2,1)S(1)} %rows_low.4.refs_2_, ...), custom_call_target="tpu_custom_call" | custom-call | flops 1000 | bytes 1000 | tf_op jit(solution)/shard_map/rows_even/pallas_call | solution.py:183
  39.8 0.1 collective-permute-start.8
  39.9 0.5 collective-permute-start.7
  40.4 0.1 collective-permute-start.6
  40.5 0.8 collective-permute-start.4
  41.3 2.3 %collective-permute-done.6.refs_3_.refs_12_ = bf16[512,256]{1,0:T(8,128)(2,1)S(1)} collective-permute-done((bf16[512,256]{1,0:T(8,128)(2,1)S(1)}, bf16[512,256]{1,0:T(8,128)(2,1)S(1)}, u32[]{:S(2)}, u32[]{:S(2)}) %collective-permute-start.6) | collective-permute-done | bytes 262176 | tf_op jit(solution)/shard_map/ppermute | solution.py:462
  43.7 0.0 collective-permute-done.8.refs_5_.refs_14_
  43.7 0.0 collective-permute-done.7.refs_4_.refs_13_
  43.7 2.7 %gram_share.2.refs_2_ = f32[640,128]{1,0:T(8,128)S(1)} custom-call(s32[3]{0:T(128)S(1)} %pad_add_fusion.info, bf16[512,256]{1,0:T(8,128)(2,1)S(1)} %bitcast.16, bf16[1536,256]{1,0:T(8,128)(2,1)S(1)} %bitcast.13, bf16[1536,256]{1,0:T(8,128)(2,1)S(1)} %bitcast.10, bf16[512,256]{1,0:T(8,128)(2,1)S(1)} %collective-permute-done.6.refs_3_.refs_12_, ...), custom_call_target="tpu_custom_call" | custom-call | flops 1000 | bytes 1000 | tf_op jit(solution)/shard_map/gram_share/pallas_call | solution.py:243
  46.4 1.1 %rows_odd.5 = bf16[4,128,256]{2,1,0:T(8,128)(2,1)S(1)} custom-call(s32[3]{0:T(128)S(1)} %pad_add_fusion.info, s32[256]{0:T(256)S(1)} %reshape.18.cols_ref, bf16[4,128,256]{2,1,0:T(8,128)(2,1)S(1)} %collective-permute-done.4.refs_0_, bf16[4,128,256]{2,1,0:T(8,128)(2,1)S(1)} %rows_odd.4.refs_1_, bf16[12,128,256]{2,1,0:T(8,128)(2,1)S(1)} %rows_low.4.refs_2_, ...), custom_call_target="tpu_custom_call" | custom-call | flops 1000 | bytes 1000 | tf_op jit(solution)/shard_map/rows_odd/pallas_call | solution.py:183
  47.5 0.2 collective-permute-start.9
  47.7 1.4 %collective-permute-done.9.refs_1_.refs_15_ = bf16[512,256]{1,0:T(8,128)(2,1)S(1)} collective-permute-done((bf16[512,256]{1,0:T(8,128)(2,1)S(1)}, bf16[512,256]{1,0:T(8,128)(2,1)S(1)}, u32[]{:S(2)}, u32[]{:S(2)}) %collective-permute-start.9) | collective-permute-done | bytes 262176 | tf_op jit(solution)/shard_map/ppermute | solution.py:462
  49.1 0.9 gram_share.3
  50.0 7.9 %collective-permute-start.10 = (f32[160,128]{1,0:T(8,128)S(1)}, f32[160,128]{1,0:T(8,128)S(1)}, u32[]{:S(2)}, u32[]{:S(2)}) collective-permute-start(f32[160,128]{1,0:T(8,128)S(1)} %get-tuple-element.48), channel_id=1, source_target_pairs={{0,1},{1,0},{2,3},{3,2},{4,5},{5,4},{6,7},{7,6},{8,9},{9,8},{10,11... | collective-permute-start | bytes 245768 | tf_op jit(solution)/shard_map/ppermute | solution.py:275
  57.9 2.1 %collective-permute-start.11 = (f32[160,128]{1,0:T(8,128)S(1)}, f32[160,128]{1,0:T(8,128)S(1)}, u32[]{:S(2)}, u32[]{:S(2)}) collective-permute-start(f32[160,128]{1,0:T(8,128)S(1)} %get-tuple-element.49), channel_id=1, source_target_pairs={{0,2},{1,3},{2,0},{3,1},{4,6},{5,7},{6,4},{7,5},{8,10},{9,11},{10,... | collective-permute-start | bytes 245768 | tf_op jit(solution)/shard_map/ppermute | solution.py:275
  60.0 0.6 collective-permute-start.12
  60.5 0.1 collective-permute-done.10.b
  60.6 2.9 %collective-permute-done.11.c = f32[160,128]{1,0:T(8,128)S(1)} collective-permute-done((f32[160,128]{1,0:T(8,128)S(1)}, f32[160,128]{1,0:T(8,128)S(1)}, u32[]{:S(2)}, u32[]{:S(2)}) %collective-permute-start.11) | collective-permute-done | bytes 81952 | tf_op jit(solution)/shard_map/ppermute | solution.py:275
  63.5 1.8 %collective-permute-done.12.d = f32[160,128]{1,0:T(8,128)S(1)} collective-permute-done((f32[160,128]{1,0:T(8,128)S(1)}, f32[160,128]{1,0:T(8,128)S(1)}, u32[]{:S(2)}, u32[]{:S(2)}) %collective-permute-start.12) | collective-permute-done | bytes 81952 | tf_op jit(solution)/shard_map/ppermute | solution.py:275
  65.3 2.5 %collective-permute-start.13 = (f32[160,128]{1,0:T(8,128)S(1)}, f32[160,128]{1,0:T(8,128)S(1)}, u32[]{:S(2)}, u32[]{:S(2)}) collective-permute-start(f32[160,128]{1,0:T(8,128)S(1)} %add_four.2.a), channel_id=1, source_target_pairs={{0,4},{1,5},{2,6},{3,7},{4,0},{5,1},{6,2},{7,3},{8,12},{9,13},{10,... | collective-permute-start | bytes 245768 | tf_op jit(solution)/shard_map/ppermute | solution.py:275
  67.8 1.1 %collective-permute-start.14 = (f32[160,128]{1,0:T(8,128)S(1)}, f32[160,128]{1,0:T(8,128)S(1)}, u32[]{:S(2)}, u32[]{:S(2)}) collective-permute-start(f32[160,128]{1,0:T(8,128)S(1)} %add_four.2.a), channel_id=1, source_target_pairs={{0,8},{1,9},{2,10},{3,11},{4,12},{5,13},{6,14},{7,15},{8,0},{9,1},... | collective-permute-start | bytes 245768 | tf_op jit(solution)/shard_map/ppermute | solution.py:275
  68.9 1.4 %collective-permute-start.15 = (f32[160,128]{1,0:T(8,128)S(1)}, f32[160,128]{1,0:T(8,128)S(1)}, u32[]{:S(2)}, u32[]{:S(2)}) collective-permute-start(f32[160,128]{1,0:T(8,128)S(1)} %add_four.2.a), channel_id=1, source_target_pairs={{0,12},{1,13},{2,14},{3,15},{4,8},{5,9},{6,10},{7,11},{8,4},{9,5},... | collective-permute-start | bytes 245768 | tf_op jit(solution)/shard_map/ppermute | solution.py:275
  70.3 0.8 collective-permute-done.13.b
  71.0 4.6 %collective-permute-done.14.c = f32[160,128]{1,0:T(8,128)S(1)} collective-permute-done((f32[160,128]{1,0:T(8,128)S(1)}, f32[160,128]{1,0:T(8,128)S(1)}, u32[]{:S(2)}, u32[]{:S(2)}) %collective-permute-start.14) | collective-permute-done | bytes 81952 | tf_op jit(solution)/shard_map/ppermute | solution.py:275
  75.6 0.0 collective-permute-done.15.d
  75.6 1.3 %collective-permute-start.16 = (f32[160,128]{1,0:T(8,128)S(1)}, f32[160,128]{1,0:T(8,128)S(1)}, u32[]{:S(2)}, u32[]{:S(2)}) collective-permute-start(f32[160,128]{1,0:T(8,128)S(1)} %add_four.3.refs_0_), channel_id=1, source_target_pairs={{0,1},{1,0},{2,3},{3,2},{4,5},{5,4},{6,7},{7,6},{8,9},{9,8},{10,11... | collective-permute-start | bytes 245768 | tf_op jit(solution)/shard_map/ppermute | solution.py:275
  76.9 0.8 collective-permute-start.17
  77.7 1.5 %collective-permute-start.18 = (f32[160,128]{1,0:T(8,128)S(1)}, f32[160,128]{1,0:T(8,128)S(1)}, u32[]{:S(2)}, u32[]{:S(2)}) collective-permute-start(f32[160,128]{1,0:T(8,128)S(1)} %add_four.3.refs_0_), channel_id=1, source_target_pairs={{0,3},{1,2},{2,1},{3,0},{4,7},{5,6},{6,5},{7,4},{8,11},{9,10},{10,... | collective-permute-start | bytes 245768 | tf_op jit(solution)/shard_map/ppermute | solution.py:275
  79.2 0.0 collective-permute-start.19
  79.2 0.9 collective-permute-done.16.refs_1_
  80.1 0.0 collective-permute-start.20
  80.1 1.2 %collective-permute-done.17.refs_2_ = f32[160,128]{1,0:T(8,128)S(1)} collective-permute-done((f32[160,128]{1,0:T(8,128)S(1)}, f32[160,128]{1,0:T(8,128)S(1)}, u32[]{:S(2)}, u32[]{:S(2)}) %collective-permute-start.17) | collective-permute-done | bytes 81952 | tf_op jit(solution)/shard_map/ppermute | solution.py:275
  81.3 0.0 collective-permute-start.21
  81.3 1.7 %collective-permute-done.18.refs_3_ = f32[160,128]{1,0:T(8,128)S(1)} collective-permute-done((f32[160,128]{1,0:T(8,128)S(1)}, f32[160,128]{1,0:T(8,128)S(1)}, u32[]{:S(2)}, u32[]{:S(2)}) %collective-permute-start.18) | collective-permute-done | bytes 81952 | tf_op jit(solution)/shard_map/ppermute | solution.py:275
  83.0 0.0 collective-permute-done.20.refs_5_
  83.0 0.0 collective-permute-done.21.refs_6_
  83.1 1.3 %collective-permute-done.22.refs_7_ = f32[160,128]{1,0:T(8,128)S(1)} collective-permute-done((f32[160,128]{1,0:T(8,128)S(1)}, f32[160,128]{1,0:T(8,128)S(1)}, u32[]{:S(2)}, u32[]{:S(2)}) %collective-permute-start.22) | collective-permute-done | bytes 81952 | tf_op jit(solution)/shard_map/ppermute | solution.py:462
  84.3 20.2 %rotate.1 = bf16[4096,256]{1,0:T(8,128)(2,1)} custom-call(s32[3]{0:T(128)S(1)} %pad_add_fusion.info, f32[160,128]{1,0:T(8,128)S(1)} %add_four.3.refs_0_, f32[160,128]{1,0:T(8,128)S(1)} %collective-permute-done.16.refs_1_, f32[160,128]{1,0:T(8,128)S(1)} %collective-permute-done.17.refs_2_, f32[160,128]{1,0:T(8,128)S(1)} %collective-permute-done.18.refs_3_, ...), custom_call_target="tpu_custom_call" | custom-call | flops 17985175552 | bytes 6291456 | tf_op jit(solution)/shard_map/rotate/pallas_call | solution.py:420
  (10 shorter events, 0.1 us)
Async XLA Ops:
  1.6 1.6 %copy-start.1 = (bf16[4096,256]{1,0:T(8,128)(2,1)S(1)}, bf16[4096,256]{1,0:T(8,128)(2,1)}, u32[]{:S(2)}) copy-start(bf16[4096,256]{1,0:T(8,128)(2,1)} %param.4) | copy-start | bytes 6291460
  3.2 4.3 %copy-start.2 = (bf16[4096,256]{1,0:T(8,128)(2,1)S(1)}, bf16[4096,256]{1,0:T(8,128)(2,1)}, u32[]{:S(2)}) copy-start(bf16[4096,256]{1,0:T(8,128)(2,1)} %param.4) | copy-start | bytes 6291460
  3.8 14.2 %collective-permute-start.1 = (bf16[4,128,256]{2,1,0:T(8,128)(2,1)S(1)}, bf16[4,128,256]{2,1,0:T(8,128)(2,1)S(1)}, u32[]{:S(2)}, u32[]{:S(2)}) collective-permute-start(bf16[4,128,256]{2,1,0:T(8,128)(2,1)S(1)} %get-tuple-element.30.refs_0_.refs_1_.refs_4_), channel_id=1, source_target_pairs={{0,1},{1,0},{2,3},{3,2},{4,5},{5,4},{6,7},{7,6},{8,9},{9,8},{10,11... | collective-permute-start | bytes 786440 | tf_op jit(solution)/shard_map/ppermute | solution.py:459
  6.8 16.9 %collective-permute-start = (bf16[4,128,256]{2,1,0:T(8,128)(2,1)S(1)}, bf16[4,128,256]{2,1,0:T(8,128)(2,1)S(1)}, u32[]{:S(2)}, u32[]{:S(2)}) collective-permute-start(bf16[4,128,256]{2,1,0:T(8,128)(2,1)S(1)} %get-tuple-element.29.refs_1_.refs_4_), channel_id=1, source_target_pairs={{1,2},{2,1},{3,4},{4,3},{5,6},{6,5},{7,8},{8,7},{9,10},{10,9},{11,... | collective-permute-start | bytes 786440 | tf_op jit(solution)/shard_map/ppermute | solution.py:459
  7.5 3.4 %copy-start = (bf16[32,8,128,128]{3,2,1,0:T(8,128)(2,1)S(1)}, bf16[32,8,128,128]{3,2,1,0:T(8,128)(2,1)}, u32[]{:S(2)}) copy-start(bf16[32,8,128,128]{3,2,1,0:T(8,128)(2,1)} %blocks_ref.1) | copy-start | bytes 25165828
  19.1 8.6 %collective-permute-start.3 = (bf16[4,128,256]{2,1,0:T(8,128)(2,1)S(1)}, bf16[4,128,256]{2,1,0:T(8,128)(2,1)S(1)}, u32[]{:S(2)}, u32[]{:S(2)}) collective-permute-start(bf16[4,128,256]{2,1,0:T(8,128)(2,1)S(1)} %rows_even.3.refs_0_.refs_1_.refs_4_), channel_id=1, source_target_pairs={{0,1},{1,0},{2,3},{3,2},{4,5},{5,4},{6,7},{7,6},{8,9},{9,8},{10,11... | collective-permute-start | bytes 786440 | tf_op jit(solution)/shard_map/ppermute | solution.py:459
  24.9 8.4 %collective-permute-start.2 = (bf16[4,128,256]{2,1,0:T(8,128)(2,1)S(1)}, bf16[4,128,256]{2,1,0:T(8,128)(2,1)S(1)}, u32[]{:S(2)}, u32[]{:S(2)}) collective-permute-start(bf16[4,128,256]{2,1,0:T(8,128)(2,1)S(1)} %rows_odd.3.refs_1_.refs_4_), channel_id=1, source_target_pairs={{1,2},{2,1},{3,4},{4,3},{5,6},{6,5},{7,8},{8,7},{9,10},{10,9},{11,... | collective-permute-start | bytes 786440 | tf_op jit(solution)/shard_map/ppermute | solution.py:459
  28.8 9.9 %collective-permute-start.5 = (bf16[4,128,256]{2,1,0:T(8,128)(2,1)S(1)}, bf16[4,128,256]{2,1,0:T(8,128)(2,1)S(1)}, u32[]{:S(2)}, u32[]{:S(2)}) collective-permute-start(bf16[4,128,256]{2,1,0:T(8,128)(2,1)S(1)} %rows_even.4.refs_0_.refs_1_), channel_id=1, source_target_pairs={{0,1},{1,0},{2,3},{3,2},{4,5},{5,4},{6,7},{7,6},{8,9},{9,8},{10,11... | collective-permute-start | bytes 786440 | tf_op jit(solution)/shard_map/ppermute | solution.py:459
  39.8 3.9 %collective-permute-start.8 = (bf16[1536,256]{1,0:T(8,128)(2,1)S(1)}, bf16[1536,256]{1,0:T(8,128)(2,1)S(1)}, u32[]{:S(2)}, u32[]{:S(2)}) collective-permute-start(bf16[1536,256]{1,0:T(8,128)(2,1)S(1)} %bitcast.9), channel_id=1, source_target_pairs={{0,16},{16,0},{1,17},{17,1},{2,18},{18,2},{3,19},{19,3},{4,20},{20... | collective-permute-start | bytes 2359304 | tf_op jit(solution)/shard_map/ppermute | solution.py:462
  39.9 3.8 %collective-permute-start.7 = (bf16[1536,256]{1,0:T(8,128)(2,1)S(1)}, bf16[1536,256]{1,0:T(8,128)(2,1)S(1)}, u32[]{:S(2)}, u32[]{:S(2)}) collective-permute-start(bf16[1536,256]{1,0:T(8,128)(2,1)S(1)} %bitcast.12), channel_id=1, source_target_pairs={{0,16},{16,0},{1,17},{17,1},{2,18},{18,2},{3,19},{19,3},{4,20},{20... | collective-permute-start | bytes 2359304 | tf_op jit(solution)/shard_map/ppermute | solution.py:462
  40.4 3.3 %collective-permute-start.6 = (bf16[512,256]{1,0:T(8,128)(2,1)S(1)}, bf16[512,256]{1,0:T(8,128)(2,1)S(1)}, u32[]{:S(2)}, u32[]{:S(2)}) collective-permute-start(bf16[512,256]{1,0:T(8,128)(2,1)S(1)} %bitcast.15), channel_id=1, source_target_pairs={{0,16},{16,0},{1,17},{17,1},{2,18},{18,2},{3,19},{19,3},{4,20},{20... | collective-permute-start | bytes 786440 | tf_op jit(solution)/shard_map/ppermute | solution.py:462
  40.5 5.9 %collective-permute-start.4 = (bf16[4,128,256]{2,1,0:T(8,128)(2,1)S(1)}, bf16[4,128,256]{2,1,0:T(8,128)(2,1)S(1)}, u32[]{:S(2)}, u32[]{:S(2)}) collective-permute-start(bf16[4,128,256]{2,1,0:T(8,128)(2,1)S(1)} %rows_odd.4.refs_1_), channel_id=1, source_target_pairs={{1,2},{2,1},{3,4},{4,3},{5,6},{6,5},{7,8},{8,7},{9,10},{10,9},{11,... | collective-permute-start | bytes 786440 | tf_op jit(solution)/shard_map/ppermute | solution.py:459
  47.5 1.6 %collective-permute-start.9 = (bf16[512,256]{1,0:T(8,128)(2,1)S(1)}, bf16[512,256]{1,0:T(8,128)(2,1)S(1)}, u32[]{:S(2)}, u32[]{:S(2)}) collective-permute-start(bf16[512,256]{1,0:T(8,128)(2,1)S(1)} %bitcast.18), channel_id=1, source_target_pairs={{0,16},{16,0},{1,17},{17,1},{2,18},{18,2},{3,19},{19,3},{4,20},{20... | collective-permute-start | bytes 786440 | tf_op jit(solution)/shard_map/ppermute | solution.py:462
  50.0 10.7 %collective-permute-start.10 = (f32[160,128]{1,0:T(8,128)S(1)}, f32[160,128]{1,0:T(8,128)S(1)}, u32[]{:S(2)}, u32[]{:S(2)}) collective-permute-start(f32[160,128]{1,0:T(8,128)S(1)} %get-tuple-element.48), channel_id=1, source_target_pairs={{0,1},{1,0},{2,3},{3,2},{4,5},{5,4},{6,7},{7,6},{8,9},{9,8},{10,11... | collective-permute-start | bytes 245768 | tf_op jit(solution)/shard_map/ppermute | solution.py:275
  57.9 5.6 %collective-permute-start.11 = (f32[160,128]{1,0:T(8,128)S(1)}, f32[160,128]{1,0:T(8,128)S(1)}, u32[]{:S(2)}, u32[]{:S(2)}) collective-permute-start(f32[160,128]{1,0:T(8,128)S(1)} %get-tuple-element.49), channel_id=1, source_target_pairs={{0,2},{1,3},{2,0},{3,1},{4,6},{5,7},{6,4},{7,5},{8,10},{9,11},{10,... | collective-permute-start | bytes 245768 | tf_op jit(solution)/shard_map/ppermute | solution.py:275
  60.0 5.3 %collective-permute-start.12 = (f32[160,128]{1,0:T(8,128)S(1)}, f32[160,128]{1,0:T(8,128)S(1)}, u32[]{:S(2)}, u32[]{:S(2)}) collective-permute-start(f32[160,128]{1,0:T(8,128)S(1)} %get-tuple-element.50), channel_id=1, source_target_pairs={{0,3},{1,2},{2,1},{3,0},{4,7},{5,6},{6,5},{7,4},{8,11},{9,10},{10,... | collective-permute-start | bytes 245768 | tf_op jit(solution)/shard_map/ppermute | solution.py:275
  65.3 5.7 %collective-permute-start.13 = (f32[160,128]{1,0:T(8,128)S(1)}, f32[160,128]{1,0:T(8,128)S(1)}, u32[]{:S(2)}, u32[]{:S(2)}) collective-permute-start(f32[160,128]{1,0:T(8,128)S(1)} %add_four.2.a), channel_id=1, source_target_pairs={{0,4},{1,5},{2,6},{3,7},{4,0},{5,1},{6,2},{7,3},{8,12},{9,13},{10,... | collective-permute-start | bytes 245768 | tf_op jit(solution)/shard_map/ppermute | solution.py:275
  67.8 7.8 %collective-permute-start.14 = (f32[160,128]{1,0:T(8,128)S(1)}, f32[160,128]{1,0:T(8,128)S(1)}, u32[]{:S(2)}, u32[]{:S(2)}) collective-permute-start(f32[160,128]{1,0:T(8,128)S(1)} %add_four.2.a), channel_id=1, source_target_pairs={{0,8},{1,9},{2,10},{3,11},{4,12},{5,13},{6,14},{7,15},{8,0},{9,1},... | collective-permute-start | bytes 245768 | tf_op jit(solution)/shard_map/ppermute | solution.py:275
  68.9 6.7 %collective-permute-start.15 = (f32[160,128]{1,0:T(8,128)S(1)}, f32[160,128]{1,0:T(8,128)S(1)}, u32[]{:S(2)}, u32[]{:S(2)}) collective-permute-start(f32[160,128]{1,0:T(8,128)S(1)} %add_four.2.a), channel_id=1, source_target_pairs={{0,12},{1,13},{2,14},{3,15},{4,8},{5,9},{6,10},{7,11},{8,4},{9,5},... | collective-permute-start | bytes 245768 | tf_op jit(solution)/shard_map/ppermute | solution.py:275
  75.6 4.5 %collective-permute-start.16 = (f32[160,128]{1,0:T(8,128)S(1)}, f32[160,128]{1,0:T(8,128)S(1)}, u32[]{:S(2)}, u32[]{:S(2)}) collective-permute-start(f32[160,128]{1,0:T(8,128)S(1)} %add_four.3.refs_0_), channel_id=1, source_target_pairs={{0,1},{1,0},{2,3},{3,2},{4,5},{5,4},{6,7},{7,6},{8,9},{9,8},{10,11... | collective-permute-start | bytes 245768 | tf_op jit(solution)/shard_map/ppermute | solution.py:275
  76.9 4.4 %collective-permute-start.17 = (f32[160,128]{1,0:T(8,128)S(1)}, f32[160,128]{1,0:T(8,128)S(1)}, u32[]{:S(2)}, u32[]{:S(2)}) collective-permute-start(f32[160,128]{1,0:T(8,128)S(1)} %add_four.3.refs_0_), channel_id=1, source_target_pairs={{0,2},{1,3},{2,0},{3,1},{4,6},{5,7},{6,4},{7,5},{8,10},{9,11},{10,... | collective-permute-start | bytes 245768 | tf_op jit(solution)/shard_map/ppermute | solution.py:275
  77.7 5.3 %collective-permute-start.18 = (f32[160,128]{1,0:T(8,128)S(1)}, f32[160,128]{1,0:T(8,128)S(1)}, u32[]{:S(2)}, u32[]{:S(2)}) collective-permute-start(f32[160,128]{1,0:T(8,128)S(1)} %add_four.3.refs_0_), channel_id=1, source_target_pairs={{0,3},{1,2},{2,1},{3,0},{4,7},{5,6},{6,5},{7,4},{8,11},{9,10},{10,... | collective-permute-start | bytes 245768 | tf_op jit(solution)/shard_map/ppermute | solution.py:275
  79.2 3.9 %collective-permute-start.19 = (f32[160,128]{1,0:T(8,128)S(1)}, f32[160,128]{1,0:T(8,128)S(1)}, u32[]{:S(2)}, u32[]{:S(2)}) collective-permute-start(f32[160,128]{1,0:T(8,128)S(1)} %add_four.3.refs_0_), channel_id=1, source_target_pairs={{0,16},{16,0},{1,17},{17,1},{2,18},{18,2},{3,19},{19,3},{4,20},{20... | collective-permute-start | bytes 245768 | tf_op jit(solution)/shard_map/ppermute | solution.py:462
  80.1 2.9 %collective-permute-start.20 = (f32[160,128]{1,0:T(8,128)S(1)}, f32[160,128]{1,0:T(8,128)S(1)}, u32[]{:S(2)}, u32[]{:S(2)}) collective-permute-start(f32[160,128]{1,0:T(8,128)S(1)} %collective-permute-done.16.refs_1_), channel_id=1, source_target_pairs={{0,16},{16,0},{1,17},{17,1},{2,18},{18,2},{3,19},{19,3},{4,20},{20... | collective-permute-start | bytes 245768 | tf_op jit(solution)/shard_map/ppermute | solution.py:462
  81.3 1.7 %collective-permute-start.21 = (f32[160,128]{1,0:T(8,128)S(1)}, f32[160,128]{1,0:T(8,128)S(1)}, u32[]{:S(2)}, u32[]{:S(2)}) collective-permute-start(f32[160,128]{1,0:T(8,128)S(1)} %collective-permute-done.17.refs_2_), channel_id=1, source_target_pairs={{0,16},{16,0},{1,17},{17,1},{2,18},{18,2},{3,19},{19,3},{4,20},{20... | collective-permute-start | bytes 245768 | tf_op jit(solution)/shard_map/ppermute | solution.py:462
  83.0 1.3 %collective-permute-start.22 = (f32[160,128]{1,0:T(8,128)S(1)}, f32[160,128]{1,0:T(8,128)S(1)}, u32[]{:S(2)}, u32[]{:S(2)}) collective-permute-start(f32[160,128]{1,0:T(8,128)S(1)} %collective-permute-done.18.refs_3_), channel_id=1, source_target_pairs={{0,16},{16,0},{1,17},{17,1},{2,18},{18,2},{3,19},{19,3},{4,20},{20... | collective-permute-start | bytes 245768 | tf_op jit(solution)/shard_map/ppermute | solution.py:462

commit v4 on v3

--- a/solution.py
+++ b/solution.py
@@ -14,6 +14,7 @@
 GROUP = 4
 
 SMALL = pl.CostEstimate(flops=1000, bytes_accessed=1000, transcendentals=0)
+LARGE = pl.CostEstimate(flops=10**11, bytes_accessed=1000, transcendentals=0)
 PART, PATCH, LIVE = range(3)
 SMALL_VMEM = pltpu.CompilerParams(vmem_limit_bytes=8 * 1024 * 1024)
 ANY = pl.BlockSpec(memory_space=pl.ANY)
@@ -168,7 +169,7 @@
     lax.fori_loop(0, out_ref.shape[0] // GROUP, group, 0)
 
 
-def tile_rows(name, info, cols, blocks, pieces, prev):
+def tile_rows(name, info, cols, blocks, pieces, prev, cost):
     rows, nnz, tile, _ = blocks.shape
     tiles = cols.shape[0] // nnz
     width = pieces[0].shape[-1]
@@ -187,7 +188,7 @@
         out_shape=jax.ShapeDtypeStruct((rows, tile, width), BF16),
         scratch_shapes=[pltpu.VMEM((window, tile, width), BF16)],
         compiler_params=SMALL_VMEM,
-        cost_estimate=SMALL,
+        cost_estimate=cost,
         name="rows_" + name,
     )(info, cols, *args)
 
@@ -287,33 +288,47 @@
     return high, (value - high.astype(F32)).astype(BF16)
 
 
-def put_left(ref, row, col, value):
-    size, width = ref.shape[0], value.shape[0]
+def put_row(ref, size, col, value):
+    width = value.shape[0]
     high, low = split(value)
     for i, piece in enumerate((high, high, low)):
-        ref[pl.ds(row * width, width), pl.ds(i * size + col * width, width)] = piece
-
-
-def put_right(ref, row, col, value):
-    size, width = ref.shape[1], value.shape[0]
+        ref[:, pl.ds(i * size + col * width, width)] = piece
+
+
+def put_col(ref, size, row, col, value):
+    width = value.shape[0]
     high, low = split(value)
     for i, piece in enumerate((high, low, high)):
         ref[pl.ds(i * size + row * width, width), pl.ds(col * width, width)] = piece
 
 
-def put_symmetric(put, ref, blocks):
-    first, across, second = blocks
-    put(ref, 0, 0, first)
-    put(ref, 0, 1, across)
-    put(ref, 1, 0, across.T)
-    put(ref, 1, 1, second)
-
-
-def product(left_ref, right_ref):
-    width = left_ref.shape[0] // 2
-    second = dot(left_ref[...], right_ref[:, width:])
-    first = dot(left_ref[:width, :], right_ref[:, :width])
-    return first, second[:width], second[width:]
+def put_left(refs, blocks):
+    row_ref, col_ref = refs
+    size = 2 * blocks[0].shape[0]
+    put_row(row_ref, size, 0, blocks[0])
+    put_row(row_ref, size, 1, blocks[1])
+    put_col(col_ref, size, 0, 0, blocks[1])
+    put_col(col_ref, size, 1, 0, blocks[2])
+
+
+def put_right(refs, blocks):
+    last_ref, all_ref = refs
+    size = 2 * blocks[0].shape[0]
+    across = blocks[1].T
+    put_col(all_ref, size, 0, 0, blocks[0])
+    put_col(all_ref, size, 0, 1, blocks[1])
+    put_col(all_ref, size, 1, 0, across)
+    put_col(all_ref, size, 1, 1, blocks[2])
+    put_row(last_ref, size, 0, across)
+    put_row(last_ref, size, 1, blocks[2])
+
+
+def times_middle(blocks, left, right):
+    width = blocks[0].shape[0]
+    first = dot(left[0][...], right[1][...])
+    second = dot(right[0][...], left[1][...])
+    parts = first[:, :width], first[:, width:], second
+    return tuple(1.5 * block - 0.5 * part for block, part in zip(blocks, parts))
 
 
 def middle(blocks):
@@ -327,9 +342,9 @@
 def finish_kernel(total_rows, chunk, info, *refs):
     mine, theirs = refs[:WAYS], refs[WAYS : 2 * WAYS]
     fields, out_ref = refs[2 * WAYS : 2 * WAYS + 8], refs[2 * WAYS + 8]
-    shares, x_ref, x_left, w_left, z_left, m_right, wide, result, sem, out_sem = refs[
-        2 * WAYS + 9 :
-    ]
+    shares, x_ref, x_held, w_held, z_held, *rest = refs[2 * WAYS + 9 :]
+    x_left, w_left, z_left, x_right = rest[0:2], rest[2:4], rest[4:6], (rest[6:8], rest[8:10])
+    wide, result, sem, out_sem = rest[10:]
     part, quarter = info[PART], info[PATCH] % WAYS
     size = x_ref.shape[0]
     width = size // 2
@@ -373,29 +388,51 @@
     gram = x_ref[:width, :width], x_ref[:width, width:], x_ref[width:, width:]
     squares = gram[0] * gram[0] + 2.0 * (gram[1] * gram[1]) + gram[2] * gram[2]
     norm = jnp.sqrt(jnp.sum(squares, keepdims=True))
+    def hold(ref, blocks):
+        for i, value in enumerate(blocks):
+            ref[i] = value
+
+    def held(ref):
+        return tuple(ref[i] for i in range(3))
+
+    def set_x(x, right):
+        hold(x_held, x)
+        put_left(x_left, x)
+        put_right(right, x)
+
+    def advance(now, then):
+        w = times_middle(held(x_held), x_left, now)
+        hold(w_held, w)
+        put_left(w_left, w)
+        z = times_middle(held(z_held), z_left, now)
+        x = times_middle(w, w_left, now)
+        hold(z_held, z)
+        put_left(z_left, z)
+        set_x(x, then)
+
     x = tuple(value / norm for value in gram)
-    put_symmetric(put_left, x_left, x)
-    factors = middle(x)
-    put_symmetric(put_right, m_right, factors)
-    put_symmetric(put_left, z_left, factors)
-
-    def advance(first):
-        put_symmetric(put_left, w_left, product(x_left, m_right))
-        if not first:
-            put_symmetric(put_left, z_left, product(z_left, m_right))
-        x = product(w_left, m_right)
-        put_symmetric(put_left, x_left, x)
-        put_symmetric(put_right, m_right, middle(x))
-
-    advance(True)
-
-    def sweep(index, carry):
-        advance(False)
+    set_x(x, x_right[0])
+    z = middle(x)
+    hold(z_held, z)
+    put_left(z_left, z)
+    w = times_middle(x, x_left, x_right[0])
+    put_left(w_left, w)
+    set_x(times_middle(w, w_left, x_right[0]), x_right[1])
+
+    def sweeps(index, carry):
+        advance(x_right[1], x_right[0])
+        advance(x_right[0], x_right[1])
         return carry
 
-    lax.fori_loop(1, ITERS - 1, sweep, 0)
+    lax.fori_loop(0, (ITERS - 2) // 2, sweeps, 0)
+    first, across, second = times_middle(held(z_held), z_left, x_right[1])
+    z_ref = x_ref
+    z_ref[:width, :width] = first
+    z_ref[:width, width:] = across
+    z_ref[width:, :width] = across.T
+    z_ref[width:, width:] = second
     own = pl.ds(pl.multiple_of(part * width, width), width)
-    rotation = dot(z_left[...], m_right[:, own]).astype(BF16)
+    rotation = z_ref[:, own].astype(BF16)
     factor = jnp.sqrt(total_rows / norm)
     for copy in copies:
         copy.wait()
@@ -416,7 +453,10 @@
     size = 2 * width
     chunk = min(rows, 512)
     body = functools.partial(finish_kernel, float(total_rows), chunk)
-    left = pltpu.VMEM((size, 3 * size), BF16)
+    blocks = pltpu.VMEM((3, width, width), F32)
+    row_form = pltpu.VMEM((width, 3 * size), BF16)
+    col_form = pltpu.VMEM((3 * size, width), BF16)
+    all_form = pltpu.VMEM((3 * size, size), BF16)
     return pl.pallas_call(
         body,
         in_specs=[SMEM] + [VMEM] * (2 * WAYS) + [ANY] * 8,
@@ -425,14 +465,15 @@
         scratch_shapes=[
             pltpu.VMEM((2, 5 * width // 2, width // 2), F32),
             pltpu.VMEM((size, size), F32),
-            left, left, left,
-            pltpu.VMEM((3 * size, size), BF16),
+            blocks, blocks, blocks,
+            row_form, col_form, row_form, col_form, row_form, col_form,
+            row_form, all_form, row_form, all_form,
             pltpu.VMEM((rows, size), BF16),
             pltpu.VMEM((rows, width), BF16),
             pltpu.SemaphoreType.DMA((8,)),
             pltpu.SemaphoreType.DMA((rows // chunk,)),
         ],
-        compiler_params=pltpu.CompilerParams(vmem_limit_bytes=20 * 1024 * 1024),
+        compiler_params=pltpu.CompilerParams(vmem_limit_bytes=28 * 1024 * 1024),
         cost_estimate=pl.CostEstimate(
             flops=21 * 6 * size**3 + 2 * rows * size * width,
             bytes_accessed=3 * rows * width * 2,
@@ -468,37 +509,40 @@
     cols = tile_cols.reshape(-1)
 
     even, odd = masked_edges(after(info, cols), start)
-    even_halo, odd_halo = exchange("even", even), exchange("odd", odd)
+    even_halo = exchange("even", even)
     ready = prepare(after(info, even), start, blocks)
     low, high = ready[:2]
     stored = dict(zip(("even", "odd", "low", "high"), ready[2:]))
+    odd_halo = exchange("odd", after(odd, low))
     prev = dict.fromkeys(stored)
 
-    def rows(name, *pieces):
-        return tile_rows(name, info, cols, stored[name], pieces, prev[name])
+    def rows(name, *pieces, cost=SMALL):
+        return tile_rows(name, info, cols, stored[name], pieces, prev[name], cost)
 
     for step in range(STEPS):
-        final = step == STEPS - 1
-        new_low = rows("low", even, odd, low, high)
-        even_halo = after(even_halo, new_low)
+        first, final = step == 0, step == STEPS - 1
+        if not first:
+            new_low = rows("low", even, odd, low, high)
+            even_halo = after(even_halo, new_low)
         new_even = rows("even", even_halo, even, low, high)
         if not final:
             even_halo = exchange("even", new_even)
+        if first:
+            new_low = rows("low", after(even, new_even), odd, low, high)
         new_high = rows("high", even, odd, low, high)
         if final:
             flat = [value.reshape(-1, width) for value in (new_even, new_low, new_high)]
             others = [sibling(after(value, new_even)) for value in flat]
-            share = gram_share(info, flat, others, None)
-            odd_halo = after(odd_halo, share)
-        else:
-            odd_halo = after(odd_halo, new_even, new_high)
-        new_odd = rows("odd", odd_halo, odd, low, high)
+        odd_halo = after(odd_halo, new_even, new_low, new_high)
+        new_odd = rows("odd", odd_halo, odd, low, high, cost=LARGE if final else SMALL)
         if not final:
             odd_halo = exchange("odd", new_odd)
         prev = {"even": even, "odd": odd, "low": low, "high": high}
         even, odd, low, high = new_even, new_odd, new_low, new_high
     last = odd.reshape(-1, width)
     other_last = sibling(last)
+    others = [after(other, last) for other in others]
+    share = gram_share(info, flat, others, None)
     parts = gram_share(info, [last], [other_last], share)
     mine = sum_over_patch(parts)
     theirs = [sibling(value) for value in mine]

time: 105 us -> 99.9 us (0.951)
  waiting for transfers between devices: 22.5 us -> 19.7 us
  starting transfers between devices: 30 us -> 28.5 us
    ppermute x9, starting transfers between devices: 19.1 us -> 14.1 us  [exchange(): lax.ppermute(value, 'patch', [(i, i ^ distance) for i in range(count)])]
    ppermute x6, starting transfers between devices: 10.1 us -> 13.2 us  [exchange(): return lax.ppermute(value, 'patch', pairs[name])]
    ppermute x8, waiting for transfers between devices: 5.01 us -> 2.86 us  [sibling(): return lax.ppermute(value, 'cols', [(0, 1), (1, 0)])]
  transfers between devices with their start and end apart: 23 -> 23, of which waited for: 12 -> 12; matrix products, arithmetic and copies ran while one was open for 0% -> 0% of each run, Pallas kernels for 20% -> 23%
where the time goes in v4:
time: 99.9 us; the launch traced here: 99.6 us
  Pallas kernels  44.4 us (44%)
  starting transfers between devices  28.5 us (29%)
  waiting for transfers between devices  19.7 us (20%)
  local copies, waits for them, and re-layouts  5.83 us (6%)
  between operations  1.05 us (1%)
    pallas_call x1, Pallas kernels, rotate(): pl.pallas_call(body, in_specs=[SMEM] + [VMEM] * (2 * WAYS) + [ANY] * 8, o...  19.5 us
    pallas_call x12, Pallas kernels, tile_rows(): pl.pallas_call(functools.partial(rows_kernel, name, counts, tiles), in_sp...  19.3 us
    ppermute x9, starting transfers between devices, exchange(): lax.ppermute(value, 'patch', [(i, i ^ distance) for i in range(count)])  14.1 us
    ppermute x9, waiting for transfers between devices, exchange(): lax.ppermute(value, 'patch', [(i, i ^ distance) for i in range(count)])  13.8 us
    ppermute x6, starting transfers between devices, exchange(): return lax.ppermute(value, 'patch', pairs[name])  13.2 us
    unnamed x7, local copies, waits for them, and re-layouts  5.74 us
    pallas_call x2, Pallas kernels, gram_share(): pl.pallas_call(functools.partial(gram_kernel, len(owns), chunk, last), in...  3.54 us
    ppermute x6, waiting for transfers between devices, exchange(): return lax.ppermute(value, 'patch', pairs[name])  3.13 us
  transfers between devices with their start and end apart: 23, of which 12 were waited for; matrix products, arithmetic and copies ran while one was open for 0% of the time, Pallas kernels for 23%

profile of v4, /device:TPU:0, one launch (start us, length us, event | category | flops | bytes accessed | tf_op | source)
XLA Modules:
  0.0 99.6 jit_solution(4770362195157383246)
XLA Ops:
  0.7 0.8 copy.5
  1.4 0.1 reshape.18.cols_ref
  1.5 0.1 pad_add_fusion.info
  1.6 1.6 %copy-done.1 = bf16[4096,256]{1,0:T(8,128)(2,1)S(1)} copy-done((bf16[4096,256]{1,0:T(8,128)(2,1)S(1)}, bf16[4096,256]{1,0:T(8,128)(2,1)}, u32[]{:S(2)}) %copy-start.1) | copy-done | bytes 2097176
  3.2 0.6 masked_edges.1
  3.8 3.0 %collective-permute-start.1 = (bf16[4,128,256]{2,1,0:T(8,128)(2,1)S(1)}, bf16[4,128,256]{2,1,0:T(8,128)(2,1)S(1)}, u32[]{:S(2)}, u32[]{:S(2)}) collective-permute-start(bf16[4,128,256]{2,1,0:T(8,128)(2,1)S(1)} %get-tuple-element.40.refs_1_.refs_0_.refs_4_), channel_id=1, source_target_pairs={{0,1},{1,0},{2,3},{3,2},{4,5},{5,4},{6,7},{7,6},{8,9},{9,8},{10,11... | collective-permute-start | bytes 786440 | tf_op jit(solution)/shard_map/ppermute | solution.py:500
  6.8 3.4 %copy-done = bf16[32,8,128,128]{3,2,1,0:T(8,128)(2,1)S(1)} copy-done((bf16[32,8,128,128]{3,2,1,0:T(8,128)(2,1)S(1)}, bf16[32,8,128,128]{3,2,1,0:T(8,128)(2,1)}, u32[]{:S(2)}) %copy-start) | copy-done | bytes 8388632
  10.2 1.3 %prepare.1 = (bf16[12,128,256]{2,1,0:T(8,128)(2,1)S(1)}, bf16[12,128,256]{2,1,0:T(8,128)(2,1)S(1)}, bf16[4,8,128,128]{3,2,1,0:T(8,128)(2,1)S(1)}, bf16[4,8,128,1...) custom-call(s32[3]{0:T(128)S(1)} %pad_add_fusion.info, ...), custom_call_target="tpu_custom_call" | custom-call | flops 1000 | bytes 1000 | tf_op jit(solution)/shard_map/prepare/pallas_call | solution.py:118
  11.6 0.7 collective-permute-start
  12.2 2.1 %rows_high.3.refs_3_.refs_4_ = bf16[12,128,256]{2,1,0:T(8,128)(2,1)S(1)} custom-call(s32[3]{0:T(128)S(1)} %pad_add_fusion.info, s32[256]{0:T(256)S(1)} %reshape.18.cols_ref, bf16[4,128,256]{2,1,0:T(8,128)(2,1)S(1)} %get-tuple-element.40.refs_1_.refs_0_.refs_4_, bf16[4,128,256]{2,1,0:T(8,128)(2,1)S(1)} %get-tuple-element.37.refs_1_.refs_4_, ...), custom_call_target="tpu_custom_call" | custom-call | flops 1000 | bytes 1000 | tf_op jit(solution)/shard_map/rows_high/pallas_call | solution.py:184
  14.3 0.0 collective-permute-done.1.refs_0_
  14.3 1.1 %rows_even.3.refs_0_.refs_1_.refs_4_ = bf16[4,128,256]{2,1,0:T(8,128)(2,1)S(1)} custom-call(s32[3]{0:T(128)S(1)} %pad_add_fusion.info, s32[256]{0:T(256)S(1)} %reshape.18.cols_ref, bf16[4,128,256]{2,1,0:T(8,128)(2,1)S(1)} %collective-permute-done.1.refs_0_, bf16[4,128,256]{2,1,0:T(8,128)(2,1)S(1)} %get-tuple-element.40.refs_1_.refs_0_.refs_4_, ...), custom_call_target="tpu_custom_call" | custom-call | flops 1000 | bytes 1000 | tf_op jit(solution)/shard_map/rows_even/pallas_call | solution.py:184
  15.5 4.4 %collective-permute-start.3 = (bf16[4,128,256]{2,1,0:T(8,128)(2,1)S(1)}, bf16[4,128,256]{2,1,0:T(8,128)(2,1)S(1)}, u32[]{:S(2)}, u32[]{:S(2)}) collective-permute-start(bf16[4,128,256]{2,1,0:T(8,128)(2,1)S(1)} %rows_even.3.refs_0_.refs_1_.refs_4_), channel_id=1, source_target_pairs={{0,1},{1,0},{2,3},{3,2},{4,5},{5,4},{6,7},{7,6},{8,9},{9,8},{10,11... | collective-permute-start | bytes 786440 | tf_op jit(solution)/shard_map/ppermute | solution.py:500
  19.8 2.1 %rows_low.3.refs_2_.refs_4_ = bf16[12,128,256]{2,1,0:T(8,128)(2,1)S(1)} custom-call(s32[3]{0:T(128)S(1)} %pad_add_fusion.info, s32[256]{0:T(256)S(1)} %reshape.18.cols_ref, bf16[4,128,256]{2,1,0:T(8,128)(2,1)S(1)} %get-tuple-element.40.refs_1_.refs_0_.refs_4_, bf16[4,128,256]{2,1,0:T(8,128)(2,1)S(1)} %get-tuple-element.37.refs_1_.refs_4_, ...), custom_call_target="tpu_custom_call" | custom-call | flops 1000 | bytes 1000 | tf_op jit(solution)/shard_map/rows_low/pallas_call | solution.py:184
  21.9 0.0 collective-permute-done.refs_0_
  21.9 1.1 %rows_odd.3.refs_1_.refs_4_ = bf16[4,128,256]{2,1,0:T(8,128)(2,1)S(1)} custom-call(s32[3]{0:T(128)S(1)} %pad_add_fusion.info, s32[256]{0:T(256)S(1)} %reshape.18.cols_ref, bf16[4,128,256]{2,1,0:T(8,128)(2,1)S(1)} %collective-permute-done.refs_0_, bf16[4,128,256]{2,1,0:T(8,128)(2,1)S(1)} %get-tuple-element.37.refs_1_.refs_4_, ...), custom_call_target="tpu_custom_call" | custom-call | flops 1000 | bytes 1000 | tf_op jit(solution)/shard_map/rows_odd/pallas_call | solution.py:184
  23.1 0.7 collective-permute-start.2
  23.7 2.1 %rows_low.4.refs_2_ = bf16[12,128,256]{2,1,0:T(8,128)(2,1)S(1)} custom-call(s32[3]{0:T(128)S(1)} %pad_add_fusion.info, s32[256]{0:T(256)S(1)} %reshape.18.cols_ref, bf16[4,128,256]{2,1,0:T(8,128)(2,1)S(1)} %rows_even.3.refs_0_.refs_1_.refs_4_, bf16[4,128,256]{2,1,0:T(8,128)(2,1)S(1)} %rows_odd.3.refs_1_.refs_4_, ...), custom_call_target="tpu_custom_call" | custom-call | flops 1000 | bytes 1000 | tf_op jit(solution)/shard_map/rows_low/pallas_call | solution.py:184
  25.9 2.4 %collective-permute-done.3.refs_0_ = bf16[4,128,256]{2,1,0:T(8,128)(2,1)S(1)} collective-permute-done((bf16[4,128,256]{2,1,0:T(8,128)(2,1)S(1)}, bf16[4,128,256]{2,1,0:T(8,128)(2,1)S(1)}, u32[]{:S(2)}, u32[]{:S(2)}) %collective-permute-start.3) | collective-permute-done | bytes 262176 | tf_op jit(solution)/shard_map/ppermute | solution.py:500
  28.3 1.1 %rows_even.4.refs_0_.refs_1_ = bf16[4,128,256]{2,1,0:T(8,128)(2,1)S(1)} custom-call(s32[3]{0:T(128)S(1)} %pad_add_fusion.info, s32[256]{0:T(256)S(1)} %reshape.18.cols_ref, bf16[4,128,256]{2,1,0:T(8,128)(2,1)S(1)} %collective-permute-done.3.refs_0_, bf16[4,128,256]{2,1,0:T(8,128)(2,1)S(1)} %rows_even.3.refs_0_.refs_1_.refs_4_, ...), custom_call_target="tpu_custom_call" | custom-call | flops 1000 | bytes 1000 | tf_op jit(solution)/shard_map/rows_even/pallas_call | solution.py:184
  29.4 3.6 %collective-permute-start.5 = (bf16[4,128,256]{2,1,0:T(8,128)(2,1)S(1)}, bf16[4,128,256]{2,1,0:T(8,128)(2,1)S(1)}, u32[]{:S(2)}, u32[]{:S(2)}) collective-permute-start(bf16[4,128,256]{2,1,0:T(8,128)(2,1)S(1)} %rows_even.4.refs_0_.refs_1_), channel_id=1, source_target_pairs={{0,1},{1,0},{2,3},{3,2},{4,5},{5,4},{6,7},{7,6},{8,9},{9,8},{10,11... | collective-permute-start | bytes 786440 | tf_op jit(solution)/shard_map/ppermute | solution.py:500
  33.0 2.1 %rows_high.4.refs_3_ = bf16[12,128,256]{2,1,0:T(8,128)(2,1)S(1)} custom-call(s32[3]{0:T(128)S(1)} %pad_add_fusion.info, s32[256]{0:T(256)S(1)} %reshape.18.cols_ref, bf16[4,128,256]{2,1,0:T(8,128)(2,1)S(1)} %rows_even.3.refs_0_.refs_1_.refs_4_, bf16[4,128,256]{2,1,0:T(8,128)(2,1)S(1)} %rows_odd.3.refs_1_.refs_4_, ...), custom_call_target="tpu_custom_call" | custom-call | flops 1000 | bytes 1000 | tf_op jit(solution)/shard_map/rows_high/pallas_call | solution.py:184
  35.1 0.0 collective-permute-done.2.refs_0_
  35.1 1.1 %rows_odd.4.refs_1_ = bf16[4,128,256]{2,1,0:T(8,128)(2,1)S(1)} custom-call(s32[3]{0:T(128)S(1)} %pad_add_fusion.info, s32[256]{0:T(256)S(1)} %reshape.18.cols_ref, bf16[4,128,256]{2,1,0:T(8,128)(2,1)S(1)} %collective-permute-done.2.refs_0_, bf16[4,128,256]{2,1,0:T(8,128)(2,1)S(1)} %rows_odd.3.refs_1_.refs_4_, ...), custom_call_target="tpu_custom_call" | custom-call | flops 1000 | bytes 1000 | tf_op jit(solution)/shard_map/rows_odd/pallas_call | solution.py:184
  36.2 0.9 collective-permute-start.4
  37.1 2.1 %rows_high.5 = bf16[12,128,256]{2,1,0:T(8,128)(2,1)S(1)} custom-call(s32[3]{0:T(128)S(1)} %pad_add_fusion.info, s32[256]{0:T(256)S(1)} %reshape.18.cols_ref, bf16[4,128,256]{2,1,0:T(8,128)(2,1)S(1)} %rows_even.4.refs_0_.refs_1_, bf16[4,128,256]{2,1,0:T(8,128)(2,1)S(1)} %rows_odd.4.refs_1_, bf16[12,128,256]{2,1,0:T(8,128)(2,1)S(1)} %rows_low.4.refs_2_, ...), custom_call_target="tpu_custom_call" | custom-call | flops 1000 | bytes 1000 | tf_op jit(solution)/shard_map/rows_high/pallas_call | solution.py:184
  39.3 2.1 %rows_low.5 = bf16[12,128,256]{2,1,0:T(8,128)(2,1)S(1)} custom-call(s32[3]{0:T(128)S(1)} %pad_add_fusion.info, s32[256]{0:T(256)S(1)} %reshape.18.cols_ref, bf16[4,128,256]{2,1,0:T(8,128)(2,1)S(1)} %rows_even.4.refs_0_.refs_1_, bf16[4,128,256]{2,1,0:T(8,128)(2,1)S(1)} %rows_odd.4.refs_1_, bf16[12,128,256]{2,1,0:T(8,128)(2,1)S(1)} %rows_low.4.refs_2_, ...), custom_call_target="tpu_custom_call" | custom-call | flops 1000 | bytes 1000 | tf_op jit(solution)/shard_map/rows_low/pallas_call | solution.py:184
  41.4 0.7 collective-permute-done.5.refs_0_
  42.1 1.1 %rows_even.5 = bf16[4,128,256]{2,1,0:T(8,128)(2,1)S(1)} custom-call(s32[3]{0:T(128)S(1)} %pad_add_fusion.info, s32[256]{0:T(256)S(1)} %reshape.18.cols_ref, bf16[4,128,256]{2,1,0:T(8,128)(2,1)S(1)} %collective-permute-done.5.refs_0_, bf16[4,128,256]{2,1,0:T(8,128)(2,1)S(1)} %rows_even.4.refs_0_.refs_1_, bf16[12,128,256]{2,1,0:T(8,128)(2,1)S(1)} %rows_low.4.refs_2_, ...), custom_call_target="tpu_custom_call" | custom-call | flops 1000 | bytes 1000 | tf_op jit(solution)/shard_map/rows_even/pallas_call | solution.py:184
  43.3 0.1 collective-permute-start.9
  43.3 0.0 collective-permute-done.4.refs_0_
  43.3 0.5 collective-permute-start.8
  43.8 0.1 collective-permute-start.7
  43.9 1.1 %rows_odd.5 = bf16[4,128,256]{2,1,0:T(8,128)(2,1)S(1)} custom-call(s32[3]{0:T(128)S(1)} %pad_add_fusion.info, s32[256]{0:T(256)S(1)} %reshape.18.cols_ref, bf16[4,128,256]{2,1,0:T(8,128)(2,1)S(1)} %collective-permute-done.4.refs_0_, bf16[4,128,256]{2,1,0:T(8,128)(2,1)S(1)} %rows_odd.4.refs_1_, bf16[12,128,256]{2,1,0:T(8,128)(2,1)S(1)} %rows_low.4.refs_2_, ...), custom_call_target="tpu_custom_call" | custom-call | flops 99999997952 | bytes 1000 | tf_op jit(solution)/shard_map/rows_odd/pallas_call | solution.py:184
  45.0 0.5 collective-permute-start.6
  45.5 1.6 %collective-permute-done.7.refs_3_.refs_12_ = bf16[512,256]{1,0:T(8,128)(2,1)S(1)} collective-permute-done((bf16[512,256]{1,0:T(8,128)(2,1)S(1)}, bf16[512,256]{1,0:T(8,128)(2,1)S(1)}, u32[]{:S(2)}, u32[]{:S(2)}) %collective-permute-start.7) | collective-permute-done | bytes 262176 | tf_op jit(solution)/shard_map/ppermute | solution.py:503
  47.1 0.0 collective-permute-done.9.refs_5_.refs_14_
  47.1 2.7 %gram_share.2.refs_2_ = f32[640,128]{1,0:T(8,128)S(1)} custom-call(s32[3]{0:T(128)S(1)} %pad_add_fusion.info, bf16[512,256]{1,0:T(8,128)(2,1)S(1)} %bitcast.16, bf16[1536,256]{1,0:T(8,128)(2,1)S(1)} %bitcast.13, bf16[1536,256]{1,0:T(8,128)(2,1)S(1)} %bitcast.10, bf16[512,256]{1,0:T(8,128)(2,1)S(1)} %collective-permute-done.7.refs_3_.refs_12_, ...), custom_call_target="tpu_custom_call" | custom-call | flops 1000 | bytes 1000 | tf_op jit(solution)/shard_map/gram_share/pallas_call | solution.py:244
  49.8 0.0 collective-permute-done.6.refs_1_.refs_15_
  49.8 0.9 gram_share.3
  50.7 4.6 %collective-permute-start.10 = (f32[160,128]{1,0:T(8,128)S(1)}, f32[160,128]{1,0:T(8,128)S(1)}, u32[]{:S(2)}, u32[]{:S(2)}) collective-permute-start(f32[160,128]{1,0:T(8,128)S(1)} %get-tuple-element.56), channel_id=1, source_target_pairs={{0,1},{1,0},{2,3},{3,2},{4,5},{5,4},{6,7},{7,6},{8,9},{9,8},{10,11... | collective-permute-start | bytes 245768 | tf_op jit(solution)/shard_map/ppermute | solution.py:276
  55.2 0.4 collective-permute-start.11
  55.7 1.1 %collective-permute-start.12 = (f32[160,128]{1,0:T(8,128)S(1)}, f32[160,128]{1,0:T(8,128)S(1)}, u32[]{:S(2)}, u32[]{:S(2)}) collective-permute-start(f32[160,128]{1,0:T(8,128)S(1)} %get-tuple-element.58), channel_id=1, source_target_pairs={{0,3},{1,2},{2,1},{3,0},{4,7},{5,6},{6,5},{7,4},{8,11},{9,10},{10,... | collective-permute-start | bytes 245768 | tf_op jit(solution)/shard_map/ppermute | solution.py:276
  56.8 1.2 %collective-permute-done.10.b = f32[160,128]{1,0:T(8,128)S(1)} collective-permute-done((f32[160,128]{1,0:T(8,128)S(1)}, f32[160,128]{1,0:T(8,128)S(1)}, u32[]{:S(2)}, u32[]{:S(2)}) %collective-permute-start.10) | collective-permute-done | bytes 81952 | tf_op jit(solution)/shard_map/ppermute | solution.py:276
  58.0 3.4 %collective-permute-done.11.c = f32[160,128]{1,0:T(8,128)S(1)} collective-permute-done((f32[160,128]{1,0:T(8,128)S(1)}, f32[160,128]{1,0:T(8,128)S(1)}, u32[]{:S(2)}, u32[]{:S(2)}) %collective-permute-start.11) | collective-permute-done | bytes 81952 | tf_op jit(solution)/shard_map/ppermute | solution.py:276
  61.4 0.0 collective-permute-done.12.d
  61.4 1.2 %collective-permute-start.13 = (f32[160,128]{1,0:T(8,128)S(1)}, f32[160,128]{1,0:T(8,128)S(1)}, u32[]{:S(2)}, u32[]{:S(2)}) collective-permute-start(f32[160,128]{1,0:T(8,128)S(1)} %add_four.2.a), channel_id=1, source_target_pairs={{0,4},{1,5},{2,6},{3,7},{4,0},{5,1},{6,2},{7,3},{8,12},{9,13},{10,... | collective-permute-start | bytes 245768 | tf_op jit(solution)/shard_map/ppermute | solution.py:276
  62.6 1.9 %collective-permute-start.14 = (f32[160,128]{1,0:T(8,128)S(1)}, f32[160,128]{1,0:T(8,128)S(1)}, u32[]{:S(2)}, u32[]{:S(2)}) collective-permute-start(f32[160,128]{1,0:T(8,128)S(1)} %add_four.2.a), channel_id=1, source_target_pairs={{0,8},{1,9},{2,10},{3,11},{4,12},{5,13},{6,14},{7,15},{8,0},{9,1},... | collective-permute-start | bytes 245768 | tf_op jit(solution)/shard_map/ppermute | solution.py:276
  64.6 1.3 %collective-permute-start.15 = (f32[160,128]{1,0:T(8,128)S(1)}, f32[160,128]{1,0:T(8,128)S(1)}, u32[]{:S(2)}, u32[]{:S(2)}) collective-permute-start(f32[160,128]{1,0:T(8,128)S(1)} %add_four.2.a), channel_id=1, source_target_pairs={{0,12},{1,13},{2,14},{3,15},{4,8},{5,9},{6,10},{7,11},{8,4},{9,5},... | collective-permute-start | bytes 245768 | tf_op jit(solution)/shard_map/ppermute | solution.py:276
  65.9 0.1 collective-permute-done.13.b
  66.0 3.7 %collective-permute-done.14.c = f32[160,128]{1,0:T(8,128)S(1)} collective-permute-done((f32[160,128]{1,0:T(8,128)S(1)}, f32[160,128]{1,0:T(8,128)S(1)}, u32[]{:S(2)}, u32[]{:S(2)}) %collective-permute-start.14) | collective-permute-done | bytes 81952 | tf_op jit(solution)/shard_map/ppermute | solution.py:276
  69.7 1.2 %collective-permute-done.15.d = f32[160,128]{1,0:T(8,128)S(1)} collective-permute-done((f32[160,128]{1,0:T(8,128)S(1)}, f32[160,128]{1,0:T(8,128)S(1)}, u32[]{:S(2)}, u32[]{:S(2)}) %collective-permute-start.15) | collective-permute-done | bytes 81952 | tf_op jit(solution)/shard_map/ppermute | solution.py:276
  70.9 1.4 %collective-permute-start.16 = (f32[160,128]{1,0:T(8,128)S(1)}, f32[160,128]{1,0:T(8,128)S(1)}, u32[]{:S(2)}, u32[]{:S(2)}) collective-permute-start(f32[160,128]{1,0:T(8,128)S(1)} %add_four.3.refs_0_), channel_id=1, source_target_pairs={{0,1},{1,0},{2,3},{3,2},{4,5},{5,4},{6,7},{7,6},{8,9},{9,8},{10,11... | collective-permute-start | bytes 245768 | tf_op jit(solution)/shard_map/ppermute | solution.py:276
  72.3 0.9 collective-permute-start.17
  73.3 1.2 %collective-permute-start.18 = (f32[160,128]{1,0:T(8,128)S(1)}, f32[160,128]{1,0:T(8,128)S(1)}, u32[]{:S(2)}, u32[]{:S(2)}) collective-permute-start(f32[160,128]{1,0:T(8,128)S(1)} %add_four.3.refs_0_), channel_id=1, source_target_pairs={{0,3},{1,2},{2,1},{3,0},{4,7},{5,6},{6,5},{7,4},{8,11},{9,10},{10,... | collective-permute-start | bytes 245768 | tf_op jit(solution)/shard_map/ppermute | solution.py:276
  74.5 0.9 collective-permute-done.16.refs_1_
  75.4 0.0 collective-permute-start.20
  75.5 1.3 %collective-permute-done.17.refs_2_ = f32[160,128]{1,0:T(8,128)S(1)} collective-permute-done((f32[160,128]{1,0:T(8,128)S(1)}, f32[160,128]{1,0:T(8,128)S(1)}, u32[]{:S(2)}, u32[]{:S(2)}) %collective-permute-start.17) | collective-permute-done | bytes 81952 | tf_op jit(solution)/shard_map/ppermute | solution.py:276
  76.8 1.8 %collective-permute-done.18.refs_3_ = f32[160,128]{1,0:T(8,128)S(1)} collective-permute-done((f32[160,128]{1,0:T(8,128)S(1)}, f32[160,128]{1,0:T(8,128)S(1)}, u32[]{:S(2)}, u32[]{:S(2)}) %collective-permute-start.18) | collective-permute-done | bytes 81952 | tf_op jit(solution)/shard_map/ppermute | solution.py:276
  78.6 0.0 collective-permute-start.22
  78.6 0.0 collective-permute-done.19.refs_4_
  78.6 0.0 collective-permute-done.20.refs_5_
  78.6 1.3 %collective-permute-done.22.refs_7_ = f32[160,128]{1,0:T(8,128)S(1)} collective-permute-done((f32[160,128]{1,0:T(8,128)S(1)}, f32[160,128]{1,0:T(8,128)S(1)}, u32[]{:S(2)}, u32[]{:S(2)}) %collective-permute-start.22) | collective-permute-done | bytes 81952 | tf_op jit(solution)/shard_map/ppermute | solution.py:503
  79.9 19.5 %rotate.1 = bf16[4096,256]{1,0:T(8,128)(2,1)} custom-call(s32[3]{0:T(128)S(1)} %pad_add_fusion.info, f32[160,128]{1,0:T(8,128)S(1)} %add_four.3.refs_0_, f32[160,128]{1,0:T(8,128)S(1)} %collective-permute-done.16.refs_1_, f32[160,128]{1,0:T(8,128)S(1)} %collective-permute-done.17.refs_2_, f32[160,128]{1,0:T(8,128)S(1)} %collective-permute-done.18.refs_3_, ...), custom_call_target="tpu_custom_call" | custom-call | flops 17985175552 | bytes 6291456 | tf_op jit(solution)/shard_map/rotate/pallas_call | solution.py:460
  (10 shorter events, 0.1 us)
Async XLA Ops:
  1.6 1.6 %copy-start.1 = (bf16[4096,256]{1,0:T(8,128)(2,1)S(1)}, bf16[4096,256]{1,0:T(8,128)(2,1)}, u32[]{:S(2)}) copy-start(bf16[4096,256]{1,0:T(8,128)(2,1)} %param.4) | copy-start | bytes 6291460
  3.2 3.7 %copy-start.2 = (bf16[4096,256]{1,0:T(8,128)(2,1)S(1)}, bf16[4096,256]{1,0:T(8,128)(2,1)}, u32[]{:S(2)}) copy-start(bf16[4096,256]{1,0:T(8,128)(2,1)} %param.4) | copy-start | bytes 6291460
  3.8 10.5 %collective-permute-start.1 = (bf16[4,128,256]{2,1,0:T(8,128)(2,1)S(1)}, bf16[4,128,256]{2,1,0:T(8,128)(2,1)S(1)}, u32[]{:S(2)}, u32[]{:S(2)}) collective-permute-start(bf16[4,128,256]{2,1,0:T(8,128)(2,1)S(1)} %get-tuple-element.40.refs_1_.refs_0_.refs_4_), channel_id=1, source_target_pairs={{0,1},{1,0},{2,3},{3,2},{4,5},{5,4},{6,7},{7,6},{8,9},{9,8},{10,11... | collective-permute-start | bytes 786440 | tf_op jit(solution)/shard_map/ppermute | solution.py:500
  6.8 3.4 %copy-start = (bf16[32,8,128,128]{3,2,1,0:T(8,128)(2,1)S(1)}, bf16[32,8,128,128]{3,2,1,0:T(8,128)(2,1)}, u32[]{:S(2)}) copy-start(bf16[32,8,128,128]{3,2,1,0:T(8,128)(2,1)} %blocks_ref.1) | copy-start | bytes 25165828
  11.6 10.4 %collective-permute-start = (bf16[4,128,256]{2,1,0:T(8,128)(2,1)S(1)}, bf16[4,128,256]{2,1,0:T(8,128)(2,1)S(1)}, u32[]{:S(2)}, u32[]{:S(2)}) collective-permute-start(bf16[4,128,256]{2,1,0:T(8,128)(2,1)S(1)} %get-tuple-element.37.refs_1_.refs_4_), channel_id=1, source_target_pairs={{1,2},{2,1},{3,4},{4,3},{5,6},{6,5},{7,8},{8,7},{9,10},{10,9},{11,... | collective-permute-start | bytes 786440 | tf_op jit(solution)/shard_map/ppermute | solution.py:500
  15.5 12.8 %collective-permute-start.3 = (bf16[4,128,256]{2,1,0:T(8,128)(2,1)S(1)}, bf16[4,128,256]{2,1,0:T(8,128)(2,1)S(1)}, u32[]{:S(2)}, u32[]{:S(2)}) collective-permute-start(bf16[4,128,256]{2,1,0:T(8,128)(2,1)S(1)} %rows_even.3.refs_0_.refs_1_.refs_4_), channel_id=1, source_target_pairs={{0,1},{1,0},{2,3},{3,2},{4,5},{5,4},{6,7},{7,6},{8,9},{9,8},{10,11... | collective-permute-start | bytes 786440 | tf_op jit(solution)/shard_map/ppermute | solution.py:500
  23.1 12.1 %collective-permute-start.2 = (bf16[4,128,256]{2,1,0:T(8,128)(2,1)S(1)}, bf16[4,128,256]{2,1,0:T(8,128)(2,1)S(1)}, u32[]{:S(2)}, u32[]{:S(2)}) collective-permute-start(bf16[4,128,256]{2,1,0:T(8,128)(2,1)S(1)} %rows_odd.3.refs_1_.refs_4_), channel_id=1, source_target_pairs={{1,2},{2,1},{3,4},{4,3},{5,6},{6,5},{7,8},{8,7},{9,10},{10,9},{11,... | collective-permute-start | bytes 786440 | tf_op jit(solution)/shard_map/ppermute | solution.py:500
  29.4 12.8 %collective-permute-start.5 = (bf16[4,128,256]{2,1,0:T(8,128)(2,1)S(1)}, bf16[4,128,256]{2,1,0:T(8,128)(2,1)S(1)}, u32[]{:S(2)}, u32[]{:S(2)}) collective-permute-start(bf16[4,128,256]{2,1,0:T(8,128)(2,1)S(1)} %rows_even.4.refs_0_.refs_1_), channel_id=1, source_target_pairs={{0,1},{1,0},{2,3},{3,2},{4,5},{5,4},{6,7},{7,6},{8,9},{9,8},{10,11... | collective-permute-start | bytes 786440 | tf_op jit(solution)/shard_map/ppermute | solution.py:500
  36.2 7.1 %collective-permute-start.4 = (bf16[4,128,256]{2,1,0:T(8,128)(2,1)S(1)}, bf16[4,128,256]{2,1,0:T(8,128)(2,1)S(1)}, u32[]{:S(2)}, u32[]{:S(2)}) collective-permute-start(bf16[4,128,256]{2,1,0:T(8,128)(2,1)S(1)} %rows_odd.4.refs_1_), channel_id=1, source_target_pairs={{1,2},{2,1},{3,4},{4,3},{5,6},{6,5},{7,8},{8,7},{9,10},{10,9},{11,... | collective-permute-start | bytes 786440 | tf_op jit(solution)/shard_map/ppermute | solution.py:500
  43.3 3.9 %collective-permute-start.9 = (bf16[1536,256]{1,0:T(8,128)(2,1)S(1)}, bf16[1536,256]{1,0:T(8,128)(2,1)S(1)}, u32[]{:S(2)}, u32[]{:S(2)}) collective-permute-start(bf16[1536,256]{1,0:T(8,128)(2,1)S(1)} %bitcast.9), channel_id=1, source_target_pairs={{0,16},{16,0},{1,17},{17,1},{2,18},{18,2},{3,19},{19,3},{4,20},{20... | collective-permute-start | bytes 2359304 | tf_op jit(solution)/shard_map/ppermute | solution.py:503
  43.3 3.8 %collective-permute-start.8 = (bf16[1536,256]{1,0:T(8,128)(2,1)S(1)}, bf16[1536,256]{1,0:T(8,128)(2,1)S(1)}, u32[]{:S(2)}, u32[]{:S(2)}) collective-permute-start(bf16[1536,256]{1,0:T(8,128)(2,1)S(1)} %bitcast.12), channel_id=1, source_target_pairs={{0,16},{16,0},{1,17},{17,1},{2,18},{18,2},{3,19},{19,3},{4,20},{20... | collective-permute-start | bytes 2359304 | tf_op jit(solution)/shard_map/ppermute | solution.py:503
  43.8 3.3 %collective-permute-start.7 = (bf16[512,256]{1,0:T(8,128)(2,1)S(1)}, bf16[512,256]{1,0:T(8,128)(2,1)S(1)}, u32[]{:S(2)}, u32[]{:S(2)}) collective-permute-start(bf16[512,256]{1,0:T(8,128)(2,1)S(1)} %bitcast.15), channel_id=1, source_target_pairs={{0,16},{16,0},{1,17},{17,1},{2,18},{18,2},{3,19},{19,3},{4,20},{20... | collective-permute-start | bytes 786440 | tf_op jit(solution)/shard_map/ppermute | solution.py:503
  45.0 4.8 %collective-permute-start.6 = (bf16[512,256]{1,0:T(8,128)(2,1)S(1)}, bf16[512,256]{1,0:T(8,128)(2,1)S(1)}, u32[]{:S(2)}, u32[]{:S(2)}) collective-permute-start(bf16[512,256]{1,0:T(8,128)(2,1)S(1)} %bitcast.18), channel_id=1, source_target_pairs={{0,16},{16,0},{1,17},{17,1},{2,18},{18,2},{3,19},{19,3},{4,20},{20... | collective-permute-start | bytes 786440 | tf_op jit(solution)/shard_map/ppermute | solution.py:503
  50.7 7.3 %collective-permute-start.10 = (f32[160,128]{1,0:T(8,128)S(1)}, f32[160,128]{1,0:T(8,128)S(1)}, u32[]{:S(2)}, u32[]{:S(2)}) collective-permute-start(f32[160,128]{1,0:T(8,128)S(1)} %get-tuple-element.56), channel_id=1, source_target_pairs={{0,1},{1,0},{2,3},{3,2},{4,5},{5,4},{6,7},{7,6},{8,9},{9,8},{10,11... | collective-permute-start | bytes 245768 | tf_op jit(solution)/shard_map/ppermute | solution.py:276
  55.2 6.1 %collective-permute-start.11 = (f32[160,128]{1,0:T(8,128)S(1)}, f32[160,128]{1,0:T(8,128)S(1)}, u32[]{:S(2)}, u32[]{:S(2)}) collective-permute-start(f32[160,128]{1,0:T(8,128)S(1)} %get-tuple-element.57), channel_id=1, source_target_pairs={{0,2},{1,3},{2,0},{3,1},{4,6},{5,7},{6,4},{7,5},{8,10},{9,11},{10,... | collective-permute-start | bytes 245768 | tf_op jit(solution)/shard_map/ppermute | solution.py:276
  55.7 5.7 %collective-permute-start.12 = (f32[160,128]{1,0:T(8,128)S(1)}, f32[160,128]{1,0:T(8,128)S(1)}, u32[]{:S(2)}, u32[]{:S(2)}) collective-permute-start(f32[160,128]{1,0:T(8,128)S(1)} %get-tuple-element.58), channel_id=1, source_target_pairs={{0,3},{1,2},{2,1},{3,0},{4,7},{5,6},{6,5},{7,4},{8,11},{9,10},{10,... | collective-permute-start | bytes 245768 | tf_op jit(solution)/shard_map/ppermute | solution.py:276
  61.4 4.6 %collective-permute-start.13 = (f32[160,128]{1,0:T(8,128)S(1)}, f32[160,128]{1,0:T(8,128)S(1)}, u32[]{:S(2)}, u32[]{:S(2)}) collective-permute-start(f32[160,128]{1,0:T(8,128)S(1)} %add_four.2.a), channel_id=1, source_target_pairs={{0,4},{1,5},{2,6},{3,7},{4,0},{5,1},{6,2},{7,3},{8,12},{9,13},{10,... | collective-permute-start | bytes 245768 | tf_op jit(solution)/shard_map/ppermute | solution.py:276
  62.6 7.1 %collective-permute-start.14 = (f32[160,128]{1,0:T(8,128)S(1)}, f32[160,128]{1,0:T(8,128)S(1)}, u32[]{:S(2)}, u32[]{:S(2)}) collective-permute-start(f32[160,128]{1,0:T(8,128)S(1)} %add_four.2.a), channel_id=1, source_target_pairs={{0,8},{1,9},{2,10},{3,11},{4,12},{5,13},{6,14},{7,15},{8,0},{9,1},... | collective-permute-start | bytes 245768 | tf_op jit(solution)/shard_map/ppermute | solution.py:276
  64.6 6.3 %collective-permute-start.15 = (f32[160,128]{1,0:T(8,128)S(1)}, f32[160,128]{1,0:T(8,128)S(1)}, u32[]{:S(2)}, u32[]{:S(2)}) collective-permute-start(f32[160,128]{1,0:T(8,128)S(1)} %add_four.2.a), channel_id=1, source_target_pairs={{0,12},{1,13},{2,14},{3,15},{4,8},{5,9},{6,10},{7,11},{8,4},{9,5},... | collective-permute-start | bytes 245768 | tf_op jit(solution)/shard_map/ppermute | solution.py:276
  70.9 4.5 %collective-permute-start.16 = (f32[160,128]{1,0:T(8,128)S(1)}, f32[160,128]{1,0:T(8,128)S(1)}, u32[]{:S(2)}, u32[]{:S(2)}) collective-permute-start(f32[160,128]{1,0:T(8,128)S(1)} %add_four.3.refs_0_), channel_id=1, source_target_pairs={{0,1},{1,0},{2,3},{3,2},{4,5},{5,4},{6,7},{7,6},{8,9},{9,8},{10,11... | collective-permute-start | bytes 245768 | tf_op jit(solution)/shard_map/ppermute | solution.py:276
  72.3 4.4 %collective-permute-start.17 = (f32[160,128]{1,0:T(8,128)S(1)}, f32[160,128]{1,0:T(8,128)S(1)}, u32[]{:S(2)}, u32[]{:S(2)}) collective-permute-start(f32[160,128]{1,0:T(8,128)S(1)} %add_four.3.refs_0_), channel_id=1, source_target_pairs={{0,2},{1,3},{2,0},{3,1},{4,6},{5,7},{6,4},{7,5},{8,10},{9,11},{10,... | collective-permute-start | bytes 245768 | tf_op jit(solution)/shard_map/ppermute | solution.py:276
  73.3 5.3 %collective-permute-start.18 = (f32[160,128]{1,0:T(8,128)S(1)}, f32[160,128]{1,0:T(8,128)S(1)}, u32[]{:S(2)}, u32[]{:S(2)}) collective-permute-start(f32[160,128]{1,0:T(8,128)S(1)} %add_four.3.refs_0_), channel_id=1, source_target_pairs={{0,3},{1,2},{2,1},{3,0},{4,7},{5,6},{6,5},{7,4},{8,11},{9,10},{10,... | collective-permute-start | bytes 245768 | tf_op jit(solution)/shard_map/ppermute | solution.py:276
  74.5 4.1 %collective-permute-start.19 = (f32[160,128]{1,0:T(8,128)S(1)}, f32[160,128]{1,0:T(8,128)S(1)}, u32[]{:S(2)}, u32[]{:S(2)}) collective-permute-start(f32[160,128]{1,0:T(8,128)S(1)} %add_four.3.refs_0_), channel_id=1, source_target_pairs={{0,16},{16,0},{1,17},{17,1},{2,18},{18,2},{3,19},{19,3},{4,20},{20... | collective-permute-start | bytes 245768 | tf_op jit(solution)/shard_map/ppermute | solution.py:503
  75.4 3.2 %collective-permute-start.20 = (f32[160,128]{1,0:T(8,128)S(1)}, f32[160,128]{1,0:T(8,128)S(1)}, u32[]{:S(2)}, u32[]{:S(2)}) collective-permute-start(f32[160,128]{1,0:T(8,128)S(1)} %collective-permute-done.16.refs_1_), channel_id=1, source_target_pairs={{0,16},{16,0},{1,17},{17,1},{2,18},{18,2},{3,19},{19,3},{4,20},{20... | collective-permute-start | bytes 245768 | tf_op jit(solution)/shard_map/ppermute | solution.py:503
  76.7 1.9 %collective-permute-start.21 = (f32[160,128]{1,0:T(8,128)S(1)}, f32[160,128]{1,0:T(8,128)S(1)}, u32[]{:S(2)}, u32[]{:S(2)}) collective-permute-start(f32[160,128]{1,0:T(8,128)S(1)} %collective-permute-done.17.refs_2_), channel_id=1, source_target_pairs={{0,16},{16,0},{1,17},{17,1},{2,18},{18,2},{3,19},{19,3},{4,20},{20... | collective-permute-start | bytes 245768 | tf_op jit(solution)/shard_map/ppermute | solution.py:503
  78.6 1.3 %collective-permute-start.22 = (f32[160,128]{1,0:T(8,128)S(1)}, f32[160,128]{1,0:T(8,128)S(1)}, u32[]{:S(2)}, u32[]{:S(2)}) collective-permute-start(f32[160,128]{1,0:T(8,128)S(1)} %collective-permute-done.18.refs_3_), channel_id=1, source_target_pairs={{0,16},{16,0},{1,17},{17,1},{2,18},{18,2},{3,19},{19,3},{4,20},{20... | collective-permute-start | bytes 245768 | tf_op jit(solution)/shard_map/ppermute | solution.py:503

commit v5 on v4

--- a/solution.py
+++ b/solution.py
@@ -10,7 +10,6 @@
 HALO_T = 4
 STEPS = 3
 ITERS = 8
-WAYS = 4
 GROUP = 4
 
 SMALL = pl.CostEstimate(flops=1000, bytes_accessed=1000, transcendentals=0)
@@ -193,94 +192,115 @@
     )(info, cols, *args)
 
 
-def gram_kernel(pairs, chunk, last, info, *refs):
-    fields = refs[: 2 * pairs]
-    start_ref = refs[2 * pairs] if last else None
-    square, cross = refs[-2:]
-    half = square.shape[0] // 2
-    square[...] = jnp.zeros(square.shape, F32)
-    cross[...] = jnp.zeros(cross.shape, F32)
+ACROSS = (((0,), (0,)), ((), ()))
+
+
+def add_square(chunk, own_ref, square):
+    def add(index, carry):
+        own = own_ref[pl.ds(pl.multiple_of(index * chunk, chunk), chunk), :]
+        square[...] += lax.dot_general(own, own, ACROSS, preferred_element_type=F32)
+        return carry
+
+    lax.fori_loop(0, own_ref.shape[0] // chunk, add, 0)
+
+
+def add_cross(chunk, info, own_ref, other_ref, cross):
+    half = cross.shape[0]
     is_first = info[PART] == 0
-    across = (((0,), (0,)), ((), ()))
-    for own_ref, other_ref in zip(fields[:pairs], fields[pairs:]):
-
-        def add(index, carry):
-            rows = pl.ds(pl.multiple_of(index * chunk, chunk), chunk)
-            own, other = own_ref[rows, :], other_ref[rows, :]
-            square[...] += lax.dot_general(own, own, across, preferred_element_type=F32)
-            left = jnp.where(is_first, own[:, :half], other[:, half:])
-            right = jnp.where(is_first, other, own)
-            cross[...] += lax.dot_general(left, right, across, preferred_element_type=F32)
-            return carry
-
-        lax.fori_loop(0, own_ref.shape[0] // chunk, add, 0)
+
+    def add(index, carry):
+        rows = pl.ds(pl.multiple_of(index * chunk, chunk), chunk)
+        own, other = own_ref[rows, :], other_ref[rows, :]
+        left = jnp.where(is_first, own[:, :half], other[:, half:])
+        right = jnp.where(is_first, other, own)
+        cross[...] += lax.dot_general(left, right, ACROSS, preferred_element_type=F32)
+        return carry
+
+    lax.fori_loop(0, own_ref.shape[0] // chunk, add, 0)
+
+
+def square_kernel(chunk, *refs):
+    refs[-1][...] = jnp.zeros(refs[-1].shape, F32)
+    for own_ref in refs[:-1]:
+        add_square(chunk, own_ref, refs[-1])
+
+
+def cross_kernel(chunk, info, *refs):
+    count = len(refs) // 2
+    refs[-1][...] = jnp.zeros(refs[-1].shape, F32)
+    for own_ref, other_ref in zip(refs[:count], refs[count:-1]):
+        add_cross(chunk, info, own_ref, other_ref, refs[-1])
+
+
+def share_kernel(chunk, info, own_ref, other_ref, square_ref, cross_ref, out_ref, square, cross):
+    square[...] = square_ref[...]
+    cross[...] = cross_ref[...]
+    add_square(chunk, own_ref, square)
+    add_cross(chunk, info, own_ref, other_ref, cross)
+    half = cross.shape[0]
     blocks = [
         square[:half, :half], square[:half, half:], square[half:, half:],
         cross[:, :half], cross[:, half:],
     ]
-    if not last:
-        for i, block in enumerate(blocks):
-            refs[2 * pairs][pl.ds(i * half, half), :] = block
-        return
-    outs, share = refs[2 * pairs + 1 : 2 * pairs + 1 + WAYS], refs[-3]
     for i, block in enumerate(blocks):
-        at = pl.ds(i * half, half)
-        share[at, :] = block + start_ref[at, :]
-    piece = outs[0].shape[0]
-    quarter = info[PATCH] % WAYS
-    for d, out in enumerate(outs):
-        out[...] = share[pl.ds(pl.multiple_of((quarter ^ d) * piece, 8), piece), :]
-
-
-def gram_share(info, owns, others, start):
-    width = owns[0].shape[1]
-    half = width // 2
-    chunk = min(own.shape[0] for own in owns)
-    last = start is not None
-    args = list(owns) + list(others) + ([start] if last else [])
-    shape = jax.ShapeDtypeStruct((5 * half, half), F32)
-    piece = jax.ShapeDtypeStruct((5 * half // WAYS, half), F32)
-    scratch = [pltpu.VMEM((width, width), F32), pltpu.VMEM((half, width), F32)]
+        out_ref[pl.ds(i * half, half), :] = block
+    used = len(blocks) * half
+    if used < out_ref.shape[0]:
+        out_ref[used:, :] = jnp.zeros((out_ref.shape[0] - used, half), F32)
+
+
+def gram_call(body, name, args, shape, scratch=(), scalars=()):
     return pl.pallas_call(
-        functools.partial(gram_kernel, len(owns), chunk, last),
-        in_specs=[SMEM] + [VMEM] * len(args),
-        out_specs=[VMEM] * WAYS if last else VMEM,
-        out_shape=[piece] * WAYS if last else shape,
-        scratch_shapes=([pltpu.VMEM(shape.shape, F32)] if last else []) + scratch,
+        body,
+        in_specs=[SMEM] * len(scalars) + [VMEM] * len(args),
+        out_specs=VMEM,
+        out_shape=jax.ShapeDtypeStruct(shape, F32),
+        scratch_shapes=scratch,
         compiler_params=SMALL_VMEM,
         cost_estimate=SMALL,
-        name="gram_share",
-    )(info, *args)
-
-
-def add_kernel(a, b, c, d, out):
-    out[...] = (a[...] + b[...]) + (c[...] + d[...])
-
-
-def add_four(values):
-    return pl.pallas_call(
-        add_kernel,
-        in_specs=[VMEM] * WAYS,
-        out_specs=VMEM,
-        out_shape=jax.ShapeDtypeStruct(values[0].shape, F32),
-        compiler_params=SMALL_VMEM,
-        cost_estimate=SMALL,
-        name="add_four",
-    )(*values)
-
-
-def sum_over_patch(parts):
+        name=name,
+    )(*scalars, *args)
+
+
+def gram_square(owns):
+    chunk, width = min(own.shape[0] for own in owns), owns[0].shape[1]
+    body = functools.partial(square_kernel, chunk)
+    return gram_call(body, "gram_square", owns, (width, width))
+
+
+def gram_cross(info, owns, others):
+    chunk, width = min(own.shape[0] for own in owns), owns[0].shape[1]
+    body = functools.partial(cross_kernel, chunk)
+    shape = (width // 2, width)
+    return gram_call(body, "gram_cross", owns + others, shape, scalars=[info])
+
+
+def gram_share(info, own, other, square, cross, count):
+    width = own.shape[1]
+    half = width // 2
+    rows = -(-5 * half // (8 * count)) * 8 * count
+    body = functools.partial(share_kernel, own.shape[0])
+    scratch = [pltpu.VMEM((width, width), F32), pltpu.VMEM((half, width), F32)]
+    args = [own, other, square, cross]
+    return gram_call(body, "gram_share", args, (rows, half), scratch, [info])
+
+
+def sum_kernel(parts_ref, out_ref):
+    count = parts_ref.shape[0]
+    values = [parts_ref[i] for i in range(count)]
+    while len(values) > 1:
+        pairs = zip(values[::2], values[1::2])
+        values = [one + two for one, two in pairs] + values[len(values) // 2 * 2 :]
+    for i in range(count):
+        out_ref[i] = values[0]
+
+
+def sum_over_patch(share):
     count = lax.axis_size("patch")
-
-    def exchange(value, distance):
-        return lax.ppermute(value, "patch", [(i, i ^ distance) for i in range(count)])
-
-    total = add_four([parts[0]] + [exchange(parts[d], d) for d in range(1, WAYS)])
-    stride = WAYS
-    while stride < count:
-        total = add_four([total] + [exchange(total, d * stride) for d in range(1, WAYS)])
-        stride *= WAYS
-    return [total] + [exchange(total, d) for d in range(1, WAYS)]
+    parts = share.reshape(count, -1, share.shape[1])
+    parts = lax.all_to_all(parts, "patch", 0, 0, tiled=True)
+    totals = gram_call(sum_kernel, "sum_parts", [parts], parts.shape)
+    return lax.all_to_all(totals, "patch", 0, 0, tiled=True).reshape(share.shape)
 
 
 def split(value):
@@ -288,64 +308,50 @@
     return high, (value - high.astype(F32)).astype(BF16)
 
 
-def put_row(ref, size, col, value):
-    width = value.shape[0]
-    high, low = split(value)
-    for i, piece in enumerate((high, high, low)):
-        ref[:, pl.ds(i * size + col * width, width)] = piece
-
-
-def put_col(ref, size, row, col, value):
-    width = value.shape[0]
-    high, low = split(value)
-    for i, piece in enumerate((high, low, high)):
-        ref[pl.ds(i * size + row * width, width), pl.ds(col * width, width)] = piece
-
-
-def put_left(refs, blocks):
-    row_ref, col_ref = refs
-    size = 2 * blocks[0].shape[0]
-    put_row(row_ref, size, 0, blocks[0])
-    put_row(row_ref, size, 1, blocks[1])
-    put_col(col_ref, size, 0, 0, blocks[1])
-    put_col(col_ref, size, 1, 0, blocks[2])
-
-
-def put_right(refs, blocks):
-    last_ref, all_ref = refs
-    size = 2 * blocks[0].shape[0]
-    across = blocks[1].T
-    put_col(all_ref, size, 0, 0, blocks[0])
-    put_col(all_ref, size, 0, 1, blocks[1])
-    put_col(all_ref, size, 1, 0, across)
-    put_col(all_ref, size, 1, 1, blocks[2])
-    put_row(last_ref, size, 0, across)
-    put_row(last_ref, size, 1, blocks[2])
-
-
-def times_middle(blocks, left, right):
+def put(pair, blocks, right=False):
     width = blocks[0].shape[0]
-    first = dot(left[0][...], right[1][...])
-    second = dot(right[0][...], left[1][...])
-    parts = first[:, :width], first[:, width:], second
-    return tuple(1.5 * block - 0.5 * part for block, part in zip(blocks, parts))
-
-
-def middle(blocks):
-    first, across, second = blocks
-    row = lax.broadcasted_iota(jnp.int32, first.shape, 0)
-    col = lax.broadcasted_iota(jnp.int32, first.shape, 1)
-    diagonal = jnp.where(row == col, 1.5, 0.0)
-    return diagonal - 0.5 * first, -0.5 * across, diagonal - 0.5 * second
-
-
-def finish_kernel(total_rows, chunk, info, *refs):
-    mine, theirs = refs[:WAYS], refs[WAYS : 2 * WAYS]
-    fields, out_ref = refs[2 * WAYS : 2 * WAYS + 8], refs[2 * WAYS + 8]
-    shares, x_ref, x_held, w_held, z_held, *rest = refs[2 * WAYS + 9 :]
-    x_left, w_left, z_left, x_right = rest[0:2], rest[2:4], rest[4:6], (rest[6:8], rest[8:10])
-    wide, result, sem, out_sem = rest[10:]
-    part, quarter = info[PART], info[PATCH] % WAYS
+    places = [(0, 0), (0, 1), (1, 1)]
+    if right:
+        blocks, places = tuple(blocks) + (blocks[1].T,), places + [(1, 0)]
+    for (row, col), block in zip(places, blocks):
+        for i, piece in enumerate(split(block)):
+            pair[i, pl.ds(row * width, width), pl.ds(col * width, width)] = piece
+
+
+def product3(left, right):
+    rows = left[0].shape[0]
+    both = dot(jnp.concatenate(left, axis=0), right[0])
+    return both[:rows] + both[rows:] + dot(left[0], right[1])
+
+
+def product(left, right):
+    width = left.shape[1] // 2
+    first = product3(
+        (left[0, :width, :], left[1, :width, :]), (right[0], right[1])
+    )
+    second = product3(
+        (right[0, width:, :], right[1, width:, :]), (left[0, :, width:], left[1, :, width:])
+    )
+    return first[:, :width], first[:, width:], second
+
+
+def combine(*terms, unit=0.0):
+    width = terms[0][1][0].shape[0]
+    row = lax.broadcasted_iota(jnp.int32, (width, width), 0)
+    col = lax.broadcasted_iota(jnp.int32, (width, width), 1)
+    diagonal = jnp.where(row == col, unit, 0.0)
+    out = []
+    for i in range(3):
+        value = functools.reduce(jnp.add, [factor * matrix[i] for factor, matrix in terms])
+        out.append(value if i == 1 else value + diagonal)
+    return tuple(out)
+
+
+def finish_kernel(total_rows, chunk, info, mine, theirs, *refs):
+    fields, out_ref = refs[:8], refs[8]
+    x_ref, x_held, x_pair, q_pair, u_pair, n_pair, v_pair, z_pair = refs[9:17]
+    wide, result, sem, out_sem = refs[17:]
+    part = info[PART]
     size = x_ref.shape[0]
     width = size // 2
     half = width // 2
@@ -364,14 +370,9 @@
     for copy in copies:
         copy.start()
 
-    piece = mine[0].shape[0]
-    for d in range(WAYS):
-        rows = pl.ds(pl.multiple_of((quarter ^ d) * piece, 8), piece)
-        shares[part, rows, :] = mine[d][...]
-        shares[1 - part, rows, :] = theirs[d][...]
-
     def block(side, index):
-        return shares[side, pl.ds(index * half, half), :]
+        rows = pl.ds(index * half, half)
+        return jnp.where(part == side, mine[rows, :], theirs[rows, :])
 
     def place(row, col, value):
         x_ref[pl.ds(row * half, half), pl.ds(col * half, half)] = value
@@ -388,44 +389,38 @@
     gram = x_ref[:width, :width], x_ref[:width, width:], x_ref[width:, width:]
     squares = gram[0] * gram[0] + 2.0 * (gram[1] * gram[1]) + gram[2] * gram[2]
     norm = jnp.sqrt(jnp.sum(squares, keepdims=True))
-    def hold(ref, blocks):
-        for i, value in enumerate(blocks):
-            ref[i] = value
-
-    def held(ref):
-        return tuple(ref[i] for i in range(3))
-
-    def set_x(x, right):
-        hold(x_held, x)
-        put_left(x_left, x)
-        put_right(right, x)
-
-    def advance(now, then):
-        w = times_middle(held(x_held), x_left, now)
-        hold(w_held, w)
-        put_left(w_left, w)
-        z = times_middle(held(z_held), z_left, now)
-        x = times_middle(w, w_left, now)
-        hold(z_held, z)
-        put_left(z_left, z)
-        set_x(x, then)
-
-    x = tuple(value / norm for value in gram)
-    set_x(x, x_right[0])
-    z = middle(x)
-    hold(z_held, z)
-    put_left(z_left, z)
-    w = times_middle(x, x_left, x_right[0])
-    put_left(w_left, w)
-    set_x(times_middle(w, w_left, x_right[0]), x_right[1])
-
-    def sweeps(index, carry):
-        advance(x_right[1], x_right[0])
-        advance(x_right[0], x_right[1])
+
+    def set_x(x):
+        put(x_pair, x, right=True)
+        for i, value in enumerate(x):
+            x_held[i] = value
+
+    def two_sweeps(first=False, last=False):
+        x = tuple(x_held[i] for i in range(3))
+        q = product(x_pair, x_pair)
+        put(q_pair, q)
+        put(u_pair, combine((0.0625, q), (-0.5625, x), unit=1.6875), right=True)
+        qu = product(q_pair, u_pair)
+        x = tuple(x_held[i] for i in range(3))
+        n = combine((1.0, qu), (-2.4375, x), unit=2.25)
+        put(n_pair, n, right=True)
+        if not last:
+            put(v_pair, product(x_pair, n_pair))
+        z = n if first else product(z_pair, n_pair)
+        if last:
+            return z
+        put(z_pair, z)
+        set_x(product(v_pair, n_pair))
+
+    set_x(tuple(value / norm for value in gram))
+    two_sweeps(first=True)
+
+    def body(index, carry):
+        two_sweeps()
         return carry
 
-    lax.fori_loop(0, (ITERS - 2) // 2, sweeps, 0)
-    first, across, second = times_middle(held(z_held), z_left, x_right[1])
+    lax.fori_loop(0, ITERS // 2 - 2, body, 0)
+    first, across, second = two_sweeps(last=True)
     z_ref = x_ref
     z_ref[:width, :width] = first
     z_ref[:width, width:] = across
@@ -453,21 +448,16 @@
     size = 2 * width
     chunk = min(rows, 512)
     body = functools.partial(finish_kernel, float(total_rows), chunk)
-    blocks = pltpu.VMEM((3, width, width), F32)
-    row_form = pltpu.VMEM((width, 3 * size), BF16)
-    col_form = pltpu.VMEM((3 * size, width), BF16)
-    all_form = pltpu.VMEM((3 * size, size), BF16)
+    pair = pltpu.VMEM((2, size, size), BF16)
     return pl.pallas_call(
         body,
-        in_specs=[SMEM] + [VMEM] * (2 * WAYS) + [ANY] * 8,
+        in_specs=[SMEM, VMEM, VMEM] + [ANY] * 8,
         out_specs=ANY,
         out_shape=jax.ShapeDtypeStruct((rows, width), BF16),
         scratch_shapes=[
-            pltpu.VMEM((2, 5 * width // 2, width // 2), F32),
             pltpu.VMEM((size, size), F32),
-            blocks, blocks, blocks,
-            row_form, col_form, row_form, col_form, row_form, col_form,
-            row_form, all_form, row_form, all_form,
+            pltpu.VMEM((3, width, width), F32),
+            pair, pair, pair, pair, pair, pair,
             pltpu.VMEM((rows, size), BF16),
             pltpu.VMEM((rows, width), BF16),
             pltpu.SemaphoreType.DMA((8,)),
@@ -480,7 +470,7 @@
             transcendentals=0,
         ),
         name="rotate",
-    )(info, *mine, *theirs, *owns, *others)
+    )(info, mine, theirs, *owns, *others)
 
 
 def after(value, *others):
@@ -530,10 +520,12 @@
         if first:
             new_low = rows("low", after(even, new_even), odd, low, high)
         new_high = rows("high", even, odd, low, high)
+        odd_halo = after(odd_halo, new_even, new_low, new_high)
         if final:
             flat = [value.reshape(-1, width) for value in (new_even, new_low, new_high)]
             others = [sibling(after(value, new_even)) for value in flat]
-        odd_halo = after(odd_halo, new_even, new_low, new_high)
+            square = gram_square(flat)
+            odd_halo = after(odd_halo, square)
         new_odd = rows("odd", odd_halo, odd, low, high, cost=LARGE if final else SMALL)
         if not final:
             odd_halo = exchange("odd", new_odd)
@@ -542,10 +534,10 @@
     last = odd.reshape(-1, width)
     other_last = sibling(last)
     others = [after(other, last) for other in others]
-    share = gram_share(info, flat, others, None)
-    parts = gram_share(info, [last], [other_last], share)
-    mine = sum_over_patch(parts)
-    theirs = [sibling(value) for value in mine]
+    cross = gram_cross(info, flat, others)
+    share = gram_share(info, last, other_last, square, cross, count)
+    mine = sum_over_patch(share)
+    theirs = sibling(mine)
     total_rows = tiles * tile * count
     return rotate(info, mine, theirs, flat + [last], others + [other_last], total_rows)
 

time: 99.9 us -> 105 us (1.051)
  blocking collectives: 0 us -> 34.4 us
  starting transfers between devices: 28.5 us -> 13.3 us
  waiting for transfers between devices: 19.7 us -> 6.37 us
  Pallas kernels: 44.4 us -> 43.3 us
    all_to_all x0 -> x2, blocking collectives: none -> 34.4 us  [the longest x1 20.3 us: sum_over_patch(): parts = lax.all_to_all(parts, 'patch', 0, 0, tiled=True)]
    ppermute x9 -> x0, starting transfers between devices: 14.1 us -> none  [exchange(): lax.ppermute(value, 'patch', [(i, i ^ distance) for i in range(count)])]
    ppermute x9 -> x0, waiting for transfers between devices: 13.8 us -> none  [exchange(): lax.ppermute(value, 'patch', [(i, i ^ distance) for i in range(count)])]
    pallas_call x5, Pallas kernels: 23.1 us -> 22 us  [the longest x1 17 us: rotate(): pl.pallas_call(body, in_specs=[SMEM, VMEM, VMEM] + [ANY] * 8, out_specs=A...]
    ppermute x8 -> x5, waiting for transfers between devices: 2.86 us -> 3.22 us  [sibling(): return lax.ppermute(value, 'cols', [(0, 1), (1, 0)])]
  transfers between devices with their start and end apart: 23 -> 11, of which waited for: 12 -> 4; matrix products, arithmetic and copies ran while one was open for 0% -> 0% of each run, Pallas kernels for 23% -> 24%
where the time goes in v5:
time: 105 us; the launch traced here: 104 us
  Pallas kernels  43.3 us (41%)
  blocking collectives  34.4 us (33%)
  starting transfers between devices  13.3 us (13%)
  waiting for transfers between devices  6.37 us (6%)
  local copies, waits for them, and re-layouts  5.83 us (6%)
    all_to_all x1, blocking collectives, sum_over_patch(): parts = lax.all_to_all(parts, 'patch', 0, 0, tiled=True)  20.3 us
    pallas_call x12, Pallas kernels, tile_rows(): pl.pallas_call(functools.partial(rows_kernel, name, counts, tiles), in_sp...  19.3 us
    pallas_call x1, Pallas kernels, rotate(): pl.pallas_call(body, in_specs=[SMEM, VMEM, VMEM] + [ANY] * 8, out_specs=A...  17 us
    all_to_all x1, blocking collectives, sum_over_patch(): lax.all_to_all(totals, 'patch', 0, 0, tiled=True).reshape(share.shape)  14.1 us
    ppermute x6, starting transfers between devices, exchange(): return lax.ppermute(value, 'patch', pairs[name])  12.2 us
    unnamed x7, local copies, waits for them, and re-layouts  5.74 us
    pallas_call x4, Pallas kernels, gram_call(): pl.pallas_call(body, in_specs=[SMEM] * len(scalars) + [VMEM] * len(args),...  5.02 us
    ppermute x5, waiting for transfers between devices, sibling(): return lax.ppermute(value, 'cols', [(0, 1), (1, 0)])  3.22 us
  transfers between devices with their start and end apart: 11, of which 4 were waited for; matrix products, arithmetic and copies ran while one was open for 0% of the time, Pallas kernels for 24%

profile of v5, /device:TPU:0, one launch (start us, length us, event | category | flops | bytes accessed | tf_op | source)
XLA Modules:
  0.0 104.4 jit_solution(244009257288140506)
XLA Ops:
  0.7 0.8 copy.5
  1.4 0.1 reshape.24.cols_ref
  1.5 0.1 pad_add_fusion.info
  1.6 0.0 copy-start.1
  1.6 1.6 %copy-done.1 = bf16[4096,256]{1,0:T(8,128)(2,1)S(1)} copy-done((bf16[4096,256]{1,0:T(8,128)(2,1)S(1)}, bf16[4096,256]{1,0:T(8,128)(2,1)}, u32[]{:S(2)}) %copy-start.1) | copy-done | bytes 2097176
  3.2 0.0 copy-start.2
  3.2 0.6 masked_edges.1
  3.8 3.0 %collective-permute-start.1 = (bf16[4,128,256]{2,1,0:T(8,128)(2,1)S(1)}, bf16[4,128,256]{2,1,0:T(8,128)(2,1)S(1)}, u32[]{:S(2)}, u32[]{:S(2)}) collective-permute-start(bf16[4,128,256]{2,1,0:T(8,128)(2,1)S(1)} %get-tuple-element.37.refs_1_.refs_0_.refs_4_), channel_id=1, source_target_pairs={{0,1},{1,0},{2,3},{3,2},{4,5},{5,4},{6,7},{7,6},{8,9},{9,8},{10,11... | collective-permute-start | bytes 786440 | tf_op jit(solution)/shard_map/ppermute | solution.py:490
  6.8 0.0 copy-done.2
  6.8 0.0 copy-start
  6.8 3.4 %copy-done = bf16[32,8,128,128]{3,2,1,0:T(8,128)(2,1)S(1)} copy-done((bf16[32,8,128,128]{3,2,1,0:T(8,128)(2,1)S(1)}, bf16[32,8,128,128]{3,2,1,0:T(8,128)(2,1)}, u32[]{:S(2)}) %copy-start) | copy-done | bytes 8388632
  10.2 1.3 %prepare.1 = (bf16[12,128,256]{2,1,0:T(8,128)(2,1)S(1)}, bf16[12,128,256]{2,1,0:T(8,128)(2,1)S(1)}, bf16[4,8,128,128]{3,2,1,0:T(8,128)(2,1)S(1)}, bf16[4,8,128,1...) custom-call(s32[3]{0:T(128)S(1)} %pad_add_fusion.info, ...), custom_call_target="tpu_custom_call" | custom-call | flops 1000 | bytes 1000 | tf_op jit(solution)/shard_map/prepare/pallas_call | solution.py:117
  11.6 0.7 collective-permute-start
  12.2 0.9 collective-permute-done.1.refs_0_
  13.1 1.1 %rows_even.3.refs_0_.refs_1_.refs_4_ = bf16[4,128,256]{2,1,0:T(8,128)(2,1)S(1)} custom-call(s32[3]{0:T(128)S(1)} %pad_add_fusion.info, s32[256]{0:T(256)S(1)} %reshape.24.cols_ref, bf16[4,128,256]{2,1,0:T(8,128)(2,1)S(1)} %collective-permute-done.1.refs_0_, bf16[4,128,256]{2,1,0:T(8,128)(2,1)S(1)} %get-tuple-element.37.refs_1_.refs_0_.refs_4_, ...), custom_call_target="tpu_custom_call" | custom-call | flops 1000 | bytes 1000 | tf_op jit(solution)/shard_map/rows_even/pallas_call | solution.py:183
  14.3 3.4 %collective-permute-start.3 = (bf16[4,128,256]{2,1,0:T(8,128)(2,1)S(1)}, bf16[4,128,256]{2,1,0:T(8,128)(2,1)S(1)}, u32[]{:S(2)}, u32[]{:S(2)}) collective-permute-start(bf16[4,128,256]{2,1,0:T(8,128)(2,1)S(1)} %rows_even.3.refs_0_.refs_1_.refs_4_), channel_id=1, source_target_pairs={{0,1},{1,0},{2,3},{3,2},{4,5},{5,4},{6,7},{7,6},{8,9},{9,8},{10,11... | collective-permute-start | bytes 786440 | tf_op jit(solution)/shard_map/ppermute | solution.py:490
  17.7 2.1 %rows_high.3.refs_3_.refs_4_ = bf16[12,128,256]{2,1,0:T(8,128)(2,1)S(1)} custom-call(s32[3]{0:T(128)S(1)} %pad_add_fusion.info, s32[256]{0:T(256)S(1)} %reshape.24.cols_ref, bf16[4,128,256]{2,1,0:T(8,128)(2,1)S(1)} %get-tuple-element.37.refs_1_.refs_0_.refs_4_, bf16[4,128,256]{2,1,0:T(8,128)(2,1)S(1)} %get-tuple-element.34.refs_1_.refs_4_, ...), custom_call_target="tpu_custom_call" | custom-call | flops 1000 | bytes 1000 | tf_op jit(solution)/shard_map/rows_high/pallas_call | solution.py:183
  19.7 2.1 %rows_low.3.refs_2_.refs_4_ = bf16[12,128,256]{2,1,0:T(8,128)(2,1)S(1)} custom-call(s32[3]{0:T(128)S(1)} %pad_add_fusion.info, s32[256]{0:T(256)S(1)} %reshape.24.cols_ref, bf16[4,128,256]{2,1,0:T(8,128)(2,1)S(1)} %get-tuple-element.37.refs_1_.refs_0_.refs_4_, bf16[4,128,256]{2,1,0:T(8,128)(2,1)S(1)} %get-tuple-element.34.refs_1_.refs_4_, ...), custom_call_target="tpu_custom_call" | custom-call | flops 1000 | bytes 1000 | tf_op jit(solution)/shard_map/rows_low/pallas_call | solution.py:183
  21.9 0.0 collective-permute-done.refs_0_
  21.9 1.1 %rows_odd.3.refs_1_.refs_4_ = bf16[4,128,256]{2,1,0:T(8,128)(2,1)S(1)} custom-call(s32[3]{0:T(128)S(1)} %pad_add_fusion.info, s32[256]{0:T(256)S(1)} %reshape.24.cols_ref, bf16[4,128,256]{2,1,0:T(8,128)(2,1)S(1)} %collective-permute-done.refs_0_, bf16[4,128,256]{2,1,0:T(8,128)(2,1)S(1)} %get-tuple-element.34.refs_1_.refs_4_, ...), custom_call_target="tpu_custom_call" | custom-call | flops 1000 | bytes 1000 | tf_op jit(solution)/shard_map/rows_odd/pallas_call | solution.py:183
  23.0 0.7 collective-permute-start.2
  23.7 2.1 %rows_low.4.refs_2_ = bf16[12,128,256]{2,1,0:T(8,128)(2,1)S(1)} custom-call(s32[3]{0:T(128)S(1)} %pad_add_fusion.info, s32[256]{0:T(256)S(1)} %reshape.24.cols_ref, bf16[4,128,256]{2,1,0:T(8,128)(2,1)S(1)} %rows_even.3.refs_0_.refs_1_.refs_4_, bf16[4,128,256]{2,1,0:T(8,128)(2,1)S(1)} %rows_odd.3.refs_1_.refs_4_, ...), custom_call_target="tpu_custom_call" | custom-call | flops 1000 | bytes 1000 | tf_op jit(solution)/shard_map/rows_low/pallas_call | solution.py:183
  25.8 2.2 %collective-permute-done.3.refs_0_ = bf16[4,128,256]{2,1,0:T(8,128)(2,1)S(1)} collective-permute-done((bf16[4,128,256]{2,1,0:T(8,128)(2,1)S(1)}, bf16[4,128,256]{2,1,0:T(8,128)(2,1)S(1)}, u32[]{:S(2)}, u32[]{:S(2)}) %collective-permute-start.3) | collective-permute-done | bytes 262176 | tf_op jit(solution)/shard_map/ppermute | solution.py:490
  28.0 1.1 %rows_even.4.refs_0_.refs_1_ = bf16[4,128,256]{2,1,0:T(8,128)(2,1)S(1)} custom-call(s32[3]{0:T(128)S(1)} %pad_add_fusion.info, s32[256]{0:T(256)S(1)} %reshape.24.cols_ref, bf16[4,128,256]{2,1,0:T(8,128)(2,1)S(1)} %collective-permute-done.3.refs_0_, bf16[4,128,256]{2,1,0:T(8,128)(2,1)S(1)} %rows_even.3.refs_0_.refs_1_.refs_4_, ...), custom_call_target="tpu_custom_call" | custom-call | flops 1000 | bytes 1000 | tf_op jit(solution)/shard_map/rows_even/pallas_call | solution.py:183
  29.1 3.8 %collective-permute-start.5 = (bf16[4,128,256]{2,1,0:T(8,128)(2,1)S(1)}, bf16[4,128,256]{2,1,0:T(8,128)(2,1)S(1)}, u32[]{:S(2)}, u32[]{:S(2)}) collective-permute-start(bf16[4,128,256]{2,1,0:T(8,128)(2,1)S(1)} %rows_even.4.refs_0_.refs_1_), channel_id=1, source_target_pairs={{0,1},{1,0},{2,3},{3,2},{4,5},{5,4},{6,7},{7,6},{8,9},{9,8},{10,11... | collective-permute-start | bytes 786440 | tf_op jit(solution)/shard_map/ppermute | solution.py:490
  32.9 2.1 %rows_high.4.refs_3_ = bf16[12,128,256]{2,1,0:T(8,128)(2,1)S(1)} custom-call(s32[3]{0:T(128)S(1)} %pad_add_fusion.info, s32[256]{0:T(256)S(1)} %reshape.24.cols_ref, bf16[4,128,256]{2,1,0:T(8,128)(2,1)S(1)} %rows_even.3.refs_0_.refs_1_.refs_4_, bf16[4,128,256]{2,1,0:T(8,128)(2,1)S(1)} %rows_odd.3.refs_1_.refs_4_, ...), custom_call_target="tpu_custom_call" | custom-call | flops 1000 | bytes 1000 | tf_op jit(solution)/shard_map/rows_high/pallas_call | solution.py:183
  35.0 0.0 collective-permute-done.2.refs_0_
  35.1 1.1 %rows_odd.4.refs_1_ = bf16[4,128,256]{2,1,0:T(8,128)(2,1)S(1)} custom-call(s32[3]{0:T(128)S(1)} %pad_add_fusion.info, s32[256]{0:T(256)S(1)} %reshape.24.cols_ref, bf16[4,128,256]{2,1,0:T(8,128)(2,1)S(1)} %collective-permute-done.2.refs_0_, bf16[4,128,256]{2,1,0:T(8,128)(2,1)S(1)} %rows_odd.3.refs_1_.refs_4_, ...), custom_call_target="tpu_custom_call" | custom-call | flops 1000 | bytes 1000 | tf_op jit(solution)/shard_map/rows_odd/pallas_call | solution.py:183
  36.2 0.7 collective-permute-start.4
  36.9 2.1 %rows_high.5 = bf16[12,128,256]{2,1,0:T(8,128)(2,1)S(1)} custom-call(s32[3]{0:T(128)S(1)} %pad_add_fusion.info, s32[256]{0:T(256)S(1)} %reshape.24.cols_ref, bf16[4,128,256]{2,1,0:T(8,128)(2,1)S(1)} %rows_even.4.refs_0_.refs_1_, bf16[4,128,256]{2,1,0:T(8,128)(2,1)S(1)} %rows_odd.4.refs_1_, bf16[12,128,256]{2,1,0:T(8,128)(2,1)S(1)} %rows_low.4.refs_2_, ...), custom_call_target="tpu_custom_call" | custom-call | flops 1000 | bytes 1000 | tf_op jit(solution)/shard_map/rows_high/pallas_call | solution.py:183
  39.0 2.1 %rows_low.5 = bf16[12,128,256]{2,1,0:T(8,128)(2,1)S(1)} custom-call(s32[3]{0:T(128)S(1)} %pad_add_fusion.info, s32[256]{0:T(256)S(1)} %reshape.24.cols_ref, bf16[4,128,256]{2,1,0:T(8,128)(2,1)S(1)} %rows_even.4.refs_0_.refs_1_, bf16[4,128,256]{2,1,0:T(8,128)(2,1)S(1)} %rows_odd.4.refs_1_, bf16[12,128,256]{2,1,0:T(8,128)(2,1)S(1)} %rows_low.4.refs_2_, ...), custom_call_target="tpu_custom_call" | custom-call | flops 1000 | bytes 1000 | tf_op jit(solution)/shard_map/rows_low/pallas_call | solution.py:183
  41.2 0.0 collective-permute-done.5.refs_0_
  41.2 1.1 %rows_even.5 = bf16[4,128,256]{2,1,0:T(8,128)(2,1)S(1)} custom-call(s32[3]{0:T(128)S(1)} %pad_add_fusion.info, s32[256]{0:T(256)S(1)} %reshape.24.cols_ref, bf16[4,128,256]{2,1,0:T(8,128)(2,1)S(1)} %collective-permute-done.5.refs_0_, bf16[4,128,256]{2,1,0:T(8,128)(2,1)S(1)} %rows_even.4.refs_0_.refs_1_, bf16[12,128,256]{2,1,0:T(8,128)(2,1)S(1)} %rows_low.4.refs_2_, ...), custom_call_target="tpu_custom_call" | custom-call | flops 1000 | bytes 1000 | tf_op jit(solution)/shard_map/rows_even/pallas_call | solution.py:183
  42.3 1.9 %gram_square.1.square_ref = f32[256,256]{1,0:T(8,128)S(1)} custom-call(bf16[512,256]{1,0:T(8,128)(2,1)S(1)} %bitcast.19, bf16[1536,256]{1,0:T(8,128)(2,1)S(1)} %bitcast.15, bf16[1536,256]{1,0:T(8,128)(2,1)S(1)} %bitcast.11), custom_call_target="tpu_custom_call" | custom-call | flops 1000 | bytes 1000 | tf_op jit(solution)/shard_map/gram_square/pallas_call | solution.py:253
  44.2 0.1 collective-permute-start.9
  44.3 0.0 collective-permute-done.4.refs_0_
  44.3 0.5 collective-permute-start.8
  44.8 0.1 collective-permute-start.7
  44.9 1.1 %rows_odd.5 = bf16[4,128,256]{2,1,0:T(8,128)(2,1)S(1)} custom-call(s32[3]{0:T(128)S(1)} %pad_add_fusion.info, s32[256]{0:T(256)S(1)} %reshape.24.cols_ref, bf16[4,128,256]{2,1,0:T(8,128)(2,1)S(1)} %collective-permute-done.4.refs_0_, bf16[4,128,256]{2,1,0:T(8,128)(2,1)S(1)} %rows_odd.4.refs_1_, bf16[12,128,256]{2,1,0:T(8,128)(2,1)S(1)} %rows_low.4.refs_2_, ...), custom_call_target="tpu_custom_call" | custom-call | flops 99999997952 | bytes 1000 | tf_op jit(solution)/shard_map/rows_odd/pallas_call | solution.py:183
  46.0 0.5 collective-permute-start.6
  46.5 1.6 %collective-permute-done.7.refs_3_.refs_4_ = bf16[512,256]{1,0:T(8,128)(2,1)S(1)} collective-permute-done((bf16[512,256]{1,0:T(8,128)(2,1)S(1)}, bf16[512,256]{1,0:T(8,128)(2,1)S(1)}, u32[]{:S(2)}, u32[]{:S(2)}) %collective-permute-start.7) | collective-permute-done | bytes 262176 | tf_op jit(solution)/shard_map/ppermute | solution.py:493
  48.1 0.0 collective-permute-done.9.refs_5_.refs_6_
  48.1 0.0 collective-permute-done.8.refs_4_.refs_5_
  48.1 2.2 %gram_cross.1.cross_ref = f32[128,256]{1,0:T(8,128)S(1)} custom-call(s32[3]{0:T(128)S(1)} %pad_add_fusion.info, bf16[512,256]{1,0:T(8,128)(2,1)S(1)} %bitcast.21, bf16[1536,256]{1,0:T(8,128)(2,1)S(1)} %bitcast.17, bf16[1536,256]{1,0:T(8,128)(2,1)S(1)} %bitcast.13, bf16[512,256]{1,0:T(8,128)(2,1)S(1)} %collective-permute-done.7.refs_3_.refs_4_, ...), custom_call_target="tpu_custom_call" | custom-call | flops 1000 | bytes 1000 | tf_op jit(solution)/shard_map/gram_cross/pallas_call | solution.py:253
  50.3 0.0 collective-permute-done.6.other_ref.refs_7_
  50.3 0.8 gram_share.1
  51.2 20.3 %all_to_all.10.parts_ref = f32[16,40,128]{2,1,0:T(8,128)S(1)} all-to-all(f32[16,40,128]{2,1,0:T(8,128)S(1)} %bitcast.23), channel_id=1, replica_groups=mesh['cols'=2,'patch'=16] {'patch'}, dimensions={0} | all-to-all | bytes 655360 | tf_op jit(solution)/shard_map/all_to_all | solution.py:301
  71.5 14.1 %all_to_all.11 = f32[16,40,128]{2,1,0:T(8,128)S(1)} all-to-all(f32[16,40,128]{2,1,0:T(8,128)S(1)} %sum_parts.1), channel_id=1, replica_groups=mesh['cols'=2,'patch'=16] {'patch'}, dimensions={0} | all-to-all | bytes 655360 | tf_op jit(solution)/shard_map/all_to_all | solution.py:303
  85.6 0.0 collective-permute-start.10
  85.6 1.6 %collective-permute-done.10.theirs = f32[640,128]{1,0:T(8,128)S(1)} collective-permute-done((f32[640,128]{1,0:T(8,128)S(1)}, f32[640,128]{1,0:T(8,128)S(1)}, u32[]{:S(2)}, u32[]{:S(2)}) %collective-permute-start.10) | collective-permute-done | bytes 327712 | tf_op jit(solution)/shard_map/ppermute | solution.py:493
  87.3 17.0 %rotate.1 = bf16[4096,256]{1,0:T(8,128)(2,1)} custom-call(s32[3]{0:T(128)S(1)} %pad_add_fusion.info, f32[640,128]{1,0:T(8,128)S(1)} %bitcast.25, f32[640,128]{1,0:T(8,128)S(1)} %collective-permute-done.10.theirs, bf16[512,256]{1,0:T(8,128)(2,1)S(1)} %bitcast.22, bf16[1536,256]{1,0:T(8,128)(2,1)S(1)} %bitcast.18, bf16[1536,256]{1,0:T(8,128)(2,1)S(1)} %bitcast.14, ...), custom_call_target="tpu_custom_call" | custom-call | flops 17985175552 | bytes 6291456 | tf_op jit(solution)/shard_map/rotate/pallas_call | solution.py:452
  (1 shorter events, 0.0 us)
Async XLA Ops:
  1.6 1.6 %copy-start.1 = (bf16[4096,256]{1,0:T(8,128)(2,1)S(1)}, bf16[4096,256]{1,0:T(8,128)(2,1)}, u32[]{:S(2)}) copy-start(bf16[4096,256]{1,0:T(8,128)(2,1)} %param.4) | copy-start | bytes 6291460
  3.2 3.7 %copy-start.2 = (bf16[4096,256]{1,0:T(8,128)(2,1)S(1)}, bf16[4096,256]{1,0:T(8,128)(2,1)}, u32[]{:S(2)}) copy-start(bf16[4096,256]{1,0:T(8,128)(2,1)} %param.4) | copy-start | bytes 6291460
  3.8 9.3 %collective-permute-start.1 = (bf16[4,128,256]{2,1,0:T(8,128)(2,1)S(1)}, bf16[4,128,256]{2,1,0:T(8,128)(2,1)S(1)}, u32[]{:S(2)}, u32[]{:S(2)}) collective-permute-start(bf16[4,128,256]{2,1,0:T(8,128)(2,1)S(1)} %get-tuple-element.37.refs_1_.refs_0_.refs_4_), channel_id=1, source_target_pairs={{0,1},{1,0},{2,3},{3,2},{4,5},{5,4},{6,7},{7,6},{8,9},{9,8},{10,11... | collective-permute-start | bytes 786440 | tf_op jit(solution)/shard_map/ppermute | solution.py:490
  6.8 3.4 %copy-start = (bf16[32,8,128,128]{3,2,1,0:T(8,128)(2,1)S(1)}, bf16[32,8,128,128]{3,2,1,0:T(8,128)(2,1)}, u32[]{:S(2)}) copy-start(bf16[32,8,128,128]{3,2,1,0:T(8,128)(2,1)} %blocks_ref.1) | copy-start | bytes 25165828
  11.6 10.3 %collective-permute-start = (bf16[4,128,256]{2,1,0:T(8,128)(2,1)S(1)}, bf16[4,128,256]{2,1,0:T(8,128)(2,1)S(1)}, u32[]{:S(2)}, u32[]{:S(2)}) collective-permute-start(bf16[4,128,256]{2,1,0:T(8,128)(2,1)S(1)} %get-tuple-element.34.refs_1_.refs_4_), channel_id=1, source_target_pairs={{1,2},{2,1},{3,4},{4,3},{5,6},{6,5},{7,8},{8,7},{9,10},{10,9},{11,... | collective-permute-start | bytes 786440 | tf_op jit(solution)/shard_map/ppermute | solution.py:490
  14.3 13.8 %collective-permute-start.3 = (bf16[4,128,256]{2,1,0:T(8,128)(2,1)S(1)}, bf16[4,128,256]{2,1,0:T(8,128)(2,1)S(1)}, u32[]{:S(2)}, u32[]{:S(2)}) collective-permute-start(bf16[4,128,256]{2,1,0:T(8,128)(2,1)S(1)} %rows_even.3.refs_0_.refs_1_.refs_4_), channel_id=1, source_target_pairs={{0,1},{1,0},{2,3},{3,2},{4,5},{5,4},{6,7},{7,6},{8,9},{9,8},{10,11... | collective-permute-start | bytes 786440 | tf_op jit(solution)/shard_map/ppermute | solution.py:490
  23.0 12.1 %collective-permute-start.2 = (bf16[4,128,256]{2,1,0:T(8,128)(2,1)S(1)}, bf16[4,128,256]{2,1,0:T(8,128)(2,1)S(1)}, u32[]{:S(2)}, u32[]{:S(2)}) collective-permute-start(bf16[4,128,256]{2,1,0:T(8,128)(2,1)S(1)} %rows_odd.3.refs_1_.refs_4_), channel_id=1, source_target_pairs={{1,2},{2,1},{3,4},{4,3},{5,6},{6,5},{7,8},{8,7},{9,10},{10,9},{11,... | collective-permute-start | bytes 786440 | tf_op jit(solution)/shard_map/ppermute | solution.py:490
  29.1 12.0 %collective-permute-start.5 = (bf16[4,128,256]{2,1,0:T(8,128)(2,1)S(1)}, bf16[4,128,256]{2,1,0:T(8,128)(2,1)S(1)}, u32[]{:S(2)}, u32[]{:S(2)}) collective-permute-start(bf16[4,128,256]{2,1,0:T(8,128)(2,1)S(1)} %rows_even.4.refs_0_.refs_1_), channel_id=1, source_target_pairs={{0,1},{1,0},{2,3},{3,2},{4,5},{5,4},{6,7},{7,6},{8,9},{9,8},{10,11... | collective-permute-start | bytes 786440 | tf_op jit(solution)/shard_map/ppermute | solution.py:490
  36.2 8.1 %collective-permute-start.4 = (bf16[4,128,256]{2,1,0:T(8,128)(2,1)S(1)}, bf16[4,128,256]{2,1,0:T(8,128)(2,1)S(1)}, u32[]{:S(2)}, u32[]{:S(2)}) collective-permute-start(bf16[4,128,256]{2,1,0:T(8,128)(2,1)S(1)} %rows_odd.4.refs_1_), channel_id=1, source_target_pairs={{1,2},{2,1},{3,4},{4,3},{5,6},{6,5},{7,8},{8,7},{9,10},{10,9},{11,... | collective-permute-start | bytes 786440 | tf_op jit(solution)/shard_map/ppermute | solution.py:490
  44.2 3.9 %collective-permute-start.9 = (bf16[1536,256]{1,0:T(8,128)(2,1)S(1)}, bf16[1536,256]{1,0:T(8,128)(2,1)S(1)}, u32[]{:S(2)}, u32[]{:S(2)}) collective-permute-start(bf16[1536,256]{1,0:T(8,128)(2,1)S(1)} %bitcast.12), channel_id=1, source_target_pairs={{0,16},{16,0},{1,17},{17,1},{2,18},{18,2},{3,19},{19,3},{4,20},{20... | collective-permute-start | bytes 2359304 | tf_op jit(solution)/shard_map/ppermute | solution.py:493
  44.3 3.8 %collective-permute-start.8 = (bf16[1536,256]{1,0:T(8,128)(2,1)S(1)}, bf16[1536,256]{1,0:T(8,128)(2,1)S(1)}, u32[]{:S(2)}, u32[]{:S(2)}) collective-permute-start(bf16[1536,256]{1,0:T(8,128)(2,1)S(1)} %bitcast.16), channel_id=1, source_target_pairs={{0,16},{16,0},{1,17},{17,1},{2,18},{18,2},{3,19},{19,3},{4,20},{20... | collective-permute-start | bytes 2359304 | tf_op jit(solution)/shard_map/ppermute | solution.py:493
  44.8 3.3 %collective-permute-start.7 = (bf16[512,256]{1,0:T(8,128)(2,1)S(1)}, bf16[512,256]{1,0:T(8,128)(2,1)S(1)}, u32[]{:S(2)}, u32[]{:S(2)}) collective-permute-start(bf16[512,256]{1,0:T(8,128)(2,1)S(1)} %bitcast.20), channel_id=1, source_target_pairs={{0,16},{16,0},{1,17},{17,1},{2,18},{18,2},{3,19},{19,3},{4,20},{20... | collective-permute-start | bytes 786440 | tf_op jit(solution)/shard_map/ppermute | solution.py:493
  46.0 4.3 %collective-permute-start.6 = (bf16[512,256]{1,0:T(8,128)(2,1)S(1)}, bf16[512,256]{1,0:T(8,128)(2,1)S(1)}, u32[]{:S(2)}, u32[]{:S(2)}) collective-permute-start(bf16[512,256]{1,0:T(8,128)(2,1)S(1)} %bitcast.26), channel_id=1, source_target_pairs={{0,16},{16,0},{1,17},{17,1},{2,18},{18,2},{3,19},{19,3},{4,20},{20... | collective-permute-start | bytes 786440 | tf_op jit(solution)/shard_map/ppermute | solution.py:493
  85.6 1.6 %collective-permute-start.10 = (f32[640,128]{1,0:T(8,128)S(1)}, f32[640,128]{1,0:T(8,128)S(1)}, u32[]{:S(2)}, u32[]{:S(2)}) collective-permute-start(f32[640,128]{1,0:T(8,128)S(1)} %bitcast.24), channel_id=1, source_target_pairs={{0,16},{16,0},{1,17},{17,1},{2,18},{18,2},{3,19},{19,3},{4,20},{20... | collective-permute-start | bytes 983048 | tf_op jit(solution)/shard_map/ppermute | solution.py:493

commit v6 on v5

--- a/solution.py
+++ b/solution.py
@@ -10,6 +10,7 @@
 HALO_T = 4
 STEPS = 3
 ITERS = 8
+WAYS = 4
 GROUP = 4
 
 SMALL = pl.CostEstimate(flops=1000, bytes_accessed=1000, transcendentals=0)
@@ -19,6 +20,7 @@
 ANY = pl.BlockSpec(memory_space=pl.ANY)
 HBM = pl.BlockSpec(memory_space=pltpu.HBM)
 VMEM = pl.BlockSpec(memory_space=pltpu.VMEM)
+EDGES_MB, FIELDS_MB, BLOCKS_MB = 53, 50, 44
 SMEM = pl.BlockSpec(memory_space=pltpu.SMEM)
 F32, BF16 = jnp.float32, jnp.bfloat16
 
@@ -68,17 +70,7 @@
     lax.fori_loop(jnp.clip(live - first, 0, count), count, clear, 0)
 
 
-def prepare_kernel(info, whole_ref, blocks_ref, *refs):
-    low_ref, high_ref, even_blocks, odd_blocks, low_blocks, high_blocks, sem = refs
-    edge, tiles = HALO_T, whole_ref.shape[0]
-    half = tiles // 2 - edge
-    moves = [
-        (whole_ref, edge, low_ref), (whole_ref, edge + half, high_ref),
-        (blocks_ref, edge, low_blocks),
-        (blocks_ref, at_end("even", info) * (tiles - edge), even_blocks),
-        (blocks_ref, edge + half, high_blocks),
-        (blocks_ref, at_end("odd", info) * (tiles - edge), odd_blocks),
-    ]
+def load(moves, sem):
     copies = [
         pltpu.make_async_copy(source.at[pl.ds(first, target.shape[0])], target, sem.at[i])
         for i, (source, first, target) in enumerate(moves)
@@ -87,9 +79,25 @@
         copy.start()
     for copy in copies:
         copy.wait()
+
+
+def fields_kernel(info, whole_ref, blocks_ref, low_ref, high_ref, even_blocks, odd_blocks, sem):
+    edge, tiles = HALO_T, whole_ref.shape[0]
+    half = tiles // 2 - edge
+    moves = [
+        (blocks_ref, at_end("even", info) * (tiles - edge), even_blocks),
+        (blocks_ref, at_end("odd", info) * (tiles - edge), odd_blocks),
+        (whole_ref, edge, low_ref), (whole_ref, edge + half, high_ref),
+    ]
+    load(moves, sem)
     live = info[LIVE]
     clear_dead(low_ref, edge, live)
     clear_dead(high_ref, edge + half, live)
+
+
+def blocks_kernel(info, blocks_ref, low_blocks, high_blocks, sem):
+    half = low_blocks.shape[0]
+    load([(blocks_ref, HALO_T, low_blocks), (blocks_ref, HALO_T + half, high_blocks)], sem)
 
 
 def masked_edges(info, start):
@@ -100,30 +108,36 @@
         out_specs=[VMEM] * 2,
         out_shape=[jax.ShapeDtypeStruct((HALO_T, tile, width), BF16)] * 2,
         scratch_shapes=[pltpu.SemaphoreType.DMA((2,))],
-        compiler_params=pltpu.CompilerParams(vmem_limit_bytes=4 * 1024 * 1024),
+        compiler_params=pltpu.CompilerParams(vmem_limit_bytes=EDGES_MB * 1024 * 1024),
         cost_estimate=SMALL,
         name="masked_edges",
     )(info, start)
 
 
-def prepare(info, start, blocks):
+def load_call(body, name, info, args, shapes, megabytes):
+    return pl.pallas_call(
+        body,
+        in_specs=[SMEM] + [HBM] * len(args),
+        out_specs=[VMEM] * len(shapes),
+        out_shape=shapes,
+        scratch_shapes=[pltpu.SemaphoreType.DMA((len(shapes),))],
+        compiler_params=pltpu.CompilerParams(vmem_limit_bytes=megabytes * 1024 * 1024),
+        cost_estimate=SMALL,
+        name=name,
+    )(info, *args)
+
+
+def load_fields(info, start, blocks):
     tiles, tile, width = start.shape
-    half = tiles // 2 - HALO_T
-    block_counts = (HALO_T, HALO_T, half, half)
-    shapes = [jax.ShapeDtypeStruct((half, tile, width), BF16)] * 2
-    shapes += [
-        jax.ShapeDtypeStruct((count,) + blocks.shape[1:], blocks.dtype) for count in block_counts
-    ]
-    return pl.pallas_call(
-        prepare_kernel,
-        in_specs=[SMEM, HBM, HBM],
-        out_specs=[VMEM] * 6,
-        out_shape=shapes,
-        scratch_shapes=[pltpu.SemaphoreType.DMA((6,))],
-        compiler_params=pltpu.CompilerParams(vmem_limit_bytes=16 * 1024 * 1024),
-        cost_estimate=SMALL,
-        name="prepare",
-    )(info, start, blocks)
+    shapes = [jax.ShapeDtypeStruct((tiles // 2 - HALO_T, tile, width), BF16)] * 2
+    shapes += [jax.ShapeDtypeStruct((HALO_T,) + blocks.shape[1:], blocks.dtype)] * 2
+    return load_call(fields_kernel, "load_fields", info, [start, blocks], shapes, FIELDS_MB)
+
+
+def load_blocks(info, blocks):
+    half = blocks.shape[0] // 2 - HALO_T
+    shapes = [jax.ShapeDtypeStruct((half,) + blocks.shape[1:], blocks.dtype)] * 2
+    return load_call(blocks_kernel, "load_blocks", info, [blocks], shapes, BLOCKS_MB)
 
 
 def layout(name, info, tiles):
@@ -232,7 +246,8 @@
         add_cross(chunk, info, own_ref, other_ref, refs[-1])
 
 
-def share_kernel(chunk, info, own_ref, other_ref, square_ref, cross_ref, out_ref, square, cross):
+def share_kernel(chunk, info, own_ref, other_ref, square_ref, cross_ref, *refs):
+    outs, (square, cross, share) = refs[:WAYS], refs[WAYS:]
     square[...] = square_ref[...]
     cross[...] = cross_ref[...]
     add_square(chunk, own_ref, square)
@@ -243,18 +258,20 @@
         cross[:, :half], cross[:, half:],
     ]
     for i, block in enumerate(blocks):
-        out_ref[pl.ds(i * half, half), :] = block
-    used = len(blocks) * half
-    if used < out_ref.shape[0]:
-        out_ref[used:, :] = jnp.zeros((out_ref.shape[0] - used, half), F32)
-
-
-def gram_call(body, name, args, shape, scratch=(), scalars=()):
+        share[pl.ds(i * half, half), :] = block
+    quarter = info[PATCH] % WAYS
+    for d, out in enumerate(outs):
+        rows = out.shape[0]
+        out[...] = share[pl.ds(pl.multiple_of((quarter ^ d) * rows, 8), rows), :]
+
+
+def gram_call(body, name, args, shape, scratch=(), scalars=(), outs=0):
+    out_shape = jax.ShapeDtypeStruct(shape, F32)
     return pl.pallas_call(
         body,
         in_specs=[SMEM] * len(scalars) + [VMEM] * len(args),
-        out_specs=VMEM,
-        out_shape=jax.ShapeDtypeStruct(shape, F32),
+        out_specs=[VMEM] * outs if outs else VMEM,
+        out_shape=[out_shape] * outs if outs else out_shape,
         scratch_shapes=scratch,
         compiler_params=SMALL_VMEM,
         cost_estimate=SMALL,
@@ -275,32 +292,51 @@
     return gram_call(body, "gram_cross", owns + others, shape, scalars=[info])
 
 
-def gram_share(info, own, other, square, cross, count):
+def gram_share(info, own, other, square, cross):
     width = own.shape[1]
     half = width // 2
-    rows = -(-5 * half // (8 * count)) * 8 * count
     body = functools.partial(share_kernel, own.shape[0])
-    scratch = [pltpu.VMEM((width, width), F32), pltpu.VMEM((half, width), F32)]
+    scratch = [
+        pltpu.VMEM((width, width), F32), pltpu.VMEM((half, width), F32),
+        pltpu.VMEM((5 * half, half), F32),
+    ]
     args = [own, other, square, cross]
-    return gram_call(body, "gram_share", args, (rows, half), scratch, [info])
-
-
-def sum_kernel(parts_ref, out_ref):
-    count = parts_ref.shape[0]
-    values = [parts_ref[i] for i in range(count)]
-    while len(values) > 1:
-        pairs = zip(values[::2], values[1::2])
-        values = [one + two for one, two in pairs] + values[len(values) // 2 * 2 :]
-    for i in range(count):
-        out_ref[i] = values[0]
-
-
-def sum_over_patch(share):
+    shape = (5 * half // WAYS, half)
+    return gram_call(body, "gram_share", args, shape, scratch, [info], outs=WAYS)
+
+
+def add_kernel(a, b, c, d, out):
+    out[...] = (a[...] + b[...]) + (c[...] + d[...])
+
+
+def join_kernel(info, *refs):
+    parts, out = refs[:-1], refs[-1]
+    rows = parts[0].shape[0]
+    quarter = info[PATCH] % WAYS
+    for d, part in enumerate(parts):
+        out[pl.ds(pl.multiple_of((quarter ^ d) * rows, 8), rows), :] = part[...]
+
+
+def sum_over_patch(info, parts):
     count = lax.axis_size("patch")
-    parts = share.reshape(count, -1, share.shape[1])
-    parts = lax.all_to_all(parts, "patch", 0, 0, tiled=True)
-    totals = gram_call(sum_kernel, "sum_parts", [parts], parts.shape)
-    return lax.all_to_all(totals, "patch", 0, 0, tiled=True).reshape(share.shape)
+    rows, columns = parts[0].shape
+
+    def add_four(values):
+        return gram_call(add_kernel, "add_four", values, (rows, columns))
+
+    def from_others(values, stride=1):
+        return [
+            lax.ppermute(values[d], "patch", [(i, i ^ (d * stride)) for i in range(count)])
+            for d in range(1, WAYS)
+        ]
+
+    total = add_four([parts[0]] + from_others(parts))
+    stride = WAYS
+    while stride < count:
+        total = add_four([total] + from_others([total] * WAYS, stride))
+        stride *= WAYS
+    quarters = [total] + from_others([total] * WAYS)
+    return gram_call(join_kernel, "join", quarters, (WAYS * rows, columns), scalars=[info])
 
 
 def split(value):
@@ -500,30 +536,26 @@
 
     even, odd = masked_edges(after(info, cols), start)
     even_halo = exchange("even", even)
-    ready = prepare(after(info, even), start, blocks)
-    low, high = ready[:2]
-    stored = dict(zip(("even", "odd", "low", "high"), ready[2:]))
+    low, high, even_blocks, odd_blocks = load_fields(after(info, even), start, blocks)
     odd_halo = exchange("odd", after(odd, low))
+    low_blocks, high_blocks = load_blocks(after(info, low), blocks)
+    stored = {"even": even_blocks, "odd": odd_blocks, "low": low_blocks, "high": high_blocks}
     prev = dict.fromkeys(stored)
 
     def rows(name, *pieces, cost=SMALL):
         return tile_rows(name, info, cols, stored[name], pieces, prev[name], cost)
 
     for step in range(STEPS):
-        first, final = step == 0, step == STEPS - 1
-        if not first:
-            new_low = rows("low", even, odd, low, high)
-            even_halo = after(even_halo, new_low)
-        new_even = rows("even", even_halo, even, low, high)
+        final = step == STEPS - 1
+        new_even = rows("even", after(even_halo, low_blocks), even, low, high)
         if not final:
             even_halo = exchange("even", new_even)
-        if first:
-            new_low = rows("low", after(even, new_even), odd, low, high)
-        new_high = rows("high", even, odd, low, high)
-        odd_halo = after(odd_halo, new_even, new_low, new_high)
+        held = after(even, new_even)
+        new_low, new_high = rows("low", held, odd, low, high), rows("high", held, odd, low, high)
+        odd_halo = after(odd_halo, new_low, new_high)
         if final:
             flat = [value.reshape(-1, width) for value in (new_even, new_low, new_high)]
-            others = [sibling(after(value, new_even)) for value in flat]
+            others = [sibling(value) for value in flat]
             square = gram_square(flat)
             odd_halo = after(odd_halo, square)
         new_odd = rows("odd", odd_halo, odd, low, high, cost=LARGE if final else SMALL)
@@ -535,8 +567,7 @@
     other_last = sibling(last)
     others = [after(other, last) for other in others]
     cross = gram_cross(info, flat, others)
-    share = gram_share(info, last, other_last, square, cross, count)
-    mine = sum_over_patch(share)
+    mine = sum_over_patch(info, gram_share(info, last, other_last, square, cross))
     theirs = sibling(mine)
     total_rows = tiles * tile * count
     return rotate(info, mine, theirs, flat + [last], others + [other_last], total_rows)

time: 105 us -> 99.8 us (0.950)
  blocking collectives: 34.4 us -> 0 us
  waiting for transfers between devices: 6.37 us -> 20.5 us
  starting transfers between devices: 13.3 us -> 27.2 us
  Pallas kernels: 43.3 us -> 49.9 us
  local copies, waits for them, and re-layouts: 5.83 us -> 0.85 us
    all_to_all x2 -> x0, blocking collectives: 34.4 us -> none  [the longest x1 20.3 us: sum_over_patch(): parts = lax.all_to_all(parts, 'patch', 0, 0, tiled=True)]
    ppermute x0 -> x9, waiting for transfers between devices: none -> 14.1 us  [from_others(): lax.ppermute(values[d], 'patch', [(i, i ^ d * stride) for i in range(coun...]
    ppermute x0 -> x9, starting transfers between devices: none -> 13.1 us  [from_others(): lax.ppermute(values[d], 'patch', [(i, i ^ d * stride) for i in range(coun...]
    unnamed x7 -> x1, local copies, waits for them, and re-layouts: 5.74 us -> 0.76 us
    pallas_call x1 -> x2, Pallas kernels: 1.32 us -> 6.11 us  [load_call(): pl.pallas_call(body, in_specs=[SMEM] + [HBM] * len(args), out_specs=[VMEM...]
    ppermute x6, waiting for transfers between devices: 3.15 us -> 4.21 us  [exchange(): return lax.ppermute(value, 'patch', pairs[name])]
    pallas_call x4 -> x6, Pallas kernels: 5.02 us -> 5.62 us  [gram_call(): pl.pallas_call(body, in_specs=[SMEM] * len(scalars) + [VMEM] * len(args),...]
  transfers between devices with their start and end apart: 11 -> 20, of which waited for: 4 -> 11; matrix products, arithmetic and copies ran while one was open for 0% -> 0% of each run, Pallas kernels for 24% -> 30%
where the time goes in v6:
time: 99.8 us; the launch traced here: 99.7 us
  Pallas kernels  49.9 us (50%)
  starting transfers between devices  27.2 us (27%)
  waiting for transfers between devices  20.5 us (21%)
  between operations  1.08 us (1%)
    pallas_call x12, Pallas kernels, tile_rows(): pl.pallas_call(functools.partial(rows_kernel, name, counts, tiles), in_sp...  19.4 us
    pallas_call x1, Pallas kernels, rotate(): pl.pallas_call(body, in_specs=[SMEM, VMEM, VMEM] + [ANY] * 8, out_specs=A...  17.2 us
    ppermute x9, waiting for transfers between devices, from_others(): lax.ppermute(values[d], 'patch', [(i, i ^ d * stride) for i in range(coun...  14.1 us
    ppermute x9, starting transfers between devices, from_others(): lax.ppermute(values[d], 'patch', [(i, i ^ d * stride) for i in range(coun...  13.1 us
    ppermute x6, starting transfers between devices, exchange(): return lax.ppermute(value, 'patch', pairs[name])  12.9 us
    pallas_call x2, Pallas kernels, load_call(): pl.pallas_call(body, in_specs=[SMEM] + [HBM] * len(args), out_specs=[VMEM...  6.11 us
    pallas_call x6, Pallas kernels, gram_call(): pl.pallas_call(body, in_specs=[SMEM] * len(scalars) + [VMEM] * len(args),...  5.62 us
    ppermute x6, waiting for transfers between devices, exchange(): return lax.ppermute(value, 'patch', pairs[name])  4.21 us
  transfers between devices with their start and end apart: 20, of which 11 were waited for; matrix products, arithmetic and copies ran while one was open for 0% of the time, Pallas kernels for 30%

profile of v6, /device:TPU:0, one launch (start us, length us, event | category | flops | bytes accessed | tf_op | source)
XLA Modules:
  0.0 99.7 jit_solution(12272678846903054156)
XLA Ops:
  0.7 0.8 copy.5
  1.4 0.1 reshape.18.cols_ref
  1.5 0.1 pad_add_fusion.info
  1.6 1.6 %masked_edges.1 = (bf16[4,128,256]{2,1,0:T(8,128)(2,1)S(1)}, bf16[4,128,256]{2,1,0:T(8,128)(2,1)S(1)}) custom-call(s32[3]{0:T(128)S(1)} %pad_add_fusion.info, bf16[32,128,256]{2,1,0:T(8,128)(2,1)} %bitcast.22), custom_call_target="tpu_custom_call" | custom-call | flops 1000 | bytes 1000 | tf_op jit(solution)/shard_map/masked_edges/pallas_call | solution.py:105
  3.2 3.0 %collective-permute-start.1 = (bf16[4,128,256]{2,1,0:T(8,128)(2,1)S(1)}, bf16[4,128,256]{2,1,0:T(8,128)(2,1)S(1)}, u32[]{:S(2)}, u32[]{:S(2)}) collective-permute-start(bf16[4,128,256]{2,1,0:T(8,128)(2,1)S(1)} %get-tuple-element.45.refs_1_.refs_0_.refs_4_), channel_id=1, source_target_pairs={{0,1},{1,0},{2,3},{3,2},{4,5},{5,4},{6,7},{7,6},{8,9},{9,8},{10,11... | collective-permute-start | bytes 786440 | tf_op jit(solution)/shard_map/ppermute | solution.py:526
  6.2 2.7 %load_fields.1 = (bf16[12,128,256]{2,1,0:T(8,128)(2,1)S(1)}, bf16[12,128,256]{2,1,0:T(8,128)(2,1)S(1)}, bf16[4,8,128,128]{3,2,1,0:T(8,128)(2,1)S(1)}, bf16[4,8,128,128]{3,2,1,0:T(8,128)(2,1)S(1)}) custom-call(s32[3]{0:T(128)S(1)} %pad_add_fusion.info, bf16[32,128,256]{2,1,0:T(8,128)(2,1)} %bitcast.23, bf16[32,8,128,128]{3,2,1,0:T(8,128)(2,1)} %blocks_ref.3), custom_call_target="tpu_custom_call" | custom-call | flops 1000 | bytes 1000 | tf_op jit(solution)/shard_map/load_fields/pallas_call | solution.py:118
  8.9 0.7 collective-permute-start
  9.6 3.4 %load_blocks.1 = (bf16[12,8,128,128]{3,2,1,0:T(8,128)(2,1)S(1)}, bf16[12,8,128,128]{3,2,1,0:T(8,128)(2,1)S(1)}) custom-call(s32[3]{0:T(128)S(1)} %pad_add_fusion.info, bf16[32,8,128,128]{3,2,1,0:T(8,128)(2,1)} %blocks_ref.3), custom_call_target="tpu_custom_call" | custom-call | flops 1000 | bytes 1000 | tf_op jit(solution)/shard_map/load_blocks/pallas_call | solution.py:118
  13.0 0.0 collective-permute-done.1.refs_0_
  13.0 1.1 %rows_even.3.refs_1_.refs_0_.refs_4_ = bf16[4,128,256]{2,1,0:T(8,128)(2,1)S(1)} custom-call(s32[3]{0:T(128)S(1)} %pad_add_fusion.info, s32[256]{0:T(256)S(1)} %reshape.18.cols_ref, bf16[4,128,256]{2,1,0:T(8,128)(2,1)S(1)} %collective-permute-done.1.refs_0_, bf16[4,128,256]{2,1,0:T(8,128)(2,1)S(1)} %get-tuple-element.45.refs_1_.refs_0_.refs_4_, ...), custom_call_target="tpu_custom_call" | custom-call | flops 1000 | bytes 1000 | tf_op jit(solution)/shard_map/rows_even/pallas_call | solution.py:197
  14.1 4.2 %collective-permute-start.3 = (bf16[4,128,256]{2,1,0:T(8,128)(2,1)S(1)}, bf16[4,128,256]{2,1,0:T(8,128)(2,1)S(1)}, u32[]{:S(2)}, u32[]{:S(2)}) collective-permute-start(bf16[4,128,256]{2,1,0:T(8,128)(2,1)S(1)} %rows_even.3.refs_1_.refs_0_.refs_4_), channel_id=1, source_target_pairs={{0,1},{1,0},{2,3},{3,2},{4,5},{5,4},{6,7},{7,6},{8,9},{9,8},{10,11... | collective-permute-start | bytes 786440 | tf_op jit(solution)/shard_map/ppermute | solution.py:526
  18.3 2.1 %rows_low.3.refs_2_.refs_4_ = bf16[12,128,256]{2,1,0:T(8,128)(2,1)S(1)} custom-call(s32[3]{0:T(128)S(1)} %pad_add_fusion.info, s32[256]{0:T(256)S(1)} %reshape.18.cols_ref, bf16[4,128,256]{2,1,0:T(8,128)(2,1)S(1)} %get-tuple-element.45.refs_1_.refs_0_.refs_4_, bf16[4,128,256]{2,1,0:T(8,128)(2,1)S(1)} %get-tuple-element.39.refs_1_.refs_4_, ...), custom_call_target="tpu_custom_call" | custom-call | flops 1000 | bytes 1000 | tf_op jit(solution)/shard_map/rows_low/pallas_call | solution.py:197
  20.4 2.1 %rows_high.3.refs_3_.refs_4_ = bf16[12,128,256]{2,1,0:T(8,128)(2,1)S(1)} custom-call(s32[3]{0:T(128)S(1)} %pad_add_fusion.info, s32[256]{0:T(256)S(1)} %reshape.18.cols_ref, bf16[4,128,256]{2,1,0:T(8,128)(2,1)S(1)} %get-tuple-element.45.refs_1_.refs_0_.refs_4_, bf16[4,128,256]{2,1,0:T(8,128)(2,1)S(1)} %get-tuple-element.39.refs_1_.refs_4_, ...), custom_call_target="tpu_custom_call" | custom-call | flops 1000 | bytes 1000 | tf_op jit(solution)/shard_map/rows_high/pallas_call | solution.py:197
  22.5 0.0 collective-permute-done.refs_0_
  22.5 1.1 %rows_odd.3.refs_1_.refs_4_ = bf16[4,128,256]{2,1,0:T(8,128)(2,1)S(1)} custom-call(s32[3]{0:T(128)S(1)} %pad_add_fusion.info, s32[256]{0:T(256)S(1)} %reshape.18.cols_ref, bf16[4,128,256]{2,1,0:T(8,128)(2,1)S(1)} %collective-permute-done.refs_0_, bf16[4,128,256]{2,1,0:T(8,128)(2,1)S(1)} %get-tuple-element.39.refs_1_.refs_4_, ...), custom_call_target="tpu_custom_call" | custom-call | flops 1000 | bytes 1000 | tf_op jit(solution)/shard_map/rows_odd/pallas_call | solution.py:197
  23.6 0.7 collective-permute-start.2
  24.3 0.7 collective-permute-done.3.refs_0_
  25.0 1.1 %rows_even.4.refs_1_.refs_0_ = bf16[4,128,256]{2,1,0:T(8,128)(2,1)S(1)} custom-call(s32[3]{0:T(128)S(1)} %pad_add_fusion.info, s32[256]{0:T(256)S(1)} %reshape.18.cols_ref, bf16[4,128,256]{2,1,0:T(8,128)(2,1)S(1)} %collective-permute-done.3.refs_0_, bf16[4,128,256]{2,1,0:T(8,128)(2,1)S(1)} %rows_even.3.refs_1_.refs_0_.refs_4_, ...), custom_call_target="tpu_custom_call" | custom-call | flops 1000 | bytes 1000 | tf_op jit(solution)/shard_map/rows_even/pallas_call | solution.py:197
  26.1 3.5 %collective-permute-start.5 = (bf16[4,128,256]{2,1,0:T(8,128)(2,1)S(1)}, bf16[4,128,256]{2,1,0:T(8,128)(2,1)S(1)}, u32[]{:S(2)}, u32[]{:S(2)}) collective-permute-start(bf16[4,128,256]{2,1,0:T(8,128)(2,1)S(1)} %rows_even.4.refs_1_.refs_0_), channel_id=1, source_target_pairs={{0,1},{1,0},{2,3},{3,2},{4,5},{5,4},{6,7},{7,6},{8,9},{9,8},{10,11... | collective-permute-start | bytes 786440 | tf_op jit(solution)/shard_map/ppermute | solution.py:526
  29.7 2.1 %rows_high.4.refs_3_ = bf16[12,128,256]{2,1,0:T(8,128)(2,1)S(1)} custom-call(s32[3]{0:T(128)S(1)} %pad_add_fusion.info, s32[256]{0:T(256)S(1)} %reshape.18.cols_ref, bf16[4,128,256]{2,1,0:T(8,128)(2,1)S(1)} %rows_even.3.refs_1_.refs_0_.refs_4_, bf16[4,128,256]{2,1,0:T(8,128)(2,1)S(1)} %rows_odd.3.refs_1_.refs_4_, ...), custom_call_target="tpu_custom_call" | custom-call | flops 1000 | bytes 1000 | tf_op jit(solution)/shard_map/rows_high/pallas_call | solution.py:197
  31.8 2.1 %rows_low.4.refs_2_ = bf16[12,128,256]{2,1,0:T(8,128)(2,1)S(1)} custom-call(s32[3]{0:T(128)S(1)} %pad_add_fusion.info, s32[256]{0:T(256)S(1)} %reshape.18.cols_ref, bf16[4,128,256]{2,1,0:T(8,128)(2,1)S(1)} %rows_even.3.refs_1_.refs_0_.refs_4_, bf16[4,128,256]{2,1,0:T(8,128)(2,1)S(1)} %rows_odd.3.refs_1_.refs_4_, ...), custom_call_target="tpu_custom_call" | custom-call | flops 1000 | bytes 1000 | tf_op jit(solution)/shard_map/rows_low/pallas_call | solution.py:197
  34.0 0.0 collective-permute-done.2.refs_0_
  34.0 1.1 %rows_odd.4.refs_1_ = bf16[4,128,256]{2,1,0:T(8,128)(2,1)S(1)} custom-call(s32[3]{0:T(128)S(1)} %pad_add_fusion.info, s32[256]{0:T(256)S(1)} %reshape.18.cols_ref, bf16[4,128,256]{2,1,0:T(8,128)(2,1)S(1)} %collective-permute-done.2.refs_0_, bf16[4,128,256]{2,1,0:T(8,128)(2,1)S(1)} %rows_odd.3.refs_1_.refs_4_, ...), custom_call_target="tpu_custom_call" | custom-call | flops 1000 | bytes 1000 | tf_op jit(solution)/shard_map/rows_odd/pallas_call | solution.py:197
  35.1 0.9 collective-permute-start.4
  35.9 3.5 %collective-permute-done.5.refs_0_ = bf16[4,128,256]{2,1,0:T(8,128)(2,1)S(1)} collective-permute-done((bf16[4,128,256]{2,1,0:T(8,128)(2,1)S(1)}, bf16[4,128,256]{2,1,0:T(8,128)(2,1)S(1)}, u32[]{:S(2)}, u32[]{:S(2)}) %collective-permute-start.5) | collective-permute-done | bytes 262176 | tf_op jit(solution)/shard_map/ppermute | solution.py:526
  39.4 1.1 %rows_even.5 = bf16[4,128,256]{2,1,0:T(8,128)(2,1)S(1)} custom-call(s32[3]{0:T(128)S(1)} %pad_add_fusion.info, s32[256]{0:T(256)S(1)} %reshape.18.cols_ref, bf16[4,128,256]{2,1,0:T(8,128)(2,1)S(1)} %collective-permute-done.5.refs_0_, bf16[4,128,256]{2,1,0:T(8,128)(2,1)S(1)} %rows_even.4.refs_1_.refs_0_, bf16[12,128,256]{2,1,0:T(8,128)(2,1)S(1)} %rows_low.4.refs_2_, ...), custom_call_target="tpu_custom_call" | custom-call | flops 1000 | bytes 1000 | tf_op jit(solution)/shard_map/rows_even/pallas_call | solution.py:197
  40.5 2.1 %rows_high.5 = bf16[12,128,256]{2,1,0:T(8,128)(2,1)S(1)} custom-call(s32[3]{0:T(128)S(1)} %pad_add_fusion.info, s32[256]{0:T(256)S(1)} %reshape.18.cols_ref, bf16[4,128,256]{2,1,0:T(8,128)(2,1)S(1)} %rows_even.4.refs_1_.refs_0_, bf16[4,128,256]{2,1,0:T(8,128)(2,1)S(1)} %rows_odd.4.refs_1_, bf16[12,128,256]{2,1,0:T(8,128)(2,1)S(1)} %rows_low.4.refs_2_, ...), custom_call_target="tpu_custom_call" | custom-call | flops 1000 | bytes 1000 | tf_op jit(solution)/shard_map/rows_high/pallas_call | solution.py:197
  42.7 2.1 %rows_low.5 = bf16[12,128,256]{2,1,0:T(8,128)(2,1)S(1)} custom-call(s32[3]{0:T(128)S(1)} %pad_add_fusion.info, s32[256]{0:T(256)S(1)} %reshape.18.cols_ref, bf16[4,128,256]{2,1,0:T(8,128)(2,1)S(1)} %rows_even.4.refs_1_.refs_0_, bf16[4,128,256]{2,1,0:T(8,128)(2,1)S(1)} %rows_odd.4.refs_1_, bf16[12,128,256]{2,1,0:T(8,128)(2,1)S(1)} %rows_low.4.refs_2_, ...), custom_call_target="tpu_custom_call" | custom-call | flops 1000 | bytes 1000 | tf_op jit(solution)/shard_map/rows_low/pallas_call | solution.py:197
  44.8 0.1 collective-permute-start.7
  44.9 0.5 collective-permute-start.9
  45.4 1.9 %gram_square.1.square_ref = f32[256,256]{1,0:T(8,128)S(1)} custom-call(bf16[512,256]{1,0:T(8,128)(2,1)S(1)} %bitcast.16, bf16[1536,256]{1,0:T(8,128)(2,1)S(1)} %bitcast.11, bf16[1536,256]{1,0:T(8,128)(2,1)S(1)} %bitcast.8), custom_call_target="tpu_custom_call" | custom-call | flops 1000 | bytes 1000 | tf_op jit(solution)/shard_map/gram_square/pallas_call | solution.py:270
  47.3 0.1 collective-permute-start.8
  47.5 0.0 collective-permute-done.4.refs_0_
  47.5 1.1 %rows_odd.5 = bf16[4,128,256]{2,1,0:T(8,128)(2,1)S(1)} custom-call(s32[3]{0:T(128)S(1)} %pad_add_fusion.info, s32[256]{0:T(256)S(1)} %reshape.18.cols_ref, bf16[4,128,256]{2,1,0:T(8,128)(2,1)S(1)} %collective-permute-done.4.refs_0_, bf16[4,128,256]{2,1,0:T(8,128)(2,1)S(1)} %rows_odd.4.refs_1_, bf16[12,128,256]{2,1,0:T(8,128)(2,1)S(1)} %rows_low.4.refs_2_, ...), custom_call_target="tpu_custom_call" | custom-call | flops 99999997952 | bytes 1000 | tf_op jit(solution)/shard_map/rows_odd/pallas_call | solution.py:197
  48.6 0.5 collective-permute-start.6
  49.1 0.0 collective-permute-done.7.refs_3_.refs_4_
  49.1 0.0 collective-permute-done.9.refs_5_.refs_6_
  49.1 0.6 collective-permute-done.8.refs_4_.refs_5_
  49.7 2.2 %gram_cross.1.cross_ref = f32[128,256]{1,0:T(8,128)S(1)} custom-call(s32[3]{0:T(128)S(1)} %pad_add_fusion.info, bf16[512,256]{1,0:T(8,128)(2,1)S(1)} %bitcast.17, bf16[1536,256]{1,0:T(8,128)(2,1)S(1)} %bitcast.13, bf16[1536,256]{1,0:T(8,128)(2,1)S(1)} %bitcast.9, bf16[512,256]{1,0:T(8,128)(2,1)S(1)} %collective-permute-done.7.refs_3_.refs_4_, ...), custom_call_target="tpu_custom_call" | custom-call | flops 1000 | bytes 1000 | tf_op jit(solution)/shard_map/gram_cross/pallas_call | solution.py:270
  51.9 0.0 collective-permute-done.6.other_ref.refs_7_
  51.9 0.9 gram_share.1
  52.8 2.5 %collective-permute-start.10 = (f32[160,128]{1,0:T(8,128)S(1)}, f32[160,128]{1,0:T(8,128)S(1)}, u32[]{:S(2)}, u32[]{:S(2)}) collective-permute-start(f32[160,128]{1,0:T(8,128)S(1)} %get-tuple-element.60), channel_id=1, source_target_pairs={{0,1},{1,0},{2,3},{3,2},{4,5},{5,4},{6,7},{7,6},{8,9},{9,8},{10,11... | collective-permute-start | bytes 245768 | tf_op jit(solution)/shard_map/ppermute | solution.py:329
  55.3 0.6 collective-permute-start.11
  55.9 0.9 collective-permute-start.12
  56.8 1.2 %collective-permute-done.10.b = f32[160,128]{1,0:T(8,128)S(1)} collective-permute-done((f32[160,128]{1,0:T(8,128)S(1)}, f32[160,128]{1,0:T(8,128)S(1)}, u32[]{:S(2)}, u32[]{:S(2)}) %collective-permute-start.10) | collective-permute-done | bytes 81952 | tf_op jit(solution)/shard_map/ppermute | solution.py:329
  58.0 3.5 %collective-permute-done.11.c = f32[160,128]{1,0:T(8,128)S(1)} collective-permute-done((f32[160,128]{1,0:T(8,128)S(1)}, f32[160,128]{1,0:T(8,128)S(1)}, u32[]{:S(2)}, u32[]{:S(2)}) %collective-permute-start.11) | collective-permute-done | bytes 81952 | tf_op jit(solution)/shard_map/ppermute | solution.py:329
  61.5 0.0 collective-permute-done.12.d
  61.5 4.8 %collective-permute-start.15 = (f32[160,128]{1,0:T(8,128)S(1)}, f32[160,128]{1,0:T(8,128)S(1)}, u32[]{:S(2)}, u32[]{:S(2)}) collective-permute-start(f32[160,128]{1,0:T(8,128)S(1)} %add_four.2.a), channel_id=1, source_target_pairs={{0,12},{1,13},{2,14},{3,15},{4,8},{5,9},{6,10},{7,11},{8,4},{9,5},... | collective-permute-start | bytes 245768 | tf_op jit(solution)/shard_map/ppermute | solution.py:329
  66.4 0.0 collective-permute-start.14
  66.4 0.6 collective-permute-start.13
  67.0 2.5 %collective-permute-done.15.d = f32[160,128]{1,0:T(8,128)S(1)} collective-permute-done((f32[160,128]{1,0:T(8,128)S(1)}, f32[160,128]{1,0:T(8,128)S(1)}, u32[]{:S(2)}, u32[]{:S(2)}) %collective-permute-start.15) | collective-permute-done | bytes 81952 | tf_op jit(solution)/shard_map/ppermute | solution.py:329
  69.5 3.4 %collective-permute-done.14.c = f32[160,128]{1,0:T(8,128)S(1)} collective-permute-done((f32[160,128]{1,0:T(8,128)S(1)}, f32[160,128]{1,0:T(8,128)S(1)}, u32[]{:S(2)}, u32[]{:S(2)}) %collective-permute-start.14) | collective-permute-done | bytes 81952 | tf_op jit(solution)/shard_map/ppermute | solution.py:329
  72.9 0.0 collective-permute-done.13.b
  73.0 1.1 %collective-permute-start.18 = (f32[160,128]{1,0:T(8,128)S(1)}, f32[160,128]{1,0:T(8,128)S(1)}, u32[]{:S(2)}, u32[]{:S(2)}) collective-permute-start(f32[160,128]{1,0:T(8,128)S(1)} %add_four.3.refs_0_), channel_id=1, source_target_pairs={{0,3},{1,2},{2,1},{3,0},{4,7},{5,6},{6,5},{7,4},{8,11},{9,10},{10,... | collective-permute-start | bytes 245768 | tf_op jit(solution)/shard_map/ppermute | solution.py:329
  74.0 1.5 %collective-permute-start.17 = (f32[160,128]{1,0:T(8,128)S(1)}, f32[160,128]{1,0:T(8,128)S(1)}, u32[]{:S(2)}, u32[]{:S(2)}) collective-permute-start(f32[160,128]{1,0:T(8,128)S(1)} %add_four.3.refs_0_), channel_id=1, source_target_pairs={{0,2},{1,3},{2,0},{3,1},{4,6},{5,7},{6,4},{7,5},{8,10},{9,11},{10,... | collective-permute-start | bytes 245768 | tf_op jit(solution)/shard_map/ppermute | solution.py:329
  75.6 0.9 collective-permute-start.16
  76.5 1.9 %collective-permute-done.18.refs_3_ = f32[160,128]{1,0:T(8,128)S(1)} collective-permute-done((f32[160,128]{1,0:T(8,128)S(1)}, f32[160,128]{1,0:T(8,128)S(1)}, u32[]{:S(2)}, u32[]{:S(2)}) %collective-permute-start.18) | collective-permute-done | bytes 81952 | tf_op jit(solution)/shard_map/ppermute | solution.py:329
  78.5 0.8 collective-permute-done.17.refs_2_
  79.3 0.8 collective-permute-done.16.refs_1_
  80.0 0.6 join.1.mine
  80.6 0.1 collective-permute-start.19
  80.7 1.6 %collective-permute-done.19.theirs = f32[640,128]{1,0:T(8,128)S(1)} collective-permute-done((f32[640,128]{1,0:T(8,128)S(1)}, f32[640,128]{1,0:T(8,128)S(1)}, u32[]{:S(2)}, u32[]{:S(2)}) %collective-permute-start.19) | collective-permute-done | bytes 327712 | tf_op jit(solution)/shard_map/ppermute | solution.py:529
  82.3 17.2 %rotate.1 = bf16[4096,256]{1,0:T(8,128)(2,1)} custom-call(s32[3]{0:T(128)S(1)} %pad_add_fusion.info, f32[640,128]{1,0:T(8,128)S(1)} %join.1.mine, f32[640,128]{1,0:T(8,128)S(1)} %collective-permute-done.19.theirs, bf16[512,256]{1,0:T(8,128)(2,1)S(1)} %bitcast.18, bf16[1536,256]{1,0:T(8,128)(2,1)S(1)} %bitcast.14, bf16[1536,256]{1,0:T(8,128)(2,1)S(1)} %bitcast.10, ...), custom_call_target="tpu_custom_call" | custom-call | flops 17985175552 | bytes 6291456 | tf_op jit(solution)/shard_map/rotate/pallas_call | solution.py:488
  (2 shorter events, 0.0 us)
Async XLA Ops:
  3.2 9.8 %collective-permute-start.1 = (bf16[4,128,256]{2,1,0:T(8,128)(2,1)S(1)}, bf16[4,128,256]{2,1,0:T(8,128)(2,1)S(1)}, u32[]{:S(2)}, u32[]{:S(2)}) collective-permute-start(bf16[4,128,256]{2,1,0:T(8,128)(2,1)S(1)} %get-tuple-element.45.refs_1_.refs_0_.refs_4_), channel_id=1, source_target_pairs={{0,1},{1,0},{2,3},{3,2},{4,5},{5,4},{6,7},{7,6},{8,9},{9,8},{10,11... | collective-permute-start | bytes 786440 | tf_op jit(solution)/shard_map/ppermute | solution.py:526
  8.9 13.6 %collective-permute-start = (bf16[4,128,256]{2,1,0:T(8,128)(2,1)S(1)}, bf16[4,128,256]{2,1,0:T(8,128)(2,1)S(1)}, u32[]{:S(2)}, u32[]{:S(2)}) collective-permute-start(bf16[4,128,256]{2,1,0:T(8,128)(2,1)S(1)} %get-tuple-element.39.refs_1_.refs_4_), channel_id=1, source_target_pairs={{1,2},{2,1},{3,4},{4,3},{5,6},{6,5},{7,8},{8,7},{9,10},{10,9},{11,... | collective-permute-start | bytes 786440 | tf_op jit(solution)/shard_map/ppermute | solution.py:526
  14.1 10.9 %collective-permute-start.3 = (bf16[4,128,256]{2,1,0:T(8,128)(2,1)S(1)}, bf16[4,128,256]{2,1,0:T(8,128)(2,1)S(1)}, u32[]{:S(2)}, u32[]{:S(2)}) collective-permute-start(bf16[4,128,256]{2,1,0:T(8,128)(2,1)S(1)} %rows_even.3.refs_1_.refs_0_.refs_4_), channel_id=1, source_target_pairs={{0,1},{1,0},{2,3},{3,2},{4,5},{5,4},{6,7},{7,6},{8,9},{9,8},{10,11... | collective-permute-start | bytes 786440 | tf_op jit(solution)/shard_map/ppermute | solution.py:526
  23.6 10.3 %collective-permute-start.2 = (bf16[4,128,256]{2,1,0:T(8,128)(2,1)S(1)}, bf16[4,128,256]{2,1,0:T(8,128)(2,1)S(1)}, u32[]{:S(2)}, u32[]{:S(2)}) collective-permute-start(bf16[4,128,256]{2,1,0:T(8,128)(2,1)S(1)} %rows_odd.3.refs_1_.refs_4_), channel_id=1, source_target_pairs={{1,2},{2,1},{3,4},{4,3},{5,6},{6,5},{7,8},{8,7},{9,10},{10,9},{11,... | collective-permute-start | bytes 786440 | tf_op jit(solution)/shard_map/ppermute | solution.py:526
  26.1 13.3 %collective-permute-start.5 = (bf16[4,128,256]{2,1,0:T(8,128)(2,1)S(1)}, bf16[4,128,256]{2,1,0:T(8,128)(2,1)S(1)}, u32[]{:S(2)}, u32[]{:S(2)}) collective-permute-start(bf16[4,128,256]{2,1,0:T(8,128)(2,1)S(1)} %rows_even.4.refs_1_.refs_0_), channel_id=1, source_target_pairs={{0,1},{1,0},{2,3},{3,2},{4,5},{5,4},{6,7},{7,6},{8,9},{9,8},{10,11... | collective-permute-start | bytes 786440 | tf_op jit(solution)/shard_map/ppermute | solution.py:526
  35.1 12.4 %collective-permute-start.4 = (bf16[4,128,256]{2,1,0:T(8,128)(2,1)S(1)}, bf16[4,128,256]{2,1,0:T(8,128)(2,1)S(1)}, u32[]{:S(2)}, u32[]{:S(2)}) collective-permute-start(bf16[4,128,256]{2,1,0:T(8,128)(2,1)S(1)} %rows_odd.4.refs_1_), channel_id=1, source_target_pairs={{1,2},{2,1},{3,4},{4,3},{5,6},{6,5},{7,8},{8,7},{9,10},{10,9},{11,... | collective-permute-start | bytes 786440 | tf_op jit(solution)/shard_map/ppermute | solution.py:526
  44.8 4.3 %collective-permute-start.7 = (bf16[512,256]{1,0:T(8,128)(2,1)S(1)}, bf16[512,256]{1,0:T(8,128)(2,1)S(1)}, u32[]{:S(2)}, u32[]{:S(2)}) collective-permute-start(bf16[512,256]{1,0:T(8,128)(2,1)S(1)} %bitcast.15), channel_id=1, source_target_pairs={{0,16},{16,0},{1,17},{17,1},{2,18},{18,2},{3,19},{19,3},{4,20},{20... | collective-permute-start | bytes 786440 | tf_op jit(solution)/shard_map/ppermute | solution.py:529
  44.9 4.2 %collective-permute-start.9 = (bf16[1536,256]{1,0:T(8,128)(2,1)S(1)}, bf16[1536,256]{1,0:T(8,128)(2,1)S(1)}, u32[]{:S(2)}, u32[]{:S(2)}) collective-permute-start(bf16[1536,256]{1,0:T(8,128)(2,1)S(1)} %bitcast.7), channel_id=1, source_target_pairs={{0,16},{16,0},{1,17},{17,1},{2,18},{18,2},{3,19},{19,3},{4,20},{20... | collective-permute-start | bytes 2359304 | tf_op jit(solution)/shard_map/ppermute | solution.py:529
  47.3 2.4 %collective-permute-start.8 = (bf16[1536,256]{1,0:T(8,128)(2,1)S(1)}, bf16[1536,256]{1,0:T(8,128)(2,1)S(1)}, u32[]{:S(2)}, u32[]{:S(2)}) collective-permute-start(bf16[1536,256]{1,0:T(8,128)(2,1)S(1)} %bitcast.12), channel_id=1, source_target_pairs={{0,16},{16,0},{1,17},{17,1},{2,18},{18,2},{3,19},{19,3},{4,20},{20... | collective-permute-start | bytes 2359304 | tf_op jit(solution)/shard_map/ppermute | solution.py:529
  48.6 3.3 %collective-permute-start.6 = (bf16[512,256]{1,0:T(8,128)(2,1)S(1)}, bf16[512,256]{1,0:T(8,128)(2,1)S(1)}, u32[]{:S(2)}, u32[]{:S(2)}) collective-permute-start(bf16[512,256]{1,0:T(8,128)(2,1)S(1)} %bitcast.19), channel_id=1, source_target_pairs={{0,16},{16,0},{1,17},{17,1},{2,18},{18,2},{3,19},{19,3},{4,20},{20... | collective-permute-start | bytes 786440 | tf_op jit(solution)/shard_map/ppermute | solution.py:529
  52.8 5.2 %collective-permute-start.10 = (f32[160,128]{1,0:T(8,128)S(1)}, f32[160,128]{1,0:T(8,128)S(1)}, u32[]{:S(2)}, u32[]{:S(2)}) collective-permute-start(f32[160,128]{1,0:T(8,128)S(1)} %get-tuple-element.60), channel_id=1, source_target_pairs={{0,1},{1,0},{2,3},{3,2},{4,5},{5,4},{6,7},{7,6},{8,9},{9,8},{10,11... | collective-permute-start | bytes 245768 | tf_op jit(solution)/shard_map/ppermute | solution.py:329
  55.3 6.2 %collective-permute-start.11 = (f32[160,128]{1,0:T(8,128)S(1)}, f32[160,128]{1,0:T(8,128)S(1)}, u32[]{:S(2)}, u32[]{:S(2)}) collective-permute-start(f32[160,128]{1,0:T(8,128)S(1)} %get-tuple-element.61), channel_id=1, source_target_pairs={{0,2},{1,3},{2,0},{3,1},{4,6},{5,7},{6,4},{7,5},{8,10},{9,11},{10,... | collective-permute-start | bytes 245768 | tf_op jit(solution)/shard_map/ppermute | solution.py:329
  55.9 5.6 %collective-permute-start.12 = (f32[160,128]{1,0:T(8,128)S(1)}, f32[160,128]{1,0:T(8,128)S(1)}, u32[]{:S(2)}, u32[]{:S(2)}) collective-permute-start(f32[160,128]{1,0:T(8,128)S(1)} %get-tuple-element.62), channel_id=1, source_target_pairs={{0,3},{1,2},{2,1},{3,0},{4,7},{5,6},{6,5},{7,4},{8,11},{9,10},{10,... | collective-permute-start | bytes 245768 | tf_op jit(solution)/shard_map/ppermute | solution.py:329
  61.5 8.0 %collective-permute-start.15 = (f32[160,128]{1,0:T(8,128)S(1)}, f32[160,128]{1,0:T(8,128)S(1)}, u32[]{:S(2)}, u32[]{:S(2)}) collective-permute-start(f32[160,128]{1,0:T(8,128)S(1)} %add_four.2.a), channel_id=1, source_target_pairs={{0,12},{1,13},{2,14},{3,15},{4,8},{5,9},{6,10},{7,11},{8,4},{9,5},... | collective-permute-start | bytes 245768 | tf_op jit(solution)/shard_map/ppermute | solution.py:329
  66.4 6.6 %collective-permute-start.14 = (f32[160,128]{1,0:T(8,128)S(1)}, f32[160,128]{1,0:T(8,128)S(1)}, u32[]{:S(2)}, u32[]{:S(2)}) collective-permute-start(f32[160,128]{1,0:T(8,128)S(1)} %add_four.2.a), channel_id=1, source_target_pairs={{0,8},{1,9},{2,10},{3,11},{4,12},{5,13},{6,14},{7,15},{8,0},{9,1},... | collective-permute-start | bytes 245768 | tf_op jit(solution)/shard_map/ppermute | solution.py:329
  66.4 6.6 %collective-permute-start.13 = (f32[160,128]{1,0:T(8,128)S(1)}, f32[160,128]{1,0:T(8,128)S(1)}, u32[]{:S(2)}, u32[]{:S(2)}) collective-permute-start(f32[160,128]{1,0:T(8,128)S(1)} %add_four.2.a), channel_id=1, source_target_pairs={{0,4},{1,5},{2,6},{3,7},{4,0},{5,1},{6,2},{7,3},{8,12},{9,13},{10,... | collective-permute-start | bytes 245768 | tf_op jit(solution)/shard_map/ppermute | solution.py:329
  73.0 5.5 %collective-permute-start.18 = (f32[160,128]{1,0:T(8,128)S(1)}, f32[160,128]{1,0:T(8,128)S(1)}, u32[]{:S(2)}, u32[]{:S(2)}) collective-permute-start(f32[160,128]{1,0:T(8,128)S(1)} %add_four.3.refs_0_), channel_id=1, source_target_pairs={{0,3},{1,2},{2,1},{3,0},{4,7},{5,6},{6,5},{7,4},{8,11},{9,10},{10,... | collective-permute-start | bytes 245768 | tf_op jit(solution)/shard_map/ppermute | solution.py:329
  74.0 5.2 %collective-permute-start.17 = (f32[160,128]{1,0:T(8,128)S(1)}, f32[160,128]{1,0:T(8,128)S(1)}, u32[]{:S(2)}, u32[]{:S(2)}) collective-permute-start(f32[160,128]{1,0:T(8,128)S(1)} %add_four.3.refs_0_), channel_id=1, source_target_pairs={{0,2},{1,3},{2,0},{3,1},{4,6},{5,7},{6,4},{7,5},{8,10},{9,11},{10,... | collective-permute-start | bytes 245768 | tf_op jit(solution)/shard_map/ppermute | solution.py:329
  75.6 4.4 %collective-permute-start.16 = (f32[160,128]{1,0:T(8,128)S(1)}, f32[160,128]{1,0:T(8,128)S(1)}, u32[]{:S(2)}, u32[]{:S(2)}) collective-permute-start(f32[160,128]{1,0:T(8,128)S(1)} %add_four.3.refs_0_), channel_id=1, source_target_pairs={{0,1},{1,0},{2,3},{3,2},{4,5},{5,4},{6,7},{7,6},{8,9},{9,8},{10,11... | collective-permute-start | bytes 245768 | tf_op jit(solution)/shard_map/ppermute | solution.py:329
  80.6 1.7 %collective-permute-start.19 = (f32[640,128]{1,0:T(8,128)S(1)}, f32[640,128]{1,0:T(8,128)S(1)}, u32[]{:S(2)}, u32[]{:S(2)}) collective-permute-start(f32[640,128]{1,0:T(8,128)S(1)} %join.1.mine), channel_id=1, source_target_pairs={{0,16},{16,0},{1,17},{17,1},{2,18},{18,2},{3,19},{19,3},{4,20},{20... | collective-permute-start | bytes 983048 | tf_op jit(solution)/shard_map/ppermute | solution.py:529

commit v7 on v6

--- a/solution.py
+++ b/solution.py
@@ -11,6 +11,7 @@
 STEPS = 3
 ITERS = 8
 WAYS = 4
+LOAD_CUTS = 4
 GROUP = 4
 
 SMALL = pl.CostEstimate(flops=1000, bytes_accessed=1000, transcendentals=0)
@@ -71,10 +72,17 @@
 
 
 def load(moves, sem):
-    copies = [
-        pltpu.make_async_copy(source.at[pl.ds(first, target.shape[0])], target, sem.at[i])
-        for i, (source, first, target) in enumerate(moves)
-    ]
+    copies = []
+    for source, first, target in moves:
+        count = target.shape[0] // LOAD_CUTS
+        for cut in range(LOAD_CUTS):
+            copies.append(
+                pltpu.make_async_copy(
+                    source.at[pl.ds(first + cut * count, count)],
+                    target.at[pl.ds(cut * count, count)],
+                    sem.at[len(copies)],
+                )
+            )
     for copy in copies:
         copy.start()
     for copy in copies:
@@ -120,7 +128,7 @@
         in_specs=[SMEM] + [HBM] * len(args),
         out_specs=[VMEM] * len(shapes),
         out_shape=shapes,
-        scratch_shapes=[pltpu.SemaphoreType.DMA((len(shapes),))],
+        scratch_shapes=[pltpu.SemaphoreType.DMA((len(shapes) * LOAD_CUTS,))],
         compiler_params=pltpu.CompilerParams(vmem_limit_bytes=megabytes * 1024 * 1024),
         cost_estimate=SMALL,
         name=name,
@@ -173,7 +181,7 @@
     def group(index, carry):
         for r in range(GROUP):
             row = index * GROUP + r
-            listed = [cols_ref[(first + row) * nnz + n] - shift for n in range(nnz)]
+            listed = [cols_ref[n, first + row] - shift for n in range(nnz)]
             acc = tile_row(lambda n: blocks_ref[row, n], listed, lambda c: held[c])
             prev = None if prev_ref is None else prev_ref[row]
             out_ref[row] = finish(acc, prev, first + row < live)
@@ -183,8 +191,8 @@
 
 
 def tile_rows(name, info, cols, blocks, pieces, prev, cost):
-    rows, nnz, tile, _ = blocks.shape
-    tiles = cols.shape[0] // nnz
+    rows, _, tile, _ = blocks.shape
+    tiles = cols.shape[1]
     width = pieces[0].shape[-1]
     edge, half = HALO_T, tiles // 2 - HALO_T
     if name in ("even", "odd"):
@@ -209,54 +217,34 @@
 ACROSS = (((0,), (0,)), ((), ()))
 
 
-def add_square(chunk, own_ref, square):
-    def add(index, carry):
-        own = own_ref[pl.ds(pl.multiple_of(index * chunk, chunk), chunk), :]
-        square[...] += lax.dot_general(own, own, ACROSS, preferred_element_type=F32)
-        return carry
-
-    lax.fori_loop(0, own_ref.shape[0] // chunk, add, 0)
-
-
-def add_cross(chunk, info, own_ref, other_ref, cross):
-    half = cross.shape[0]
-    is_first = info[PART] == 0
-
+def add_gram(chunk, own_ref, other_ref, total):
     def add(index, carry):
         rows = pl.ds(pl.multiple_of(index * chunk, chunk), chunk)
-        own, other = own_ref[rows, :], other_ref[rows, :]
-        left = jnp.where(is_first, own[:, :half], other[:, half:])
-        right = jnp.where(is_first, other, own)
-        cross[...] += lax.dot_general(left, right, ACROSS, preferred_element_type=F32)
+        own = own_ref[rows, :]
+        both = jnp.concatenate([own, other_ref[rows, :]], axis=1)
+        total[...] += lax.dot_general(own, both, ACROSS, preferred_element_type=F32)
         return carry
 
     lax.fori_loop(0, own_ref.shape[0] // chunk, add, 0)
 
 
-def square_kernel(chunk, *refs):
-    refs[-1][...] = jnp.zeros(refs[-1].shape, F32)
-    for own_ref in refs[:-1]:
-        add_square(chunk, own_ref, refs[-1])
-
-
-def cross_kernel(chunk, info, *refs):
+def gram_kernel(chunk, *refs):
     count = len(refs) // 2
     refs[-1][...] = jnp.zeros(refs[-1].shape, F32)
     for own_ref, other_ref in zip(refs[:count], refs[count:-1]):
-        add_cross(chunk, info, own_ref, other_ref, refs[-1])
-
-
-def share_kernel(chunk, info, own_ref, other_ref, square_ref, cross_ref, *refs):
-    outs, (square, cross, share) = refs[:WAYS], refs[WAYS:]
-    square[...] = square_ref[...]
-    cross[...] = cross_ref[...]
-    add_square(chunk, own_ref, square)
-    add_cross(chunk, info, own_ref, other_ref, cross)
-    half = cross.shape[0]
-    blocks = [
-        square[:half, :half], square[:half, half:], square[half:, half:],
-        cross[:, :half], cross[:, half:],
-    ]
+        add_gram(chunk, own_ref, other_ref, refs[-1])
+
+
+def share_kernel(chunk, info, own_ref, other_ref, start_ref, *refs):
+    outs, (total, share) = refs[:WAYS], refs[WAYS:]
+    total[...] = start_ref[...]
+    add_gram(chunk, own_ref, other_ref, total)
+    width = total.shape[0]
+    half = width // 2
+    own, other = total[:, :width], total[:, width:]
+    second = jnp.where(info[PART] == 0, other[:half, :half], other[:half, half:])
+    third = jnp.where(info[PART] == 0, other[:half, half:], other[half:, half:])
+    blocks = [own[:half, :half], own[:half, half:], own[half:, half:], second, third]
     for i, block in enumerate(blocks):
         share[pl.ds(i * half, half), :] = block
     quarter = info[PATCH] % WAYS
@@ -279,29 +267,19 @@
     )(*scalars, *args)
 
 
-def gram_square(owns):
+def gram(owns, others):
     chunk, width = min(own.shape[0] for own in owns), owns[0].shape[1]
-    body = functools.partial(square_kernel, chunk)
-    return gram_call(body, "gram_square", owns, (width, width))
-
-
-def gram_cross(info, owns, others):
-    chunk, width = min(own.shape[0] for own in owns), owns[0].shape[1]
-    body = functools.partial(cross_kernel, chunk)
-    shape = (width // 2, width)
-    return gram_call(body, "gram_cross", owns + others, shape, scalars=[info])
-
-
-def gram_share(info, own, other, square, cross):
-    width = own.shape[1]
+    body = functools.partial(gram_kernel, chunk)
+    return gram_call(body, "gram", owns + others, (width, 2 * width))
+
+
+def gram_share(info, own, other, start):
+    rows, width = own.shape
     half = width // 2
-    body = functools.partial(share_kernel, own.shape[0])
-    scratch = [
-        pltpu.VMEM((width, width), F32), pltpu.VMEM((half, width), F32),
-        pltpu.VMEM((5 * half, half), F32),
-    ]
-    args = [own, other, square, cross]
+    body = functools.partial(share_kernel, rows)
+    scratch = [pltpu.VMEM((width, 2 * width), F32), pltpu.VMEM((5 * half, half), F32)]
     shape = (5 * half // WAYS, half)
+    args = [own, other, start]
     return gram_call(body, "gram_share", args, shape, scratch, [info], outs=WAYS)
 
 
@@ -419,8 +397,9 @@
         place(2 * side, 2 * side + 1, across)
         place(2 * side + 1, 2 * side, across.T)
         place(2 * side + 1, 2 * side + 1, block(side, 2))
-        place(side, 2, block(side, 3))
-        place(side, 3, block(side, 4))
+        for col in (0, 1):
+            part_of = block(side, 3 + col)
+            place(side, 2 + col, part_of if side == 0 else part_of.T)
 
     gram = x_ref[:width, :width], x_ref[:width, width:], x_ref[width:, width:]
     squares = gram[0] * gram[0] + 2.0 * (gram[1] * gram[1]) + gram[2] * gram[2]
@@ -532,42 +511,48 @@
     scalars = [lax.axis_index("cols"), lax.axis_index("patch"), live_tiles[0]]
     info = jnp.stack(scalars).astype(jnp.int32)
 
-    cols = tile_cols.reshape(-1)
+    cols = tile_cols.T
 
     even, odd = masked_edges(after(info, cols), start)
     even_halo = exchange("even", even)
     low, high, even_blocks, odd_blocks = load_fields(after(info, even), start, blocks)
     odd_halo = exchange("odd", after(odd, low))
-    low_blocks, high_blocks = load_blocks(after(info, low), blocks)
-    stored = {"even": even_blocks, "odd": odd_blocks, "low": low_blocks, "high": high_blocks}
-    prev = dict.fromkeys(stored)
+    stored = {"even": even_blocks, "odd": odd_blocks}
+    prev = dict.fromkeys(("even", "odd", "low", "high"))
 
     def rows(name, *pieces, cost=SMALL):
         return tile_rows(name, info, cols, stored[name], pieces, prev[name], cost)
 
     for step in range(STEPS):
-        final = step == STEPS - 1
-        new_even = rows("even", after(even_halo, low_blocks), even, low, high)
-        if not final:
-            even_halo = exchange("even", new_even)
-        held = after(even, new_even)
-        new_low, new_high = rows("low", held, odd, low, high), rows("high", held, odd, low, high)
-        odd_halo = after(odd_halo, new_low, new_high)
+        first, final = step == 0, step == STEPS - 1
+        if final:
+            new_low = rows("low", even, odd, low, high)
+            new_high = rows("high", even, odd, low, high)
+            even_halo = after(even_halo, new_low, new_high)
+        new_even = rows("even", even_halo, even, low, high)
         if final:
             flat = [value.reshape(-1, width) for value in (new_even, new_low, new_high)]
             others = [sibling(value) for value in flat]
-            square = gram_square(flat)
-            odd_halo = after(odd_halo, square)
+        else:
+            even_halo = exchange("even", new_even)
+        odd_halo = after(odd_halo, new_even)
         new_odd = rows("odd", odd_halo, odd, low, high, cost=LARGE if final else SMALL)
+        if first:
+            stored["low"], stored["high"] = load_blocks(after(info, new_odd), blocks)
+            odd_halo = exchange("odd", after(new_odd, stored["low"]))
         if not final:
-            odd_halo = exchange("odd", new_odd)
+            held = after(even, new_odd)
+            new_low = rows("low", held, odd, low, high)
+            new_high = rows("high", held, odd, low, high)
+            if not first:
+                odd_halo = exchange("odd", after(new_odd, new_low, new_high))
         prev = {"even": even, "odd": odd, "low": low, "high": high}
         even, odd, low, high = new_even, new_odd, new_low, new_high
     last = odd.reshape(-1, width)
     other_last = sibling(last)
     others = [after(other, last) for other in others]
-    cross = gram_cross(info, flat, others)
-    mine = sum_over_patch(info, gram_share(info, last, other_last, square, cross))
+    share = gram_share(info, last, other_last, gram(flat, others))
+    mine = sum_over_patch(info, share)
     theirs = sibling(mine)
     total_rows = tiles * tile * count
     return rotate(info, mine, theirs, flat + [last], others + [other_last], total_rows)

time: 99.8 us -> 100 us (level)
  starting transfers between devices: 27.2 us -> 31.8 us
  waiting for transfers between devices: 20.5 us -> 18.7 us
  Pallas kernels: 49.9 us -> 48.5 us
    ppermute x6, starting transfers between devices: 12.9 us -> 16.6 us  [exchange(): return lax.ppermute(value, 'patch', pairs[name])]
    pallas_call x6 -> x5, Pallas kernels: 5.62 us -> 3.76 us  [gram_call(): pl.pallas_call(body, in_specs=[SMEM] * len(scalars) + [VMEM] * len(args),...]
    ppermute x6, waiting for transfers between devices: 4.21 us -> 3.05 us  [exchange(): return lax.ppermute(value, 'patch', pairs[name])]
  transfers between devices with their start and end apart: 20 -> 20, of which waited for: 11 -> 12; matrix products, arithmetic and copies ran while one was open for 0% -> 0% of each run, Pallas kernels for 30% -> 28%
where the time goes in v7:
time: 100 us
  Pallas kernels  48.5 us (48%)
  starting transfers between devices  31.8 us (32%)
  waiting for transfers between devices  18.7 us (19%)
  between operations  1.06 us (1%)
    pallas_call x12, Pallas kernels, tile_rows(): pl.pallas_call(functools.partial(rows_kernel, name, counts, tiles), in_sp...  19.8 us
    pallas_call x1, Pallas kernels, rotate(): pl.pallas_call(body, in_specs=[SMEM, VMEM, VMEM] + [ANY] * 8, out_specs=A...  17.2 us
    ppermute x6, starting transfers between devices, exchange(): return lax.ppermute(value, 'patch', pairs[name])  16.6 us
    ppermute x9, starting transfers between devices, from_others(): lax.ppermute(values[d], 'patch', [(i, i ^ d * stride) for i in range(coun...  13.9 us
    ppermute x9, waiting for transfers between devices, from_others(): lax.ppermute(values[d], 'patch', [(i, i ^ d * stride) for i in range(coun...  13.7 us
    pallas_call x2, Pallas kernels, load_call(): pl.pallas_call(body, in_specs=[SMEM] + [HBM] * len(args), out_specs=[VMEM...  6.1 us
    pallas_call x5, Pallas kernels, gram_call(): pl.pallas_call(body, in_specs=[SMEM] * len(scalars) + [VMEM] * len(args),...  3.76 us
    ppermute x6, waiting for transfers between devices, exchange(): return lax.ppermute(value, 'patch', pairs[name])  3.05 us
  transfers between devices with their start and end apart: 20, of which 12 were waited for; matrix products, arithmetic and copies ran while one was open for 0% of the time, Pallas kernels for 28%

profile of v7, /device:TPU:0, one launch (start us, length us, event | category | flops | bytes accessed | tf_op | source)
XLA Modules:
  0.0 100.1 jit_solution(16776620950688244500)
XLA Ops:
  0.7 0.1 pad_add_fusion.info
  0.7 1.6 %masked_edges.1 = (bf16[4,128,256]{2,1,0:T(8,128)(2,1)S(1)}, bf16[4,128,256]{2,1,0:T(8,128)(2,1)S(1)}) custom-call(s32[3]{0:T(128)S(1)} %pad_add_fusion.info, bf16[32,128,256]{2,1,0:T(8,128)(2,1)} %bitcast.32), custom_call_target="tpu_custom_call" | custom-call | flops 1000 | bytes 1000 | tf_op jit(solution)/shard_map/masked_edges/pallas_call | solution.py:113
  2.4 0.0 copy-start
  2.4 3.0 %collective-permute-start.1 = (bf16[4,128,256]{2,1,0:T(8,128)(2,1)S(1)}, bf16[4,128,256]{2,1,0:T(8,128)(2,1)S(1)}, u32[]{:S(2)}, u32[]{:S(2)}) collective-permute-start(bf16[4,128,256]{2,1,0:T(8,128)(2,1)S(1)} %get-tuple-element.45.refs_1_.refs_0_.refs_4_), channel_id=1, source_target_pairs={{0,1},{1,0},{2,3},{3,2},{4,5},{5,4},{6,7},{7,6},{8,9},{9,8},{10,11... | collective-permute-start | bytes 786440 | tf_op jit(solution)/shard_map/ppermute | solution.py:505
  5.4 2.7 %load_fields.1 = (bf16[12,128,256]{2,1,0:T(8,128)(2,1)S(1)}, bf16[12,128,256]{2,1,0:T(8,128)(2,1)S(1)}, bf16[4,8,128,128]{3,2,1,0:T(8,128)(2,1)S(1)}, bf16[4,8,128,128]{3,2,1,0:T(8,128)(2,1)S(1)}) custom-call(s32[3]{0:T(128)S(1)} %pad_add_fusion.info, bf16[32,128,256]{2,1,0:T(8,128)(2,1)} %bitcast.33, bf16[32,8,128,128]{3,2,1,0:T(8,128)(2,1)} %blocks_ref.3), custom_call_target="tpu_custom_call" | custom-call | flops 1000 | bytes 1000 | tf_op jit(solution)/shard_map/load_fields/pallas_call | solution.py:126
  8.1 0.7 collective-permute-start
  8.8 2.9 %collective-permute-done.1.refs_0_ = bf16[4,128,256]{2,1,0:T(8,128)(2,1)S(1)} collective-permute-done((bf16[4,128,256]{2,1,0:T(8,128)(2,1)S(1)}, bf16[4,128,256]{2,1,0:T(8,128)(2,1)S(1)}, u32[]{:S(2)}, u32[]{:S(2)}) %collective-permute-start.1) | collective-permute-done | bytes 262176 | tf_op jit(solution)/shard_map/ppermute | solution.py:505
  11.7 0.0 copy-done
  11.7 1.2 %rows_even.3.refs_1_.refs_0_.refs_4_ = bf16[4,128,256]{2,1,0:T(8,128)(2,1)S(1)} custom-call(s32[3]{0:T(128)S(1)} %pad_add_fusion.info, s32[8,32]{1,0:T(8,128)S(1)} %bitcast.17, bf16[4,128,256]{2,1,0:T(8,128)(2,1)S(1)} %collective-permute-done.1.refs_0_, bf16[4,128,256]{2,1,0:T(8,128)(2,1)S(1)} %get-tuple-element.45.refs_1_.refs_0_.refs_4_, ...), custom_call_target="tpu_custom_call" | custom-call | flops 1000 | bytes 1000 | tf_op jit(solution)/shard_map/rows_even/pallas_call | solution.py:205
  12.8 1.8 %collective-permute-start.3 = (bf16[4,128,256]{2,1,0:T(8,128)(2,1)S(1)}, bf16[4,128,256]{2,1,0:T(8,128)(2,1)S(1)}, u32[]{:S(2)}, u32[]{:S(2)}) collective-permute-start(bf16[4,128,256]{2,1,0:T(8,128)(2,1)S(1)} %rows_even.3.refs_1_.refs_0_.refs_4_), channel_id=1, source_target_pairs={{0,1},{1,0},{2,3},{3,2},{4,5},{5,4},{6,7},{7,6},{8,9},{9,8},{10,11... | collective-permute-start | bytes 786440 | tf_op jit(solution)/shard_map/ppermute | solution.py:505
  14.6 0.0 collective-permute-done.refs_0_
  14.6 1.2 %rows_odd.3.refs_1_.refs_4_ = bf16[4,128,256]{2,1,0:T(8,128)(2,1)S(1)} custom-call(s32[3]{0:T(128)S(1)} %pad_add_fusion.info, s32[8,32]{1,0:T(8,128)S(1)} %bitcast.18, bf16[4,128,256]{2,1,0:T(8,128)(2,1)S(1)} %collective-permute-done.refs_0_, bf16[4,128,256]{2,1,0:T(8,128)(2,1)S(1)} %get-tuple-element.37.refs_1_.refs_4_, ...), custom_call_target="tpu_custom_call" | custom-call | flops 1000 | bytes 1000 | tf_op jit(solution)/shard_map/rows_odd/pallas_call | solution.py:205
  15.8 3.4 %load_blocks.1 = (bf16[12,8,128,128]{3,2,1,0:T(8,128)(2,1)S(1)}, bf16[12,8,128,128]{3,2,1,0:T(8,128)(2,1)S(1)}) custom-call(s32[3]{0:T(128)S(1)} %pad_add_fusion.info, bf16[32,8,128,128]{3,2,1,0:T(8,128)(2,1)} %blocks_ref.3), custom_call_target="tpu_custom_call" | custom-call | flops 1000 | bytes 1000 | tf_op jit(solution)/shard_map/load_blocks/pallas_call | solution.py:126
  19.2 0.7 collective-permute-start.2
  19.9 2.1 %rows_low.3.refs_2_.refs_4_ = bf16[12,128,256]{2,1,0:T(8,128)(2,1)S(1)} custom-call(s32[3]{0:T(128)S(1)} %pad_add_fusion.info, s32[8,32]{1,0:T(8,128)S(1)} %bitcast.19, bf16[4,128,256]{2,1,0:T(8,128)(2,1)S(1)} %get-tuple-element.45.refs_1_.refs_0_.refs_4_, bf16[4,128,256]{2,1,0:T(8,128)(2,1)S(1)} %get-tuple-element.37.refs_1_.refs_4_, ...), custom_call_target="tpu_custom_call" | custom-call | flops 1000 | bytes 1000 | tf_op jit(solution)/shard_map/rows_low/pallas_call | solution.py:205
  22.0 2.1 %rows_high.3.refs_3_.refs_4_ = bf16[12,128,256]{2,1,0:T(8,128)(2,1)S(1)} custom-call(s32[3]{0:T(128)S(1)} %pad_add_fusion.info, s32[8,32]{1,0:T(8,128)S(1)} %bitcast.20, bf16[4,128,256]{2,1,0:T(8,128)(2,1)S(1)} %get-tuple-element.45.refs_1_.refs_0_.refs_4_, bf16[4,128,256]{2,1,0:T(8,128)(2,1)S(1)} %get-tuple-element.37.refs_1_.refs_4_, ...), custom_call_target="tpu_custom_call" | custom-call | flops 1000 | bytes 1000 | tf_op jit(solution)/shard_map/rows_high/pallas_call | solution.py:205
  24.2 0.1 collective-permute-done.3.refs_0_
  24.3 1.2 %rows_even.4.refs_0_.refs_1_ = bf16[4,128,256]{2,1,0:T(8,128)(2,1)S(1)} custom-call(s32[3]{0:T(128)S(1)} %pad_add_fusion.info, s32[8,32]{1,0:T(8,128)S(1)} %bitcast.21, bf16[4,128,256]{2,1,0:T(8,128)(2,1)S(1)} %collective-permute-done.3.refs_0_, bf16[4,128,256]{2,1,0:T(8,128)(2,1)S(1)} %rows_even.3.refs_1_.refs_0_.refs_4_, ...), custom_call_target="tpu_custom_call" | custom-call | flops 1000 | bytes 1000 | tf_op jit(solution)/shard_map/rows_even/pallas_call | solution.py:205
  25.4 9.6 %collective-permute-start.5 = (bf16[4,128,256]{2,1,0:T(8,128)(2,1)S(1)}, bf16[4,128,256]{2,1,0:T(8,128)(2,1)S(1)}, u32[]{:S(2)}, u32[]{:S(2)}) collective-permute-start(bf16[4,128,256]{2,1,0:T(8,128)(2,1)S(1)} %rows_even.4.refs_0_.refs_1_), channel_id=1, source_target_pairs={{0,1},{1,0},{2,3},{3,2},{4,5},{5,4},{6,7},{7,6},{8,9},{9,8},{10,11... | collective-permute-start | bytes 786440 | tf_op jit(solution)/shard_map/ppermute | solution.py:505
  35.0 0.0 collective-permute-done.2.refs_0_
  35.0 1.2 %rows_odd.4.refs_1_ = bf16[4,128,256]{2,1,0:T(8,128)(2,1)S(1)} custom-call(s32[3]{0:T(128)S(1)} %pad_add_fusion.info, s32[8,32]{1,0:T(8,128)S(1)} %bitcast.22, bf16[4,128,256]{2,1,0:T(8,128)(2,1)S(1)} %collective-permute-done.2.refs_0_, bf16[4,128,256]{2,1,0:T(8,128)(2,1)S(1)} %rows_odd.3.refs_1_.refs_4_, bf16[12,128,256]{2,1,0:T(8,128)(2,1)S(1)} %rows_low.3.refs_2_.refs_4_, ...), custom_call_target="tpu_custom_call" | custom-call | flops 1000 | bytes 1000 | tf_op jit(solution)/shard_map/rows_odd/pallas_call | solution.py:205
  36.2 2.1 %rows_high.4.refs_3_ = bf16[12,128,256]{2,1,0:T(8,128)(2,1)S(1)} custom-call(s32[3]{0:T(128)S(1)} %pad_add_fusion.info, s32[8,32]{1,0:T(8,128)S(1)} %bitcast.23, bf16[4,128,256]{2,1,0:T(8,128)(2,1)S(1)} %rows_even.3.refs_1_.refs_0_.refs_4_, bf16[4,128,256]{2,1,0:T(8,128)(2,1)S(1)} %rows_odd.3.refs_1_.refs_4_, ...), custom_call_target="tpu_custom_call" | custom-call | flops 1000 | bytes 1000 | tf_op jit(solution)/shard_map/rows_high/pallas_call | solution.py:205
  38.3 2.1 %rows_low.4.refs_2_ = bf16[12,128,256]{2,1,0:T(8,128)(2,1)S(1)} custom-call(s32[3]{0:T(128)S(1)} %pad_add_fusion.info, s32[8,32]{1,0:T(8,128)S(1)} %bitcast.24, bf16[4,128,256]{2,1,0:T(8,128)(2,1)S(1)} %rows_even.3.refs_1_.refs_0_.refs_4_, bf16[4,128,256]{2,1,0:T(8,128)(2,1)S(1)} %rows_odd.3.refs_1_.refs_4_, ...), custom_call_target="tpu_custom_call" | custom-call | flops 1000 | bytes 1000 | tf_op jit(solution)/shard_map/rows_low/pallas_call | solution.py:205
  40.5 0.9 collective-permute-start.4
  41.4 2.2 %rows_high.5 = bf16[12,128,256]{2,1,0:T(8,128)(2,1)S(1)} custom-call(s32[3]{0:T(128)S(1)} %pad_add_fusion.info, s32[8,32]{1,0:T(8,128)S(1)} %bitcast.25, bf16[4,128,256]{2,1,0:T(8,128)(2,1)S(1)} %rows_even.4.refs_0_.refs_1_, bf16[4,128,256]{2,1,0:T(8,128)(2,1)S(1)} %rows_odd.4.refs_1_, bf16[12,128,256]{2,1,0:T(8,128)(2,1)S(1)} %rows_low.4.refs_2_, ...), custom_call_target="tpu_custom_call" | custom-call | flops 1000 | bytes 1000 | tf_op jit(solution)/shard_map/rows_high/pallas_call | solution.py:205
  43.5 2.2 %rows_low.5 = bf16[12,128,256]{2,1,0:T(8,128)(2,1)S(1)} custom-call(s32[3]{0:T(128)S(1)} %pad_add_fusion.info, s32[8,32]{1,0:T(8,128)S(1)} %bitcast.26, bf16[4,128,256]{2,1,0:T(8,128)(2,1)S(1)} %rows_even.4.refs_0_.refs_1_, bf16[4,128,256]{2,1,0:T(8,128)(2,1)S(1)} %rows_odd.4.refs_1_, bf16[12,128,256]{2,1,0:T(8,128)(2,1)S(1)} %rows_low.4.refs_2_, ...), custom_call_target="tpu_custom_call" | custom-call | flops 1000 | bytes 1000 | tf_op jit(solution)/shard_map/rows_low/pallas_call | solution.py:205
  45.7 0.1 collective-permute-start.9
  45.8 0.5 collective-permute-start.8
  46.3 0.0 collective-permute-done.5.refs_0_
  46.3 1.2 %rows_even.5 = bf16[4,128,256]{2,1,0:T(8,128)(2,1)S(1)} custom-call(s32[3]{0:T(128)S(1)} %pad_add_fusion.info, s32[8,32]{1,0:T(8,128)S(1)} %bitcast.27, bf16[4,128,256]{2,1,0:T(8,128)(2,1)S(1)} %collective-permute-done.5.refs_0_, bf16[4,128,256]{2,1,0:T(8,128)(2,1)S(1)} %rows_even.4.refs_0_.refs_1_, bf16[12,128,256]{2,1,0:T(8,128)(2,1)S(1)} %rows_low.4.refs_2_, ...), custom_call_target="tpu_custom_call" | custom-call | flops 1000 | bytes 1000 | tf_op jit(solution)/shard_map/rows_even/pallas_call | solution.py:205
  47.4 0.0 collective-permute-done.4.refs_0_
  47.4 0.1 collective-permute-start.7
  47.6 1.2 %rows_odd.5 = bf16[4,128,256]{2,1,0:T(8,128)(2,1)S(1)} custom-call(s32[3]{0:T(128)S(1)} %pad_add_fusion.info, s32[8,32]{1,0:T(8,128)S(1)} %bitcast.28, bf16[4,128,256]{2,1,0:T(8,128)(2,1)S(1)} %collective-permute-done.4.refs_0_, bf16[4,128,256]{2,1,0:T(8,128)(2,1)S(1)} %rows_odd.4.refs_1_, bf16[12,128,256]{2,1,0:T(8,128)(2,1)S(1)} %rows_low.4.refs_2_, ...), custom_call_target="tpu_custom_call" | custom-call | flops 99999997952 | bytes 1000 | tf_op jit(solution)/shard_map/rows_odd/pallas_call | solution.py:205
  48.8 0.5 collective-permute-start.6
  49.2 0.3 collective-permute-done.7.refs_3_.refs_4_
  49.5 0.0 collective-permute-done.9.refs_5_.refs_6_
  49.5 0.0 collective-permute-done.8.refs_4_.refs_5_
  49.6 2.3 %gram.1.start_ref = f32[256,512]{1,0:T(8,128)S(1)} custom-call(bf16[512,256]{1,0:T(8,128)(2,1)S(1)} %bitcast.15, bf16[1536,256]{1,0:T(8,128)(2,1)S(1)} %bitcast.12, bf16[1536,256]{1,0:T(8,128)(2,1)S(1)} %bitcast.9, bf16[512,256]{1,0:T(8,128)(2,1)S(1)} %collective-permute-done.7.refs_3_.refs_4_, bf16[1536,256]{1,0:T(8,128)(2,1)S(1)} %collective-permute-done.8.refs_4_.refs_5_, ...), custom_call_target="tpu_custom_call" | custom-call | flops 1000 | bytes 1000 | tf_op jit(solution)/shard_map/gram/pallas_call | solution.py:258
  51.8 0.0 collective-permute-done.6.other_ref.refs_7_
  51.8 0.9 gram_share.1
  52.7 4.0 %collective-permute-start.10 = (f32[160,128]{1,0:T(8,128)S(1)}, f32[160,128]{1,0:T(8,128)S(1)}, u32[]{:S(2)}, u32[]{:S(2)}) collective-permute-start(f32[160,128]{1,0:T(8,128)S(1)} %get-tuple-element.56), channel_id=1, source_target_pairs={{0,1},{1,0},{2,3},{3,2},{4,5},{5,4},{6,7},{7,6},{8,9},{9,8},{10,11... | collective-permute-start | bytes 245768 | tf_op jit(solution)/shard_map/ppermute | solution.py:307
  56.8 1.9 %collective-permute-start.11 = (f32[160,128]{1,0:T(8,128)S(1)}, f32[160,128]{1,0:T(8,128)S(1)}, u32[]{:S(2)}, u32[]{:S(2)}) collective-permute-start(f32[160,128]{1,0:T(8,128)S(1)} %get-tuple-element.57), channel_id=1, source_target_pairs={{0,2},{1,3},{2,0},{3,1},{4,6},{5,7},{6,4},{7,5},{8,10},{9,11},{10,... | collective-permute-start | bytes 245768 | tf_op jit(solution)/shard_map/ppermute | solution.py:307
  58.7 0.0 collective-permute-start.12
  58.7 0.8 collective-permute-done.10.b
  59.5 2.7 %collective-permute-done.11.c = f32[160,128]{1,0:T(8,128)S(1)} collective-permute-done((f32[160,128]{1,0:T(8,128)S(1)}, f32[160,128]{1,0:T(8,128)S(1)}, u32[]{:S(2)}, u32[]{:S(2)}) %collective-permute-start.11) | collective-permute-done | bytes 81952 | tf_op jit(solution)/shard_map/ppermute | solution.py:307
  62.2 1.8 %collective-permute-done.12.d = f32[160,128]{1,0:T(8,128)S(1)} collective-permute-done((f32[160,128]{1,0:T(8,128)S(1)}, f32[160,128]{1,0:T(8,128)S(1)}, u32[]{:S(2)}, u32[]{:S(2)}) %collective-permute-start.12) | collective-permute-done | bytes 81952 | tf_op jit(solution)/shard_map/ppermute | solution.py:307
  64.0 1.6 %collective-permute-start.15 = (f32[160,128]{1,0:T(8,128)S(1)}, f32[160,128]{1,0:T(8,128)S(1)}, u32[]{:S(2)}, u32[]{:S(2)}) collective-permute-start(f32[160,128]{1,0:T(8,128)S(1)} %add_four.2.a), channel_id=1, source_target_pairs={{0,12},{1,13},{2,14},{3,15},{4,8},{5,9},{6,10},{7,11},{8,4},{9,5},... | collective-permute-start | bytes 245768 | tf_op jit(solution)/shard_map/ppermute | solution.py:307
  65.7 1.4 %collective-permute-start.14 = (f32[160,128]{1,0:T(8,128)S(1)}, f32[160,128]{1,0:T(8,128)S(1)}, u32[]{:S(2)}, u32[]{:S(2)}) collective-permute-start(f32[160,128]{1,0:T(8,128)S(1)} %add_four.2.a), channel_id=1, source_target_pairs={{0,8},{1,9},{2,10},{3,11},{4,12},{5,13},{6,14},{7,15},{8,0},{9,1},... | collective-permute-start | bytes 245768 | tf_op jit(solution)/shard_map/ppermute | solution.py:307
  67.1 1.4 %collective-permute-start.13 = (f32[160,128]{1,0:T(8,128)S(1)}, f32[160,128]{1,0:T(8,128)S(1)}, u32[]{:S(2)}, u32[]{:S(2)}) collective-permute-start(f32[160,128]{1,0:T(8,128)S(1)} %add_four.2.a), channel_id=1, source_target_pairs={{0,4},{1,5},{2,6},{3,7},{4,0},{5,1},{6,2},{7,3},{8,12},{9,13},{10,... | collective-permute-start | bytes 245768 | tf_op jit(solution)/shard_map/ppermute | solution.py:307
  68.5 2.4 %collective-permute-done.15.d = f32[160,128]{1,0:T(8,128)S(1)} collective-permute-done((f32[160,128]{1,0:T(8,128)S(1)}, f32[160,128]{1,0:T(8,128)S(1)}, u32[]{:S(2)}, u32[]{:S(2)}) %collective-permute-start.15) | collective-permute-done | bytes 81952 | tf_op jit(solution)/shard_map/ppermute | solution.py:307
  70.8 2.2 %collective-permute-done.14.c = f32[160,128]{1,0:T(8,128)S(1)} collective-permute-done((f32[160,128]{1,0:T(8,128)S(1)}, f32[160,128]{1,0:T(8,128)S(1)}, u32[]{:S(2)}, u32[]{:S(2)}) %collective-permute-start.14) | collective-permute-done | bytes 81952 | tf_op jit(solution)/shard_map/ppermute | solution.py:307
  73.1 0.0 collective-permute-done.13.b
  73.1 1.0 %collective-permute-start.18 = (f32[160,128]{1,0:T(8,128)S(1)}, f32[160,128]{1,0:T(8,128)S(1)}, u32[]{:S(2)}, u32[]{:S(2)}) collective-permute-start(f32[160,128]{1,0:T(8,128)S(1)} %add_four.3.refs_0_), channel_id=1, source_target_pairs={{0,3},{1,2},{2,1},{3,0},{4,7},{5,6},{6,5},{7,4},{8,11},{9,10},{10,... | collective-permute-start | bytes 245768 | tf_op jit(solution)/shard_map/ppermute | solution.py:307
  74.1 1.9 %collective-permute-start.17 = (f32[160,128]{1,0:T(8,128)S(1)}, f32[160,128]{1,0:T(8,128)S(1)}, u32[]{:S(2)}, u32[]{:S(2)}) collective-permute-start(f32[160,128]{1,0:T(8,128)S(1)} %add_four.3.refs_0_), channel_id=1, source_target_pairs={{0,2},{1,3},{2,0},{3,1},{4,6},{5,7},{6,4},{7,5},{8,10},{9,11},{10,... | collective-permute-start | bytes 245768 | tf_op jit(solution)/shard_map/ppermute | solution.py:307
  76.0 0.6 collective-permute-start.16
  76.7 2.1 %collective-permute-done.18.refs_3_ = f32[160,128]{1,0:T(8,128)S(1)} collective-permute-done((f32[160,128]{1,0:T(8,128)S(1)}, f32[160,128]{1,0:T(8,128)S(1)}, u32[]{:S(2)}, u32[]{:S(2)}) %collective-permute-start.18) | collective-permute-done | bytes 81952 | tf_op jit(solution)/shard_map/ppermute | solution.py:307
  78.8 0.6 collective-permute-done.17.refs_2_
  79.4 1.1 %collective-permute-done.16.refs_1_ = f32[160,128]{1,0:T(8,128)S(1)} collective-permute-done((f32[160,128]{1,0:T(8,128)S(1)}, f32[160,128]{1,0:T(8,128)S(1)}, u32[]{:S(2)}, u32[]{:S(2)}) %collective-permute-start.16) | collective-permute-done | bytes 81952 | tf_op jit(solution)/shard_map/ppermute | solution.py:307
  80.5 0.6 join.1.mine
  81.0 0.1 collective-permute-start.19
  81.1 1.6 %collective-permute-done.19.theirs = f32[640,128]{1,0:T(8,128)S(1)} collective-permute-done((f32[640,128]{1,0:T(8,128)S(1)}, f32[640,128]{1,0:T(8,128)S(1)}, u32[]{:S(2)}, u32[]{:S(2)}) %collective-permute-start.19) | collective-permute-done | bytes 327712 | tf_op jit(solution)/shard_map/ppermute | solution.py:508
  82.7 17.2 %rotate.1 = bf16[4096,256]{1,0:T(8,128)(2,1)} custom-call(s32[3]{0:T(128)S(1)} %pad_add_fusion.info, f32[640,128]{1,0:T(8,128)S(1)} %join.1.mine, f32[640,128]{1,0:T(8,128)S(1)} %collective-permute-done.19.theirs, bf16[512,256]{1,0:T(8,128)(2,1)S(1)} %bitcast.16, bf16[1536,256]{1,0:T(8,128)(2,1)S(1)} %bitcast.13, bf16[1536,256]{1,0:T(8,128)(2,1)S(1)} %bitcast.10, ...), custom_call_target="tpu_custom_call" | custom-call | flops 17985175552 | bytes 6291456 | tf_op jit(solution)/shard_map/rotate/pallas_call | solution.py:467
  (2 shorter events, 0.0 us)
Async XLA Ops:
  2.4 9.3 %copy-start = (s32[32,8]{0,1:T(8,128)S(1)}, s32[32,8]{0,1:T(8,128)}, u32[]{:S(2)}) copy-start(s32[32,8]{0,1:T(8,128)} %param.6) | copy-start | bytes 3076
  2.4 9.3 %collective-permute-start.1 = (bf16[4,128,256]{2,1,0:T(8,128)(2,1)S(1)}, bf16[4,128,256]{2,1,0:T(8,128)(2,1)S(1)}, u32[]{:S(2)}, u32[]{:S(2)}) collective-permute-start(bf16[4,128,256]{2,1,0:T(8,128)(2,1)S(1)} %get-tuple-element.45.refs_1_.refs_0_.refs_4_), channel_id=1, source_target_pairs={{0,1},{1,0},{2,3},{3,2},{4,5},{5,4},{6,7},{7,6},{8,9},{9,8},{10,11... | collective-permute-start | bytes 786440 | tf_op jit(solution)/shard_map/ppermute | solution.py:505
  8.1 6.6 %collective-permute-start = (bf16[4,128,256]{2,1,0:T(8,128)(2,1)S(1)}, bf16[4,128,256]{2,1,0:T(8,128)(2,1)S(1)}, u32[]{:S(2)}, u32[]{:S(2)}) collective-permute-start(bf16[4,128,256]{2,1,0:T(8,128)(2,1)S(1)} %get-tuple-element.37.refs_1_.refs_4_), channel_id=1, source_target_pairs={{1,2},{2,1},{3,4},{4,3},{5,6},{6,5},{7,8},{8,7},{9,10},{10,9},{11,... | collective-permute-start | bytes 786440 | tf_op jit(solution)/shard_map/ppermute | solution.py:505
  12.8 11.4 %collective-permute-start.3 = (bf16[4,128,256]{2,1,0:T(8,128)(2,1)S(1)}, bf16[4,128,256]{2,1,0:T(8,128)(2,1)S(1)}, u32[]{:S(2)}, u32[]{:S(2)}) collective-permute-start(bf16[4,128,256]{2,1,0:T(8,128)(2,1)S(1)} %rows_even.3.refs_1_.refs_0_.refs_4_), channel_id=1, source_target_pairs={{0,1},{1,0},{2,3},{3,2},{4,5},{5,4},{6,7},{7,6},{8,9},{9,8},{10,11... | collective-permute-start | bytes 786440 | tf_op jit(solution)/shard_map/ppermute | solution.py:505
  19.2 15.8 %collective-permute-start.2 = (bf16[4,128,256]{2,1,0:T(8,128)(2,1)S(1)}, bf16[4,128,256]{2,1,0:T(8,128)(2,1)S(1)}, u32[]{:S(2)}, u32[]{:S(2)}) collective-permute-start(bf16[4,128,256]{2,1,0:T(8,128)(2,1)S(1)} %rows_odd.3.refs_1_.refs_4_), channel_id=1, source_target_pairs={{1,2},{2,1},{3,4},{4,3},{5,6},{6,5},{7,8},{8,7},{9,10},{10,9},{11,... | collective-permute-start | bytes 786440 | tf_op jit(solution)/shard_map/ppermute | solution.py:505
  25.4 20.8 %collective-permute-start.5 = (bf16[4,128,256]{2,1,0:T(8,128)(2,1)S(1)}, bf16[4,128,256]{2,1,0:T(8,128)(2,1)S(1)}, u32[]{:S(2)}, u32[]{:S(2)}) collective-permute-start(bf16[4,128,256]{2,1,0:T(8,128)(2,1)S(1)} %rows_even.4.refs_0_.refs_1_), channel_id=1, source_target_pairs={{0,1},{1,0},{2,3},{3,2},{4,5},{5,4},{6,7},{7,6},{8,9},{9,8},{10,11... | collective-permute-start | bytes 786440 | tf_op jit(solution)/shard_map/ppermute | solution.py:505
  40.5 6.9 %collective-permute-start.4 = (bf16[4,128,256]{2,1,0:T(8,128)(2,1)S(1)}, bf16[4,128,256]{2,1,0:T(8,128)(2,1)S(1)}, u32[]{:S(2)}, u32[]{:S(2)}) collective-permute-start(bf16[4,128,256]{2,1,0:T(8,128)(2,1)S(1)} %rows_odd.4.refs_1_), channel_id=1, source_target_pairs={{1,2},{2,1},{3,4},{4,3},{5,6},{6,5},{7,8},{8,7},{9,10},{10,9},{11,... | collective-permute-start | bytes 786440 | tf_op jit(solution)/shard_map/ppermute | solution.py:505
  45.7 3.9 %collective-permute-start.9 = (bf16[1536,256]{1,0:T(8,128)(2,1)S(1)}, bf16[1536,256]{1,0:T(8,128)(2,1)S(1)}, u32[]{:S(2)}, u32[]{:S(2)}) collective-permute-start(bf16[1536,256]{1,0:T(8,128)(2,1)S(1)} %bitcast.8), channel_id=1, source_target_pairs={{0,16},{16,0},{1,17},{17,1},{2,18},{18,2},{3,19},{19,3},{4,20},{20... | collective-permute-start | bytes 2359304 | tf_op jit(solution)/shard_map/ppermute | solution.py:508
  45.8 3.8 %collective-permute-start.8 = (bf16[1536,256]{1,0:T(8,128)(2,1)S(1)}, bf16[1536,256]{1,0:T(8,128)(2,1)S(1)}, u32[]{:S(2)}, u32[]{:S(2)}) collective-permute-start(bf16[1536,256]{1,0:T(8,128)(2,1)S(1)} %bitcast.11), channel_id=1, source_target_pairs={{0,16},{16,0},{1,17},{17,1},{2,18},{18,2},{3,19},{19,3},{4,20},{20... | collective-permute-start | bytes 2359304 | tf_op jit(solution)/shard_map/ppermute | solution.py:508
  47.4 2.1 %collective-permute-start.7 = (bf16[512,256]{1,0:T(8,128)(2,1)S(1)}, bf16[512,256]{1,0:T(8,128)(2,1)S(1)}, u32[]{:S(2)}, u32[]{:S(2)}) collective-permute-start(bf16[512,256]{1,0:T(8,128)(2,1)S(1)} %bitcast.14), channel_id=1, source_target_pairs={{0,16},{16,0},{1,17},{17,1},{2,18},{18,2},{3,19},{19,3},{4,20},{20... | collective-permute-start | bytes 786440 | tf_op jit(solution)/shard_map/ppermute | solution.py:508
  48.8 3.1 %collective-permute-start.6 = (bf16[512,256]{1,0:T(8,128)(2,1)S(1)}, bf16[512,256]{1,0:T(8,128)(2,1)S(1)}, u32[]{:S(2)}, u32[]{:S(2)}) collective-permute-start(bf16[512,256]{1,0:T(8,128)(2,1)S(1)} %bitcast.29), channel_id=1, source_target_pairs={{0,16},{16,0},{1,17},{17,1},{2,18},{18,2},{3,19},{19,3},{4,20},{20... | collective-permute-start | bytes 786440 | tf_op jit(solution)/shard_map/ppermute | solution.py:508
  52.7 6.8 %collective-permute-start.10 = (f32[160,128]{1,0:T(8,128)S(1)}, f32[160,128]{1,0:T(8,128)S(1)}, u32[]{:S(2)}, u32[]{:S(2)}) collective-permute-start(f32[160,128]{1,0:T(8,128)S(1)} %get-tuple-element.56), channel_id=1, source_target_pairs={{0,1},{1,0},{2,3},{3,2},{4,5},{5,4},{6,7},{7,6},{8,9},{9,8},{10,11... | collective-permute-start | bytes 245768 | tf_op jit(solution)/shard_map/ppermute | solution.py:307
  56.8 5.4 %collective-permute-start.11 = (f32[160,128]{1,0:T(8,128)S(1)}, f32[160,128]{1,0:T(8,128)S(1)}, u32[]{:S(2)}, u32[]{:S(2)}) collective-permute-start(f32[160,128]{1,0:T(8,128)S(1)} %get-tuple-element.57), channel_id=1, source_target_pairs={{0,2},{1,3},{2,0},{3,1},{4,6},{5,7},{6,4},{7,5},{8,10},{9,11},{10,... | collective-permute-start | bytes 245768 | tf_op jit(solution)/shard_map/ppermute | solution.py:307
  58.7 5.3 %collective-permute-start.12 = (f32[160,128]{1,0:T(8,128)S(1)}, f32[160,128]{1,0:T(8,128)S(1)}, u32[]{:S(2)}, u32[]{:S(2)}) collective-permute-start(f32[160,128]{1,0:T(8,128)S(1)} %get-tuple-element.58), channel_id=1, source_target_pairs={{0,3},{1,2},{2,1},{3,0},{4,7},{5,6},{6,5},{7,4},{8,11},{9,10},{10,... | collective-permute-start | bytes 245768 | tf_op jit(solution)/shard_map/ppermute | solution.py:307
  64.0 6.8 %collective-permute-start.15 = (f32[160,128]{1,0:T(8,128)S(1)}, f32[160,128]{1,0:T(8,128)S(1)}, u32[]{:S(2)}, u32[]{:S(2)}) collective-permute-start(f32[160,128]{1,0:T(8,128)S(1)} %add_four.2.a), channel_id=1, source_target_pairs={{0,12},{1,13},{2,14},{3,15},{4,8},{5,9},{6,10},{7,11},{8,4},{9,5},... | collective-permute-start | bytes 245768 | tf_op jit(solution)/shard_map/ppermute | solution.py:307
  65.7 7.4 %collective-permute-start.14 = (f32[160,128]{1,0:T(8,128)S(1)}, f32[160,128]{1,0:T(8,128)S(1)}, u32[]{:S(2)}, u32[]{:S(2)}) collective-permute-start(f32[160,128]{1,0:T(8,128)S(1)} %add_four.2.a), channel_id=1, source_target_pairs={{0,8},{1,9},{2,10},{3,11},{4,12},{5,13},{6,14},{7,15},{8,0},{9,1},... | collective-permute-start | bytes 245768 | tf_op jit(solution)/shard_map/ppermute | solution.py:307
  67.1 6.0 %collective-permute-start.13 = (f32[160,128]{1,0:T(8,128)S(1)}, f32[160,128]{1,0:T(8,128)S(1)}, u32[]{:S(2)}, u32[]{:S(2)}) collective-permute-start(f32[160,128]{1,0:T(8,128)S(1)} %add_four.2.a), channel_id=1, source_target_pairs={{0,4},{1,5},{2,6},{3,7},{4,0},{5,1},{6,2},{7,3},{8,12},{9,13},{10,... | collective-permute-start | bytes 245768 | tf_op jit(solution)/shard_map/ppermute | solution.py:307
  73.1 5.7 %collective-permute-start.18 = (f32[160,128]{1,0:T(8,128)S(1)}, f32[160,128]{1,0:T(8,128)S(1)}, u32[]{:S(2)}, u32[]{:S(2)}) collective-permute-start(f32[160,128]{1,0:T(8,128)S(1)} %add_four.3.refs_0_), channel_id=1, source_target_pairs={{0,3},{1,2},{2,1},{3,0},{4,7},{5,6},{6,5},{7,4},{8,11},{9,10},{10,... | collective-permute-start | bytes 245768 | tf_op jit(solution)/shard_map/ppermute | solution.py:307
  74.1 5.3 %collective-permute-start.17 = (f32[160,128]{1,0:T(8,128)S(1)}, f32[160,128]{1,0:T(8,128)S(1)}, u32[]{:S(2)}, u32[]{:S(2)}) collective-permute-start(f32[160,128]{1,0:T(8,128)S(1)} %add_four.3.refs_0_), channel_id=1, source_target_pairs={{0,2},{1,3},{2,0},{3,1},{4,6},{5,7},{6,4},{7,5},{8,10},{9,11},{10,... | collective-permute-start | bytes 245768 | tf_op jit(solution)/shard_map/ppermute | solution.py:307
  76.0 4.4 %collective-permute-start.16 = (f32[160,128]{1,0:T(8,128)S(1)}, f32[160,128]{1,0:T(8,128)S(1)}, u32[]{:S(2)}, u32[]{:S(2)}) collective-permute-start(f32[160,128]{1,0:T(8,128)S(1)} %add_four.3.refs_0_), channel_id=1, source_target_pairs={{0,1},{1,0},{2,3},{3,2},{4,5},{5,4},{6,7},{7,6},{8,9},{9,8},{10,11... | collective-permute-start | bytes 245768 | tf_op jit(solution)/shard_map/ppermute | solution.py:307
  81.0 1.7 %collective-permute-start.19 = (f32[640,128]{1,0:T(8,128)S(1)}, f32[640,128]{1,0:T(8,128)S(1)}, u32[]{:S(2)}, u32[]{:S(2)}) collective-permute-start(f32[640,128]{1,0:T(8,128)S(1)} %join.1.mine), channel_id=1, source_target_pairs={{0,16},{16,0},{1,17},{17,1},{2,18},{18,2},{3,19},{19,3},{4,20},{20... | collective-permute-start | bytes 983048 | tf_op jit(solution)/shard_map/ppermute | solution.py:508

commit v8 on v7

v8 whole, which is shorter than its diff:
```python
import functools

import jax
import jax.numpy as jnp
from jax import lax
from jax.experimental import pallas as pl
from jax.experimental.pallas import tpu as pltpu
from jax.sharding import PartitionSpec as P

HALO_T = 4
STEPS = 3
ITERS = 8
WAYS = 4
LOAD_CUTS = 4
GROUP = 8

SMALL = pl.CostEstimate(flops=1000, bytes_accessed=1000, transcendentals=0)
LARGE = pl.CostEstimate(flops=10**11, bytes_accessed=1000, transcendentals=0)
SMALL_VMEM = pltpu.CompilerParams(vmem_limit_bytes=8 * 1024 * 1024)
ANY = pl.BlockSpec(memory_space=pl.ANY)
HBM = pl.BlockSpec(memory_space=pltpu.HBM)
VMEM = pl.BlockSpec(memory_space=pltpu.VMEM)
EDGES_MB, FIELDS_MB, BLOCKS_MB = 53, 50, 44
SMEM = pl.BlockSpec(memory_space=pltpu.SMEM)
F32, BF16 = jnp.float32, jnp.bfloat16


def dot(a, b):
    return jnp.dot(a, b, preferred_element_type=F32)


def tile_row(blocks, listed, field):
    wide = jnp.concatenate([blocks(n) for n in range(len(listed))], axis=1)
    tall = jnp.concatenate([field(tile) for tile in listed], axis=0)
    return dot(wide, tall)


def finish(acc, prev, alive):
    value = acc if prev is None else 2.0 * acc - prev.astype(F32)
    return jnp.where(alive, value, 0.0).astype(BF16)


def at_end(name):
    odd = lax.axis_index("patch") % 2
    return 1 - odd if name == "even" else odd


def live_count(table):
    return table[table.shape[0] - 1, 0]


def edges_kernel(table, whole_ref, even_ref, odd_ref, sem):
    edge, tiles = HALO_T, whole_ref.shape[0]
    outs = {"even": even_ref, "odd": odd_ref}
    firsts = {name: at_end(name) * (tiles - edge) for name in outs}
    load([(whole_ref, firsts[name], outs[name]) for name in outs], sem)
    for name in outs:
        clear_dead(outs[name], firsts[name], live_count(table))


def clear_dead(ref, first, live):
    def clear(index, carry):
        ref[index] = jnp.zeros(ref.shape[1:], BF16)
        return carry

    count = ref.shape[0]
    lax.fori_loop(jnp.clip(live - first, 0, count), count, clear, 0)


def load(moves, sem):
    copies = []
    for source, first, target in moves:
        count = target.shape[0] // LOAD_CUTS
        for cut in range(LOAD_CUTS):
            copies.append(
                pltpu.make_async_copy(
                    source.at[pl.ds(first + cut * count, count)],
                    target.at[pl.ds(cut * count, count)],
                    sem.at[len(copies)],
                )
            )
    for copy in copies:
        copy.start()
    for copy in copies:
        copy.wait()


def fields_kernel(table, whole_ref, blocks_ref, inner_ref, even_blocks, odd_blocks, sem):
    last = whole_ref.shape[0] - HALO_T
    moves = [
        (blocks_ref, at_end("even") * last, even_blocks),
        (blocks_ref, at_end("odd") * last, odd_blocks),
        (whole_ref, HALO_T, inner_ref),
    ]
    load(moves, sem)
    clear_dead(inner_ref, HALO_T, live_count(table))


def blocks_kernel(blocks_ref, inner_blocks, sem):
    load([(blocks_ref, HALO_T, inner_blocks)], sem)


def load_call(body, name, args, shapes, megabytes, table=()):
    return pl.pallas_call(
        body,
        in_specs=[SMEM] * len(table) + [HBM] * len(args),
        out_specs=[VMEM] * len(shapes),
        out_shape=shapes,
        scratch_shapes=[pltpu.SemaphoreType.DMA((len(shapes) * LOAD_CUTS,))],
        compiler_params=pltpu.CompilerParams(vmem_limit_bytes=megabytes * 1024 * 1024),
        cost_estimate=SMALL,
        name=name,
    )(*table, *args)


def masked_edges(table, start):
    shapes = [jax.ShapeDtypeStruct((HALO_T,) + start.shape[1:], BF16)] * 2
    return load_call(edges_kernel, "masked_edges", [start], shapes, EDGES_MB, [table])


def load_fields(table, start, blocks):
    inner = start.shape[0] - 2 * HALO_T
    shapes = [jax.ShapeDtypeStruct((inner,) + start.shape[1:], BF16)]
    shapes += [jax.ShapeDtypeStruct((HALO_T,) + blocks.shape[1:], blocks.dtype)] * 2
    return load_call(fields_kernel, "load_fields", [start, blocks], shapes, FIELDS_MB, [table])


def load_blocks(blocks):
    inner = blocks.shape[0] - 2 * HALO_T
    shapes = [jax.ShapeDtypeStruct((inner,) + blocks.shape[1:], blocks.dtype)]
    return load_call(blocks_kernel, "load_blocks", [blocks], shapes, BLOCKS_MB)[0]


def layout(name, tiles):
    edge, last = HALO_T, tiles - HALO_T
    if name == "inner":
        ends = [at_end(which) for which in ("even", "odd")]
        pieces = [(i, 0, edge, end * last) for i, end in enumerate(ends)]
        return edge, 0, pieces + [(2, 0, tiles - 2 * edge, edge)]
    end = at_end(name)
    pieces = [
        (0, 0, edge, 2 * edge * end), (1, 0, edge, edge), (2, 0, edge, (2 + end) * edge),
        (2, tiles - 3 * edge, edge, 3 * edge * (1 - end)),
    ]
    return end * last, end * last - edge, pieces


def rows_kernel(name, table_ref, *refs):
    sources, (out_ref, held, table, sem) = refs[:3], refs[-4:]
    blocks_ref = refs[-5]
    prev_ref = refs[3] if len(refs) == 9 else None
    fetch = pltpu.make_async_copy(table_ref, table, sem)
    fetch.start()
    nnz, tiles = blocks_ref.shape[1], table.shape[1]
    first, base, pieces = layout(name, tiles)
    for i, begin, count, slot in pieces:
        held[pl.ds(slot, count)] = sources[i][pl.ds(begin, count)]
    fetch.wait()
    live = live_count(table)
    shift = lax.axis_index("patch") * tiles + base
    rows = out_ref.shape[0]
    together = min(GROUP, rows)

    def group(index, carry):
        for r in range(together):
            row = index * together + r
            listed = [table[n, first + row] - shift for n in range(nnz)]
            acc = tile_row(lambda n: blocks_ref[row, n], listed, lambda c: held[c])
            prev = None if prev_ref is None else prev_ref[row]
            out_ref[row] = finish(acc, prev, first + row < live)
        return carry

    lax.fori_loop(0, rows // together, group, 0)


def tile_rows(name, table, blocks, sources, prev, cost):
    rows, _, tile, _ = blocks.shape
    width = sources[0].shape[-1]
    window = table.shape[1] if name == "inner" else 4 * HALO_T
    args = [table] + list(sources) + ([] if prev is None else [prev]) + [blocks]
    return pl.pallas_call(
        functools.partial(rows_kernel, name),
        in_specs=[VMEM] * len(args),
        out_specs=VMEM,
        out_shape=jax.ShapeDtypeStruct((rows, tile, width), BF16),
        scratch_shapes=[
            pltpu.VMEM((window, tile, width), BF16),
            pltpu.SMEM(table.shape, jnp.int32),
            pltpu.SemaphoreType.DMA,
        ],
        compiler_params=SMALL_VMEM,
        cost_estimate=cost,
        name="rows_" + name,
    )(*args)


ACROSS = (((0,), (0,)), ((), ()))


def add_gram(chunk, own_ref, other_ref, total):
    def add(index, carry):
        rows = pl.ds(pl.multiple_of(index * chunk, chunk), chunk)
        own = own_ref[rows, :]
        both = jnp.concatenate([own, other_ref[rows, :]], axis=1)
        total[...] += lax.dot_general(own, both, ACROSS, preferred_element_type=F32)
        return carry

    lax.fori_loop(0, own_ref.shape[0] // chunk, add, 0)


def gram_kernel(chunk, *refs):
    count = len(refs) // 2
    refs[-1][...] = jnp.zeros(refs[-1].shape, F32)
    for own_ref, other_ref in zip(refs[:count], refs[count:-1]):
        add_gram(chunk, own_ref, other_ref, refs[-1])


def share_kernel(chunk, own_ref, other_ref, start_ref, *refs):
    outs, (total, share) = refs[:WAYS], refs[WAYS:]
    total[...] = start_ref[...]
    add_gram(chunk, own_ref, other_ref, total)
    width = total.shape[0]
    half = width // 2
    own, other = total[:, :width], total[:, width:]
    first_core = lax.axis_index("cols") == 0
    second = jnp.where(first_core, other[:half, :half], other[:half, half:])
    third = jnp.where(first_core, other[:half, half:], other[half:, half:])
    blocks = [own[:half, :half], own[:half, half:], own[half:, half:], second, third]
    for i, block in enumerate(blocks):
        share[pl.ds(i * half, half), :] = block
    quarter = lax.axis_index("patch") % WAYS
    for d, out in enumerate(outs):
        rows = out.shape[0]
        out[...] = share[pl.ds(pl.multiple_of((quarter ^ d) * rows, 8), rows), :]


def gram_call(body, name, args, shape, scratch=(), outs=0):
    out_shape = jax.ShapeDtypeStruct(shape, F32)
    return pl.pallas_call(
        body,
        in_specs=[VMEM] * len(args),
        out_specs=[VMEM] * outs if outs else VMEM,
        out_shape=[out_shape] * outs if outs else out_shape,
        scratch_shapes=scratch,
        compiler_params=SMALL_VMEM,
        cost_estimate=SMALL,
        name=name,
    )(*args)


def gram(owns, others):
    chunk, width = min(own.shape[0] for own in owns), owns[0].shape[1]
    body = functools.partial(gram_kernel, chunk)
    return gram_call(body, "gram", owns + others, (width, 2 * width))


def gram_share(own, other, start):
    rows, width = own.shape
    half = width // 2
    body = functools.partial(share_kernel, rows)
    scratch = [pltpu.VMEM((width, 2 * width), F32), pltpu.VMEM((5 * half, half), F32)]
    shape = (5 * half // WAYS, half)
    args = [own, other, start]
    return gram_call(body, "gram_share", args, shape, scratch, outs=WAYS)


def add_kernel(a, b, c, d, out):
    out[...] = (a[...] + b[...]) + (c[...] + d[...])


def join_kernel(*refs):
    parts, out = refs[:-1], refs[-1]
    rows = parts[0].shape[0]
    quarter = lax.axis_index("patch") % WAYS
    for d, part in enumerate(parts):
        out[pl.ds(pl.multiple_of((quarter ^ d) * rows, 8), rows), :] = part[...]


def sum_over_patch(parts):
    count = lax.axis_size("patch")
    rows, columns = parts[0].shape

    def add_four(values):
        return gram_call(add_kernel, "add_four", values, (rows, columns))

    def from_others(values, stride=1):
        return [
            lax.ppermute(values[d], "patch", [(i, i ^ (d * stride)) for i in range(count)])
            for d in range(1, WAYS)
        ]

    total = add_four([parts[0]] + from_others(parts))
    stride = WAYS
    while stride < count:
        total = add_four([total] + from_others([total] * WAYS, stride))
        stride *= WAYS
    quarters = [total] + from_others([total] * WAYS)
    return gram_call(join_kernel, "join", quarters, (WAYS * rows, columns))


def split(value):
    high = value.astype(BF16)
    return high, (value - high.astype(F32)).astype(BF16)


def put(pair, blocks, right=False):
    width = blocks[0].shape[0]
    places = [(0, 0), (0, 1), (1, 1)]
    if right:
        blocks, places = tuple(blocks) + (blocks[1].T,), places + [(1, 0)]
    for (row, col), block in zip(places, blocks):
        for i, piece in enumerate(split(block)):
            pair[i, pl.ds(row * width, width), pl.ds(col * width, width)] = piece


def product3(left, right):
    rows = left[0].shape[0]
    both = dot(jnp.concatenate(left, axis=0), right[0])
    return both[:rows] + both[rows:] + dot(left[0], right[1])


def product(left, right):
    width = left.shape[1] // 2
    first = product3(
        (left[0, :width, :], left[1, :width, :]), (right[0], right[1])
    )
    second = product3(
        (right[0, width:, :], right[1, width:, :]), (left[0, :, width:], left[1, :, width:])
    )
    return first[:, :width], first[:, width:], second


def combine(*terms, unit=0.0):
    width = terms[0][1][0].shape[0]
    row = lax.broadcasted_iota(jnp.int32, (width, width), 0)
    col = lax.broadcasted_iota(jnp.int32, (width, width), 1)
    diagonal = jnp.where(row == col, unit, 0.0)
    out = []
    for i in range(3):
        value = functools.reduce(jnp.add, [factor * matrix[i] for factor, matrix in terms])
        out.append(value if i == 1 else value + diagonal)
    return tuple(out)


def finish_kernel(total_rows, chunk, mine, theirs, *refs):
    fields, out_ref = refs[:6], refs[6]
    x_ref, x_held, x_pair, q_pair, u_pair, n_pair, v_pair, z_pair = refs[7:15]
    wide, result, sem, out_sem = refs[15:]
    part = lax.axis_index("cols")
    size = x_ref.shape[0]
    width = size // 2
    half = width // 2
    edge_size = fields[0].shape[0]
    end = wide.shape[0] - edge_size
    starts = [at_end("even") * end, edge_size, at_end("odd") * end]
    copies = []
    for i, source in enumerate(fields):
        rows = pl.ds(pl.multiple_of(starts[i % 3], edge_size), source.shape[0])
        side = part if i < 3 else 1 - part
        target = wide.at[rows, pl.ds(pl.multiple_of(side * width, width), width)]
        copies.append(pltpu.make_async_copy(source, target, sem.at[i]))
    for copy in copies:
        copy.start()

    def block(side, index):
        rows = pl.ds(index * half, half)
        return jnp.where(part == side, mine[rows, :], theirs[rows, :])

    def place(row, col, value):
        x_ref[pl.ds(row * half, half), pl.ds(col * half, half)] = value

    for side in range(2):
        across = block(side, 1)
        place(2 * side, 2 * side, block(side, 0))
        place(2 * side, 2 * side + 1, across)
        place(2 * side + 1, 2 * side, across.T)
        place(2 * side + 1, 2 * side + 1, block(side, 2))
        for col in (0, 1):
            part_of = block(side, 3 + col)
            place(side, 2 + col, part_of if side == 0 else part_of.T)

    gram = x_ref[:width, :width], x_ref[:width, width:], x_ref[width:, width:]
    squares = gram[0] * gram[0] + 2.0 * (gram[1] * gram[1]) + gram[2] * gram[2]
    norm = jnp.sqrt(jnp.sum(squares, keepdims=True))

    def set_x(x):
        put(x_pair, x, right=True)
        for i, value in enumerate(x):
            x_held[i] = value

    def two_sweeps(first=False, last=False):
        x = tuple(x_held[i] for i in range(3))
        q = product(x_pair, x_pair)
        put(q_pair, q)
        put(u_pair, combine((0.0625, q), (-0.5625, x), unit=1.6875), right=True)
        qu = product(q_pair, u_pair)
        x = tuple(x_held[i] for i in range(3))
        n = combine((1.0, qu), (-2.4375, x), unit=2.25)
        put(n_pair, n, right=True)
        if not last:
            put(v_pair, product(x_pair, n_pair))
        z = n if first else product(z_pair, n_pair)
        if last:
            return z
        put(z_pair, z)
        set_x(product(v_pair, n_pair))

    set_x(tuple(value / norm for value in gram))
    two_sweeps(first=True)

    def body(index, carry):
        two_sweeps()
        return carry

    lax.fori_loop(0, ITERS // 2 - 2, body, 0)
    first, across, second = two_sweeps(last=True)
    z_ref = x_ref
    z_ref[:width, :width] = first
    z_ref[:width, width:] = across
    z_ref[width:, :width] = across.T
    z_ref[width:, width:] = second
    own = pl.ds(pl.multiple_of(part * width, width), width)
    rotation = z_ref[:, own].astype(BF16)
    factor = jnp.sqrt(total_rows / norm)
    for copy in copies:
        copy.wait()
    count = wide.shape[0] // chunk
    outs = []
    for i in range(count):
        rows = pl.ds(i * chunk, chunk)
        result[rows, :] = (dot(wide[rows, :], rotation) * factor).astype(BF16)
        outs.append(pltpu.make_async_copy(result.at[rows], out_ref.at[rows], out_sem.at[i]))
        outs[-1].start()
    for out in outs:
        out.wait()


def rotate(mine, theirs, owns, others, total_rows):
    width = owns[0].shape[1]
    rows = sum(own.shape[0] for own in owns)
    size = 2 * width
    chunk = min(rows, 512)
    body = functools.partial(finish_kernel, float(total_rows), chunk)
    pair = pltpu.VMEM((2, size, size), BF16)
    return pl.pallas_call(
        body,
        in_specs=[VMEM, VMEM] + [ANY] * 6,
        out_specs=ANY,
        out_shape=jax.ShapeDtypeStruct((rows, width), BF16),
        scratch_shapes=[
            pltpu.VMEM((size, size), F32),
            pltpu.VMEM((3, width, width), F32),
            pair, pair, pair, pair, pair, pair,
            pltpu.VMEM((rows, size), BF16),
            pltpu.VMEM((rows, width), BF16),
            pltpu.SemaphoreType.DMA((6,)),
            pltpu.SemaphoreType.DMA((rows // chunk,)),
        ],
        compiler_params=pltpu.CompilerParams(vmem_limit_bytes=28 * 1024 * 1024),
        cost_estimate=pl.CostEstimate(
            flops=21 * 6 * size**3 + 2 * rows * size * width,
            bytes_accessed=3 * rows * width * 2,
            transcendentals=0,
        ),
        name="rotate",
    )(mine, theirs, *owns, *others)


def after(value, *others):
    return lax.optimization_barrier((value, others))[0]


def on_device(vectors, blocks, tile_cols, live_tiles):
    tiles, _, tile, _ = blocks.shape
    width = vectors.shape[1]
    count = lax.axis_size("patch")
    pairs = {
        "even": [(i, i ^ 1) for i in range(count)],
        "odd": [(i, ((i + 1) ^ 1) - 1) for i in range(1, count - 1)],
    }

    def exchange(name, value):
        return lax.ppermute(value, "patch", pairs[name])

    def sibling(value):
        return lax.ppermute(value, "cols", [(0, 1), (1, 0)])

    start = vectors.reshape(tiles, tile, width)
    table = jnp.concatenate([tile_cols.T, jnp.broadcast_to(live_tiles[None], (1, tiles))])

    even, odd = masked_edges(table, start)
    even_halo = exchange("even", even)
    inner, even_blocks, odd_blocks = load_fields(after(table, even), start, blocks)
    odd_halo = exchange("odd", after(odd, inner))
    stored = {"even": even_blocks, "odd": odd_blocks}
    prev = dict.fromkeys(("even", "odd", "inner"))

    def rows(name, *sources, cost=SMALL):
        return tile_rows(name, table, stored[name], sources, prev[name], cost)

    for step in range(STEPS):
        first, final = step == 0, step == STEPS - 1
        if final:
            new_inner = rows("inner", even, odd, inner)
            even_halo = after(even_halo, new_inner)
        new_even = rows("even", even_halo, even, inner)
        if final:
            flat = [value.reshape(-1, width) for value in (new_even, new_inner)]
            others = [sibling(value) for value in flat]
        else:
            even_halo = exchange("even", new_even)
        if first:
            stored["inner"] = load_blocks(after(blocks, new_even))
            odd_halo = after(odd_halo, stored["inner"])
        odd_halo = after(odd_halo, new_even)
        new_odd = rows("odd", odd_halo, odd, inner, cost=LARGE if final else SMALL)
        if not final:
            odd_halo = exchange("odd", new_odd)
            new_inner = rows("inner", after(even, new_odd), odd, inner)
            even_halo = after(even_halo, new_inner)
        prev = {"even": even, "odd": odd, "inner": inner}
        even, odd, inner = new_even, new_odd, new_inner
    last = odd.reshape(-1, width)
    other_last = sibling(last)
    others = [after(other, last) for other in others]
    mine = sum_over_patch(gram_share(last, other_last, gram(flat, others)))
    theirs = sibling(mine)
    total_rows = tiles * tile * count
    return rotate(mine, theirs, flat + [last], others + [other_last], total_rows)


def solution(mesh):
    in_specs = (P("patch", "cols"), P("patch", None, None, None), P("patch", None), P("patch"))
    return jax.shard_map(
        on_device, mesh=mesh, in_specs=in_specs, out_specs=P("patch", "cols"), check_vma=False
    )
```

time: 100 us -> 93.1 us (0.931)
  Pallas kernels: 48.5 us -> 42.2 us
  starting transfers between devices: 31.8 us -> 28.7 us
  waiting for transfers between devices: 18.7 us -> 20.2 us
    pallas_call x21 -> x18, Pallas kernels: 48.5 us -> 42.2 us  [the longest x1 16.7 us: rotate(): pl.pallas_call(body, in_specs=[VMEM, VMEM] + [ANY] * 6, out_specs=ANY, ou...]
    ppermute x6, starting transfers between devices: 16.6 us -> 11.4 us  [exchange(): return lax.ppermute(value, 'patch', pairs[name])]
    ppermute x9, starting transfers between devices: 13.9 us -> 16.5 us  [from_others(): lax.ppermute(values[d], 'patch', [(i, i ^ d * stride) for i in range(coun...]
    ppermute x6, waiting for transfers between devices: 3.05 us -> 5.46 us  [exchange(): return lax.ppermute(value, 'patch', pairs[name])]
    ppermute x9, waiting for transfers between devices: 13.7 us -> 12.2 us  [from_others(): lax.ppermute(values[d], 'patch', [(i, i ^ d * stride) for i in range(coun...]
    ppermute x5 -> x4, waiting for transfers between devices: 1.92 us -> 2.47 us  [sibling(): return lax.ppermute(value, 'cols', [(0, 1), (1, 0)])]
  transfers between devices with their start and end apart: 20 -> 19, of which waited for: 12 -> 11; matrix products, arithmetic and copies ran while one was open for 0% -> 0% of each run, Pallas kernels for 28% -> 25%
where the time goes in v8:
time: 93.1 us; the launch traced here: 92.9 us
  Pallas kernels  42.2 us (45%)
  starting transfers between devices  28.7 us (31%)
  waiting for transfers between devices  20.2 us (22%)
  between operations  1.04 us (1%)
    pallas_call x1, Pallas kernels, rotate(): pl.pallas_call(body, in_specs=[VMEM, VMEM] + [ANY] * 6, out_specs=ANY, ou...  16.7 us
    ppermute x9, starting transfers between devices, from_others(): lax.ppermute(values[d], 'patch', [(i, i ^ d * stride) for i in range(coun...  16.5 us
    pallas_call x9, Pallas kernels, tile_rows(): pl.pallas_call(functools.partial(rows_kernel, name), in_specs=[VMEM] * le...  15.4 us
    ppermute x9, waiting for transfers between devices, from_others(): lax.ppermute(values[d], 'patch', [(i, i ^ d * stride) for i in range(coun...  12.2 us
    ppermute x6, starting transfers between devices, exchange(): return lax.ppermute(value, 'patch', pairs[name])  11.4 us
    pallas_call x3, Pallas kernels, load_call(): pl.pallas_call(body, in_specs=[SMEM] * len(table) + [HBM] * len(args), ou...  7.45 us
    ppermute x6, waiting for transfers between devices, exchange(): return lax.ppermute(value, 'patch', pairs[name])  5.46 us
    pallas_call x5, Pallas kernels, gram_call(): pl.pallas_call(body, in_specs=[VMEM] * len(args), out_specs=[VMEM] * outs...  2.68 us
  transfers between devices with their start and end apart: 19, of which 11 were waited for; matrix products, arithmetic and copies ran while one was open for 0% of the time, Pallas kernels for 25%

profile of v8, /device:TPU:0, one launch (start us, length us, event | category | flops | bytes accessed | tf_op | source)
XLA Modules:
  0.0 92.9 jit_solution(14051928435167944747)
XLA Ops:
  0.7 0.7 concatenate.3.table.table_ref
  1.3 1.8 %masked_edges.1 = (bf16[4,128,256]{2,1,0:T(8,128)(2,1)S(1)}, bf16[4,128,256]{2,1,0:T(8,128)(2,1)S(1)}) custom-call(s32[9,32]{1,0:T(8,128)S(1)} %concatenate.3.table.table_ref, bf16[32,128,256]{2,1,0:T(8,128)(2,1)} %bitcast.16), custom_call_target="tpu_custom_call" | custom-call | flops 1000 | bytes 1000 | tf_op jit(solution)/shard_map/masked_edges/pallas_call | solution.py:104
  3.2 3.0 %collective-permute-start.1 = (bf16[4,128,256]{2,1,0:T(8,128)(2,1)S(1)}, bf16[4,128,256]{2,1,0:T(8,128)(2,1)S(1)}, u32[]{:S(2)}, u32[]{:S(2)}) collective-permute-start(bf16[4,128,256]{2,1,0:T(8,128)(2,1)S(1)} %get-tuple-element.38.refs_1_.refs_0_.refs_3_), channel_id=1, source_target_pairs={{0,1},{1,0},{2,3},{3,2},{4,5},{5,4},{6,7},{7,6},{8,9},{9,8},{10,11... | collective-permute-start | bytes 786440 | tf_op jit(solution)/shard_map/ppermute | solution.py:483
  6.2 2.8 %load_fields.1 = (bf16[24,128,256]{2,1,0:T(8,128)(2,1)S(1)}, bf16[4,8,128,128]{3,2,1,0:T(8,128)(2,1)S(1)}, bf16[4,8,128,128]{3,2,1,0:T(8,128)(2,1)S(1)}) custom-call(s32[9,32]{1,0:T(8,128)S(1)} %concatenate.3.table.table_ref, bf16[32,128,256]{2,1,0:T(8,128)(2,1)} %bitcast.17, bf16[32,8,128,128]{3,2,1,0:T(8,128)(2,1)} %blocks_ref.2), custom_call_target="tpu_custom_call" | custom-call | flops 1000 | bytes 1000 | tf_op jit(solution)/shard_map/load_fields/pallas_call | solution.py:104
  9.0 0.7 collective-permute-start
  9.6 2.8 %collective-permute-done.1.refs_0_ = bf16[4,128,256]{2,1,0:T(8,128)(2,1)S(1)} collective-permute-done((bf16[4,128,256]{2,1,0:T(8,128)(2,1)S(1)}, bf16[4,128,256]{2,1,0:T(8,128)(2,1)S(1)}, u32[]{:S(2)}, u32[]{:S(2)}) %collective-permute-start.1) | collective-permute-done | bytes 262176 | tf_op jit(solution)/shard_map/ppermute | solution.py:483
  12.5 1.1 %rows_even.3.refs_1_.refs_0_.refs_3_ = bf16[4,128,256]{2,1,0:T(8,128)(2,1)S(1)} custom-call(s32[9,32]{1,0:T(8,128)S(1)} %concatenate.3.table.table_ref, bf16[4,128,256]{2,1,0:T(8,128)(2,1)S(1)} %collective-permute-done.1.refs_0_, bf16[4,128,256]{2,1,0:T(8,128)(2,1)S(1)} %get-tuple-element.38.refs_1_.refs_0_.refs_3_, ...), custom_call_target="tpu_custom_call" | custom-call | flops 1000 | bytes 1000 | tf_op jit(solution)/shard_map/rows_even/pallas_call | solution.py:181
  13.6 1.8 %collective-permute-start.3 = (bf16[4,128,256]{2,1,0:T(8,128)(2,1)S(1)}, bf16[4,128,256]{2,1,0:T(8,128)(2,1)S(1)}, u32[]{:S(2)}, u32[]{:S(2)}) collective-permute-start(bf16[4,128,256]{2,1,0:T(8,128)(2,1)S(1)} %rows_even.3.refs_1_.refs_0_.refs_3_), channel_id=1, source_target_pairs={{0,1},{1,0},{2,3},{3,2},{4,5},{5,4},{6,7},{7,6},{8,9},{9,8},{10,11... | collective-permute-start | bytes 786440 | tf_op jit(solution)/shard_map/ppermute | solution.py:483
  15.4 2.9 %load_blocks.1.refs_3_.refs_4_ = bf16[24,8,128,128]{3,2,1,0:T(8,128)(2,1)S(1)} custom-call(bf16[32,8,128,128]{3,2,1,0:T(8,128)(2,1)} %blocks_ref.2), custom_call_target="tpu_custom_call" | custom-call | flops 1000 | bytes 1000 | tf_op jit(solution)/shard_map/load_blocks/pallas_call | solution.py:104
  18.3 0.0 collective-permute-done.refs_0_
  18.3 1.1 %rows_odd.3.refs_1_.refs_3_ = bf16[4,128,256]{2,1,0:T(8,128)(2,1)S(1)} custom-call(s32[9,32]{1,0:T(8,128)S(1)} %concatenate.3.table.table_ref, bf16[4,128,256]{2,1,0:T(8,128)(2,1)S(1)} %collective-permute-done.refs_0_, bf16[4,128,256]{2,1,0:T(8,128)(2,1)S(1)} %get-tuple-element.32.refs_1_.refs_3_, ...), custom_call_target="tpu_custom_call" | custom-call | flops 1000 | bytes 1000 | tf_op jit(solution)/shard_map/rows_odd/pallas_call | solution.py:181
  19.4 0.7 collective-permute-start.2
  20.1 2.9 %rows_inner.3.refs_2_.refs_3_ = bf16[24,128,256]{2,1,0:T(8,128)(2,1)S(1)} custom-call(s32[9,32]{1,0:T(8,128)S(1)} %concatenate.3.table.table_ref, bf16[4,128,256]{2,1,0:T(8,128)(2,1)S(1)} %get-tuple-element.38.refs_1_.refs_0_.refs_3_, bf16[4,128,256]{2,1,0:T(8,128)(2,1)S(1)} %get-tuple-element.32.refs_1_.refs_3_, ...), custom_call_target="tpu_custom_call" | custom-call | flops 1000 | bytes 1000 | tf_op jit(solution)/shard_map/rows_inner/pallas_call | solution.py:181
  23.0 2.6 %collective-permute-done.3.refs_0_ = bf16[4,128,256]{2,1,0:T(8,128)(2,1)S(1)} collective-permute-done((bf16[4,128,256]{2,1,0:T(8,128)(2,1)S(1)}, bf16[4,128,256]{2,1,0:T(8,128)(2,1)S(1)}, u32[]{:S(2)}, u32[]{:S(2)}) %collective-permute-start.3) | collective-permute-done | bytes 262176 | tf_op jit(solution)/shard_map/ppermute | solution.py:483
  25.6 1.1 %rows_even.4.refs_0_.refs_1_ = bf16[4,128,256]{2,1,0:T(8,128)(2,1)S(1)} custom-call(s32[9,32]{1,0:T(8,128)S(1)} %concatenate.3.table.table_ref, bf16[4,128,256]{2,1,0:T(8,128)(2,1)S(1)} %collective-permute-done.3.refs_0_, bf16[4,128,256]{2,1,0:T(8,128)(2,1)S(1)} %rows_even.3.refs_1_.refs_0_.refs_3_, bf16[24,128,256]{2,1,0:T(8,128)(2,1)S(1)} %rows_inner.3.refs_2_.refs_3_, ...), custom_call_target="tpu_custom_call" | custom-call | flops 1000 | bytes 1000 | tf_op jit(solution)/shard_map/rows_even/pallas_call | solution.py:181
  26.8 4.4 %collective-permute-start.5 = (bf16[4,128,256]{2,1,0:T(8,128)(2,1)S(1)}, bf16[4,128,256]{2,1,0:T(8,128)(2,1)S(1)}, u32[]{:S(2)}, u32[]{:S(2)}) collective-permute-start(bf16[4,128,256]{2,1,0:T(8,128)(2,1)S(1)} %rows_even.4.refs_0_.refs_1_), channel_id=1, source_target_pairs={{0,1},{1,0},{2,3},{3,2},{4,5},{5,4},{6,7},{7,6},{8,9},{9,8},{10,11... | collective-permute-start | bytes 786440 | tf_op jit(solution)/shard_map/ppermute | solution.py:483
  31.2 0.0 collective-permute-done.2.refs_0_
  31.2 1.1 %rows_odd.4.refs_1_ = bf16[4,128,256]{2,1,0:T(8,128)(2,1)S(1)} custom-call(s32[9,32]{1,0:T(8,128)S(1)} %concatenate.3.table.table_ref, bf16[4,128,256]{2,1,0:T(8,128)(2,1)S(1)} %collective-permute-done.2.refs_0_, bf16[4,128,256]{2,1,0:T(8,128)(2,1)S(1)} %rows_odd.3.refs_1_.refs_3_, bf16[24,128,256]{2,1,0:T(8,128)(2,1)S(1)} %rows_inner.3.refs_2_.refs_3_, ...), custom_call_target="tpu_custom_call" | custom-call | flops 1000 | bytes 1000 | tf_op jit(solution)/shard_map/rows_odd/pallas_call | solution.py:181
  32.3 0.9 collective-permute-start.4
  33.2 2.9 %rows_inner.4.refs_2_ = bf16[24,128,256]{2,1,0:T(8,128)(2,1)S(1)} custom-call(s32[9,32]{1,0:T(8,128)S(1)} %concatenate.3.table.table_ref, bf16[4,128,256]{2,1,0:T(8,128)(2,1)S(1)} %rows_even.3.refs_1_.refs_0_.refs_3_, bf16[4,128,256]{2,1,0:T(8,128)(2,1)S(1)} %rows_odd.3.refs_1_.refs_3_, bf16[24,128,256]{2,1,0:T(8,128)(2,1)S(1)} %rows_inner.3.refs_2_.refs_3_, ...), custom_call_target="tpu_custom_call" | custom-call | flops 1000 | bytes 1000 | tf_op jit(solution)/shard_map/rows_inner/pallas_call | solution.py:181
  36.1 2.9 %rows_inner.5 = bf16[24,128,256]{2,1,0:T(8,128)(2,1)S(1)} custom-call(s32[9,32]{1,0:T(8,128)S(1)} %concatenate.3.table.table_ref, bf16[4,128,256]{2,1,0:T(8,128)(2,1)S(1)} %rows_even.4.refs_0_.refs_1_, bf16[4,128,256]{2,1,0:T(8,128)(2,1)S(1)} %rows_odd.4.refs_1_, bf16[24,128,256]{2,1,0:T(8,128)(2,1)S(1)} %rows_inner.4.refs_2_, ...), custom_call_target="tpu_custom_call" | custom-call | flops 1000 | bytes 1000 | tf_op jit(solution)/shard_map/rows_inner/pallas_call | solution.py:181
  39.0 0.1 collective-permute-start.8
  39.1 0.0 collective-permute-done.5.refs_0_
  39.1 1.1 %rows_even.5 = bf16[4,128,256]{2,1,0:T(8,128)(2,1)S(1)} custom-call(s32[9,32]{1,0:T(8,128)S(1)} %concatenate.3.table.table_ref, bf16[4,128,256]{2,1,0:T(8,128)(2,1)S(1)} %collective-permute-done.5.refs_0_, bf16[4,128,256]{2,1,0:T(8,128)(2,1)S(1)} %rows_even.4.refs_0_.refs_1_, bf16[24,128,256]{2,1,0:T(8,128)(2,1)S(1)} %rows_inner.4.refs_2_, ...), custom_call_target="tpu_custom_call" | custom-call | flops 1000 | bytes 1000 | tf_op jit(solution)/shard_map/rows_even/pallas_call | solution.py:181
  40.2 0.0 collective-permute-done.4.refs_0_
  40.2 0.6 collective-permute-start.7
  40.8 1.1 %rows_odd.5 = bf16[4,128,256]{2,1,0:T(8,128)(2,1)S(1)} custom-call(s32[9,32]{1,0:T(8,128)S(1)} %concatenate.3.table.table_ref, bf16[4,128,256]{2,1,0:T(8,128)(2,1)S(1)} %collective-permute-done.4.refs_0_, bf16[4,128,256]{2,1,0:T(8,128)(2,1)S(1)} %rows_odd.4.refs_1_, bf16[24,128,256]{2,1,0:T(8,128)(2,1)S(1)} %rows_inner.4.refs_2_, ...), custom_call_target="tpu_custom_call" | custom-call | flops 99999997952 | bytes 1000 | tf_op jit(solution)/shard_map/rows_odd/pallas_call | solution.py:181
  41.9 0.1 collective-permute-start.6
  42.0 0.8 collective-permute-done.7.refs_2_.refs_3_
  42.8 0.0 collective-permute-done.8.refs_3_.refs_4_
  42.8 2.3 %gram.1.start_ref = f32[256,512]{1,0:T(8,128)S(1)} custom-call(bf16[512,256]{1,0:T(8,128)(2,1)S(1)} %bitcast.11, bf16[3072,256]{1,0:T(8,128)(2,1)S(1)} %bitcast.8, bf16[512,256]{1,0:T(8,128)(2,1)S(1)} %collective-permute-done.7.refs_2_.refs_3_, bf16[3072,256]{1,0:T(8,128)(2,1)S(1)} %collective-permute-done.8.refs_3_.refs_4_), custom_call_target="tpu_custom_call" | custom-call | flops 1000 | bytes 1000 | tf_op jit(solution)/shard_map/gram/pallas_call | solution.py:239
  45.1 0.0 collective-permute-done.6.other_ref.refs_5_
  45.1 0.3 gram_share.1
  45.5 7.0 %collective-permute-start.9 = (f32[160,128]{1,0:T(8,128)S(1)}, f32[160,128]{1,0:T(8,128)S(1)}, u32[]{:S(2)}, u32[]{:S(2)}) collective-permute-start(f32[160,128]{1,0:T(8,128)S(1)} %get-tuple-element.48), channel_id=1, source_target_pairs={{0,1},{1,0},{2,3},{3,2},{4,5},{5,4},{6,7},{7,6},{8,9},{9,8},{10,11... | collective-permute-start | bytes 245768 | tf_op jit(solution)/shard_map/ppermute | solution.py:288
  52.4 0.0 collective-permute-start.10
  52.4 1.5 %collective-permute-start.11 = (f32[160,128]{1,0:T(8,128)S(1)}, f32[160,128]{1,0:T(8,128)S(1)}, u32[]{:S(2)}, u32[]{:S(2)}) collective-permute-start(f32[160,128]{1,0:T(8,128)S(1)} %get-tuple-element.50), channel_id=1, source_target_pairs={{0,3},{1,2},{2,1},{3,0},{4,7},{5,6},{6,5},{7,4},{8,11},{9,10},{10,... | collective-permute-start | bytes 245768 | tf_op jit(solution)/shard_map/ppermute | solution.py:288
  54.0 1.2 %collective-permute-done.9.b = f32[160,128]{1,0:T(8,128)S(1)} collective-permute-done((f32[160,128]{1,0:T(8,128)S(1)}, f32[160,128]{1,0:T(8,128)S(1)}, u32[]{:S(2)}, u32[]{:S(2)}) %collective-permute-start.9) | collective-permute-done | bytes 81952 | tf_op jit(solution)/shard_map/ppermute | solution.py:288
  55.2 3.2 %collective-permute-done.10.c = f32[160,128]{1,0:T(8,128)S(1)} collective-permute-done((f32[160,128]{1,0:T(8,128)S(1)}, f32[160,128]{1,0:T(8,128)S(1)}, u32[]{:S(2)}, u32[]{:S(2)}) %collective-permute-start.10) | collective-permute-done | bytes 81952 | tf_op jit(solution)/shard_map/ppermute | solution.py:288
  58.4 0.0 collective-permute-done.11.d
  58.4 2.5 %collective-permute-start.14 = (f32[160,128]{1,0:T(8,128)S(1)}, f32[160,128]{1,0:T(8,128)S(1)}, u32[]{:S(2)}, u32[]{:S(2)}) collective-permute-start(f32[160,128]{1,0:T(8,128)S(1)} %add_four.2.a), channel_id=1, source_target_pairs={{0,12},{1,13},{2,14},{3,15},{4,8},{5,9},{6,10},{7,11},{8,4},{9,5},... | collective-permute-start | bytes 245768 | tf_op jit(solution)/shard_map/ppermute | solution.py:288
  61.0 0.0 collective-permute-start.13
  61.0 1.9 %collective-permute-start.12 = (f32[160,128]{1,0:T(8,128)S(1)}, f32[160,128]{1,0:T(8,128)S(1)}, u32[]{:S(2)}, u32[]{:S(2)}) collective-permute-start(f32[160,128]{1,0:T(8,128)S(1)} %add_four.2.a), channel_id=1, source_target_pairs={{0,4},{1,5},{2,6},{3,7},{4,0},{5,1},{6,2},{7,3},{8,12},{9,13},{10,... | collective-permute-start | bytes 245768 | tf_op jit(solution)/shard_map/ppermute | solution.py:288
  62.9 2.4 %collective-permute-done.14.d = f32[160,128]{1,0:T(8,128)S(1)} collective-permute-done((f32[160,128]{1,0:T(8,128)S(1)}, f32[160,128]{1,0:T(8,128)S(1)}, u32[]{:S(2)}, u32[]{:S(2)}) %collective-permute-start.14) | collective-permute-done | bytes 81952 | tf_op jit(solution)/shard_map/ppermute | solution.py:288
  65.3 2.2 %collective-permute-done.13.c = f32[160,128]{1,0:T(8,128)S(1)} collective-permute-done((f32[160,128]{1,0:T(8,128)S(1)}, f32[160,128]{1,0:T(8,128)S(1)}, u32[]{:S(2)}, u32[]{:S(2)}) %collective-permute-start.13) | collective-permute-done | bytes 81952 | tf_op jit(solution)/shard_map/ppermute | solution.py:288
  67.5 0.0 collective-permute-done.12.b
  67.5 1.7 %collective-permute-start.17 = (f32[160,128]{1,0:T(8,128)S(1)}, f32[160,128]{1,0:T(8,128)S(1)}, u32[]{:S(2)}, u32[]{:S(2)}) collective-permute-start(f32[160,128]{1,0:T(8,128)S(1)} %add_four.3.refs_0_), channel_id=1, source_target_pairs={{0,3},{1,2},{2,1},{3,0},{4,7},{5,6},{6,5},{7,4},{8,11},{9,10},{10,... | collective-permute-start | bytes 245768 | tf_op jit(solution)/shard_map/ppermute | solution.py:288
  69.2 0.6 collective-permute-start.16
  69.8 1.2 %collective-permute-start.15 = (f32[160,128]{1,0:T(8,128)S(1)}, f32[160,128]{1,0:T(8,128)S(1)}, u32[]{:S(2)}, u32[]{:S(2)}) collective-permute-start(f32[160,128]{1,0:T(8,128)S(1)} %add_four.3.refs_0_), channel_id=1, source_target_pairs={{0,1},{1,0},{2,3},{3,2},{4,5},{5,4},{6,7},{7,6},{8,9},{9,8},{10,11... | collective-permute-start | bytes 245768 | tf_op jit(solution)/shard_map/ppermute | solution.py:288
  71.1 2.2 %collective-permute-done.17.refs_3_ = f32[160,128]{1,0:T(8,128)S(1)} collective-permute-done((f32[160,128]{1,0:T(8,128)S(1)}, f32[160,128]{1,0:T(8,128)S(1)}, u32[]{:S(2)}, u32[]{:S(2)}) %collective-permute-start.17) | collective-permute-done | bytes 81952 | tf_op jit(solution)/shard_map/ppermute | solution.py:288
  73.2 0.9 collective-permute-done.16.refs_2_
  74.1 0.1 collective-permute-done.15.refs_1_
  74.3 0.1 collective-permute-start.18
  74.4 1.6 %collective-permute-done.18.theirs = f32[640,128]{1,0:T(8,128)S(1)} collective-permute-done((f32[640,128]{1,0:T(8,128)S(1)}, f32[640,128]{1,0:T(8,128)S(1)}, u32[]{:S(2)}, u32[]{:S(2)}) %collective-permute-start.18) | collective-permute-done | bytes 327712 | tf_op jit(solution)/shard_map/ppermute | solution.py:486
  76.0 16.7 %rotate.1 = bf16[4096,256]{1,0:T(8,128)(2,1)} custom-call(f32[640,128]{1,0:T(8,128)S(1)} %join.1.mine, f32[640,128]{1,0:T(8,128)S(1)} %collective-permute-done.18.theirs, bf16[512,256]{1,0:T(8,128)(2,1)S(1)} %bitcast.12, bf16[3072,256]{1,0:T(8,128)(2,1)S(1)} %bitcast.9, bf16[512,256]{1,0:T(8,128)(2,1)S(1)} %bitcast.15, ...), custom_call_target="tpu_custom_call" | custom-call | flops 17985175552 | bytes 6291456 | tf_op jit(solution)/shard_map/rotate/pallas_call | solution.py:445
  (3 shorter events, 0.1 us)
Async XLA Ops:
  3.2 9.3 %collective-permute-start.1 = (bf16[4,128,256]{2,1,0:T(8,128)(2,1)S(1)}, bf16[4,128,256]{2,1,0:T(8,128)(2,1)S(1)}, u32[]{:S(2)}, u32[]{:S(2)}) collective-permute-start(bf16[4,128,256]{2,1,0:T(8,128)(2,1)S(1)} %get-tuple-element.38.refs_1_.refs_0_.refs_3_), channel_id=1, source_target_pairs={{0,1},{1,0},{2,3},{3,2},{4,5},{5,4},{6,7},{7,6},{8,9},{9,8},{10,11... | collective-permute-start | bytes 786440 | tf_op jit(solution)/shard_map/ppermute | solution.py:483
  9.0 9.3 %collective-permute-start = (bf16[4,128,256]{2,1,0:T(8,128)(2,1)S(1)}, bf16[4,128,256]{2,1,0:T(8,128)(2,1)S(1)}, u32[]{:S(2)}, u32[]{:S(2)}) collective-permute-start(bf16[4,128,256]{2,1,0:T(8,128)(2,1)S(1)} %get-tuple-element.32.refs_1_.refs_3_), channel_id=1, source_target_pairs={{1,2},{2,1},{3,4},{4,3},{5,6},{6,5},{7,8},{8,7},{9,10},{10,9},{11,... | collective-permute-start | bytes 786440 | tf_op jit(solution)/shard_map/ppermute | solution.py:483
  13.6 12.0 %collective-permute-start.3 = (bf16[4,128,256]{2,1,0:T(8,128)(2,1)S(1)}, bf16[4,128,256]{2,1,0:T(8,128)(2,1)S(1)}, u32[]{:S(2)}, u32[]{:S(2)}) collective-permute-start(bf16[4,128,256]{2,1,0:T(8,128)(2,1)S(1)} %rows_even.3.refs_1_.refs_0_.refs_3_), channel_id=1, source_target_pairs={{0,1},{1,0},{2,3},{3,2},{4,5},{5,4},{6,7},{7,6},{8,9},{9,8},{10,11... | collective-permute-start | bytes 786440 | tf_op jit(solution)/shard_map/ppermute | solution.py:483
  19.4 11.7 %collective-permute-start.2 = (bf16[4,128,256]{2,1,0:T(8,128)(2,1)S(1)}, bf16[4,128,256]{2,1,0:T(8,128)(2,1)S(1)}, u32[]{:S(2)}, u32[]{:S(2)}) collective-permute-start(bf16[4,128,256]{2,1,0:T(8,128)(2,1)S(1)} %rows_odd.3.refs_1_.refs_3_), channel_id=1, source_target_pairs={{1,2},{2,1},{3,4},{4,3},{5,6},{6,5},{7,8},{8,7},{9,10},{10,9},{11,... | collective-permute-start | bytes 786440 | tf_op jit(solution)/shard_map/ppermute | solution.py:483
  26.8 12.3 %collective-permute-start.5 = (bf16[4,128,256]{2,1,0:T(8,128)(2,1)S(1)}, bf16[4,128,256]{2,1,0:T(8,128)(2,1)S(1)}, u32[]{:S(2)}, u32[]{:S(2)}) collective-permute-start(bf16[4,128,256]{2,1,0:T(8,128)(2,1)S(1)} %rows_even.4.refs_0_.refs_1_), channel_id=1, source_target_pairs={{0,1},{1,0},{2,3},{3,2},{4,5},{5,4},{6,7},{7,6},{8,9},{9,8},{10,11... | collective-permute-start | bytes 786440 | tf_op jit(solution)/shard_map/ppermute | solution.py:483
  32.3 7.9 %collective-permute-start.4 = (bf16[4,128,256]{2,1,0:T(8,128)(2,1)S(1)}, bf16[4,128,256]{2,1,0:T(8,128)(2,1)S(1)}, u32[]{:S(2)}, u32[]{:S(2)}) collective-permute-start(bf16[4,128,256]{2,1,0:T(8,128)(2,1)S(1)} %rows_odd.4.refs_1_), channel_id=1, source_target_pairs={{1,2},{2,1},{3,4},{4,3},{5,6},{6,5},{7,8},{8,7},{9,10},{10,9},{11,... | collective-permute-start | bytes 786440 | tf_op jit(solution)/shard_map/ppermute | solution.py:483
  39.0 3.9 %collective-permute-start.8 = (bf16[3072,256]{1,0:T(8,128)(2,1)S(1)}, bf16[3072,256]{1,0:T(8,128)(2,1)S(1)}, u32[]{:S(2)}, u32[]{:S(2)}) collective-permute-start(bf16[3072,256]{1,0:T(8,128)(2,1)S(1)} %bitcast.7), channel_id=1, source_target_pairs={{0,16},{16,0},{1,17},{17,1},{2,18},{18,2},{3,19},{19,3},{4,20},{20... | collective-permute-start | bytes 4718600 | tf_op jit(solution)/shard_map/ppermute | solution.py:486
  40.2 2.6 %collective-permute-start.7 = (bf16[512,256]{1,0:T(8,128)(2,1)S(1)}, bf16[512,256]{1,0:T(8,128)(2,1)S(1)}, u32[]{:S(2)}, u32[]{:S(2)}) collective-permute-start(bf16[512,256]{1,0:T(8,128)(2,1)S(1)} %bitcast.10), channel_id=1, source_target_pairs={{0,16},{16,0},{1,17},{17,1},{2,18},{18,2},{3,19},{19,3},{4,20},{20... | collective-permute-start | bytes 786440 | tf_op jit(solution)/shard_map/ppermute | solution.py:486
  41.9 3.2 %collective-permute-start.6 = (bf16[512,256]{1,0:T(8,128)(2,1)S(1)}, bf16[512,256]{1,0:T(8,128)(2,1)S(1)}, u32[]{:S(2)}, u32[]{:S(2)}) collective-permute-start(bf16[512,256]{1,0:T(8,128)(2,1)S(1)} %bitcast.13), channel_id=1, source_target_pairs={{0,16},{16,0},{1,17},{17,1},{2,18},{18,2},{3,19},{19,3},{4,20},{20... | collective-permute-start | bytes 786440 | tf_op jit(solution)/shard_map/ppermute | solution.py:486
  45.5 9.7 %collective-permute-start.9 = (f32[160,128]{1,0:T(8,128)S(1)}, f32[160,128]{1,0:T(8,128)S(1)}, u32[]{:S(2)}, u32[]{:S(2)}) collective-permute-start(f32[160,128]{1,0:T(8,128)S(1)} %get-tuple-element.48), channel_id=1, source_target_pairs={{0,1},{1,0},{2,3},{3,2},{4,5},{5,4},{6,7},{7,6},{8,9},{9,8},{10,11... | collective-permute-start | bytes 245768 | tf_op jit(solution)/shard_map/ppermute | solution.py:288
  52.4 6.0 %collective-permute-start.10 = (f32[160,128]{1,0:T(8,128)S(1)}, f32[160,128]{1,0:T(8,128)S(1)}, u32[]{:S(2)}, u32[]{:S(2)}) collective-permute-start(f32[160,128]{1,0:T(8,128)S(1)} %get-tuple-element.49), channel_id=1, source_target_pairs={{0,2},{1,3},{2,0},{3,1},{4,6},{5,7},{6,4},{7,5},{8,10},{9,11},{10,... | collective-permute-start | bytes 245768 | tf_op jit(solution)/shard_map/ppermute | solution.py:288
  52.4 6.0 %collective-permute-start.11 = (f32[160,128]{1,0:T(8,128)S(1)}, f32[160,128]{1,0:T(8,128)S(1)}, u32[]{:S(2)}, u32[]{:S(2)}) collective-permute-start(f32[160,128]{1,0:T(8,128)S(1)} %get-tuple-element.50), channel_id=1, source_target_pairs={{0,3},{1,2},{2,1},{3,0},{4,7},{5,6},{6,5},{7,4},{8,11},{9,10},{10,... | collective-permute-start | bytes 245768 | tf_op jit(solution)/shard_map/ppermute | solution.py:288
  58.4 6.8 %collective-permute-start.14 = (f32[160,128]{1,0:T(8,128)S(1)}, f32[160,128]{1,0:T(8,128)S(1)}, u32[]{:S(2)}, u32[]{:S(2)}) collective-permute-start(f32[160,128]{1,0:T(8,128)S(1)} %add_four.2.a), channel_id=1, source_target_pairs={{0,12},{1,13},{2,14},{3,15},{4,8},{5,9},{6,10},{7,11},{8,4},{9,5},... | collective-permute-start | bytes 245768 | tf_op jit(solution)/shard_map/ppermute | solution.py:288
  61.0 6.5 %collective-permute-start.13 = (f32[160,128]{1,0:T(8,128)S(1)}, f32[160,128]{1,0:T(8,128)S(1)}, u32[]{:S(2)}, u32[]{:S(2)}) collective-permute-start(f32[160,128]{1,0:T(8,128)S(1)} %add_four.2.a), channel_id=1, source_target_pairs={{0,8},{1,9},{2,10},{3,11},{4,12},{5,13},{6,14},{7,15},{8,0},{9,1},... | collective-permute-start | bytes 245768 | tf_op jit(solution)/shard_map/ppermute | solution.py:288
  61.0 6.5 %collective-permute-start.12 = (f32[160,128]{1,0:T(8,128)S(1)}, f32[160,128]{1,0:T(8,128)S(1)}, u32[]{:S(2)}, u32[]{:S(2)}) collective-permute-start(f32[160,128]{1,0:T(8,128)S(1)} %add_four.2.a), channel_id=1, source_target_pairs={{0,4},{1,5},{2,6},{3,7},{4,0},{5,1},{6,2},{7,3},{8,12},{9,13},{10,... | collective-permute-start | bytes 245768 | tf_op jit(solution)/shard_map/ppermute | solution.py:288
  67.5 5.7 %collective-permute-start.17 = (f32[160,128]{1,0:T(8,128)S(1)}, f32[160,128]{1,0:T(8,128)S(1)}, u32[]{:S(2)}, u32[]{:S(2)}) collective-permute-start(f32[160,128]{1,0:T(8,128)S(1)} %add_four.3.refs_0_), channel_id=1, source_target_pairs={{0,3},{1,2},{2,1},{3,0},{4,7},{5,6},{6,5},{7,4},{8,11},{9,10},{10,... | collective-permute-start | bytes 245768 | tf_op jit(solution)/shard_map/ppermute | solution.py:288
  69.2 4.9 %collective-permute-start.16 = (f32[160,128]{1,0:T(8,128)S(1)}, f32[160,128]{1,0:T(8,128)S(1)}, u32[]{:S(2)}, u32[]{:S(2)}) collective-permute-start(f32[160,128]{1,0:T(8,128)S(1)} %add_four.3.refs_0_), channel_id=1, source_target_pairs={{0,2},{1,3},{2,0},{3,1},{4,6},{5,7},{6,4},{7,5},{8,10},{9,11},{10,... | collective-permute-start | bytes 245768 | tf_op jit(solution)/shard_map/ppermute | solution.py:288
  69.8 4.4 %collective-permute-start.15 = (f32[160,128]{1,0:T(8,128)S(1)}, f32[160,128]{1,0:T(8,128)S(1)}, u32[]{:S(2)}, u32[]{:S(2)}) collective-permute-start(f32[160,128]{1,0:T(8,128)S(1)} %add_four.3.refs_0_), channel_id=1, source_target_pairs={{0,1},{1,0},{2,3},{3,2},{4,5},{5,4},{6,7},{7,6},{8,9},{9,8},{10,11... | collective-permute-start | bytes 245768 | tf_op jit(solution)/shard_map/ppermute | solution.py:288
  74.3 1.7 %collective-permute-start.18 = (f32[640,128]{1,0:T(8,128)S(1)}, f32[640,128]{1,0:T(8,128)S(1)}, u32[]{:S(2)}, u32[]{:S(2)}) collective-permute-start(f32[640,128]{1,0:T(8,128)S(1)} %join.1.mine), channel_id=1, source_target_pairs={{0,16},{16,0},{1,17},{17,1},{2,18},{18,2},{3,19},{19,3},{4,20},{20... | collective-permute-start | bytes 983048 | tf_op jit(solution)/shard_map/ppermute | solution.py:486

commit v9 on v8

--- a/solution.py
+++ b/solution.py
@@ -12,6 +12,7 @@
 ITERS = 8
 WAYS = 4
 LOAD_CUTS = 4
+GRAM_ROWS = 1024
 GROUP = 8
 
 SMALL = pl.CostEstimate(flops=1000, bytes_accessed=1000, transcendentals=0)
@@ -198,6 +199,8 @@
 
 
 def add_gram(chunk, own_ref, other_ref, total):
+    chunk = min(chunk, own_ref.shape[0])
+
     def add(index, carry):
         rows = pl.ds(pl.multiple_of(index * chunk, chunk), chunk)
         own = own_ref[rows, :]
@@ -216,7 +219,7 @@
 
 
 def share_kernel(chunk, own_ref, other_ref, start_ref, *refs):
-    outs, (total, share) = refs[:WAYS], refs[WAYS:]
+    share, total = refs
     total[...] = start_ref[...]
     add_gram(chunk, own_ref, other_ref, total)
     width = total.shape[0]
@@ -228,10 +231,6 @@
     blocks = [own[:half, :half], own[:half, half:], own[half:, half:], second, third]
     for i, block in enumerate(blocks):
         share[pl.ds(i * half, half), :] = block
-    quarter = lax.axis_index("patch") % WAYS
-    for d, out in enumerate(outs):
-        rows = out.shape[0]
-        out[...] = share[pl.ds(pl.multiple_of((quarter ^ d) * rows, 8), rows), :]
 
 
 def gram_call(body, name, args, shape, scratch=(), outs=0):
@@ -249,8 +248,8 @@
 
 
 def gram(owns, others):
-    chunk, width = min(own.shape[0] for own in owns), owns[0].shape[1]
-    body = functools.partial(gram_kernel, chunk)
+    width = owns[0].shape[1]
+    body = functools.partial(gram_kernel, GRAM_ROWS)
     return gram_call(body, "gram", owns + others, (width, 2 * width))
 
 
@@ -258,14 +257,15 @@
     rows, width = own.shape
     half = width // 2
     body = functools.partial(share_kernel, rows)
-    scratch = [pltpu.VMEM((width, 2 * width), F32), pltpu.VMEM((5 * half, half), F32)]
-    shape = (5 * half // WAYS, half)
-    args = [own, other, start]
-    return gram_call(body, "gram_share", args, shape, scratch, outs=WAYS)
-
-
-def add_kernel(a, b, c, d, out):
-    out[...] = (a[...] + b[...]) + (c[...] + d[...])
+    scratch = [pltpu.VMEM((width, 2 * width), F32)]
+    return gram_call(body, "gram_share", [own, other, start], (5 * half, half), scratch)
+
+
+def add_kernel(*refs):
+    parts = [ref[...] for ref in refs[:-1]]
+    if len(parts) == 1:
+        parts = [parts[0][i] for i in range(WAYS)]
+    refs[-1][...] = (parts[0] + parts[1]) + (parts[2] + parts[3])
 
 
 def join_kernel(*refs):
@@ -276,25 +276,30 @@
         out[pl.ds(pl.multiple_of((quarter ^ d) * rows, 8), rows), :] = part[...]
 
 
-def sum_over_patch(parts):
+def sum_over_patch(share):
     count = lax.axis_size("patch")
-    rows, columns = parts[0].shape
+    columns = share.shape[1]
+    parts = share.reshape(WAYS, -1, columns)
+    rows = parts.shape[1]
 
     def add_four(values):
         return gram_call(add_kernel, "add_four", values, (rows, columns))
 
-    def from_others(values, stride=1):
+    def from_others(value, stride=1):
         return [
-            lax.ppermute(values[d], "patch", [(i, i ^ (d * stride)) for i in range(count)])
+            lax.ppermute(value, "patch", [(i, i ^ (d * stride)) for i in range(count)])
             for d in range(1, WAYS)
         ]
 
-    total = add_four([parts[0]] + from_others(parts))
+    groups = [list(range(i, i + WAYS)) for i in range(0, count, WAYS)]
+    total = add_four(
+        [lax.all_to_all(parts, "patch", 0, 0, axis_index_groups=groups, tiled=True)]
+    )
     stride = WAYS
     while stride < count:
-        total = add_four([total] + from_others([total] * WAYS, stride))
+        total = add_four([total] + from_others(total, stride))
         stride *= WAYS
-    quarters = [total] + from_others([total] * WAYS)
+    quarters = [total] + from_others(total)
     return gram_call(join_kernel, "join", quarters, (WAYS * rows, columns))
 
 
@@ -314,9 +319,10 @@
 
 
 def product3(left, right):
-    rows = left[0].shape[0]
-    both = dot(jnp.concatenate(left, axis=0), right[0])
-    return both[:rows] + both[rows:] + dot(left[0], right[1])
+    return dot(
+        jnp.concatenate([left[0], left[0], left[1]], axis=1),
+        jnp.concatenate([right[0], right[1], right[0]], axis=0),
+    )
 
 
 def product(left, right):
@@ -499,7 +505,7 @@
         return tile_rows(name, table, stored[name], sources, prev[name], cost)
 
     for step in range(STEPS):
-        first, final = step == 0, step == STEPS - 1
+        final = step == STEPS - 1
         if final:
             new_inner = rows("inner", even, odd, inner)
             even_halo = after(even_halo, new_inner)
@@ -507,17 +513,17 @@
         if final:
             flat = [value.reshape(-1, width) for value in (new_even, new_inner)]
             others = [sibling(value) for value in flat]
+            odd_halo = after(odd_halo, new_even)
         else:
             even_halo = exchange("even", new_even)
-        if first:
-            stored["inner"] = load_blocks(after(blocks, new_even))
-            odd_halo = after(odd_halo, stored["inner"])
-        odd_halo = after(odd_halo, new_even)
+            if step == 0:
+                stored["inner"] = load_blocks(after(blocks, new_even))
+            new_inner = rows("inner", after(even, new_even), odd, inner)
+            odd_halo = after(odd_halo, new_inner)
         new_odd = rows("odd", odd_halo, odd, inner, cost=LARGE if final else SMALL)
         if not final:
             odd_halo = exchange("odd", new_odd)
-            new_inner = rows("inner", after(even, new_odd), odd, inner)
-            even_halo = after(even_halo, new_inner)
+            even_halo = after(even_halo, new_odd)
         prev = {"even": even, "odd": odd, "inner": inner}
         even, odd, inner = new_even, new_odd, new_inner
     last = odd.reshape(-1, width)

time: 93.1 us -> 92.7 us (level)
  blocking collectives: 0 us -> 13.9 us
  starting transfers between devices: 28.7 us -> 18.1 us
  waiting for transfers between devices: 20.2 us -> 17.7 us
  Pallas kernels: 42.2 us -> 41 us
    all_to_all x0 -> x1, blocking collectives: none -> 13.9 us  [sum_over_patch(): lax.all_to_all(parts, 'patch', 0, 0, axis_index_groups=groups, tiled=True)]
    ppermute x9 -> x6, starting transfers between devices: 16.5 us -> 7.71 us  [from_others(): lax.ppermute(value, 'patch', [(i, i ^ d * stride) for i in range(count)])]
    ppermute x9 -> x6, waiting for transfers between devices: 12.2 us -> 8.42 us  [from_others(): lax.ppermute(value, 'patch', [(i, i ^ d * stride) for i in range(count)])]
    ppermute x6, waiting for transfers between devices: 5.46 us -> 7.67 us  [exchange(): return lax.ppermute(value, 'patch', pairs[name])]
    ppermute x6, starting transfers between devices: 11.4 us -> 9.64 us  [exchange(): return lax.ppermute(value, 'patch', pairs[name])]
  transfers between devices with their start and end apart: 19 -> 16, of which waited for: 11 -> 10; matrix products, arithmetic and copies ran while one was open for 0% -> 0% of each run, Pallas kernels for 25% -> 25%
where the time goes in v9:
time: 92.7 us; the launch traced here: 92.4 us
  Pallas kernels  41 us (44%)
  starting transfers between devices  18.1 us (20%)
  waiting for transfers between devices  17.7 us (19%)
  blocking collectives  13.9 us (15%)
  between operations  1.02 us (1%)
    pallas_call x1, Pallas kernels, rotate(): pl.pallas_call(body, in_specs=[VMEM, VMEM] + [ANY] * 6, out_specs=ANY, ou...  16 us
    pallas_call x9, Pallas kernels, tile_rows(): pl.pallas_call(functools.partial(rows_kernel, name), in_specs=[VMEM] * le...  15.4 us
    all_to_all x1, blocking collectives, sum_over_patch(): lax.all_to_all(parts, 'patch', 0, 0, axis_index_groups=groups, tiled=True)  13.9 us
    ppermute x6, starting transfers between devices, exchange(): return lax.ppermute(value, 'patch', pairs[name])  9.64 us
    ppermute x6, waiting for transfers between devices, from_others(): lax.ppermute(value, 'patch', [(i, i ^ d * stride) for i in range(count)])  8.42 us
    ppermute x6, starting transfers between devices, from_others(): lax.ppermute(value, 'patch', [(i, i ^ d * stride) for i in range(count)])  7.71 us
    ppermute x6, waiting for transfers between devices, exchange(): return lax.ppermute(value, 'patch', pairs[name])  7.67 us
    pallas_call x3, Pallas kernels, load_call(): pl.pallas_call(body, in_specs=[SMEM] * len(table) + [HBM] * len(args), ou...  7.5 us
  transfers between devices with their start and end apart: 16, of which 10 were waited for; matrix products, arithmetic and copies ran while one was open for 0% of the time, Pallas kernels for 25%

profile of v9, /device:TPU:0, one launch (start us, length us, event | category | flops | bytes accessed | tf_op | source)
XLA Modules:
  0.0 92.4 jit_solution(11492501811186250012)
XLA Ops:
  0.7 0.7 concatenate.3.table.table_ref
  1.3 1.8 %masked_edges.1 = (bf16[4,128,256]{2,1,0:T(8,128)(2,1)S(1)}, bf16[4,128,256]{2,1,0:T(8,128)(2,1)S(1)}) custom-call(s32[9,32]{1,0:T(8,128)S(1)} %concatenate.3.table.table_ref, bf16[32,128,256]{2,1,0:T(8,128)(2,1)} %bitcast.18), custom_call_target="tpu_custom_call" | custom-call | flops 1000 | bytes 1000 | tf_op jit(solution)/shard_map/masked_edges/pallas_call | solution.py:105
  3.2 3.0 %collective-permute-start.1 = (bf16[4,128,256]{2,1,0:T(8,128)(2,1)S(1)}, bf16[4,128,256]{2,1,0:T(8,128)(2,1)S(1)}, u32[]{:S(2)}, u32[]{:S(2)}) collective-permute-start(bf16[4,128,256]{2,1,0:T(8,128)(2,1)S(1)} %get-tuple-element.29.refs_1_.refs_0_.refs_3_), channel_id=1, source_target_pairs={{0,1},{1,0},{2,3},{3,2},{4,5},{5,4},{6,7},{7,6},{8,9},{9,8},{10,11... | collective-permute-start | bytes 786440 | tf_op jit(solution)/shard_map/ppermute | solution.py:489
  6.2 2.8 %load_fields.1 = (bf16[24,128,256]{2,1,0:T(8,128)(2,1)S(1)}, bf16[4,8,128,128]{3,2,1,0:T(8,128)(2,1)S(1)}, bf16[4,8,128,128]{3,2,1,0:T(8,128)(2,1)S(1)}) custom-call(s32[9,32]{1,0:T(8,128)S(1)} %concatenate.3.table.table_ref, bf16[32,128,256]{2,1,0:T(8,128)(2,1)} %bitcast.19, bf16[32,8,128,128]{3,2,1,0:T(8,128)(2,1)} %blocks_ref.2), custom_call_target="tpu_custom_call" | custom-call | flops 1000 | bytes 1000 | tf_op jit(solution)/shard_map/load_fields/pallas_call | solution.py:105
  9.0 0.7 collective-permute-start
  9.7 2.8 %collective-permute-done.1.refs_0_ = bf16[4,128,256]{2,1,0:T(8,128)(2,1)S(1)} collective-permute-done((bf16[4,128,256]{2,1,0:T(8,128)(2,1)S(1)}, bf16[4,128,256]{2,1,0:T(8,128)(2,1)S(1)}, u32[]{:S(2)}, u32[]{:S(2)}) %collective-permute-start.1) | collective-permute-done | bytes 262176 | tf_op jit(solution)/shard_map/ppermute | solution.py:489
  12.5 1.1 %rows_even.3.refs_1_.refs_0_.refs_3_ = bf16[4,128,256]{2,1,0:T(8,128)(2,1)S(1)} custom-call(s32[9,32]{1,0:T(8,128)S(1)} %concatenate.3.table.table_ref, bf16[4,128,256]{2,1,0:T(8,128)(2,1)S(1)} %collective-permute-done.1.refs_0_, bf16[4,128,256]{2,1,0:T(8,128)(2,1)S(1)} %get-tuple-element.29.refs_1_.refs_0_.refs_3_, ...), custom_call_target="tpu_custom_call" | custom-call | flops 1000 | bytes 1000 | tf_op jit(solution)/shard_map/rows_even/pallas_call | solution.py:182
  13.6 1.8 %collective-permute-start.3 = (bf16[4,128,256]{2,1,0:T(8,128)(2,1)S(1)}, bf16[4,128,256]{2,1,0:T(8,128)(2,1)S(1)}, u32[]{:S(2)}, u32[]{:S(2)}) collective-permute-start(bf16[4,128,256]{2,1,0:T(8,128)(2,1)S(1)} %rows_even.3.refs_1_.refs_0_.refs_3_), channel_id=1, source_target_pairs={{0,1},{1,0},{2,3},{3,2},{4,5},{5,4},{6,7},{7,6},{8,9},{9,8},{10,11... | collective-permute-start | bytes 786440 | tf_op jit(solution)/shard_map/ppermute | solution.py:489
  15.4 2.9 %load_blocks.1.refs_3_.refs_4_ = bf16[24,8,128,128]{3,2,1,0:T(8,128)(2,1)S(1)} custom-call(bf16[32,8,128,128]{3,2,1,0:T(8,128)(2,1)} %blocks_ref.2), custom_call_target="tpu_custom_call" | custom-call | flops 1000 | bytes 1000 | tf_op jit(solution)/shard_map/load_blocks/pallas_call | solution.py:105
  18.3 2.9 %rows_inner.3.refs_2_.refs_3_ = bf16[24,128,256]{2,1,0:T(8,128)(2,1)S(1)} custom-call(s32[9,32]{1,0:T(8,128)S(1)} %concatenate.3.table.table_ref, bf16[4,128,256]{2,1,0:T(8,128)(2,1)S(1)} %get-tuple-element.29.refs_1_.refs_0_.refs_3_, bf16[4,128,256]{2,1,0:T(8,128)(2,1)S(1)} %get-tuple-element.27.refs_1_.refs_3_, ...), custom_call_target="tpu_custom_call" | custom-call | flops 1000 | bytes 1000 | tf_op jit(solution)/shard_map/rows_inner/pallas_call | solution.py:182
  21.2 0.0 collective-permute-done.refs_0_
  21.2 1.1 %rows_odd.3.refs_1_.refs_3_ = bf16[4,128,256]{2,1,0:T(8,128)(2,1)S(1)} custom-call(s32[9,32]{1,0:T(8,128)S(1)} %concatenate.3.table.table_ref, bf16[4,128,256]{2,1,0:T(8,128)(2,1)S(1)} %collective-permute-done.refs_0_, bf16[4,128,256]{2,1,0:T(8,128)(2,1)S(1)} %get-tuple-element.27.refs_1_.refs_3_, ...), custom_call_target="tpu_custom_call" | custom-call | flops 1000 | bytes 1000 | tf_op jit(solution)/shard_map/rows_odd/pallas_call | solution.py:182
  22.3 0.7 collective-permute-start.2
  23.0 2.3 %collective-permute-done.3.refs_0_ = bf16[4,128,256]{2,1,0:T(8,128)(2,1)S(1)} collective-permute-done((bf16[4,128,256]{2,1,0:T(8,128)(2,1)S(1)}, bf16[4,128,256]{2,1,0:T(8,128)(2,1)S(1)}, u32[]{:S(2)}, u32[]{:S(2)}) %collective-permute-start.3) | collective-permute-done | bytes 262176 | tf_op jit(solution)/shard_map/ppermute | solution.py:489
  25.3 1.1 %rows_even.4.refs_0_.refs_1_ = bf16[4,128,256]{2,1,0:T(8,128)(2,1)S(1)} custom-call(s32[9,32]{1,0:T(8,128)S(1)} %concatenate.3.table.table_ref, bf16[4,128,256]{2,1,0:T(8,128)(2,1)S(1)} %collective-permute-done.3.refs_0_, bf16[4,128,256]{2,1,0:T(8,128)(2,1)S(1)} %rows_even.3.refs_1_.refs_0_.refs_3_, bf16[24,128,256]{2,1,0:T(8,128)(2,1)S(1)} %rows_inner.3.refs_2_.refs_3_, ...), custom_call_target="tpu_custom_call" | custom-call | flops 1000 | bytes 1000 | tf_op jit(solution)/shard_map/rows_even/pallas_call | solution.py:182
  26.4 2.8 %collective-permute-start.5 = (bf16[4,128,256]{2,1,0:T(8,128)(2,1)S(1)}, bf16[4,128,256]{2,1,0:T(8,128)(2,1)S(1)}, u32[]{:S(2)}, u32[]{:S(2)}) collective-permute-start(bf16[4,128,256]{2,1,0:T(8,128)(2,1)S(1)} %rows_even.4.refs_0_.refs_1_), channel_id=1, source_target_pairs={{0,1},{1,0},{2,3},{3,2},{4,5},{5,4},{6,7},{7,6},{8,9},{9,8},{10,11... | collective-permute-start | bytes 786440 | tf_op jit(solution)/shard_map/ppermute | solution.py:489
  29.2 2.9 %rows_inner.4.refs_2_ = bf16[24,128,256]{2,1,0:T(8,128)(2,1)S(1)} custom-call(s32[9,32]{1,0:T(8,128)S(1)} %concatenate.3.table.table_ref, bf16[4,128,256]{2,1,0:T(8,128)(2,1)S(1)} %rows_even.3.refs_1_.refs_0_.refs_3_, bf16[4,128,256]{2,1,0:T(8,128)(2,1)S(1)} %rows_odd.3.refs_1_.refs_3_, bf16[24,128,256]{2,1,0:T(8,128)(2,1)S(1)} %rows_inner.3.refs_2_.refs_3_, ...), custom_call_target="tpu_custom_call" | custom-call | flops 1000 | bytes 1000 | tf_op jit(solution)/shard_map/rows_inner/pallas_call | solution.py:182
  32.1 0.0 collective-permute-done.2.refs_0_
  32.1 1.1 %rows_odd.4.refs_1_ = bf16[4,128,256]{2,1,0:T(8,128)(2,1)S(1)} custom-call(s32[9,32]{1,0:T(8,128)S(1)} %concatenate.3.table.table_ref, bf16[4,128,256]{2,1,0:T(8,128)(2,1)S(1)} %collective-permute-done.2.refs_0_, bf16[4,128,256]{2,1,0:T(8,128)(2,1)S(1)} %rows_odd.3.refs_1_.refs_3_, bf16[24,128,256]{2,1,0:T(8,128)(2,1)S(1)} %rows_inner.3.refs_2_.refs_3_, ...), custom_call_target="tpu_custom_call" | custom-call | flops 1000 | bytes 1000 | tf_op jit(solution)/shard_map/rows_odd/pallas_call | solution.py:182
  33.3 0.7 collective-permute-start.4
  33.9 2.9 %rows_inner.5 = bf16[24,128,256]{2,1,0:T(8,128)(2,1)S(1)} custom-call(s32[9,32]{1,0:T(8,128)S(1)} %concatenate.3.table.table_ref, bf16[4,128,256]{2,1,0:T(8,128)(2,1)S(1)} %rows_even.4.refs_0_.refs_1_, bf16[4,128,256]{2,1,0:T(8,128)(2,1)S(1)} %rows_odd.4.refs_1_, bf16[24,128,256]{2,1,0:T(8,128)(2,1)S(1)} %rows_inner.4.refs_2_, ...), custom_call_target="tpu_custom_call" | custom-call | flops 1000 | bytes 1000 | tf_op jit(solution)/shard_map/rows_inner/pallas_call | solution.py:182
  36.8 0.1 collective-permute-start.8
  36.9 2.6 %collective-permute-done.5.refs_0_ = bf16[4,128,256]{2,1,0:T(8,128)(2,1)S(1)} collective-permute-done((bf16[4,128,256]{2,1,0:T(8,128)(2,1)S(1)}, bf16[4,128,256]{2,1,0:T(8,128)(2,1)S(1)}, u32[]{:S(2)}, u32[]{:S(2)}) %collective-permute-start.5) | collective-permute-done | bytes 262176 | tf_op jit(solution)/shard_map/ppermute | solution.py:489
  39.5 1.1 %rows_even.5 = bf16[4,128,256]{2,1,0:T(8,128)(2,1)S(1)} custom-call(s32[9,32]{1,0:T(8,128)S(1)} %concatenate.3.table.table_ref, bf16[4,128,256]{2,1,0:T(8,128)(2,1)S(1)} %collective-permute-done.5.refs_0_, bf16[4,128,256]{2,1,0:T(8,128)(2,1)S(1)} %rows_even.4.refs_0_.refs_1_, bf16[24,128,256]{2,1,0:T(8,128)(2,1)S(1)} %rows_inner.4.refs_2_, ...), custom_call_target="tpu_custom_call" | custom-call | flops 1000 | bytes 1000 | tf_op jit(solution)/shard_map/rows_even/pallas_call | solution.py:182
  40.6 0.0 collective-permute-done.4.refs_0_
  40.6 0.1 collective-permute-start.7
  40.7 1.1 %rows_odd.5 = bf16[4,128,256]{2,1,0:T(8,128)(2,1)S(1)} custom-call(s32[9,32]{1,0:T(8,128)S(1)} %concatenate.3.table.table_ref, bf16[4,128,256]{2,1,0:T(8,128)(2,1)S(1)} %collective-permute-done.4.refs_0_, bf16[4,128,256]{2,1,0:T(8,128)(2,1)S(1)} %rows_odd.4.refs_1_, bf16[24,128,256]{2,1,0:T(8,128)(2,1)S(1)} %rows_inner.4.refs_2_, ...), custom_call_target="tpu_custom_call" | custom-call | flops 99999997952 | bytes 1000 | tf_op jit(solution)/shard_map/rows_odd/pallas_call | solution.py:182
  41.8 0.6 collective-permute-start.6
  42.4 0.0 collective-permute-done.7.refs_2_.refs_3_
  42.4 0.0 collective-permute-done.8.refs_3_.refs_4_
  42.4 1.7 %gram.1.start_ref = f32[256,512]{1,0:T(8,128)S(1)} custom-call(bf16[512,256]{1,0:T(8,128)(2,1)S(1)} %bitcast.13, bf16[3072,256]{1,0:T(8,128)(2,1)S(1)} %bitcast.9, bf16[512,256]{1,0:T(8,128)(2,1)S(1)} %collective-permute-done.7.refs_2_.refs_3_, bf16[3072,256]{1,0:T(8,128)(2,1)S(1)} %collective-permute-done.8.refs_3_.refs_4_), custom_call_target="tpu_custom_call" | custom-call | flops 1000 | bytes 1000 | tf_op jit(solution)/shard_map/gram/pallas_call | solution.py:238
  44.1 0.0 collective-permute-done.6.other_ref.refs_5_
  44.1 0.3 gram_share.1
  44.5 13.9 %all_to_all.5.refs_0_ = f32[4,160,128]{2,1,0:T(8,128)S(1)} all-to-all(f32[4,160,128]{2,1,0:T(8,128)S(1)} %bitcast.11), channel_id=1, replica_groups={{0,1,2,3},{4,5,6,7},{8,9,10,11},{12,13,14,15},{16,17,18,19},{20,21,22,2..., dimensions={0} | all-to-all | bytes 655360 | tf_op jit(solution)/shard_map/all_to_all | solution.py:296
  58.4 2.6 %collective-permute-start.10 = (f32[160,128]{1,0:T(8,128)S(1)}, f32[160,128]{1,0:T(8,128)S(1)}, u32[]{:S(2)}, u32[]{:S(2)}) collective-permute-start(f32[160,128]{1,0:T(8,128)S(1)} %add_four.2.refs_0_), channel_id=1, source_target_pairs={{0,8},{1,9},{2,10},{3,11},{4,12},{5,13},{6,14},{7,15},{8,0},{9,1},... | collective-permute-start | bytes 245768 | tf_op jit(solution)/shard_map/ppermute | solution.py:290
  60.9 1.3 %collective-permute-start.11 = (f32[160,128]{1,0:T(8,128)S(1)}, f32[160,128]{1,0:T(8,128)S(1)}, u32[]{:S(2)}, u32[]{:S(2)}) collective-permute-start(f32[160,128]{1,0:T(8,128)S(1)} %add_four.2.refs_0_), channel_id=1, source_target_pairs={{0,12},{1,13},{2,14},{3,15},{4,8},{5,9},{6,10},{7,11},{8,4},{9,5},... | collective-permute-start | bytes 245768 | tf_op jit(solution)/shard_map/ppermute | solution.py:290
  62.3 0.2 collective-permute-start.9
  62.5 3.8 %collective-permute-done.10.refs_2_ = f32[160,128]{1,0:T(8,128)S(1)} collective-permute-done((f32[160,128]{1,0:T(8,128)S(1)}, f32[160,128]{1,0:T(8,128)S(1)}, u32[]{:S(2)}, u32[]{:S(2)}) %collective-permute-start.10) | collective-permute-done | bytes 81952 | tf_op jit(solution)/shard_map/ppermute | solution.py:290
  66.3 1.1 %collective-permute-done.11.refs_3_ = f32[160,128]{1,0:T(8,128)S(1)} collective-permute-done((f32[160,128]{1,0:T(8,128)S(1)}, f32[160,128]{1,0:T(8,128)S(1)}, u32[]{:S(2)}, u32[]{:S(2)}) %collective-permute-start.11) | collective-permute-done | bytes 81952 | tf_op jit(solution)/shard_map/ppermute | solution.py:290
  67.5 0.4 collective-permute-done.9.refs_1_
  67.9 0.7 collective-permute-start.12
  68.6 0.6 collective-permute-start.13
  69.2 2.2 %collective-permute-start.14 = (f32[160,128]{1,0:T(8,128)S(1)}, f32[160,128]{1,0:T(8,128)S(1)}, u32[]{:S(2)}, u32[]{:S(2)}) collective-permute-start(f32[160,128]{1,0:T(8,128)S(1)} %add_four.3.refs_0_), channel_id=1, source_target_pairs={{0,3},{1,2},{2,1},{3,0},{4,7},{5,6},{6,5},{7,4},{8,11},{9,10},{10,... | collective-permute-start | bytes 245768 | tf_op jit(solution)/shard_map/ppermute | solution.py:290
  71.4 1.0 %collective-permute-done.12.refs_1_ = f32[160,128]{1,0:T(8,128)S(1)} collective-permute-done((f32[160,128]{1,0:T(8,128)S(1)}, f32[160,128]{1,0:T(8,128)S(1)}, u32[]{:S(2)}, u32[]{:S(2)}) %collective-permute-start.12) | collective-permute-done | bytes 81952 | tf_op jit(solution)/shard_map/ppermute | solution.py:290
  72.4 0.7 collective-permute-done.13.refs_2_
  73.0 1.5 %collective-permute-done.14.refs_3_ = f32[160,128]{1,0:T(8,128)S(1)} collective-permute-done((f32[160,128]{1,0:T(8,128)S(1)}, f32[160,128]{1,0:T(8,128)S(1)}, u32[]{:S(2)}, u32[]{:S(2)}) %collective-permute-start.14) | collective-permute-done | bytes 81952 | tf_op jit(solution)/shard_map/ppermute | solution.py:290
  74.6 0.1 collective-permute-start.15
  74.6 1.6 %collective-permute-done.15.theirs = f32[640,128]{1,0:T(8,128)S(1)} collective-permute-done((f32[640,128]{1,0:T(8,128)S(1)}, f32[640,128]{1,0:T(8,128)S(1)}, u32[]{:S(2)}, u32[]{:S(2)}) %collective-permute-start.15) | collective-permute-done | bytes 327712 | tf_op jit(solution)/shard_map/ppermute | solution.py:492
  76.2 16.0 %rotate.1 = bf16[4096,256]{1,0:T(8,128)(2,1)} custom-call(f32[640,128]{1,0:T(8,128)S(1)} %join.1.mine, f32[640,128]{1,0:T(8,128)S(1)} %collective-permute-done.15.theirs, bf16[512,256]{1,0:T(8,128)(2,1)S(1)} %bitcast.14, bf16[3072,256]{1,0:T(8,128)(2,1)S(1)} %bitcast.10, bf16[512,256]{1,0:T(8,128)(2,1)S(1)} %bitcast.17, ...), custom_call_target="tpu_custom_call" | custom-call | flops 17985175552 | bytes 6291456 | tf_op jit(solution)/shard_map/rotate/pallas_call | solution.py:451
  (3 shorter events, 0.1 us)
Async XLA Ops:
  3.2 9.3 %collective-permute-start.1 = (bf16[4,128,256]{2,1,0:T(8,128)(2,1)S(1)}, bf16[4,128,256]{2,1,0:T(8,128)(2,1)S(1)}, u32[]{:S(2)}, u32[]{:S(2)}) collective-permute-start(bf16[4,128,256]{2,1,0:T(8,128)(2,1)S(1)} %get-tuple-element.29.refs_1_.refs_0_.refs_3_), channel_id=1, source_target_pairs={{0,1},{1,0},{2,3},{3,2},{4,5},{5,4},{6,7},{7,6},{8,9},{9,8},{10,11... | collective-permute-start | bytes 786440 | tf_op jit(solution)/shard_map/ppermute | solution.py:489
  9.0 12.2 %collective-permute-start = (bf16[4,128,256]{2,1,0:T(8,128)(2,1)S(1)}, bf16[4,128,256]{2,1,0:T(8,128)(2,1)S(1)}, u32[]{:S(2)}, u32[]{:S(2)}) collective-permute-start(bf16[4,128,256]{2,1,0:T(8,128)(2,1)S(1)} %get-tuple-element.27.refs_1_.refs_3_), channel_id=1, source_target_pairs={{1,2},{2,1},{3,4},{4,3},{5,6},{6,5},{7,8},{8,7},{9,10},{10,9},{11,... | collective-permute-start | bytes 786440 | tf_op jit(solution)/shard_map/ppermute | solution.py:489
  13.6 11.7 %collective-permute-start.3 = (bf16[4,128,256]{2,1,0:T(8,128)(2,1)S(1)}, bf16[4,128,256]{2,1,0:T(8,128)(2,1)S(1)}, u32[]{:S(2)}, u32[]{:S(2)}) collective-permute-start(bf16[4,128,256]{2,1,0:T(8,128)(2,1)S(1)} %rows_even.3.refs_1_.refs_0_.refs_3_), channel_id=1, source_target_pairs={{0,1},{1,0},{2,3},{3,2},{4,5},{5,4},{6,7},{7,6},{8,9},{9,8},{10,11... | collective-permute-start | bytes 786440 | tf_op jit(solution)/shard_map/ppermute | solution.py:489
  22.3 9.8 %collective-permute-start.2 = (bf16[4,128,256]{2,1,0:T(8,128)(2,1)S(1)}, bf16[4,128,256]{2,1,0:T(8,128)(2,1)S(1)}, u32[]{:S(2)}, u32[]{:S(2)}) collective-permute-start(bf16[4,128,256]{2,1,0:T(8,128)(2,1)S(1)} %rows_odd.3.refs_1_.refs_3_), channel_id=1, source_target_pairs={{1,2},{2,1},{3,4},{4,3},{5,6},{6,5},{7,8},{8,7},{9,10},{10,9},{11,... | collective-permute-start | bytes 786440 | tf_op jit(solution)/shard_map/ppermute | solution.py:489
  26.4 13.1 %collective-permute-start.5 = (bf16[4,128,256]{2,1,0:T(8,128)(2,1)S(1)}, bf16[4,128,256]{2,1,0:T(8,128)(2,1)S(1)}, u32[]{:S(2)}, u32[]{:S(2)}) collective-permute-start(bf16[4,128,256]{2,1,0:T(8,128)(2,1)S(1)} %rows_even.4.refs_0_.refs_1_), channel_id=1, source_target_pairs={{0,1},{1,0},{2,3},{3,2},{4,5},{5,4},{6,7},{7,6},{8,9},{9,8},{10,11... | collective-permute-start | bytes 786440 | tf_op jit(solution)/shard_map/ppermute | solution.py:489
  33.3 7.4 %collective-permute-start.4 = (bf16[4,128,256]{2,1,0:T(8,128)(2,1)S(1)}, bf16[4,128,256]{2,1,0:T(8,128)(2,1)S(1)}, u32[]{:S(2)}, u32[]{:S(2)}) collective-permute-start(bf16[4,128,256]{2,1,0:T(8,128)(2,1)S(1)} %rows_odd.4.refs_1_), channel_id=1, source_target_pairs={{1,2},{2,1},{3,4},{4,3},{5,6},{6,5},{7,8},{8,7},{9,10},{10,9},{11,... | collective-permute-start | bytes 786440 | tf_op jit(solution)/shard_map/ppermute | solution.py:489
  36.8 5.6 %collective-permute-start.8 = (bf16[3072,256]{1,0:T(8,128)(2,1)S(1)}, bf16[3072,256]{1,0:T(8,128)(2,1)S(1)}, u32[]{:S(2)}, u32[]{:S(2)}) collective-permute-start(bf16[3072,256]{1,0:T(8,128)(2,1)S(1)} %bitcast.8), channel_id=1, source_target_pairs={{0,16},{16,0},{1,17},{17,1},{2,18},{18,2},{3,19},{19,3},{4,20},{20... | collective-permute-start | bytes 4718600 | tf_op jit(solution)/shard_map/ppermute | solution.py:492
  40.6 1.8 %collective-permute-start.7 = (bf16[512,256]{1,0:T(8,128)(2,1)S(1)}, bf16[512,256]{1,0:T(8,128)(2,1)S(1)}, u32[]{:S(2)}, u32[]{:S(2)}) collective-permute-start(bf16[512,256]{1,0:T(8,128)(2,1)S(1)} %bitcast.12), channel_id=1, source_target_pairs={{0,16},{16,0},{1,17},{17,1},{2,18},{18,2},{3,19},{19,3},{4,20},{20... | collective-permute-start | bytes 786440 | tf_op jit(solution)/shard_map/ppermute | solution.py:492
  41.8 2.3 %collective-permute-start.6 = (bf16[512,256]{1,0:T(8,128)(2,1)S(1)}, bf16[512,256]{1,0:T(8,128)(2,1)S(1)}, u32[]{:S(2)}, u32[]{:S(2)}) collective-permute-start(bf16[512,256]{1,0:T(8,128)(2,1)S(1)} %bitcast.15), channel_id=1, source_target_pairs={{0,16},{16,0},{1,17},{17,1},{2,18},{18,2},{3,19},{19,3},{4,20},{20... | collective-permute-start | bytes 786440 | tf_op jit(solution)/shard_map/ppermute | solution.py:492
  58.4 8.0 %collective-permute-start.10 = (f32[160,128]{1,0:T(8,128)S(1)}, f32[160,128]{1,0:T(8,128)S(1)}, u32[]{:S(2)}, u32[]{:S(2)}) collective-permute-start(f32[160,128]{1,0:T(8,128)S(1)} %add_four.2.refs_0_), channel_id=1, source_target_pairs={{0,8},{1,9},{2,10},{3,11},{4,12},{5,13},{6,14},{7,15},{8,0},{9,1},... | collective-permute-start | bytes 245768 | tf_op jit(solution)/shard_map/ppermute | solution.py:290
  60.9 6.5 %collective-permute-start.11 = (f32[160,128]{1,0:T(8,128)S(1)}, f32[160,128]{1,0:T(8,128)S(1)}, u32[]{:S(2)}, u32[]{:S(2)}) collective-permute-start(f32[160,128]{1,0:T(8,128)S(1)} %add_four.2.refs_0_), channel_id=1, source_target_pairs={{0,12},{1,13},{2,14},{3,15},{4,8},{5,9},{6,10},{7,11},{8,4},{9,5},... | collective-permute-start | bytes 245768 | tf_op jit(solution)/shard_map/ppermute | solution.py:290
  62.3 5.6 %collective-permute-start.9 = (f32[160,128]{1,0:T(8,128)S(1)}, f32[160,128]{1,0:T(8,128)S(1)}, u32[]{:S(2)}, u32[]{:S(2)}) collective-permute-start(f32[160,128]{1,0:T(8,128)S(1)} %add_four.2.refs_0_), channel_id=1, source_target_pairs={{0,4},{1,5},{2,6},{3,7},{4,0},{5,1},{6,2},{7,3},{8,12},{9,13},{10,... | collective-permute-start | bytes 245768 | tf_op jit(solution)/shard_map/ppermute | solution.py:290
  67.9 4.5 %collective-permute-start.12 = (f32[160,128]{1,0:T(8,128)S(1)}, f32[160,128]{1,0:T(8,128)S(1)}, u32[]{:S(2)}, u32[]{:S(2)}) collective-permute-start(f32[160,128]{1,0:T(8,128)S(1)} %add_four.3.refs_0_), channel_id=1, source_target_pairs={{0,1},{1,0},{2,3},{3,2},{4,5},{5,4},{6,7},{7,6},{8,9},{9,8},{10,11... | collective-permute-start | bytes 245768 | tf_op jit(solution)/shard_map/ppermute | solution.py:290
  68.6 4.4 %collective-permute-start.13 = (f32[160,128]{1,0:T(8,128)S(1)}, f32[160,128]{1,0:T(8,128)S(1)}, u32[]{:S(2)}, u32[]{:S(2)}) collective-permute-start(f32[160,128]{1,0:T(8,128)S(1)} %add_four.3.refs_0_), channel_id=1, source_target_pairs={{0,2},{1,3},{2,0},{3,1},{4,6},{5,7},{6,4},{7,5},{8,10},{9,11},{10,... | collective-permute-start | bytes 245768 | tf_op jit(solution)/shard_map/ppermute | solution.py:290
  69.2 5.3 %collective-permute-start.14 = (f32[160,128]{1,0:T(8,128)S(1)}, f32[160,128]{1,0:T(8,128)S(1)}, u32[]{:S(2)}, u32[]{:S(2)}) collective-permute-start(f32[160,128]{1,0:T(8,128)S(1)} %add_four.3.refs_0_), channel_id=1, source_target_pairs={{0,3},{1,2},{2,1},{3,0},{4,7},{5,6},{6,5},{7,4},{8,11},{9,10},{10,... | collective-permute-start | bytes 245768 | tf_op jit(solution)/shard_map/ppermute | solution.py:290
  74.6 1.7 %collective-permute-start.15 = (f32[640,128]{1,0:T(8,128)S(1)}, f32[640,128]{1,0:T(8,128)S(1)}, u32[]{:S(2)}, u32[]{:S(2)}) collective-permute-start(f32[640,128]{1,0:T(8,128)S(1)} %join.1.mine), channel_id=1, source_target_pairs={{0,16},{16,0},{1,17},{17,1},{2,18},{18,2},{3,19},{19,3},{4,20},{20... | collective-permute-start | bytes 983048 | tf_op jit(solution)/shard_map/ppermute | solution.py:492

commit v10 on v8

--- a/solution.py
+++ b/solution.py
@@ -12,6 +12,7 @@
 ITERS = 8
 WAYS = 4
 LOAD_CUTS = 4
+GRAM_ROWS = 1024
 GROUP = 8
 
 SMALL = pl.CostEstimate(flops=1000, bytes_accessed=1000, transcendentals=0)
@@ -198,6 +199,8 @@
 
 
 def add_gram(chunk, own_ref, other_ref, total):
+    chunk = min(chunk, own_ref.shape[0])
+
     def add(index, carry):
         rows = pl.ds(pl.multiple_of(index * chunk, chunk), chunk)
         own = own_ref[rows, :]
@@ -249,8 +252,8 @@
 
 
 def gram(owns, others):
-    chunk, width = min(own.shape[0] for own in owns), owns[0].shape[1]
-    body = functools.partial(gram_kernel, chunk)
+    width = owns[0].shape[1]
+    body = functools.partial(gram_kernel, GRAM_ROWS)
     return gram_call(body, "gram", owns + others, (width, 2 * width))
 
 
@@ -260,8 +263,7 @@
     body = functools.partial(share_kernel, rows)
     scratch = [pltpu.VMEM((width, 2 * width), F32), pltpu.VMEM((5 * half, half), F32)]
     shape = (5 * half // WAYS, half)
-    args = [own, other, start]
-    return gram_call(body, "gram_share", args, shape, scratch, outs=WAYS)
+    return gram_call(body, "gram_share", [own, other, start], shape, scratch, outs=WAYS)
 
 
 def add_kernel(a, b, c, d, out):
@@ -314,20 +316,23 @@
 
 
 def product3(left, right):
-    rows = left[0].shape[0]
-    both = dot(jnp.concatenate(left, axis=0), right[0])
-    return both[:rows] + both[rows:] + dot(left[0], right[1])
-
-
-def product(left, right):
-    width = left.shape[1] // 2
-    first = product3(
-        (left[0, :width, :], left[1, :width, :]), (right[0], right[1])
+    return dot(
+        jnp.concatenate([left[0], left[0], left[1]], axis=1),
+        jnp.concatenate([right[0], right[1], right[0]], axis=0),
     )
-    second = product3(
-        (right[0, width:, :], right[1, width:, :]), (left[0, :, width:], left[1, :, width:])
-    )
-    return first[:, :width], first[:, width:], second
+
+
+def product(lefts, right):
+    width = right.shape[1] // 2
+    rows = [jnp.concatenate([left[i, :width, :] for left in lefts], axis=0) for i in range(2)]
+    cols = [jnp.concatenate([left[i, :, width:] for left in lefts], axis=1) for i in range(2)]
+    first = product3(rows, (right[0], right[1]))
+    second = product3((right[0, width:, :], right[1, width:, :]), cols)
+    out = []
+    for i in range(len(lefts)):
+        at = slice(i * width, (i + 1) * width)
+        out.append((first[at, :width], first[at, width:], second[:, at]))
+    return out
 
 
 def combine(*terms, unit=0.0):
@@ -342,7 +347,7 @@
     return tuple(out)
 
 
-def finish_kernel(total_rows, chunk, mine, theirs, *refs):
+def finish_kernel(total_rows, chunk, names, mine, theirs, *refs):
     fields, out_ref = refs[:6], refs[6]
     x_ref, x_held, x_pair, q_pair, u_pair, n_pair, v_pair, z_pair = refs[7:15]
     wide, result, sem, out_sem = refs[15:]
@@ -352,7 +357,7 @@
     half = width // 2
     edge_size = fields[0].shape[0]
     end = wide.shape[0] - edge_size
-    starts = [at_end("even") * end, edge_size, at_end("odd") * end]
+    starts = [at_end(names[0]) * end, edge_size, at_end(names[1]) * end]
     copies = []
     for i, source in enumerate(fields):
         rows = pl.ds(pl.multiple_of(starts[i % 3], edge_size), source.shape[0])
@@ -390,20 +395,23 @@
 
     def two_sweeps(first=False, last=False):
         x = tuple(x_held[i] for i in range(3))
-        q = product(x_pair, x_pair)
+        (q,) = product([x_pair], x_pair)
         put(q_pair, q)
         put(u_pair, combine((0.0625, q), (-0.5625, x), unit=1.6875), right=True)
-        qu = product(q_pair, u_pair)
+        (qu,) = product([q_pair], u_pair)
         x = tuple(x_held[i] for i in range(3))
         n = combine((1.0, qu), (-2.4375, x), unit=2.25)
         put(n_pair, n, right=True)
-        if not last:
-            put(v_pair, product(x_pair, n_pair))
-        z = n if first else product(z_pair, n_pair)
         if last:
-            return z
+            return product([z_pair], n_pair)[0]
+        if first:
+            z = n
+            (v,) = product([x_pair], n_pair)
+        else:
+            v, z = product([x_pair, z_pair], n_pair)
+        put(v_pair, v)
         put(z_pair, z)
-        set_x(product(v_pair, n_pair))
+        set_x(product([v_pair], n_pair)[0])
 
     set_x(tuple(value / norm for value in gram))
     two_sweeps(first=True)
@@ -435,12 +443,12 @@
         out.wait()
 
 
-def rotate(mine, theirs, owns, others, total_rows):
+def rotate(mine, theirs, owns, others, total_rows, names):
     width = owns[0].shape[1]
     rows = sum(own.shape[0] for own in owns)
     size = 2 * width
     chunk = min(rows, 512)
-    body = functools.partial(finish_kernel, float(total_rows), chunk)
+    body = functools.partial(finish_kernel, float(total_rows), chunk, names)
     pair = pltpu.VMEM((2, size, size), BF16)
     return pl.pallas_call(
         body,
@@ -488,45 +496,48 @@
     start = vectors.reshape(tiles, tile, width)
     table = jnp.concatenate([tile_cols.T, jnp.broadcast_to(live_tiles[None], (1, tiles))])
 
-    even, odd = masked_edges(table, start)
-    even_halo = exchange("even", even)
-    inner, even_blocks, odd_blocks = load_fields(after(table, even), start, blocks)
-    odd_halo = exchange("odd", after(odd, inner))
-    stored = {"even": even_blocks, "odd": odd_blocks}
+    edges = dict(zip(("even", "odd"), masked_edges(table, start)))
+    lead, lag = "odd", "even"
+    halo = {lead: exchange(lead, edges[lead])}
+    inner, *edge_blocks = load_fields(after(table, edges[lead]), start, blocks)
+    halo[lag] = exchange(lag, after(edges[lag], inner))
+    stored = dict(zip(("even", "odd"), edge_blocks))
     prev = dict.fromkeys(("even", "odd", "inner"))
 
-    def rows(name, *sources, cost=SMALL):
+    def inner_rows(behind):
+        sources = after(edges["even"], behind), edges["odd"], inner
+        return tile_rows("inner", table, stored["inner"], sources, prev["inner"], SMALL)
+
+    def edge_rows(name, behind, cost=SMALL):
+        sources = after(halo[name], behind), edges[name], inner
         return tile_rows(name, table, stored[name], sources, prev[name], cost)
 
     for step in range(STEPS):
-        first, final = step == 0, step == STEPS - 1
+        final = step == STEPS - 1
+        new = {}
         if final:
-            new_inner = rows("inner", even, odd, inner)
-            even_halo = after(even_halo, new_inner)
-        new_even = rows("even", even_halo, even, inner)
-        if final:
-            flat = [value.reshape(-1, width) for value in (new_even, new_inner)]
+            new["inner"] = inner_rows(edges["odd"])
+            new[lead] = edge_rows(lead, new["inner"])
+            flat = [new[name].reshape(-1, width) for name in (lead, "inner")]
             others = [sibling(value) for value in flat]
+            new[lag] = edge_rows(lag, new[lead], LARGE)
         else:
-            even_halo = exchange("even", new_even)
-        if first:
-            stored["inner"] = load_blocks(after(blocks, new_even))
-            odd_halo = after(odd_halo, stored["inner"])
-        odd_halo = after(odd_halo, new_even)
-        new_odd = rows("odd", odd_halo, odd, inner, cost=LARGE if final else SMALL)
-        if not final:
-            odd_halo = exchange("odd", new_odd)
-            new_inner = rows("inner", after(even, new_odd), odd, inner)
-            even_halo = after(even_halo, new_inner)
-        prev = {"even": even, "odd": odd, "inner": inner}
-        even, odd, inner = new_even, new_odd, new_inner
-    last = odd.reshape(-1, width)
+            new[lead] = edge_rows(lead, inner)
+            halo[lead] = exchange(lead, new[lead])
+            new[lag] = edge_rows(lag, new[lead])
+            halo[lag] = exchange(lag, new[lag])
+            if step == 0:
+                stored["inner"] = load_blocks(after(blocks, new[lag]))
+            new["inner"] = inner_rows(new[lag])
+        prev = dict(edges, inner=inner)
+        edges, inner = {name: new[name] for name in edges}, new["inner"]
+    last = edges[lag].reshape(-1, width)
     other_last = sibling(last)
     others = [after(other, last) for other in others]
     mine = sum_over_patch(gram_share(last, other_last, gram(flat, others)))
     theirs = sibling(mine)
     total_rows = tiles * tile * count
-    return rotate(mine, theirs, flat + [last], others + [other_last], total_rows)
+    return rotate(mine, theirs, flat + [last], others + [other_last], total_rows, (lead, lag))
 
 
 def solution(mesh):

time: 93.1 us -> 93.1 us (level)
  waiting for transfers between devices: 20.2 us -> 24.2 us
  starting transfers between devices: 28.7 us -> 25.9 us
  Pallas kernels: 42.2 us -> 41 us
    ppermute x9, starting transfers between devices: 16.5 us -> 12.1 us  [from_others(): lax.ppermute(values[d], 'patch', [(i, i ^ d * stride) for i in range(coun...]
    ppermute x6, waiting for transfers between devices: 5.46 us -> 9.55 us  [exchange(): return lax.ppermute(value, 'patch', pairs[name])]
    ppermute x6, starting transfers between devices: 11.4 us -> 13.1 us  [exchange(): return lax.ppermute(value, 'patch', pairs[name])]
  transfers between devices with their start and end apart: 19 -> 19, of which waited for: 11 -> 11; matrix products, arithmetic and copies ran while one was open for 0% -> 0% of each run, Pallas kernels for 25% -> 24%
where the time goes in v10:
time: 93.1 us; the launch traced here: 92.8 us
  Pallas kernels  41 us (44%)
  starting transfers between devices  25.9 us (28%)
  waiting for transfers between devices  24.2 us (26%)
  between operations  1.04 us (1%)
    pallas_call x1, Pallas kernels, rotate(): pl.pallas_call(body, in_specs=[VMEM, VMEM] + [ANY] * 6, out_specs=ANY, ou...  16 us
    pallas_call x9, Pallas kernels, tile_rows(): pl.pallas_call(functools.partial(rows_kernel, name), in_specs=[VMEM] * le...  15.4 us
    ppermute x6, starting transfers between devices, exchange(): return lax.ppermute(value, 'patch', pairs[name])  13.1 us
    ppermute x9, waiting for transfers between devices, from_others(): lax.ppermute(values[d], 'patch', [(i, i ^ d * stride) for i in range(coun...  13 us
    ppermute x9, starting transfers between devices, from_others(): lax.ppermute(values[d], 'patch', [(i, i ^ d * stride) for i in range(coun...  12.1 us
    ppermute x6, waiting for transfers between devices, exchange(): return lax.ppermute(value, 'patch', pairs[name])  9.55 us
    pallas_call x3, Pallas kernels, load_call(): pl.pallas_call(body, in_specs=[SMEM] * len(table) + [HBM] * len(args), ou...  7.44 us
    pallas_call x5, Pallas kernels, gram_call(): pl.pallas_call(body, in_specs=[VMEM] * len(args), out_specs=[VMEM] * outs...  2.13 us
  transfers between devices with their start and end apart: 19, of which 11 were waited for; matrix products, arithmetic and copies ran while one was open for 0% of the time, Pallas kernels for 24%

profile of v10, /device:TPU:0, one launch (start us, length us, event | category | flops | bytes accessed | tf_op | source)
XLA Modules:
  0.0 92.8 jit_solution(18074782287225822201)
XLA Ops:
  0.7 0.7 concatenate.3.table.table_ref
  1.3 1.8 %masked_edges.1 = (bf16[4,128,256]{2,1,0:T(8,128)(2,1)S(1)}, bf16[4,128,256]{2,1,0:T(8,128)(2,1)S(1)}) custom-call(s32[9,32]{1,0:T(8,128)S(1)} %concatenate.3.table.table_ref, bf16[32,128,256]{2,1,0:T(8,128)(2,1)} %bitcast.16), custom_call_target="tpu_custom_call" | custom-call | flops 1000 | bytes 1000 | tf_op jit(solution)/shard_map/masked_edges/pallas_call | solution.py:105
  3.2 0.7 collective-permute-start.1
  3.8 2.8 %load_fields.1 = (bf16[24,128,256]{2,1,0:T(8,128)(2,1)S(1)}, bf16[4,8,128,128]{3,2,1,0:T(8,128)(2,1)S(1)}, bf16[4,8,128,128]{3,2,1,0:T(8,128)(2,1)S(1)}) custom-call(s32[9,32]{1,0:T(8,128)S(1)} %concatenate.3.table.table_ref, bf16[32,128,256]{2,1,0:T(8,128)(2,1)} %bitcast.17, bf16[32,8,128,128]{3,2,1,0:T(8,128)(2,1)} %blocks_ref.2), custom_call_target="tpu_custom_call" | custom-call | flops 1000 | bytes 1000 | tf_op jit(solution)/shard_map/load_fields/pallas_call | solution.py:105
  6.6 5.8 %collective-permute-start = (bf16[4,128,256]{2,1,0:T(8,128)(2,1)S(1)}, bf16[4,128,256]{2,1,0:T(8,128)(2,1)S(1)}, u32[]{:S(2)}, u32[]{:S(2)}) collective-permute-start(bf16[4,128,256]{2,1,0:T(8,128)(2,1)S(1)} %get-tuple-element.37.refs_1_.refs_0_.refs_3_), channel_id=1, source_target_pairs={{0,1},{1,0},{2,3},{3,2},{4,5},{5,4},{6,7},{7,6},{8,9},{9,8},{10,11... | collective-permute-start | bytes 786440 | tf_op jit(solution)/shard_map/ppermute | solution.py:491
  12.5 0.0 collective-permute-done.1.refs_0_
  12.5 1.1 %rows_odd.3.refs_1_.refs_3_ = bf16[4,128,256]{2,1,0:T(8,128)(2,1)S(1)} custom-call(s32[9,32]{1,0:T(8,128)S(1)} %concatenate.3.table.table_ref, bf16[4,128,256]{2,1,0:T(8,128)(2,1)S(1)} %collective-permute-done.1.refs_0_, bf16[4,128,256]{2,1,0:T(8,128)(2,1)S(1)} %get-tuple-element.29.refs_1_.refs_3_, ...), custom_call_target="tpu_custom_call" | custom-call | flops 1000 | bytes 1000 | tf_op jit(solution)/shard_map/rows_odd/pallas_call | solution.py:182
  13.6 0.7 collective-permute-start.3
  14.3 7.0 %collective-permute-done.refs_0_ = bf16[4,128,256]{2,1,0:T(8,128)(2,1)S(1)} collective-permute-done((bf16[4,128,256]{2,1,0:T(8,128)(2,1)S(1)}, bf16[4,128,256]{2,1,0:T(8,128)(2,1)S(1)}, u32[]{:S(2)}, u32[]{:S(2)}) %collective-permute-start) | collective-permute-done | bytes 262176 | tf_op jit(solution)/shard_map/ppermute | solution.py:491
  21.2 1.1 %rows_even.3.refs_1_.refs_0_.refs_3_ = bf16[4,128,256]{2,1,0:T(8,128)(2,1)S(1)} custom-call(s32[9,32]{1,0:T(8,128)S(1)} %concatenate.3.table.table_ref, bf16[4,128,256]{2,1,0:T(8,128)(2,1)S(1)} %collective-permute-done.refs_0_, bf16[4,128,256]{2,1,0:T(8,128)(2,1)S(1)} %get-tuple-element.37.refs_1_.refs_0_.refs_3_, ...), custom_call_target="tpu_custom_call" | custom-call | flops 1000 | bytes 1000 | tf_op jit(solution)/shard_map/rows_even/pallas_call | solution.py:182
  22.4 2.4 %collective-permute-start.2 = (bf16[4,128,256]{2,1,0:T(8,128)(2,1)S(1)}, bf16[4,128,256]{2,1,0:T(8,128)(2,1)S(1)}, u32[]{:S(2)}, u32[]{:S(2)}) collective-permute-start(bf16[4,128,256]{2,1,0:T(8,128)(2,1)S(1)} %rows_even.3.refs_1_.refs_0_.refs_3_), channel_id=1, source_target_pairs={{0,1},{1,0},{2,3},{3,2},{4,5},{5,4},{6,7},{7,6},{8,9},{9,8},{10,11... | collective-permute-start | bytes 786440 | tf_op jit(solution)/shard_map/ppermute | solution.py:491
  24.7 2.9 %load_blocks.1.refs_3_.refs_4_ = bf16[24,8,128,128]{3,2,1,0:T(8,128)(2,1)S(1)} custom-call(bf16[32,8,128,128]{3,2,1,0:T(8,128)(2,1)} %blocks_ref.2), custom_call_target="tpu_custom_call" | custom-call | flops 1000 | bytes 1000 | tf_op jit(solution)/shard_map/load_blocks/pallas_call | solution.py:105
  27.6 2.9 %rows_inner.3.refs_2_.refs_3_ = bf16[24,128,256]{2,1,0:T(8,128)(2,1)S(1)} custom-call(s32[9,32]{1,0:T(8,128)S(1)} %concatenate.3.table.table_ref, bf16[4,128,256]{2,1,0:T(8,128)(2,1)S(1)} %get-tuple-element.37.refs_1_.refs_0_.refs_3_, bf16[4,128,256]{2,1,0:T(8,128)(2,1)S(1)} %get-tuple-element.29.refs_1_.refs_3_, ...), custom_call_target="tpu_custom_call" | custom-call | flops 1000 | bytes 1000 | tf_op jit(solution)/shard_map/rows_inner/pallas_call | solution.py:182
  30.5 0.0 collective-permute-done.3.refs_0_
  30.5 1.1 %rows_odd.4.refs_1_ = bf16[4,128,256]{2,1,0:T(8,128)(2,1)S(1)} custom-call(s32[9,32]{1,0:T(8,128)S(1)} %concatenate.3.table.table_ref, bf16[4,128,256]{2,1,0:T(8,128)(2,1)S(1)} %collective-permute-done.3.refs_0_, bf16[4,128,256]{2,1,0:T(8,128)(2,1)S(1)} %rows_odd.3.refs_1_.refs_3_, bf16[24,128,256]{2,1,0:T(8,128)(2,1)S(1)} %rows_inner.3.refs_2_.refs_3_, ...), custom_call_target="tpu_custom_call" | custom-call | flops 1000 | bytes 1000 | tf_op jit(solution)/shard_map/rows_odd/pallas_call | solution.py:182
  31.6 0.9 collective-permute-start.5
  32.5 0.6 collective-permute-done.2.refs_0_
  33.1 1.1 %rows_even.4.refs_0_.refs_1_ = bf16[4,128,256]{2,1,0:T(8,128)(2,1)S(1)} custom-call(s32[9,32]{1,0:T(8,128)S(1)} %concatenate.3.table.table_ref, bf16[4,128,256]{2,1,0:T(8,128)(2,1)S(1)} %collective-permute-done.2.refs_0_, bf16[4,128,256]{2,1,0:T(8,128)(2,1)S(1)} %rows_even.3.refs_1_.refs_0_.refs_3_, bf16[24,128,256]{2,1,0:T(8,128)(2,1)S(1)} %rows_inner.3.refs_2_.refs_3_, ...), custom_call_target="tpu_custom_call" | custom-call | flops 1000 | bytes 1000 | tf_op jit(solution)/shard_map/rows_even/pallas_call | solution.py:182
  34.2 2.7 %collective-permute-start.4 = (bf16[4,128,256]{2,1,0:T(8,128)(2,1)S(1)}, bf16[4,128,256]{2,1,0:T(8,128)(2,1)S(1)}, u32[]{:S(2)}, u32[]{:S(2)}) collective-permute-start(bf16[4,128,256]{2,1,0:T(8,128)(2,1)S(1)} %rows_even.4.refs_0_.refs_1_), channel_id=1, source_target_pairs={{0,1},{1,0},{2,3},{3,2},{4,5},{5,4},{6,7},{7,6},{8,9},{9,8},{10,11... | collective-permute-start | bytes 786440 | tf_op jit(solution)/shard_map/ppermute | solution.py:491
  36.9 2.9 %rows_inner.4.refs_2_ = bf16[24,128,256]{2,1,0:T(8,128)(2,1)S(1)} custom-call(s32[9,32]{1,0:T(8,128)S(1)} %concatenate.3.table.table_ref, bf16[4,128,256]{2,1,0:T(8,128)(2,1)S(1)} %rows_even.3.refs_1_.refs_0_.refs_3_, bf16[4,128,256]{2,1,0:T(8,128)(2,1)S(1)} %rows_odd.3.refs_1_.refs_3_, bf16[24,128,256]{2,1,0:T(8,128)(2,1)S(1)} %rows_inner.3.refs_2_.refs_3_, ...), custom_call_target="tpu_custom_call" | custom-call | flops 1000 | bytes 1000 | tf_op jit(solution)/shard_map/rows_inner/pallas_call | solution.py:182
  39.8 2.9 %rows_inner.5 = bf16[24,128,256]{2,1,0:T(8,128)(2,1)S(1)} custom-call(s32[9,32]{1,0:T(8,128)S(1)} %concatenate.3.table.table_ref, bf16[4,128,256]{2,1,0:T(8,128)(2,1)S(1)} %rows_even.4.refs_0_.refs_1_, bf16[4,128,256]{2,1,0:T(8,128)(2,1)S(1)} %rows_odd.4.refs_1_, bf16[24,128,256]{2,1,0:T(8,128)(2,1)S(1)} %rows_inner.4.refs_2_, ...), custom_call_target="tpu_custom_call" | custom-call | flops 1000 | bytes 1000 | tf_op jit(solution)/shard_map/rows_inner/pallas_call | solution.py:182
  42.7 0.1 collective-permute-start.8
  42.8 0.0 collective-permute-done.5.refs_0_
  42.8 1.1 %rows_odd.5 = bf16[4,128,256]{2,1,0:T(8,128)(2,1)S(1)} custom-call(s32[9,32]{1,0:T(8,128)S(1)} %concatenate.3.table.table_ref, bf16[4,128,256]{2,1,0:T(8,128)(2,1)S(1)} %collective-permute-done.5.refs_0_, bf16[4,128,256]{2,1,0:T(8,128)(2,1)S(1)} %rows_odd.4.refs_1_, bf16[24,128,256]{2,1,0:T(8,128)(2,1)S(1)} %rows_inner.4.refs_2_, ...), custom_call_target="tpu_custom_call" | custom-call | flops 1000 | bytes 1000 | tf_op jit(solution)/shard_map/rows_odd/pallas_call | solution.py:182
  43.9 2.0 %collective-permute-done.4.refs_0_ = bf16[4,128,256]{2,1,0:T(8,128)(2,1)S(1)} collective-permute-done((bf16[4,128,256]{2,1,0:T(8,128)(2,1)S(1)}, bf16[4,128,256]{2,1,0:T(8,128)(2,1)S(1)}, u32[]{:S(2)}, u32[]{:S(2)}) %collective-permute-start.4) | collective-permute-done | bytes 262176 | tf_op jit(solution)/shard_map/ppermute | solution.py:491
  45.9 0.0 collective-permute-start.7
  45.9 1.1 %rows_even.5 = bf16[4,128,256]{2,1,0:T(8,128)(2,1)S(1)} custom-call(s32[9,32]{1,0:T(8,128)S(1)} %concatenate.3.table.table_ref, bf16[4,128,256]{2,1,0:T(8,128)(2,1)S(1)} %collective-permute-done.4.refs_0_, bf16[4,128,256]{2,1,0:T(8,128)(2,1)S(1)} %rows_even.4.refs_0_.refs_1_, bf16[24,128,256]{2,1,0:T(8,128)(2,1)S(1)} %rows_inner.4.refs_2_, ...), custom_call_target="tpu_custom_call" | custom-call | flops 99999997952 | bytes 1000 | tf_op jit(solution)/shard_map/rows_even/pallas_call | solution.py:182
  47.1 0.6 collective-permute-start.6
  47.6 0.0 collective-permute-done.7.refs_2_.refs_3_
  47.6 0.0 collective-permute-done.8.refs_3_.refs_4_
  47.6 1.7 %gram.1.start_ref = f32[256,512]{1,0:T(8,128)S(1)} custom-call(bf16[512,256]{1,0:T(8,128)(2,1)S(1)} %bitcast.11, bf16[3072,256]{1,0:T(8,128)(2,1)S(1)} %bitcast.8, bf16[512,256]{1,0:T(8,128)(2,1)S(1)} %collective-permute-done.7.refs_2_.refs_3_, bf16[3072,256]{1,0:T(8,128)(2,1)S(1)} %collective-permute-done.8.refs_3_.refs_4_), custom_call_target="tpu_custom_call" | custom-call | flops 1000 | bytes 1000 | tf_op jit(solution)/shard_map/gram/pallas_call | solution.py:242
  49.4 0.0 collective-permute-done.6.other_ref.refs_5_
  49.4 0.3 gram_share.1
  49.7 2.5 %collective-permute-start.9 = (f32[160,128]{1,0:T(8,128)S(1)}, f32[160,128]{1,0:T(8,128)S(1)}, u32[]{:S(2)}, u32[]{:S(2)}) collective-permute-start(f32[160,128]{1,0:T(8,128)S(1)} %get-tuple-element.48), channel_id=1, source_target_pairs={{0,1},{1,0},{2,3},{3,2},{4,5},{5,4},{6,7},{7,6},{8,9},{9,8},{10,11... | collective-permute-start | bytes 245768 | tf_op jit(solution)/shard_map/ppermute | solution.py:290
  52.3 0.4 collective-permute-start.10
  52.7 1.1 %collective-permute-start.11 = (f32[160,128]{1,0:T(8,128)S(1)}, f32[160,128]{1,0:T(8,128)S(1)}, u32[]{:S(2)}, u32[]{:S(2)}) collective-permute-start(f32[160,128]{1,0:T(8,128)S(1)} %get-tuple-element.50), channel_id=1, source_target_pairs={{0,3},{1,2},{2,1},{3,0},{4,7},{5,6},{6,5},{7,4},{8,11},{9,10},{10,... | collective-permute-start | bytes 245768 | tf_op jit(solution)/shard_map/ppermute | solution.py:290
  53.8 1.1 %collective-permute-done.9.b = f32[160,128]{1,0:T(8,128)S(1)} collective-permute-done((f32[160,128]{1,0:T(8,128)S(1)}, f32[160,128]{1,0:T(8,128)S(1)}, u32[]{:S(2)}, u32[]{:S(2)}) %collective-permute-start.9) | collective-permute-done | bytes 81952 | tf_op jit(solution)/shard_map/ppermute | solution.py:290
  54.9 3.4 %collective-permute-done.10.c = f32[160,128]{1,0:T(8,128)S(1)} collective-permute-done((f32[160,128]{1,0:T(8,128)S(1)}, f32[160,128]{1,0:T(8,128)S(1)}, u32[]{:S(2)}, u32[]{:S(2)}) %collective-permute-start.10) | collective-permute-done | bytes 81952 | tf_op jit(solution)/shard_map/ppermute | solution.py:290
  58.3 0.0 collective-permute-done.11.d
  58.3 2.1 %collective-permute-start.14 = (f32[160,128]{1,0:T(8,128)S(1)}, f32[160,128]{1,0:T(8,128)S(1)}, u32[]{:S(2)}, u32[]{:S(2)}) collective-permute-start(f32[160,128]{1,0:T(8,128)S(1)} %add_four.2.a), channel_id=1, source_target_pairs={{0,12},{1,13},{2,14},{3,15},{4,8},{5,9},{6,10},{7,11},{8,4},{9,5},... | collective-permute-start | bytes 245768 | tf_op jit(solution)/shard_map/ppermute | solution.py:290
  60.4 1.7 %collective-permute-start.13 = (f32[160,128]{1,0:T(8,128)S(1)}, f32[160,128]{1,0:T(8,128)S(1)}, u32[]{:S(2)}, u32[]{:S(2)}) collective-permute-start(f32[160,128]{1,0:T(8,128)S(1)} %add_four.2.a), channel_id=1, source_target_pairs={{0,8},{1,9},{2,10},{3,11},{4,12},{5,13},{6,14},{7,15},{8,0},{9,1},... | collective-permute-start | bytes 245768 | tf_op jit(solution)/shard_map/ppermute | solution.py:290
  62.1 0.7 collective-permute-start.12
  62.8 2.4 %collective-permute-done.14.d = f32[160,128]{1,0:T(8,128)S(1)} collective-permute-done((f32[160,128]{1,0:T(8,128)S(1)}, f32[160,128]{1,0:T(8,128)S(1)}, u32[]{:S(2)}, u32[]{:S(2)}) %collective-permute-start.14) | collective-permute-done | bytes 81952 | tf_op jit(solution)/shard_map/ppermute | solution.py:290
  65.1 3.1 %collective-permute-done.13.c = f32[160,128]{1,0:T(8,128)S(1)} collective-permute-done((f32[160,128]{1,0:T(8,128)S(1)}, f32[160,128]{1,0:T(8,128)S(1)}, u32[]{:S(2)}, u32[]{:S(2)}) %collective-permute-start.13) | collective-permute-done | bytes 81952 | tf_op jit(solution)/shard_map/ppermute | solution.py:290
  68.2 0.0 collective-permute-done.12.b
  68.3 1.3 %collective-permute-start.17 = (f32[160,128]{1,0:T(8,128)S(1)}, f32[160,128]{1,0:T(8,128)S(1)}, u32[]{:S(2)}, u32[]{:S(2)}) collective-permute-start(f32[160,128]{1,0:T(8,128)S(1)} %add_four.3.refs_0_), channel_id=1, source_target_pairs={{0,3},{1,2},{2,1},{3,0},{4,7},{5,6},{6,5},{7,4},{8,11},{9,10},{10,... | collective-permute-start | bytes 245768 | tf_op jit(solution)/shard_map/ppermute | solution.py:290
  69.6 0.8 collective-permute-start.16
  70.4 1.4 %collective-permute-start.15 = (f32[160,128]{1,0:T(8,128)S(1)}, f32[160,128]{1,0:T(8,128)S(1)}, u32[]{:S(2)}, u32[]{:S(2)}) collective-permute-start(f32[160,128]{1,0:T(8,128)S(1)} %add_four.3.refs_0_), channel_id=1, source_target_pairs={{0,1},{1,0},{2,3},{3,2},{4,5},{5,4},{6,7},{7,6},{8,9},{9,8},{10,11... | collective-permute-start | bytes 245768 | tf_op jit(solution)/shard_map/ppermute | solution.py:290
  71.8 1.9 %collective-permute-done.17.refs_3_ = f32[160,128]{1,0:T(8,128)S(1)} collective-permute-done((f32[160,128]{1,0:T(8,128)S(1)}, f32[160,128]{1,0:T(8,128)S(1)}, u32[]{:S(2)}, u32[]{:S(2)}) %collective-permute-start.17) | collective-permute-done | bytes 81952 | tf_op jit(solution)/shard_map/ppermute | solution.py:290
  73.7 0.8 collective-permute-done.16.refs_2_
  74.5 0.3 collective-permute-done.15.refs_1_
  74.9 0.1 collective-permute-start.18
  75.0 1.6 %collective-permute-done.18.theirs = f32[640,128]{1,0:T(8,128)S(1)} collective-permute-done((f32[640,128]{1,0:T(8,128)S(1)}, f32[640,128]{1,0:T(8,128)S(1)}, u32[]{:S(2)}, u32[]{:S(2)}) %collective-permute-start.18) | collective-permute-done | bytes 327712 | tf_op jit(solution)/shard_map/ppermute | solution.py:494
  76.6 16.0 %rotate.1 = bf16[4096,256]{1,0:T(8,128)(2,1)} custom-call(f32[640,128]{1,0:T(8,128)S(1)} %join.1.mine, f32[640,128]{1,0:T(8,128)S(1)} %collective-permute-done.18.theirs, bf16[512,256]{1,0:T(8,128)(2,1)S(1)} %bitcast.12, bf16[3072,256]{1,0:T(8,128)(2,1)S(1)} %bitcast.9, bf16[512,256]{1,0:T(8,128)(2,1)S(1)} %bitcast.15, ...), custom_call_target="tpu_custom_call" | custom-call | flops 17985175552 | bytes 6291456 | tf_op jit(solution)/shard_map/rotate/pallas_call | solution.py:453
  (3 shorter events, 0.1 us)
Async XLA Ops:
  3.2 9.3 %collective-permute-start.1 = (bf16[4,128,256]{2,1,0:T(8,128)(2,1)S(1)}, bf16[4,128,256]{2,1,0:T(8,128)(2,1)S(1)}, u32[]{:S(2)}, u32[]{:S(2)}) collective-permute-start(bf16[4,128,256]{2,1,0:T(8,128)(2,1)S(1)} %get-tuple-element.29.refs_1_.refs_3_), channel_id=1, source_target_pairs={{1,2},{2,1},{3,4},{4,3},{5,6},{6,5},{7,8},{8,7},{9,10},{10,9},{11,... | collective-permute-start | bytes 786440 | tf_op jit(solution)/shard_map/ppermute | solution.py:491
  6.6 14.6 %collective-permute-start = (bf16[4,128,256]{2,1,0:T(8,128)(2,1)S(1)}, bf16[4,128,256]{2,1,0:T(8,128)(2,1)S(1)}, u32[]{:S(2)}, u32[]{:S(2)}) collective-permute-start(bf16[4,128,256]{2,1,0:T(8,128)(2,1)S(1)} %get-tuple-element.37.refs_1_.refs_0_.refs_3_), channel_id=1, source_target_pairs={{0,1},{1,0},{2,3},{3,2},{4,5},{5,4},{6,7},{7,6},{8,9},{9,8},{10,11... | collective-permute-start | bytes 786440 | tf_op jit(solution)/shard_map/ppermute | solution.py:491
  13.6 16.9 %collective-permute-start.3 = (bf16[4,128,256]{2,1,0:T(8,128)(2,1)S(1)}, bf16[4,128,256]{2,1,0:T(8,128)(2,1)S(1)}, u32[]{:S(2)}, u32[]{:S(2)}) collective-permute-start(bf16[4,128,256]{2,1,0:T(8,128)(2,1)S(1)} %rows_odd.3.refs_1_.refs_3_), channel_id=1, source_target_pairs={{1,2},{2,1},{3,4},{4,3},{5,6},{6,5},{7,8},{8,7},{9,10},{10,9},{11,... | collective-permute-start | bytes 786440 | tf_op jit(solution)/shard_map/ppermute | solution.py:491
  22.4 10.7 %collective-permute-start.2 = (bf16[4,128,256]{2,1,0:T(8,128)(2,1)S(1)}, bf16[4,128,256]{2,1,0:T(8,128)(2,1)S(1)}, u32[]{:S(2)}, u32[]{:S(2)}) collective-permute-start(bf16[4,128,256]{2,1,0:T(8,128)(2,1)S(1)} %rows_even.3.refs_1_.refs_0_.refs_3_), channel_id=1, source_target_pairs={{0,1},{1,0},{2,3},{3,2},{4,5},{5,4},{6,7},{7,6},{8,9},{9,8},{10,11... | collective-permute-start | bytes 786440 | tf_op jit(solution)/shard_map/ppermute | solution.py:491
  31.6 11.2 %collective-permute-start.5 = (bf16[4,128,256]{2,1,0:T(8,128)(2,1)S(1)}, bf16[4,128,256]{2,1,0:T(8,128)(2,1)S(1)}, u32[]{:S(2)}, u32[]{:S(2)}) collective-permute-start(bf16[4,128,256]{2,1,0:T(8,128)(2,1)S(1)} %rows_odd.4.refs_1_), channel_id=1, source_target_pairs={{1,2},{2,1},{3,4},{4,3},{5,6},{6,5},{7,8},{8,7},{9,10},{10,9},{11,... | collective-permute-start | bytes 786440 | tf_op jit(solution)/shard_map/ppermute | solution.py:491
  34.2 11.7 %collective-permute-start.4 = (bf16[4,128,256]{2,1,0:T(8,128)(2,1)S(1)}, bf16[4,128,256]{2,1,0:T(8,128)(2,1)S(1)}, u32[]{:S(2)}, u32[]{:S(2)}) collective-permute-start(bf16[4,128,256]{2,1,0:T(8,128)(2,1)S(1)} %rows_even.4.refs_0_.refs_1_), channel_id=1, source_target_pairs={{0,1},{1,0},{2,3},{3,2},{4,5},{5,4},{6,7},{7,6},{8,9},{9,8},{10,11... | collective-permute-start | bytes 786440 | tf_op jit(solution)/shard_map/ppermute | solution.py:491
  42.7 4.9 %collective-permute-start.8 = (bf16[3072,256]{1,0:T(8,128)(2,1)S(1)}, bf16[3072,256]{1,0:T(8,128)(2,1)S(1)}, u32[]{:S(2)}, u32[]{:S(2)}) collective-permute-start(bf16[3072,256]{1,0:T(8,128)(2,1)S(1)} %bitcast.7), channel_id=1, source_target_pairs={{0,16},{16,0},{1,17},{17,1},{2,18},{18,2},{3,19},{19,3},{4,20},{20... | collective-permute-start | bytes 4718600 | tf_op jit(solution)/shard_map/ppermute | solution.py:494
  45.9 1.7 %collective-permute-start.7 = (bf16[512,256]{1,0:T(8,128)(2,1)S(1)}, bf16[512,256]{1,0:T(8,128)(2,1)S(1)}, u32[]{:S(2)}, u32[]{:S(2)}) collective-permute-start(bf16[512,256]{1,0:T(8,128)(2,1)S(1)} %bitcast.10), channel_id=1, source_target_pairs={{0,16},{16,0},{1,17},{17,1},{2,18},{18,2},{3,19},{19,3},{4,20},{20... | collective-permute-start | bytes 786440 | tf_op jit(solution)/shard_map/ppermute | solution.py:494
  47.1 2.3 %collective-permute-start.6 = (bf16[512,256]{1,0:T(8,128)(2,1)S(1)}, bf16[512,256]{1,0:T(8,128)(2,1)S(1)}, u32[]{:S(2)}, u32[]{:S(2)}) collective-permute-start(bf16[512,256]{1,0:T(8,128)(2,1)S(1)} %bitcast.13), channel_id=1, source_target_pairs={{0,16},{16,0},{1,17},{17,1},{2,18},{18,2},{3,19},{19,3},{4,20},{20... | collective-permute-start | bytes 786440 | tf_op jit(solution)/shard_map/ppermute | solution.py:494
  49.7 5.2 %collective-permute-start.9 = (f32[160,128]{1,0:T(8,128)S(1)}, f32[160,128]{1,0:T(8,128)S(1)}, u32[]{:S(2)}, u32[]{:S(2)}) collective-permute-start(f32[160,128]{1,0:T(8,128)S(1)} %get-tuple-element.48), channel_id=1, source_target_pairs={{0,1},{1,0},{2,3},{3,2},{4,5},{5,4},{6,7},{7,6},{8,9},{9,8},{10,11... | collective-permute-start | bytes 245768 | tf_op jit(solution)/shard_map/ppermute | solution.py:290
  52.3 6.0 %collective-permute-start.10 = (f32[160,128]{1,0:T(8,128)S(1)}, f32[160,128]{1,0:T(8,128)S(1)}, u32[]{:S(2)}, u32[]{:S(2)}) collective-permute-start(f32[160,128]{1,0:T(8,128)S(1)} %get-tuple-element.49), channel_id=1, source_target_pairs={{0,2},{1,3},{2,0},{3,1},{4,6},{5,7},{6,4},{7,5},{8,10},{9,11},{10,... | collective-permute-start | bytes 245768 | tf_op jit(solution)/shard_map/ppermute | solution.py:290
  52.7 5.6 %collective-permute-start.11 = (f32[160,128]{1,0:T(8,128)S(1)}, f32[160,128]{1,0:T(8,128)S(1)}, u32[]{:S(2)}, u32[]{:S(2)}) collective-permute-start(f32[160,128]{1,0:T(8,128)S(1)} %get-tuple-element.50), channel_id=1, source_target_pairs={{0,3},{1,2},{2,1},{3,0},{4,7},{5,6},{6,5},{7,4},{8,11},{9,10},{10,... | collective-permute-start | bytes 245768 | tf_op jit(solution)/shard_map/ppermute | solution.py:290
  58.3 6.8 %collective-permute-start.14 = (f32[160,128]{1,0:T(8,128)S(1)}, f32[160,128]{1,0:T(8,128)S(1)}, u32[]{:S(2)}, u32[]{:S(2)}) collective-permute-start(f32[160,128]{1,0:T(8,128)S(1)} %add_four.2.a), channel_id=1, source_target_pairs={{0,12},{1,13},{2,14},{3,15},{4,8},{5,9},{6,10},{7,11},{8,4},{9,5},... | collective-permute-start | bytes 245768 | tf_op jit(solution)/shard_map/ppermute | solution.py:290
  60.4 7.8 %collective-permute-start.13 = (f32[160,128]{1,0:T(8,128)S(1)}, f32[160,128]{1,0:T(8,128)S(1)}, u32[]{:S(2)}, u32[]{:S(2)}) collective-permute-start(f32[160,128]{1,0:T(8,128)S(1)} %add_four.2.a), channel_id=1, source_target_pairs={{0,8},{1,9},{2,10},{3,11},{4,12},{5,13},{6,14},{7,15},{8,0},{9,1},... | collective-permute-start | bytes 245768 | tf_op jit(solution)/shard_map/ppermute | solution.py:290
  62.1 6.1 %collective-permute-start.12 = (f32[160,128]{1,0:T(8,128)S(1)}, f32[160,128]{1,0:T(8,128)S(1)}, u32[]{:S(2)}, u32[]{:S(2)}) collective-permute-start(f32[160,128]{1,0:T(8,128)S(1)} %add_four.2.a), channel_id=1, source_target_pairs={{0,4},{1,5},{2,6},{3,7},{4,0},{5,1},{6,2},{7,3},{8,12},{9,13},{10,... | collective-permute-start | bytes 245768 | tf_op jit(solution)/shard_map/ppermute | solution.py:290
  68.3 5.5 %collective-permute-start.17 = (f32[160,128]{1,0:T(8,128)S(1)}, f32[160,128]{1,0:T(8,128)S(1)}, u32[]{:S(2)}, u32[]{:S(2)}) collective-permute-start(f32[160,128]{1,0:T(8,128)S(1)} %add_four.3.refs_0_), channel_id=1, source_target_pairs={{0,3},{1,2},{2,1},{3,0},{4,7},{5,6},{6,5},{7,4},{8,11},{9,10},{10,... | collective-permute-start | bytes 245768 | tf_op jit(solution)/shard_map/ppermute | solution.py:290
  69.6 4.9 %collective-permute-start.16 = (f32[160,128]{1,0:T(8,128)S(1)}, f32[160,128]{1,0:T(8,128)S(1)}, u32[]{:S(2)}, u32[]{:S(2)}) collective-permute-start(f32[160,128]{1,0:T(8,128)S(1)} %add_four.3.refs_0_), channel_id=1, source_target_pairs={{0,2},{1,3},{2,0},{3,1},{4,6},{5,7},{6,4},{7,5},{8,10},{9,11},{10,... | collective-permute-start | bytes 245768 | tf_op jit(solution)/shard_map/ppermute | solution.py:290
  70.4 4.4 %collective-permute-start.15 = (f32[160,128]{1,0:T(8,128)S(1)}, f32[160,128]{1,0:T(8,128)S(1)}, u32[]{:S(2)}, u32[]{:S(2)}) collective-permute-start(f32[160,128]{1,0:T(8,128)S(1)} %add_four.3.refs_0_), channel_id=1, source_target_pairs={{0,1},{1,0},{2,3},{3,2},{4,5},{5,4},{6,7},{7,6},{8,9},{9,8},{10,11... | collective-permute-start | bytes 245768 | tf_op jit(solution)/shard_map/ppermute | solution.py:290
  74.9 1.7 %collective-permute-start.18 = (f32[640,128]{1,0:T(8,128)S(1)}, f32[640,128]{1,0:T(8,128)S(1)}, u32[]{:S(2)}, u32[]{:S(2)}) collective-permute-start(f32[640,128]{1,0:T(8,128)S(1)} %join.1.mine), channel_id=1, source_target_pairs={{0,16},{16,0},{1,17},{17,1},{2,18},{18,2},{3,19},{19,3},{4,20},{20... | collective-permute-start | bytes 983048 | tf_op jit(solution)/shard_map/ppermute | solution.py:494

commit v11 on v10

--- a/solution.py
+++ b/solution.py
@@ -13,7 +13,7 @@
 WAYS = 4
 LOAD_CUTS = 4
 GRAM_ROWS = 1024
-GROUP = 8
+GROUP = 12
 
 SMALL = pl.CostEstimate(flops=1000, bytes_accessed=1000, transcendentals=0)
 LARGE = pl.CostEstimate(flops=10**11, bytes_accessed=1000, transcendentals=0)
@@ -50,11 +50,11 @@
     return table[table.shape[0] - 1, 0]
 
 
-def edges_kernel(table, whole_ref, even_ref, odd_ref, sem):
+def edges_kernel(table_ref, whole_ref, even_ref, odd_ref, sem, table):
     edge, tiles = HALO_T, whole_ref.shape[0]
     outs = {"even": even_ref, "odd": odd_ref}
     firsts = {name: at_end(name) * (tiles - edge) for name in outs}
-    load([(whole_ref, firsts[name], outs[name]) for name in outs], sem)
+    load([(whole_ref, firsts[name], outs[name]) for name in outs], sem, (table_ref, table))
     for name in outs:
         clear_dead(outs[name], firsts[name], live_count(table))
 
@@ -68,7 +68,7 @@
     lax.fori_loop(jnp.clip(live - first, 0, count), count, clear, 0)
 
 
-def load(moves, sem):
+def load(moves, sem, *whole):
     copies = []
     for source, first, target in moves:
         count = target.shape[0] // LOAD_CUTS
@@ -80,20 +80,24 @@
                     sem.at[len(copies)],
                 )
             )
+    for source, target in whole:
+        copies.append(pltpu.make_async_copy(source, target, sem.at[len(copies)]))
     for copy in copies:
         copy.start()
     for copy in copies:
         copy.wait()
 
 
-def fields_kernel(table, whole_ref, blocks_ref, inner_ref, even_blocks, odd_blocks, sem):
+def fields_kernel(
+    table_ref, whole_ref, blocks_ref, inner_ref, even_blocks, odd_blocks, sem, table
+):
     last = whole_ref.shape[0] - HALO_T
     moves = [
         (blocks_ref, at_end("even") * last, even_blocks),
         (blocks_ref, at_end("odd") * last, odd_blocks),
         (whole_ref, HALO_T, inner_ref),
     ]
-    load(moves, sem)
+    load(moves, sem, (table_ref, table))
     clear_dead(inner_ref, HALO_T, live_count(table))
 
 
@@ -104,10 +108,11 @@
 def load_call(body, name, args, shapes, megabytes, table=()):
     return pl.pallas_call(
         body,
-        in_specs=[SMEM] * len(table) + [HBM] * len(args),
+        in_specs=[VMEM] * len(table) + [HBM] * len(args),
         out_specs=[VMEM] * len(shapes),
         out_shape=shapes,
-        scratch_shapes=[pltpu.SemaphoreType.DMA((len(shapes) * LOAD_CUTS,))],
+        scratch_shapes=[pltpu.SemaphoreType.DMA((len(shapes) * LOAD_CUTS + len(table),))]
+        + [pltpu.SMEM(array.shape, array.dtype) for array in table],
         compiler_params=pltpu.CompilerParams(vmem_limit_bytes=megabytes * 1024 * 1024),
         cost_estimate=SMALL,
         name=name,
@@ -198,6 +203,16 @@
 ACROSS = (((0,), (0,)), ((), ()))
 
 
+NEAR = (1, 2, 3), (2, 1, 3)
+FAR = (2, 3, 1), (3, 2, 1)
+
+
+def quarter_order():
+    own = lax.axis_index("patch") % WAYS
+    first_core = lax.axis_index("cols") == 0
+    return [own] + [own ^ jnp.where(first_core, one, two) for one, two in zip(*NEAR)]
+
+
 def add_gram(chunk, own_ref, other_ref, total):
     chunk = min(chunk, own_ref.shape[0])
 
@@ -231,10 +246,9 @@
     blocks = [own[:half, :half], own[:half, half:], own[half:, half:], second, third]
     for i, block in enumerate(blocks):
         share[pl.ds(i * half, half), :] = block
-    quarter = lax.axis_index("patch") % WAYS
-    for d, out in enumerate(outs):
+    for out, quarter in zip(outs, quarter_order()):
         rows = out.shape[0]
-        out[...] = share[pl.ds(pl.multiple_of((quarter ^ d) * rows, 8), rows), :]
+        out[...] = share[pl.ds(pl.multiple_of(quarter * rows, 8), rows), :]
 
 
 def gram_call(body, name, args, shape, scratch=(), outs=0):
@@ -273,9 +287,8 @@
 def join_kernel(*refs):
     parts, out = refs[:-1], refs[-1]
     rows = parts[0].shape[0]
-    quarter = lax.axis_index("patch") % WAYS
-    for d, part in enumerate(parts):
-        out[pl.ds(pl.multiple_of((quarter ^ d) * rows, 8), rows), :] = part[...]
+    for part, quarter in zip(parts, quarter_order()):
+        out[pl.ds(pl.multiple_of(quarter * rows, 8), rows), :] = part[...]
 
 
 def sum_over_patch(parts):
@@ -285,18 +298,23 @@
     def add_four(values):
         return gram_call(add_kernel, "add_four", values, (rows, columns))
 
-    def from_others(values, stride=1):
-        return [
-            lax.ppermute(values[d], "patch", [(i, i ^ (d * stride)) for i in range(count)])
-            for d in range(1, WAYS)
-        ]
-
-    total = add_four([parts[0]] + from_others(parts))
+    def from_others(values, distances, stride=1):
+        got = []
+        for value, both in zip(values, zip(*distances)):
+            pairs = [
+                (core * count + i, core * count + (i ^ (distance * stride)))
+                for core, distance in enumerate(both)
+                for i in range(count)
+            ]
+            got.append(lax.ppermute(value, ("cols", "patch"), pairs))
+        return got
+
+    total = add_four([parts[0]] + from_others(parts[1:], NEAR))
     stride = WAYS
     while stride < count:
-        total = add_four([total] + from_others([total] * WAYS, stride))
+        total = add_four([total] + from_others([total] * (WAYS - 1), FAR, stride))
         stride *= WAYS
-    quarters = [total] + from_others([total] * WAYS)
+    quarters = [total] + from_others([total] * (WAYS - 1), NEAR)
     return gram_call(join_kernel, "join", quarters, (WAYS * rows, columns))
 
 
@@ -501,7 +519,8 @@
     halo = {lead: exchange(lead, edges[lead])}
     inner, *edge_blocks = load_fields(after(table, edges[lead]), start, blocks)
     halo[lag] = exchange(lag, after(edges[lag], inner))
-    stored = dict(zip(("even", "odd"), edge_blocks))
+    stored = dict(zip(("even", "odd"), edge_blocks), inner=load_blocks(after(blocks, inner)))
+    halo[lead] = after(halo[lead], stored["inner"])
     prev = dict.fromkeys(("even", "odd", "inner"))
 
     def inner_rows(behind):
@@ -526,8 +545,6 @@
             halo[lead] = exchange(lead, new[lead])
             new[lag] = edge_rows(lag, new[lead])
             halo[lag] = exchange(lag, new[lag])
-            if step == 0:
-                stored["inner"] = load_blocks(after(blocks, new[lag]))
             new["inner"] = inner_rows(new[lag])
         prev = dict(edges, inner=inner)
         edges, inner = {name: new[name] for name in edges}, new["inner"]

time: 93.1 us -> 93.2 us (level)
  Pallas kernels: 41 us -> 39.3 us
  starting transfers between devices: 25.9 us -> 27 us
    ppermute x6, starting transfers between devices: 13.1 us -> 15 us  [exchange(): return lax.ppermute(value, 'patch', pairs[name])]
    pallas_call x3, Pallas kernels: 7.44 us -> 6.24 us  [load_call(): pl.pallas_call(body, in_specs=[VMEM] * len(table) + [HBM] * len(args), ou...]
  transfers between devices with their start and end apart: 19 -> 19, of which waited for: 11 -> 11; matrix products, arithmetic and copies ran while one was open for 0% -> 0% of each run, Pallas kernels for 24% -> 23%
where the time goes in v11:
time: 93.2 us; the launch traced here: 92.9 us
  Pallas kernels  39.3 us (42%)
  starting transfers between devices  27 us (29%)
  waiting for transfers between devices  24.9 us (27%)
  between operations  1.05 us (1%)
    pallas_call x1, Pallas kernels, rotate(): pl.pallas_call(body, in_specs=[VMEM, VMEM] + [ANY] * 6, out_specs=ANY, ou...  16 us
    ppermute x6, starting transfers between devices, exchange(): return lax.ppermute(value, 'patch', pairs[name])  15 us
    pallas_call x9, Pallas kernels, tile_rows(): pl.pallas_call(functools.partial(rows_kernel, name), in_specs=[VMEM] * le...  14.9 us
    ppermute x9, waiting for transfers between devices, from_others(): got.append(lax.ppermute(value, ('cols', 'patch'), pairs))  13.4 us
    ppermute x9, starting transfers between devices, from_others(): got.append(lax.ppermute(value, ('cols', 'patch'), pairs))  11.2 us
    ppermute x6, waiting for transfers between devices, exchange(): return lax.ppermute(value, 'patch', pairs[name])  9.05 us
    pallas_call x3, Pallas kernels, load_call(): pl.pallas_call(body, in_specs=[VMEM] * len(table) + [HBM] * len(args), ou...  6.24 us
    ppermute x4, waiting for transfers between devices, sibling(): return lax.ppermute(value, 'cols', [(0, 1), (1, 0)])  2.47 us
  transfers between devices with their start and end apart: 19, of which 11 were waited for; matrix products, arithmetic and copies ran while one was open for 0% of the time, Pallas kernels for 23%

profile of v11, /device:TPU:0, one launch (start us, length us, event | category | flops | bytes accessed | tf_op | source)
XLA Modules:
  0.0 92.9 jit_solution(3206141681253259291)
XLA Ops:
  0.7 0.7 concatenate.3.table_ref
  1.3 1.2 %masked_edges.1 = (bf16[4,128,256]{2,1,0:T(8,128)(2,1)S(1)}, bf16[4,128,256]{2,1,0:T(8,128)(2,1)S(1)}) custom-call(s32[9,32]{1,0:T(8,128)S(1)} %concatenate.3.table_ref, bf16[32,128,256]{2,1,0:T(8,128)(2,1)} %bitcast.16), custom_call_target="tpu_custom_call" | custom-call | flops 1000 | bytes 1000 | tf_op jit(solution)/shard_map/masked_edges/pallas_call | solution.py:109
  2.5 0.7 collective-permute-start.1
  3.2 2.2 %load_fields.1 = (bf16[24,128,256]{2,1,0:T(8,128)(2,1)S(1)}, bf16[4,8,128,128]{3,2,1,0:T(8,128)(2,1)S(1)}, bf16[4,8,128,128]{3,2,1,0:T(8,128)(2,1)S(1)}) custom-call(s32[9,32]{1,0:T(8,128)S(1)} %concatenate.3.table_ref, bf16[32,128,256]{2,1,0:T(8,128)(2,1)} %bitcast.17, bf16[32,8,128,128]{3,2,1,0:T(8,128)(2,1)} %blocks_ref.2), custom_call_target="tpu_custom_call" | custom-call | flops 1000 | bytes 1000 | tf_op jit(solution)/shard_map/load_fields/pallas_call | solution.py:109
  5.4 5.7 %collective-permute-start = (bf16[4,128,256]{2,1,0:T(8,128)(2,1)S(1)}, bf16[4,128,256]{2,1,0:T(8,128)(2,1)S(1)}, u32[]{:S(2)}, u32[]{:S(2)}) collective-permute-start(bf16[4,128,256]{2,1,0:T(8,128)(2,1)S(1)} %get-tuple-element.40.refs_1_.refs_0_.refs_3_), channel_id=1, source_target_pairs={{0,1},{1,0},{2,3},{3,2},{4,5},{5,4},{6,7},{7,6},{8,9},{9,8},{10,11... | collective-permute-start | bytes 786440 | tf_op jit(solution)/shard_map/ppermute | solution.py:509
  11.1 2.9 %load_blocks.1.refs_3_.refs_4_ = bf16[24,8,128,128]{3,2,1,0:T(8,128)(2,1)S(1)} custom-call(bf16[32,8,128,128]{3,2,1,0:T(8,128)(2,1)} %blocks_ref.2), custom_call_target="tpu_custom_call" | custom-call | flops 1000 | bytes 1000 | tf_op jit(solution)/shard_map/load_blocks/pallas_call | solution.py:109
  14.0 0.0 collective-permute-done.1.refs_0_
  14.0 1.1 %rows_odd.3.refs_1_.refs_3_ = bf16[4,128,256]{2,1,0:T(8,128)(2,1)S(1)} custom-call(s32[9,32]{1,0:T(8,128)S(1)} %concatenate.3.table_ref, bf16[4,128,256]{2,1,0:T(8,128)(2,1)S(1)} %collective-permute-done.1.refs_0_, bf16[4,128,256]{2,1,0:T(8,128)(2,1)S(1)} %get-tuple-element.30.refs_1_.refs_3_, bf16[24,128,256]{2,1,0:T(8,128)(2,1)S(1)} %get-tuple-element.32.refs_2_.refs_3_, ...), custom_call_target="tpu_custom_call" | custom-call | flops 1000 | bytes 1000 | tf_op jit(solution)/shard_map/rows_odd/pallas_call | solution.py:187
  15.1 0.7 collective-permute-start.3
  15.8 4.8 %collective-permute-done.refs_0_ = bf16[4,128,256]{2,1,0:T(8,128)(2,1)S(1)} collective-permute-done((bf16[4,128,256]{2,1,0:T(8,128)(2,1)S(1)}, bf16[4,128,256]{2,1,0:T(8,128)(2,1)S(1)}, u32[]{:S(2)}, u32[]{:S(2)}) %collective-permute-start) | collective-permute-done | bytes 262176 | tf_op jit(solution)/shard_map/ppermute | solution.py:509
  20.6 1.1 %rows_even.3.refs_1_.refs_0_.refs_3_ = bf16[4,128,256]{2,1,0:T(8,128)(2,1)S(1)} custom-call(s32[9,32]{1,0:T(8,128)S(1)} %concatenate.3.table_ref, bf16[4,128,256]{2,1,0:T(8,128)(2,1)S(1)} %collective-permute-done.refs_0_, bf16[4,128,256]{2,1,0:T(8,128)(2,1)S(1)} %get-tuple-element.40.refs_1_.refs_0_.refs_3_, ...), custom_call_target="tpu_custom_call" | custom-call | flops 1000 | bytes 1000 | tf_op jit(solution)/shard_map/rows_even/pallas_call | solution.py:187
  21.7 2.4 %collective-permute-start.2 = (bf16[4,128,256]{2,1,0:T(8,128)(2,1)S(1)}, bf16[4,128,256]{2,1,0:T(8,128)(2,1)S(1)}, u32[]{:S(2)}, u32[]{:S(2)}) collective-permute-start(bf16[4,128,256]{2,1,0:T(8,128)(2,1)S(1)} %rows_even.3.refs_1_.refs_0_.refs_3_), channel_id=1, source_target_pairs={{0,1},{1,0},{2,3},{3,2},{4,5},{5,4},{6,7},{7,6},{8,9},{9,8},{10,11... | collective-permute-start | bytes 786440 | tf_op jit(solution)/shard_map/ppermute | solution.py:509
  24.1 2.7 %rows_inner.3.refs_2_.refs_3_ = bf16[24,128,256]{2,1,0:T(8,128)(2,1)S(1)} custom-call(s32[9,32]{1,0:T(8,128)S(1)} %concatenate.3.table_ref, bf16[4,128,256]{2,1,0:T(8,128)(2,1)S(1)} %get-tuple-element.40.refs_1_.refs_0_.refs_3_, bf16[4,128,256]{2,1,0:T(8,128)(2,1)S(1)} %get-tuple-element.30.refs_1_.refs_3_, ...), custom_call_target="tpu_custom_call" | custom-call | flops 1000 | bytes 1000 | tf_op jit(solution)/shard_map/rows_inner/pallas_call | solution.py:187
  26.8 0.0 collective-permute-done.3.refs_0_
  26.8 1.1 %rows_odd.4.refs_1_ = bf16[4,128,256]{2,1,0:T(8,128)(2,1)S(1)} custom-call(s32[9,32]{1,0:T(8,128)S(1)} %concatenate.3.table_ref, bf16[4,128,256]{2,1,0:T(8,128)(2,1)S(1)} %collective-permute-done.3.refs_0_, bf16[4,128,256]{2,1,0:T(8,128)(2,1)S(1)} %rows_odd.3.refs_1_.refs_3_, bf16[24,128,256]{2,1,0:T(8,128)(2,1)S(1)} %rows_inner.3.refs_2_.refs_3_, ...), custom_call_target="tpu_custom_call" | custom-call | flops 1000 | bytes 1000 | tf_op jit(solution)/shard_map/rows_odd/pallas_call | solution.py:187
  27.9 0.9 collective-permute-start.5
  28.8 4.3 %collective-permute-done.2.refs_0_ = bf16[4,128,256]{2,1,0:T(8,128)(2,1)S(1)} collective-permute-done((bf16[4,128,256]{2,1,0:T(8,128)(2,1)S(1)}, bf16[4,128,256]{2,1,0:T(8,128)(2,1)S(1)}, u32[]{:S(2)}, u32[]{:S(2)}) %collective-permute-start.2) | collective-permute-done | bytes 262176 | tf_op jit(solution)/shard_map/ppermute | solution.py:509
  33.1 1.1 %rows_even.4.refs_0_.refs_1_ = bf16[4,128,256]{2,1,0:T(8,128)(2,1)S(1)} custom-call(s32[9,32]{1,0:T(8,128)S(1)} %concatenate.3.table_ref, bf16[4,128,256]{2,1,0:T(8,128)(2,1)S(1)} %collective-permute-done.2.refs_0_, bf16[4,128,256]{2,1,0:T(8,128)(2,1)S(1)} %rows_even.3.refs_1_.refs_0_.refs_3_, bf16[24,128,256]{2,1,0:T(8,128)(2,1)S(1)} %rows_inner.3.refs_2_.refs_3_, ...), custom_call_target="tpu_custom_call" | custom-call | flops 1000 | bytes 1000 | tf_op jit(solution)/shard_map/rows_even/pallas_call | solution.py:187
  34.2 4.7 %collective-permute-start.4 = (bf16[4,128,256]{2,1,0:T(8,128)(2,1)S(1)}, bf16[4,128,256]{2,1,0:T(8,128)(2,1)S(1)}, u32[]{:S(2)}, u32[]{:S(2)}) collective-permute-start(bf16[4,128,256]{2,1,0:T(8,128)(2,1)S(1)} %rows_even.4.refs_0_.refs_1_), channel_id=1, source_target_pairs={{0,1},{1,0},{2,3},{3,2},{4,5},{5,4},{6,7},{7,6},{8,9},{9,8},{10,11... | collective-permute-start | bytes 786440 | tf_op jit(solution)/shard_map/ppermute | solution.py:509
  38.9 2.7 %rows_inner.4.refs_2_ = bf16[24,128,256]{2,1,0:T(8,128)(2,1)S(1)} custom-call(s32[9,32]{1,0:T(8,128)S(1)} %concatenate.3.table_ref, bf16[4,128,256]{2,1,0:T(8,128)(2,1)S(1)} %rows_even.3.refs_1_.refs_0_.refs_3_, bf16[4,128,256]{2,1,0:T(8,128)(2,1)S(1)} %rows_odd.3.refs_1_.refs_3_, bf16[24,128,256]{2,1,0:T(8,128)(2,1)S(1)} %rows_inner.3.refs_2_.refs_3_, ...), custom_call_target="tpu_custom_call" | custom-call | flops 1000 | bytes 1000 | tf_op jit(solution)/shard_map/rows_inner/pallas_call | solution.py:187
  41.7 2.7 %rows_inner.5 = bf16[24,128,256]{2,1,0:T(8,128)(2,1)S(1)} custom-call(s32[9,32]{1,0:T(8,128)S(1)} %concatenate.3.table_ref, bf16[4,128,256]{2,1,0:T(8,128)(2,1)S(1)} %rows_even.4.refs_0_.refs_1_, bf16[4,128,256]{2,1,0:T(8,128)(2,1)S(1)} %rows_odd.4.refs_1_, bf16[24,128,256]{2,1,0:T(8,128)(2,1)S(1)} %rows_inner.4.refs_2_, ...), custom_call_target="tpu_custom_call" | custom-call | flops 1000 | bytes 1000 | tf_op jit(solution)/shard_map/rows_inner/pallas_call | solution.py:187
  44.4 0.1 collective-permute-start.8
  44.5 0.0 collective-permute-done.5.refs_0_
  44.5 1.1 %rows_odd.5 = bf16[4,128,256]{2,1,0:T(8,128)(2,1)S(1)} custom-call(s32[9,32]{1,0:T(8,128)S(1)} %concatenate.3.table_ref, bf16[4,128,256]{2,1,0:T(8,128)(2,1)S(1)} %collective-permute-done.5.refs_0_, bf16[4,128,256]{2,1,0:T(8,128)(2,1)S(1)} %rows_odd.4.refs_1_, bf16[24,128,256]{2,1,0:T(8,128)(2,1)S(1)} %rows_inner.4.refs_2_, ...), custom_call_target="tpu_custom_call" | custom-call | flops 1000 | bytes 1000 | tf_op jit(solution)/shard_map/rows_odd/pallas_call | solution.py:187
  45.6 0.0 collective-permute-done.4.refs_0_
  45.6 0.6 collective-permute-start.7
  46.2 1.1 %rows_even.5 = bf16[4,128,256]{2,1,0:T(8,128)(2,1)S(1)} custom-call(s32[9,32]{1,0:T(8,128)S(1)} %concatenate.3.table_ref, bf16[4,128,256]{2,1,0:T(8,128)(2,1)S(1)} %collective-permute-done.4.refs_0_, bf16[4,128,256]{2,1,0:T(8,128)(2,1)S(1)} %rows_even.4.refs_0_.refs_1_, bf16[24,128,256]{2,1,0:T(8,128)(2,1)S(1)} %rows_inner.4.refs_2_, ...), custom_call_target="tpu_custom_call" | custom-call | flops 99999997952 | bytes 1000 | tf_op jit(solution)/shard_map/rows_even/pallas_call | solution.py:187
  47.3 0.1 collective-permute-start.6
  47.4 0.8 collective-permute-done.7.refs_2_.refs_3_
  48.2 0.0 collective-permute-done.8.refs_3_.refs_4_
  48.2 1.7 %gram.1.start_ref = f32[256,512]{1,0:T(8,128)S(1)} custom-call(bf16[512,256]{1,0:T(8,128)(2,1)S(1)} %bitcast.11, bf16[3072,256]{1,0:T(8,128)(2,1)S(1)} %bitcast.8, bf16[512,256]{1,0:T(8,128)(2,1)S(1)} %collective-permute-done.7.refs_2_.refs_3_, bf16[3072,256]{1,0:T(8,128)(2,1)S(1)} %collective-permute-done.8.refs_3_.refs_4_), custom_call_target="tpu_custom_call" | custom-call | flops 1000 | bytes 1000 | tf_op jit(solution)/shard_map/gram/pallas_call | solution.py:256
  50.0 0.0 collective-permute-done.6.other_ref.refs_5_
  50.0 0.3 gram_share.1
  50.3 0.7 collective-permute-start.9
  51.0 0.0 collective-permute-start.10
  51.0 2.9 %collective-permute-start.11 = (f32[160,128]{1,0:T(8,128)S(1)}, f32[160,128]{1,0:T(8,128)S(1)}, u32[]{:S(2)}, u32[]{:S(2)}) collective-permute-start(f32[160,128]{1,0:T(8,128)S(1)} %get-tuple-element.52), channel_id=1, source_target_pairs={{0,3},{1,2},{2,1},{3,0},{4,7},{5,6},{6,5},{7,4},{8,11},{9,10},{10,... | collective-permute-start | bytes 245768 | tf_op jit(solution)/shard_map/ppermute | solution.py:309
  53.9 1.5 %collective-permute-done.9.b = f32[160,128]{1,0:T(8,128)S(1)} collective-permute-done((f32[160,128]{1,0:T(8,128)S(1)}, f32[160,128]{1,0:T(8,128)S(1)}, u32[]{:S(2)}, u32[]{:S(2)}) %collective-permute-start.9) | collective-permute-done | bytes 81952 | tf_op jit(solution)/shard_map/ppermute | solution.py:309
  55.4 1.8 %collective-permute-done.10.c = f32[160,128]{1,0:T(8,128)S(1)} collective-permute-done((f32[160,128]{1,0:T(8,128)S(1)}, f32[160,128]{1,0:T(8,128)S(1)}, u32[]{:S(2)}, u32[]{:S(2)}) %collective-permute-start.10) | collective-permute-done | bytes 81952 | tf_op jit(solution)/shard_map/ppermute | solution.py:309
  57.2 0.0 collective-permute-done.11.d
  57.3 1.6 %collective-permute-start.14 = (f32[160,128]{1,0:T(8,128)S(1)}, f32[160,128]{1,0:T(8,128)S(1)}, u32[]{:S(2)}, u32[]{:S(2)}) collective-permute-start(f32[160,128]{1,0:T(8,128)S(1)} %add_four.2.a), channel_id=1, source_target_pairs={{0,4},{1,5},{2,6},{3,7},{4,0},{5,1},{6,2},{7,3},{8,12},{9,13},{10,... | collective-permute-start | bytes 245768 | tf_op jit(solution)/shard_map/ppermute | solution.py:309
  58.9 2.5 %collective-permute-start.13 = (f32[160,128]{1,0:T(8,128)S(1)}, f32[160,128]{1,0:T(8,128)S(1)}, u32[]{:S(2)}, u32[]{:S(2)}) collective-permute-start(f32[160,128]{1,0:T(8,128)S(1)} %add_four.2.a), channel_id=1, source_target_pairs={{0,12},{1,13},{2,14},{3,15},{4,8},{5,9},{6,10},{7,11},{8,4},{9,5},... | collective-permute-start | bytes 245768 | tf_op jit(solution)/shard_map/ppermute | solution.py:309
  61.4 0.0 collective-permute-start.12
  61.4 1.2 %collective-permute-done.14.d = f32[160,128]{1,0:T(8,128)S(1)} collective-permute-done((f32[160,128]{1,0:T(8,128)S(1)}, f32[160,128]{1,0:T(8,128)S(1)}, u32[]{:S(2)}, u32[]{:S(2)}) %collective-permute-start.14) | collective-permute-done | bytes 81952 | tf_op jit(solution)/shard_map/ppermute | solution.py:309
  62.6 3.4 %collective-permute-done.13.c = f32[160,128]{1,0:T(8,128)S(1)} collective-permute-done((f32[160,128]{1,0:T(8,128)S(1)}, f32[160,128]{1,0:T(8,128)S(1)}, u32[]{:S(2)}, u32[]{:S(2)}) %collective-permute-start.13) | collective-permute-done | bytes 81952 | tf_op jit(solution)/shard_map/ppermute | solution.py:309
  65.9 2.8 %collective-permute-done.12.b = f32[160,128]{1,0:T(8,128)S(1)} collective-permute-done((f32[160,128]{1,0:T(8,128)S(1)}, f32[160,128]{1,0:T(8,128)S(1)}, u32[]{:S(2)}, u32[]{:S(2)}) %collective-permute-start.12) | collective-permute-done | bytes 81952 | tf_op jit(solution)/shard_map/ppermute | solution.py:309
  68.7 0.9 %collective-permute-start.17 = (f32[160,128]{1,0:T(8,128)S(1)}, f32[160,128]{1,0:T(8,128)S(1)}, u32[]{:S(2)}, u32[]{:S(2)}) collective-permute-start(f32[160,128]{1,0:T(8,128)S(1)} %add_four.3.refs_0_), channel_id=1, source_target_pairs={{0,3},{1,2},{2,1},{3,0},{4,7},{5,6},{6,5},{7,4},{8,11},{9,10},{10,... | collective-permute-start | bytes 245768 | tf_op jit(solution)/shard_map/ppermute | solution.py:309
  69.6 0.4 collective-permute-start.16
  70.1 2.2 %collective-permute-start.15 = (f32[160,128]{1,0:T(8,128)S(1)}, f32[160,128]{1,0:T(8,128)S(1)}, u32[]{:S(2)}, u32[]{:S(2)}) collective-permute-start(f32[160,128]{1,0:T(8,128)S(1)} %add_four.3.refs_0_), channel_id=1, source_target_pairs={{0,1},{1,0},{2,3},{3,2},{4,5},{5,4},{6,7},{7,6},{8,9},{9,8},{10,11... | collective-permute-start | bytes 245768 | tf_op jit(solution)/shard_map/ppermute | solution.py:309
  72.3 2.0 %collective-permute-done.17.refs_3_ = f32[160,128]{1,0:T(8,128)S(1)} collective-permute-done((f32[160,128]{1,0:T(8,128)S(1)}, f32[160,128]{1,0:T(8,128)S(1)}, u32[]{:S(2)}, u32[]{:S(2)}) %collective-permute-start.17) | collective-permute-done | bytes 81952 | tf_op jit(solution)/shard_map/ppermute | solution.py:309
  74.2 0.8 collective-permute-done.16.refs_2_
  75.0 0.0 collective-permute-done.15.refs_1_
  75.0 0.1 collective-permute-start.18
  75.1 1.6 %collective-permute-done.18.theirs = f32[640,128]{1,0:T(8,128)S(1)} collective-permute-done((f32[640,128]{1,0:T(8,128)S(1)}, f32[640,128]{1,0:T(8,128)S(1)}, u32[]{:S(2)}, u32[]{:S(2)}) %collective-permute-start.18) | collective-permute-done | bytes 327712 | tf_op jit(solution)/shard_map/ppermute | solution.py:512
  76.7 16.0 %rotate.1 = bf16[4096,256]{1,0:T(8,128)(2,1)} custom-call(f32[640,128]{1,0:T(8,128)S(1)} %join.1.mine, f32[640,128]{1,0:T(8,128)S(1)} %collective-permute-done.18.theirs, bf16[512,256]{1,0:T(8,128)(2,1)S(1)} %bitcast.12, bf16[3072,256]{1,0:T(8,128)(2,1)S(1)} %bitcast.9, bf16[512,256]{1,0:T(8,128)(2,1)S(1)} %bitcast.15, ...), custom_call_target="tpu_custom_call" | custom-call | flops 17985175552 | bytes 6291456 | tf_op jit(solution)/shard_map/rotate/pallas_call | solution.py:471
  (3 shorter events, 0.1 us)
Async XLA Ops:
  2.5 11.4 %collective-permute-start.1 = (bf16[4,128,256]{2,1,0:T(8,128)(2,1)S(1)}, bf16[4,128,256]{2,1,0:T(8,128)(2,1)S(1)}, u32[]{:S(2)}, u32[]{:S(2)}) collective-permute-start(bf16[4,128,256]{2,1,0:T(8,128)(2,1)S(1)} %get-tuple-element.30.refs_1_.refs_3_), channel_id=1, source_target_pairs={{1,2},{2,1},{3,4},{4,3},{5,6},{6,5},{7,8},{8,7},{9,10},{10,9},{11,... | collective-permute-start | bytes 786440 | tf_op jit(solution)/shard_map/ppermute | solution.py:509
  5.4 15.2 %collective-permute-start = (bf16[4,128,256]{2,1,0:T(8,128)(2,1)S(1)}, bf16[4,128,256]{2,1,0:T(8,128)(2,1)S(1)}, u32[]{:S(2)}, u32[]{:S(2)}) collective-permute-start(bf16[4,128,256]{2,1,0:T(8,128)(2,1)S(1)} %get-tuple-element.40.refs_1_.refs_0_.refs_3_), channel_id=1, source_target_pairs={{0,1},{1,0},{2,3},{3,2},{4,5},{5,4},{6,7},{7,6},{8,9},{9,8},{10,11... | collective-permute-start | bytes 786440 | tf_op jit(solution)/shard_map/ppermute | solution.py:509
  15.1 11.7 %collective-permute-start.3 = (bf16[4,128,256]{2,1,0:T(8,128)(2,1)S(1)}, bf16[4,128,256]{2,1,0:T(8,128)(2,1)S(1)}, u32[]{:S(2)}, u32[]{:S(2)}) collective-permute-start(bf16[4,128,256]{2,1,0:T(8,128)(2,1)S(1)} %rows_odd.3.refs_1_.refs_3_), channel_id=1, source_target_pairs={{1,2},{2,1},{3,4},{4,3},{5,6},{6,5},{7,8},{8,7},{9,10},{10,9},{11,... | collective-permute-start | bytes 786440 | tf_op jit(solution)/shard_map/ppermute | solution.py:509
  21.7 11.4 %collective-permute-start.2 = (bf16[4,128,256]{2,1,0:T(8,128)(2,1)S(1)}, bf16[4,128,256]{2,1,0:T(8,128)(2,1)S(1)}, u32[]{:S(2)}, u32[]{:S(2)}) collective-permute-start(bf16[4,128,256]{2,1,0:T(8,128)(2,1)S(1)} %rows_even.3.refs_1_.refs_0_.refs_3_), channel_id=1, source_target_pairs={{0,1},{1,0},{2,3},{3,2},{4,5},{5,4},{6,7},{7,6},{8,9},{9,8},{10,11... | collective-permute-start | bytes 786440 | tf_op jit(solution)/shard_map/ppermute | solution.py:509
  27.9 16.5 %collective-permute-start.5 = (bf16[4,128,256]{2,1,0:T(8,128)(2,1)S(1)}, bf16[4,128,256]{2,1,0:T(8,128)(2,1)S(1)}, u32[]{:S(2)}, u32[]{:S(2)}) collective-permute-start(bf16[4,128,256]{2,1,0:T(8,128)(2,1)S(1)} %rows_odd.4.refs_1_), channel_id=1, source_target_pairs={{1,2},{2,1},{3,4},{4,3},{5,6},{6,5},{7,8},{8,7},{9,10},{10,9},{11,... | collective-permute-start | bytes 786440 | tf_op jit(solution)/shard_map/ppermute | solution.py:509
  34.2 11.4 %collective-permute-start.4 = (bf16[4,128,256]{2,1,0:T(8,128)(2,1)S(1)}, bf16[4,128,256]{2,1,0:T(8,128)(2,1)S(1)}, u32[]{:S(2)}, u32[]{:S(2)}) collective-permute-start(bf16[4,128,256]{2,1,0:T(8,128)(2,1)S(1)} %rows_even.4.refs_0_.refs_1_), channel_id=1, source_target_pairs={{0,1},{1,0},{2,3},{3,2},{4,5},{5,4},{6,7},{7,6},{8,9},{9,8},{10,11... | collective-permute-start | bytes 786440 | tf_op jit(solution)/shard_map/ppermute | solution.py:509
  44.4 3.9 %collective-permute-start.8 = (bf16[3072,256]{1,0:T(8,128)(2,1)S(1)}, bf16[3072,256]{1,0:T(8,128)(2,1)S(1)}, u32[]{:S(2)}, u32[]{:S(2)}) collective-permute-start(bf16[3072,256]{1,0:T(8,128)(2,1)S(1)} %bitcast.7), channel_id=1, source_target_pairs={{0,16},{16,0},{1,17},{17,1},{2,18},{18,2},{3,19},{19,3},{4,20},{20... | collective-permute-start | bytes 4718600 | tf_op jit(solution)/shard_map/ppermute | solution.py:512
  45.6 2.6 %collective-permute-start.7 = (bf16[512,256]{1,0:T(8,128)(2,1)S(1)}, bf16[512,256]{1,0:T(8,128)(2,1)S(1)}, u32[]{:S(2)}, u32[]{:S(2)}) collective-permute-start(bf16[512,256]{1,0:T(8,128)(2,1)S(1)} %bitcast.10), channel_id=1, source_target_pairs={{0,16},{16,0},{1,17},{17,1},{2,18},{18,2},{3,19},{19,3},{4,20},{20... | collective-permute-start | bytes 786440 | tf_op jit(solution)/shard_map/ppermute | solution.py:512
  47.3 2.7 %collective-permute-start.6 = (bf16[512,256]{1,0:T(8,128)(2,1)S(1)}, bf16[512,256]{1,0:T(8,128)(2,1)S(1)}, u32[]{:S(2)}, u32[]{:S(2)}) collective-permute-start(bf16[512,256]{1,0:T(8,128)(2,1)S(1)} %bitcast.13), channel_id=1, source_target_pairs={{0,16},{16,0},{1,17},{17,1},{2,18},{18,2},{3,19},{19,3},{4,20},{20... | collective-permute-start | bytes 786440 | tf_op jit(solution)/shard_map/ppermute | solution.py:512
  50.3 5.1 %collective-permute-start.9 = (f32[160,128]{1,0:T(8,128)S(1)}, f32[160,128]{1,0:T(8,128)S(1)}, u32[]{:S(2)}, u32[]{:S(2)}) collective-permute-start(f32[160,128]{1,0:T(8,128)S(1)} %get-tuple-element.50), channel_id=1, source_target_pairs={{0,1},{1,0},{2,3},{3,2},{4,5},{5,4},{6,7},{7,6},{8,9},{9,8},{10,11... | collective-permute-start | bytes 245768 | tf_op jit(solution)/shard_map/ppermute | solution.py:309
  51.0 6.2 %collective-permute-start.10 = (f32[160,128]{1,0:T(8,128)S(1)}, f32[160,128]{1,0:T(8,128)S(1)}, u32[]{:S(2)}, u32[]{:S(2)}) collective-permute-start(f32[160,128]{1,0:T(8,128)S(1)} %get-tuple-element.51), channel_id=1, source_target_pairs={{0,2},{1,3},{2,0},{3,1},{4,6},{5,7},{6,4},{7,5},{8,10},{9,11},{10,... | collective-permute-start | bytes 245768 | tf_op jit(solution)/shard_map/ppermute | solution.py:309
  51.0 6.2 %collective-permute-start.11 = (f32[160,128]{1,0:T(8,128)S(1)}, f32[160,128]{1,0:T(8,128)S(1)}, u32[]{:S(2)}, u32[]{:S(2)}) collective-permute-start(f32[160,128]{1,0:T(8,128)S(1)} %get-tuple-element.52), channel_id=1, source_target_pairs={{0,3},{1,2},{2,1},{3,0},{4,7},{5,6},{6,5},{7,4},{8,11},{9,10},{10,... | collective-permute-start | bytes 245768 | tf_op jit(solution)/shard_map/ppermute | solution.py:309
  57.3 5.3 %collective-permute-start.14 = (f32[160,128]{1,0:T(8,128)S(1)}, f32[160,128]{1,0:T(8,128)S(1)}, u32[]{:S(2)}, u32[]{:S(2)}) collective-permute-start(f32[160,128]{1,0:T(8,128)S(1)} %add_four.2.a), channel_id=1, source_target_pairs={{0,4},{1,5},{2,6},{3,7},{4,0},{5,1},{6,2},{7,3},{8,12},{9,13},{10,... | collective-permute-start | bytes 245768 | tf_op jit(solution)/shard_map/ppermute | solution.py:309
  58.9 7.0 %collective-permute-start.13 = (f32[160,128]{1,0:T(8,128)S(1)}, f32[160,128]{1,0:T(8,128)S(1)}, u32[]{:S(2)}, u32[]{:S(2)}) collective-permute-start(f32[160,128]{1,0:T(8,128)S(1)} %add_four.2.a), channel_id=1, source_target_pairs={{0,12},{1,13},{2,14},{3,15},{4,8},{5,9},{6,10},{7,11},{8,4},{9,5},... | collective-permute-start | bytes 245768 | tf_op jit(solution)/shard_map/ppermute | solution.py:309
  61.4 7.3 %collective-permute-start.12 = (f32[160,128]{1,0:T(8,128)S(1)}, f32[160,128]{1,0:T(8,128)S(1)}, u32[]{:S(2)}, u32[]{:S(2)}) collective-permute-start(f32[160,128]{1,0:T(8,128)S(1)} %add_four.2.a), channel_id=1, source_target_pairs={{0,8},{1,9},{2,10},{3,11},{4,12},{5,13},{6,14},{7,15},{8,0},{9,1},... | collective-permute-start | bytes 245768 | tf_op jit(solution)/shard_map/ppermute | solution.py:309
  68.7 5.5 %collective-permute-start.17 = (f32[160,128]{1,0:T(8,128)S(1)}, f32[160,128]{1,0:T(8,128)S(1)}, u32[]{:S(2)}, u32[]{:S(2)}) collective-permute-start(f32[160,128]{1,0:T(8,128)S(1)} %add_four.3.refs_0_), channel_id=1, source_target_pairs={{0,3},{1,2},{2,1},{3,0},{4,7},{5,6},{6,5},{7,4},{8,11},{9,10},{10,... | collective-permute-start | bytes 245768 | tf_op jit(solution)/shard_map/ppermute | solution.py:309
  69.6 5.3 %collective-permute-start.16 = (f32[160,128]{1,0:T(8,128)S(1)}, f32[160,128]{1,0:T(8,128)S(1)}, u32[]{:S(2)}, u32[]{:S(2)}) collective-permute-start(f32[160,128]{1,0:T(8,128)S(1)} %add_four.3.refs_0_), channel_id=1, source_target_pairs={{0,2},{1,3},{2,0},{3,1},{4,6},{5,7},{6,4},{7,5},{8,10},{9,11},{10,... | collective-permute-start | bytes 245768 | tf_op jit(solution)/shard_map/ppermute | solution.py:309
  70.1 4.9 %collective-permute-start.15 = (f32[160,128]{1,0:T(8,128)S(1)}, f32[160,128]{1,0:T(8,128)S(1)}, u32[]{:S(2)}, u32[]{:S(2)}) collective-permute-start(f32[160,128]{1,0:T(8,128)S(1)} %add_four.3.refs_0_), channel_id=1, source_target_pairs={{0,1},{1,0},{2,3},{3,2},{4,5},{5,4},{6,7},{7,6},{8,9},{9,8},{10,11... | collective-permute-start | bytes 245768 | tf_op jit(solution)/shard_map/ppermute | solution.py:309
  75.0 1.7 %collective-permute-start.18 = (f32[640,128]{1,0:T(8,128)S(1)}, f32[640,128]{1,0:T(8,128)S(1)}, u32[]{:S(2)}, u32[]{:S(2)}) collective-permute-start(f32[640,128]{1,0:T(8,128)S(1)} %join.1.mine), channel_id=1, source_target_pairs={{0,16},{16,0},{1,17},{17,1},{2,18},{18,2},{3,19},{19,3},{4,20},{20... | collective-permute-start | bytes 983048 | tf_op jit(solution)/shard_map/ppermute | solution.py:512

commit v12 on v11

--- a/solution.py
+++ b/solution.py
@@ -16,7 +16,7 @@
 GROUP = 12
 
 SMALL = pl.CostEstimate(flops=1000, bytes_accessed=1000, transcendentals=0)
-LARGE = pl.CostEstimate(flops=10**11, bytes_accessed=1000, transcendentals=0)
+LARGE = pl.CostEstimate(flops=2 * 10**10, bytes_accessed=1000, transcendentals=0)
 SMALL_VMEM = pltpu.CompilerParams(vmem_limit_bytes=8 * 1024 * 1024)
 ANY = pl.BlockSpec(memory_space=pl.ANY)
 HBM = pl.BlockSpec(memory_space=pltpu.HBM)
@@ -204,7 +204,7 @@
 
 
 NEAR = (1, 2, 3), (2, 1, 3)
-FAR = (2, 3, 1), (3, 2, 1)
+FAR = (1, 3, 2), (1, 2, 3)
 
 
 def quarter_order():
@@ -531,23 +531,29 @@
         sources = after(halo[name], behind), edges[name], inner
         return tile_rows(name, table, stored[name], sources, prev[name], cost)
 
+    ahead = None
     for step in range(STEPS):
-        final = step == STEPS - 1
+        first, final = step == 0, step == STEPS - 1
         new = {}
+        if not first:
+            new["inner"] = inner_rows(edges["odd"]) if ahead is None else ahead
+        cost = LARGE if final else SMALL
+        new[lead] = edge_rows(lead, new.get("inner", inner), cost)
+        if first:
+            new["inner"] = inner_rows(new[lead])
         if final:
-            new["inner"] = inner_rows(edges["odd"])
-            new[lead] = edge_rows(lead, new["inner"])
             flat = [new[name].reshape(-1, width) for name in (lead, "inner")]
             others = [sibling(value) for value in flat]
-            new[lag] = edge_rows(lag, new[lead], LARGE)
         else:
-            new[lead] = edge_rows(lead, inner)
-            halo[lead] = exchange(lead, new[lead])
-            new[lag] = edge_rows(lag, new[lead])
-            halo[lag] = exchange(lag, new[lag])
-            new["inner"] = inner_rows(new[lag])
+            halo[lead] = exchange(lead, after(new[lead], new["inner"]))
+        new[lag] = edge_rows(lag, new[lead], cost)
         prev = dict(edges, inner=inner)
         edges, inner = {name: new[name] for name in edges}, new["inner"]
+        if step == STEPS - 2:
+            ahead = inner_rows(new[lag])
+            halo[lag] = exchange(lag, after(new[lag], ahead))
+        elif not final:
+            halo[lag] = exchange(lag, new[lag])
     last = edges[lag].reshape(-1, width)
     other_last = sibling(last)
     others = [after(other, last) for other in others]

time: 93.2 us -> 100 us (1.073)
  waiting for transfers between devices: 24.9 us -> 29.3 us
  starting transfers between devices: 27 us -> 29.4 us
    ppermute x6, waiting for transfers between devices: 9.05 us -> 12.3 us  [exchange(): return lax.ppermute(value, 'patch', pairs[name])]
    ppermute x6, starting transfers between devices: 15 us -> 17.5 us  [exchange(): return lax.ppermute(value, 'patch', pairs[name])]
    ppermute x9, waiting for transfers between devices: 13.4 us -> 15.3 us  [from_others(): got.append(lax.ppermute(value, ('cols', 'patch'), pairs))]
  transfers between devices with their start and end apart: 19 -> 19, of which waited for: 11 -> 12; matrix products, arithmetic and copies ran while one was open for 0% -> 0% of each run, Pallas kernels for 23% -> 22%
where the time goes in v12:
time: 100 us; the launch traced here: 99.7 us
  Pallas kernels  39.3 us (39%)
  starting transfers between devices  29.4 us (29%)
  waiting for transfers between devices  29.3 us (29%)
  between operations  1.04 us (1%)
    ppermute x6, starting transfers between devices, exchange(): return lax.ppermute(value, 'patch', pairs[name])  17.5 us
    pallas_call x1, Pallas kernels, rotate(): pl.pallas_call(body, in_specs=[VMEM, VMEM] + [ANY] * 6, out_specs=ANY, ou...  16 us
    ppermute x9, waiting for transfers between devices, from_others(): got.append(lax.ppermute(value, ('cols', 'patch'), pairs))  15.3 us
    pallas_call x9, Pallas kernels, tile_rows(): pl.pallas_call(functools.partial(rows_kernel, name), in_specs=[VMEM] * le...  14.9 us
    ppermute x6, waiting for transfers between devices, exchange(): return lax.ppermute(value, 'patch', pairs[name])  12.3 us
    ppermute x9, starting transfers between devices, from_others(): got.append(lax.ppermute(value, ('cols', 'patch'), pairs))  11.2 us
    pallas_call x3, Pallas kernels, load_call(): pl.pallas_call(body, in_specs=[VMEM] * len(table) + [HBM] * len(args), ou...  6.22 us
    pallas_call x5, Pallas kernels, gram_call(): pl.pallas_call(body, in_specs=[VMEM] * len(args), out_specs=[VMEM] * outs...  2.14 us
  transfers between devices with their start and end apart: 19, of which 12 were waited for; matrix products, arithmetic and copies ran while one was open for 0% of the time, Pallas kernels for 22%

profile of v12, /device:TPU:0, one launch (start us, length us, event | category | flops | bytes accessed | tf_op | source)
XLA Modules:
  0.0 99.7 jit_solution(14917586225998287559)
XLA Ops:
  0.7 0.7 concatenate.3.table_ref
  1.3 1.2 %masked_edges.1 = (bf16[4,128,256]{2,1,0:T(8,128)(2,1)S(1)}, bf16[4,128,256]{2,1,0:T(8,128)(2,1)S(1)}) custom-call(s32[9,32]{1,0:T(8,128)S(1)} %concatenate.3.table_ref, bf16[32,128,256]{2,1,0:T(8,128)(2,1)} %bitcast.16), custom_call_target="tpu_custom_call" | custom-call | flops 1000 | bytes 1000 | tf_op jit(solution)/shard_map/masked_edges/pallas_call | solution.py:109
  2.5 0.7 collective-permute-start.1
  3.2 2.2 %load_fields.1 = (bf16[24,128,256]{2,1,0:T(8,128)(2,1)S(1)}, bf16[4,8,128,128]{3,2,1,0:T(8,128)(2,1)S(1)}, bf16[4,8,128,128]{3,2,1,0:T(8,128)(2,1)S(1)}) custom-call(s32[9,32]{1,0:T(8,128)S(1)} %concatenate.3.table_ref, bf16[32,128,256]{2,1,0:T(8,128)(2,1)} %bitcast.17, bf16[32,8,128,128]{3,2,1,0:T(8,128)(2,1)} %blocks_ref.2), custom_call_target="tpu_custom_call" | custom-call | flops 1000 | bytes 1000 | tf_op jit(solution)/shard_map/load_fields/pallas_call | solution.py:109
  5.4 5.7 %collective-permute-start = (bf16[4,128,256]{2,1,0:T(8,128)(2,1)S(1)}, bf16[4,128,256]{2,1,0:T(8,128)(2,1)S(1)}, u32[]{:S(2)}, u32[]{:S(2)}) collective-permute-start(bf16[4,128,256]{2,1,0:T(8,128)(2,1)S(1)} %get-tuple-element.43.refs_1_.refs_0_.refs_3_), channel_id=1, source_target_pairs={{0,1},{1,0},{2,3},{3,2},{4,5},{5,4},{6,7},{7,6},{8,9},{9,8},{10,11... | collective-permute-start | bytes 786440 | tf_op jit(solution)/shard_map/ppermute | solution.py:509
  11.1 2.9 %load_blocks.1.refs_3_.refs_4_ = bf16[24,8,128,128]{3,2,1,0:T(8,128)(2,1)S(1)} custom-call(bf16[32,8,128,128]{3,2,1,0:T(8,128)(2,1)} %blocks_ref.2), custom_call_target="tpu_custom_call" | custom-call | flops 1000 | bytes 1000 | tf_op jit(solution)/shard_map/load_blocks/pallas_call | solution.py:109
  14.0 0.0 collective-permute-done.1.refs_0_
  14.0 1.1 %rows_odd.3.refs_1_.refs_3_ = bf16[4,128,256]{2,1,0:T(8,128)(2,1)S(1)} custom-call(s32[9,32]{1,0:T(8,128)S(1)} %concatenate.3.table_ref, bf16[4,128,256]{2,1,0:T(8,128)(2,1)S(1)} %collective-permute-done.1.refs_0_, bf16[4,128,256]{2,1,0:T(8,128)(2,1)S(1)} %get-tuple-element.33.refs_1_.refs_3_, bf16[24,128,256]{2,1,0:T(8,128)(2,1)S(1)} %get-tuple-element.35.refs_2_.refs_3_, ...), custom_call_target="tpu_custom_call" | custom-call | flops 1000 | bytes 1000 | tf_op jit(solution)/shard_map/rows_odd/pallas_call | solution.py:187
  15.1 2.7 %rows_inner.3.refs_2_.refs_3_ = bf16[24,128,256]{2,1,0:T(8,128)(2,1)S(1)} custom-call(s32[9,32]{1,0:T(8,128)S(1)} %concatenate.3.table_ref, bf16[4,128,256]{2,1,0:T(8,128)(2,1)S(1)} %get-tuple-element.43.refs_1_.refs_0_.refs_3_, bf16[4,128,256]{2,1,0:T(8,128)(2,1)S(1)} %get-tuple-element.33.refs_1_.refs_3_, ...), custom_call_target="tpu_custom_call" | custom-call | flops 1000 | bytes 1000 | tf_op jit(solution)/shard_map/rows_inner/pallas_call | solution.py:187
  17.8 0.7 collective-permute-start.3
  18.5 2.0 %collective-permute-done.refs_0_ = bf16[4,128,256]{2,1,0:T(8,128)(2,1)S(1)} collective-permute-done((bf16[4,128,256]{2,1,0:T(8,128)(2,1)S(1)}, bf16[4,128,256]{2,1,0:T(8,128)(2,1)S(1)}, u32[]{:S(2)}, u32[]{:S(2)}) %collective-permute-start) | collective-permute-done | bytes 262176 | tf_op jit(solution)/shard_map/ppermute | solution.py:509
  20.5 1.1 %rows_even.3.refs_0_.refs_1_.refs_3_ = bf16[4,128,256]{2,1,0:T(8,128)(2,1)S(1)} custom-call(s32[9,32]{1,0:T(8,128)S(1)} %concatenate.3.table_ref, bf16[4,128,256]{2,1,0:T(8,128)(2,1)S(1)} %collective-permute-done.refs_0_, bf16[4,128,256]{2,1,0:T(8,128)(2,1)S(1)} %get-tuple-element.43.refs_1_.refs_0_.refs_3_, ...), custom_call_target="tpu_custom_call" | custom-call | flops 1000 | bytes 1000 | tf_op jit(solution)/shard_map/rows_even/pallas_call | solution.py:187
  21.6 4.3 %collective-permute-start.2 = (bf16[4,128,256]{2,1,0:T(8,128)(2,1)S(1)}, bf16[4,128,256]{2,1,0:T(8,128)(2,1)S(1)}, u32[]{:S(2)}, u32[]{:S(2)}) collective-permute-start(bf16[4,128,256]{2,1,0:T(8,128)(2,1)S(1)} %rows_even.3.refs_0_.refs_1_.refs_3_), channel_id=1, source_target_pairs={{0,1},{1,0},{2,3},{3,2},{4,5},{5,4},{6,7},{7,6},{8,9},{9,8},{10,11... | collective-permute-start | bytes 786440 | tf_op jit(solution)/shard_map/ppermute | solution.py:509
  25.9 2.7 %rows_inner.4.refs_2_ = bf16[24,128,256]{2,1,0:T(8,128)(2,1)S(1)} custom-call(s32[9,32]{1,0:T(8,128)S(1)} %concatenate.3.table_ref, bf16[4,128,256]{2,1,0:T(8,128)(2,1)S(1)} %rows_even.3.refs_0_.refs_1_.refs_3_, bf16[4,128,256]{2,1,0:T(8,128)(2,1)S(1)} %rows_odd.3.refs_1_.refs_3_, bf16[24,128,256]{2,1,0:T(8,128)(2,1)S(1)} %rows_inner.3.refs_2_.refs_3_, ...), custom_call_target="tpu_custom_call" | custom-call | flops 1000 | bytes 1000 | tf_op jit(solution)/shard_map/rows_inner/pallas_call | solution.py:187
  28.6 0.0 collective-permute-done.3.refs_0_
  28.7 1.1 %rows_odd.4.refs_1_ = bf16[4,128,256]{2,1,0:T(8,128)(2,1)S(1)} custom-call(s32[9,32]{1,0:T(8,128)S(1)} %concatenate.3.table_ref, bf16[4,128,256]{2,1,0:T(8,128)(2,1)S(1)} %collective-permute-done.3.refs_0_, bf16[4,128,256]{2,1,0:T(8,128)(2,1)S(1)} %rows_odd.3.refs_1_.refs_3_, bf16[24,128,256]{2,1,0:T(8,128)(2,1)S(1)} %rows_inner.3.refs_2_.refs_3_, ...), custom_call_target="tpu_custom_call" | custom-call | flops 1000 | bytes 1000 | tf_op jit(solution)/shard_map/rows_odd/pallas_call | solution.py:187
  29.8 0.9 collective-permute-start.5
  30.7 4.6 %collective-permute-done.2.refs_0_ = bf16[4,128,256]{2,1,0:T(8,128)(2,1)S(1)} collective-permute-done((bf16[4,128,256]{2,1,0:T(8,128)(2,1)S(1)}, bf16[4,128,256]{2,1,0:T(8,128)(2,1)S(1)}, u32[]{:S(2)}, u32[]{:S(2)}) %collective-permute-start.2) | collective-permute-done | bytes 262176 | tf_op jit(solution)/shard_map/ppermute | solution.py:509
  35.2 1.1 %rows_even.4.refs_0_.refs_1_ = bf16[4,128,256]{2,1,0:T(8,128)(2,1)S(1)} custom-call(s32[9,32]{1,0:T(8,128)S(1)} %concatenate.3.table_ref, bf16[4,128,256]{2,1,0:T(8,128)(2,1)S(1)} %collective-permute-done.2.refs_0_, bf16[4,128,256]{2,1,0:T(8,128)(2,1)S(1)} %rows_even.3.refs_0_.refs_1_.refs_3_, bf16[24,128,256]{2,1,0:T(8,128)(2,1)S(1)} %rows_inner.3.refs_2_.refs_3_, ...), custom_call_target="tpu_custom_call" | custom-call | flops 1000 | bytes 1000 | tf_op jit(solution)/shard_map/rows_even/pallas_call | solution.py:187
  36.4 2.7 %rows_inner.5 = bf16[24,128,256]{2,1,0:T(8,128)(2,1)S(1)} custom-call(s32[9,32]{1,0:T(8,128)S(1)} %concatenate.3.table_ref, bf16[4,128,256]{2,1,0:T(8,128)(2,1)S(1)} %rows_even.4.refs_0_.refs_1_, bf16[4,128,256]{2,1,0:T(8,128)(2,1)S(1)} %rows_odd.4.refs_1_, bf16[24,128,256]{2,1,0:T(8,128)(2,1)S(1)} %rows_inner.4.refs_2_, ...), custom_call_target="tpu_custom_call" | custom-call | flops 1000 | bytes 1000 | tf_op jit(solution)/shard_map/rows_inner/pallas_call | solution.py:187
  39.1 0.1 collective-permute-start.8
  39.2 5.3 %collective-permute-start.4 = (bf16[4,128,256]{2,1,0:T(8,128)(2,1)S(1)}, bf16[4,128,256]{2,1,0:T(8,128)(2,1)S(1)}, u32[]{:S(2)}, u32[]{:S(2)}) collective-permute-start(bf16[4,128,256]{2,1,0:T(8,128)(2,1)S(1)} %rows_even.4.refs_0_.refs_1_), channel_id=1, source_target_pairs={{0,1},{1,0},{2,3},{3,2},{4,5},{5,4},{6,7},{7,6},{8,9},{9,8},{10,11... | collective-permute-start | bytes 786440 | tf_op jit(solution)/shard_map/ppermute | solution.py:509
  44.5 0.0 collective-permute-done.5.refs_0_
  44.5 1.1 %rows_odd.5 = bf16[4,128,256]{2,1,0:T(8,128)(2,1)S(1)} custom-call(s32[9,32]{1,0:T(8,128)S(1)} %concatenate.3.table_ref, bf16[4,128,256]{2,1,0:T(8,128)(2,1)S(1)} %collective-permute-done.5.refs_0_, bf16[4,128,256]{2,1,0:T(8,128)(2,1)S(1)} %rows_odd.4.refs_1_, bf16[24,128,256]{2,1,0:T(8,128)(2,1)S(1)} %rows_inner.4.refs_2_, ...), custom_call_target="tpu_custom_call" | custom-call | flops 20000000000 | bytes 1000 | tf_op jit(solution)/shard_map/rows_odd/pallas_call | solution.py:187
  45.6 5.8 %collective-permute-done.4.refs_0_ = bf16[4,128,256]{2,1,0:T(8,128)(2,1)S(1)} collective-permute-done((bf16[4,128,256]{2,1,0:T(8,128)(2,1)S(1)}, bf16[4,128,256]{2,1,0:T(8,128)(2,1)S(1)}, u32[]{:S(2)}, u32[]{:S(2)}) %collective-permute-start.4) | collective-permute-done | bytes 262176 | tf_op jit(solution)/shard_map/ppermute | solution.py:509
  51.4 0.0 collective-permute-start.7
  51.4 1.1 %rows_even.5 = bf16[4,128,256]{2,1,0:T(8,128)(2,1)S(1)} custom-call(s32[9,32]{1,0:T(8,128)S(1)} %concatenate.3.table_ref, bf16[4,128,256]{2,1,0:T(8,128)(2,1)S(1)} %collective-permute-done.4.refs_0_, bf16[4,128,256]{2,1,0:T(8,128)(2,1)S(1)} %rows_even.4.refs_0_.refs_1_, bf16[24,128,256]{2,1,0:T(8,128)(2,1)S(1)} %rows_inner.4.refs_2_, ...), custom_call_target="tpu_custom_call" | custom-call | flops 20000000000 | bytes 1000 | tf_op jit(solution)/shard_map/rows_even/pallas_call | solution.py:187
  52.5 0.6 collective-permute-start.6
  53.1 0.0 collective-permute-done.7.refs_2_.refs_3_
  53.1 0.0 collective-permute-done.8.refs_3_.refs_4_
  53.1 1.7 %gram.1.start_ref = f32[256,512]{1,0:T(8,128)S(1)} custom-call(bf16[512,256]{1,0:T(8,128)(2,1)S(1)} %bitcast.11, bf16[3072,256]{1,0:T(8,128)(2,1)S(1)} %bitcast.8, bf16[512,256]{1,0:T(8,128)(2,1)S(1)} %collective-permute-done.7.refs_2_.refs_3_, bf16[3072,256]{1,0:T(8,128)(2,1)S(1)} %collective-permute-done.8.refs_3_.refs_4_), custom_call_target="tpu_custom_call" | custom-call | flops 1000 | bytes 1000 | tf_op jit(solution)/shard_map/gram/pallas_call | solution.py:256
  54.8 0.0 collective-permute-done.6.other_ref.refs_5_
  54.8 0.3 gram_share.1
  55.2 0.1 collective-permute-start.10
  55.3 3.2 %collective-permute-start.11 = (f32[160,128]{1,0:T(8,128)S(1)}, f32[160,128]{1,0:T(8,128)S(1)}, u32[]{:S(2)}, u32[]{:S(2)}) collective-permute-start(f32[160,128]{1,0:T(8,128)S(1)} %get-tuple-element.58), channel_id=1, source_target_pairs={{0,3},{1,2},{2,1},{3,0},{4,7},{5,6},{6,5},{7,4},{8,11},{9,10},{10,... | collective-permute-start | bytes 245768 | tf_op jit(solution)/shard_map/ppermute | solution.py:309
  58.4 0.3 collective-permute-start.9
  58.7 3.0 %collective-permute-done.10.c = f32[160,128]{1,0:T(8,128)S(1)} collective-permute-done((f32[160,128]{1,0:T(8,128)S(1)}, f32[160,128]{1,0:T(8,128)S(1)}, u32[]{:S(2)}, u32[]{:S(2)}) %collective-permute-start.10) | collective-permute-done | bytes 81952 | tf_op jit(solution)/shard_map/ppermute | solution.py:309
  61.7 0.0 collective-permute-done.11.d
  61.7 1.2 %collective-permute-done.9.b = f32[160,128]{1,0:T(8,128)S(1)} collective-permute-done((f32[160,128]{1,0:T(8,128)S(1)}, f32[160,128]{1,0:T(8,128)S(1)}, u32[]{:S(2)}, u32[]{:S(2)}) %collective-permute-start.9) | collective-permute-done | bytes 81952 | tf_op jit(solution)/shard_map/ppermute | solution.py:309
  62.9 1.7 %collective-permute-start.12 = (f32[160,128]{1,0:T(8,128)S(1)}, f32[160,128]{1,0:T(8,128)S(1)}, u32[]{:S(2)}, u32[]{:S(2)}) collective-permute-start(f32[160,128]{1,0:T(8,128)S(1)} %add_four.2.a), channel_id=1, source_target_pairs={{0,4},{1,5},{2,6},{3,7},{4,0},{5,1},{6,2},{7,3},{8,12},{9,13},{10,... | collective-permute-start | bytes 245768 | tf_op jit(solution)/shard_map/ppermute | solution.py:309
  64.6 2.5 %collective-permute-start.13 = (f32[160,128]{1,0:T(8,128)S(1)}, f32[160,128]{1,0:T(8,128)S(1)}, u32[]{:S(2)}, u32[]{:S(2)}) collective-permute-start(f32[160,128]{1,0:T(8,128)S(1)} %add_four.2.a), channel_id=1, source_target_pairs={{0,12},{1,13},{2,14},{3,15},{4,8},{5,9},{6,10},{7,11},{8,4},{9,5},... | collective-permute-start | bytes 245768 | tf_op jit(solution)/shard_map/ppermute | solution.py:309
  67.0 0.0 collective-permute-start.14
  67.0 0.4 collective-permute-done.12.b
  67.4 4.2 %collective-permute-done.13.c = f32[160,128]{1,0:T(8,128)S(1)} collective-permute-done((f32[160,128]{1,0:T(8,128)S(1)}, f32[160,128]{1,0:T(8,128)S(1)}, u32[]{:S(2)}, u32[]{:S(2)}) %collective-permute-start.13) | collective-permute-done | bytes 81952 | tf_op jit(solution)/shard_map/ppermute | solution.py:309
  71.6 2.8 %collective-permute-done.14.d = f32[160,128]{1,0:T(8,128)S(1)} collective-permute-done((f32[160,128]{1,0:T(8,128)S(1)}, f32[160,128]{1,0:T(8,128)S(1)}, u32[]{:S(2)}, u32[]{:S(2)}) %collective-permute-start.14) | collective-permute-done | bytes 81952 | tf_op jit(solution)/shard_map/ppermute | solution.py:309
  74.4 1.7 %collective-permute-start.15 = (f32[160,128]{1,0:T(8,128)S(1)}, f32[160,128]{1,0:T(8,128)S(1)}, u32[]{:S(2)}, u32[]{:S(2)}) collective-permute-start(f32[160,128]{1,0:T(8,128)S(1)} %add_four.3.refs_0_), channel_id=1, source_target_pairs={{0,1},{1,0},{2,3},{3,2},{4,5},{5,4},{6,7},{7,6},{8,9},{9,8},{10,11... | collective-permute-start | bytes 245768 | tf_op jit(solution)/shard_map/ppermute | solution.py:309
  76.0 0.4 collective-permute-start.16
  76.5 1.5 %collective-permute-start.17 = (f32[160,128]{1,0:T(8,128)S(1)}, f32[160,128]{1,0:T(8,128)S(1)}, u32[]{:S(2)}, u32[]{:S(2)}) collective-permute-start(f32[160,128]{1,0:T(8,128)S(1)} %add_four.3.refs_0_), channel_id=1, source_target_pairs={{0,3},{1,2},{2,1},{3,0},{4,7},{5,6},{6,5},{7,4},{8,11},{9,10},{10,... | collective-permute-start | bytes 245768 | tf_op jit(solution)/shard_map/ppermute | solution.py:309
  77.9 1.0 collective-permute-done.15.refs_1_
  78.9 1.6 %collective-permute-done.16.refs_2_ = f32[160,128]{1,0:T(8,128)S(1)} collective-permute-done((f32[160,128]{1,0:T(8,128)S(1)}, f32[160,128]{1,0:T(8,128)S(1)}, u32[]{:S(2)}, u32[]{:S(2)}) %collective-permute-start.16) | collective-permute-done | bytes 81952 | tf_op jit(solution)/shard_map/ppermute | solution.py:309
  80.5 1.3 %collective-permute-done.17.refs_3_ = f32[160,128]{1,0:T(8,128)S(1)} collective-permute-done((f32[160,128]{1,0:T(8,128)S(1)}, f32[160,128]{1,0:T(8,128)S(1)}, u32[]{:S(2)}, u32[]{:S(2)}) %collective-permute-start.17) | collective-permute-done | bytes 81952 | tf_op jit(solution)/shard_map/ppermute | solution.py:309
  81.8 0.1 collective-permute-start.18
  81.9 1.6 %collective-permute-done.18.theirs = f32[640,128]{1,0:T(8,128)S(1)} collective-permute-done((f32[640,128]{1,0:T(8,128)S(1)}, f32[640,128]{1,0:T(8,128)S(1)}, u32[]{:S(2)}, u32[]{:S(2)}) %collective-permute-start.18) | collective-permute-done | bytes 327712 | tf_op jit(solution)/shard_map/ppermute | solution.py:512
  83.5 16.0 %rotate.1 = bf16[4096,256]{1,0:T(8,128)(2,1)} custom-call(f32[640,128]{1,0:T(8,128)S(1)} %join.1.mine, f32[640,128]{1,0:T(8,128)S(1)} %collective-permute-done.18.theirs, bf16[512,256]{1,0:T(8,128)(2,1)S(1)} %bitcast.12, bf16[3072,256]{1,0:T(8,128)(2,1)S(1)} %bitcast.9, bf16[512,256]{1,0:T(8,128)(2,1)S(1)} %bitcast.15, ...), custom_call_target="tpu_custom_call" | custom-call | flops 17985175552 | bytes 6291456 | tf_op jit(solution)/shard_map/rotate/pallas_call | solution.py:471
  (3 shorter events, 0.1 us)
Async XLA Ops:
  2.5 11.4 %collective-permute-start.1 = (bf16[4,128,256]{2,1,0:T(8,128)(2,1)S(1)}, bf16[4,128,256]{2,1,0:T(8,128)(2,1)S(1)}, u32[]{:S(2)}, u32[]{:S(2)}) collective-permute-start(bf16[4,128,256]{2,1,0:T(8,128)(2,1)S(1)} %get-tuple-element.33.refs_1_.refs_3_), channel_id=1, source_target_pairs={{1,2},{2,1},{3,4},{4,3},{5,6},{6,5},{7,8},{8,7},{9,10},{10,9},{11,... | collective-permute-start | bytes 786440 | tf_op jit(solution)/shard_map/ppermute | solution.py:509
  5.4 15.1 %collective-permute-start = (bf16[4,128,256]{2,1,0:T(8,128)(2,1)S(1)}, bf16[4,128,256]{2,1,0:T(8,128)(2,1)S(1)}, u32[]{:S(2)}, u32[]{:S(2)}) collective-permute-start(bf16[4,128,256]{2,1,0:T(8,128)(2,1)S(1)} %get-tuple-element.43.refs_1_.refs_0_.refs_3_), channel_id=1, source_target_pairs={{0,1},{1,0},{2,3},{3,2},{4,5},{5,4},{6,7},{7,6},{8,9},{9,8},{10,11... | collective-permute-start | bytes 786440 | tf_op jit(solution)/shard_map/ppermute | solution.py:509
  17.8 10.8 %collective-permute-start.3 = (bf16[4,128,256]{2,1,0:T(8,128)(2,1)S(1)}, bf16[4,128,256]{2,1,0:T(8,128)(2,1)S(1)}, u32[]{:S(2)}, u32[]{:S(2)}) collective-permute-start(bf16[4,128,256]{2,1,0:T(8,128)(2,1)S(1)} %rows_odd.3.refs_1_.refs_3_), channel_id=1, source_target_pairs={{1,2},{2,1},{3,4},{4,3},{5,6},{6,5},{7,8},{8,7},{9,10},{10,9},{11,... | collective-permute-start | bytes 786440 | tf_op jit(solution)/shard_map/ppermute | solution.py:509
  21.6 13.6 %collective-permute-start.2 = (bf16[4,128,256]{2,1,0:T(8,128)(2,1)S(1)}, bf16[4,128,256]{2,1,0:T(8,128)(2,1)S(1)}, u32[]{:S(2)}, u32[]{:S(2)}) collective-permute-start(bf16[4,128,256]{2,1,0:T(8,128)(2,1)S(1)} %rows_even.3.refs_0_.refs_1_.refs_3_), channel_id=1, source_target_pairs={{0,1},{1,0},{2,3},{3,2},{4,5},{5,4},{6,7},{7,6},{8,9},{9,8},{10,11... | collective-permute-start | bytes 786440 | tf_op jit(solution)/shard_map/ppermute | solution.py:509
  29.8 14.7 %collective-permute-start.5 = (bf16[4,128,256]{2,1,0:T(8,128)(2,1)S(1)}, bf16[4,128,256]{2,1,0:T(8,128)(2,1)S(1)}, u32[]{:S(2)}, u32[]{:S(2)}) collective-permute-start(bf16[4,128,256]{2,1,0:T(8,128)(2,1)S(1)} %rows_odd.4.refs_1_), channel_id=1, source_target_pairs={{1,2},{2,1},{3,4},{4,3},{5,6},{6,5},{7,8},{8,7},{9,10},{10,9},{11,... | collective-permute-start | bytes 786440 | tf_op jit(solution)/shard_map/ppermute | solution.py:509
  39.1 14.0 %collective-permute-start.8 = (bf16[3072,256]{1,0:T(8,128)(2,1)S(1)}, bf16[3072,256]{1,0:T(8,128)(2,1)S(1)}, u32[]{:S(2)}, u32[]{:S(2)}) collective-permute-start(bf16[3072,256]{1,0:T(8,128)(2,1)S(1)} %bitcast.7), channel_id=1, source_target_pairs={{0,16},{16,0},{1,17},{17,1},{2,18},{18,2},{3,19},{19,3},{4,20},{20... | collective-permute-start | bytes 4718600 | tf_op jit(solution)/shard_map/ppermute | solution.py:512
  39.2 12.2 %collective-permute-start.4 = (bf16[4,128,256]{2,1,0:T(8,128)(2,1)S(1)}, bf16[4,128,256]{2,1,0:T(8,128)(2,1)S(1)}, u32[]{:S(2)}, u32[]{:S(2)}) collective-permute-start(bf16[4,128,256]{2,1,0:T(8,128)(2,1)S(1)} %rows_even.4.refs_0_.refs_1_), channel_id=1, source_target_pairs={{0,1},{1,0},{2,3},{3,2},{4,5},{5,4},{6,7},{7,6},{8,9},{9,8},{10,11... | collective-permute-start | bytes 786440 | tf_op jit(solution)/shard_map/ppermute | solution.py:509
  51.4 1.7 %collective-permute-start.7 = (bf16[512,256]{1,0:T(8,128)(2,1)S(1)}, bf16[512,256]{1,0:T(8,128)(2,1)S(1)}, u32[]{:S(2)}, u32[]{:S(2)}) collective-permute-start(bf16[512,256]{1,0:T(8,128)(2,1)S(1)} %bitcast.10), channel_id=1, source_target_pairs={{0,16},{16,0},{1,17},{17,1},{2,18},{18,2},{3,19},{19,3},{4,20},{20... | collective-permute-start | bytes 786440 | tf_op jit(solution)/shard_map/ppermute | solution.py:512
  52.5 2.3 %collective-permute-start.6 = (bf16[512,256]{1,0:T(8,128)(2,1)S(1)}, bf16[512,256]{1,0:T(8,128)(2,1)S(1)}, u32[]{:S(2)}, u32[]{:S(2)}) collective-permute-start(bf16[512,256]{1,0:T(8,128)(2,1)S(1)} %bitcast.13), channel_id=1, source_target_pairs={{0,16},{16,0},{1,17},{17,1},{2,18},{18,2},{3,19},{19,3},{4,20},{20... | collective-permute-start | bytes 786440 | tf_op jit(solution)/shard_map/ppermute | solution.py:512
  55.2 6.5 %collective-permute-start.10 = (f32[160,128]{1,0:T(8,128)S(1)}, f32[160,128]{1,0:T(8,128)S(1)}, u32[]{:S(2)}, u32[]{:S(2)}) collective-permute-start(f32[160,128]{1,0:T(8,128)S(1)} %get-tuple-element.57), channel_id=1, source_target_pairs={{0,2},{1,3},{2,0},{3,1},{4,6},{5,7},{6,4},{7,5},{8,10},{9,11},{10,... | collective-permute-start | bytes 245768 | tf_op jit(solution)/shard_map/ppermute | solution.py:309
  55.3 6.5 %collective-permute-start.11 = (f32[160,128]{1,0:T(8,128)S(1)}, f32[160,128]{1,0:T(8,128)S(1)}, u32[]{:S(2)}, u32[]{:S(2)}) collective-permute-start(f32[160,128]{1,0:T(8,128)S(1)} %get-tuple-element.58), channel_id=1, source_target_pairs={{0,3},{1,2},{2,1},{3,0},{4,7},{5,6},{6,5},{7,4},{8,11},{9,10},{10,... | collective-permute-start | bytes 245768 | tf_op jit(solution)/shard_map/ppermute | solution.py:309
  58.4 4.4 %collective-permute-start.9 = (f32[160,128]{1,0:T(8,128)S(1)}, f32[160,128]{1,0:T(8,128)S(1)}, u32[]{:S(2)}, u32[]{:S(2)}) collective-permute-start(f32[160,128]{1,0:T(8,128)S(1)} %get-tuple-element.56), channel_id=1, source_target_pairs={{0,1},{1,0},{2,3},{3,2},{4,5},{5,4},{6,7},{7,6},{8,9},{9,8},{10,11... | collective-permute-start | bytes 245768 | tf_op jit(solution)/shard_map/ppermute | solution.py:309
  62.9 4.5 %collective-permute-start.12 = (f32[160,128]{1,0:T(8,128)S(1)}, f32[160,128]{1,0:T(8,128)S(1)}, u32[]{:S(2)}, u32[]{:S(2)}) collective-permute-start(f32[160,128]{1,0:T(8,128)S(1)} %add_four.2.a), channel_id=1, source_target_pairs={{0,4},{1,5},{2,6},{3,7},{4,0},{5,1},{6,2},{7,3},{8,12},{9,13},{10,... | collective-permute-start | bytes 245768 | tf_op jit(solution)/shard_map/ppermute | solution.py:309
  64.6 7.0 %collective-permute-start.13 = (f32[160,128]{1,0:T(8,128)S(1)}, f32[160,128]{1,0:T(8,128)S(1)}, u32[]{:S(2)}, u32[]{:S(2)}) collective-permute-start(f32[160,128]{1,0:T(8,128)S(1)} %add_four.2.a), channel_id=1, source_target_pairs={{0,12},{1,13},{2,14},{3,15},{4,8},{5,9},{6,10},{7,11},{8,4},{9,5},... | collective-permute-start | bytes 245768 | tf_op jit(solution)/shard_map/ppermute | solution.py:309
  67.0 7.3 %collective-permute-start.14 = (f32[160,128]{1,0:T(8,128)S(1)}, f32[160,128]{1,0:T(8,128)S(1)}, u32[]{:S(2)}, u32[]{:S(2)}) collective-permute-start(f32[160,128]{1,0:T(8,128)S(1)} %add_four.2.a), channel_id=1, source_target_pairs={{0,8},{1,9},{2,10},{3,11},{4,12},{5,13},{6,14},{7,15},{8,0},{9,1},... | collective-permute-start | bytes 245768 | tf_op jit(solution)/shard_map/ppermute | solution.py:309
  74.4 4.5 %collective-permute-start.15 = (f32[160,128]{1,0:T(8,128)S(1)}, f32[160,128]{1,0:T(8,128)S(1)}, u32[]{:S(2)}, u32[]{:S(2)}) collective-permute-start(f32[160,128]{1,0:T(8,128)S(1)} %add_four.3.refs_0_), channel_id=1, source_target_pairs={{0,1},{1,0},{2,3},{3,2},{4,5},{5,4},{6,7},{7,6},{8,9},{9,8},{10,11... | collective-permute-start | bytes 245768 | tf_op jit(solution)/shard_map/ppermute | solution.py:309
  76.0 4.4 %collective-permute-start.16 = (f32[160,128]{1,0:T(8,128)S(1)}, f32[160,128]{1,0:T(8,128)S(1)}, u32[]{:S(2)}, u32[]{:S(2)}) collective-permute-start(f32[160,128]{1,0:T(8,128)S(1)} %add_four.3.refs_0_), channel_id=1, source_target_pairs={{0,2},{1,3},{2,0},{3,1},{4,6},{5,7},{6,4},{7,5},{8,10},{9,11},{10,... | collective-permute-start | bytes 245768 | tf_op jit(solution)/shard_map/ppermute | solution.py:309
  76.5 5.3 %collective-permute-start.17 = (f32[160,128]{1,0:T(8,128)S(1)}, f32[160,128]{1,0:T(8,128)S(1)}, u32[]{:S(2)}, u32[]{:S(2)}) collective-permute-start(f32[160,128]{1,0:T(8,128)S(1)} %add_four.3.refs_0_), channel_id=1, source_target_pairs={{0,3},{1,2},{2,1},{3,0},{4,7},{5,6},{6,5},{7,4},{8,11},{9,10},{10,... | collective-permute-start | bytes 245768 | tf_op jit(solution)/shard_map/ppermute | solution.py:309
  81.8 1.7 %collective-permute-start.18 = (f32[640,128]{1,0:T(8,128)S(1)}, f32[640,128]{1,0:T(8,128)S(1)}, u32[]{:S(2)}, u32[]{:S(2)}) collective-permute-start(f32[640,128]{1,0:T(8,128)S(1)} %join.1.mine), channel_id=1, source_target_pairs={{0,16},{16,0},{1,17},{17,1},{2,18},{18,2},{3,19},{19,3},{4,20},{20... | collective-permute-start | bytes 983048 | tf_op jit(solution)/shard_map/ppermute | solution.py:512

commit v13 on v11

--- a/solution.py
+++ b/solution.py
@@ -204,7 +204,7 @@
 
 
 NEAR = (1, 2, 3), (2, 1, 3)
-FAR = (2, 3, 1), (3, 2, 1)
+FAR = (1, 2, 3), (1, 2, 3)
 
 
 def quarter_order():
@@ -515,12 +515,11 @@
     table = jnp.concatenate([tile_cols.T, jnp.broadcast_to(live_tiles[None], (1, tiles))])
 
     edges = dict(zip(("even", "odd"), masked_edges(table, start)))
-    lead, lag = "odd", "even"
+    lead, lag = "even", "odd"
     halo = {lead: exchange(lead, edges[lead])}
     inner, *edge_blocks = load_fields(after(table, edges[lead]), start, blocks)
     halo[lag] = exchange(lag, after(edges[lag], inner))
-    stored = dict(zip(("even", "odd"), edge_blocks), inner=load_blocks(after(blocks, inner)))
-    halo[lead] = after(halo[lead], stored["inner"])
+    stored = dict(zip(("even", "odd"), edge_blocks))
     prev = dict.fromkeys(("even", "odd", "inner"))
 
     def inner_rows(behind):
@@ -543,9 +542,12 @@
         else:
             new[lead] = edge_rows(lead, inner)
             halo[lead] = exchange(lead, new[lead])
-            new[lag] = edge_rows(lag, new[lead])
+            if step == 0:
+                stored["inner"] = load_blocks(after(blocks, new[lead]))
+            new["inner"] = inner_rows(new[lead])
+            new[lag] = edge_rows(lag, new["inner"])
             halo[lag] = exchange(lag, new[lag])
-            new["inner"] = inner_rows(new[lag])
+            halo[lead] = after(halo[lead], new[lag])
         prev = dict(edges, inner=inner)
         edges, inner = {name: new[name] for name in edges}, new["inner"]
     last = edges[lag].reshape(-1, width)

time: 93.2 us -> 92 us (0.987)
  waiting for transfers between devices: 24.9 us -> 23.8 us
    ppermute x9, starting transfers between devices: 11.2 us -> 15.6 us  [from_others(): got.append(lax.ppermute(value, ('cols', 'patch'), pairs))]
    ppermute x6, starting transfers between devices: 15 us -> 10.7 us  [exchange(): return lax.ppermute(value, 'patch', pairs[name])]
    ppermute x6, waiting for transfers between devices: 9.05 us -> 7.61 us  [exchange(): return lax.ppermute(value, 'patch', pairs[name])]
    ppermute x9, waiting for transfers between devices: 13.4 us -> 14.5 us  [from_others(): got.append(lax.ppermute(value, ('cols', 'patch'), pairs))]
  transfers between devices with their start and end apart: 19 -> 19, of which waited for: 11 -> 11; matrix products, arithmetic and copies ran while one was open for 0% -> 0% of each run, Pallas kernels for 23% -> 24%
where the time goes in v13:
time: 92 us; the launch traced here: 91.8 us
  Pallas kernels  39.2 us (43%)
  starting transfers between devices  27 us (29%)
  waiting for transfers between devices  23.8 us (26%)
  between operations  1.05 us (1%)
    pallas_call x1, Pallas kernels, rotate(): pl.pallas_call(body, in_specs=[VMEM, VMEM] + [ANY] * 6, out_specs=ANY, ou...  16 us
    ppermute x9, starting transfers between devices, from_others(): got.append(lax.ppermute(value, ('cols', 'patch'), pairs))  15.6 us
    pallas_call x9, Pallas kernels, tile_rows(): pl.pallas_call(functools.partial(rows_kernel, name), in_specs=[VMEM] * le...  14.9 us
    ppermute x9, waiting for transfers between devices, from_others(): got.append(lax.ppermute(value, ('cols', 'patch'), pairs))  14.5 us
    ppermute x6, starting transfers between devices, exchange(): return lax.ppermute(value, 'patch', pairs[name])  10.7 us
    ppermute x6, waiting for transfers between devices, exchange(): return lax.ppermute(value, 'patch', pairs[name])  7.61 us
    pallas_call x3, Pallas kernels, load_call(): pl.pallas_call(body, in_specs=[VMEM] * len(table) + [HBM] * len(args), ou...  6.17 us
    pallas_call x5, Pallas kernels, gram_call(): pl.pallas_call(body, in_specs=[VMEM] * len(args), out_specs=[VMEM] * outs...  2.14 us
  transfers between devices with their start and end apart: 19, of which 11 were waited for; matrix products, arithmetic and copies ran while one was open for 0% of the time, Pallas kernels for 24%

profile of v13, /device:TPU:0, one launch (start us, length us, event | category | flops | bytes accessed | tf_op | source)
XLA Modules:
  0.0 91.8 jit_solution(17385527775751932139)
XLA Ops:
  0.7 0.7 concatenate.3.table_ref
  1.3 1.2 %masked_edges.1 = (bf16[4,128,256]{2,1,0:T(8,128)(2,1)S(1)}, bf16[4,128,256]{2,1,0:T(8,128)(2,1)S(1)}) custom-call(s32[9,32]{1,0:T(8,128)S(1)} %concatenate.3.table_ref, bf16[32,128,256]{2,1,0:T(8,128)(2,1)} %bitcast.16), custom_call_target="tpu_custom_call" | custom-call | flops 1000 | bytes 1000 | tf_op jit(solution)/shard_map/masked_edges/pallas_call | solution.py:109
  2.5 3.0 %collective-permute-start.1 = (bf16[4,128,256]{2,1,0:T(8,128)(2,1)S(1)}, bf16[4,128,256]{2,1,0:T(8,128)(2,1)S(1)}, u32[]{:S(2)}, u32[]{:S(2)}) collective-permute-start(bf16[4,128,256]{2,1,0:T(8,128)(2,1)S(1)} %get-tuple-element.37.refs_1_.refs_0_.refs_3_), channel_id=1, source_target_pairs={{0,1},{1,0},{2,3},{3,2},{4,5},{5,4},{6,7},{7,6},{8,9},{9,8},{10,11... | collective-permute-start | bytes 786440 | tf_op jit(solution)/shard_map/ppermute | solution.py:509
  5.6 2.1 %load_fields.1 = (bf16[24,128,256]{2,1,0:T(8,128)(2,1)S(1)}, bf16[4,8,128,128]{3,2,1,0:T(8,128)(2,1)S(1)}, bf16[4,8,128,128]{3,2,1,0:T(8,128)(2,1)S(1)}) custom-call(s32[9,32]{1,0:T(8,128)S(1)} %concatenate.3.table_ref, bf16[32,128,256]{2,1,0:T(8,128)(2,1)} %bitcast.17, bf16[32,8,128,128]{3,2,1,0:T(8,128)(2,1)} %blocks_ref.2), custom_call_target="tpu_custom_call" | custom-call | flops 1000 | bytes 1000 | tf_op jit(solution)/shard_map/load_fields/pallas_call | solution.py:109
  7.7 0.7 collective-permute-start
  8.4 3.5 %collective-permute-done.1.refs_0_ = bf16[4,128,256]{2,1,0:T(8,128)(2,1)S(1)} collective-permute-done((bf16[4,128,256]{2,1,0:T(8,128)(2,1)S(1)}, bf16[4,128,256]{2,1,0:T(8,128)(2,1)S(1)}, u32[]{:S(2)}, u32[]{:S(2)}) %collective-permute-start.1) | collective-permute-done | bytes 262176 | tf_op jit(solution)/shard_map/ppermute | solution.py:509
  11.9 1.1 %rows_even.3.refs_1_.refs_0_.refs_3_ = bf16[4,128,256]{2,1,0:T(8,128)(2,1)S(1)} custom-call(s32[9,32]{1,0:T(8,128)S(1)} %concatenate.3.table_ref, bf16[4,128,256]{2,1,0:T(8,128)(2,1)S(1)} %collective-permute-done.1.refs_0_, bf16[4,128,256]{2,1,0:T(8,128)(2,1)S(1)} %get-tuple-element.37.refs_1_.refs_0_.refs_3_, ...), custom_call_target="tpu_custom_call" | custom-call | flops 1000 | bytes 1000 | tf_op jit(solution)/shard_map/rows_even/pallas_call | solution.py:187
  13.0 1.8 %collective-permute-start.3 = (bf16[4,128,256]{2,1,0:T(8,128)(2,1)S(1)}, bf16[4,128,256]{2,1,0:T(8,128)(2,1)S(1)}, u32[]{:S(2)}, u32[]{:S(2)}) collective-permute-start(bf16[4,128,256]{2,1,0:T(8,128)(2,1)S(1)} %rows_even.3.refs_1_.refs_0_.refs_3_), channel_id=1, source_target_pairs={{0,1},{1,0},{2,3},{3,2},{4,5},{5,4},{6,7},{7,6},{8,9},{9,8},{10,11... | collective-permute-start | bytes 786440 | tf_op jit(solution)/shard_map/ppermute | solution.py:509
  14.8 2.9 %load_blocks.1.refs_3_.refs_4_ = bf16[24,8,128,128]{3,2,1,0:T(8,128)(2,1)S(1)} custom-call(bf16[32,8,128,128]{3,2,1,0:T(8,128)(2,1)} %blocks_ref.2), custom_call_target="tpu_custom_call" | custom-call | flops 1000 | bytes 1000 | tf_op jit(solution)/shard_map/load_blocks/pallas_call | solution.py:109
  17.7 2.7 %rows_inner.3.refs_2_.refs_3_ = bf16[24,128,256]{2,1,0:T(8,128)(2,1)S(1)} custom-call(s32[9,32]{1,0:T(8,128)S(1)} %concatenate.3.table_ref, bf16[4,128,256]{2,1,0:T(8,128)(2,1)S(1)} %get-tuple-element.37.refs_1_.refs_0_.refs_3_, bf16[4,128,256]{2,1,0:T(8,128)(2,1)S(1)} %get-tuple-element.34.refs_1_.refs_3_, ...), custom_call_target="tpu_custom_call" | custom-call | flops 1000 | bytes 1000 | tf_op jit(solution)/shard_map/rows_inner/pallas_call | solution.py:187
  20.4 0.0 collective-permute-done.refs_0_
  20.4 1.1 %rows_odd.3.refs_1_.refs_3_ = bf16[4,128,256]{2,1,0:T(8,128)(2,1)S(1)} custom-call(s32[9,32]{1,0:T(8,128)S(1)} %concatenate.3.table_ref, bf16[4,128,256]{2,1,0:T(8,128)(2,1)S(1)} %collective-permute-done.refs_0_, bf16[4,128,256]{2,1,0:T(8,128)(2,1)S(1)} %get-tuple-element.34.refs_1_.refs_3_, bf16[24,128,256]{2,1,0:T(8,128)(2,1)S(1)} %get-tuple-element.33.refs_2_.refs_3_, ...), custom_call_target="tpu_custom_call" | custom-call | flops 1000 | bytes 1000 | tf_op jit(solution)/shard_map/rows_odd/pallas_call | solution.py:187
  21.5 0.7 collective-permute-start.2
  22.2 1.8 %collective-permute-done.3.refs_0_ = bf16[4,128,256]{2,1,0:T(8,128)(2,1)S(1)} collective-permute-done((bf16[4,128,256]{2,1,0:T(8,128)(2,1)S(1)}, bf16[4,128,256]{2,1,0:T(8,128)(2,1)S(1)}, u32[]{:S(2)}, u32[]{:S(2)}) %collective-permute-start.3) | collective-permute-done | bytes 262176 | tf_op jit(solution)/shard_map/ppermute | solution.py:509
  24.0 1.1 %rows_even.4.refs_0_.refs_1_ = bf16[4,128,256]{2,1,0:T(8,128)(2,1)S(1)} custom-call(s32[9,32]{1,0:T(8,128)S(1)} %concatenate.3.table_ref, bf16[4,128,256]{2,1,0:T(8,128)(2,1)S(1)} %collective-permute-done.3.refs_0_, bf16[4,128,256]{2,1,0:T(8,128)(2,1)S(1)} %rows_even.3.refs_1_.refs_0_.refs_3_, bf16[24,128,256]{2,1,0:T(8,128)(2,1)S(1)} %rows_inner.3.refs_2_.refs_3_, ...), custom_call_target="tpu_custom_call" | custom-call | flops 1000 | bytes 1000 | tf_op jit(solution)/shard_map/rows_even/pallas_call | solution.py:187
  25.1 3.6 %collective-permute-start.5 = (bf16[4,128,256]{2,1,0:T(8,128)(2,1)S(1)}, bf16[4,128,256]{2,1,0:T(8,128)(2,1)S(1)}, u32[]{:S(2)}, u32[]{:S(2)}) collective-permute-start(bf16[4,128,256]{2,1,0:T(8,128)(2,1)S(1)} %rows_even.4.refs_0_.refs_1_), channel_id=1, source_target_pairs={{0,1},{1,0},{2,3},{3,2},{4,5},{5,4},{6,7},{7,6},{8,9},{9,8},{10,11... | collective-permute-start | bytes 786440 | tf_op jit(solution)/shard_map/ppermute | solution.py:509
  28.8 2.7 %rows_inner.4.refs_2_ = bf16[24,128,256]{2,1,0:T(8,128)(2,1)S(1)} custom-call(s32[9,32]{1,0:T(8,128)S(1)} %concatenate.3.table_ref, bf16[4,128,256]{2,1,0:T(8,128)(2,1)S(1)} %rows_even.3.refs_1_.refs_0_.refs_3_, bf16[4,128,256]{2,1,0:T(8,128)(2,1)S(1)} %rows_odd.3.refs_1_.refs_3_, bf16[24,128,256]{2,1,0:T(8,128)(2,1)S(1)} %rows_inner.3.refs_2_.refs_3_, ...), custom_call_target="tpu_custom_call" | custom-call | flops 1000 | bytes 1000 | tf_op jit(solution)/shard_map/rows_inner/pallas_call | solution.py:187
  31.5 0.0 collective-permute-done.2.refs_0_
  31.5 1.1 %rows_odd.4.refs_1_ = bf16[4,128,256]{2,1,0:T(8,128)(2,1)S(1)} custom-call(s32[9,32]{1,0:T(8,128)S(1)} %concatenate.3.table_ref, bf16[4,128,256]{2,1,0:T(8,128)(2,1)S(1)} %collective-permute-done.2.refs_0_, bf16[4,128,256]{2,1,0:T(8,128)(2,1)S(1)} %rows_odd.3.refs_1_.refs_3_, bf16[24,128,256]{2,1,0:T(8,128)(2,1)S(1)} %rows_inner.3.refs_2_.refs_3_, ...), custom_call_target="tpu_custom_call" | custom-call | flops 1000 | bytes 1000 | tf_op jit(solution)/shard_map/rows_odd/pallas_call | solution.py:187
  32.6 0.9 collective-permute-start.4
  33.5 2.7 %rows_inner.5 = bf16[24,128,256]{2,1,0:T(8,128)(2,1)S(1)} custom-call(s32[9,32]{1,0:T(8,128)S(1)} %concatenate.3.table_ref, bf16[4,128,256]{2,1,0:T(8,128)(2,1)S(1)} %rows_even.4.refs_0_.refs_1_, bf16[4,128,256]{2,1,0:T(8,128)(2,1)S(1)} %rows_odd.4.refs_1_, bf16[24,128,256]{2,1,0:T(8,128)(2,1)S(1)} %rows_inner.4.refs_2_, ...), custom_call_target="tpu_custom_call" | custom-call | flops 1000 | bytes 1000 | tf_op jit(solution)/shard_map/rows_inner/pallas_call | solution.py:187
  36.3 0.1 collective-permute-start.8
  36.3 2.3 %collective-permute-done.5.refs_0_ = bf16[4,128,256]{2,1,0:T(8,128)(2,1)S(1)} collective-permute-done((bf16[4,128,256]{2,1,0:T(8,128)(2,1)S(1)}, bf16[4,128,256]{2,1,0:T(8,128)(2,1)S(1)}, u32[]{:S(2)}, u32[]{:S(2)}) %collective-permute-start.5) | collective-permute-done | bytes 262176 | tf_op jit(solution)/shard_map/ppermute | solution.py:509
  38.6 1.1 %rows_even.5 = bf16[4,128,256]{2,1,0:T(8,128)(2,1)S(1)} custom-call(s32[9,32]{1,0:T(8,128)S(1)} %concatenate.3.table_ref, bf16[4,128,256]{2,1,0:T(8,128)(2,1)S(1)} %collective-permute-done.5.refs_0_, bf16[4,128,256]{2,1,0:T(8,128)(2,1)S(1)} %rows_even.4.refs_0_.refs_1_, bf16[24,128,256]{2,1,0:T(8,128)(2,1)S(1)} %rows_inner.4.refs_2_, ...), custom_call_target="tpu_custom_call" | custom-call | flops 1000 | bytes 1000 | tf_op jit(solution)/shard_map/rows_even/pallas_call | solution.py:187
  39.8 0.0 collective-permute-done.4.refs_0_
  39.8 0.1 collective-permute-start.7
  39.9 1.1 %rows_odd.5 = bf16[4,128,256]{2,1,0:T(8,128)(2,1)S(1)} custom-call(s32[9,32]{1,0:T(8,128)S(1)} %concatenate.3.table_ref, bf16[4,128,256]{2,1,0:T(8,128)(2,1)S(1)} %collective-permute-done.4.refs_0_, bf16[4,128,256]{2,1,0:T(8,128)(2,1)S(1)} %rows_odd.4.refs_1_, bf16[24,128,256]{2,1,0:T(8,128)(2,1)S(1)} %rows_inner.4.refs_2_, ...), custom_call_target="tpu_custom_call" | custom-call | flops 99999997952 | bytes 1000 | tf_op jit(solution)/shard_map/rows_odd/pallas_call | solution.py:187
  41.0 0.6 collective-permute-start.6
  41.6 0.0 collective-permute-done.7.refs_2_.refs_3_
  41.6 0.0 collective-permute-done.8.refs_3_.refs_4_
  41.6 1.7 %gram.1.start_ref = f32[256,512]{1,0:T(8,128)S(1)} custom-call(bf16[512,256]{1,0:T(8,128)(2,1)S(1)} %bitcast.11, bf16[3072,256]{1,0:T(8,128)(2,1)S(1)} %bitcast.8, bf16[512,256]{1,0:T(8,128)(2,1)S(1)} %collective-permute-done.7.refs_2_.refs_3_, bf16[3072,256]{1,0:T(8,128)(2,1)S(1)} %collective-permute-done.8.refs_3_.refs_4_), custom_call_target="tpu_custom_call" | custom-call | flops 1000 | bytes 1000 | tf_op jit(solution)/shard_map/gram/pallas_call | solution.py:256
  43.3 0.0 collective-permute-done.6.other_ref.refs_5_
  43.3 0.3 gram_share.1
  43.7 6.0 %collective-permute-start.10 = (f32[160,128]{1,0:T(8,128)S(1)}, f32[160,128]{1,0:T(8,128)S(1)}, u32[]{:S(2)}, u32[]{:S(2)}) collective-permute-start(f32[160,128]{1,0:T(8,128)S(1)} %get-tuple-element.53), channel_id=1, source_target_pairs={{0,2},{1,3},{2,0},{3,1},{4,6},{5,7},{6,4},{7,5},{8,10},{9,11},{10,... | collective-permute-start | bytes 245768 | tf_op jit(solution)/shard_map/ppermute | solution.py:309
  49.7 0.7 collective-permute-start.11
  50.4 0.8 collective-permute-start.9
  51.2 2.9 %collective-permute-done.10.c = f32[160,128]{1,0:T(8,128)S(1)} collective-permute-done((f32[160,128]{1,0:T(8,128)S(1)}, f32[160,128]{1,0:T(8,128)S(1)}, u32[]{:S(2)}, u32[]{:S(2)}) %collective-permute-start.10) | collective-permute-done | bytes 81952 | tf_op jit(solution)/shard_map/ppermute | solution.py:309
  54.2 1.0 %collective-permute-done.11.d = f32[160,128]{1,0:T(8,128)S(1)} collective-permute-done((f32[160,128]{1,0:T(8,128)S(1)}, f32[160,128]{1,0:T(8,128)S(1)}, u32[]{:S(2)}, u32[]{:S(2)}) %collective-permute-start.11) | collective-permute-done | bytes 81952 | tf_op jit(solution)/shard_map/ppermute | solution.py:309
  55.1 0.0 collective-permute-done.9.b
  55.2 1.6 %collective-permute-start.12 = (f32[160,128]{1,0:T(8,128)S(1)}, f32[160,128]{1,0:T(8,128)S(1)}, u32[]{:S(2)}, u32[]{:S(2)}) collective-permute-start(f32[160,128]{1,0:T(8,128)S(1)} %add_four.2.a), channel_id=1, source_target_pairs={{0,4},{1,5},{2,6},{3,7},{4,0},{5,1},{6,2},{7,3},{8,12},{9,13},{10,... | collective-permute-start | bytes 245768 | tf_op jit(solution)/shard_map/ppermute | solution.py:309
  56.8 2.6 %collective-permute-start.13 = (f32[160,128]{1,0:T(8,128)S(1)}, f32[160,128]{1,0:T(8,128)S(1)}, u32[]{:S(2)}, u32[]{:S(2)}) collective-permute-start(f32[160,128]{1,0:T(8,128)S(1)} %add_four.2.a), channel_id=1, source_target_pairs={{0,8},{1,9},{2,10},{3,11},{4,12},{5,13},{6,14},{7,15},{8,0},{9,1},... | collective-permute-start | bytes 245768 | tf_op jit(solution)/shard_map/ppermute | solution.py:309
  59.4 0.2 collective-permute-start.14
  59.6 0.1 collective-permute-done.12.b
  59.7 6.5 %collective-permute-done.13.c = f32[160,128]{1,0:T(8,128)S(1)} collective-permute-done((f32[160,128]{1,0:T(8,128)S(1)}, f32[160,128]{1,0:T(8,128)S(1)}, u32[]{:S(2)}, u32[]{:S(2)}) %collective-permute-start.13) | collective-permute-done | bytes 81952 | tf_op jit(solution)/shard_map/ppermute | solution.py:309
  66.2 0.0 collective-permute-done.14.d
  66.2 1.1 %collective-permute-start.15 = (f32[160,128]{1,0:T(8,128)S(1)}, f32[160,128]{1,0:T(8,128)S(1)}, u32[]{:S(2)}, u32[]{:S(2)}) collective-permute-start(f32[160,128]{1,0:T(8,128)S(1)} %add_four.3.refs_0_), channel_id=1, source_target_pairs={{0,1},{1,0},{2,3},{3,2},{4,5},{5,4},{6,7},{7,6},{8,9},{9,8},{10,11... | collective-permute-start | bytes 245768 | tf_op jit(solution)/shard_map/ppermute | solution.py:309
  67.3 1.2 %collective-permute-start.16 = (f32[160,128]{1,0:T(8,128)S(1)}, f32[160,128]{1,0:T(8,128)S(1)}, u32[]{:S(2)}, u32[]{:S(2)}) collective-permute-start(f32[160,128]{1,0:T(8,128)S(1)} %add_four.3.refs_0_), channel_id=1, source_target_pairs={{0,2},{1,3},{2,0},{3,1},{4,6},{5,7},{6,4},{7,5},{8,10},{9,11},{10,... | collective-permute-start | bytes 245768 | tf_op jit(solution)/shard_map/ppermute | solution.py:309
  68.5 1.3 %collective-permute-start.17 = (f32[160,128]{1,0:T(8,128)S(1)}, f32[160,128]{1,0:T(8,128)S(1)}, u32[]{:S(2)}, u32[]{:S(2)}) collective-permute-start(f32[160,128]{1,0:T(8,128)S(1)} %add_four.3.refs_0_), channel_id=1, source_target_pairs={{0,3},{1,2},{2,1},{3,0},{4,7},{5,6},{6,5},{7,4},{8,11},{9,10},{10,... | collective-permute-start | bytes 245768 | tf_op jit(solution)/shard_map/ppermute | solution.py:309
  69.8 1.0 %collective-permute-done.15.refs_1_ = f32[160,128]{1,0:T(8,128)S(1)} collective-permute-done((f32[160,128]{1,0:T(8,128)S(1)}, f32[160,128]{1,0:T(8,128)S(1)}, u32[]{:S(2)}, u32[]{:S(2)}) %collective-permute-start.15) | collective-permute-done | bytes 81952 | tf_op jit(solution)/shard_map/ppermute | solution.py:309
  70.8 1.0 %collective-permute-done.16.refs_2_ = f32[160,128]{1,0:T(8,128)S(1)} collective-permute-done((f32[160,128]{1,0:T(8,128)S(1)}, f32[160,128]{1,0:T(8,128)S(1)}, u32[]{:S(2)}, u32[]{:S(2)}) %collective-permute-start.16) | collective-permute-done | bytes 81952 | tf_op jit(solution)/shard_map/ppermute | solution.py:309
  71.8 2.1 %collective-permute-done.17.refs_3_ = f32[160,128]{1,0:T(8,128)S(1)} collective-permute-done((f32[160,128]{1,0:T(8,128)S(1)}, f32[160,128]{1,0:T(8,128)S(1)}, u32[]{:S(2)}, u32[]{:S(2)}) %collective-permute-start.17) | collective-permute-done | bytes 81952 | tf_op jit(solution)/shard_map/ppermute | solution.py:309
  73.9 0.1 collective-permute-start.18
  73.9 1.6 %collective-permute-done.18.theirs = f32[640,128]{1,0:T(8,128)S(1)} collective-permute-done((f32[640,128]{1,0:T(8,128)S(1)}, f32[640,128]{1,0:T(8,128)S(1)}, u32[]{:S(2)}, u32[]{:S(2)}) %collective-permute-start.18) | collective-permute-done | bytes 327712 | tf_op jit(solution)/shard_map/ppermute | solution.py:512
  75.6 16.0 %rotate.1 = bf16[4096,256]{1,0:T(8,128)(2,1)} custom-call(f32[640,128]{1,0:T(8,128)S(1)} %join.1.mine, f32[640,128]{1,0:T(8,128)S(1)} %collective-permute-done.18.theirs, bf16[512,256]{1,0:T(8,128)(2,1)S(1)} %bitcast.12, bf16[3072,256]{1,0:T(8,128)(2,1)S(1)} %bitcast.9, bf16[512,256]{1,0:T(8,128)(2,1)S(1)} %bitcast.15, ...), custom_call_target="tpu_custom_call" | custom-call | flops 17985175552 | bytes 6291456 | tf_op jit(solution)/shard_map/rotate/pallas_call | solution.py:471
  (3 shorter events, 0.1 us)
Async XLA Ops:
  2.5 9.3 %collective-permute-start.1 = (bf16[4,128,256]{2,1,0:T(8,128)(2,1)S(1)}, bf16[4,128,256]{2,1,0:T(8,128)(2,1)S(1)}, u32[]{:S(2)}, u32[]{:S(2)}) collective-permute-start(bf16[4,128,256]{2,1,0:T(8,128)(2,1)S(1)} %get-tuple-element.37.refs_1_.refs_0_.refs_3_), channel_id=1, source_target_pairs={{0,1},{1,0},{2,3},{3,2},{4,5},{5,4},{6,7},{7,6},{8,9},{9,8},{10,11... | collective-permute-start | bytes 786440 | tf_op jit(solution)/shard_map/ppermute | solution.py:509
  7.7 12.7 %collective-permute-start = (bf16[4,128,256]{2,1,0:T(8,128)(2,1)S(1)}, bf16[4,128,256]{2,1,0:T(8,128)(2,1)S(1)}, u32[]{:S(2)}, u32[]{:S(2)}) collective-permute-start(bf16[4,128,256]{2,1,0:T(8,128)(2,1)S(1)} %get-tuple-element.34.refs_1_.refs_3_), channel_id=1, source_target_pairs={{1,2},{2,1},{3,4},{4,3},{5,6},{6,5},{7,8},{8,7},{9,10},{10,9},{11,... | collective-permute-start | bytes 786440 | tf_op jit(solution)/shard_map/ppermute | solution.py:509
  13.0 11.0 %collective-permute-start.3 = (bf16[4,128,256]{2,1,0:T(8,128)(2,1)S(1)}, bf16[4,128,256]{2,1,0:T(8,128)(2,1)S(1)}, u32[]{:S(2)}, u32[]{:S(2)}) collective-permute-start(bf16[4,128,256]{2,1,0:T(8,128)(2,1)S(1)} %rows_even.3.refs_1_.refs_0_.refs_3_), channel_id=1, source_target_pairs={{0,1},{1,0},{2,3},{3,2},{4,5},{5,4},{6,7},{7,6},{8,9},{9,8},{10,11... | collective-permute-start | bytes 786440 | tf_op jit(solution)/shard_map/ppermute | solution.py:509
  21.5 10.0 %collective-permute-start.2 = (bf16[4,128,256]{2,1,0:T(8,128)(2,1)S(1)}, bf16[4,128,256]{2,1,0:T(8,128)(2,1)S(1)}, u32[]{:S(2)}, u32[]{:S(2)}) collective-permute-start(bf16[4,128,256]{2,1,0:T(8,128)(2,1)S(1)} %rows_odd.3.refs_1_.refs_3_), channel_id=1, source_target_pairs={{1,2},{2,1},{3,4},{4,3},{5,6},{6,5},{7,8},{8,7},{9,10},{10,9},{11,... | collective-permute-start | bytes 786440 | tf_op jit(solution)/shard_map/ppermute | solution.py:509
  25.1 13.5 %collective-permute-start.5 = (bf16[4,128,256]{2,1,0:T(8,128)(2,1)S(1)}, bf16[4,128,256]{2,1,0:T(8,128)(2,1)S(1)}, u32[]{:S(2)}, u32[]{:S(2)}) collective-permute-start(bf16[4,128,256]{2,1,0:T(8,128)(2,1)S(1)} %rows_even.4.refs_0_.refs_1_), channel_id=1, source_target_pairs={{0,1},{1,0},{2,3},{3,2},{4,5},{5,4},{6,7},{7,6},{8,9},{9,8},{10,11... | collective-permute-start | bytes 786440 | tf_op jit(solution)/shard_map/ppermute | solution.py:509
  32.6 7.1 %collective-permute-start.4 = (bf16[4,128,256]{2,1,0:T(8,128)(2,1)S(1)}, bf16[4,128,256]{2,1,0:T(8,128)(2,1)S(1)}, u32[]{:S(2)}, u32[]{:S(2)}) collective-permute-start(bf16[4,128,256]{2,1,0:T(8,128)(2,1)S(1)} %rows_odd.4.refs_1_), channel_id=1, source_target_pairs={{1,2},{2,1},{3,4},{4,3},{5,6},{6,5},{7,8},{8,7},{9,10},{10,9},{11,... | collective-permute-start | bytes 786440 | tf_op jit(solution)/shard_map/ppermute | solution.py:509
  36.3 5.3 %collective-permute-start.8 = (bf16[3072,256]{1,0:T(8,128)(2,1)S(1)}, bf16[3072,256]{1,0:T(8,128)(2,1)S(1)}, u32[]{:S(2)}, u32[]{:S(2)}) collective-permute-start(bf16[3072,256]{1,0:T(8,128)(2,1)S(1)} %bitcast.7), channel_id=1, source_target_pairs={{0,16},{16,0},{1,17},{17,1},{2,18},{18,2},{3,19},{19,3},{4,20},{20... | collective-permute-start | bytes 4718600 | tf_op jit(solution)/shard_map/ppermute | solution.py:512
  39.8 1.8 %collective-permute-start.7 = (bf16[512,256]{1,0:T(8,128)(2,1)S(1)}, bf16[512,256]{1,0:T(8,128)(2,1)S(1)}, u32[]{:S(2)}, u32[]{:S(2)}) collective-permute-start(bf16[512,256]{1,0:T(8,128)(2,1)S(1)} %bitcast.10), channel_id=1, source_target_pairs={{0,16},{16,0},{1,17},{17,1},{2,18},{18,2},{3,19},{19,3},{4,20},{20... | collective-permute-start | bytes 786440 | tf_op jit(solution)/shard_map/ppermute | solution.py:512
  41.0 2.3 %collective-permute-start.6 = (bf16[512,256]{1,0:T(8,128)(2,1)S(1)}, bf16[512,256]{1,0:T(8,128)(2,1)S(1)}, u32[]{:S(2)}, u32[]{:S(2)}) collective-permute-start(bf16[512,256]{1,0:T(8,128)(2,1)S(1)} %bitcast.13), channel_id=1, source_target_pairs={{0,16},{16,0},{1,17},{17,1},{2,18},{18,2},{3,19},{19,3},{4,20},{20... | collective-permute-start | bytes 786440 | tf_op jit(solution)/shard_map/ppermute | solution.py:512
  43.7 10.5 %collective-permute-start.10 = (f32[160,128]{1,0:T(8,128)S(1)}, f32[160,128]{1,0:T(8,128)S(1)}, u32[]{:S(2)}, u32[]{:S(2)}) collective-permute-start(f32[160,128]{1,0:T(8,128)S(1)} %get-tuple-element.53), channel_id=1, source_target_pairs={{0,2},{1,3},{2,0},{3,1},{4,6},{5,7},{6,4},{7,5},{8,10},{9,11},{10,... | collective-permute-start | bytes 245768 | tf_op jit(solution)/shard_map/ppermute | solution.py:309
  49.7 5.4 %collective-permute-start.11 = (f32[160,128]{1,0:T(8,128)S(1)}, f32[160,128]{1,0:T(8,128)S(1)}, u32[]{:S(2)}, u32[]{:S(2)}) collective-permute-start(f32[160,128]{1,0:T(8,128)S(1)} %get-tuple-element.54), channel_id=1, source_target_pairs={{0,3},{1,2},{2,1},{3,0},{4,7},{5,6},{6,5},{7,4},{8,11},{9,10},{10,... | collective-permute-start | bytes 245768 | tf_op jit(solution)/shard_map/ppermute | solution.py:309
  50.4 4.7 %collective-permute-start.9 = (f32[160,128]{1,0:T(8,128)S(1)}, f32[160,128]{1,0:T(8,128)S(1)}, u32[]{:S(2)}, u32[]{:S(2)}) collective-permute-start(f32[160,128]{1,0:T(8,128)S(1)} %get-tuple-element.52), channel_id=1, source_target_pairs={{0,1},{1,0},{2,3},{3,2},{4,5},{5,4},{6,7},{7,6},{8,9},{9,8},{10,11... | collective-permute-start | bytes 245768 | tf_op jit(solution)/shard_map/ppermute | solution.py:309
  55.2 4.5 %collective-permute-start.12 = (f32[160,128]{1,0:T(8,128)S(1)}, f32[160,128]{1,0:T(8,128)S(1)}, u32[]{:S(2)}, u32[]{:S(2)}) collective-permute-start(f32[160,128]{1,0:T(8,128)S(1)} %add_four.2.a), channel_id=1, source_target_pairs={{0,4},{1,5},{2,6},{3,7},{4,0},{5,1},{6,2},{7,3},{8,12},{9,13},{10,... | collective-permute-start | bytes 245768 | tf_op jit(solution)/shard_map/ppermute | solution.py:309
  56.8 9.4 %collective-permute-start.13 = (f32[160,128]{1,0:T(8,128)S(1)}, f32[160,128]{1,0:T(8,128)S(1)}, u32[]{:S(2)}, u32[]{:S(2)}) collective-permute-start(f32[160,128]{1,0:T(8,128)S(1)} %add_four.2.a), channel_id=1, source_target_pairs={{0,8},{1,9},{2,10},{3,11},{4,12},{5,13},{6,14},{7,15},{8,0},{9,1},... | collective-permute-start | bytes 245768 | tf_op jit(solution)/shard_map/ppermute | solution.py:309
  59.4 6.8 %collective-permute-start.14 = (f32[160,128]{1,0:T(8,128)S(1)}, f32[160,128]{1,0:T(8,128)S(1)}, u32[]{:S(2)}, u32[]{:S(2)}) collective-permute-start(f32[160,128]{1,0:T(8,128)S(1)} %add_four.2.a), channel_id=1, source_target_pairs={{0,12},{1,13},{2,14},{3,15},{4,8},{5,9},{6,10},{7,11},{8,4},{9,5},... | collective-permute-start | bytes 245768 | tf_op jit(solution)/shard_map/ppermute | solution.py:309
  66.2 4.6 %collective-permute-start.15 = (f32[160,128]{1,0:T(8,128)S(1)}, f32[160,128]{1,0:T(8,128)S(1)}, u32[]{:S(2)}, u32[]{:S(2)}) collective-permute-start(f32[160,128]{1,0:T(8,128)S(1)} %add_four.3.refs_0_), channel_id=1, source_target_pairs={{0,1},{1,0},{2,3},{3,2},{4,5},{5,4},{6,7},{7,6},{8,9},{9,8},{10,11... | collective-permute-start | bytes 245768 | tf_op jit(solution)/shard_map/ppermute | solution.py:309
  67.3 4.4 %collective-permute-start.16 = (f32[160,128]{1,0:T(8,128)S(1)}, f32[160,128]{1,0:T(8,128)S(1)}, u32[]{:S(2)}, u32[]{:S(2)}) collective-permute-start(f32[160,128]{1,0:T(8,128)S(1)} %add_four.3.refs_0_), channel_id=1, source_target_pairs={{0,2},{1,3},{2,0},{3,1},{4,6},{5,7},{6,4},{7,5},{8,10},{9,11},{10,... | collective-permute-start | bytes 245768 | tf_op jit(solution)/shard_map/ppermute | solution.py:309
  68.5 5.3 %collective-permute-start.17 = (f32[160,128]{1,0:T(8,128)S(1)}, f32[160,128]{1,0:T(8,128)S(1)}, u32[]{:S(2)}, u32[]{:S(2)}) collective-permute-start(f32[160,128]{1,0:T(8,128)S(1)} %add_four.3.refs_0_), channel_id=1, source_target_pairs={{0,3},{1,2},{2,1},{3,0},{4,7},{5,6},{6,5},{7,4},{8,11},{9,10},{10,... | collective-permute-start | bytes 245768 | tf_op jit(solution)/shard_map/ppermute | solution.py:309
  73.9 1.7 %collective-permute-start.18 = (f32[640,128]{1,0:T(8,128)S(1)}, f32[640,128]{1,0:T(8,128)S(1)}, u32[]{:S(2)}, u32[]{:S(2)}) collective-permute-start(f32[640,128]{1,0:T(8,128)S(1)} %join.1.mine), channel_id=1, source_target_pairs={{0,16},{16,0},{1,17},{17,1},{2,18},{18,2},{3,19},{19,3},{4,20},{20... | collective-permute-start | bytes 983048 | tf_op jit(solution)/shard_map/ppermute | solution.py:512

commit v14 on v13

--- a/solution.py
+++ b/solution.py
@@ -203,14 +203,15 @@
 ACROSS = (((0,), (0,)), ((), ()))
 
 
-NEAR = (1, 2, 3), (2, 1, 3)
-FAR = (1, 2, 3), (1, 2, 3)
-
-
-def quarter_order():
+SPREAD = (2, 3, 1), (1, 3, 2)
+ACROSS_GROUPS = (3, 2, 1), (2, 3, 1)
+GATHER = (3, 1, 2), (3, 2, 1)
+
+
+def quarter_order(distances):
     own = lax.axis_index("patch") % WAYS
     first_core = lax.axis_index("cols") == 0
-    return [own] + [own ^ jnp.where(first_core, one, two) for one, two in zip(*NEAR)]
+    return [own] + [own ^ jnp.where(first_core, one, two) for one, two in zip(*distances)]
 
 
 def add_gram(chunk, own_ref, other_ref, total):
@@ -246,7 +247,7 @@
     blocks = [own[:half, :half], own[:half, half:], own[half:, half:], second, third]
     for i, block in enumerate(blocks):
         share[pl.ds(i * half, half), :] = block
-    for out, quarter in zip(outs, quarter_order()):
+    for out, quarter in zip(outs, quarter_order(SPREAD)):
         rows = out.shape[0]
         out[...] = share[pl.ds(pl.multiple_of(quarter * rows, 8), rows), :]
 
@@ -287,7 +288,7 @@
 def join_kernel(*refs):
     parts, out = refs[:-1], refs[-1]
     rows = parts[0].shape[0]
-    for part, quarter in zip(parts, quarter_order()):
+    for part, quarter in zip(parts, quarter_order(GATHER)):
         out[pl.ds(pl.multiple_of(quarter * rows, 8), rows), :] = part[...]
 
 
@@ -309,12 +310,12 @@
             got.append(lax.ppermute(value, ("cols", "patch"), pairs))
         return got
 
-    total = add_four([parts[0]] + from_others(parts[1:], NEAR))
+    total = add_four([parts[0]] + from_others(parts[1:], SPREAD))
     stride = WAYS
     while stride < count:
-        total = add_four([total] + from_others([total] * (WAYS - 1), FAR, stride))
+        total = add_four([total] + from_others([total] * (WAYS - 1), ACROSS_GROUPS, stride))
         stride *= WAYS
-    quarters = [total] + from_others([total] * (WAYS - 1), NEAR)
+    quarters = [total] + from_others([total] * (WAYS - 1), GATHER)
     return gram_call(join_kernel, "join", quarters, (WAYS * rows, columns))
 
 

time: 92 us -> 90.5 us (0.984)
  waiting for transfers between devices: 23.8 us -> 22.2 us
    ppermute x9, waiting for transfers between devices: 14.5 us -> 13.1 us  [from_others(): got.append(lax.ppermute(value, ('cols', 'patch'), pairs))]
  transfers between devices with their start and end apart: 19 -> 19, of which waited for: 11 -> 12; matrix products, arithmetic and copies ran while one was open for 0% -> 0% of each run, Pallas kernels for 24% -> 24%
where the time goes in v14:
time: 90.5 us; the launch traced here: 90.3 us
  Pallas kernels  39.3 us (43%)
  starting transfers between devices  27 us (30%)
  waiting for transfers between devices  22.2 us (25%)
  between operations  1.05 us (1%)
    pallas_call x1, Pallas kernels, rotate(): pl.pallas_call(body, in_specs=[VMEM, VMEM] + [ANY] * 6, out_specs=ANY, ou...  16 us
    ppermute x9, starting transfers between devices, from_others(): got.append(lax.ppermute(value, ('cols', 'patch'), pairs))  15.5 us
    pallas_call x9, Pallas kernels, tile_rows(): pl.pallas_call(functools.partial(rows_kernel, name), in_specs=[VMEM] * le...  14.9 us
    ppermute x9, waiting for transfers between devices, from_others(): got.append(lax.ppermute(value, ('cols', 'patch'), pairs))  13.1 us
    ppermute x6, starting transfers between devices, exchange(): return lax.ppermute(value, 'patch', pairs[name])  10.7 us
    ppermute x6, waiting for transfers between devices, exchange(): return lax.ppermute(value, 'patch', pairs[name])  7.53 us
    pallas_call x3, Pallas kernels, load_call(): pl.pallas_call(body, in_specs=[VMEM] * len(table) + [HBM] * len(args), ou...  6.23 us
    pallas_call x5, Pallas kernels, gram_call(): pl.pallas_call(body, in_specs=[VMEM] * len(args), out_specs=[VMEM] * outs...  2.14 us
  transfers between devices with their start and end apart: 19, of which 12 were waited for; matrix products, arithmetic and copies ran while one was open for 0% of the time, Pallas kernels for 24%

profile of v14, /device:TPU:0, one launch (start us, length us, event | category | flops | bytes accessed | tf_op | source)
XLA Modules:
  0.0 90.3 jit_solution(6101777336262181824)
XLA Ops:
  0.7 0.7 concatenate.3.table_ref
  1.3 1.2 %masked_edges.1 = (bf16[4,128,256]{2,1,0:T(8,128)(2,1)S(1)}, bf16[4,128,256]{2,1,0:T(8,128)(2,1)S(1)}) custom-call(s32[9,32]{1,0:T(8,128)S(1)} %concatenate.3.table_ref, bf16[32,128,256]{2,1,0:T(8,128)(2,1)} %bitcast.16), custom_call_target="tpu_custom_call" | custom-call | flops 1000 | bytes 1000 | tf_op jit(solution)/shard_map/masked_edges/pallas_call | solution.py:109
  2.5 3.0 %collective-permute-start.1 = (bf16[4,128,256]{2,1,0:T(8,128)(2,1)S(1)}, bf16[4,128,256]{2,1,0:T(8,128)(2,1)S(1)}, u32[]{:S(2)}, u32[]{:S(2)}) collective-permute-start(bf16[4,128,256]{2,1,0:T(8,128)(2,1)S(1)} %get-tuple-element.37.refs_1_.refs_0_.refs_3_), channel_id=1, source_target_pairs={{0,1},{1,0},{2,3},{3,2},{4,5},{5,4},{6,7},{7,6},{8,9},{9,8},{10,11... | collective-permute-start | bytes 786440 | tf_op jit(solution)/shard_map/ppermute | solution.py:510
  5.5 2.2 %load_fields.1 = (bf16[24,128,256]{2,1,0:T(8,128)(2,1)S(1)}, bf16[4,8,128,128]{3,2,1,0:T(8,128)(2,1)S(1)}, bf16[4,8,128,128]{3,2,1,0:T(8,128)(2,1)S(1)}) custom-call(s32[9,32]{1,0:T(8,128)S(1)} %concatenate.3.table_ref, bf16[32,128,256]{2,1,0:T(8,128)(2,1)} %bitcast.17, bf16[32,8,128,128]{3,2,1,0:T(8,128)(2,1)} %blocks_ref.2), custom_call_target="tpu_custom_call" | custom-call | flops 1000 | bytes 1000 | tf_op jit(solution)/shard_map/load_fields/pallas_call | solution.py:109
  7.7 0.7 collective-permute-start
  8.4 3.4 %collective-permute-done.1.refs_0_ = bf16[4,128,256]{2,1,0:T(8,128)(2,1)S(1)} collective-permute-done((bf16[4,128,256]{2,1,0:T(8,128)(2,1)S(1)}, bf16[4,128,256]{2,1,0:T(8,128)(2,1)S(1)}, u32[]{:S(2)}, u32[]{:S(2)}) %collective-permute-start.1) | collective-permute-done | bytes 262176 | tf_op jit(solution)/shard_map/ppermute | solution.py:510
  11.8 1.1 %rows_even.3.refs_1_.refs_0_.refs_3_ = bf16[4,128,256]{2,1,0:T(8,128)(2,1)S(1)} custom-call(s32[9,32]{1,0:T(8,128)S(1)} %concatenate.3.table_ref, bf16[4,128,256]{2,1,0:T(8,128)(2,1)S(1)} %collective-permute-done.1.refs_0_, bf16[4,128,256]{2,1,0:T(8,128)(2,1)S(1)} %get-tuple-element.37.refs_1_.refs_0_.refs_3_, ...), custom_call_target="tpu_custom_call" | custom-call | flops 1000 | bytes 1000 | tf_op jit(solution)/shard_map/rows_even/pallas_call | solution.py:187
  13.0 1.8 %collective-permute-start.3 = (bf16[4,128,256]{2,1,0:T(8,128)(2,1)S(1)}, bf16[4,128,256]{2,1,0:T(8,128)(2,1)S(1)}, u32[]{:S(2)}, u32[]{:S(2)}) collective-permute-start(bf16[4,128,256]{2,1,0:T(8,128)(2,1)S(1)} %rows_even.3.refs_1_.refs_0_.refs_3_), channel_id=1, source_target_pairs={{0,1},{1,0},{2,3},{3,2},{4,5},{5,4},{6,7},{7,6},{8,9},{9,8},{10,11... | collective-permute-start | bytes 786440 | tf_op jit(solution)/shard_map/ppermute | solution.py:510
  14.8 2.9 %load_blocks.1.refs_3_.refs_4_ = bf16[24,8,128,128]{3,2,1,0:T(8,128)(2,1)S(1)} custom-call(bf16[32,8,128,128]{3,2,1,0:T(8,128)(2,1)} %blocks_ref.2), custom_call_target="tpu_custom_call" | custom-call | flops 1000 | bytes 1000 | tf_op jit(solution)/shard_map/load_blocks/pallas_call | solution.py:109
  17.7 2.7 %rows_inner.3.refs_2_.refs_3_ = bf16[24,128,256]{2,1,0:T(8,128)(2,1)S(1)} custom-call(s32[9,32]{1,0:T(8,128)S(1)} %concatenate.3.table_ref, bf16[4,128,256]{2,1,0:T(8,128)(2,1)S(1)} %get-tuple-element.37.refs_1_.refs_0_.refs_3_, bf16[4,128,256]{2,1,0:T(8,128)(2,1)S(1)} %get-tuple-element.34.refs_1_.refs_3_, ...), custom_call_target="tpu_custom_call" | custom-call | flops 1000 | bytes 1000 | tf_op jit(solution)/shard_map/rows_inner/pallas_call | solution.py:187
  20.4 0.0 collective-permute-done.refs_0_
  20.4 1.1 %rows_odd.3.refs_1_.refs_3_ = bf16[4,128,256]{2,1,0:T(8,128)(2,1)S(1)} custom-call(s32[9,32]{1,0:T(8,128)S(1)} %concatenate.3.table_ref, bf16[4,128,256]{2,1,0:T(8,128)(2,1)S(1)} %collective-permute-done.refs_0_, bf16[4,128,256]{2,1,0:T(8,128)(2,1)S(1)} %get-tuple-element.34.refs_1_.refs_3_, bf16[24,128,256]{2,1,0:T(8,128)(2,1)S(1)} %get-tuple-element.33.refs_2_.refs_3_, ...), custom_call_target="tpu_custom_call" | custom-call | flops 1000 | bytes 1000 | tf_op jit(solution)/shard_map/rows_odd/pallas_call | solution.py:187
  21.5 0.7 collective-permute-start.2
  22.2 1.8 %collective-permute-done.3.refs_0_ = bf16[4,128,256]{2,1,0:T(8,128)(2,1)S(1)} collective-permute-done((bf16[4,128,256]{2,1,0:T(8,128)(2,1)S(1)}, bf16[4,128,256]{2,1,0:T(8,128)(2,1)S(1)}, u32[]{:S(2)}, u32[]{:S(2)}) %collective-permute-start.3) | collective-permute-done | bytes 262176 | tf_op jit(solution)/shard_map/ppermute | solution.py:510
  24.0 1.1 %rows_even.4.refs_0_.refs_1_ = bf16[4,128,256]{2,1,0:T(8,128)(2,1)S(1)} custom-call(s32[9,32]{1,0:T(8,128)S(1)} %concatenate.3.table_ref, bf16[4,128,256]{2,1,0:T(8,128)(2,1)S(1)} %collective-permute-done.3.refs_0_, bf16[4,128,256]{2,1,0:T(8,128)(2,1)S(1)} %rows_even.3.refs_1_.refs_0_.refs_3_, bf16[24,128,256]{2,1,0:T(8,128)(2,1)S(1)} %rows_inner.3.refs_2_.refs_3_, ...), custom_call_target="tpu_custom_call" | custom-call | flops 1000 | bytes 1000 | tf_op jit(solution)/shard_map/rows_even/pallas_call | solution.py:187
  25.1 3.7 %collective-permute-start.5 = (bf16[4,128,256]{2,1,0:T(8,128)(2,1)S(1)}, bf16[4,128,256]{2,1,0:T(8,128)(2,1)S(1)}, u32[]{:S(2)}, u32[]{:S(2)}) collective-permute-start(bf16[4,128,256]{2,1,0:T(8,128)(2,1)S(1)} %rows_even.4.refs_0_.refs_1_), channel_id=1, source_target_pairs={{0,1},{1,0},{2,3},{3,2},{4,5},{5,4},{6,7},{7,6},{8,9},{9,8},{10,11... | collective-permute-start | bytes 786440 | tf_op jit(solution)/shard_map/ppermute | solution.py:510
  28.8 2.7 %rows_inner.4.refs_2_ = bf16[24,128,256]{2,1,0:T(8,128)(2,1)S(1)} custom-call(s32[9,32]{1,0:T(8,128)S(1)} %concatenate.3.table_ref, bf16[4,128,256]{2,1,0:T(8,128)(2,1)S(1)} %rows_even.3.refs_1_.refs_0_.refs_3_, bf16[4,128,256]{2,1,0:T(8,128)(2,1)S(1)} %rows_odd.3.refs_1_.refs_3_, bf16[24,128,256]{2,1,0:T(8,128)(2,1)S(1)} %rows_inner.3.refs_2_.refs_3_, ...), custom_call_target="tpu_custom_call" | custom-call | flops 1000 | bytes 1000 | tf_op jit(solution)/shard_map/rows_inner/pallas_call | solution.py:187
  31.5 0.0 collective-permute-done.2.refs_0_
  31.5 1.1 %rows_odd.4.refs_1_ = bf16[4,128,256]{2,1,0:T(8,128)(2,1)S(1)} custom-call(s32[9,32]{1,0:T(8,128)S(1)} %concatenate.3.table_ref, bf16[4,128,256]{2,1,0:T(8,128)(2,1)S(1)} %collective-permute-done.2.refs_0_, bf16[4,128,256]{2,1,0:T(8,128)(2,1)S(1)} %rows_odd.3.refs_1_.refs_3_, bf16[24,128,256]{2,1,0:T(8,128)(2,1)S(1)} %rows_inner.3.refs_2_.refs_3_, ...), custom_call_target="tpu_custom_call" | custom-call | flops 1000 | bytes 1000 | tf_op jit(solution)/shard_map/rows_odd/pallas_call | solution.py:187
  32.6 0.9 collective-permute-start.4
  33.5 2.7 %rows_inner.5 = bf16[24,128,256]{2,1,0:T(8,128)(2,1)S(1)} custom-call(s32[9,32]{1,0:T(8,128)S(1)} %concatenate.3.table_ref, bf16[4,128,256]{2,1,0:T(8,128)(2,1)S(1)} %rows_even.4.refs_0_.refs_1_, bf16[4,128,256]{2,1,0:T(8,128)(2,1)S(1)} %rows_odd.4.refs_1_, bf16[24,128,256]{2,1,0:T(8,128)(2,1)S(1)} %rows_inner.4.refs_2_, ...), custom_call_target="tpu_custom_call" | custom-call | flops 1000 | bytes 1000 | tf_op jit(solution)/shard_map/rows_inner/pallas_call | solution.py:187
  36.3 0.1 collective-permute-start.8
  36.3 2.3 %collective-permute-done.5.refs_0_ = bf16[4,128,256]{2,1,0:T(8,128)(2,1)S(1)} collective-permute-done((bf16[4,128,256]{2,1,0:T(8,128)(2,1)S(1)}, bf16[4,128,256]{2,1,0:T(8,128)(2,1)S(1)}, u32[]{:S(2)}, u32[]{:S(2)}) %collective-permute-start.5) | collective-permute-done | bytes 262176 | tf_op jit(solution)/shard_map/ppermute | solution.py:510
  38.6 1.1 %rows_even.5 = bf16[4,128,256]{2,1,0:T(8,128)(2,1)S(1)} custom-call(s32[9,32]{1,0:T(8,128)S(1)} %concatenate.3.table_ref, bf16[4,128,256]{2,1,0:T(8,128)(2,1)S(1)} %collective-permute-done.5.refs_0_, bf16[4,128,256]{2,1,0:T(8,128)(2,1)S(1)} %rows_even.4.refs_0_.refs_1_, bf16[24,128,256]{2,1,0:T(8,128)(2,1)S(1)} %rows_inner.4.refs_2_, ...), custom_call_target="tpu_custom_call" | custom-call | flops 1000 | bytes 1000 | tf_op jit(solution)/shard_map/rows_even/pallas_call | solution.py:187
  39.8 0.0 collective-permute-done.4.refs_0_
  39.8 0.1 collective-permute-start.7
  39.9 1.1 %rows_odd.5 = bf16[4,128,256]{2,1,0:T(8,128)(2,1)S(1)} custom-call(s32[9,32]{1,0:T(8,128)S(1)} %concatenate.3.table_ref, bf16[4,128,256]{2,1,0:T(8,128)(2,1)S(1)} %collective-permute-done.4.refs_0_, bf16[4,128,256]{2,1,0:T(8,128)(2,1)S(1)} %rows_odd.4.refs_1_, bf16[24,128,256]{2,1,0:T(8,128)(2,1)S(1)} %rows_inner.4.refs_2_, ...), custom_call_target="tpu_custom_call" | custom-call | flops 99999997952 | bytes 1000 | tf_op jit(solution)/shard_map/rows_odd/pallas_call | solution.py:187
  41.0 0.6 collective-permute-start.6
  41.6 0.0 collective-permute-done.7.refs_2_.refs_3_
  41.6 0.0 collective-permute-done.8.refs_3_.refs_4_
  41.6 1.7 %gram.1.start_ref = f32[256,512]{1,0:T(8,128)S(1)} custom-call(bf16[512,256]{1,0:T(8,128)(2,1)S(1)} %bitcast.11, bf16[3072,256]{1,0:T(8,128)(2,1)S(1)} %bitcast.8, bf16[512,256]{1,0:T(8,128)(2,1)S(1)} %collective-permute-done.7.refs_2_.refs_3_, bf16[3072,256]{1,0:T(8,128)(2,1)S(1)} %collective-permute-done.8.refs_3_.refs_4_), custom_call_target="tpu_custom_call" | custom-call | flops 1000 | bytes 1000 | tf_op jit(solution)/shard_map/gram/pallas_call | solution.py:257
  43.3 0.0 collective-permute-done.6.other_ref.refs_5_
  43.3 0.3 gram_share.1
  43.7 5.2 %collective-permute-start.10 = (f32[160,128]{1,0:T(8,128)S(1)}, f32[160,128]{1,0:T(8,128)S(1)}, u32[]{:S(2)}, u32[]{:S(2)}) collective-permute-start(f32[160,128]{1,0:T(8,128)S(1)} %get-tuple-element.53), channel_id=1, source_target_pairs={{0,3},{1,2},{2,1},{3,0},{4,7},{5,6},{6,5},{7,4},{8,11},{9,10},{10,... | collective-permute-start | bytes 245768 | tf_op jit(solution)/shard_map/ppermute | solution.py:310
  48.8 2.3 %collective-permute-start.11 = (f32[160,128]{1,0:T(8,128)S(1)}, f32[160,128]{1,0:T(8,128)S(1)}, u32[]{:S(2)}, u32[]{:S(2)}) collective-permute-start(f32[160,128]{1,0:T(8,128)S(1)} %get-tuple-element.54), channel_id=1, source_target_pairs={{0,1},{1,0},{2,3},{3,2},{4,5},{5,4},{6,7},{7,6},{8,9},{9,8},{10,11... | collective-permute-start | bytes 245768 | tf_op jit(solution)/shard_map/ppermute | solution.py:310
  51.2 0.0 collective-permute-start.9
  51.2 0.3 collective-permute-done.10.c
  51.5 3.8 %collective-permute-done.11.d = f32[160,128]{1,0:T(8,128)S(1)} collective-permute-done((f32[160,128]{1,0:T(8,128)S(1)}, f32[160,128]{1,0:T(8,128)S(1)}, u32[]{:S(2)}, u32[]{:S(2)}) %collective-permute-start.11) | collective-permute-done | bytes 81952 | tf_op jit(solution)/shard_map/ppermute | solution.py:310
  55.3 0.3 collective-permute-done.9.b
  55.6 3.7 %collective-permute-start.12 = (f32[160,128]{1,0:T(8,128)S(1)}, f32[160,128]{1,0:T(8,128)S(1)}, u32[]{:S(2)}, u32[]{:S(2)}) collective-permute-start(f32[160,128]{1,0:T(8,128)S(1)} %add_four.2.a), channel_id=1, source_target_pairs={{0,12},{1,13},{2,14},{3,15},{4,8},{5,9},{6,10},{7,11},{8,4},{9,5},... | collective-permute-start | bytes 245768 | tf_op jit(solution)/shard_map/ppermute | solution.py:310
  59.3 0.0 collective-permute-start.13
  59.3 0.8 collective-permute-start.14
  60.1 2.8 %collective-permute-done.12.b = f32[160,128]{1,0:T(8,128)S(1)} collective-permute-done((f32[160,128]{1,0:T(8,128)S(1)}, f32[160,128]{1,0:T(8,128)S(1)}, u32[]{:S(2)}, u32[]{:S(2)}) %collective-permute-start.12) | collective-permute-done | bytes 81952 | tf_op jit(solution)/shard_map/ppermute | solution.py:310
  62.9 2.6 %collective-permute-done.13.c = f32[160,128]{1,0:T(8,128)S(1)} collective-permute-done((f32[160,128]{1,0:T(8,128)S(1)}, f32[160,128]{1,0:T(8,128)S(1)}, u32[]{:S(2)}, u32[]{:S(2)}) %collective-permute-start.13) | collective-permute-done | bytes 81952 | tf_op jit(solution)/shard_map/ppermute | solution.py:310
  65.4 0.0 collective-permute-done.14.d
  65.5 1.6 %collective-permute-start.15 = (f32[160,128]{1,0:T(8,128)S(1)}, f32[160,128]{1,0:T(8,128)S(1)}, u32[]{:S(2)}, u32[]{:S(2)}) collective-permute-start(f32[160,128]{1,0:T(8,128)S(1)} %add_four.3.refs_0_), channel_id=1, source_target_pairs={{0,3},{1,2},{2,1},{3,0},{4,7},{5,6},{6,5},{7,4},{8,11},{9,10},{10,... | collective-permute-start | bytes 245768 | tf_op jit(solution)/shard_map/ppermute | solution.py:310
  67.1 0.8 collective-permute-start.16
  67.9 1.1 %collective-permute-start.17 = (f32[160,128]{1,0:T(8,128)S(1)}, f32[160,128]{1,0:T(8,128)S(1)}, u32[]{:S(2)}, u32[]{:S(2)}) collective-permute-start(f32[160,128]{1,0:T(8,128)S(1)} %add_four.3.refs_0_), channel_id=1, source_target_pairs={{0,2},{1,3},{2,0},{3,1},{4,6},{5,7},{6,4},{7,5},{8,10},{9,11},{10,... | collective-permute-start | bytes 245768 | tf_op jit(solution)/shard_map/ppermute | solution.py:310
  69.0 1.9 %collective-permute-done.15.refs_1_ = f32[160,128]{1,0:T(8,128)S(1)} collective-permute-done((f32[160,128]{1,0:T(8,128)S(1)}, f32[160,128]{1,0:T(8,128)S(1)}, u32[]{:S(2)}, u32[]{:S(2)}) %collective-permute-start.15) | collective-permute-done | bytes 81952 | tf_op jit(solution)/shard_map/ppermute | solution.py:310
  70.9 0.6 collective-permute-done.16.refs_2_
  71.5 0.8 collective-permute-done.17.refs_3_
  72.4 0.1 collective-permute-start.18
  72.4 1.6 %collective-permute-done.18.theirs = f32[640,128]{1,0:T(8,128)S(1)} collective-permute-done((f32[640,128]{1,0:T(8,128)S(1)}, f32[640,128]{1,0:T(8,128)S(1)}, u32[]{:S(2)}, u32[]{:S(2)}) %collective-permute-start.18) | collective-permute-done | bytes 327712 | tf_op jit(solution)/shard_map/ppermute | solution.py:513
  74.1 16.0 %rotate.1 = bf16[4096,256]{1,0:T(8,128)(2,1)} custom-call(f32[640,128]{1,0:T(8,128)S(1)} %join.1.mine, f32[640,128]{1,0:T(8,128)S(1)} %collective-permute-done.18.theirs, bf16[512,256]{1,0:T(8,128)(2,1)S(1)} %bitcast.12, bf16[3072,256]{1,0:T(8,128)(2,1)S(1)} %bitcast.9, bf16[512,256]{1,0:T(8,128)(2,1)S(1)} %bitcast.15, ...), custom_call_target="tpu_custom_call" | custom-call | flops 17985175552 | bytes 6291456 | tf_op jit(solution)/shard_map/rotate/pallas_call | solution.py:472
  (3 shorter events, 0.1 us)
Async XLA Ops:
  2.5 9.3 %collective-permute-start.1 = (bf16[4,128,256]{2,1,0:T(8,128)(2,1)S(1)}, bf16[4,128,256]{2,1,0:T(8,128)(2,1)S(1)}, u32[]{:S(2)}, u32[]{:S(2)}) collective-permute-start(bf16[4,128,256]{2,1,0:T(8,128)(2,1)S(1)} %get-tuple-element.37.refs_1_.refs_0_.refs_3_), channel_id=1, source_target_pairs={{0,1},{1,0},{2,3},{3,2},{4,5},{5,4},{6,7},{7,6},{8,9},{9,8},{10,11... | collective-permute-start | bytes 786440 | tf_op jit(solution)/shard_map/ppermute | solution.py:510
  7.7 12.7 %collective-permute-start = (bf16[4,128,256]{2,1,0:T(8,128)(2,1)S(1)}, bf16[4,128,256]{2,1,0:T(8,128)(2,1)S(1)}, u32[]{:S(2)}, u32[]{:S(2)}) collective-permute-start(bf16[4,128,256]{2,1,0:T(8,128)(2,1)S(1)} %get-tuple-element.34.refs_1_.refs_3_), channel_id=1, source_target_pairs={{1,2},{2,1},{3,4},{4,3},{5,6},{6,5},{7,8},{8,7},{9,10},{10,9},{11,... | collective-permute-start | bytes 786440 | tf_op jit(solution)/shard_map/ppermute | solution.py:510
  13.0 11.0 %collective-permute-start.3 = (bf16[4,128,256]{2,1,0:T(8,128)(2,1)S(1)}, bf16[4,128,256]{2,1,0:T(8,128)(2,1)S(1)}, u32[]{:S(2)}, u32[]{:S(2)}) collective-permute-start(bf16[4,128,256]{2,1,0:T(8,128)(2,1)S(1)} %rows_even.3.refs_1_.refs_0_.refs_3_), channel_id=1, source_target_pairs={{0,1},{1,0},{2,3},{3,2},{4,5},{5,4},{6,7},{7,6},{8,9},{9,8},{10,11... | collective-permute-start | bytes 786440 | tf_op jit(solution)/shard_map/ppermute | solution.py:510
  21.5 10.0 %collective-permute-start.2 = (bf16[4,128,256]{2,1,0:T(8,128)(2,1)S(1)}, bf16[4,128,256]{2,1,0:T(8,128)(2,1)S(1)}, u32[]{:S(2)}, u32[]{:S(2)}) collective-permute-start(bf16[4,128,256]{2,1,0:T(8,128)(2,1)S(1)} %rows_odd.3.refs_1_.refs_3_), channel_id=1, source_target_pairs={{1,2},{2,1},{3,4},{4,3},{5,6},{6,5},{7,8},{8,7},{9,10},{10,9},{11,... | collective-permute-start | bytes 786440 | tf_op jit(solution)/shard_map/ppermute | solution.py:510
  25.1 13.5 %collective-permute-start.5 = (bf16[4,128,256]{2,1,0:T(8,128)(2,1)S(1)}, bf16[4,128,256]{2,1,0:T(8,128)(2,1)S(1)}, u32[]{:S(2)}, u32[]{:S(2)}) collective-permute-start(bf16[4,128,256]{2,1,0:T(8,128)(2,1)S(1)} %rows_even.4.refs_0_.refs_1_), channel_id=1, source_target_pairs={{0,1},{1,0},{2,3},{3,2},{4,5},{5,4},{6,7},{7,6},{8,9},{9,8},{10,11... | collective-permute-start | bytes 786440 | tf_op jit(solution)/shard_map/ppermute | solution.py:510
  32.6 7.1 %collective-permute-start.4 = (bf16[4,128,256]{2,1,0:T(8,128)(2,1)S(1)}, bf16[4,128,256]{2,1,0:T(8,128)(2,1)S(1)}, u32[]{:S(2)}, u32[]{:S(2)}) collective-permute-start(bf16[4,128,256]{2,1,0:T(8,128)(2,1)S(1)} %rows_odd.4.refs_1_), channel_id=1, source_target_pairs={{1,2},{2,1},{3,4},{4,3},{5,6},{6,5},{7,8},{8,7},{9,10},{10,9},{11,... | collective-permute-start | bytes 786440 | tf_op jit(solution)/shard_map/ppermute | solution.py:510
  36.3 5.3 %collective-permute-start.8 = (bf16[3072,256]{1,0:T(8,128)(2,1)S(1)}, bf16[3072,256]{1,0:T(8,128)(2,1)S(1)}, u32[]{:S(2)}, u32[]{:S(2)}) collective-permute-start(bf16[3072,256]{1,0:T(8,128)(2,1)S(1)} %bitcast.7), channel_id=1, source_target_pairs={{0,16},{16,0},{1,17},{17,1},{2,18},{18,2},{3,19},{19,3},{4,20},{20... | collective-permute-start | bytes 4718600 | tf_op jit(solution)/shard_map/ppermute | solution.py:513
  39.8 1.8 %collective-permute-start.7 = (bf16[512,256]{1,0:T(8,128)(2,1)S(1)}, bf16[512,256]{1,0:T(8,128)(2,1)S(1)}, u32[]{:S(2)}, u32[]{:S(2)}) collective-permute-start(bf16[512,256]{1,0:T(8,128)(2,1)S(1)} %bitcast.10), channel_id=1, source_target_pairs={{0,16},{16,0},{1,17},{17,1},{2,18},{18,2},{3,19},{19,3},{4,20},{20... | collective-permute-start | bytes 786440 | tf_op jit(solution)/shard_map/ppermute | solution.py:513
  41.0 2.3 %collective-permute-start.6 = (bf16[512,256]{1,0:T(8,128)(2,1)S(1)}, bf16[512,256]{1,0:T(8,128)(2,1)S(1)}, u32[]{:S(2)}, u32[]{:S(2)}) collective-permute-start(bf16[512,256]{1,0:T(8,128)(2,1)S(1)} %bitcast.13), channel_id=1, source_target_pairs={{0,16},{16,0},{1,17},{17,1},{2,18},{18,2},{3,19},{19,3},{4,20},{20... | collective-permute-start | bytes 786440 | tf_op jit(solution)/shard_map/ppermute | solution.py:513
  43.7 7.8 %collective-permute-start.10 = (f32[160,128]{1,0:T(8,128)S(1)}, f32[160,128]{1,0:T(8,128)S(1)}, u32[]{:S(2)}, u32[]{:S(2)}) collective-permute-start(f32[160,128]{1,0:T(8,128)S(1)} %get-tuple-element.53), channel_id=1, source_target_pairs={{0,3},{1,2},{2,1},{3,0},{4,7},{5,6},{6,5},{7,4},{8,11},{9,10},{10,... | collective-permute-start | bytes 245768 | tf_op jit(solution)/shard_map/ppermute | solution.py:310
  48.8 6.5 %collective-permute-start.11 = (f32[160,128]{1,0:T(8,128)S(1)}, f32[160,128]{1,0:T(8,128)S(1)}, u32[]{:S(2)}, u32[]{:S(2)}) collective-permute-start(f32[160,128]{1,0:T(8,128)S(1)} %get-tuple-element.54), channel_id=1, source_target_pairs={{0,1},{1,0},{2,3},{3,2},{4,5},{5,4},{6,7},{7,6},{8,9},{9,8},{10,11... | collective-permute-start | bytes 245768 | tf_op jit(solution)/shard_map/ppermute | solution.py:310
  51.2 4.4 %collective-permute-start.9 = (f32[160,128]{1,0:T(8,128)S(1)}, f32[160,128]{1,0:T(8,128)S(1)}, u32[]{:S(2)}, u32[]{:S(2)}) collective-permute-start(f32[160,128]{1,0:T(8,128)S(1)} %get-tuple-element.52), channel_id=1, source_target_pairs={{0,2},{1,3},{2,0},{3,1},{4,6},{5,7},{6,4},{7,5},{8,10},{9,11},{10,... | collective-permute-start | bytes 245768 | tf_op jit(solution)/shard_map/ppermute | solution.py:310
  55.6 7.2 %collective-permute-start.12 = (f32[160,128]{1,0:T(8,128)S(1)}, f32[160,128]{1,0:T(8,128)S(1)}, u32[]{:S(2)}, u32[]{:S(2)}) collective-permute-start(f32[160,128]{1,0:T(8,128)S(1)} %add_four.2.a), channel_id=1, source_target_pairs={{0,12},{1,13},{2,14},{3,15},{4,8},{5,9},{6,10},{7,11},{8,4},{9,5},... | collective-permute-start | bytes 245768 | tf_op jit(solution)/shard_map/ppermute | solution.py:310
  59.3 6.1 %collective-permute-start.13 = (f32[160,128]{1,0:T(8,128)S(1)}, f32[160,128]{1,0:T(8,128)S(1)}, u32[]{:S(2)}, u32[]{:S(2)}) collective-permute-start(f32[160,128]{1,0:T(8,128)S(1)} %add_four.2.a), channel_id=1, source_target_pairs={{0,8},{1,9},{2,10},{3,11},{4,12},{5,13},{6,14},{7,15},{8,0},{9,1},... | collective-permute-start | bytes 245768 | tf_op jit(solution)/shard_map/ppermute | solution.py:310
  59.3 6.1 %collective-permute-start.14 = (f32[160,128]{1,0:T(8,128)S(1)}, f32[160,128]{1,0:T(8,128)S(1)}, u32[]{:S(2)}, u32[]{:S(2)}) collective-permute-start(f32[160,128]{1,0:T(8,128)S(1)} %add_four.2.a), channel_id=1, source_target_pairs={{0,4},{1,5},{2,6},{3,7},{4,0},{5,1},{6,2},{7,3},{8,12},{9,13},{10,... | collective-permute-start | bytes 245768 | tf_op jit(solution)/shard_map/ppermute | solution.py:310
  65.5 5.4 %collective-permute-start.15 = (f32[160,128]{1,0:T(8,128)S(1)}, f32[160,128]{1,0:T(8,128)S(1)}, u32[]{:S(2)}, u32[]{:S(2)}) collective-permute-start(f32[160,128]{1,0:T(8,128)S(1)} %add_four.3.refs_0_), channel_id=1, source_target_pairs={{0,3},{1,2},{2,1},{3,0},{4,7},{5,6},{6,5},{7,4},{8,11},{9,10},{10,... | collective-permute-start | bytes 245768 | tf_op jit(solution)/shard_map/ppermute | solution.py:310
  67.1 4.4 %collective-permute-start.16 = (f32[160,128]{1,0:T(8,128)S(1)}, f32[160,128]{1,0:T(8,128)S(1)}, u32[]{:S(2)}, u32[]{:S(2)}) collective-permute-start(f32[160,128]{1,0:T(8,128)S(1)} %add_four.3.refs_0_), channel_id=1, source_target_pairs={{0,1},{1,0},{2,3},{3,2},{4,5},{5,4},{6,7},{7,6},{8,9},{9,8},{10,11... | collective-permute-start | bytes 245768 | tf_op jit(solution)/shard_map/ppermute | solution.py:310
  67.9 4.4 %collective-permute-start.17 = (f32[160,128]{1,0:T(8,128)S(1)}, f32[160,128]{1,0:T(8,128)S(1)}, u32[]{:S(2)}, u32[]{:S(2)}) collective-permute-start(f32[160,128]{1,0:T(8,128)S(1)} %add_four.3.refs_0_), channel_id=1, source_target_pairs={{0,2},{1,3},{2,0},{3,1},{4,6},{5,7},{6,4},{7,5},{8,10},{9,11},{10,... | collective-permute-start | bytes 245768 | tf_op jit(solution)/shard_map/ppermute | solution.py:310
  72.4 1.7 %collective-permute-start.18 = (f32[640,128]{1,0:T(8,128)S(1)}, f32[640,128]{1,0:T(8,128)S(1)}, u32[]{:S(2)}, u32[]{:S(2)}) collective-permute-start(f32[640,128]{1,0:T(8,128)S(1)} %join.1.mine), channel_id=1, source_target_pairs={{0,16},{16,0},{1,17},{17,1},{2,18},{18,2},{3,19},{19,3},{4,20},{20... | collective-permute-start | bytes 983048 | tf_op jit(solution)/shard_map/ppermute | solution.py:513

commit v15 on v14

--- a/solution.py
+++ b/solution.py
@@ -12,7 +12,7 @@
 ITERS = 8
 WAYS = 4
 LOAD_CUTS = 4
-GRAM_ROWS = 1024
+GRAM_ROWS = 1536
 GROUP = 12
 
 SMALL = pl.CostEstimate(flops=1000, bytes_accessed=1000, transcendentals=0)
@@ -204,7 +204,7 @@
 
 
 SPREAD = (2, 3, 1), (1, 3, 2)
-ACROSS_GROUPS = (3, 2, 1), (2, 3, 1)
+ACROSS_GROUPS = (3, 2, 1), (3, 2, 1)
 GATHER = (3, 1, 2), (3, 2, 1)
 
 

time: 90.5 us -> 90.4 us (level)
  no operation moved by 1% of the time
where the time goes in v15:
time: 90.4 us; the launch traced here: 90.1 us
  Pallas kernels  39.1 us (43%)
  starting transfers between devices  26.9 us (30%)
  waiting for transfers between devices  22.4 us (25%)
  between operations  1.05 us (1%)
    pallas_call x1, Pallas kernels, rotate(): pl.pallas_call(body, in_specs=[VMEM, VMEM] + [ANY] * 6, out_specs=ANY, ou...  16 us
    ppermute x9, starting transfers between devices, from_others(): got.append(lax.ppermute(value, ('cols', 'patch'), pairs))  15.5 us
    pallas_call x9, Pallas kernels, tile_rows(): pl.pallas_call(functools.partial(rows_kernel, name), in_specs=[VMEM] * le...  14.9 us
    ppermute x9, waiting for transfers between devices, from_others(): got.append(lax.ppermute(value, ('cols', 'patch'), pairs))  13.2 us
    ppermute x6, starting transfers between devices, exchange(): return lax.ppermute(value, 'patch', pairs[name])  10.6 us
    ppermute x6, waiting for transfers between devices, exchange(): return lax.ppermute(value, 'patch', pairs[name])  7.59 us
    pallas_call x3, Pallas kernels, load_call(): pl.pallas_call(body, in_specs=[VMEM] * len(table) + [HBM] * len(args), ou...  6.23 us
    pallas_call x5, Pallas kernels, gram_call(): pl.pallas_call(body, in_specs=[VMEM] * len(args), out_specs=[VMEM] * outs...  1.94 us
  transfers between devices with their start and end apart: 19, of which 12 were waited for; matrix products, arithmetic and copies ran while one was open for 0% of the time, Pallas kernels for 24%

profile of v15, /device:TPU:0, one launch (start us, length us, event | category | flops | bytes accessed | tf_op | source)
XLA Modules:
  0.0 90.1 jit_solution(5431763158986364409)
XLA Ops:
  0.7 0.7 concatenate.3.table_ref
  1.3 1.2 %masked_edges.1 = (bf16[4,128,256]{2,1,0:T(8,128)(2,1)S(1)}, bf16[4,128,256]{2,1,0:T(8,128)(2,1)S(1)}) custom-call(s32[9,32]{1,0:T(8,128)S(1)} %concatenate.3.table_ref, bf16[32,128,256]{2,1,0:T(8,128)(2,1)} %bitcast.16), custom_call_target="tpu_custom_call" | custom-call | flops 1000 | bytes 1000 | tf_op jit(solution)/shard_map/masked_edges/pallas_call | solution.py:109
  2.5 3.0 %collective-permute-start.1 = (bf16[4,128,256]{2,1,0:T(8,128)(2,1)S(1)}, bf16[4,128,256]{2,1,0:T(8,128)(2,1)S(1)}, u32[]{:S(2)}, u32[]{:S(2)}) collective-permute-start(bf16[4,128,256]{2,1,0:T(8,128)(2,1)S(1)} %get-tuple-element.37.refs_1_.refs_0_.refs_3_), channel_id=1, source_target_pairs={{0,1},{1,0},{2,3},{3,2},{4,5},{5,4},{6,7},{7,6},{8,9},{9,8},{10,11... | collective-permute-start | bytes 786440 | tf_op jit(solution)/shard_map/ppermute | solution.py:510
  5.5 2.2 %load_fields.1 = (bf16[24,128,256]{2,1,0:T(8,128)(2,1)S(1)}, bf16[4,8,128,128]{3,2,1,0:T(8,128)(2,1)S(1)}, bf16[4,8,128,128]{3,2,1,0:T(8,128)(2,1)S(1)}) custom-call(s32[9,32]{1,0:T(8,128)S(1)} %concatenate.3.table_ref, bf16[32,128,256]{2,1,0:T(8,128)(2,1)} %bitcast.17, bf16[32,8,128,128]{3,2,1,0:T(8,128)(2,1)} %blocks_ref.2), custom_call_target="tpu_custom_call" | custom-call | flops 1000 | bytes 1000 | tf_op jit(solution)/shard_map/load_fields/pallas_call | solution.py:109
  7.7 0.7 collective-permute-start
  8.4 3.4 %collective-permute-done.1.refs_0_ = bf16[4,128,256]{2,1,0:T(8,128)(2,1)S(1)} collective-permute-done((bf16[4,128,256]{2,1,0:T(8,128)(2,1)S(1)}, bf16[4,128,256]{2,1,0:T(8,128)(2,1)S(1)}, u32[]{:S(2)}, u32[]{:S(2)}) %collective-permute-start.1) | collective-permute-done | bytes 262176 | tf_op jit(solution)/shard_map/ppermute | solution.py:510
  11.8 1.1 %rows_even.3.refs_1_.refs_0_.refs_3_ = bf16[4,128,256]{2,1,0:T(8,128)(2,1)S(1)} custom-call(s32[9,32]{1,0:T(8,128)S(1)} %concatenate.3.table_ref, bf16[4,128,256]{2,1,0:T(8,128)(2,1)S(1)} %collective-permute-done.1.refs_0_, bf16[4,128,256]{2,1,0:T(8,128)(2,1)S(1)} %get-tuple-element.37.refs_1_.refs_0_.refs_3_, ...), custom_call_target="tpu_custom_call" | custom-call | flops 1000 | bytes 1000 | tf_op jit(solution)/shard_map/rows_even/pallas_call | solution.py:187
  13.0 1.8 %collective-permute-start.3 = (bf16[4,128,256]{2,1,0:T(8,128)(2,1)S(1)}, bf16[4,128,256]{2,1,0:T(8,128)(2,1)S(1)}, u32[]{:S(2)}, u32[]{:S(2)}) collective-permute-start(bf16[4,128,256]{2,1,0:T(8,128)(2,1)S(1)} %rows_even.3.refs_1_.refs_0_.refs_3_), channel_id=1, source_target_pairs={{0,1},{1,0},{2,3},{3,2},{4,5},{5,4},{6,7},{7,6},{8,9},{9,8},{10,11... | collective-permute-start | bytes 786440 | tf_op jit(solution)/shard_map/ppermute | solution.py:510
  14.8 2.9 %load_blocks.1.refs_3_.refs_4_ = bf16[24,8,128,128]{3,2,1,0:T(8,128)(2,1)S(1)} custom-call(bf16[32,8,128,128]{3,2,1,0:T(8,128)(2,1)} %blocks_ref.2), custom_call_target="tpu_custom_call" | custom-call | flops 1000 | bytes 1000 | tf_op jit(solution)/shard_map/load_blocks/pallas_call | solution.py:109
  17.6 2.7 %rows_inner.3.refs_2_.refs_3_ = bf16[24,128,256]{2,1,0:T(8,128)(2,1)S(1)} custom-call(s32[9,32]{1,0:T(8,128)S(1)} %concatenate.3.table_ref, bf16[4,128,256]{2,1,0:T(8,128)(2,1)S(1)} %get-tuple-element.37.refs_1_.refs_0_.refs_3_, bf16[4,128,256]{2,1,0:T(8,128)(2,1)S(1)} %get-tuple-element.34.refs_1_.refs_3_, ...), custom_call_target="tpu_custom_call" | custom-call | flops 1000 | bytes 1000 | tf_op jit(solution)/shard_map/rows_inner/pallas_call | solution.py:187
  20.4 0.0 collective-permute-done.refs_0_
  20.4 1.1 %rows_odd.3.refs_1_.refs_3_ = bf16[4,128,256]{2,1,0:T(8,128)(2,1)S(1)} custom-call(s32[9,32]{1,0:T(8,128)S(1)} %concatenate.3.table_ref, bf16[4,128,256]{2,1,0:T(8,128)(2,1)S(1)} %collective-permute-done.refs_0_, bf16[4,128,256]{2,1,0:T(8,128)(2,1)S(1)} %get-tuple-element.34.refs_1_.refs_3_, bf16[24,128,256]{2,1,0:T(8,128)(2,1)S(1)} %get-tuple-element.33.refs_2_.refs_3_, ...), custom_call_target="tpu_custom_call" | custom-call | flops 1000 | bytes 1000 | tf_op jit(solution)/shard_map/rows_odd/pallas_call | solution.py:187
  21.5 0.7 collective-permute-start.2
  22.2 1.8 %collective-permute-done.3.refs_0_ = bf16[4,128,256]{2,1,0:T(8,128)(2,1)S(1)} collective-permute-done((bf16[4,128,256]{2,1,0:T(8,128)(2,1)S(1)}, bf16[4,128,256]{2,1,0:T(8,128)(2,1)S(1)}, u32[]{:S(2)}, u32[]{:S(2)}) %collective-permute-start.3) | collective-permute-done | bytes 262176 | tf_op jit(solution)/shard_map/ppermute | solution.py:510
  24.0 1.1 %rows_even.4.refs_0_.refs_1_ = bf16[4,128,256]{2,1,0:T(8,128)(2,1)S(1)} custom-call(s32[9,32]{1,0:T(8,128)S(1)} %concatenate.3.table_ref, bf16[4,128,256]{2,1,0:T(8,128)(2,1)S(1)} %collective-permute-done.3.refs_0_, bf16[4,128,256]{2,1,0:T(8,128)(2,1)S(1)} %rows_even.3.refs_1_.refs_0_.refs_3_, bf16[24,128,256]{2,1,0:T(8,128)(2,1)S(1)} %rows_inner.3.refs_2_.refs_3_, ...), custom_call_target="tpu_custom_call" | custom-call | flops 1000 | bytes 1000 | tf_op jit(solution)/shard_map/rows_even/pallas_call | solution.py:187
  25.2 3.6 %collective-permute-start.5 = (bf16[4,128,256]{2,1,0:T(8,128)(2,1)S(1)}, bf16[4,128,256]{2,1,0:T(8,128)(2,1)S(1)}, u32[]{:S(2)}, u32[]{:S(2)}) collective-permute-start(bf16[4,128,256]{2,1,0:T(8,128)(2,1)S(1)} %rows_even.4.refs_0_.refs_1_), channel_id=1, source_target_pairs={{0,1},{1,0},{2,3},{3,2},{4,5},{5,4},{6,7},{7,6},{8,9},{9,8},{10,11... | collective-permute-start | bytes 786440 | tf_op jit(solution)/shard_map/ppermute | solution.py:510
  28.8 2.7 %rows_inner.4.refs_2_ = bf16[24,128,256]{2,1,0:T(8,128)(2,1)S(1)} custom-call(s32[9,32]{1,0:T(8,128)S(1)} %concatenate.3.table_ref, bf16[4,128,256]{2,1,0:T(8,128)(2,1)S(1)} %rows_even.3.refs_1_.refs_0_.refs_3_, bf16[4,128,256]{2,1,0:T(8,128)(2,1)S(1)} %rows_odd.3.refs_1_.refs_3_, bf16[24,128,256]{2,1,0:T(8,128)(2,1)S(1)} %rows_inner.3.refs_2_.refs_3_, ...), custom_call_target="tpu_custom_call" | custom-call | flops 1000 | bytes 1000 | tf_op jit(solution)/shard_map/rows_inner/pallas_call | solution.py:187
  31.5 0.0 collective-permute-done.2.refs_0_
  31.5 1.1 %rows_odd.4.refs_1_ = bf16[4,128,256]{2,1,0:T(8,128)(2,1)S(1)} custom-call(s32[9,32]{1,0:T(8,128)S(1)} %concatenate.3.table_ref, bf16[4,128,256]{2,1,0:T(8,128)(2,1)S(1)} %collective-permute-done.2.refs_0_, bf16[4,128,256]{2,1,0:T(8,128)(2,1)S(1)} %rows_odd.3.refs_1_.refs_3_, bf16[24,128,256]{2,1,0:T(8,128)(2,1)S(1)} %rows_inner.3.refs_2_.refs_3_, ...), custom_call_target="tpu_custom_call" | custom-call | flops 1000 | bytes 1000 | tf_op jit(solution)/shard_map/rows_odd/pallas_call | solution.py:187
  32.6 0.9 collective-permute-start.4
  33.5 2.7 %rows_inner.5 = bf16[24,128,256]{2,1,0:T(8,128)(2,1)S(1)} custom-call(s32[9,32]{1,0:T(8,128)S(1)} %concatenate.3.table_ref, bf16[4,128,256]{2,1,0:T(8,128)(2,1)S(1)} %rows_even.4.refs_0_.refs_1_, bf16[4,128,256]{2,1,0:T(8,128)(2,1)S(1)} %rows_odd.4.refs_1_, bf16[24,128,256]{2,1,0:T(8,128)(2,1)S(1)} %rows_inner.4.refs_2_, ...), custom_call_target="tpu_custom_call" | custom-call | flops 1000 | bytes 1000 | tf_op jit(solution)/shard_map/rows_inner/pallas_call | solution.py:187
  36.3 0.1 collective-permute-start.8
  36.3 2.3 %collective-permute-done.5.refs_0_ = bf16[4,128,256]{2,1,0:T(8,128)(2,1)S(1)} collective-permute-done((bf16[4,128,256]{2,1,0:T(8,128)(2,1)S(1)}, bf16[4,128,256]{2,1,0:T(8,128)(2,1)S(1)}, u32[]{:S(2)}, u32[]{:S(2)}) %collective-permute-start.5) | collective-permute-done | bytes 262176 | tf_op jit(solution)/shard_map/ppermute | solution.py:510
  38.6 1.1 %rows_even.5 = bf16[4,128,256]{2,1,0:T(8,128)(2,1)S(1)} custom-call(s32[9,32]{1,0:T(8,128)S(1)} %concatenate.3.table_ref, bf16[4,128,256]{2,1,0:T(8,128)(2,1)S(1)} %collective-permute-done.5.refs_0_, bf16[4,128,256]{2,1,0:T(8,128)(2,1)S(1)} %rows_even.4.refs_0_.refs_1_, bf16[24,128,256]{2,1,0:T(8,128)(2,1)S(1)} %rows_inner.4.refs_2_, ...), custom_call_target="tpu_custom_call" | custom-call | flops 1000 | bytes 1000 | tf_op jit(solution)/shard_map/rows_even/pallas_call | solution.py:187
  39.8 0.0 collective-permute-done.4.refs_0_
  39.8 0.1 collective-permute-start.7
  39.9 1.1 %rows_odd.5 = bf16[4,128,256]{2,1,0:T(8,128)(2,1)S(1)} custom-call(s32[9,32]{1,0:T(8,128)S(1)} %concatenate.3.table_ref, bf16[4,128,256]{2,1,0:T(8,128)(2,1)S(1)} %collective-permute-done.4.refs_0_, bf16[4,128,256]{2,1,0:T(8,128)(2,1)S(1)} %rows_odd.4.refs_1_, bf16[24,128,256]{2,1,0:T(8,128)(2,1)S(1)} %rows_inner.4.refs_2_, ...), custom_call_target="tpu_custom_call" | custom-call | flops 99999997952 | bytes 1000 | tf_op jit(solution)/shard_map/rows_odd/pallas_call | solution.py:187
  41.0 0.6 collective-permute-start.6
  41.6 0.0 collective-permute-done.7.refs_2_.refs_3_
  41.6 0.0 collective-permute-done.8.refs_3_.refs_4_
  41.6 1.5 %gram.1.start_ref = f32[256,512]{1,0:T(8,128)S(1)} custom-call(bf16[512,256]{1,0:T(8,128)(2,1)S(1)} %bitcast.11, bf16[3072,256]{1,0:T(8,128)(2,1)S(1)} %bitcast.8, bf16[512,256]{1,0:T(8,128)(2,1)S(1)} %collective-permute-done.7.refs_2_.refs_3_, bf16[3072,256]{1,0:T(8,128)(2,1)S(1)} %collective-permute-done.8.refs_3_.refs_4_), custom_call_target="tpu_custom_call" | custom-call | flops 1000 | bytes 1000 | tf_op jit(solution)/shard_map/gram/pallas_call | solution.py:257
  43.1 0.0 collective-permute-done.6.other_ref.refs_5_
  43.1 0.3 gram_share.1
  43.5 5.2 %collective-permute-start.10 = (f32[160,128]{1,0:T(8,128)S(1)}, f32[160,128]{1,0:T(8,128)S(1)}, u32[]{:S(2)}, u32[]{:S(2)}) collective-permute-start(f32[160,128]{1,0:T(8,128)S(1)} %get-tuple-element.53), channel_id=1, source_target_pairs={{0,3},{1,2},{2,1},{3,0},{4,7},{5,6},{6,5},{7,4},{8,11},{9,10},{10,... | collective-permute-start | bytes 245768 | tf_op jit(solution)/shard_map/ppermute | solution.py:310
  48.6 2.3 %collective-permute-start.11 = (f32[160,128]{1,0:T(8,128)S(1)}, f32[160,128]{1,0:T(8,128)S(1)}, u32[]{:S(2)}, u32[]{:S(2)}) collective-permute-start(f32[160,128]{1,0:T(8,128)S(1)} %get-tuple-element.54), channel_id=1, source_target_pairs={{0,1},{1,0},{2,3},{3,2},{4,5},{5,4},{6,7},{7,6},{8,9},{9,8},{10,11... | collective-permute-start | bytes 245768 | tf_op jit(solution)/shard_map/ppermute | solution.py:310
  51.0 0.0 collective-permute-start.9
  51.0 0.3 collective-permute-done.10.c
  51.3 3.8 %collective-permute-done.11.d = f32[160,128]{1,0:T(8,128)S(1)} collective-permute-done((f32[160,128]{1,0:T(8,128)S(1)}, f32[160,128]{1,0:T(8,128)S(1)}, u32[]{:S(2)}, u32[]{:S(2)}) %collective-permute-start.11) | collective-permute-done | bytes 81952 | tf_op jit(solution)/shard_map/ppermute | solution.py:310
  55.1 0.3 collective-permute-done.9.b
  55.4 3.7 %collective-permute-start.12 = (f32[160,128]{1,0:T(8,128)S(1)}, f32[160,128]{1,0:T(8,128)S(1)}, u32[]{:S(2)}, u32[]{:S(2)}) collective-permute-start(f32[160,128]{1,0:T(8,128)S(1)} %add_four.2.a), channel_id=1, source_target_pairs={{0,12},{1,13},{2,14},{3,15},{4,8},{5,9},{6,10},{7,11},{8,4},{9,5},... | collective-permute-start | bytes 245768 | tf_op jit(solution)/shard_map/ppermute | solution.py:310
  59.1 0.0 collective-permute-start.13
  59.1 0.8 collective-permute-start.14
  59.9 1.9 %collective-permute-done.12.b = f32[160,128]{1,0:T(8,128)S(1)} collective-permute-done((f32[160,128]{1,0:T(8,128)S(1)}, f32[160,128]{1,0:T(8,128)S(1)}, u32[]{:S(2)}, u32[]{:S(2)}) %collective-permute-start.12) | collective-permute-done | bytes 81952 | tf_op jit(solution)/shard_map/ppermute | solution.py:310
  61.7 3.4 %collective-permute-done.13.c = f32[160,128]{1,0:T(8,128)S(1)} collective-permute-done((f32[160,128]{1,0:T(8,128)S(1)}, f32[160,128]{1,0:T(8,128)S(1)}, u32[]{:S(2)}, u32[]{:S(2)}) %collective-permute-start.13) | collective-permute-done | bytes 81952 | tf_op jit(solution)/shard_map/ppermute | solution.py:310
  65.1 0.0 collective-permute-done.14.d
  65.1 1.7 %collective-permute-start.15 = (f32[160,128]{1,0:T(8,128)S(1)}, f32[160,128]{1,0:T(8,128)S(1)}, u32[]{:S(2)}, u32[]{:S(2)}) collective-permute-start(f32[160,128]{1,0:T(8,128)S(1)} %add_four.3.refs_0_), channel_id=1, source_target_pairs={{0,3},{1,2},{2,1},{3,0},{4,7},{5,6},{6,5},{7,4},{8,11},{9,10},{10,... | collective-permute-start | bytes 245768 | tf_op jit(solution)/shard_map/ppermute | solution.py:310
  66.9 0.8 collective-permute-start.16
  67.7 1.0 %collective-permute-start.17 = (f32[160,128]{1,0:T(8,128)S(1)}, f32[160,128]{1,0:T(8,128)S(1)}, u32[]{:S(2)}, u32[]{:S(2)}) collective-permute-start(f32[160,128]{1,0:T(8,128)S(1)} %add_four.3.refs_0_), channel_id=1, source_target_pairs={{0,2},{1,3},{2,0},{3,1},{4,6},{5,7},{6,4},{7,5},{8,10},{9,11},{10,... | collective-permute-start | bytes 245768 | tf_op jit(solution)/shard_map/ppermute | solution.py:310
  68.7 2.7 %collective-permute-done.15.refs_1_ = f32[160,128]{1,0:T(8,128)S(1)} collective-permute-done((f32[160,128]{1,0:T(8,128)S(1)}, f32[160,128]{1,0:T(8,128)S(1)}, u32[]{:S(2)}, u32[]{:S(2)}) %collective-permute-start.15) | collective-permute-done | bytes 81952 | tf_op jit(solution)/shard_map/ppermute | solution.py:310
  71.4 0.5 collective-permute-done.16.refs_2_
  71.9 0.3 collective-permute-done.17.refs_3_
  72.2 0.1 collective-permute-start.18
  72.3 1.6 %collective-permute-done.18.theirs = f32[640,128]{1,0:T(8,128)S(1)} collective-permute-done((f32[640,128]{1,0:T(8,128)S(1)}, f32[640,128]{1,0:T(8,128)S(1)}, u32[]{:S(2)}, u32[]{:S(2)}) %collective-permute-start.18) | collective-permute-done | bytes 327712 | tf_op jit(solution)/shard_map/ppermute | solution.py:513
  73.9 16.0 %rotate.1 = bf16[4096,256]{1,0:T(8,128)(2,1)} custom-call(f32[640,128]{1,0:T(8,128)S(1)} %join.1.mine, f32[640,128]{1,0:T(8,128)S(1)} %collective-permute-done.18.theirs, bf16[512,256]{1,0:T(8,128)(2,1)S(1)} %bitcast.12, bf16[3072,256]{1,0:T(8,128)(2,1)S(1)} %bitcast.9, bf16[512,256]{1,0:T(8,128)(2,1)S(1)} %bitcast.15, ...), custom_call_target="tpu_custom_call" | custom-call | flops 17985175552 | bytes 6291456 | tf_op jit(solution)/shard_map/rotate/pallas_call | solution.py:472
  (3 shorter events, 0.1 us)
Async XLA Ops:
  2.5 9.3 %collective-permute-start.1 = (bf16[4,128,256]{2,1,0:T(8,128)(2,1)S(1)}, bf16[4,128,256]{2,1,0:T(8,128)(2,1)S(1)}, u32[]{:S(2)}, u32[]{:S(2)}) collective-permute-start(bf16[4,128,256]{2,1,0:T(8,128)(2,1)S(1)} %get-tuple-element.37.refs_1_.refs_0_.refs_3_), channel_id=1, source_target_pairs={{0,1},{1,0},{2,3},{3,2},{4,5},{5,4},{6,7},{7,6},{8,9},{9,8},{10,11... | collective-permute-start | bytes 786440 | tf_op jit(solution)/shard_map/ppermute | solution.py:510
  7.7 12.7 %collective-permute-start = (bf16[4,128,256]{2,1,0:T(8,128)(2,1)S(1)}, bf16[4,128,256]{2,1,0:T(8,128)(2,1)S(1)}, u32[]{:S(2)}, u32[]{:S(2)}) collective-permute-start(bf16[4,128,256]{2,1,0:T(8,128)(2,1)S(1)} %get-tuple-element.34.refs_1_.refs_3_), channel_id=1, source_target_pairs={{1,2},{2,1},{3,4},{4,3},{5,6},{6,5},{7,8},{8,7},{9,10},{10,9},{11,... | collective-permute-start | bytes 786440 | tf_op jit(solution)/shard_map/ppermute | solution.py:510
  13.0 11.1 %collective-permute-start.3 = (bf16[4,128,256]{2,1,0:T(8,128)(2,1)S(1)}, bf16[4,128,256]{2,1,0:T(8,128)(2,1)S(1)}, u32[]{:S(2)}, u32[]{:S(2)}) collective-permute-start(bf16[4,128,256]{2,1,0:T(8,128)(2,1)S(1)} %rows_even.3.refs_1_.refs_0_.refs_3_), channel_id=1, source_target_pairs={{0,1},{1,0},{2,3},{3,2},{4,5},{5,4},{6,7},{7,6},{8,9},{9,8},{10,11... | collective-permute-start | bytes 786440 | tf_op jit(solution)/shard_map/ppermute | solution.py:510
  21.5 10.0 %collective-permute-start.2 = (bf16[4,128,256]{2,1,0:T(8,128)(2,1)S(1)}, bf16[4,128,256]{2,1,0:T(8,128)(2,1)S(1)}, u32[]{:S(2)}, u32[]{:S(2)}) collective-permute-start(bf16[4,128,256]{2,1,0:T(8,128)(2,1)S(1)} %rows_odd.3.refs_1_.refs_3_), channel_id=1, source_target_pairs={{1,2},{2,1},{3,4},{4,3},{5,6},{6,5},{7,8},{8,7},{9,10},{10,9},{11,... | collective-permute-start | bytes 786440 | tf_op jit(solution)/shard_map/ppermute | solution.py:510
  25.2 13.5 %collective-permute-start.5 = (bf16[4,128,256]{2,1,0:T(8,128)(2,1)S(1)}, bf16[4,128,256]{2,1,0:T(8,128)(2,1)S(1)}, u32[]{:S(2)}, u32[]{:S(2)}) collective-permute-start(bf16[4,128,256]{2,1,0:T(8,128)(2,1)S(1)} %rows_even.4.refs_0_.refs_1_), channel_id=1, source_target_pairs={{0,1},{1,0},{2,3},{3,2},{4,5},{5,4},{6,7},{7,6},{8,9},{9,8},{10,11... | collective-permute-start | bytes 786440 | tf_op jit(solution)/shard_map/ppermute | solution.py:510
  32.6 7.1 %collective-permute-start.4 = (bf16[4,128,256]{2,1,0:T(8,128)(2,1)S(1)}, bf16[4,128,256]{2,1,0:T(8,128)(2,1)S(1)}, u32[]{:S(2)}, u32[]{:S(2)}) collective-permute-start(bf16[4,128,256]{2,1,0:T(8,128)(2,1)S(1)} %rows_odd.4.refs_1_), channel_id=1, source_target_pairs={{1,2},{2,1},{3,4},{4,3},{5,6},{6,5},{7,8},{8,7},{9,10},{10,9},{11,... | collective-permute-start | bytes 786440 | tf_op jit(solution)/shard_map/ppermute | solution.py:510
  36.3 5.3 %collective-permute-start.8 = (bf16[3072,256]{1,0:T(8,128)(2,1)S(1)}, bf16[3072,256]{1,0:T(8,128)(2,1)S(1)}, u32[]{:S(2)}, u32[]{:S(2)}) collective-permute-start(bf16[3072,256]{1,0:T(8,128)(2,1)S(1)} %bitcast.7), channel_id=1, source_target_pairs={{0,16},{16,0},{1,17},{17,1},{2,18},{18,2},{3,19},{19,3},{4,20},{20... | collective-permute-start | bytes 4718600 | tf_op jit(solution)/shard_map/ppermute | solution.py:513
  39.8 1.8 %collective-permute-start.7 = (bf16[512,256]{1,0:T(8,128)(2,1)S(1)}, bf16[512,256]{1,0:T(8,128)(2,1)S(1)}, u32[]{:S(2)}, u32[]{:S(2)}) collective-permute-start(bf16[512,256]{1,0:T(8,128)(2,1)S(1)} %bitcast.10), channel_id=1, source_target_pairs={{0,16},{16,0},{1,17},{17,1},{2,18},{18,2},{3,19},{19,3},{4,20},{20... | collective-permute-start | bytes 786440 | tf_op jit(solution)/shard_map/ppermute | solution.py:513
  41.0 2.1 %collective-permute-start.6 = (bf16[512,256]{1,0:T(8,128)(2,1)S(1)}, bf16[512,256]{1,0:T(8,128)(2,1)S(1)}, u32[]{:S(2)}, u32[]{:S(2)}) collective-permute-start(bf16[512,256]{1,0:T(8,128)(2,1)S(1)} %bitcast.13), channel_id=1, source_target_pairs={{0,16},{16,0},{1,17},{17,1},{2,18},{18,2},{3,19},{19,3},{4,20},{20... | collective-permute-start | bytes 786440 | tf_op jit(solution)/shard_map/ppermute | solution.py:513
  43.5 7.8 %collective-permute-start.10 = (f32[160,128]{1,0:T(8,128)S(1)}, f32[160,128]{1,0:T(8,128)S(1)}, u32[]{:S(2)}, u32[]{:S(2)}) collective-permute-start(f32[160,128]{1,0:T(8,128)S(1)} %get-tuple-element.53), channel_id=1, source_target_pairs={{0,3},{1,2},{2,1},{3,0},{4,7},{5,6},{6,5},{7,4},{8,11},{9,10},{10,... | collective-permute-start | bytes 245768 | tf_op jit(solution)/shard_map/ppermute | solution.py:310
  48.6 6.5 %collective-permute-start.11 = (f32[160,128]{1,0:T(8,128)S(1)}, f32[160,128]{1,0:T(8,128)S(1)}, u32[]{:S(2)}, u32[]{:S(2)}) collective-permute-start(f32[160,128]{1,0:T(8,128)S(1)} %get-tuple-element.54), channel_id=1, source_target_pairs={{0,1},{1,0},{2,3},{3,2},{4,5},{5,4},{6,7},{7,6},{8,9},{9,8},{10,11... | collective-permute-start | bytes 245768 | tf_op jit(solution)/shard_map/ppermute | solution.py:310
  51.0 4.4 %collective-permute-start.9 = (f32[160,128]{1,0:T(8,128)S(1)}, f32[160,128]{1,0:T(8,128)S(1)}, u32[]{:S(2)}, u32[]{:S(2)}) collective-permute-start(f32[160,128]{1,0:T(8,128)S(1)} %get-tuple-element.52), channel_id=1, source_target_pairs={{0,2},{1,3},{2,0},{3,1},{4,6},{5,7},{6,4},{7,5},{8,10},{9,11},{10,... | collective-permute-start | bytes 245768 | tf_op jit(solution)/shard_map/ppermute | solution.py:310
  55.4 6.3 %collective-permute-start.12 = (f32[160,128]{1,0:T(8,128)S(1)}, f32[160,128]{1,0:T(8,128)S(1)}, u32[]{:S(2)}, u32[]{:S(2)}) collective-permute-start(f32[160,128]{1,0:T(8,128)S(1)} %add_four.2.a), channel_id=1, source_target_pairs={{0,12},{1,13},{2,14},{3,15},{4,8},{5,9},{6,10},{7,11},{8,4},{9,5},... | collective-permute-start | bytes 245768 | tf_op jit(solution)/shard_map/ppermute | solution.py:310
  59.1 6.0 %collective-permute-start.13 = (f32[160,128]{1,0:T(8,128)S(1)}, f32[160,128]{1,0:T(8,128)S(1)}, u32[]{:S(2)}, u32[]{:S(2)}) collective-permute-start(f32[160,128]{1,0:T(8,128)S(1)} %add_four.2.a), channel_id=1, source_target_pairs={{0,8},{1,9},{2,10},{3,11},{4,12},{5,13},{6,14},{7,15},{8,0},{9,1},... | collective-permute-start | bytes 245768 | tf_op jit(solution)/shard_map/ppermute | solution.py:310
  59.1 6.0 %collective-permute-start.14 = (f32[160,128]{1,0:T(8,128)S(1)}, f32[160,128]{1,0:T(8,128)S(1)}, u32[]{:S(2)}, u32[]{:S(2)}) collective-permute-start(f32[160,128]{1,0:T(8,128)S(1)} %add_four.2.a), channel_id=1, source_target_pairs={{0,4},{1,5},{2,6},{3,7},{4,0},{5,1},{6,2},{7,3},{8,12},{9,13},{10,... | collective-permute-start | bytes 245768 | tf_op jit(solution)/shard_map/ppermute | solution.py:310
  65.1 6.2 %collective-permute-start.15 = (f32[160,128]{1,0:T(8,128)S(1)}, f32[160,128]{1,0:T(8,128)S(1)}, u32[]{:S(2)}, u32[]{:S(2)}) collective-permute-start(f32[160,128]{1,0:T(8,128)S(1)} %add_four.3.refs_0_), channel_id=1, source_target_pairs={{0,3},{1,2},{2,1},{3,0},{4,7},{5,6},{6,5},{7,4},{8,11},{9,10},{10,... | collective-permute-start | bytes 245768 | tf_op jit(solution)/shard_map/ppermute | solution.py:310
  66.9 5.0 %collective-permute-start.16 = (f32[160,128]{1,0:T(8,128)S(1)}, f32[160,128]{1,0:T(8,128)S(1)}, u32[]{:S(2)}, u32[]{:S(2)}) collective-permute-start(f32[160,128]{1,0:T(8,128)S(1)} %add_four.3.refs_0_), channel_id=1, source_target_pairs={{0,1},{1,0},{2,3},{3,2},{4,5},{5,4},{6,7},{7,6},{8,9},{9,8},{10,11... | collective-permute-start | bytes 245768 | tf_op jit(solution)/shard_map/ppermute | solution.py:310
  67.7 4.5 %collective-permute-start.17 = (f32[160,128]{1,0:T(8,128)S(1)}, f32[160,128]{1,0:T(8,128)S(1)}, u32[]{:S(2)}, u32[]{:S(2)}) collective-permute-start(f32[160,128]{1,0:T(8,128)S(1)} %add_four.3.refs_0_), channel_id=1, source_target_pairs={{0,2},{1,3},{2,0},{3,1},{4,6},{5,7},{6,4},{7,5},{8,10},{9,11},{10,... | collective-permute-start | bytes 245768 | tf_op jit(solution)/shard_map/ppermute | solution.py:310
  72.2 1.7 %collective-permute-start.18 = (f32[640,128]{1,0:T(8,128)S(1)}, f32[640,128]{1,0:T(8,128)S(1)}, u32[]{:S(2)}, u32[]{:S(2)}) collective-permute-start(f32[640,128]{1,0:T(8,128)S(1)} %join.1.mine), channel_id=1, source_target_pairs={{0,16},{16,0},{1,17},{17,1},{2,18},{18,2},{3,19},{19,3},{4,20},{20... | collective-permute-start | bytes 983048 | tf_op jit(solution)/shard_map/ppermute | solution.py:513

commit v16 on v15

--- a/solution.py
+++ b/solution.py
@@ -545,10 +545,13 @@
             halo[lead] = exchange(lead, new[lead])
             if step == 0:
                 stored["inner"] = load_blocks(after(blocks, new[lead]))
-            new["inner"] = inner_rows(new[lead])
-            new[lag] = edge_rows(lag, new["inner"])
+                new[lag] = edge_rows(lag, stored["inner"])
+                new["inner"] = inner_rows(new[lag])
+            else:
+                new["inner"] = inner_rows(new[lead])
+                new[lag] = edge_rows(lag, new["inner"])
             halo[lag] = exchange(lag, new[lag])
-            halo[lead] = after(halo[lead], new[lag])
+            halo[lead] = after(halo[lead], new[lag], new["inner"])
         prev = dict(edges, inner=inner)
         edges, inner = {name: new[name] for name in edges}, new["inner"]
     last = edges[lag].reshape(-1, width)

time: 90.4 us -> 89.7 us (level)
    ppermute x6, waiting for transfers between devices: 7.59 us -> 5.54 us  [exchange(): return lax.ppermute(value, 'patch', pairs[name])]
where the time goes in v16:
time: 89.7 us; the launch traced here: 89.4 us
  Pallas kernels  39.2 us (44%)
  starting transfers between devices  26.7 us (30%)
  waiting for transfers between devices  21.8 us (24%)
  between operations  1.05 us (1%)
    pallas_call x1, Pallas kernels, rotate(): pl.pallas_call(body, in_specs=[VMEM, VMEM] + [ANY] * 6, out_specs=ANY, ou...  16 us
    pallas_call x9, Pallas kernels, tile_rows(): pl.pallas_call(functools.partial(rows_kernel, name), in_specs=[VMEM] * le...  14.9 us
    ppermute x9, starting transfers between devices, from_others(): got.append(lax.ppermute(value, ('cols', 'patch'), pairs))  14.7 us
    ppermute x9, waiting for transfers between devices, from_others(): got.append(lax.ppermute(value, ('cols', 'patch'), pairs))  13.8 us
    ppermute x6, starting transfers between devices, exchange(): return lax.ppermute(value, 'patch', pairs[name])  11.2 us
    pallas_call x3, Pallas kernels, load_call(): pl.pallas_call(body, in_specs=[VMEM] * len(table) + [HBM] * len(args), ou...  6.29 us
    ppermute x6, waiting for transfers between devices, exchange(): return lax.ppermute(value, 'patch', pairs[name])  5.54 us
    ppermute x4, waiting for transfers between devices, sibling(): return lax.ppermute(value, 'cols', [(0, 1), (1, 0)])  2.47 us
  transfers between devices with their start and end apart: 19, of which 12 were waited for; matrix products, arithmetic and copies ran while one was open for 0% of the time, Pallas kernels for 24%

profile of v16, /device:TPU:0, one launch (start us, length us, event | category | flops | bytes accessed | tf_op | source)
XLA Modules:
  0.0 89.4 jit_solution(8475099780998236400)
XLA Ops:
  0.7 0.7 concatenate.3.table_ref
  1.3 1.2 %masked_edges.1 = (bf16[4,128,256]{2,1,0:T(8,128)(2,1)S(1)}, bf16[4,128,256]{2,1,0:T(8,128)(2,1)S(1)}) custom-call(s32[9,32]{1,0:T(8,128)S(1)} %concatenate.3.table_ref, bf16[32,128,256]{2,1,0:T(8,128)(2,1)} %bitcast.16), custom_call_target="tpu_custom_call" | custom-call | flops 1000 | bytes 1000 | tf_op jit(solution)/shard_map/masked_edges/pallas_call | solution.py:109
  2.5 3.0 %collective-permute-start.1 = (bf16[4,128,256]{2,1,0:T(8,128)(2,1)S(1)}, bf16[4,128,256]{2,1,0:T(8,128)(2,1)S(1)}, u32[]{:S(2)}, u32[]{:S(2)}) collective-permute-start(bf16[4,128,256]{2,1,0:T(8,128)(2,1)S(1)} %get-tuple-element.40.refs_1_.refs_0_.refs_3_), channel_id=1, source_target_pairs={{0,1},{1,0},{2,3},{3,2},{4,5},{5,4},{6,7},{7,6},{8,9},{9,8},{10,11... | collective-permute-start | bytes 786440 | tf_op jit(solution)/shard_map/ppermute | solution.py:510
  5.5 2.2 %load_fields.1 = (bf16[24,128,256]{2,1,0:T(8,128)(2,1)S(1)}, bf16[4,8,128,128]{3,2,1,0:T(8,128)(2,1)S(1)}, bf16[4,8,128,128]{3,2,1,0:T(8,128)(2,1)S(1)}) custom-call(s32[9,32]{1,0:T(8,128)S(1)} %concatenate.3.table_ref, bf16[32,128,256]{2,1,0:T(8,128)(2,1)} %bitcast.17, bf16[32,8,128,128]{3,2,1,0:T(8,128)(2,1)} %blocks_ref.2), custom_call_target="tpu_custom_call" | custom-call | flops 1000 | bytes 1000 | tf_op jit(solution)/shard_map/load_fields/pallas_call | solution.py:109
  7.8 0.7 collective-permute-start
  8.5 3.4 %collective-permute-done.1.refs_0_ = bf16[4,128,256]{2,1,0:T(8,128)(2,1)S(1)} collective-permute-done((bf16[4,128,256]{2,1,0:T(8,128)(2,1)S(1)}, bf16[4,128,256]{2,1,0:T(8,128)(2,1)S(1)}, u32[]{:S(2)}, u32[]{:S(2)}) %collective-permute-start.1) | collective-permute-done | bytes 262176 | tf_op jit(solution)/shard_map/ppermute | solution.py:510
  11.8 1.1 %rows_even.3.refs_1_.refs_0_.refs_3_ = bf16[4,128,256]{2,1,0:T(8,128)(2,1)S(1)} custom-call(s32[9,32]{1,0:T(8,128)S(1)} %concatenate.3.table_ref, bf16[4,128,256]{2,1,0:T(8,128)(2,1)S(1)} %collective-permute-done.1.refs_0_, bf16[4,128,256]{2,1,0:T(8,128)(2,1)S(1)} %get-tuple-element.40.refs_1_.refs_0_.refs_3_, ...), custom_call_target="tpu_custom_call" | custom-call | flops 1000 | bytes 1000 | tf_op jit(solution)/shard_map/rows_even/pallas_call | solution.py:187
  13.0 1.8 %collective-permute-start.3 = (bf16[4,128,256]{2,1,0:T(8,128)(2,1)S(1)}, bf16[4,128,256]{2,1,0:T(8,128)(2,1)S(1)}, u32[]{:S(2)}, u32[]{:S(2)}) collective-permute-start(bf16[4,128,256]{2,1,0:T(8,128)(2,1)S(1)} %rows_even.3.refs_1_.refs_0_.refs_3_), channel_id=1, source_target_pairs={{0,1},{1,0},{2,3},{3,2},{4,5},{5,4},{6,7},{7,6},{8,9},{9,8},{10,11... | collective-permute-start | bytes 786440 | tf_op jit(solution)/shard_map/ppermute | solution.py:510
  14.8 2.9 %load_blocks.1.refs_3_.refs_4_ = bf16[24,8,128,128]{3,2,1,0:T(8,128)(2,1)S(1)} custom-call(bf16[32,8,128,128]{3,2,1,0:T(8,128)(2,1)} %blocks_ref.2), custom_call_target="tpu_custom_call" | custom-call | flops 1000 | bytes 1000 | tf_op jit(solution)/shard_map/load_blocks/pallas_call | solution.py:109
  17.6 0.0 collective-permute-done.refs_0_
  17.6 1.1 %rows_odd.3.refs_1_.refs_3_ = bf16[4,128,256]{2,1,0:T(8,128)(2,1)S(1)} custom-call(s32[9,32]{1,0:T(8,128)S(1)} %concatenate.3.table_ref, bf16[4,128,256]{2,1,0:T(8,128)(2,1)S(1)} %collective-permute-done.refs_0_, bf16[4,128,256]{2,1,0:T(8,128)(2,1)S(1)} %get-tuple-element.34.refs_1_.refs_3_, bf16[24,128,256]{2,1,0:T(8,128)(2,1)S(1)} %get-tuple-element.33.refs_2_.refs_3_, ...), custom_call_target="tpu_custom_call" | custom-call | flops 1000 | bytes 1000 | tf_op jit(solution)/shard_map/rows_odd/pallas_call | solution.py:187
  18.8 0.7 collective-permute-start.2
  19.5 2.7 %rows_inner.3.refs_2_.refs_3_ = bf16[24,128,256]{2,1,0:T(8,128)(2,1)S(1)} custom-call(s32[9,32]{1,0:T(8,128)S(1)} %concatenate.3.table_ref, bf16[4,128,256]{2,1,0:T(8,128)(2,1)S(1)} %get-tuple-element.40.refs_1_.refs_0_.refs_3_, bf16[4,128,256]{2,1,0:T(8,128)(2,1)S(1)} %get-tuple-element.34.refs_1_.refs_3_, ...), custom_call_target="tpu_custom_call" | custom-call | flops 1000 | bytes 1000 | tf_op jit(solution)/shard_map/rows_inner/pallas_call | solution.py:187
  22.2 2.2 %collective-permute-done.3.refs_0_ = bf16[4,128,256]{2,1,0:T(8,128)(2,1)S(1)} collective-permute-done((bf16[4,128,256]{2,1,0:T(8,128)(2,1)S(1)}, bf16[4,128,256]{2,1,0:T(8,128)(2,1)S(1)}, u32[]{:S(2)}, u32[]{:S(2)}) %collective-permute-start.3) | collective-permute-done | bytes 262176 | tf_op jit(solution)/shard_map/ppermute | solution.py:510
  24.3 1.1 %rows_even.4.refs_0_.refs_1_ = bf16[4,128,256]{2,1,0:T(8,128)(2,1)S(1)} custom-call(s32[9,32]{1,0:T(8,128)S(1)} %concatenate.3.table_ref, bf16[4,128,256]{2,1,0:T(8,128)(2,1)S(1)} %collective-permute-done.3.refs_0_, bf16[4,128,256]{2,1,0:T(8,128)(2,1)S(1)} %rows_even.3.refs_1_.refs_0_.refs_3_, bf16[24,128,256]{2,1,0:T(8,128)(2,1)S(1)} %rows_inner.3.refs_2_.refs_3_, ...), custom_call_target="tpu_custom_call" | custom-call | flops 1000 | bytes 1000 | tf_op jit(solution)/shard_map/rows_even/pallas_call | solution.py:187
  25.5 4.2 %collective-permute-start.5 = (bf16[4,128,256]{2,1,0:T(8,128)(2,1)S(1)}, bf16[4,128,256]{2,1,0:T(8,128)(2,1)S(1)}, u32[]{:S(2)}, u32[]{:S(2)}) collective-permute-start(bf16[4,128,256]{2,1,0:T(8,128)(2,1)S(1)} %rows_even.4.refs_0_.refs_1_), channel_id=1, source_target_pairs={{0,1},{1,0},{2,3},{3,2},{4,5},{5,4},{6,7},{7,6},{8,9},{9,8},{10,11... | collective-permute-start | bytes 786440 | tf_op jit(solution)/shard_map/ppermute | solution.py:510
  29.7 2.7 %rows_inner.4.refs_2_ = bf16[24,128,256]{2,1,0:T(8,128)(2,1)S(1)} custom-call(s32[9,32]{1,0:T(8,128)S(1)} %concatenate.3.table_ref, bf16[4,128,256]{2,1,0:T(8,128)(2,1)S(1)} %rows_even.3.refs_1_.refs_0_.refs_3_, bf16[4,128,256]{2,1,0:T(8,128)(2,1)S(1)} %rows_odd.3.refs_1_.refs_3_, bf16[24,128,256]{2,1,0:T(8,128)(2,1)S(1)} %rows_inner.3.refs_2_.refs_3_, ...), custom_call_target="tpu_custom_call" | custom-call | flops 1000 | bytes 1000 | tf_op jit(solution)/shard_map/rows_inner/pallas_call | solution.py:187
  32.4 0.0 collective-permute-done.2.refs_0_
  32.5 1.1 %rows_odd.4.refs_1_ = bf16[4,128,256]{2,1,0:T(8,128)(2,1)S(1)} custom-call(s32[9,32]{1,0:T(8,128)S(1)} %concatenate.3.table_ref, bf16[4,128,256]{2,1,0:T(8,128)(2,1)S(1)} %collective-permute-done.2.refs_0_, bf16[4,128,256]{2,1,0:T(8,128)(2,1)S(1)} %rows_odd.3.refs_1_.refs_3_, bf16[24,128,256]{2,1,0:T(8,128)(2,1)S(1)} %rows_inner.3.refs_2_.refs_3_, ...), custom_call_target="tpu_custom_call" | custom-call | flops 1000 | bytes 1000 | tf_op jit(solution)/shard_map/rows_odd/pallas_call | solution.py:187
  33.6 0.9 collective-permute-start.4
  34.5 2.7 %rows_inner.5 = bf16[24,128,256]{2,1,0:T(8,128)(2,1)S(1)} custom-call(s32[9,32]{1,0:T(8,128)S(1)} %concatenate.3.table_ref, bf16[4,128,256]{2,1,0:T(8,128)(2,1)S(1)} %rows_even.4.refs_0_.refs_1_, bf16[4,128,256]{2,1,0:T(8,128)(2,1)S(1)} %rows_odd.4.refs_1_, bf16[24,128,256]{2,1,0:T(8,128)(2,1)S(1)} %rows_inner.4.refs_2_, ...), custom_call_target="tpu_custom_call" | custom-call | flops 1000 | bytes 1000 | tf_op jit(solution)/shard_map/rows_inner/pallas_call | solution.py:187
  37.2 0.1 collective-permute-start.8
  37.3 0.0 collective-permute-done.5.refs_0_
  37.3 1.1 %rows_even.5 = bf16[4,128,256]{2,1,0:T(8,128)(2,1)S(1)} custom-call(s32[9,32]{1,0:T(8,128)S(1)} %concatenate.3.table_ref, bf16[4,128,256]{2,1,0:T(8,128)(2,1)S(1)} %collective-permute-done.5.refs_0_, bf16[4,128,256]{2,1,0:T(8,128)(2,1)S(1)} %rows_even.4.refs_0_.refs_1_, bf16[24,128,256]{2,1,0:T(8,128)(2,1)S(1)} %rows_inner.4.refs_2_, ...), custom_call_target="tpu_custom_call" | custom-call | flops 1000 | bytes 1000 | tf_op jit(solution)/shard_map/rows_even/pallas_call | solution.py:187
  38.4 0.0 collective-permute-done.4.refs_0_
  38.4 0.6 collective-permute-start.7
  39.0 1.1 %rows_odd.5 = bf16[4,128,256]{2,1,0:T(8,128)(2,1)S(1)} custom-call(s32[9,32]{1,0:T(8,128)S(1)} %concatenate.3.table_ref, bf16[4,128,256]{2,1,0:T(8,128)(2,1)S(1)} %collective-permute-done.4.refs_0_, bf16[4,128,256]{2,1,0:T(8,128)(2,1)S(1)} %rows_odd.4.refs_1_, bf16[24,128,256]{2,1,0:T(8,128)(2,1)S(1)} %rows_inner.4.refs_2_, ...), custom_call_target="tpu_custom_call" | custom-call | flops 99999997952 | bytes 1000 | tf_op jit(solution)/shard_map/rows_odd/pallas_call | solution.py:187
  40.1 0.1 collective-permute-start.6
  40.2 0.8 collective-permute-done.7.refs_2_.refs_3_
  41.0 0.0 collective-permute-done.8.refs_3_.refs_4_
  41.1 1.5 %gram.1.start_ref = f32[256,512]{1,0:T(8,128)S(1)} custom-call(bf16[512,256]{1,0:T(8,128)(2,1)S(1)} %bitcast.11, bf16[3072,256]{1,0:T(8,128)(2,1)S(1)} %bitcast.8, bf16[512,256]{1,0:T(8,128)(2,1)S(1)} %collective-permute-done.7.refs_2_.refs_3_, bf16[3072,256]{1,0:T(8,128)(2,1)S(1)} %collective-permute-done.8.refs_3_.refs_4_), custom_call_target="tpu_custom_call" | custom-call | flops 1000 | bytes 1000 | tf_op jit(solution)/shard_map/gram/pallas_call | solution.py:257
  42.6 0.0 collective-permute-done.6.other_ref.refs_5_
  42.6 0.3 gram_share.1
  42.9 5.9 %collective-permute-start.10 = (f32[160,128]{1,0:T(8,128)S(1)}, f32[160,128]{1,0:T(8,128)S(1)}, u32[]{:S(2)}, u32[]{:S(2)}) collective-permute-start(f32[160,128]{1,0:T(8,128)S(1)} %get-tuple-element.53), channel_id=1, source_target_pairs={{0,3},{1,2},{2,1},{3,0},{4,7},{5,6},{6,5},{7,4},{8,11},{9,10},{10,... | collective-permute-start | bytes 245768 | tf_op jit(solution)/shard_map/ppermute | solution.py:310
  48.8 0.8 collective-permute-start.11
  49.6 0.0 collective-permute-start.9
  49.6 2.0 %collective-permute-done.10.c = f32[160,128]{1,0:T(8,128)S(1)} collective-permute-done((f32[160,128]{1,0:T(8,128)S(1)}, f32[160,128]{1,0:T(8,128)S(1)}, u32[]{:S(2)}, u32[]{:S(2)}) %collective-permute-start.10) | collective-permute-done | bytes 81952 | tf_op jit(solution)/shard_map/ppermute | solution.py:310
  51.6 2.1 %collective-permute-done.11.d = f32[160,128]{1,0:T(8,128)S(1)} collective-permute-done((f32[160,128]{1,0:T(8,128)S(1)}, f32[160,128]{1,0:T(8,128)S(1)}, u32[]{:S(2)}, u32[]{:S(2)}) %collective-permute-start.11) | collective-permute-done | bytes 81952 | tf_op jit(solution)/shard_map/ppermute | solution.py:310
  53.8 0.3 collective-permute-done.9.b
  54.1 3.4 %collective-permute-start.12 = (f32[160,128]{1,0:T(8,128)S(1)}, f32[160,128]{1,0:T(8,128)S(1)}, u32[]{:S(2)}, u32[]{:S(2)}) collective-permute-start(f32[160,128]{1,0:T(8,128)S(1)} %add_four.2.a), channel_id=1, source_target_pairs={{0,12},{1,13},{2,14},{3,15},{4,8},{5,9},{6,10},{7,11},{8,4},{9,5},... | collective-permute-start | bytes 245768 | tf_op jit(solution)/shard_map/ppermute | solution.py:310
  57.4 0.1 collective-permute-start.13
  57.5 1.0 %collective-permute-start.14 = (f32[160,128]{1,0:T(8,128)S(1)}, f32[160,128]{1,0:T(8,128)S(1)}, u32[]{:S(2)}, u32[]{:S(2)}) collective-permute-start(f32[160,128]{1,0:T(8,128)S(1)} %add_four.2.a), channel_id=1, source_target_pairs={{0,4},{1,5},{2,6},{3,7},{4,0},{5,1},{6,2},{7,3},{8,12},{9,13},{10,... | collective-permute-start | bytes 245768 | tf_op jit(solution)/shard_map/ppermute | solution.py:310
  58.5 2.1 %collective-permute-done.12.b = f32[160,128]{1,0:T(8,128)S(1)} collective-permute-done((f32[160,128]{1,0:T(8,128)S(1)}, f32[160,128]{1,0:T(8,128)S(1)}, u32[]{:S(2)}, u32[]{:S(2)}) %collective-permute-start.12) | collective-permute-done | bytes 81952 | tf_op jit(solution)/shard_map/ppermute | solution.py:310
  60.6 4.0 %collective-permute-done.13.c = f32[160,128]{1,0:T(8,128)S(1)} collective-permute-done((f32[160,128]{1,0:T(8,128)S(1)}, f32[160,128]{1,0:T(8,128)S(1)}, u32[]{:S(2)}, u32[]{:S(2)}) %collective-permute-start.13) | collective-permute-done | bytes 81952 | tf_op jit(solution)/shard_map/ppermute | solution.py:310
  64.6 0.0 collective-permute-done.14.d
  64.6 1.7 %collective-permute-start.15 = (f32[160,128]{1,0:T(8,128)S(1)}, f32[160,128]{1,0:T(8,128)S(1)}, u32[]{:S(2)}, u32[]{:S(2)}) collective-permute-start(f32[160,128]{1,0:T(8,128)S(1)} %add_four.3.refs_0_), channel_id=1, source_target_pairs={{0,3},{1,2},{2,1},{3,0},{4,7},{5,6},{6,5},{7,4},{8,11},{9,10},{10,... | collective-permute-start | bytes 245768 | tf_op jit(solution)/shard_map/ppermute | solution.py:310
  66.3 0.8 collective-permute-start.16
  67.0 1.1 %collective-permute-start.17 = (f32[160,128]{1,0:T(8,128)S(1)}, f32[160,128]{1,0:T(8,128)S(1)}, u32[]{:S(2)}, u32[]{:S(2)}) collective-permute-start(f32[160,128]{1,0:T(8,128)S(1)} %add_four.3.refs_0_), channel_id=1, source_target_pairs={{0,2},{1,3},{2,0},{3,1},{4,6},{5,7},{6,4},{7,5},{8,10},{9,11},{10,... | collective-permute-start | bytes 245768 | tf_op jit(solution)/shard_map/ppermute | solution.py:310
  68.1 2.5 %collective-permute-done.15.refs_1_ = f32[160,128]{1,0:T(8,128)S(1)} collective-permute-done((f32[160,128]{1,0:T(8,128)S(1)}, f32[160,128]{1,0:T(8,128)S(1)}, u32[]{:S(2)}, u32[]{:S(2)}) %collective-permute-start.15) | collective-permute-done | bytes 81952 | tf_op jit(solution)/shard_map/ppermute | solution.py:310
  70.6 0.6 collective-permute-done.16.refs_2_
  71.2 0.3 collective-permute-done.17.refs_3_
  71.5 0.1 collective-permute-start.18
  71.6 1.6 %collective-permute-done.18.theirs = f32[640,128]{1,0:T(8,128)S(1)} collective-permute-done((f32[640,128]{1,0:T(8,128)S(1)}, f32[640,128]{1,0:T(8,128)S(1)}, u32[]{:S(2)}, u32[]{:S(2)}) %collective-permute-start.18) | collective-permute-done | bytes 327712 | tf_op jit(solution)/shard_map/ppermute | solution.py:513
  73.2 16.0 %rotate.1 = bf16[4096,256]{1,0:T(8,128)(2,1)} custom-call(f32[640,128]{1,0:T(8,128)S(1)} %join.1.mine, f32[640,128]{1,0:T(8,128)S(1)} %collective-permute-done.18.theirs, bf16[512,256]{1,0:T(8,128)(2,1)S(1)} %bitcast.12, bf16[3072,256]{1,0:T(8,128)(2,1)S(1)} %bitcast.9, bf16[512,256]{1,0:T(8,128)(2,1)S(1)} %bitcast.15, ...), custom_call_target="tpu_custom_call" | custom-call | flops 17985175552 | bytes 6291456 | tf_op jit(solution)/shard_map/rotate/pallas_call | solution.py:472
  (3 shorter events, 0.1 us)
Async XLA Ops:
  2.5 9.3 %collective-permute-start.1 = (bf16[4,128,256]{2,1,0:T(8,128)(2,1)S(1)}, bf16[4,128,256]{2,1,0:T(8,128)(2,1)S(1)}, u32[]{:S(2)}, u32[]{:S(2)}) collective-permute-start(bf16[4,128,256]{2,1,0:T(8,128)(2,1)S(1)} %get-tuple-element.40.refs_1_.refs_0_.refs_3_), channel_id=1, source_target_pairs={{0,1},{1,0},{2,3},{3,2},{4,5},{5,4},{6,7},{7,6},{8,9},{9,8},{10,11... | collective-permute-start | bytes 786440 | tf_op jit(solution)/shard_map/ppermute | solution.py:510
  7.8 9.9 %collective-permute-start = (bf16[4,128,256]{2,1,0:T(8,128)(2,1)S(1)}, bf16[4,128,256]{2,1,0:T(8,128)(2,1)S(1)}, u32[]{:S(2)}, u32[]{:S(2)}) collective-permute-start(bf16[4,128,256]{2,1,0:T(8,128)(2,1)S(1)} %get-tuple-element.34.refs_1_.refs_3_), channel_id=1, source_target_pairs={{1,2},{2,1},{3,4},{4,3},{5,6},{6,5},{7,8},{8,7},{9,10},{10,9},{11,... | collective-permute-start | bytes 786440 | tf_op jit(solution)/shard_map/ppermute | solution.py:510
  13.0 11.4 %collective-permute-start.3 = (bf16[4,128,256]{2,1,0:T(8,128)(2,1)S(1)}, bf16[4,128,256]{2,1,0:T(8,128)(2,1)S(1)}, u32[]{:S(2)}, u32[]{:S(2)}) collective-permute-start(bf16[4,128,256]{2,1,0:T(8,128)(2,1)S(1)} %rows_even.3.refs_1_.refs_0_.refs_3_), channel_id=1, source_target_pairs={{0,1},{1,0},{2,3},{3,2},{4,5},{5,4},{6,7},{7,6},{8,9},{9,8},{10,11... | collective-permute-start | bytes 786440 | tf_op jit(solution)/shard_map/ppermute | solution.py:510
  18.8 13.7 %collective-permute-start.2 = (bf16[4,128,256]{2,1,0:T(8,128)(2,1)S(1)}, bf16[4,128,256]{2,1,0:T(8,128)(2,1)S(1)}, u32[]{:S(2)}, u32[]{:S(2)}) collective-permute-start(bf16[4,128,256]{2,1,0:T(8,128)(2,1)S(1)} %rows_odd.3.refs_1_.refs_3_), channel_id=1, source_target_pairs={{1,2},{2,1},{3,4},{4,3},{5,6},{6,5},{7,8},{8,7},{9,10},{10,9},{11,... | collective-permute-start | bytes 786440 | tf_op jit(solution)/shard_map/ppermute | solution.py:510
  25.5 11.8 %collective-permute-start.5 = (bf16[4,128,256]{2,1,0:T(8,128)(2,1)S(1)}, bf16[4,128,256]{2,1,0:T(8,128)(2,1)S(1)}, u32[]{:S(2)}, u32[]{:S(2)}) collective-permute-start(bf16[4,128,256]{2,1,0:T(8,128)(2,1)S(1)} %rows_even.4.refs_0_.refs_1_), channel_id=1, source_target_pairs={{0,1},{1,0},{2,3},{3,2},{4,5},{5,4},{6,7},{7,6},{8,9},{9,8},{10,11... | collective-permute-start | bytes 786440 | tf_op jit(solution)/shard_map/ppermute | solution.py:510
  33.6 4.8 %collective-permute-start.4 = (bf16[4,128,256]{2,1,0:T(8,128)(2,1)S(1)}, bf16[4,128,256]{2,1,0:T(8,128)(2,1)S(1)}, u32[]{:S(2)}, u32[]{:S(2)}) collective-permute-start(bf16[4,128,256]{2,1,0:T(8,128)(2,1)S(1)} %rows_odd.4.refs_1_), channel_id=1, source_target_pairs={{1,2},{2,1},{3,4},{4,3},{5,6},{6,5},{7,8},{8,7},{9,10},{10,9},{11,... | collective-permute-start | bytes 786440 | tf_op jit(solution)/shard_map/ppermute | solution.py:510
  37.2 3.9 %collective-permute-start.8 = (bf16[3072,256]{1,0:T(8,128)(2,1)S(1)}, bf16[3072,256]{1,0:T(8,128)(2,1)S(1)}, u32[]{:S(2)}, u32[]{:S(2)}) collective-permute-start(bf16[3072,256]{1,0:T(8,128)(2,1)S(1)} %bitcast.7), channel_id=1, source_target_pairs={{0,16},{16,0},{1,17},{17,1},{2,18},{18,2},{3,19},{19,3},{4,20},{20... | collective-permute-start | bytes 4718600 | tf_op jit(solution)/shard_map/ppermute | solution.py:513
  38.4 2.6 %collective-permute-start.7 = (bf16[512,256]{1,0:T(8,128)(2,1)S(1)}, bf16[512,256]{1,0:T(8,128)(2,1)S(1)}, u32[]{:S(2)}, u32[]{:S(2)}) collective-permute-start(bf16[512,256]{1,0:T(8,128)(2,1)S(1)} %bitcast.10), channel_id=1, source_target_pairs={{0,16},{16,0},{1,17},{17,1},{2,18},{18,2},{3,19},{19,3},{4,20},{20... | collective-permute-start | bytes 786440 | tf_op jit(solution)/shard_map/ppermute | solution.py:513
  40.1 2.5 %collective-permute-start.6 = (bf16[512,256]{1,0:T(8,128)(2,1)S(1)}, bf16[512,256]{1,0:T(8,128)(2,1)S(1)}, u32[]{:S(2)}, u32[]{:S(2)}) collective-permute-start(bf16[512,256]{1,0:T(8,128)(2,1)S(1)} %bitcast.13), channel_id=1, source_target_pairs={{0,16},{16,0},{1,17},{17,1},{2,18},{18,2},{3,19},{19,3},{4,20},{20... | collective-permute-start | bytes 786440 | tf_op jit(solution)/shard_map/ppermute | solution.py:513
  42.9 8.7 %collective-permute-start.10 = (f32[160,128]{1,0:T(8,128)S(1)}, f32[160,128]{1,0:T(8,128)S(1)}, u32[]{:S(2)}, u32[]{:S(2)}) collective-permute-start(f32[160,128]{1,0:T(8,128)S(1)} %get-tuple-element.53), channel_id=1, source_target_pairs={{0,3},{1,2},{2,1},{3,0},{4,7},{5,6},{6,5},{7,4},{8,11},{9,10},{10,... | collective-permute-start | bytes 245768 | tf_op jit(solution)/shard_map/ppermute | solution.py:310
  48.8 4.9 %collective-permute-start.11 = (f32[160,128]{1,0:T(8,128)S(1)}, f32[160,128]{1,0:T(8,128)S(1)}, u32[]{:S(2)}, u32[]{:S(2)}) collective-permute-start(f32[160,128]{1,0:T(8,128)S(1)} %get-tuple-element.54), channel_id=1, source_target_pairs={{0,1},{1,0},{2,3},{3,2},{4,5},{5,4},{6,7},{7,6},{8,9},{9,8},{10,11... | collective-permute-start | bytes 245768 | tf_op jit(solution)/shard_map/ppermute | solution.py:310
  49.6 4.4 %collective-permute-start.9 = (f32[160,128]{1,0:T(8,128)S(1)}, f32[160,128]{1,0:T(8,128)S(1)}, u32[]{:S(2)}, u32[]{:S(2)}) collective-permute-start(f32[160,128]{1,0:T(8,128)S(1)} %get-tuple-element.52), channel_id=1, source_target_pairs={{0,2},{1,3},{2,0},{3,1},{4,6},{5,7},{6,4},{7,5},{8,10},{9,11},{10,... | collective-permute-start | bytes 245768 | tf_op jit(solution)/shard_map/ppermute | solution.py:310
  54.1 6.5 %collective-permute-start.12 = (f32[160,128]{1,0:T(8,128)S(1)}, f32[160,128]{1,0:T(8,128)S(1)}, u32[]{:S(2)}, u32[]{:S(2)}) collective-permute-start(f32[160,128]{1,0:T(8,128)S(1)} %add_four.2.a), channel_id=1, source_target_pairs={{0,12},{1,13},{2,14},{3,15},{4,8},{5,9},{6,10},{7,11},{8,4},{9,5},... | collective-permute-start | bytes 245768 | tf_op jit(solution)/shard_map/ppermute | solution.py:310
  57.4 7.1 %collective-permute-start.13 = (f32[160,128]{1,0:T(8,128)S(1)}, f32[160,128]{1,0:T(8,128)S(1)}, u32[]{:S(2)}, u32[]{:S(2)}) collective-permute-start(f32[160,128]{1,0:T(8,128)S(1)} %add_four.2.a), channel_id=1, source_target_pairs={{0,8},{1,9},{2,10},{3,11},{4,12},{5,13},{6,14},{7,15},{8,0},{9,1},... | collective-permute-start | bytes 245768 | tf_op jit(solution)/shard_map/ppermute | solution.py:310
  57.5 7.1 %collective-permute-start.14 = (f32[160,128]{1,0:T(8,128)S(1)}, f32[160,128]{1,0:T(8,128)S(1)}, u32[]{:S(2)}, u32[]{:S(2)}) collective-permute-start(f32[160,128]{1,0:T(8,128)S(1)} %add_four.2.a), channel_id=1, source_target_pairs={{0,4},{1,5},{2,6},{3,7},{4,0},{5,1},{6,2},{7,3},{8,12},{9,13},{10,... | collective-permute-start | bytes 245768 | tf_op jit(solution)/shard_map/ppermute | solution.py:310
  64.6 6.0 %collective-permute-start.15 = (f32[160,128]{1,0:T(8,128)S(1)}, f32[160,128]{1,0:T(8,128)S(1)}, u32[]{:S(2)}, u32[]{:S(2)}) collective-permute-start(f32[160,128]{1,0:T(8,128)S(1)} %add_four.3.refs_0_), channel_id=1, source_target_pairs={{0,3},{1,2},{2,1},{3,0},{4,7},{5,6},{6,5},{7,4},{8,11},{9,10},{10,... | collective-permute-start | bytes 245768 | tf_op jit(solution)/shard_map/ppermute | solution.py:310
  66.3 4.9 %collective-permute-start.16 = (f32[160,128]{1,0:T(8,128)S(1)}, f32[160,128]{1,0:T(8,128)S(1)}, u32[]{:S(2)}, u32[]{:S(2)}) collective-permute-start(f32[160,128]{1,0:T(8,128)S(1)} %add_four.3.refs_0_), channel_id=1, source_target_pairs={{0,1},{1,0},{2,3},{3,2},{4,5},{5,4},{6,7},{7,6},{8,9},{9,8},{10,11... | collective-permute-start | bytes 245768 | tf_op jit(solution)/shard_map/ppermute | solution.py:310
  67.0 4.5 %collective-permute-start.17 = (f32[160,128]{1,0:T(8,128)S(1)}, f32[160,128]{1,0:T(8,128)S(1)}, u32[]{:S(2)}, u32[]{:S(2)}) collective-permute-start(f32[160,128]{1,0:T(8,128)S(1)} %add_four.3.refs_0_), channel_id=1, source_target_pairs={{0,2},{1,3},{2,0},{3,1},{4,6},{5,7},{6,4},{7,5},{8,10},{9,11},{10,... | collective-permute-start | bytes 245768 | tf_op jit(solution)/shard_map/ppermute | solution.py:310
  71.5 1.7 %collective-permute-start.18 = (f32[640,128]{1,0:T(8,128)S(1)}, f32[640,128]{1,0:T(8,128)S(1)}, u32[]{:S(2)}, u32[]{:S(2)}) collective-permute-start(f32[640,128]{1,0:T(8,128)S(1)} %join.1.mine), channel_id=1, source_target_pairs={{0,16},{16,0},{1,17},{17,1},{2,18},{18,2},{3,19},{19,3},{4,20},{20... | collective-permute-start | bytes 983048 | tf_op jit(solution)/shard_map/ppermute | solution.py:513

commit v17 on v16

--- a/solution.py
+++ b/solution.py
@@ -519,7 +519,7 @@
     lead, lag = "even", "odd"
     halo = {lead: exchange(lead, edges[lead])}
     inner, *edge_blocks = load_fields(after(table, edges[lead]), start, blocks)
-    halo[lag] = exchange(lag, after(edges[lag], inner))
+    halo[lag] = exchange(lag, edges[lag])
     stored = dict(zip(("even", "odd"), edge_blocks))
     prev = dict.fromkeys(("even", "odd", "inner"))
 

time: 89.7 us -> 92.7 us (1.033)
  waiting for transfers between devices: 21.8 us -> 24.3 us
    ppermute x6, waiting for transfers between devices: 5.54 us -> 8.38 us  [exchange(): return lax.ppermute(value, 'patch', pairs[name])]
    ppermute x9, starting transfers between devices: 14.7 us -> 17.4 us  [from_others(): got.append(lax.ppermute(value, ('cols', 'patch'), pairs))]
    ppermute x6, starting transfers between devices: 11.2 us -> 9.09 us  [exchange(): return lax.ppermute(value, 'patch', pairs[name])]
  transfers between devices with their start and end apart: 19 -> 19, of which waited for: 12 -> 11; matrix products, arithmetic and copies ran while one was open for 0% -> 0% of each run, Pallas kernels for 24% -> 23%
where the time goes in v17:
time: 92.7 us; the launch traced here: 92.4 us
  Pallas kernels  39.1 us (42%)
  starting transfers between devices  27.3 us (29%)
  waiting for transfers between devices  24.3 us (26%)
  between operations  1.06 us (1%)
    ppermute x9, starting transfers between devices, from_others(): got.append(lax.ppermute(value, ('cols', 'patch'), pairs))  17.4 us
    pallas_call x1, Pallas kernels, rotate(): pl.pallas_call(body, in_specs=[VMEM, VMEM] + [ANY] * 6, out_specs=ANY, ou...  16 us
    pallas_call x9, Pallas kernels, tile_rows(): pl.pallas_call(functools.partial(rows_kernel, name), in_specs=[VMEM] * le...  14.9 us
    ppermute x9, waiting for transfers between devices, from_others(): got.append(lax.ppermute(value, ('cols', 'patch'), pairs))  13.5 us
    ppermute x6, starting transfers between devices, exchange(): return lax.ppermute(value, 'patch', pairs[name])  9.09 us
    ppermute x6, waiting for transfers between devices, exchange(): return lax.ppermute(value, 'patch', pairs[name])  8.38 us
    pallas_call x3, Pallas kernels, load_call(): pl.pallas_call(body, in_specs=[VMEM] * len(table) + [HBM] * len(args), ou...  6.17 us
    ppermute x4, waiting for transfers between devices, sibling(): return lax.ppermute(value, 'cols', [(0, 1), (1, 0)])  2.47 us
  transfers between devices with their start and end apart: 19, of which 11 were waited for; matrix products, arithmetic and copies ran while one was open for 0% of the time, Pallas kernels for 23%

profile of v17, /device:TPU:0, one launch (start us, length us, event | category | flops | bytes accessed | tf_op | source)
XLA Modules:
  0.0 92.4 jit_solution(11234941490969258410)
XLA Ops:
  0.7 0.7 concatenate.3.table_ref
  1.3 1.2 %masked_edges.1 = (bf16[4,128,256]{2,1,0:T(8,128)(2,1)S(1)}, bf16[4,128,256]{2,1,0:T(8,128)(2,1)S(1)}) custom-call(s32[9,32]{1,0:T(8,128)S(1)} %concatenate.3.table_ref, bf16[32,128,256]{2,1,0:T(8,128)(2,1)} %bitcast.16), custom_call_target="tpu_custom_call" | custom-call | flops 1000 | bytes 1000 | tf_op jit(solution)/shard_map/masked_edges/pallas_call | solution.py:109
  2.5 3.0 %collective-permute-start.1 = (bf16[4,128,256]{2,1,0:T(8,128)(2,1)S(1)}, bf16[4,128,256]{2,1,0:T(8,128)(2,1)S(1)}, u32[]{:S(2)}, u32[]{:S(2)}) collective-permute-start(bf16[4,128,256]{2,1,0:T(8,128)(2,1)S(1)} %get-tuple-element.38.refs_1_.refs_0_.refs_3_), channel_id=1, source_target_pairs={{0,1},{1,0},{2,3},{3,2},{4,5},{5,4},{6,7},{7,6},{8,9},{9,8},{10,11... | collective-permute-start | bytes 786440 | tf_op jit(solution)/shard_map/ppermute | solution.py:510
  5.5 0.7 collective-permute-start
  6.2 2.1 %load_fields.1 = (bf16[24,128,256]{2,1,0:T(8,128)(2,1)S(1)}, bf16[4,8,128,128]{3,2,1,0:T(8,128)(2,1)S(1)}, bf16[4,8,128,128]{3,2,1,0:T(8,128)(2,1)S(1)}) custom-call(s32[9,32]{1,0:T(8,128)S(1)} %concatenate.3.table_ref, bf16[32,128,256]{2,1,0:T(8,128)(2,1)} %bitcast.17, bf16[32,8,128,128]{3,2,1,0:T(8,128)(2,1)} %blocks_ref.2), custom_call_target="tpu_custom_call" | custom-call | flops 1000 | bytes 1000 | tf_op jit(solution)/shard_map/load_fields/pallas_call | solution.py:109
  8.4 8.4 %collective-permute-done.1.refs_0_ = bf16[4,128,256]{2,1,0:T(8,128)(2,1)S(1)} collective-permute-done((bf16[4,128,256]{2,1,0:T(8,128)(2,1)S(1)}, bf16[4,128,256]{2,1,0:T(8,128)(2,1)S(1)}, u32[]{:S(2)}, u32[]{:S(2)}) %collective-permute-start.1) | collective-permute-done | bytes 262176 | tf_op jit(solution)/shard_map/ppermute | solution.py:510
  16.7 1.1 %rows_even.3.refs_1_.refs_0_.refs_3_ = bf16[4,128,256]{2,1,0:T(8,128)(2,1)S(1)} custom-call(s32[9,32]{1,0:T(8,128)S(1)} %concatenate.3.table_ref, bf16[4,128,256]{2,1,0:T(8,128)(2,1)S(1)} %collective-permute-done.1.refs_0_, bf16[4,128,256]{2,1,0:T(8,128)(2,1)S(1)} %get-tuple-element.38.refs_1_.refs_0_.refs_3_, ...), custom_call_target="tpu_custom_call" | custom-call | flops 1000 | bytes 1000 | tf_op jit(solution)/shard_map/rows_even/pallas_call | solution.py:187
  17.8 2.5 %collective-permute-start.3 = (bf16[4,128,256]{2,1,0:T(8,128)(2,1)S(1)}, bf16[4,128,256]{2,1,0:T(8,128)(2,1)S(1)}, u32[]{:S(2)}, u32[]{:S(2)}) collective-permute-start(bf16[4,128,256]{2,1,0:T(8,128)(2,1)S(1)} %rows_even.3.refs_1_.refs_0_.refs_3_), channel_id=1, source_target_pairs={{0,1},{1,0},{2,3},{3,2},{4,5},{5,4},{6,7},{7,6},{8,9},{9,8},{10,11... | collective-permute-start | bytes 786440 | tf_op jit(solution)/shard_map/ppermute | solution.py:510
  20.4 2.9 %load_blocks.1.refs_3_.refs_4_ = bf16[24,8,128,128]{3,2,1,0:T(8,128)(2,1)S(1)} custom-call(bf16[32,8,128,128]{3,2,1,0:T(8,128)(2,1)} %blocks_ref.2), custom_call_target="tpu_custom_call" | custom-call | flops 1000 | bytes 1000 | tf_op jit(solution)/shard_map/load_blocks/pallas_call | solution.py:109
  23.3 0.0 collective-permute-done.refs_0_
  23.3 1.1 %rows_odd.3.refs_1_.refs_3_ = bf16[4,128,256]{2,1,0:T(8,128)(2,1)S(1)} custom-call(s32[9,32]{1,0:T(8,128)S(1)} %concatenate.3.table_ref, bf16[4,128,256]{2,1,0:T(8,128)(2,1)S(1)} %collective-permute-done.refs_0_, bf16[4,128,256]{2,1,0:T(8,128)(2,1)S(1)} %get-tuple-element.29.refs_1_.refs_3_, bf16[24,128,256]{2,1,0:T(8,128)(2,1)S(1)} %get-tuple-element.32.refs_2_.refs_3_, ...), custom_call_target="tpu_custom_call" | custom-call | flops 1000 | bytes 1000 | tf_op jit(solution)/shard_map/rows_odd/pallas_call | solution.py:187
  24.4 0.7 collective-permute-start.2
  25.1 2.7 %rows_inner.3.refs_2_.refs_3_ = bf16[24,128,256]{2,1,0:T(8,128)(2,1)S(1)} custom-call(s32[9,32]{1,0:T(8,128)S(1)} %concatenate.3.table_ref, bf16[4,128,256]{2,1,0:T(8,128)(2,1)S(1)} %get-tuple-element.38.refs_1_.refs_0_.refs_3_, bf16[4,128,256]{2,1,0:T(8,128)(2,1)S(1)} %get-tuple-element.29.refs_1_.refs_3_, ...), custom_call_target="tpu_custom_call" | custom-call | flops 1000 | bytes 1000 | tf_op jit(solution)/shard_map/rows_inner/pallas_call | solution.py:187
  27.8 0.0 collective-permute-done.3.refs_0_
  27.8 1.1 %rows_even.4.refs_0_.refs_1_ = bf16[4,128,256]{2,1,0:T(8,128)(2,1)S(1)} custom-call(s32[9,32]{1,0:T(8,128)S(1)} %concatenate.3.table_ref, bf16[4,128,256]{2,1,0:T(8,128)(2,1)S(1)} %collective-permute-done.3.refs_0_, bf16[4,128,256]{2,1,0:T(8,128)(2,1)S(1)} %rows_even.3.refs_1_.refs_0_.refs_3_, bf16[24,128,256]{2,1,0:T(8,128)(2,1)S(1)} %rows_inner.3.refs_2_.refs_3_, ...), custom_call_target="tpu_custom_call" | custom-call | flops 1000 | bytes 1000 | tf_op jit(solution)/shard_map/rows_even/pallas_call | solution.py:187
  29.0 1.3 %collective-permute-start.5 = (bf16[4,128,256]{2,1,0:T(8,128)(2,1)S(1)}, bf16[4,128,256]{2,1,0:T(8,128)(2,1)S(1)}, u32[]{:S(2)}, u32[]{:S(2)}) collective-permute-start(bf16[4,128,256]{2,1,0:T(8,128)(2,1)S(1)} %rows_even.4.refs_0_.refs_1_), channel_id=1, source_target_pairs={{0,1},{1,0},{2,3},{3,2},{4,5},{5,4},{6,7},{7,6},{8,9},{9,8},{10,11... | collective-permute-start | bytes 786440 | tf_op jit(solution)/shard_map/ppermute | solution.py:510
  30.3 2.7 %rows_inner.4.refs_2_ = bf16[24,128,256]{2,1,0:T(8,128)(2,1)S(1)} custom-call(s32[9,32]{1,0:T(8,128)S(1)} %concatenate.3.table_ref, bf16[4,128,256]{2,1,0:T(8,128)(2,1)S(1)} %rows_even.3.refs_1_.refs_0_.refs_3_, bf16[4,128,256]{2,1,0:T(8,128)(2,1)S(1)} %rows_odd.3.refs_1_.refs_3_, bf16[24,128,256]{2,1,0:T(8,128)(2,1)S(1)} %rows_inner.3.refs_2_.refs_3_, ...), custom_call_target="tpu_custom_call" | custom-call | flops 1000 | bytes 1000 | tf_op jit(solution)/shard_map/rows_inner/pallas_call | solution.py:187
  33.0 0.0 collective-permute-done.2.refs_0_
  33.0 1.1 %rows_odd.4.refs_1_ = bf16[4,128,256]{2,1,0:T(8,128)(2,1)S(1)} custom-call(s32[9,32]{1,0:T(8,128)S(1)} %concatenate.3.table_ref, bf16[4,128,256]{2,1,0:T(8,128)(2,1)S(1)} %collective-permute-done.2.refs_0_, bf16[4,128,256]{2,1,0:T(8,128)(2,1)S(1)} %rows_odd.3.refs_1_.refs_3_, bf16[24,128,256]{2,1,0:T(8,128)(2,1)S(1)} %rows_inner.3.refs_2_.refs_3_, ...), custom_call_target="tpu_custom_call" | custom-call | flops 1000 | bytes 1000 | tf_op jit(solution)/shard_map/rows_odd/pallas_call | solution.py:187
  34.2 0.9 collective-permute-start.4
  35.0 2.7 %rows_inner.5 = bf16[24,128,256]{2,1,0:T(8,128)(2,1)S(1)} custom-call(s32[9,32]{1,0:T(8,128)S(1)} %concatenate.3.table_ref, bf16[4,128,256]{2,1,0:T(8,128)(2,1)S(1)} %rows_even.4.refs_0_.refs_1_, bf16[4,128,256]{2,1,0:T(8,128)(2,1)S(1)} %rows_odd.4.refs_1_, bf16[24,128,256]{2,1,0:T(8,128)(2,1)S(1)} %rows_inner.4.refs_2_, ...), custom_call_target="tpu_custom_call" | custom-call | flops 1000 | bytes 1000 | tf_op jit(solution)/shard_map/rows_inner/pallas_call | solution.py:187
  37.8 0.1 collective-permute-start.8
  37.9 0.0 collective-permute-done.5.refs_0_
  37.9 1.1 %rows_even.5 = bf16[4,128,256]{2,1,0:T(8,128)(2,1)S(1)} custom-call(s32[9,32]{1,0:T(8,128)S(1)} %concatenate.3.table_ref, bf16[4,128,256]{2,1,0:T(8,128)(2,1)S(1)} %collective-permute-done.5.refs_0_, bf16[4,128,256]{2,1,0:T(8,128)(2,1)S(1)} %rows_even.4.refs_0_.refs_1_, bf16[24,128,256]{2,1,0:T(8,128)(2,1)S(1)} %rows_inner.4.refs_2_, ...), custom_call_target="tpu_custom_call" | custom-call | flops 1000 | bytes 1000 | tf_op jit(solution)/shard_map/rows_even/pallas_call | solution.py:187
  39.0 0.0 collective-permute-done.4.refs_0_
  39.0 0.6 collective-permute-start.7
  39.6 1.1 %rows_odd.5 = bf16[4,128,256]{2,1,0:T(8,128)(2,1)S(1)} custom-call(s32[9,32]{1,0:T(8,128)S(1)} %concatenate.3.table_ref, bf16[4,128,256]{2,1,0:T(8,128)(2,1)S(1)} %collective-permute-done.4.refs_0_, bf16[4,128,256]{2,1,0:T(8,128)(2,1)S(1)} %rows_odd.4.refs_1_, bf16[24,128,256]{2,1,0:T(8,128)(2,1)S(1)} %rows_inner.4.refs_2_, ...), custom_call_target="tpu_custom_call" | custom-call | flops 99999997952 | bytes 1000 | tf_op jit(solution)/shard_map/rows_odd/pallas_call | solution.py:187
  40.7 0.1 collective-permute-start.6
  40.8 0.8 collective-permute-done.7.refs_2_.refs_3_
  41.6 0.0 collective-permute-done.8.refs_3_.refs_4_
  41.6 1.5 %gram.1.start_ref = f32[256,512]{1,0:T(8,128)S(1)} custom-call(bf16[512,256]{1,0:T(8,128)(2,1)S(1)} %bitcast.11, bf16[3072,256]{1,0:T(8,128)(2,1)S(1)} %bitcast.8, bf16[512,256]{1,0:T(8,128)(2,1)S(1)} %collective-permute-done.7.refs_2_.refs_3_, bf16[3072,256]{1,0:T(8,128)(2,1)S(1)} %collective-permute-done.8.refs_3_.refs_4_), custom_call_target="tpu_custom_call" | custom-call | flops 1000 | bytes 1000 | tf_op jit(solution)/shard_map/gram/pallas_call | solution.py:257
  43.2 0.0 collective-permute-done.6.other_ref.refs_5_
  43.2 0.3 gram_share.1
  43.5 8.5 %collective-permute-start.10 = (f32[160,128]{1,0:T(8,128)S(1)}, f32[160,128]{1,0:T(8,128)S(1)}, u32[]{:S(2)}, u32[]{:S(2)}) collective-permute-start(f32[160,128]{1,0:T(8,128)S(1)} %get-tuple-element.51), channel_id=1, source_target_pairs={{0,3},{1,2},{2,1},{3,0},{4,7},{5,6},{6,5},{7,4},{8,11},{9,10},{10,... | collective-permute-start | bytes 245768 | tf_op jit(solution)/shard_map/ppermute | solution.py:310
  52.1 0.9 collective-permute-start.11
  52.9 0.0 collective-permute-start.9
  52.9 1.9 %collective-permute-done.10.c = f32[160,128]{1,0:T(8,128)S(1)} collective-permute-done((f32[160,128]{1,0:T(8,128)S(1)}, f32[160,128]{1,0:T(8,128)S(1)}, u32[]{:S(2)}, u32[]{:S(2)}) %collective-permute-start.10) | collective-permute-done | bytes 81952 | tf_op jit(solution)/shard_map/ppermute | solution.py:310
  54.9 2.2 %collective-permute-done.11.d = f32[160,128]{1,0:T(8,128)S(1)} collective-permute-done((f32[160,128]{1,0:T(8,128)S(1)}, f32[160,128]{1,0:T(8,128)S(1)}, u32[]{:S(2)}, u32[]{:S(2)}) %collective-permute-start.11) | collective-permute-done | bytes 81952 | tf_op jit(solution)/shard_map/ppermute | solution.py:310
  57.0 0.3 collective-permute-done.9.b
  57.4 2.4 %collective-permute-start.12 = (f32[160,128]{1,0:T(8,128)S(1)}, f32[160,128]{1,0:T(8,128)S(1)}, u32[]{:S(2)}, u32[]{:S(2)}) collective-permute-start(f32[160,128]{1,0:T(8,128)S(1)} %add_four.2.a), channel_id=1, source_target_pairs={{0,12},{1,13},{2,14},{3,15},{4,8},{5,9},{6,10},{7,11},{8,4},{9,5},... | collective-permute-start | bytes 245768 | tf_op jit(solution)/shard_map/ppermute | solution.py:310
  59.8 0.7 collective-permute-start.13
  60.5 1.3 %collective-permute-start.14 = (f32[160,128]{1,0:T(8,128)S(1)}, f32[160,128]{1,0:T(8,128)S(1)}, u32[]{:S(2)}, u32[]{:S(2)}) collective-permute-start(f32[160,128]{1,0:T(8,128)S(1)} %add_four.2.a), channel_id=1, source_target_pairs={{0,4},{1,5},{2,6},{3,7},{4,0},{5,1},{6,2},{7,3},{8,12},{9,13},{10,... | collective-permute-start | bytes 245768 | tf_op jit(solution)/shard_map/ppermute | solution.py:310
  61.8 2.7 %collective-permute-done.12.b = f32[160,128]{1,0:T(8,128)S(1)} collective-permute-done((f32[160,128]{1,0:T(8,128)S(1)}, f32[160,128]{1,0:T(8,128)S(1)}, u32[]{:S(2)}, u32[]{:S(2)}) %collective-permute-start.12) | collective-permute-done | bytes 81952 | tf_op jit(solution)/shard_map/ppermute | solution.py:310
  64.6 2.8 %collective-permute-done.13.c = f32[160,128]{1,0:T(8,128)S(1)} collective-permute-done((f32[160,128]{1,0:T(8,128)S(1)}, f32[160,128]{1,0:T(8,128)S(1)}, u32[]{:S(2)}, u32[]{:S(2)}) %collective-permute-start.13) | collective-permute-done | bytes 81952 | tf_op jit(solution)/shard_map/ppermute | solution.py:310
  67.4 0.0 collective-permute-done.14.d
  67.5 1.7 %collective-permute-start.15 = (f32[160,128]{1,0:T(8,128)S(1)}, f32[160,128]{1,0:T(8,128)S(1)}, u32[]{:S(2)}, u32[]{:S(2)}) collective-permute-start(f32[160,128]{1,0:T(8,128)S(1)} %add_four.3.refs_0_), channel_id=1, source_target_pairs={{0,3},{1,2},{2,1},{3,0},{4,7},{5,6},{6,5},{7,4},{8,11},{9,10},{10,... | collective-permute-start | bytes 245768 | tf_op jit(solution)/shard_map/ppermute | solution.py:310
  69.1 0.9 collective-permute-start.16
  70.0 1.0 %collective-permute-start.17 = (f32[160,128]{1,0:T(8,128)S(1)}, f32[160,128]{1,0:T(8,128)S(1)}, u32[]{:S(2)}, u32[]{:S(2)}) collective-permute-start(f32[160,128]{1,0:T(8,128)S(1)} %add_four.3.refs_0_), channel_id=1, source_target_pairs={{0,2},{1,3},{2,0},{3,1},{4,6},{5,7},{6,4},{7,5},{8,10},{9,11},{10,... | collective-permute-start | bytes 245768 | tf_op jit(solution)/shard_map/ppermute | solution.py:310
  71.0 2.6 %collective-permute-done.15.refs_1_ = f32[160,128]{1,0:T(8,128)S(1)} collective-permute-done((f32[160,128]{1,0:T(8,128)S(1)}, f32[160,128]{1,0:T(8,128)S(1)}, u32[]{:S(2)}, u32[]{:S(2)}) %collective-permute-start.15) | collective-permute-done | bytes 81952 | tf_op jit(solution)/shard_map/ppermute | solution.py:310
  73.6 0.4 collective-permute-done.16.refs_2_
  74.0 0.4 collective-permute-done.17.refs_3_
  74.5 0.1 collective-permute-start.18
  74.6 1.6 %collective-permute-done.18.theirs = f32[640,128]{1,0:T(8,128)S(1)} collective-permute-done((f32[640,128]{1,0:T(8,128)S(1)}, f32[640,128]{1,0:T(8,128)S(1)}, u32[]{:S(2)}, u32[]{:S(2)}) %collective-permute-start.18) | collective-permute-done | bytes 327712 | tf_op jit(solution)/shard_map/ppermute | solution.py:513
  76.2 16.0 %rotate.1 = bf16[4096,256]{1,0:T(8,128)(2,1)} custom-call(f32[640,128]{1,0:T(8,128)S(1)} %join.1.mine, f32[640,128]{1,0:T(8,128)S(1)} %collective-permute-done.18.theirs, bf16[512,256]{1,0:T(8,128)(2,1)S(1)} %bitcast.12, bf16[3072,256]{1,0:T(8,128)(2,1)S(1)} %bitcast.9, bf16[512,256]{1,0:T(8,128)(2,1)S(1)} %bitcast.15, ...), custom_call_target="tpu_custom_call" | custom-call | flops 17985175552 | bytes 6291456 | tf_op jit(solution)/shard_map/rotate/pallas_call | solution.py:472
  (3 shorter events, 0.1 us)
Async XLA Ops:
  2.5 14.2 %collective-permute-start.1 = (bf16[4,128,256]{2,1,0:T(8,128)(2,1)S(1)}, bf16[4,128,256]{2,1,0:T(8,128)(2,1)S(1)}, u32[]{:S(2)}, u32[]{:S(2)}) collective-permute-start(bf16[4,128,256]{2,1,0:T(8,128)(2,1)S(1)} %get-tuple-element.38.refs_1_.refs_0_.refs_3_), channel_id=1, source_target_pairs={{0,1},{1,0},{2,3},{3,2},{4,5},{5,4},{6,7},{7,6},{8,9},{9,8},{10,11... | collective-permute-start | bytes 786440 | tf_op jit(solution)/shard_map/ppermute | solution.py:510
  5.5 17.7 %collective-permute-start = (bf16[4,128,256]{2,1,0:T(8,128)(2,1)S(1)}, bf16[4,128,256]{2,1,0:T(8,128)(2,1)S(1)}, u32[]{:S(2)}, u32[]{:S(2)}) collective-permute-start(bf16[4,128,256]{2,1,0:T(8,128)(2,1)S(1)} %get-tuple-element.29.refs_1_.refs_3_), channel_id=1, source_target_pairs={{1,2},{2,1},{3,4},{4,3},{5,6},{6,5},{7,8},{8,7},{9,10},{10,9},{11,... | collective-permute-start | bytes 786440 | tf_op jit(solution)/shard_map/ppermute | solution.py:510
  17.8 10.0 %collective-permute-start.3 = (bf16[4,128,256]{2,1,0:T(8,128)(2,1)S(1)}, bf16[4,128,256]{2,1,0:T(8,128)(2,1)S(1)}, u32[]{:S(2)}, u32[]{:S(2)}) collective-permute-start(bf16[4,128,256]{2,1,0:T(8,128)(2,1)S(1)} %rows_even.3.refs_1_.refs_0_.refs_3_), channel_id=1, source_target_pairs={{0,1},{1,0},{2,3},{3,2},{4,5},{5,4},{6,7},{7,6},{8,9},{9,8},{10,11... | collective-permute-start | bytes 786440 | tf_op jit(solution)/shard_map/ppermute | solution.py:510
  24.4 8.6 %collective-permute-start.2 = (bf16[4,128,256]{2,1,0:T(8,128)(2,1)S(1)}, bf16[4,128,256]{2,1,0:T(8,128)(2,1)S(1)}, u32[]{:S(2)}, u32[]{:S(2)}) collective-permute-start(bf16[4,128,256]{2,1,0:T(8,128)(2,1)S(1)} %rows_odd.3.refs_1_.refs_3_), channel_id=1, source_target_pairs={{1,2},{2,1},{3,4},{4,3},{5,6},{6,5},{7,8},{8,7},{9,10},{10,9},{11,... | collective-permute-start | bytes 786440 | tf_op jit(solution)/shard_map/ppermute | solution.py:510
  29.0 8.9 %collective-permute-start.5 = (bf16[4,128,256]{2,1,0:T(8,128)(2,1)S(1)}, bf16[4,128,256]{2,1,0:T(8,128)(2,1)S(1)}, u32[]{:S(2)}, u32[]{:S(2)}) collective-permute-start(bf16[4,128,256]{2,1,0:T(8,128)(2,1)S(1)} %rows_even.4.refs_0_.refs_1_), channel_id=1, source_target_pairs={{0,1},{1,0},{2,3},{3,2},{4,5},{5,4},{6,7},{7,6},{8,9},{9,8},{10,11... | collective-permute-start | bytes 786440 | tf_op jit(solution)/shard_map/ppermute | solution.py:510
  34.2 4.8 %collective-permute-start.4 = (bf16[4,128,256]{2,1,0:T(8,128)(2,1)S(1)}, bf16[4,128,256]{2,1,0:T(8,128)(2,1)S(1)}, u32[]{:S(2)}, u32[]{:S(2)}) collective-permute-start(bf16[4,128,256]{2,1,0:T(8,128)(2,1)S(1)} %rows_odd.4.refs_1_), channel_id=1, source_target_pairs={{1,2},{2,1},{3,4},{4,3},{5,6},{6,5},{7,8},{8,7},{9,10},{10,9},{11,... | collective-permute-start | bytes 786440 | tf_op jit(solution)/shard_map/ppermute | solution.py:510
  37.8 3.9 %collective-permute-start.8 = (bf16[3072,256]{1,0:T(8,128)(2,1)S(1)}, bf16[3072,256]{1,0:T(8,128)(2,1)S(1)}, u32[]{:S(2)}, u32[]{:S(2)}) collective-permute-start(bf16[3072,256]{1,0:T(8,128)(2,1)S(1)} %bitcast.7), channel_id=1, source_target_pairs={{0,16},{16,0},{1,17},{17,1},{2,18},{18,2},{3,19},{19,3},{4,20},{20... | collective-permute-start | bytes 4718600 | tf_op jit(solution)/shard_map/ppermute | solution.py:513
  39.0 2.6 %collective-permute-start.7 = (bf16[512,256]{1,0:T(8,128)(2,1)S(1)}, bf16[512,256]{1,0:T(8,128)(2,1)S(1)}, u32[]{:S(2)}, u32[]{:S(2)}) collective-permute-start(bf16[512,256]{1,0:T(8,128)(2,1)S(1)} %bitcast.10), channel_id=1, source_target_pairs={{0,16},{16,0},{1,17},{17,1},{2,18},{18,2},{3,19},{19,3},{4,20},{20... | collective-permute-start | bytes 786440 | tf_op jit(solution)/shard_map/ppermute | solution.py:513
  40.7 2.5 %collective-permute-start.6 = (bf16[512,256]{1,0:T(8,128)(2,1)S(1)}, bf16[512,256]{1,0:T(8,128)(2,1)S(1)}, u32[]{:S(2)}, u32[]{:S(2)}) collective-permute-start(bf16[512,256]{1,0:T(8,128)(2,1)S(1)} %bitcast.13), channel_id=1, source_target_pairs={{0,16},{16,0},{1,17},{17,1},{2,18},{18,2},{3,19},{19,3},{4,20},{20... | collective-permute-start | bytes 786440 | tf_op jit(solution)/shard_map/ppermute | solution.py:513
  43.5 11.3 %collective-permute-start.10 = (f32[160,128]{1,0:T(8,128)S(1)}, f32[160,128]{1,0:T(8,128)S(1)}, u32[]{:S(2)}, u32[]{:S(2)}) collective-permute-start(f32[160,128]{1,0:T(8,128)S(1)} %get-tuple-element.51), channel_id=1, source_target_pairs={{0,3},{1,2},{2,1},{3,0},{4,7},{5,6},{6,5},{7,4},{8,11},{9,10},{10,... | collective-permute-start | bytes 245768 | tf_op jit(solution)/shard_map/ppermute | solution.py:310
  52.1 5.0 %collective-permute-start.11 = (f32[160,128]{1,0:T(8,128)S(1)}, f32[160,128]{1,0:T(8,128)S(1)}, u32[]{:S(2)}, u32[]{:S(2)}) collective-permute-start(f32[160,128]{1,0:T(8,128)S(1)} %get-tuple-element.52), channel_id=1, source_target_pairs={{0,1},{1,0},{2,3},{3,2},{4,5},{5,4},{6,7},{7,6},{8,9},{9,8},{10,11... | collective-permute-start | bytes 245768 | tf_op jit(solution)/shard_map/ppermute | solution.py:310
  52.9 4.4 %collective-permute-start.9 = (f32[160,128]{1,0:T(8,128)S(1)}, f32[160,128]{1,0:T(8,128)S(1)}, u32[]{:S(2)}, u32[]{:S(2)}) collective-permute-start(f32[160,128]{1,0:T(8,128)S(1)} %get-tuple-element.50), channel_id=1, source_target_pairs={{0,2},{1,3},{2,0},{3,1},{4,6},{5,7},{6,4},{7,5},{8,10},{9,11},{10,... | collective-permute-start | bytes 245768 | tf_op jit(solution)/shard_map/ppermute | solution.py:310
  57.4 7.2 %collective-permute-start.12 = (f32[160,128]{1,0:T(8,128)S(1)}, f32[160,128]{1,0:T(8,128)S(1)}, u32[]{:S(2)}, u32[]{:S(2)}) collective-permute-start(f32[160,128]{1,0:T(8,128)S(1)} %add_four.2.a), channel_id=1, source_target_pairs={{0,12},{1,13},{2,14},{3,15},{4,8},{5,9},{6,10},{7,11},{8,4},{9,5},... | collective-permute-start | bytes 245768 | tf_op jit(solution)/shard_map/ppermute | solution.py:310
  59.8 7.6 %collective-permute-start.13 = (f32[160,128]{1,0:T(8,128)S(1)}, f32[160,128]{1,0:T(8,128)S(1)}, u32[]{:S(2)}, u32[]{:S(2)}) collective-permute-start(f32[160,128]{1,0:T(8,128)S(1)} %add_four.2.a), channel_id=1, source_target_pairs={{0,8},{1,9},{2,10},{3,11},{4,12},{5,13},{6,14},{7,15},{8,0},{9,1},... | collective-permute-start | bytes 245768 | tf_op jit(solution)/shard_map/ppermute | solution.py:310
  60.5 6.9 %collective-permute-start.14 = (f32[160,128]{1,0:T(8,128)S(1)}, f32[160,128]{1,0:T(8,128)S(1)}, u32[]{:S(2)}, u32[]{:S(2)}) collective-permute-start(f32[160,128]{1,0:T(8,128)S(1)} %add_four.2.a), channel_id=1, source_target_pairs={{0,4},{1,5},{2,6},{3,7},{4,0},{5,1},{6,2},{7,3},{8,12},{9,13},{10,... | collective-permute-start | bytes 245768 | tf_op jit(solution)/shard_map/ppermute | solution.py:310
  67.5 6.2 %collective-permute-start.15 = (f32[160,128]{1,0:T(8,128)S(1)}, f32[160,128]{1,0:T(8,128)S(1)}, u32[]{:S(2)}, u32[]{:S(2)}) collective-permute-start(f32[160,128]{1,0:T(8,128)S(1)} %add_four.3.refs_0_), channel_id=1, source_target_pairs={{0,3},{1,2},{2,1},{3,0},{4,7},{5,6},{6,5},{7,4},{8,11},{9,10},{10,... | collective-permute-start | bytes 245768 | tf_op jit(solution)/shard_map/ppermute | solution.py:310
  69.1 4.9 %collective-permute-start.16 = (f32[160,128]{1,0:T(8,128)S(1)}, f32[160,128]{1,0:T(8,128)S(1)}, u32[]{:S(2)}, u32[]{:S(2)}) collective-permute-start(f32[160,128]{1,0:T(8,128)S(1)} %add_four.3.refs_0_), channel_id=1, source_target_pairs={{0,1},{1,0},{2,3},{3,2},{4,5},{5,4},{6,7},{7,6},{8,9},{9,8},{10,11... | collective-permute-start | bytes 245768 | tf_op jit(solution)/shard_map/ppermute | solution.py:310
  70.0 4.5 %collective-permute-start.17 = (f32[160,128]{1,0:T(8,128)S(1)}, f32[160,128]{1,0:T(8,128)S(1)}, u32[]{:S(2)}, u32[]{:S(2)}) collective-permute-start(f32[160,128]{1,0:T(8,128)S(1)} %add_four.3.refs_0_), channel_id=1, source_target_pairs={{0,2},{1,3},{2,0},{3,1},{4,6},{5,7},{6,4},{7,5},{8,10},{9,11},{10,... | collective-permute-start | bytes 245768 | tf_op jit(solution)/shard_map/ppermute | solution.py:310
  74.5 1.7 %collective-permute-start.18 = (f32[640,128]{1,0:T(8,128)S(1)}, f32[640,128]{1,0:T(8,128)S(1)}, u32[]{:S(2)}, u32[]{:S(2)}) collective-permute-start(f32[640,128]{1,0:T(8,128)S(1)} %join.1.mine), channel_id=1, source_target_pairs={{0,16},{16,0},{1,17},{17,1},{2,18},{18,2},{3,19},{19,3},{4,20},{20... | collective-permute-start | bytes 983048 | tf_op jit(solution)/shard_map/ppermute | solution.py:513
